TPU v7x, 32 devices: a whole 2x2x4 slice. The times are simulated.
32 devices in a mesh: groups: 2 (over y), loop: 4 (over z), far: 4 (over x, core).
Axes of the slice: x: 2, y: 2, z: 4, core: 2. Of those that a mesh axis runs over, the one named last changes fastest.
Arguments:
- block: bfloat16 [64, 32768], P(None, ('groups', 'loop', 'far')), parts along dimension 1, may hold values from -6 to 6
- near_tiles: bfloat16 [1024, 256, 256], P(('groups', 'loop', 'far')), parts along dimension 0, may hold values from -0.125 to 0.125
- near_rows: int32 [1024], P(('groups', 'loop', 'far')), parts along dimension 0, may hold values from 0 to 3, as said below
- near_offsets: int32 [1024], P(('groups', 'loop', 'far')), parts along dimension 0, may hold values from -4 to 4, as said below
- col_basis: bfloat16 [128, 32, 256], P(('groups', 'loop', 'far')), parts along dimension 0, may hold values from -0.375 to 0.375
- couplings: bfloat16 [1024, 32, 32], P(('groups', 'loop', 'far')), parts along dimension 0, may hold values from -0.375 to 0.375
- far_rows: int32 [1024], P(('groups', 'loop', 'far')), parts along dimension 0, may hold values from 0 to 47, as said below
- far_cols: int32 [1024], P(('groups', 'loop', 'far')), parts along dimension 0, may hold values from 0 to 3
- row_basis: bfloat16 [128, 32, 256], P(('groups', 'loop', 'far')), parts along dimension 0, may hold values from -1 to 1
Outputs:
- krylov: bfloat16 [4, 64, 32768], P(None, None, ('groups', 'loop', 'far')), parts along dimension 2
There are 2 independent parts, one for each index of `groups`. A program takes and returns all parts, laid end to end along the dimension named above; each array names one. Nothing has to cross between parts.
Inputs may be any that keep to these rules, and one draw needn't show every extreme that they name: Within each device block of 32 near slots no pair of near_rows and near_offsets repeats; every device block has a slot with row 0 and offset -4. `near_offsets`: every device block has a slot with offset 4 on row 3. Within each device block of 32 far slots no pair of far_rows and far_cols repeats.
All inputs are finite; a program needn't handle non-finite values.
Results may differ from a plain program's by a relative error of at most 0.0071.
Values may be sent and summed in bfloat16 or wider, within the bound.
No kernel may reach another device: no remote copies, remote signals or barrier semaphores. Data moves between devices by JAX's collectives and lax.ppermute only.
A program may use at most 64 MiB of HBM per device.

v0:
```python
import jax
import jax.numpy as jnp
from jax import lax
from jax.sharding import PartitionSpec as P

PRODUCTS = 4


def extended(block, sides, width):
    for axis, dim in sides:
        count = lax.axis_size(axis)
        forward = [(i, i + 1) for i in range(count - 1)]
        forward.append((count - 1, 0))
        backward = [(target, source) for source, target in forward]
        low = lax.ppermute(
            lax.slice_in_dim(block, block.shape[dim] - width, None, axis=dim), axis, forward
        )
        high = lax.ppermute(lax.slice_in_dim(block, 0, width, axis=dim), axis, backward)
        block = jnp.concatenate([low, block, high], axis=dim)
    return block


def from_behind(value, axis, steps):
    count = lax.axis_size(axis)
    pairs = [(source, (source + steps) % count) for source in range(count)]
    return lax.ppermute(value, axis, pairs)


def on_device(
    block, near_tiles, near_rows, near_offsets, col_basis, couplings, far_rows, far_cols, row_basis
):
    highest = lax.Precision.HIGHEST
    rhs_count, shard_len = block.shape
    tile_size = near_tiles.shape[1]
    rank_size = couplings.shape[1]
    per_device = shard_len // tile_size
    members = lax.axis_size("far")
    block_clusters = per_device * members
    level_count = 3
    loop_size = lax.axis_size("loop")
    distances = (2, loop_size - 2, loop_size // 2)
    near_hot = (near_rows[:, None] == jnp.arange(per_device, dtype=jnp.int32)[None, :]).astype(
        jnp.float32
    )
    level_hot = (
        far_rows[:, None] == jnp.arange(level_count * block_clusters, dtype=jnp.int32)[None, :]
    ).astype(jnp.float32)
    basis_rows = row_basis.astype(jnp.float32)
    window_pos = per_device + near_rows + near_offsets
    current = block
    results = []
    for index in range(PRODUCTS):
        window = extended(current, ((("loop", "far"), 1),), per_device * tile_size)
        panels = window.reshape(rhs_count, -1, tile_size)
        chosen = jnp.take(panels, window_pos, axis=1)
        contrib = jnp.einsum("esq,spq->sep", chosen, near_tiles, preferred_element_type=jnp.float32)
        near_part = jnp.einsum("sr,sep->erp", near_hot, contrib, precision=highest)
        own_panels = current.reshape(rhs_count, per_device, tile_size)
        coeffs = jnp.einsum(
            "ckq,ecq->cke", col_basis, own_panels, preferred_element_type=jnp.float32
        ).astype(jnp.bfloat16)
        far_terms = jnp.einsum(
            "skq,sqe->ske",
            couplings,
            jnp.take(coeffs, far_cols, axis=0),
            preferred_element_type=jnp.float32,
        )
        partial_value = jnp.einsum("sa,ske->ake", level_hot, far_terms, precision=highest)
        partial_value = partial_value.reshape(level_count, block_clusters, rank_size, rhs_count)
        summed = lax.psum_scatter(partial_value, "far", scatter_dimension=1, tiled=True)
        own_coeffs = sum(
            (from_behind(summed[level], "loop", distances[level]) for level in range(level_count))
        )
        far_part = jnp.einsum("ckp,cke->ecp", basis_rows, own_coeffs, precision=highest)
        current = (near_part + far_part).reshape(rhs_count, shard_len).astype(jnp.bfloat16)
        results.append(current)
    return jnp.stack(results)


def solution(mesh):
    in_specs = (
        P(None, ("groups", "loop", "far")),
        P(("groups", "loop", "far"), None, None),
        P(("groups", "loop", "far")),
        P(("groups", "loop", "far")),
        P(("groups", "loop", "far"), None, None),
        P(("groups", "loop", "far"), None, None),
        P(("groups", "loop", "far")),
        P(("groups", "loop", "far")),
        P(("groups", "loop", "far"), None, None),
    )
    out_specs = P(None, None, ("groups", "loop", "far"))
    return jax.shard_map(
        on_device, mesh=mesh, in_specs=in_specs, out_specs=out_specs, check_vma=False
    )
```

profile of v0, /device:TPU:0, one launch (start us, length us, event | category | flops | bytes accessed | tf_op | source)
XLA Modules:
  0.0 246.6 jit_solution(1181654451661668068)
XLA Ops:
  6.5 5.4 %collective-permute-start.1 = (bf16[64,1024]{1,0:T(8,128)(2,1)}, bf16[64,1024]{1,0:T(8,128)(2,1)S(1)}, u32[]{:S(2)}, u32[]{:S(2)}) collective-permute-start(bf16[64,1024]{1,0:T(8,128)(2,1)} %param.13), channel_id=1, source_target_pairs={{1,0},{2,1},{3,2},{4,3},{5,4},{6,5},{7,6},{8,7},{9,8},{10,9},{11,1... | collective-permute-start | bytes 393224 | tf_op jit(solution)/shard_map/ppermute | solution.py:18
  12.0 0.7 compare_and_fusion
  12.6 0.7 compare_select_fusion
  13.3 1.1 convolution_convert_fusion.3
  14.4 0.6 gather_fusion.1
  15.3 1.5 fusion.45
  16.9 1.2 copy.34
  18.2 0.6 dynamic-slice
  19.5 0.6 gather_fusion
  20.1 33.9 %all-reduce.9.cloned.1.call-done = f32[3,16,32,64]{3,2,1,0:T(8,128)} async-done(((f32[3,16,32,64]{3,2,1,0:T(8,128)}), f32[3,16,32,64]{3,2,1,0:T(8,128)}) %all-reduce.9.cloned.1.call-update) | async-done | bytes 393232
  54.0 0.9 dynamic-slice_bitcast_fusion.10
  55.0 2.5 %collective-permute-start.3 = (f32[4,32,64]{2,1,0:T(8,128)S(1)}, f32[4,32,64]{2,1,0:T(8,128)S(1)}, u32[]{:S(2)}, u32[]{:S(2)}) collective-permute-start(f32[4,32,64]{2,1,0:T(8,128)S(1)} %get-tuple-element.18), channel_id=1, source_target_pairs={{0,8},{4,12},{8,0},{12,4},{1,9},{5,13},{9,1},{13,5},{2,10},{6,14},... | collective-permute-start | bytes 98312 | tf_op jit(solution)/shard_map/ppermute | solution.py:26
  57.4 0.5 collective-permute-start.2
  57.9 2.4 collective-permute-start.4
  60.4 3.6 %fusion.29 = f32[32,64,256]{2,1,0:T(8,128)S(1)} fusion(bf16[32,256,256]{2,1,0:T(8,128)(2,1)} %param.14, bf16[32,64,256]{2,1,0:T(8,128)(2,1)S(1)} %gather_fusion, pred[32]{0:T(512)(128)(4,1)S(1)} %get-tuple-element.6), kind=kOutput, calls=%fused_computation.37 | convolution fusion | flops 268959744 | bytes 7340064 | tf_op jit(solution)/shard_map/esq,spq->sep/dot_general | solution.py:56
  64.3 1.4 collective-permute-done.2
  65.7 0.8 collective-permute-done.4
  66.8 2.0 fusion.54
  69.2 2.8 %collective-permute-start.6 = (bf16[64,1024]{1,0:T(8,128)(2,1)S(1)}, bf16[64,1024]{1,0:T(8,128)(2,1)S(1)}, u32[]{:S(2)}, u32[]{:S(2)}) collective-permute-start(bf16[64,1024]{1,0:T(8,128)(2,1)S(1)} %bitcast.181), channel_id=1, source_target_pairs={{1,0},{2,1},{3,2},{4,3},{5,4},{6,5},{7,6},{8,7},{9,8},{10,9},{11,1... | collective-permute-start | bytes 393224 | tf_op jit(solution)/shard_map/ppermute | solution.py:18
  71.9 0.6 gather_fusion.3
  72.8 0.8 fusion.43
  73.7 1.2 copy.40
  74.9 4.1 %collective-permute-done.5 = bf16[64,1024]{1,0:T(8,128)(2,1)S(1)} collective-permute-done((bf16[64,1024]{1,0:T(8,128)(2,1)S(1)}, bf16[64,1024]{1,0:T(8,128)(2,1)S(1)}, u32[]{:S(2)}, u32[]{:S(2)}) %collective-permute-start.5) | collective-permute-done | bytes 131104 | tf_op jit(solution)/shard_map/ppermute | solution.py:15
  79.1 0.6 gather_fusion.2
  79.7 31.1 %all-reduce.11.cloned.1.call-done = f32[3,16,32,64]{3,2,1,0:T(8,128)} async-done(((f32[3,16,32,64]{3,2,1,0:T(8,128)}), f32[3,16,32,64]{3,2,1,0:T(8,128)}) %all-reduce.11.cloned.1.call-update) | async-done | bytes 393232
  110.8 0.9 dynamic-slice_bitcast_fusion.7
  111.7 2.5 %collective-permute-start.8 = (f32[4,32,64]{2,1,0:T(8,128)S(1)}, f32[4,32,64]{2,1,0:T(8,128)S(1)}, u32[]{:S(2)}, u32[]{:S(2)}) collective-permute-start(f32[4,32,64]{2,1,0:T(8,128)S(1)} %get-tuple-element.15), channel_id=1, source_target_pairs={{0,8},{4,12},{8,0},{12,4},{1,9},{5,13},{9,1},{13,5},{2,10},{6,14},... | collective-permute-start | bytes 98312 | tf_op jit(solution)/shard_map/ppermute | solution.py:26
  114.2 0.5 collective-permute-start.7
  114.7 2.4 collective-permute-start.9
  117.1 3.6 %fusion.27 = f32[32,64,256]{2,1,0:T(8,128)S(1)} fusion(bf16[32,256,256]{2,1,0:T(8,128)(2,1)} %param.14, bf16[32,64,256]{2,1,0:T(8,128)(2,1)S(1)} %gather_fusion.2, pred[32]{0:T(512)(128)(4,1)S(1)} %get-tuple-element.6), kind=kOutput, calls=%fused_computation.35 | convolution fusion | flops 268959744 | bytes 7340064 | tf_op jit(solution)/shard_map/esq,spq->sep/dot_general | solution.py:56
  121.0 1.4 collective-permute-done.7
  122.4 0.8 collective-permute-done.9
  123.6 2.0 fusion.53
  125.9 2.8 %collective-permute-start.11 = (bf16[64,1024]{1,0:T(8,128)(2,1)S(1)}, bf16[64,1024]{1,0:T(8,128)(2,1)S(1)}, u32[]{:S(2)}, u32[]{:S(2)}) collective-permute-start(bf16[64,1024]{1,0:T(8,128)(2,1)S(1)} %bitcast.184), channel_id=1, source_target_pairs={{1,0},{2,1},{3,2},{4,3},{5,4},{6,5},{7,6},{8,7},{9,8},{10,9},{11,1... | collective-permute-start | bytes 393224 | tf_op jit(solution)/shard_map/ppermute | solution.py:18
  128.7 0.6 gather_fusion.5
  129.5 0.9 fusion.41
  130.4 1.2 copy.46
  131.7 4.1 %collective-permute-done.10 = bf16[64,1024]{1,0:T(8,128)(2,1)S(1)} collective-permute-done((bf16[64,1024]{1,0:T(8,128)(2,1)S(1)}, bf16[64,1024]{1,0:T(8,128)(2,1)S(1)}, u32[]{:S(2)}, u32[]{:S(2)}) %collective-permute-start.10) | collective-permute-done | bytes 131104 | tf_op jit(solution)/shard_map/ppermute | solution.py:15
  135.8 0.6 gather_fusion.4
  136.4 31.1 %all-reduce.13.cloned.1.call-done = f32[3,16,32,64]{3,2,1,0:T(8,128)} async-done(((f32[3,16,32,64]{3,2,1,0:T(8,128)}), f32[3,16,32,64]{3,2,1,0:T(8,128)}) %all-reduce.13.cloned.1.call-update) | async-done | bytes 393232
  167.5 0.9 dynamic-slice_bitcast_fusion.4
  168.4 2.5 %collective-permute-start.13 = (f32[4,32,64]{2,1,0:T(8,128)S(1)}, f32[4,32,64]{2,1,0:T(8,128)S(1)}, u32[]{:S(2)}, u32[]{:S(2)}) collective-permute-start(f32[4,32,64]{2,1,0:T(8,128)S(1)} %get-tuple-element.12), channel_id=1, source_target_pairs={{0,8},{4,12},{8,0},{12,4},{1,9},{5,13},{9,1},{13,5},{2,10},{6,14},... | collective-permute-start | bytes 98312 | tf_op jit(solution)/shard_map/ppermute | solution.py:26
  170.9 0.5 collective-permute-start.12
  171.4 2.4 collective-permute-start.14
  173.8 3.6 %fusion.25 = f32[32,64,256]{2,1,0:T(8,128)S(1)} fusion(bf16[32,256,256]{2,1,0:T(8,128)(2,1)} %param.14, bf16[32,64,256]{2,1,0:T(8,128)(2,1)S(1)} %gather_fusion.4, pred[32]{0:T(512)(128)(4,1)S(1)} %get-tuple-element.6), kind=kOutput, calls=%fused_computation.33 | convolution fusion | flops 268959744 | bytes 7340064 | tf_op jit(solution)/shard_map/esq,spq->sep/dot_general | solution.py:56
  177.8 1.4 collective-permute-done.12
  179.2 0.8 collective-permute-done.14
  180.3 2.0 fusion.52
  182.6 2.8 %collective-permute-start.16 = (bf16[64,1024]{1,0:T(8,128)(2,1)S(1)}, bf16[64,1024]{1,0:T(8,128)(2,1)S(1)}, u32[]{:S(2)}, u32[]{:S(2)}) collective-permute-start(bf16[64,1024]{1,0:T(8,128)(2,1)S(1)} %bitcast.187), channel_id=1, source_target_pairs={{1,0},{2,1},{3,2},{4,3},{5,4},{6,5},{7,6},{8,7},{9,8},{10,9},{11,1... | collective-permute-start | bytes 393224 | tf_op jit(solution)/shard_map/ppermute | solution.py:18
  185.4 0.6 gather_fusion.7
  186.3 0.9 fusion.39
  187.1 1.2 copy.52
  188.3 4.1 %collective-permute-done.15 = bf16[64,1024]{1,0:T(8,128)(2,1)S(1)} collective-permute-done((bf16[64,1024]{1,0:T(8,128)(2,1)S(1)}, bf16[64,1024]{1,0:T(8,128)(2,1)S(1)}, u32[]{:S(2)}, u32[]{:S(2)}) %collective-permute-start.15) | collective-permute-done | bytes 131104 | tf_op jit(solution)/shard_map/ppermute | solution.py:15
  192.5 0.6 gather_fusion.6
  193.2 31.1 %all-reduce.15.cloned.1.call-done = f32[3,16,32,64]{3,2,1,0:T(8,128)} async-done(((f32[3,16,32,64]{3,2,1,0:T(8,128)}), f32[3,16,32,64]{3,2,1,0:T(8,128)}) %all-reduce.15.cloned.1.call-update) | async-done | bytes 393232
  224.3 0.9 dynamic-slice_bitcast_fusion.1
  225.2 2.5 %collective-permute-start.18 = (f32[4,32,64]{2,1,0:T(8,128)S(1)}, f32[4,32,64]{2,1,0:T(8,128)S(1)}, u32[]{:S(2)}, u32[]{:S(2)}) collective-permute-start(f32[4,32,64]{2,1,0:T(8,128)S(1)} %get-tuple-element.9), channel_id=1, source_target_pairs={{0,8},{4,12},{8,0},{12,4},{1,9},{5,13},{9,1},{13,5},{2,10},{6,14},... | collective-permute-start | bytes 98312 | tf_op jit(solution)/shard_map/ppermute | solution.py:26
  227.7 0.5 collective-permute-start.17
  228.2 2.4 collective-permute-start.19
  230.6 3.6 %fusion.23 = f32[32,64,256]{2,1,0:T(8,128)S(1)} fusion(bf16[32,256,256]{2,1,0:T(8,128)(2,1)} %param.14, bf16[32,64,256]{2,1,0:T(8,128)(2,1)S(1)} %gather_fusion.6, pred[32]{0:T(512)(128)(4,1)S(1)} %get-tuple-element.6), kind=kOutput, calls=%fused_computation.31 | convolution fusion | flops 268959744 | bytes 7340064 | tf_op jit(solution)/shard_map/esq,spq->sep/dot_general | solution.py:56
  234.5 1.4 collective-permute-done.17
  235.9 0.8 collective-permute-done.19
  237.1 2.0 fusion.51
  239.2 0.9 pad_maximum_fusion
  (66 shorter events, 5.0 us)
Async XLA Ops:
  6.5 8.5 %copy-start = (bf16[32,32,32]{2,1,0:T(8,128)(2,1)S(1)}, bf16[32,32,32]{2,1,0:T(8,128)(2,1)}, u32[]{:S(2)}) copy-start(bf16[32,32,32]{2,1,0:T(8,128)(2,1)} %param.18) | copy-start | bytes 196612
  6.5 47.5 %all-reduce.9.cloned.1.call-start = ((), (), s32[]{:S(2)}) async-start(), calls=%async_computation | async-start | bytes 1572864
  6.5 12.9 %collective-permute-start.1 = (bf16[64,1024]{1,0:T(8,128)(2,1)}, bf16[64,1024]{1,0:T(8,128)(2,1)S(1)}, u32[]{:S(2)}, u32[]{:S(2)}) collective-permute-start(bf16[64,1024]{1,0:T(8,128)(2,1)} %param.13), channel_id=1, source_target_pairs={{1,0},{2,1},{3,2},{4,3},{5,4},{6,5},{7,6},{8,7},{9,8},{10,9},{11,1... | collective-permute-start | bytes 393224 | tf_op jit(solution)/shard_map/ppermute | solution.py:18
  12.0 7.5 %collective-permute-start = (bf16[64,1024]{1,0:T(8,128)(2,1)}, bf16[64,1024]{1,0:T(8,128)(2,1)S(1)}, u32[]{:S(2)}, u32[]{:S(2)}) collective-permute-start(bf16[64,1024]{1,0:T(8,128)(2,1)} %param.13), channel_id=1, source_target_pairs={{0,1},{1,2},{2,3},{3,4},{4,5},{5,6},{6,7},{7,8},{8,9},{9,10},{10,1... | collective-permute-start | bytes 393224 | tf_op jit(solution)/shard_map/ppermute | solution.py:15
  15.3 2.8 %copy-start.4 = (s32[32]{0:T(128)S(1)}, s32[32]{0:T(128)}, u32[]{:S(2)}) copy-start(s32[32]{0:T(128)} %param.15) | copy-start | bytes 388
  15.3 2.8 %copy-start.6 = (s32[32]{0:T(128)S(1)}, s32[32]{0:T(128)}, u32[]{:S(2)}) copy-start(s32[32]{0:T(128)} %param.16) | copy-start | bytes 388
  15.3 2.8 %copy-start.7 = (u32[32]{0:T(128)S(1)}, u32[32]{0:T(128)}, u32[]{:S(2)}) copy-start(u32[32]{0:T(128)} %constant.26) | copy-start | bytes 388
  15.3 4.1 %copy-start.2 = (bf16[64,1024]{1,0:T(8,128)(2,1)S(1)}, bf16[64,1024]{1,0:T(8,128)(2,1)}, u32[]{:S(2)}) copy-start(bf16[64,1024]{1,0:T(8,128)(2,1)} %param.13) | copy-start | bytes 393220
  18.1 92.7 %all-reduce.11.cloned.1.call-start = ((), (), s32[]{:S(2)}) async-start(), calls=%async_computation.1 | async-start | bytes 1572864
  55.0 9.3 %collective-permute-start.3 = (f32[4,32,64]{2,1,0:T(8,128)S(1)}, f32[4,32,64]{2,1,0:T(8,128)S(1)}, u32[]{:S(2)}, u32[]{:S(2)}) collective-permute-start(f32[4,32,64]{2,1,0:T(8,128)S(1)} %get-tuple-element.18), channel_id=1, source_target_pairs={{0,8},{4,12},{8,0},{12,4},{1,9},{5,13},{9,1},{13,5},{2,10},{6,14},... | collective-permute-start | bytes 98312 | tf_op jit(solution)/shard_map/ppermute | solution.py:26
  57.4 8.2 %collective-permute-start.2 = (f32[4,32,64]{2,1,0:T(8,128)S(1)}, f32[4,32,64]{2,1,0:T(8,128)S(1)}, u32[]{:S(2)}, u32[]{:S(2)}) collective-permute-start(f32[4,32,64]{2,1,0:T(8,128)S(1)} %get-tuple-element.19), channel_id=1, source_target_pairs={{0,8},{4,12},{8,0},{12,4},{1,9},{5,13},{9,1},{13,5},{2,10},{6,14},... | collective-permute-start | bytes 98312 | tf_op jit(solution)/shard_map/ppermute | solution.py:26
  57.9 8.6 %collective-permute-start.4 = (f32[4,32,64]{2,1,0:T(8,128)S(1)}, f32[4,32,64]{2,1,0:T(8,128)S(1)}, u32[]{:S(2)}, u32[]{:S(2)}) collective-permute-start(f32[4,32,64]{2,1,0:T(8,128)S(1)} %get-tuple-element.20), channel_id=1, source_target_pairs={{0,8},{4,12},{8,0},{12,4},{1,9},{5,13},{9,1},{13,5},{2,10},{6,14},... | collective-permute-start | bytes 98312 | tf_op jit(solution)/shard_map/ppermute | solution.py:26
  60.4 6.2 %copy-start.1 = (bf16[4,32,256]{2,1,0:T(8,128)(2,1)S(1)}, bf16[4,32,256]{2,1,0:T(8,128)(2,1)}, u32[]{:S(2)}) copy-start(bf16[4,32,256]{2,1,0:T(8,128)(2,1)} %param.21) | copy-start | bytes 196612
  64.0 4.9 %copy-start.3 = (bf16[4,32,256]{2,1,0:T(8,128)(2,1)S(1)}, bf16[4,32,256]{2,1,0:T(8,128)(2,1)}, u32[]{:S(2)}) copy-start(bf16[4,32,256]{2,1,0:T(8,128)(2,1)} %param.17) | copy-start | bytes 196612
  66.8 6.0 %copy-start.5 = (s32[32]{0:T(128)S(1)}, s32[32]{0:T(128)}, u32[]{:S(2)}) copy-start(s32[32]{0:T(128)} %param.19) | copy-start | bytes 388
  69.2 5.8 %collective-permute-start.6 = (bf16[64,1024]{1,0:T(8,128)(2,1)S(1)}, bf16[64,1024]{1,0:T(8,128)(2,1)S(1)}, u32[]{:S(2)}, u32[]{:S(2)}) collective-permute-start(bf16[64,1024]{1,0:T(8,128)(2,1)S(1)} %bitcast.181), channel_id=1, source_target_pairs={{1,0},{2,1},{3,2},{4,3},{5,4},{6,5},{7,6},{8,7},{9,8},{10,9},{11,1... | collective-permute-start | bytes 393224 | tf_op jit(solution)/shard_map/ppermute | solution.py:18
  71.9 7.1 %collective-permute-start.5 = (bf16[64,1024]{1,0:T(8,128)(2,1)S(1)}, bf16[64,1024]{1,0:T(8,128)(2,1)S(1)}, u32[]{:S(2)}, u32[]{:S(2)}) collective-permute-start(bf16[64,1024]{1,0:T(8,128)(2,1)S(1)} %bitcast.182), channel_id=1, source_target_pairs={{0,1},{1,2},{2,3},{3,4},{4,5},{5,6},{6,7},{7,8},{8,9},{9,10},{10,1... | collective-permute-start | bytes 393224 | tf_op jit(solution)/shard_map/ppermute | solution.py:15
  74.9 92.7 %all-reduce.13.cloned.1.call-start = ((), (), s32[]{:S(2)}) async-start(), calls=%async_computation.2 | async-start | bytes 1572864
  111.7 9.3 %collective-permute-start.8 = (f32[4,32,64]{2,1,0:T(8,128)S(1)}, f32[4,32,64]{2,1,0:T(8,128)S(1)}, u32[]{:S(2)}, u32[]{:S(2)}) collective-permute-start(f32[4,32,64]{2,1,0:T(8,128)S(1)} %get-tuple-element.15), channel_id=1, source_target_pairs={{0,8},{4,12},{8,0},{12,4},{1,9},{5,13},{9,1},{13,5},{2,10},{6,14},... | collective-permute-start | bytes 98312 | tf_op jit(solution)/shard_map/ppermute | solution.py:26
  114.2 8.2 %collective-permute-start.7 = (f32[4,32,64]{2,1,0:T(8,128)S(1)}, f32[4,32,64]{2,1,0:T(8,128)S(1)}, u32[]{:S(2)}, u32[]{:S(2)}) collective-permute-start(f32[4,32,64]{2,1,0:T(8,128)S(1)} %get-tuple-element.16), channel_id=1, source_target_pairs={{0,8},{4,12},{8,0},{12,4},{1,9},{5,13},{9,1},{13,5},{2,10},{6,14},... | collective-permute-start | bytes 98312 | tf_op jit(solution)/shard_map/ppermute | solution.py:26
  114.7 8.6 %collective-permute-start.9 = (f32[4,32,64]{2,1,0:T(8,128)S(1)}, f32[4,32,64]{2,1,0:T(8,128)S(1)}, u32[]{:S(2)}, u32[]{:S(2)}) collective-permute-start(f32[4,32,64]{2,1,0:T(8,128)S(1)} %get-tuple-element.17), channel_id=1, source_target_pairs={{0,8},{4,12},{8,0},{12,4},{1,9},{5,13},{9,1},{13,5},{2,10},{6,14},... | collective-permute-start | bytes 98312 | tf_op jit(solution)/shard_map/ppermute | solution.py:26
  125.9 5.8 %collective-permute-start.11 = (bf16[64,1024]{1,0:T(8,128)(2,1)S(1)}, bf16[64,1024]{1,0:T(8,128)(2,1)S(1)}, u32[]{:S(2)}, u32[]{:S(2)}) collective-permute-start(bf16[64,1024]{1,0:T(8,128)(2,1)S(1)} %bitcast.184), channel_id=1, source_target_pairs={{1,0},{2,1},{3,2},{4,3},{5,4},{6,5},{7,6},{8,7},{9,8},{10,9},{11,1... | collective-permute-start | bytes 393224 | tf_op jit(solution)/shard_map/ppermute | solution.py:18
  128.7 7.1 %collective-permute-start.10 = (bf16[64,1024]{1,0:T(8,128)(2,1)S(1)}, bf16[64,1024]{1,0:T(8,128)(2,1)S(1)}, u32[]{:S(2)}, u32[]{:S(2)}) collective-permute-start(bf16[64,1024]{1,0:T(8,128)(2,1)S(1)} %bitcast.185), channel_id=1, source_target_pairs={{0,1},{1,2},{2,3},{3,4},{4,5},{5,6},{6,7},{7,8},{8,9},{9,10},{10,1... | collective-permute-start | bytes 393224 | tf_op jit(solution)/shard_map/ppermute | solution.py:15
  131.6 92.7 %all-reduce.15.cloned.1.call-start = ((), (), s32[]{:S(2)}) async-start(), calls=%async_computation.3 | async-start | bytes 1572864
  168.4 9.3 %collective-permute-start.13 = (f32[4,32,64]{2,1,0:T(8,128)S(1)}, f32[4,32,64]{2,1,0:T(8,128)S(1)}, u32[]{:S(2)}, u32[]{:S(2)}) collective-permute-start(f32[4,32,64]{2,1,0:T(8,128)S(1)} %get-tuple-element.12), channel_id=1, source_target_pairs={{0,8},{4,12},{8,0},{12,4},{1,9},{5,13},{9,1},{13,5},{2,10},{6,14},... | collective-permute-start | bytes 98312 | tf_op jit(solution)/shard_map/ppermute | solution.py:26
  170.9 8.2 %collective-permute-start.12 = (f32[4,32,64]{2,1,0:T(8,128)S(1)}, f32[4,32,64]{2,1,0:T(8,128)S(1)}, u32[]{:S(2)}, u32[]{:S(2)}) collective-permute-start(f32[4,32,64]{2,1,0:T(8,128)S(1)} %get-tuple-element.13), channel_id=1, source_target_pairs={{0,8},{4,12},{8,0},{12,4},{1,9},{5,13},{9,1},{13,5},{2,10},{6,14},... | collective-permute-start | bytes 98312 | tf_op jit(solution)/shard_map/ppermute | solution.py:26
  171.4 8.6 %collective-permute-start.14 = (f32[4,32,64]{2,1,0:T(8,128)S(1)}, f32[4,32,64]{2,1,0:T(8,128)S(1)}, u32[]{:S(2)}, u32[]{:S(2)}) collective-permute-start(f32[4,32,64]{2,1,0:T(8,128)S(1)} %get-tuple-element.14), channel_id=1, source_target_pairs={{0,8},{4,12},{8,0},{12,4},{1,9},{5,13},{9,1},{13,5},{2,10},{6,14},... | collective-permute-start | bytes 98312 | tf_op jit(solution)/shard_map/ppermute | solution.py:26
  182.6 5.7 %collective-permute-start.16 = (bf16[64,1024]{1,0:T(8,128)(2,1)S(1)}, bf16[64,1024]{1,0:T(8,128)(2,1)S(1)}, u32[]{:S(2)}, u32[]{:S(2)}) collective-permute-start(bf16[64,1024]{1,0:T(8,128)(2,1)S(1)} %bitcast.187), channel_id=1, source_target_pairs={{1,0},{2,1},{3,2},{4,3},{5,4},{6,5},{7,6},{8,7},{9,8},{10,9},{11,1... | collective-permute-start | bytes 393224 | tf_op jit(solution)/shard_map/ppermute | solution.py:18
  185.4 7.1 %collective-permute-start.15 = (bf16[64,1024]{1,0:T(8,128)(2,1)S(1)}, bf16[64,1024]{1,0:T(8,128)(2,1)S(1)}, u32[]{:S(2)}, u32[]{:S(2)}) collective-permute-start(bf16[64,1024]{1,0:T(8,128)(2,1)S(1)} %bitcast.188), channel_id=1, source_target_pairs={{0,1},{1,2},{2,3},{3,4},{4,5},{5,6},{6,7},{7,8},{8,9},{9,10},{10,1... | collective-permute-start | bytes 393224 | tf_op jit(solution)/shard_map/ppermute | solution.py:15
  225.2 9.3 %collective-permute-start.18 = (f32[4,32,64]{2,1,0:T(8,128)S(1)}, f32[4,32,64]{2,1,0:T(8,128)S(1)}, u32[]{:S(2)}, u32[]{:S(2)}) collective-permute-start(f32[4,32,64]{2,1,0:T(8,128)S(1)} %get-tuple-element.9), channel_id=1, source_target_pairs={{0,8},{4,12},{8,0},{12,4},{1,9},{5,13},{9,1},{13,5},{2,10},{6,14},... | collective-permute-start | bytes 98312 | tf_op jit(solution)/shard_map/ppermute | solution.py:26
  227.7 8.2 %collective-permute-start.17 = (f32[4,32,64]{2,1,0:T(8,128)S(1)}, f32[4,32,64]{2,1,0:T(8,128)S(1)}, u32[]{:S(2)}, u32[]{:S(2)}) collective-permute-start(f32[4,32,64]{2,1,0:T(8,128)S(1)} %get-tuple-element.10), channel_id=1, source_target_pairs={{0,8},{4,12},{8,0},{12,4},{1,9},{5,13},{9,1},{13,5},{2,10},{6,14},... | collective-permute-start | bytes 98312 | tf_op jit(solution)/shard_map/ppermute | solution.py:26
  228.2 8.6 %collective-permute-start.19 = (f32[4,32,64]{2,1,0:T(8,128)S(1)}, f32[4,32,64]{2,1,0:T(8,128)S(1)}, u32[]{:S(2)}, u32[]{:S(2)}) collective-permute-start(f32[4,32,64]{2,1,0:T(8,128)S(1)} %get-tuple-element.11), channel_id=1, source_target_pairs={{0,8},{4,12},{8,0},{12,4},{1,9},{5,13},{9,1},{13,5},{2,10},{6,14},... | collective-permute-start | bytes 98312 | tf_op jit(solution)/shard_map/ppermute | solution.py:26
Sparse Core Ops, SparseCore 0:
  18.2 35.8 all-reduce.8
  75.0 35.7 all-reduce.10
  131.7 35.7 all-reduce.12
  188.4 35.7 all-reduce.14
where the time goes:
time: 247 us
  waiting for transfers between devices  150 us (61%)
  starting transfers between devices  35.4 us (14%)
  matrix products  30.4 us (12%)
  local copies, waits for them, and re-layouts  14.3 us (6%)
  between operations  14.3 us (6%)
    unnamed x8, waiting for transfers between devices  127 us
    ppermute x12, starting transfers between devices, from_behind(): return lax.ppermute(value, axis, pairs)  21.6 us
    dot_general x4, matrix products, on_device(): jnp.einsum('esq,spq->sep', chosen, near_tiles, preferred_element_type=jnp...  14.3 us
    ppermute x4, starting transfers between devices, extended(): lax.ppermute(lax.slice_in_dim(block, 0, width, axis=dim), axis, backward)  13.7 us
    ppermute x4, waiting for transfers between devices, extended(): lax.ppermute(lax.slice_in_dim(block, block.shape[dim] - width, None, axis...  12.3 us
    ppermute x12, waiting for transfers between devices, from_behind(): return lax.ppermute(value, axis, pairs)  10.3 us
    dot_general x4, matrix products, on_device(): near_part = jnp.einsum('sr,sep->erp', near_hot, contrib, precision=highest)  8.09 us
  transfers between devices with their start and end apart: 24, of which 19 were waited for; matrix products, arithmetic and copies ran while one was open for 13% of the time, Pallas kernels for 0%

commit v1 on v0

v1 whole, which is shorter than its diff:
```python
import functools

import jax
import jax.numpy as jnp
from jax import lax
from jax.experimental import pallas as pl
from jax.experimental.pallas import tpu as pltpu
from jax.sharding import PartitionSpec as P

PRODUCTS = 4
REACH = 4
LEVELS = 3
SPAN = 2 * REACH + 1

F32 = jnp.float32
BF16 = jnp.bfloat16
IN_VMEM = pl.BlockSpec(memory_space=pltpu.VMEM)
IN_SMEM = pl.BlockSpec(memory_space=pltpu.SMEM)
ANYWHERE = pl.BlockSpec(memory_space=pl.ANY)


def dot_nt(a, b):
    return lax.dot_general(a, b, (((1,), (1,)), ((), ())), preferred_element_type=F32)


def dot_nn(a, b):
    return lax.dot_general(a, b, (((1,), (0,)), ((), ())), preferred_element_type=F32)


def held(value):
    return pltpu.with_memory_space_constraint(value, pltpu.VMEM)


def far_pieces(x, cb_ref, g_ref, sets, send_refs):
    coeffs = dot_nt(x, cb_ref[...]).astype(BF16)
    width = cb_ref.shape[0]
    steps = len(send_refs) // len(sets)
    for index, levels in enumerate(sets):
        total = sum(dot_nt(coeffs, g_ref[level]) for level in levels).astype(BF16)
        for step in range(steps):
            send_refs[index * steps + step][...] = total[:, step * width : (step + 1) * width]


def prepare_kernel(
    per_device, members, sets, rows_ref, cols_ref, member_ref, x_ref, col_ref, coup_ref, row_ref, *outs
):
    g_ref, cb_ref, rb_ref, *sends = outs
    slots, rank, _ = coup_ref.shape
    size = col_ref.shape[2]
    width = per_device * rank
    block_clusters = per_device * members
    member = member_ref[0]
    cb_ref[...] = jnp.zeros_like(cb_ref)
    rb_ref[...] = jnp.zeros_like(rb_ref)
    for c in range(per_device):
        cb_ref[c * rank : (c + 1) * rank, c * size : (c + 1) * size] = col_ref[c]
        for half in range(2):
            start = half * width + c * rank
            rb_ref[start : start + rank, c * size : (c + 1) * size] = row_ref[c]
    g_ref[...] = jnp.zeros_like(g_ref)
    column = lax.broadcasted_iota(jnp.int32, (rank, width), 1) // rank
    for s in range(slots):
        level = rows_ref[s] // block_clusters
        row = rows_ref[s] % block_clusters
        step = lax.rem(row // per_device - member + members, members)
        start = pl.multiple_of((step * per_device + row % per_device) * rank, rank)
        tile = coup_ref[s].astype(F32)
        wide = jnp.where(column == cols_ref[s], jnp.concatenate([tile] * per_device, axis=1), 0.0)
        where = (level, pl.ds(start, rank), slice(None))
        g_ref[where] = g_ref[where] + wide.astype(BF16)
    far_pieces(x_ref[...], cb_ref, g_ref, sets, sends)


def own_sums(x_ref, d_ref, acc_ref, per_device):
    size = d_ref.shape[1]
    panels = [x_ref[:, c * size : (c + 1) * size] for c in range(per_device)]
    for r in range(per_device):
        acc_ref[:, r * size : (r + 1) * size] = sum(
            dot_nt(panels[c], d_ref[r * SPAN + c - r + REACH]) for c in range(per_device)
        )


def first_own_kernel(per_device, rows_ref, offsets_ref, x_ref, tiles_ref, d_ref, acc_ref, present, sems):
    slots = tiles_ref.shape[0]
    for cell in range(per_device * SPAN):
        present[cell] = 0
    for s in range(slots):
        cell = rows_ref[s] * SPAN + offsets_ref[s] + REACH
        present[cell] = 1
        pltpu.make_async_copy(tiles_ref.at[s], d_ref.at[cell], sems.at[s]).start()
    for s in range(slots):
        cell = rows_ref[s] * SPAN + offsets_ref[s] + REACH
        pltpu.make_async_copy(tiles_ref.at[s], d_ref.at[cell], sems.at[s]).wait()

    @pl.loop(0, per_device * SPAN)
    def _(cell):
        @pl.when(present[cell] == 0)
        def _():
            d_ref[cell] = jnp.zeros(d_ref.shape[1:], d_ref.dtype)

    own_sums(x_ref, d_ref, acc_ref, per_device)


def own_kernel(per_device, slot, x_ref, d_ref, *refs):
    krylov_ref, acc_ref, sem = refs[-3:]
    copy = pltpu.make_async_copy(x_ref, krylov_ref.at[slot], sem)
    copy.start()
    own_sums(x_ref, d_ref, acc_ref, per_device)
    copy.wait()


def next_block(per_device, acc_ref, low_ref, high_ref, d_ref, rb_ref, piece_refs):
    size = d_ref.shape[1]
    total = sum(piece[...].astype(F32) for piece in piece_refs)
    upper = total.astype(BF16)
    lower = (total - upper.astype(F32)).astype(BF16)
    both = jnp.concatenate([upper, lower], axis=1)
    low = [low_ref[:, c * size : (c + 1) * size] for c in range(per_device)]
    high = [high_ref[:, c * size : (c + 1) * size] for c in range(per_device)]
    parts = []
    for r in range(per_device):
        columns = slice(r * size, (r + 1) * size)
        value = acc_ref[:, columns] + dot_nn(both, rb_ref[:, columns])
        for c in range(per_device):
            for panel, place in ((low[c], c - per_device), (high[c], c + per_device)):
                offset = place - r
                if -REACH <= offset <= REACH:
                    value = value + dot_nt(panel, d_ref[r * SPAN + offset + REACH])
        parts.append(value.astype(BF16))
    return jnp.concatenate(parts, axis=1)


def finish_kernel(per_device, sets, pieces, *refs):
    acc_ref, low_ref, high_ref, d_ref, rb_ref, cb_ref, g_ref = refs[:7]
    piece_refs = refs[7 : 7 + pieces]
    x_ref, *sends = refs[7 + pieces :]
    x = next_block(per_device, acc_ref, low_ref, high_ref, d_ref, rb_ref, piece_refs)
    x_ref[...] = x
    far_pieces(x, cb_ref, g_ref, sets, sends)


def last_kernel(per_device, slot, pieces, *refs):
    acc_ref, low_ref, high_ref, d_ref, rb_ref = refs[:5]
    piece_refs = refs[5 : 5 + pieces]
    _, krylov_ref, x_ref, sem = refs[5 + pieces :]
    x_ref[...] = next_block(per_device, acc_ref, low_ref, high_ref, d_ref, rb_ref, piece_refs)
    copy = pltpu.make_async_copy(x_ref, krylov_ref.at[slot], sem)
    copy.start()
    copy.wait()


def on_device(
    block, near_tiles, near_rows, near_offsets, col_basis, couplings, far_rows, far_cols, row_basis
):
    rhs, shard_len = block.shape
    size = near_tiles.shape[1]
    rank = couplings.shape[1]
    per_device = shard_len // size
    members = lax.axis_size("far")
    loop_size = lax.axis_size("loop")
    devices = members * loop_size
    width = per_device * rank
    distances = [d % loop_size for d in (2, loop_size - 2, loop_size // 2)]
    hops = sorted(set(distances))
    sets = tuple(tuple(i for i, d in enumerate(distances) if d == hop) for hop in hops)
    pieces = len(hops) * members
    ring = [(i, (i + 1) % devices) for i in range(devices)]
    back = [(target, source) for source, target in ring]
    routes = []
    for hop in hops:
        for step in range(members):
            routes.append(
                [
                    (l * members + m, (l + hop) % loop_size * members + (m + step) % members)
                    for l in range(loop_size)
                    for m in range(members)
                ]
            )
    both_axes = ("loop", "far")
    params = pltpu.CompilerParams(vmem_limit_bytes=16 * 2**20)

    def call(kernel, ins, specs, outs, out_specs, scratch=(), aliases=None, flops=0, name=None):
        ins = [held(v) if spec is IN_VMEM else v for v, spec in zip(ins, specs)]
        return pl.pallas_call(
            kernel,
            in_specs=list(specs),
            out_specs=list(out_specs),
            out_shape=list(outs),
            scratch_shapes=list(scratch),
            input_output_aliases=aliases or {},
            compiler_params=params,
            cost_estimate=pl.CostEstimate(flops=flops, bytes_accessed=2**22, transcendentals=0),
            name=name,
        )(*ins)

    def vmem(shape, dtype):
        return pltpu.VMEM(shape, dtype)

    block_out = vmem((rhs, shard_len), BF16)
    acc_out = vmem((rhs, shard_len), F32)
    piece_outs = [vmem((rhs, width), BF16)] * pieces
    krylov_out = jax.ShapeDtypeStruct((PRODUCTS, rhs, shard_len), BF16)
    cells = per_device * SPAN

    current = block
    krylov = None
    sends = None
    for index in range(PRODUCTS):
        low = lax.ppermute(current, both_axes, ring)
        high = lax.ppermute(current, both_axes, back)
        if index == 0:
            member = lax.axis_index("far").astype(jnp.int32).reshape(1)
            coupled, col_wide, row_wide, *sends = call(
                functools.partial(prepare_kernel, per_device, members, sets),
                [far_rows, far_cols, member, block, col_basis, couplings, row_basis],
                [IN_SMEM] * 3 + [IN_VMEM] * 4,
                [
                    vmem((LEVELS, members * width, width), BF16),
                    vmem((width, shard_len), BF16),
                    vmem((2 * width, shard_len), BF16),
                    *piece_outs,
                ],
                [IN_VMEM] * (3 + pieces),
                flops=10**8,
                name="prepare",
            )
        received = [lax.ppermute(s, both_axes, route) for s, route in zip(sends, routes)]
        if index == 0:
            dense, acc = call(
                functools.partial(first_own_kernel, per_device),
                [near_rows, near_offsets, current, near_tiles],
                [IN_SMEM, IN_SMEM, IN_VMEM, ANYWHERE],
                [vmem((cells, size, size), BF16), acc_out],
                [IN_VMEM] * 2,
                [pltpu.SMEM((cells,), jnp.int32), pltpu.SemaphoreType.DMA((near_tiles.shape[0],))],
                flops=10**9,
                name="first_own",
            )
        else:
            ins, specs, aliases = [current, dense], [IN_VMEM] * 2, None
            if krylov is not None:
                ins, specs, aliases = ins + [krylov], specs + [ANYWHERE], {2: 0}
            krylov, acc = call(
                functools.partial(own_kernel, per_device, index - 1),
                ins,
                specs,
                [krylov_out, acc_out],
                [ANYWHERE, IN_VMEM],
                [pltpu.SemaphoreType.DMA],
                aliases,
                flops=10**9,
                name="own",
            )
        if index < PRODUCTS - 1:
            ins = [acc, low, high, dense, row_wide, col_wide, coupled, *received]
            current, *sends = call(
                functools.partial(finish_kernel, per_device, sets, pieces),
                ins,
                [IN_VMEM] * len(ins),
                [block_out, *piece_outs],
                [IN_VMEM] * (1 + pieces),
                flops=10**9,
                name="finish",
            )
        else:
            ins = [acc, low, high, dense, row_wide, *received, krylov]
            (krylov,) = call(
                functools.partial(last_kernel, per_device, index, pieces),
                ins,
                [IN_VMEM] * (len(ins) - 1) + [ANYWHERE],
                [krylov_out],
                [ANYWHERE],
                [pltpu.VMEM((rhs, shard_len), BF16), pltpu.SemaphoreType.DMA],
                {len(ins) - 1: 0},
                flops=10**9,
                name="last",
            )
    return krylov


def solution(mesh):
    split = ("groups", "loop", "far")
    in_specs = (
        P(None, split),
        P(split, None, None),
        P(split),
        P(split),
        P(split, None, None),
        P(split, None, None),
        P(split),
        P(split),
        P(split, None, None),
    )
    return jax.shard_map(
        on_device, mesh=mesh, in_specs=in_specs, out_specs=P(None, None, split), check_vma=False
    )
```

time: 247 us -> 77.1 us (0.31)
  waiting for transfers between devices: 150 us -> 22.9 us
  matrix products: 30.4 us -> 0 us
  Pallas kernels: 0 us -> 17.5 us
  between operations: 14.3 us -> 0.18 us
  starting transfers between devices: 35.4 us -> 26.9 us
  local copies, waits for them, and re-layouts: 14.3 us -> 9.27 us
    unnamed x8 -> x0, waiting for transfers between devices: 127 us -> none
    dot_general x24 -> x0, matrix products: 30.4 us -> none  [the longest x4 14.3 us: on_device(): jnp.einsum('esq,spq->sep', chosen, near_tiles, preferred_element_type=jnp...]
    pallas_call x0 -> x9, Pallas kernels: none -> 17.5 us  [call(): pl.pallas_call(kernel, in_specs=list(specs), out_specs=list(out_specs), o...]
    unnamed x20, local copies, waits for them, and re-layouts: 0.68 us -> 9.27 us
    ppermute x20 -> x24, starting transfers between devices: 35.3 us -> 26.9 us  [the longest x4 17.1 us: on_device(): high = lax.ppermute(current, both_axes, back)]
    gather x8 -> x0, local copies, waits for them, and re-layouts: 4.88 us -> none  [the longest x4 2.46 us: on_device(): chosen = jnp.take(panels, window_pos, axis=1)]
    reshape x8 -> x0, local copies, waits for them, and re-layouts: 4.79 us -> none  [the longest x4 4.67 us: on_device(): partial_value.reshape(level_count, block_clusters, rank_size, rhs_count)]
    squeeze x4 -> x0, local copies, waits for them, and re-layouts: 3.66 us -> none  [on_device(): summed[level]]
  transfers between devices with their start and end apart: 24 -> 24, of which waited for: 19 -> 9; matrix products, arithmetic and copies ran while one was open for 13% -> 0% of each run, Pallas kernels for 0% -> 15%
where the time goes in v1:
time: 77.1 us; the launch traced here: 76.8 us
  starting transfers between devices  26.9 us (35%)
  waiting for transfers between devices  22.9 us (30%)
  Pallas kernels  17.5 us (23%)
  local copies, waits for them, and re-layouts  9.27 us (12%)
    ppermute x16, waiting for transfers between devices, on_device(): lax.ppermute(s, both_axes, route)  22.9 us
    pallas_call x9, Pallas kernels, call(): pl.pallas_call(kernel, in_specs=list(specs), out_specs=list(out_specs), o...  17.5 us
    ppermute x4, starting transfers between devices, on_device(): high = lax.ppermute(current, both_axes, back)  17.1 us
    unnamed x20, local copies, waits for them, and re-layouts  9.27 us
    ppermute x16, starting transfers between devices, on_device(): lax.ppermute(s, both_axes, route)  8.04 us
    ppermute x4, starting transfers between devices, on_device(): low = lax.ppermute(current, both_axes, ring)  1.75 us
  transfers between devices with their start and end apart: 24, of which 9 were waited for; matrix products, arithmetic and copies ran while one was open for 0% of the time, Pallas kernels for 15%

profile of v1, /device:TPU:0, one launch (start us, length us, event | category | flops | bytes accessed | tf_op | source)
XLA Modules:
  0.0 76.8 jit_solution(18331871277348960128)
XLA Ops:
  0.0 0.5 collective-permute-start
  0.5 5.0 %collective-permute-start.1 = (bf16[64,1024]{1,0:T(8,128)(2,1)}, bf16[64,1024]{1,0:T(8,128)(2,1)S(1)}, u32[]{:S(2)}, u32[]{:S(2)}) collective-permute-start(bf16[64,1024]{1,0:T(8,128)(2,1)} %x_ref.3), channel_id=1, source_target_pairs={{1,0},{2,1},{3,2},{4,3},{5,4},{6,5},{7,6},{8,7},{9,8},{10,9},{11,1... | collective-permute-start | bytes 393224 | tf_op jit(solution)/shard_map/ppermute | solution.py:210
  5.4 0.9 %copy-done.1 = bf16[64,1024]{1,0:T(8,128)(2,1)S(1)} copy-done((bf16[64,1024]{1,0:T(8,128)(2,1)S(1)}, bf16[64,1024]{1,0:T(8,128)(2,1)}, u32[]{:S(2)}) %copy-start.1) | copy-done | bytes 131096
  6.4 0.9 %copy-done.3 = bf16[32,32,32]{2,1,0:T(8,128)(2,1)S(1)} copy-done((bf16[32,32,32]{2,1,0:T(8,128)(2,1)S(1)}, bf16[32,32,32]{2,1,0:T(8,128)(2,1)}, u32[]{:S(2)}) %copy-start.3) | copy-done | bytes 65560
  7.3 0.8 %copy-done.4 = bf16[4,32,256]{2,1,0:T(8,128)(2,1)S(1)} copy-done((bf16[4,32,256]{2,1,0:T(8,128)(2,1)S(1)}, bf16[4,32,256]{2,1,0:T(8,128)(2,1)}, u32[]{:S(2)}) %copy-start.4) | copy-done | bytes 65560
  8.2 0.8 %copy-done.5 = bf16[4,32,256]{2,1,0:T(8,128)(2,1)S(1)} copy-done((bf16[4,32,256]{2,1,0:T(8,128)(2,1)S(1)}, bf16[4,32,256]{2,1,0:T(8,128)(2,1)}, u32[]{:S(2)}) %copy-start.5) | copy-done | bytes 65560
  9.0 0.7 copy-done.6
  9.6 0.7 copy-done.7
  10.3 1.4 %prepare.1 = (bf16[3,512,128]{2,1,0:T(8,128)(2,1)S(1)}, bf16[128,1024]{1,0:T(8,128)(2,1)S(1)}, bf16[256,1024]{1,0:T(8,128)(2,1)S(1)}, bf16[64,128]{1,0:T(8,128)(...) custom-call(s32[32]{0:T(128)S(1)} %copy-done.6, s32[32]{0:T(128)S(1)} %copy-done.7, ...), custom_call_target="tpu_custom_call" | custom-call | flops 100000000 | bytes 4194304 | tf_op jit(solution)/shard_map/prepare/pallas_call | solution.py:184
  11.7 1.3 %collective-permute-start.2 = (bf16[64,128]{1,0:T(8,128)(2,1)S(1)}, bf16[64,128]{1,0:T(8,128)(2,1)S(1)}, u32[]{:S(2)}, u32[]{:S(2)}) collective-permute-start(bf16[64,128]{1,0:T(8,128)(2,1)S(1)} %get-tuple-element.40), channel_id=1, source_target_pairs={{0,8},{1,9},{2,10},{3,11},{4,12},{5,13},{6,14},{7,15},{8,0},{9,1},... | collective-permute-start | bytes 49160 | tf_op jit(solution)/shard_map/ppermute | solution.py:227
  13.1 0.0 collective-permute-start.3
  13.1 2.2 %collective-permute-start.4 = (bf16[64,128]{1,0:T(8,128)(2,1)S(1)}, bf16[64,128]{1,0:T(8,128)(2,1)S(1)}, u32[]{:S(2)}, u32[]{:S(2)}) collective-permute-start(bf16[64,128]{1,0:T(8,128)(2,1)S(1)} %get-tuple-element.42), channel_id=1, source_target_pairs={{0,10},{1,11},{2,8},{3,9},{4,14},{5,15},{6,12},{7,13},{8,2},{9,3},... | collective-permute-start | bytes 49160 | tf_op jit(solution)/shard_map/ppermute | solution.py:227
  15.3 1.2 %collective-permute-done.2.refs_7_ = bf16[64,128]{1,0:T(8,128)(2,1)S(1)} collective-permute-done((bf16[64,128]{1,0:T(8,128)(2,1)S(1)}, bf16[64,128]{1,0:T(8,128)(2,1)S(1)}, u32[]{:S(2)}, u32[]{:S(2)}) %collective-permute-start.2) | collective-permute-done | bytes 16416 | tf_op jit(solution)/shard_map/ppermute | solution.py:227
  16.4 0.3 collective-permute-start.5
  16.7 2.2 %copy-done = bf16[32,256,256]{2,1,0:T(8,128)(2,1)S(1)} copy-done((bf16[32,256,256]{2,1,0:T(8,128)(2,1)S(1)}, bf16[32,256,256]{2,1,0:T(8,128)(2,1)}, u32[]{:S(2)}) %copy-start) | copy-done | bytes 4194328
  18.9 0.9 %copy-done.2 = bf16[64,1024]{1,0:T(8,128)(2,1)S(1)} copy-done((bf16[64,1024]{1,0:T(8,128)(2,1)S(1)}, bf16[64,1024]{1,0:T(8,128)(2,1)}, u32[]{:S(2)}) %copy-start.2) | copy-done | bytes 131096
  19.8 0.7 copy-done.8
  20.4 0.7 copy-done.9
  21.1 7.7 %first_own.1 = (bf16[36,256,256]{2,1,0:T(8,128)(2,1)S(1)}, f32[64,1024]{1,0:T(8,128)S(1)}) custom-call(s32[32]{0:T(128)S(1)} %copy-done.8, s32[32]{0:T(128)S(1)} %copy-done.9, bf16[64,1024]{1,0:T(8,128)(2,1)S(1)} %copy-done.2, bf16[32,256,256]{2,1,0:T(8,128)(2,1)S(1)} %copy-done), custom_call_target="tpu_custom_call" | custom-call | flops 1000000000 | bytes 4194304 | tf_op jit(solution)/shard_map/first_own/pallas_call | solution.py:184
  28.8 0.0 collective-permute-done.3.refs_8_
  28.8 0.0 collective-permute-done.4.refs_9_
  28.9 0.0 collective-permute-done.5.refs_10_
  28.9 0.0 collective-permute-done.refs_1_
  28.9 0.0 collective-permute-done.1.refs_2_
  28.9 1.5 %finish.3 = (bf16[64,1024]{1,0:T(8,128)(2,1)S(1)}, bf16[64,128]{1,0:T(8,128)(2,1)S(1)}, bf16[64,128]{1,0:T(8,128)(2,1)S(1)}, bf16[64,128]{1,0:T(8,128)(2,1)S(1)}, bf16[64,128]{1,0:T(8,128)(2,1)S(1)}) custom-call(f32[64,1024]{1,0:T(8,128)S(1)} %get-tuple-element.35.refs_0_, bf16[64,1024]{1,0:T(8,128)(2,1)S(1)} %collective-permute-done.refs_1_, ...), custom_call_target="tpu_custom_call" | custom-call | flops 1000000000 | bytes 4194304 | tf_op jit(solution)/shard_map/finish/pallas_call | solution.py:184
  30.4 1.2 %collective-permute-start.6 = (bf16[64,1024]{1,0:T(8,128)(2,1)S(1)}, bf16[64,1024]{1,0:T(8,128)(2,1)S(1)}, u32[]{:S(2)}, u32[]{:S(2)}) collective-permute-start(bf16[64,1024]{1,0:T(8,128)(2,1)S(1)} %get-tuple-element.44.x_ref), channel_id=1, source_target_pairs={{0,1},{1,2},{2,3},{3,4},{4,5},{5,6},{6,7},{7,8},{8,9},{9,10},{10,1... | collective-permute-start | bytes 393224 | tf_op jit(solution)/shard_map/ppermute | solution.py:209
  31.5 3.3 %collective-permute-start.7 = (bf16[64,1024]{1,0:T(8,128)(2,1)S(1)}, bf16[64,1024]{1,0:T(8,128)(2,1)S(1)}, u32[]{:S(2)}, u32[]{:S(2)}) collective-permute-start(bf16[64,1024]{1,0:T(8,128)(2,1)S(1)} %get-tuple-element.44.x_ref), channel_id=1, source_target_pairs={{1,0},{2,1},{3,2},{4,3},{5,4},{6,5},{7,6},{8,7},{9,8},{10,9},{11,1... | collective-permute-start | bytes 393224 | tf_op jit(solution)/shard_map/ppermute | solution.py:210
  34.8 0.8 collective-permute-start.10
  35.6 0.8 %collective-permute-start.11 = (bf16[64,128]{1,0:T(8,128)(2,1)S(1)}, bf16[64,128]{1,0:T(8,128)(2,1)S(1)}, u32[]{:S(2)}, u32[]{:S(2)}) collective-permute-start(bf16[64,128]{1,0:T(8,128)(2,1)S(1)} %get-tuple-element.49), channel_id=1, source_target_pairs={{0,11},{1,8},{2,9},{3,10},{4,15},{5,12},{6,13},{7,14},{8,3},{9,0},... | collective-permute-start | bytes 49160 | tf_op jit(solution)/shard_map/ppermute | solution.py:227
  36.4 1.3 %collective-permute-start.8 = (bf16[64,128]{1,0:T(8,128)(2,1)S(1)}, bf16[64,128]{1,0:T(8,128)(2,1)S(1)}, u32[]{:S(2)}, u32[]{:S(2)}) collective-permute-start(bf16[64,128]{1,0:T(8,128)(2,1)S(1)} %get-tuple-element.46), channel_id=1, source_target_pairs={{0,8},{1,9},{2,10},{3,11},{4,12},{5,13},{6,14},{7,15},{8,0},{9,1},... | collective-permute-start | bytes 49160 | tf_op jit(solution)/shard_map/ppermute | solution.py:227
  37.7 2.9 %collective-permute-done.10.refs_9_ = bf16[64,128]{1,0:T(8,128)(2,1)S(1)} collective-permute-done((bf16[64,128]{1,0:T(8,128)(2,1)S(1)}, bf16[64,128]{1,0:T(8,128)(2,1)S(1)}, u32[]{:S(2)}, u32[]{:S(2)}) %collective-permute-start.10) | collective-permute-done | bytes 16416 | tf_op jit(solution)/shard_map/ppermute | solution.py:227
  40.6 0.0 collective-permute-start.9
  40.6 0.8 own.3
  41.3 0.0 collective-permute-done.11.refs_10_
  41.3 0.1 collective-permute-done.8.refs_7_
  41.4 4.1 %collective-permute-done.9.refs_8_ = bf16[64,128]{1,0:T(8,128)(2,1)S(1)} collective-permute-done((bf16[64,128]{1,0:T(8,128)(2,1)S(1)}, bf16[64,128]{1,0:T(8,128)(2,1)S(1)}, u32[]{:S(2)}, u32[]{:S(2)}) %collective-permute-start.9) | collective-permute-done | bytes 16416 | tf_op jit(solution)/shard_map/ppermute | solution.py:227
  45.5 0.0 collective-permute-done.6.refs_1_
  45.5 0.0 collective-permute-done.7.refs_2_
  45.5 1.5 %finish.4 = (bf16[64,1024]{1,0:T(8,128)(2,1)S(1)}, bf16[64,128]{1,0:T(8,128)(2,1)S(1)}, bf16[64,128]{1,0:T(8,128)(2,1)S(1)}, bf16[64,128]{1,0:T(8,128)(2,1)S(1)}, bf16[64,128]{1,0:T(8,128)(2,1)S(1)}) custom-call(f32[64,1024]{1,0:T(8,128)S(1)} %get-tuple-element.45.refs_0_, bf16[64,1024]{1,0:T(8,128)(2,1)S(1)} %collective-permute-done.6.refs_1_, ...), custom_call_target="tpu_custom_call" | custom-call | flops 1000000000 | bytes 4194304 | tf_op jit(solution)/shard_map/finish/pallas_call | solution.py:184
  47.0 0.1 collective-permute-start.12
  47.0 4.4 %collective-permute-start.13 = (bf16[64,1024]{1,0:T(8,128)(2,1)S(1)}, bf16[64,1024]{1,0:T(8,128)(2,1)S(1)}, u32[]{:S(2)}, u32[]{:S(2)}) collective-permute-start(bf16[64,1024]{1,0:T(8,128)(2,1)S(1)} %get-tuple-element.50.x_ref), channel_id=1, source_target_pairs={{1,0},{2,1},{3,2},{4,3},{5,4},{6,5},{7,6},{8,7},{9,8},{10,9},{11,1... | collective-permute-start | bytes 393224 | tf_op jit(solution)/shard_map/ppermute | solution.py:210
  51.5 0.0 collective-permute-start.14
  51.5 0.0 collective-permute-start.15
  51.5 1.3 %collective-permute-start.16 = (bf16[64,128]{1,0:T(8,128)(2,1)S(1)}, bf16[64,128]{1,0:T(8,128)(2,1)S(1)}, u32[]{:S(2)}, u32[]{:S(2)}) collective-permute-start(bf16[64,128]{1,0:T(8,128)(2,1)S(1)} %get-tuple-element.55), channel_id=1, source_target_pairs={{0,10},{1,11},{2,8},{3,9},{4,14},{5,15},{6,12},{7,13},{8,2},{9,3},... | collective-permute-start | bytes 49160 | tf_op jit(solution)/shard_map/ppermute | solution.py:227
  52.8 3.3 %collective-permute-done.14.refs_7_ = bf16[64,128]{1,0:T(8,128)(2,1)S(1)} collective-permute-done((bf16[64,128]{1,0:T(8,128)(2,1)S(1)}, bf16[64,128]{1,0:T(8,128)(2,1)S(1)}, u32[]{:S(2)}, u32[]{:S(2)}) %collective-permute-start.14) | collective-permute-done | bytes 16416 | tf_op jit(solution)/shard_map/ppermute | solution.py:227
  56.1 0.0 collective-permute-start.17
  56.1 0.8 own.4
  56.9 0.0 collective-permute-done.15.refs_8_
  56.9 0.4 collective-permute-done.16.refs_9_
  57.3 2.9 %collective-permute-done.17.refs_10_ = bf16[64,128]{1,0:T(8,128)(2,1)S(1)} collective-permute-done((bf16[64,128]{1,0:T(8,128)(2,1)S(1)}, bf16[64,128]{1,0:T(8,128)(2,1)S(1)}, u32[]{:S(2)}, u32[]{:S(2)}) %collective-permute-start.17) | collective-permute-done | bytes 16416 | tf_op jit(solution)/shard_map/ppermute | solution.py:227
  60.2 0.0 collective-permute-done.12.refs_1_
  60.2 1.5 %finish.5 = (bf16[64,1024]{1,0:T(8,128)(2,1)S(1)}, bf16[64,128]{1,0:T(8,128)(2,1)S(1)}, bf16[64,128]{1,0:T(8,128)(2,1)S(1)}, bf16[64,128]{1,0:T(8,128)(2,1)S(1)}, bf16[64,128]{1,0:T(8,128)(2,1)S(1)}) custom-call(f32[64,1024]{1,0:T(8,128)S(1)} %get-tuple-element.52.refs_0_, bf16[64,1024]{1,0:T(8,128)(2,1)S(1)} %collective-permute-done.12.refs_1_, ...), custom_call_target="tpu_custom_call" | custom-call | flops 1000000000 | bytes 4194304 | tf_op jit(solution)/shard_map/finish/pallas_call | solution.py:184
  61.7 0.1 collective-permute-start.18
  61.7 4.4 %collective-permute-start.19 = (bf16[64,1024]{1,0:T(8,128)(2,1)S(1)}, bf16[64,1024]{1,0:T(8,128)(2,1)S(1)}, u32[]{:S(2)}, u32[]{:S(2)}) collective-permute-start(bf16[64,1024]{1,0:T(8,128)(2,1)S(1)} %get-tuple-element.57.x_ref), channel_id=1, source_target_pairs={{1,0},{2,1},{3,2},{4,3},{5,4},{6,5},{7,6},{8,7},{9,8},{10,9},{11,1... | collective-permute-start | bytes 393224 | tf_op jit(solution)/shard_map/ppermute | solution.py:210
  66.1 0.0 collective-permute-start.20
  66.2 0.0 collective-permute-start.21
  66.2 0.1 collective-permute-start.22
  66.2 4.8 %collective-permute-done.20.refs_5_ = bf16[64,128]{1,0:T(8,128)(2,1)S(1)} collective-permute-done((bf16[64,128]{1,0:T(8,128)(2,1)S(1)}, bf16[64,128]{1,0:T(8,128)(2,1)S(1)}, u32[]{:S(2)}, u32[]{:S(2)}) %collective-permute-start.20) | collective-permute-done | bytes 16416 | tf_op jit(solution)/shard_map/ppermute | solution.py:227
  71.0 0.0 collective-permute-start.23
  71.0 0.8 own.5
  71.8 0.0 collective-permute-done.22.refs_7_
  71.8 3.3 %collective-permute-done.23.refs_8_ = bf16[64,128]{1,0:T(8,128)(2,1)S(1)} collective-permute-done((bf16[64,128]{1,0:T(8,128)(2,1)S(1)}, bf16[64,128]{1,0:T(8,128)(2,1)S(1)}, u32[]{:S(2)}, u32[]{:S(2)}) %collective-permute-start.23) | collective-permute-done | bytes 16416 | tf_op jit(solution)/shard_map/ppermute | solution.py:227
  75.1 0.0 collective-permute-done.19.refs_2_
  75.1 1.7 %last.1 = bf16[4,64,1024]{2,1,0:T(8,128)(2,1)} custom-call(f32[64,1024]{1,0:T(8,128)S(1)} %get-tuple-element.59.refs_0_, bf16[64,1024]{1,0:T(8,128)(2,1)S(1)} %collective-permute-done.18.refs_1_, bf16[64,1024]{1,0:T(8,128)(2,1)S(1)} %collective-permute-done.19.refs_2_, ...), custom_call_target="tpu_custom_call", output_to_operand_aliasing={{}: (9, {})} | custom-call | flops 1000000000 | bytes 4194304 | tf_op jit(solution)/shard_map/last/pallas_call | solution.py:184
  (13 shorter events, 0.0 us)
Async XLA Ops:
  0.0 28.9 %collective-permute-start = (bf16[64,1024]{1,0:T(8,128)(2,1)}, bf16[64,1024]{1,0:T(8,128)(2,1)S(1)}, u32[]{:S(2)}, u32[]{:S(2)}) collective-permute-start(bf16[64,1024]{1,0:T(8,128)(2,1)} %x_ref.3), channel_id=1, source_target_pairs={{0,1},{1,2},{2,3},{3,4},{4,5},{5,6},{6,7},{7,8},{8,9},{9,10},{10,1... | collective-permute-start | bytes 393224 | tf_op jit(solution)/shard_map/ppermute | solution.py:209
  0.5 28.4 %collective-permute-start.1 = (bf16[64,1024]{1,0:T(8,128)(2,1)}, bf16[64,1024]{1,0:T(8,128)(2,1)S(1)}, u32[]{:S(2)}, u32[]{:S(2)}) collective-permute-start(bf16[64,1024]{1,0:T(8,128)(2,1)} %x_ref.3), channel_id=1, source_target_pairs={{1,0},{2,1},{3,2},{4,3},{5,4},{6,5},{7,6},{8,7},{9,8},{10,9},{11,1... | collective-permute-start | bytes 393224 | tf_op jit(solution)/shard_map/ppermute | solution.py:210
  5.4 0.9 %copy-start.1 = (bf16[64,1024]{1,0:T(8,128)(2,1)S(1)}, bf16[64,1024]{1,0:T(8,128)(2,1)}, u32[]{:S(2)}) copy-start(bf16[64,1024]{1,0:T(8,128)(2,1)} %x_ref.3) | copy-start | bytes 393220
  6.4 0.9 %copy-start.3 = (bf16[32,32,32]{2,1,0:T(8,128)(2,1)S(1)}, bf16[32,32,32]{2,1,0:T(8,128)(2,1)}, u32[]{:S(2)}) copy-start(bf16[32,32,32]{2,1,0:T(8,128)(2,1)} %coup_ref.1) | copy-start | bytes 196612
  7.3 0.8 %copy-start.4 = (bf16[4,32,256]{2,1,0:T(8,128)(2,1)S(1)}, bf16[4,32,256]{2,1,0:T(8,128)(2,1)}, u32[]{:S(2)}) copy-start(bf16[4,32,256]{2,1,0:T(8,128)(2,1)} %col_ref.1) | copy-start | bytes 196612
  8.1 0.8 %copy-start.5 = (bf16[4,32,256]{2,1,0:T(8,128)(2,1)S(1)}, bf16[4,32,256]{2,1,0:T(8,128)(2,1)}, u32[]{:S(2)}) copy-start(bf16[4,32,256]{2,1,0:T(8,128)(2,1)} %row_ref.1) | copy-start | bytes 196612
  9.0 0.7 copy-start.6
  9.6 0.7 copy-start.7
  11.7 4.7 %collective-permute-start.2 = (bf16[64,128]{1,0:T(8,128)(2,1)S(1)}, bf16[64,128]{1,0:T(8,128)(2,1)S(1)}, u32[]{:S(2)}, u32[]{:S(2)}) collective-permute-start(bf16[64,128]{1,0:T(8,128)(2,1)S(1)} %get-tuple-element.40), channel_id=1, source_target_pairs={{0,8},{1,9},{2,10},{3,11},{4,12},{5,13},{6,14},{7,15},{8,0},{9,1},... | collective-permute-start | bytes 49160 | tf_op jit(solution)/shard_map/ppermute | solution.py:227
  13.1 15.8 %collective-permute-start.3 = (bf16[64,128]{1,0:T(8,128)(2,1)S(1)}, bf16[64,128]{1,0:T(8,128)(2,1)S(1)}, u32[]{:S(2)}, u32[]{:S(2)}) collective-permute-start(bf16[64,128]{1,0:T(8,128)(2,1)S(1)} %get-tuple-element.41), channel_id=1, source_target_pairs={{0,9},{1,10},{2,11},{3,8},{4,13},{5,14},{6,15},{7,12},{8,1},{9,2},... | collective-permute-start | bytes 49160 | tf_op jit(solution)/shard_map/ppermute | solution.py:227
  13.1 15.8 %collective-permute-start.4 = (bf16[64,128]{1,0:T(8,128)(2,1)S(1)}, bf16[64,128]{1,0:T(8,128)(2,1)S(1)}, u32[]{:S(2)}, u32[]{:S(2)}) collective-permute-start(bf16[64,128]{1,0:T(8,128)(2,1)S(1)} %get-tuple-element.42), channel_id=1, source_target_pairs={{0,10},{1,11},{2,8},{3,9},{4,14},{5,15},{6,12},{7,13},{8,2},{9,3},... | collective-permute-start | bytes 49160 | tf_op jit(solution)/shard_map/ppermute | solution.py:227
  16.4 12.4 %collective-permute-start.5 = (bf16[64,128]{1,0:T(8,128)(2,1)S(1)}, bf16[64,128]{1,0:T(8,128)(2,1)S(1)}, u32[]{:S(2)}, u32[]{:S(2)}) collective-permute-start(bf16[64,128]{1,0:T(8,128)(2,1)S(1)} %get-tuple-element.43), channel_id=1, source_target_pairs={{0,11},{1,8},{2,9},{3,10},{4,15},{5,12},{6,13},{7,14},{8,3},{9,0},... | collective-permute-start | bytes 49160 | tf_op jit(solution)/shard_map/ppermute | solution.py:227
  16.7 2.2 %copy-start = (bf16[32,256,256]{2,1,0:T(8,128)(2,1)S(1)}, bf16[32,256,256]{2,1,0:T(8,128)(2,1)}, u32[]{:S(2)}) copy-start(bf16[32,256,256]{2,1,0:T(8,128)(2,1)} %tiles_ref.1) | copy-start | bytes 12582916
  18.9 0.9 %copy-start.2 = (bf16[64,1024]{1,0:T(8,128)(2,1)S(1)}, bf16[64,1024]{1,0:T(8,128)(2,1)}, u32[]{:S(2)}) copy-start(bf16[64,1024]{1,0:T(8,128)(2,1)} %x_ref.3) | copy-start | bytes 393220
  19.8 0.7 copy-start.8
  20.4 0.7 copy-start.9
  30.4 15.2 %collective-permute-start.6 = (bf16[64,1024]{1,0:T(8,128)(2,1)S(1)}, bf16[64,1024]{1,0:T(8,128)(2,1)S(1)}, u32[]{:S(2)}, u32[]{:S(2)}) collective-permute-start(bf16[64,1024]{1,0:T(8,128)(2,1)S(1)} %get-tuple-element.44.x_ref), channel_id=1, source_target_pairs={{0,1},{1,2},{2,3},{3,4},{4,5},{5,6},{6,7},{7,8},{8,9},{9,10},{10,1... | collective-permute-start | bytes 393224 | tf_op jit(solution)/shard_map/ppermute | solution.py:209
  31.5 14.0 %collective-permute-start.7 = (bf16[64,1024]{1,0:T(8,128)(2,1)S(1)}, bf16[64,1024]{1,0:T(8,128)(2,1)S(1)}, u32[]{:S(2)}, u32[]{:S(2)}) collective-permute-start(bf16[64,1024]{1,0:T(8,128)(2,1)S(1)} %get-tuple-element.44.x_ref), channel_id=1, source_target_pairs={{1,0},{2,1},{3,2},{4,3},{5,4},{6,5},{7,6},{8,7},{9,8},{10,9},{11,1... | collective-permute-start | bytes 393224 | tf_op jit(solution)/shard_map/ppermute | solution.py:210
  34.8 5.7 %collective-permute-start.10 = (bf16[64,128]{1,0:T(8,128)(2,1)S(1)}, bf16[64,128]{1,0:T(8,128)(2,1)S(1)}, u32[]{:S(2)}, u32[]{:S(2)}) collective-permute-start(bf16[64,128]{1,0:T(8,128)(2,1)S(1)} %get-tuple-element.48), channel_id=1, source_target_pairs={{0,10},{1,11},{2,8},{3,9},{4,14},{5,15},{6,12},{7,13},{8,2},{9,3},... | collective-permute-start | bytes 49160 | tf_op jit(solution)/shard_map/ppermute | solution.py:227
  35.6 5.7 %collective-permute-start.11 = (bf16[64,128]{1,0:T(8,128)(2,1)S(1)}, bf16[64,128]{1,0:T(8,128)(2,1)S(1)}, u32[]{:S(2)}, u32[]{:S(2)}) collective-permute-start(bf16[64,128]{1,0:T(8,128)(2,1)S(1)} %get-tuple-element.49), channel_id=1, source_target_pairs={{0,11},{1,8},{2,9},{3,10},{4,15},{5,12},{6,13},{7,14},{8,3},{9,0},... | collective-permute-start | bytes 49160 | tf_op jit(solution)/shard_map/ppermute | solution.py:227
  36.4 5.0 %collective-permute-start.8 = (bf16[64,128]{1,0:T(8,128)(2,1)S(1)}, bf16[64,128]{1,0:T(8,128)(2,1)S(1)}, u32[]{:S(2)}, u32[]{:S(2)}) collective-permute-start(bf16[64,128]{1,0:T(8,128)(2,1)S(1)} %get-tuple-element.46), channel_id=1, source_target_pairs={{0,8},{1,9},{2,10},{3,11},{4,12},{5,13},{6,14},{7,15},{8,0},{9,1},... | collective-permute-start | bytes 49160 | tf_op jit(solution)/shard_map/ppermute | solution.py:227
  40.6 5.0 %collective-permute-start.9 = (bf16[64,128]{1,0:T(8,128)(2,1)S(1)}, bf16[64,128]{1,0:T(8,128)(2,1)S(1)}, u32[]{:S(2)}, u32[]{:S(2)}) collective-permute-start(bf16[64,128]{1,0:T(8,128)(2,1)S(1)} %get-tuple-element.47), channel_id=1, source_target_pairs={{0,9},{1,10},{2,11},{3,8},{4,13},{5,14},{6,15},{7,12},{8,1},{9,2},... | collective-permute-start | bytes 49160 | tf_op jit(solution)/shard_map/ppermute | solution.py:227
  47.0 13.2 %collective-permute-start.12 = (bf16[64,1024]{1,0:T(8,128)(2,1)S(1)}, bf16[64,1024]{1,0:T(8,128)(2,1)S(1)}, u32[]{:S(2)}, u32[]{:S(2)}) collective-permute-start(bf16[64,1024]{1,0:T(8,128)(2,1)S(1)} %get-tuple-element.50.x_ref), channel_id=1, source_target_pairs={{0,1},{1,2},{2,3},{3,4},{4,5},{5,6},{6,7},{7,8},{8,9},{9,10},{10,1... | collective-permute-start | bytes 393224 | tf_op jit(solution)/shard_map/ppermute | solution.py:209
  47.0 13.1 %collective-permute-start.13 = (bf16[64,1024]{1,0:T(8,128)(2,1)S(1)}, bf16[64,1024]{1,0:T(8,128)(2,1)S(1)}, u32[]{:S(2)}, u32[]{:S(2)}) collective-permute-start(bf16[64,1024]{1,0:T(8,128)(2,1)S(1)} %get-tuple-element.50.x_ref), channel_id=1, source_target_pairs={{1,0},{2,1},{3,2},{4,3},{5,4},{6,5},{7,6},{8,7},{9,8},{10,9},{11,1... | collective-permute-start | bytes 393224 | tf_op jit(solution)/shard_map/ppermute | solution.py:210
  51.5 4.6 %collective-permute-start.14 = (bf16[64,128]{1,0:T(8,128)(2,1)S(1)}, bf16[64,128]{1,0:T(8,128)(2,1)S(1)}, u32[]{:S(2)}, u32[]{:S(2)}) collective-permute-start(bf16[64,128]{1,0:T(8,128)(2,1)S(1)} %get-tuple-element.53), channel_id=1, source_target_pairs={{0,8},{1,9},{2,10},{3,11},{4,12},{5,13},{6,14},{7,15},{8,0},{9,1},... | collective-permute-start | bytes 49160 | tf_op jit(solution)/shard_map/ppermute | solution.py:227
  51.5 5.4 %collective-permute-start.15 = (bf16[64,128]{1,0:T(8,128)(2,1)S(1)}, bf16[64,128]{1,0:T(8,128)(2,1)S(1)}, u32[]{:S(2)}, u32[]{:S(2)}) collective-permute-start(bf16[64,128]{1,0:T(8,128)(2,1)S(1)} %get-tuple-element.54), channel_id=1, source_target_pairs={{0,9},{1,10},{2,11},{3,8},{4,13},{5,14},{6,15},{7,12},{8,1},{9,2},... | collective-permute-start | bytes 49160 | tf_op jit(solution)/shard_map/ppermute | solution.py:227
  51.5 5.8 %collective-permute-start.16 = (bf16[64,128]{1,0:T(8,128)(2,1)S(1)}, bf16[64,128]{1,0:T(8,128)(2,1)S(1)}, u32[]{:S(2)}, u32[]{:S(2)}) collective-permute-start(bf16[64,128]{1,0:T(8,128)(2,1)S(1)} %get-tuple-element.55), channel_id=1, source_target_pairs={{0,10},{1,11},{2,8},{3,9},{4,14},{5,15},{6,12},{7,13},{8,2},{9,3},... | collective-permute-start | bytes 49160 | tf_op jit(solution)/shard_map/ppermute | solution.py:227
  56.1 4.1 %collective-permute-start.17 = (bf16[64,128]{1,0:T(8,128)(2,1)S(1)}, bf16[64,128]{1,0:T(8,128)(2,1)S(1)}, u32[]{:S(2)}, u32[]{:S(2)}) collective-permute-start(bf16[64,128]{1,0:T(8,128)(2,1)S(1)} %get-tuple-element.56), channel_id=1, source_target_pairs={{0,11},{1,8},{2,9},{3,10},{4,15},{5,12},{6,13},{7,14},{8,3},{9,0},... | collective-permute-start | bytes 49160 | tf_op jit(solution)/shard_map/ppermute | solution.py:227
  61.7 13.5 %collective-permute-start.18 = (bf16[64,1024]{1,0:T(8,128)(2,1)S(1)}, bf16[64,1024]{1,0:T(8,128)(2,1)S(1)}, u32[]{:S(2)}, u32[]{:S(2)}) collective-permute-start(bf16[64,1024]{1,0:T(8,128)(2,1)S(1)} %get-tuple-element.57.x_ref), channel_id=1, source_target_pairs={{0,1},{1,2},{2,3},{3,4},{4,5},{5,6},{6,7},{7,8},{8,9},{9,10},{10,1... | collective-permute-start | bytes 393224 | tf_op jit(solution)/shard_map/ppermute | solution.py:209
  61.7 13.4 %collective-permute-start.19 = (bf16[64,1024]{1,0:T(8,128)(2,1)S(1)}, bf16[64,1024]{1,0:T(8,128)(2,1)S(1)}, u32[]{:S(2)}, u32[]{:S(2)}) collective-permute-start(bf16[64,1024]{1,0:T(8,128)(2,1)S(1)} %get-tuple-element.57.x_ref), channel_id=1, source_target_pairs={{1,0},{2,1},{3,2},{4,3},{5,4},{6,5},{7,6},{8,7},{9,8},{10,9},{11,1... | collective-permute-start | bytes 393224 | tf_op jit(solution)/shard_map/ppermute | solution.py:210
  66.1 4.9 %collective-permute-start.20 = (bf16[64,128]{1,0:T(8,128)(2,1)S(1)}, bf16[64,128]{1,0:T(8,128)(2,1)S(1)}, u32[]{:S(2)}, u32[]{:S(2)}) collective-permute-start(bf16[64,128]{1,0:T(8,128)(2,1)S(1)} %get-tuple-element.60), channel_id=1, source_target_pairs={{0,8},{1,9},{2,10},{3,11},{4,12},{5,13},{6,14},{7,15},{8,0},{9,1},... | collective-permute-start | bytes 49160 | tf_op jit(solution)/shard_map/ppermute | solution.py:227
  66.2 5.7 %collective-permute-start.21 = (bf16[64,128]{1,0:T(8,128)(2,1)S(1)}, bf16[64,128]{1,0:T(8,128)(2,1)S(1)}, u32[]{:S(2)}, u32[]{:S(2)}) collective-permute-start(bf16[64,128]{1,0:T(8,128)(2,1)S(1)} %get-tuple-element.61), channel_id=1, source_target_pairs={{0,9},{1,10},{2,11},{3,8},{4,13},{5,14},{6,15},{7,12},{8,1},{9,2},... | collective-permute-start | bytes 49160 | tf_op jit(solution)/shard_map/ppermute | solution.py:227
  66.2 5.7 %collective-permute-start.22 = (bf16[64,128]{1,0:T(8,128)(2,1)S(1)}, bf16[64,128]{1,0:T(8,128)(2,1)S(1)}, u32[]{:S(2)}, u32[]{:S(2)}) collective-permute-start(bf16[64,128]{1,0:T(8,128)(2,1)S(1)} %get-tuple-element.62), channel_id=1, source_target_pairs={{0,10},{1,11},{2,8},{3,9},{4,14},{5,15},{6,12},{7,13},{8,2},{9,3},... | collective-permute-start | bytes 49160 | tf_op jit(solution)/shard_map/ppermute | solution.py:227
  71.0 4.1 %collective-permute-start.23 = (bf16[64,128]{1,0:T(8,128)(2,1)S(1)}, bf16[64,128]{1,0:T(8,128)(2,1)S(1)}, u32[]{:S(2)}, u32[]{:S(2)}) collective-permute-start(bf16[64,128]{1,0:T(8,128)(2,1)S(1)} %get-tuple-element.63), channel_id=1, source_target_pairs={{0,11},{1,8},{2,9},{3,10},{4,15},{5,12},{6,13},{7,14},{8,3},{9,0},... | collective-permute-start | bytes 49160 | tf_op jit(solution)/shard_map/ppermute | solution.py:227

commit v2 on v1

v2 whole, which is shorter than its diff:
```python
import functools

import jax
import jax.numpy as jnp
from jax import lax
from jax.experimental import pallas as pl
from jax.experimental.pallas import tpu as pltpu
from jax.sharding import PartitionSpec as P

PRODUCTS = 4
REACH = 4
LEVELS = 3
SPAN = 2 * REACH + 1

F32 = jnp.float32
BF16 = jnp.bfloat16
IN_VMEM = pl.BlockSpec(memory_space=pltpu.VMEM)
IN_SMEM = pl.BlockSpec(memory_space=pltpu.SMEM)
IN_HBM = pl.BlockSpec(memory_space=pltpu.HBM)
ANYWHERE = pl.BlockSpec(memory_space=pl.ANY)


def dot_nt(a, b):
    return lax.dot_general(a, b, (((1,), (1,)), ((), ())), preferred_element_type=F32)


def dot_nn(a, b):
    return lax.dot_general(a, b, (((1,), (0,)), ((), ())), preferred_element_type=F32)


def far_pieces(x, cb_ref, g_ref, sets, members, place, send_refs):
    coeffs = dot_nt(x, cb_ref[...]).astype(BF16)
    width = cb_ref.shape[0]
    for index, levels in enumerate(sets):
        total = sum(dot_nt(coeffs, g_ref[level]) for level in levels).astype(BF16)
        for step in range(members):
            piece = total[:, step * width : (step + 1) * width]
            if place is None:
                send_refs[index * members + step][...] = piece
            else:
                send_refs[0][place + step] = piece


def prepare_kernel(
    per_device, members, sets, paired, index_ref, rows_hbm, cols_hbm, near_rows_hbm, offsets_hbm,
    x_hbm, col_hbm, coup_hbm, row_hbm, tiles_hbm, x_ref, d_ref, g_ref, cb_ref, rb_ref, *rest
):
    *sends, rows_ref, cols_ref, near_rows_ref, offsets_ref, col_ref, coup_ref, row_ref, present, sems, tile_sems = rest
    pairs = (
        (near_rows_hbm, near_rows_ref),
        (offsets_hbm, offsets_ref),
        (rows_hbm, rows_ref),
        (cols_hbm, cols_ref),
        (x_hbm, x_ref),
        (col_hbm, col_ref),
        (coup_hbm, coup_ref),
        (row_hbm, row_ref),
    )
    copies = [pltpu.make_async_copy(src, dst, sems.at[i]) for i, (src, dst) in enumerate(pairs)]
    for copy in copies:
        copy.start()
    slots, rank, _ = coup_ref.shape
    size = col_ref.shape[2]
    width = per_device * rank
    block_clusters = per_device * members
    cb_ref[...] = jnp.zeros_like(cb_ref)
    rb_ref[...] = jnp.zeros_like(rb_ref)
    g_ref[...] = jnp.zeros_like(g_ref)
    for cell in range(per_device * SPAN):
        present[cell] = 0
    copies[0].wait()
    copies[1].wait()
    tiles = []
    for s in range(tiles_hbm.shape[0]):
        cell = near_rows_ref[s] * SPAN + offsets_ref[s] + REACH
        present[cell] = 1
        tiles.append(pltpu.make_async_copy(tiles_hbm.at[s], d_ref.at[cell], tile_sems.at[s]))
        tiles[-1].start()
    for copy in copies[2:]:
        copy.wait()
    for c in range(per_device):
        cb_ref[c * rank : (c + 1) * rank, c * size : (c + 1) * size] = col_ref[c]
        for half in range(2):
            start = half * width + c * rank
            rb_ref[start : start + rank, c * size : (c + 1) * size] = row_ref[c]
    column = lax.broadcasted_iota(jnp.int32, (rank, width), 1) // rank
    shift = 0 if paired else lax.rem(index_ref[0], members)
    for s in range(slots):
        level = rows_ref[s] // block_clusters
        row = rows_ref[s] % block_clusters
        step = lax.rem(row // per_device - shift + members, members)
        start = pl.multiple_of((step * per_device + row % per_device) * rank, rank)
        tile = coup_ref[s].astype(F32)
        wide = jnp.where(column == cols_ref[s], jnp.concatenate([tile] * per_device, axis=1), 0.0)
        where = (level, pl.ds(start, rank), slice(None))
        g_ref[where] = g_ref[where] + wide.astype(BF16)
    far_pieces(x_ref[...], cb_ref, g_ref, sets, members, other_half(index_ref, members, paired), sends)
    for copy in tiles:
        copy.wait()

    @pl.loop(0, per_device * SPAN)
    def _(cell):
        @pl.when(present[cell] == 0)
        def _():
            d_ref[cell] = jnp.zeros(d_ref.shape[1:], d_ref.dtype)


def other_half(index_ref, members, paired):
    if not paired:
        return None
    return jnp.where(lax.div(index_ref[0], members) >= paired, 0, members)


def own_sums(x_ref, d_ref, acc_ref, per_device):
    size = d_ref.shape[1]
    panels = [x_ref[:, c * size : (c + 1) * size] for c in range(per_device)]
    for r in range(per_device):
        acc_ref[:, r * size : (r + 1) * size] = sum(
            dot_nt(panels[c], d_ref[r * SPAN + c - r + REACH]) for c in range(per_device)
        )


def own_kernel(per_device, x_ref, d_ref, acc_ref):
    own_sums(x_ref, d_ref, acc_ref, per_device)


def later_own_kernel(per_device, slot, x_ref, d_ref, *refs):
    krylov_ref, acc_ref, sem = refs[-3:]
    copy = pltpu.make_async_copy(x_ref, krylov_ref.at[slot], sem)
    copy.start()
    own_sums(x_ref, d_ref, acc_ref, per_device)
    copy.wait()


def next_block(per_device, members, paired, index_ref, acc_ref, near_ref, over_ref, d_ref, rb_ref, piece_refs):
    size = d_ref.shape[1]
    if paired:
        place = other_half(index_ref, members, paired)
        pieces = [piece_refs[0][place + step] for step in range(members)]
    else:
        pieces = [piece[...] for piece in piece_refs]
    total = sum(piece.astype(F32) for piece in pieces)
    upper = total.astype(BF16)
    lower = (total - upper.astype(F32)).astype(BF16)
    both = jnp.concatenate([upper, lower], axis=1)
    odd = lax.rem(index_ref[0], 2) == 1
    low, high = [], []
    for c in range(per_device):
        near, over = (ref[:, c * size : (c + 1) * size] for ref in (near_ref, over_ref))
        low.append(jnp.where(odd, near, over))
        high.append(jnp.where(odd, over, near))
    parts = []
    for r in range(per_device):
        columns = slice(r * size, (r + 1) * size)
        value = acc_ref[:, columns] + dot_nn(both, rb_ref[:, columns])
        for c in range(per_device):
            for panel, place in ((low[c], c - per_device), (high[c], c + per_device)):
                offset = place - r
                if -REACH <= offset <= REACH:
                    value = value + dot_nt(panel, d_ref[r * SPAN + offset + REACH])
        parts.append(value.astype(BF16))
    return jnp.concatenate(parts, axis=1)


def finish_kernel(per_device, members, sets, paired, pieces, *refs):
    index_ref, acc_ref, near_ref, over_ref, d_ref, rb_ref, cb_ref, g_ref = refs[:8]
    piece_refs = refs[8 : 8 + pieces]
    x_ref, *sends = refs[8 + pieces :]
    x = next_block(
        per_device, members, paired, index_ref, acc_ref, near_ref, over_ref, d_ref, rb_ref, piece_refs
    )
    x_ref[...] = x
    far_pieces(x, cb_ref, g_ref, sets, members, other_half(index_ref, members, paired), sends)


def last_kernel(per_device, members, paired, slot, pieces, *refs):
    index_ref, acc_ref, near_ref, over_ref, d_ref, rb_ref = refs[:6]
    piece_refs = refs[6 : 6 + pieces]
    _, krylov_ref, x_ref, sem = refs[6 + pieces :]
    x_ref[...] = next_block(
        per_device, members, paired, index_ref, acc_ref, near_ref, over_ref, d_ref, rb_ref, piece_refs
    )
    copy = pltpu.make_async_copy(x_ref, krylov_ref.at[slot], sem)
    copy.start()
    copy.wait()


def on_device(
    block, near_tiles, near_rows, near_offsets, col_basis, couplings, far_rows, far_cols, row_basis
):
    rhs, shard_len = block.shape
    size = near_tiles.shape[1]
    rank = couplings.shape[1]
    per_device = shard_len // size
    members = lax.axis_size("far")
    loop_size = lax.axis_size("loop")
    devices = members * loop_size
    width = per_device * rank
    distances = [d % loop_size for d in (2, loop_size - 2, loop_size // 2)]
    hops = sorted(set(distances))
    sets = tuple(tuple(i for i, d in enumerate(distances) if d == hop) for hop in hops)
    both_axes = ("loop", "far")
    paired = hops[0] if len(hops) == 1 and 2 * hops[0] == loop_size else 0
    pieces = 1 if paired else len(hops) * members
    swap = [(i, i ^ 1) for i in range(devices)]
    over = [(i, (i + 1 if i % 2 else i - 1) % devices) for i in range(devices)]

    def exchanged(sends):
        if paired:
            groups = [
                [(l + half * paired) * members + m for half in range(2) for m in range(members)]
                for l in range(paired)
            ]
            return [
                lax.all_to_all(sends[0], both_axes, 0, 0, axis_index_groups=groups, tiled=True)
            ]
        received = []
        for i, send in enumerate(sends):
            hop, step = hops[i // members], i % members
            route = [
                (l * members + m, (l + hop) % loop_size * members + (m + step) % members)
                for l in range(loop_size)
                for m in range(members)
            ]
            received.append(lax.ppermute(send, both_axes, route))
        return received

    params = pltpu.CompilerParams(vmem_limit_bytes=16 * 2**20)

    def call(kernel, ins, specs, outs, out_specs, scratch=(), aliases=None, flops=0, name=None):
        constraint = {id(IN_VMEM): pltpu.VMEM, id(IN_HBM): pltpu.HBM}
        ins = [
            pltpu.with_memory_space_constraint(v, constraint[id(spec)]) if id(spec) in constraint else v
            for v, spec in zip(ins, specs)
        ]
        return pl.pallas_call(
            kernel,
            in_specs=list(specs),
            out_specs=list(out_specs),
            out_shape=list(outs),
            scratch_shapes=list(scratch),
            input_output_aliases=aliases or {},
            compiler_params=params,
            cost_estimate=pl.CostEstimate(flops=flops, bytes_accessed=2**22, transcendentals=0),
            name=name,
        )(*ins)

    block_out = pltpu.VMEM((rhs, shard_len), BF16)
    acc_out = pltpu.VMEM((rhs, shard_len), F32)
    if paired:
        piece_outs = [pltpu.VMEM((2 * members, rhs, width), BF16)]
    else:
        piece_outs = [pltpu.VMEM((rhs, width), BF16)] * pieces
    krylov_out = jax.ShapeDtypeStruct((PRODUCTS, rhs, shard_len), BF16)
    cells = per_device * SPAN
    slots = near_tiles.shape[0]
    index = lax.axis_index(both_axes).astype(jnp.int32).reshape(1)

    current = block
    krylov = None
    for product in range(PRODUCTS):
        near = lax.ppermute(current, both_axes, swap)
        far = lax.ppermute(current, both_axes, over)
        if product == 0:
            current, dense, coupled, col_wide, row_wide, *sends = call(
                functools.partial(prepare_kernel, per_device, members, sets, paired),
                [index, far_rows, far_cols, near_rows, near_offsets]
                + [block, col_basis, couplings, row_basis, near_tiles],
                [IN_SMEM] + [IN_HBM] * 9,
                [
                    block_out,
                    pltpu.VMEM((cells, size, size), BF16),
                    pltpu.VMEM((LEVELS, members * width, width), BF16),
                    pltpu.VMEM((width, shard_len), BF16),
                    pltpu.VMEM((2 * width, shard_len), BF16),
                    *piece_outs,
                ],
                [IN_VMEM] * (5 + pieces),
                [
                    pltpu.SMEM(far_rows.shape, jnp.int32),
                    pltpu.SMEM(far_cols.shape, jnp.int32),
                    pltpu.SMEM(near_rows.shape, jnp.int32),
                    pltpu.SMEM(near_offsets.shape, jnp.int32),
                    pltpu.VMEM(col_basis.shape, BF16),
                    pltpu.VMEM(couplings.shape, BF16),
                    pltpu.VMEM(row_basis.shape, BF16),
                    pltpu.SMEM((cells,), jnp.int32),
                    pltpu.SemaphoreType.DMA((8,)),
                    pltpu.SemaphoreType.DMA((slots,)),
                ],
                flops=10**8,
                name="prepare",
            )
        received = exchanged(sends)
        if product == 0:
            (acc,) = call(
                functools.partial(own_kernel, per_device),
                [current, dense],
                [IN_VMEM] * 2,
                [acc_out],
                [IN_VMEM],
                flops=10**9,
                name="own",
            )
        else:
            ins, specs, aliases = [current, dense], [IN_VMEM] * 2, None
            if krylov is not None:
                ins, specs, aliases = ins + [krylov], specs + [ANYWHERE], {2: 0}
            krylov, acc = call(
                functools.partial(later_own_kernel, per_device, product - 1),
                ins,
                specs,
                [krylov_out, acc_out],
                [ANYWHERE, IN_VMEM],
                [pltpu.SemaphoreType.DMA],
                aliases,
                flops=10**9,
                name="own",
            )
        if product < PRODUCTS - 1:
            ins = [index, acc, near, far, dense, row_wide, col_wide, coupled, *received]
            current, *sends = call(
                functools.partial(finish_kernel, per_device, members, sets, paired, pieces),
                ins,
                [IN_SMEM] + [IN_VMEM] * (len(ins) - 1),
                [block_out, *piece_outs],
                [IN_VMEM] * (1 + pieces),
                flops=10**9,
                name="finish",
            )
        else:
            ins = [index, acc, near, far, dense, row_wide, *received, krylov]
            (krylov,) = call(
                functools.partial(last_kernel, per_device, members, paired, product, pieces),
                ins,
                [IN_SMEM] + [IN_VMEM] * (len(ins) - 2) + [ANYWHERE],
                [krylov_out],
                [ANYWHERE],
                [pltpu.VMEM((rhs, shard_len), BF16), pltpu.SemaphoreType.DMA],
                {len(ins) - 1: 0},
                flops=10**9,
                name="last",
            )
    return krylov


def solution(mesh):
    split = ("groups", "loop", "far")
    in_specs = (
        P(None, split),
        P(split, None, None),
        P(split),
        P(split),
        P(split, None, None),
        P(split, None, None),
        P(split),
        P(split),
        P(split, None, None),
    )
    return jax.shard_map(
        on_device, mesh=mesh, in_specs=in_specs, out_specs=P(None, None, split), check_vma=False
    )
```

time: 77.1 us -> 76.8 us (level)
  waiting for transfers between devices: 22.9 us -> 3.55 us
  local copies, waits for them, and re-layouts: 9.27 us -> 20.8 us
  starting transfers between devices: 26.9 us -> 36.1 us
  Pallas kernels: 17.5 us -> 15.4 us
    ppermute x24 -> x8, waiting for transfers between devices: 22.9 us -> 3.54 us  [the longest x4 3.53 us: on_device(): far = lax.ppermute(current, both_axes, over)]
    all_to_all x0 -> x4, starting transfers between devices: none -> 16.3 us  [exchanged(): lax.all_to_all(sends[0], both_axes, 0, 0, axis_index_groups=groups, tiled...]
    unnamed x20, local copies, waits for them, and re-layouts: 9.27 us -> 20.8 us
    ppermute x24 -> x8, starting transfers between devices: 26.9 us -> 19.7 us  [the longest x4 18 us: on_device(): far = lax.ppermute(current, both_axes, over)]
    pallas_call x9, Pallas kernels: 17.5 us -> 15.4 us  [call(): pl.pallas_call(kernel, in_specs=list(specs), out_specs=list(out_specs), o...]
  transfers between devices with their start and end apart: 24 -> 12, of which waited for: 9 -> 4; matrix products, arithmetic and copies ran while one was open for 0% -> 0% of each run, Pallas kernels for 15% -> 4%
where the time goes in v2:
time: 76.8 us; the launch traced here: 76 us
  starting transfers between devices  36.1 us (47%)
  local copies, waits for them, and re-layouts  20.8 us (27%)
  Pallas kernels  15.4 us (20%)
  waiting for transfers between devices  3.55 us (5%)
    unnamed x20, local copies, waits for them, and re-layouts  20.8 us
    ppermute x4, starting transfers between devices, on_device(): far = lax.ppermute(current, both_axes, over)  18 us
    all_to_all x4, starting transfers between devices, exchanged(): lax.all_to_all(sends[0], both_axes, 0, 0, axis_index_groups=groups, tiled...  16.3 us
    pallas_call x9, Pallas kernels, call(): pl.pallas_call(kernel, in_specs=list(specs), out_specs=list(out_specs), o...  15.4 us
    ppermute x4, waiting for transfers between devices, on_device(): far = lax.ppermute(current, both_axes, over)  3.53 us
    ppermute x4, starting transfers between devices, on_device(): near = lax.ppermute(current, both_axes, swap)  1.72 us
  transfers between devices with their start and end apart: 12, of which 4 were waited for; matrix products, arithmetic and copies ran while one was open for 0% of the time, Pallas kernels for 4%

profile of v2, /device:TPU:0, one launch (start us, length us, event | category | flops | bytes accessed | tf_op | source)
XLA Modules:
  0.0 76.0 jit_solution(11738591458777970047)
XLA Ops:
  0.0 0.0 copy-start.9
  0.0 4.4 %prepare.1 = (bf16[64,1024]{1,0:T(8,128)(2,1)S(1)}, bf16[36,256,256]{2,1,0:T(8,128)(2,1)S(1)}, bf16[3,512,128]{2,1,0:T(8,128)(2,1)S(1)}, bf16[128,1024]{1,0:T(8,...) custom-call(s32[1]{0:T(128)} %bitcast.index_ref.refs_0_, s32[32]{0:T(128)} %rows_hbm.1, ...), custom_call_target="tpu_custom_call" | custom-call | flops 100000000 | bytes 4194304 | tf_op jit(solution)/shard_map/prepare/pallas_call | solution.py:236
  4.4 0.0 copy-start
  4.5 2.1 %copy-done = bf16[36,256,256]{2,1,0:T(8,128)(2,1)} copy-done((bf16[36,256,256]{2,1,0:T(8,128)(2,1)}, bf16[36,256,256]{2,1,0:T(8,128)(2,1)S(1)}, u32[]{:S(2)}) %copy-start) | copy-done | bytes 4718616
  6.6 6.2 %all-to-all-start = ((bf16[8,64,128]{2,1,0:T(8,128)(2,1)}), bf16[8,64,128]{2,1,0:T(8,128)(2,1)S(1)}, u32[]{:S(2)}, u32[]{:S(2)}) async-start(bf16[8,64,128]{2,1,0:T(8,128)(2,1)} %get-tuple-element.28), calls=%async_computation | async-start | bytes 262144 | tf_op jit(solution)/shard_map/all_to_all | solution.py:215
  12.8 0.0 copy-done.9
  12.8 0.5 collective-permute-start
  13.3 4.4 %collective-permute-start.1 = (bf16[64,1024]{1,0:T(8,128)(2,1)S(1)}, bf16[64,1024]{1,0:T(8,128)(2,1)S(1)}, u32[]{:S(2)}, u32[]{:S(2)}) collective-permute-start(bf16[64,1024]{1,0:T(8,128)(2,1)S(1)} %copy-done.9), channel_id=1, source_target_pairs={{0,15},{1,2},{2,1},{3,4},{4,3},{5,6},{6,5},{7,8},{8,7},{9,10},{10,... | collective-permute-start | bytes 393224 | tf_op jit(solution)/shard_map/ppermute | solution.py:263
  17.8 0.0 copy-start.1
  17.8 2.3 %copy-done.1 = bf16[36,256,256]{2,1,0:T(8,128)(2,1)S(1)} copy-done((bf16[36,256,256]{2,1,0:T(8,128)(2,1)S(1)}, bf16[36,256,256]{2,1,0:T(8,128)(2,1)}, u32[]{:S(2)}) %copy-start.1) | copy-done | bytes 4718616
  20.1 0.7 own.4.refs_1_
  20.9 0.0 collective-permute-done.refs_2_
  20.9 0.9 %collective-permute-done.1.refs_3_ = bf16[64,1024]{1,0:T(8,128)(2,1)S(1)} collective-permute-done((bf16[64,1024]{1,0:T(8,128)(2,1)S(1)}, bf16[64,1024]{1,0:T(8,128)(2,1)S(1)}, u32[]{:S(2)}, u32[]{:S(2)}) %collective-permute-start.1) | collective-permute-done | bytes 131104 | tf_op jit(solution)/shard_map/ppermute | solution.py:263
  21.8 0.0 all-to-all-done.refs_8_
  21.8 0.0 copy-start.2
  21.8 2.3 %copy-done.2 = bf16[36,256,256]{2,1,0:T(8,128)(2,1)S(1)} copy-done((bf16[36,256,256]{2,1,0:T(8,128)(2,1)S(1)}, bf16[36,256,256]{2,1,0:T(8,128)(2,1)}, u32[]{:S(2)}) %copy-start.2) | copy-done | bytes 4718616
  24.1 2.1 %finish.3 = (bf16[64,1024]{1,0:T(8,128)(2,1)S(1)}, bf16[8,64,128]{2,1,0:T(8,128)(2,1)}) custom-call(s32[1]{0:T(128)} %bitcast.index_ref.refs_0_, f32[64,1024]{1,0:T(8,128)S(1)} %own.4.refs_1_, bf16[64,1024]{1,0:T(8,128)(2,1)S(1)} %collective-permute-done.refs_2_, bf16[64,1024]{1,0:T(8,128)(2,1)S(1)} %collective-permute-done.1.refs_3_, ...), custom_call_target="tpu_custom_call" | custom-call | flops 1000000000 | bytes 4194304 | tf_op jit(solution)/shard_map/finish/pallas_call | solution.py:236
  26.2 3.4 %all-to-all-start.1 = ((bf16[8,64,128]{2,1,0:T(8,128)(2,1)}), bf16[8,64,128]{2,1,0:T(8,128)(2,1)S(1)}, u32[]{:S(2)}, u32[]{:S(2)}) async-start(bf16[8,64,128]{2,1,0:T(8,128)(2,1)} %get-tuple-element.31), calls=%async_computation.1 | async-start | bytes 262144 | tf_op jit(solution)/shard_map/all_to_all | solution.py:215
  29.6 0.4 collective-permute-start.2
  30.0 4.5 %collective-permute-start.3 = (bf16[64,1024]{1,0:T(8,128)(2,1)S(1)}, bf16[64,1024]{1,0:T(8,128)(2,1)S(1)}, u32[]{:S(2)}, u32[]{:S(2)}) collective-permute-start(bf16[64,1024]{1,0:T(8,128)(2,1)S(1)} %get-tuple-element.29.x_ref), channel_id=1, source_target_pairs={{0,15},{1,2},{2,1},{3,4},{4,3},{5,6},{6,5},{7,8},{8,7},{9,10},{10,... | collective-permute-start | bytes 393224 | tf_op jit(solution)/shard_map/ppermute | solution.py:263
  34.5 0.0 copy-start.3
  34.5 2.3 %copy-done.3 = bf16[36,256,256]{2,1,0:T(8,128)(2,1)S(1)} copy-done((bf16[36,256,256]{2,1,0:T(8,128)(2,1)S(1)}, bf16[36,256,256]{2,1,0:T(8,128)(2,1)}, u32[]{:S(2)}) %copy-start.3) | copy-done | bytes 4718616
  36.9 0.8 %own.5 = (bf16[4,64,1024]{2,1,0:T(8,128)(2,1)}, f32[64,1024]{1,0:T(8,128)S(1)}) custom-call(bf16[64,1024]{1,0:T(8,128)(2,1)S(1)} %get-tuple-element.29.x_ref, bf16[36,256,256]{2,1,0:T(8,128)(2,1)S(1)} %copy-done.3), custom_call_target="tpu_custom_call" | custom-call | flops 1000000000 | bytes 4194304 | tf_op jit(solution)/shard_map/own/pallas_call | solution.py:236
  37.6 0.0 collective-permute-done.2.refs_2_
  37.6 0.9 %collective-permute-done.3.refs_3_ = bf16[64,1024]{1,0:T(8,128)(2,1)S(1)} collective-permute-done((bf16[64,1024]{1,0:T(8,128)(2,1)S(1)}, bf16[64,1024]{1,0:T(8,128)(2,1)S(1)}, u32[]{:S(2)}, u32[]{:S(2)}) %collective-permute-start.3) | collective-permute-done | bytes 131104 | tf_op jit(solution)/shard_map/ppermute | solution.py:263
  38.5 0.0 all-to-all-done.1.refs_8_
  38.5 0.0 copy-start.4
  38.5 2.3 %copy-done.4 = bf16[36,256,256]{2,1,0:T(8,128)(2,1)S(1)} copy-done((bf16[36,256,256]{2,1,0:T(8,128)(2,1)S(1)}, bf16[36,256,256]{2,1,0:T(8,128)(2,1)}, u32[]{:S(2)}) %copy-start.4) | copy-done | bytes 4718616
  40.9 2.1 %finish.4 = (bf16[64,1024]{1,0:T(8,128)(2,1)S(1)}, bf16[8,64,128]{2,1,0:T(8,128)(2,1)}) custom-call(s32[1]{0:T(128)} %bitcast.index_ref.refs_0_, f32[64,1024]{1,0:T(8,128)S(1)} %get-tuple-element.30.refs_1_, bf16[64,1024]{1,0:T(8,128)(2,1)S(1)} %collective-permute-done.2.refs_2_, bf16[64,1024]{1,0:T(8,128)(2,1)S(1)} %collective-permute-done.3.refs_3_, ...), custom_call_target="tpu_custom_call" | custom-call | flops 1000000000 | bytes 4194304 | tf_op jit(solution)/shard_map/finish/pallas_call | solution.py:236
  43.0 3.4 %all-to-all-start.2 = ((bf16[8,64,128]{2,1,0:T(8,128)(2,1)}), bf16[8,64,128]{2,1,0:T(8,128)(2,1)S(1)}, u32[]{:S(2)}, u32[]{:S(2)}) async-start(bf16[8,64,128]{2,1,0:T(8,128)(2,1)} %get-tuple-element.35), calls=%async_computation.2 | async-start | bytes 262144 | tf_op jit(solution)/shard_map/all_to_all | solution.py:215
  46.3 0.4 collective-permute-start.4
  46.7 4.5 %collective-permute-start.5 = (bf16[64,1024]{1,0:T(8,128)(2,1)S(1)}, bf16[64,1024]{1,0:T(8,128)(2,1)S(1)}, u32[]{:S(2)}, u32[]{:S(2)}) collective-permute-start(bf16[64,1024]{1,0:T(8,128)(2,1)S(1)} %get-tuple-element.32.x_ref), channel_id=1, source_target_pairs={{0,15},{1,2},{2,1},{3,4},{4,3},{5,6},{6,5},{7,8},{8,7},{9,10},{10,... | collective-permute-start | bytes 393224 | tf_op jit(solution)/shard_map/ppermute | solution.py:263
  51.3 0.0 copy-start.5
  51.3 2.3 %copy-done.5 = bf16[36,256,256]{2,1,0:T(8,128)(2,1)S(1)} copy-done((bf16[36,256,256]{2,1,0:T(8,128)(2,1)S(1)}, bf16[36,256,256]{2,1,0:T(8,128)(2,1)}, u32[]{:S(2)}) %copy-start.5) | copy-done | bytes 4718616
  53.6 0.8 %own.6 = (bf16[4,64,1024]{2,1,0:T(8,128)(2,1)}, f32[64,1024]{1,0:T(8,128)S(1)}) custom-call(bf16[64,1024]{1,0:T(8,128)(2,1)S(1)} %get-tuple-element.32.x_ref, bf16[36,256,256]{2,1,0:T(8,128)(2,1)S(1)} %copy-done.5, bf16[4,64,1024]{2,1,0:T(8,128)(2,1)} %get-tuple-element.33.refs_0_), custom_call_target="tpu_custom_call", output_to_operand_aliasing={{0}: (2, {})} | custom-call | flops 1000000000 | bytes 4194304 | tf_op jit(solution)/shard_map/own/pallas_call | solution.py:236
  54.4 0.0 collective-permute-done.4.refs_2_
  54.4 0.9 %collective-permute-done.5.refs_3_ = bf16[64,1024]{1,0:T(8,128)(2,1)S(1)} collective-permute-done((bf16[64,1024]{1,0:T(8,128)(2,1)S(1)}, bf16[64,1024]{1,0:T(8,128)(2,1)S(1)}, u32[]{:S(2)}, u32[]{:S(2)}) %collective-permute-start.5) | collective-permute-done | bytes 131104 | tf_op jit(solution)/shard_map/ppermute | solution.py:263
  55.3 0.0 all-to-all-done.2.refs_8_
  55.3 0.0 copy-start.6
  55.3 2.3 %copy-done.6 = bf16[36,256,256]{2,1,0:T(8,128)(2,1)S(1)} copy-done((bf16[36,256,256]{2,1,0:T(8,128)(2,1)S(1)}, bf16[36,256,256]{2,1,0:T(8,128)(2,1)}, u32[]{:S(2)}) %copy-start.6) | copy-done | bytes 4718616
  57.6 2.1 %finish.5 = (bf16[64,1024]{1,0:T(8,128)(2,1)S(1)}, bf16[8,64,128]{2,1,0:T(8,128)(2,1)}) custom-call(s32[1]{0:T(128)} %bitcast.index_ref.refs_0_, f32[64,1024]{1,0:T(8,128)S(1)} %get-tuple-element.34.refs_1_, bf16[64,1024]{1,0:T(8,128)(2,1)S(1)} %collective-permute-done.4.refs_2_, bf16[64,1024]{1,0:T(8,128)(2,1)S(1)} %collective-permute-done.5.refs_3_, ...), custom_call_target="tpu_custom_call" | custom-call | flops 1000000000 | bytes 4194304 | tf_op jit(solution)/shard_map/finish/pallas_call | solution.py:236
  59.7 3.4 %all-to-all-start.3 = ((bf16[8,64,128]{2,1,0:T(8,128)(2,1)}), bf16[8,64,128]{2,1,0:T(8,128)(2,1)S(1)}, u32[]{:S(2)}, u32[]{:S(2)}) async-start(bf16[8,64,128]{2,1,0:T(8,128)(2,1)} %get-tuple-element.39), calls=%async_computation.3 | async-start | bytes 262144 | tf_op jit(solution)/shard_map/all_to_all | solution.py:215
  63.1 0.4 collective-permute-start.6
  63.5 4.5 %collective-permute-start.7 = (bf16[64,1024]{1,0:T(8,128)(2,1)S(1)}, bf16[64,1024]{1,0:T(8,128)(2,1)S(1)}, u32[]{:S(2)}, u32[]{:S(2)}) collective-permute-start(bf16[64,1024]{1,0:T(8,128)(2,1)S(1)} %get-tuple-element.36.x_ref), channel_id=1, source_target_pairs={{0,15},{1,2},{2,1},{3,4},{4,3},{5,6},{6,5},{7,8},{8,7},{9,10},{10,... | collective-permute-start | bytes 393224 | tf_op jit(solution)/shard_map/ppermute | solution.py:263
  68.0 0.0 copy-start.7
  68.0 2.3 %copy-done.7 = bf16[36,256,256]{2,1,0:T(8,128)(2,1)S(1)} copy-done((bf16[36,256,256]{2,1,0:T(8,128)(2,1)S(1)}, bf16[36,256,256]{2,1,0:T(8,128)(2,1)}, u32[]{:S(2)}) %copy-start.7) | copy-done | bytes 4718616
  70.4 0.8 %own.7 = (bf16[4,64,1024]{2,1,0:T(8,128)(2,1)}, f32[64,1024]{1,0:T(8,128)S(1)}) custom-call(bf16[64,1024]{1,0:T(8,128)(2,1)S(1)} %get-tuple-element.36.x_ref, bf16[36,256,256]{2,1,0:T(8,128)(2,1)S(1)} %copy-done.7, bf16[4,64,1024]{2,1,0:T(8,128)(2,1)} %get-tuple-element.37.refs_0_), custom_call_target="tpu_custom_call", output_to_operand_aliasing={{0}: (2, {})} | custom-call | flops 1000000000 | bytes 4194304 | tf_op jit(solution)/shard_map/own/pallas_call | solution.py:236
  71.1 0.0 collective-permute-done.6.refs_2_
  71.1 0.9 %collective-permute-done.7.refs_3_ = bf16[64,1024]{1,0:T(8,128)(2,1)S(1)} collective-permute-done((bf16[64,1024]{1,0:T(8,128)(2,1)S(1)}, bf16[64,1024]{1,0:T(8,128)(2,1)S(1)}, u32[]{:S(2)}, u32[]{:S(2)}) %collective-permute-start.7) | collective-permute-done | bytes 131104 | tf_op jit(solution)/shard_map/ppermute | solution.py:263
  72.0 0.0 all-to-all-done.3.refs_6_
  72.0 0.0 copy-start.8
  72.0 2.3 %copy-done.8 = bf16[36,256,256]{2,1,0:T(8,128)(2,1)S(1)} copy-done((bf16[36,256,256]{2,1,0:T(8,128)(2,1)S(1)}, bf16[36,256,256]{2,1,0:T(8,128)(2,1)}, u32[]{:S(2)}) %copy-start.8) | copy-done | bytes 4718616
  74.4 1.7 %last.1 = bf16[4,64,1024]{2,1,0:T(8,128)(2,1)} custom-call(s32[1]{0:T(128)} %bitcast.index_ref.refs_0_, f32[64,1024]{1,0:T(8,128)S(1)} %get-tuple-element.38.refs_1_, bf16[64,1024]{1,0:T(8,128)(2,1)S(1)} %collective-permute-done.6.refs_2_, bf16[64,1024]{1,0:T(8,128)(2,1)S(1)} %collective-permute-done.7.refs_3_, ...), custom_call_target="tpu_custom_call", output_to_operand_aliasing={{}: (7, {})} | custom-call | flops 1000000000 | bytes 4194304 | tf_op jit(solution)/shard_map/last/pallas_call | solution.py:236
Async XLA Ops:
  0.0 12.8 %copy-start.9 = (bf16[64,1024]{1,0:T(8,128)(2,1)S(1)}, bf16[64,1024]{1,0:T(8,128)(2,1)}, u32[]{:S(2)}) copy-start(bf16[64,1024]{1,0:T(8,128)(2,1)} %x_hbm.1) | copy-start | bytes 393220
  4.4 2.2 %copy-start = (bf16[36,256,256]{2,1,0:T(8,128)(2,1)}, bf16[36,256,256]{2,1,0:T(8,128)(2,1)S(1)}, u32[]{:S(2)}) copy-start(bf16[36,256,256]{2,1,0:T(8,128)(2,1)S(1)} %get-tuple-element.24.d_ref.refs_4_) | copy-start | bytes 14155780
  6.6 15.2 %all-to-all-start = ((bf16[8,64,128]{2,1,0:T(8,128)(2,1)}), bf16[8,64,128]{2,1,0:T(8,128)(2,1)S(1)}, u32[]{:S(2)}, u32[]{:S(2)}) async-start(bf16[8,64,128]{2,1,0:T(8,128)(2,1)} %get-tuple-element.28), calls=%async_computation | async-start | bytes 262144 | tf_op jit(solution)/shard_map/all_to_all | solution.py:215
  12.8 8.0 %collective-permute-start = (bf16[64,1024]{1,0:T(8,128)(2,1)S(1)}, bf16[64,1024]{1,0:T(8,128)(2,1)S(1)}, u32[]{:S(2)}, u32[]{:S(2)}) collective-permute-start(bf16[64,1024]{1,0:T(8,128)(2,1)S(1)} %copy-done.9), channel_id=1, source_target_pairs={{0,1},{1,0},{2,3},{3,2},{4,5},{5,4},{6,7},{7,6},{8,9},{9,8},{10,11... | collective-permute-start | bytes 393224 | tf_op jit(solution)/shard_map/ppermute | solution.py:262
  13.3 8.4 %collective-permute-start.1 = (bf16[64,1024]{1,0:T(8,128)(2,1)S(1)}, bf16[64,1024]{1,0:T(8,128)(2,1)S(1)}, u32[]{:S(2)}, u32[]{:S(2)}) collective-permute-start(bf16[64,1024]{1,0:T(8,128)(2,1)S(1)} %copy-done.9), channel_id=1, source_target_pairs={{0,15},{1,2},{2,1},{3,4},{4,3},{5,6},{6,5},{7,8},{8,7},{9,10},{10,... | collective-permute-start | bytes 393224 | tf_op jit(solution)/shard_map/ppermute | solution.py:263
  17.8 2.3 %copy-start.1 = (bf16[36,256,256]{2,1,0:T(8,128)(2,1)S(1)}, bf16[36,256,256]{2,1,0:T(8,128)(2,1)}, u32[]{:S(2)}) copy-start(bf16[36,256,256]{2,1,0:T(8,128)(2,1)} %copy-done) | copy-start | bytes 14155780
  21.8 2.3 %copy-start.2 = (bf16[36,256,256]{2,1,0:T(8,128)(2,1)S(1)}, bf16[36,256,256]{2,1,0:T(8,128)(2,1)}, u32[]{:S(2)}) copy-start(bf16[36,256,256]{2,1,0:T(8,128)(2,1)} %copy-done) | copy-start | bytes 14155780
  26.2 12.3 %all-to-all-start.1 = ((bf16[8,64,128]{2,1,0:T(8,128)(2,1)}), bf16[8,64,128]{2,1,0:T(8,128)(2,1)S(1)}, u32[]{:S(2)}, u32[]{:S(2)}) async-start(bf16[8,64,128]{2,1,0:T(8,128)(2,1)} %get-tuple-element.31), calls=%async_computation.1 | async-start | bytes 262144 | tf_op jit(solution)/shard_map/all_to_all | solution.py:215
  29.6 8.0 %collective-permute-start.2 = (bf16[64,1024]{1,0:T(8,128)(2,1)S(1)}, bf16[64,1024]{1,0:T(8,128)(2,1)S(1)}, u32[]{:S(2)}, u32[]{:S(2)}) collective-permute-start(bf16[64,1024]{1,0:T(8,128)(2,1)S(1)} %get-tuple-element.29.x_ref), channel_id=1, source_target_pairs={{0,1},{1,0},{2,3},{3,2},{4,5},{5,4},{6,7},{7,6},{8,9},{9,8},{10,11... | collective-permute-start | bytes 393224 | tf_op jit(solution)/shard_map/ppermute | solution.py:262
  30.0 8.5 %collective-permute-start.3 = (bf16[64,1024]{1,0:T(8,128)(2,1)S(1)}, bf16[64,1024]{1,0:T(8,128)(2,1)S(1)}, u32[]{:S(2)}, u32[]{:S(2)}) collective-permute-start(bf16[64,1024]{1,0:T(8,128)(2,1)S(1)} %get-tuple-element.29.x_ref), channel_id=1, source_target_pairs={{0,15},{1,2},{2,1},{3,4},{4,3},{5,6},{6,5},{7,8},{8,7},{9,10},{10,... | collective-permute-start | bytes 393224 | tf_op jit(solution)/shard_map/ppermute | solution.py:263
  34.5 2.3 %copy-start.3 = (bf16[36,256,256]{2,1,0:T(8,128)(2,1)S(1)}, bf16[36,256,256]{2,1,0:T(8,128)(2,1)}, u32[]{:S(2)}) copy-start(bf16[36,256,256]{2,1,0:T(8,128)(2,1)} %copy-done) | copy-start | bytes 14155780
  38.5 2.3 %copy-start.4 = (bf16[36,256,256]{2,1,0:T(8,128)(2,1)S(1)}, bf16[36,256,256]{2,1,0:T(8,128)(2,1)}, u32[]{:S(2)}) copy-start(bf16[36,256,256]{2,1,0:T(8,128)(2,1)} %copy-done) | copy-start | bytes 14155780
  43.0 12.3 %all-to-all-start.2 = ((bf16[8,64,128]{2,1,0:T(8,128)(2,1)}), bf16[8,64,128]{2,1,0:T(8,128)(2,1)S(1)}, u32[]{:S(2)}, u32[]{:S(2)}) async-start(bf16[8,64,128]{2,1,0:T(8,128)(2,1)} %get-tuple-element.35), calls=%async_computation.2 | async-start | bytes 262144 | tf_op jit(solution)/shard_map/all_to_all | solution.py:215
  46.3 8.0 %collective-permute-start.4 = (bf16[64,1024]{1,0:T(8,128)(2,1)S(1)}, bf16[64,1024]{1,0:T(8,128)(2,1)S(1)}, u32[]{:S(2)}, u32[]{:S(2)}) collective-permute-start(bf16[64,1024]{1,0:T(8,128)(2,1)S(1)} %get-tuple-element.32.x_ref), channel_id=1, source_target_pairs={{0,1},{1,0},{2,3},{3,2},{4,5},{5,4},{6,7},{7,6},{8,9},{9,8},{10,11... | collective-permute-start | bytes 393224 | tf_op jit(solution)/shard_map/ppermute | solution.py:262
  46.7 8.5 %collective-permute-start.5 = (bf16[64,1024]{1,0:T(8,128)(2,1)S(1)}, bf16[64,1024]{1,0:T(8,128)(2,1)S(1)}, u32[]{:S(2)}, u32[]{:S(2)}) collective-permute-start(bf16[64,1024]{1,0:T(8,128)(2,1)S(1)} %get-tuple-element.32.x_ref), channel_id=1, source_target_pairs={{0,15},{1,2},{2,1},{3,4},{4,3},{5,6},{6,5},{7,8},{8,7},{9,10},{10,... | collective-permute-start | bytes 393224 | tf_op jit(solution)/shard_map/ppermute | solution.py:263
  51.3 2.3 %copy-start.5 = (bf16[36,256,256]{2,1,0:T(8,128)(2,1)S(1)}, bf16[36,256,256]{2,1,0:T(8,128)(2,1)}, u32[]{:S(2)}) copy-start(bf16[36,256,256]{2,1,0:T(8,128)(2,1)} %copy-done) | copy-start | bytes 14155780
  55.3 2.3 %copy-start.6 = (bf16[36,256,256]{2,1,0:T(8,128)(2,1)S(1)}, bf16[36,256,256]{2,1,0:T(8,128)(2,1)}, u32[]{:S(2)}) copy-start(bf16[36,256,256]{2,1,0:T(8,128)(2,1)} %copy-done) | copy-start | bytes 14155780
  59.7 12.3 %all-to-all-start.3 = ((bf16[8,64,128]{2,1,0:T(8,128)(2,1)}), bf16[8,64,128]{2,1,0:T(8,128)(2,1)S(1)}, u32[]{:S(2)}, u32[]{:S(2)}) async-start(bf16[8,64,128]{2,1,0:T(8,128)(2,1)} %get-tuple-element.39), calls=%async_computation.3 | async-start | bytes 262144 | tf_op jit(solution)/shard_map/all_to_all | solution.py:215
  63.1 8.0 %collective-permute-start.6 = (bf16[64,1024]{1,0:T(8,128)(2,1)S(1)}, bf16[64,1024]{1,0:T(8,128)(2,1)S(1)}, u32[]{:S(2)}, u32[]{:S(2)}) collective-permute-start(bf16[64,1024]{1,0:T(8,128)(2,1)S(1)} %get-tuple-element.36.x_ref), channel_id=1, source_target_pairs={{0,1},{1,0},{2,3},{3,2},{4,5},{5,4},{6,7},{7,6},{8,9},{9,8},{10,11... | collective-permute-start | bytes 393224 | tf_op jit(solution)/shard_map/ppermute | solution.py:262
  63.5 8.5 %collective-permute-start.7 = (bf16[64,1024]{1,0:T(8,128)(2,1)S(1)}, bf16[64,1024]{1,0:T(8,128)(2,1)S(1)}, u32[]{:S(2)}, u32[]{:S(2)}) collective-permute-start(bf16[64,1024]{1,0:T(8,128)(2,1)S(1)} %get-tuple-element.36.x_ref), channel_id=1, source_target_pairs={{0,15},{1,2},{2,1},{3,4},{4,3},{5,6},{6,5},{7,8},{8,7},{9,10},{10,... | collective-permute-start | bytes 393224 | tf_op jit(solution)/shard_map/ppermute | solution.py:263
  68.0 2.3 %copy-start.7 = (bf16[36,256,256]{2,1,0:T(8,128)(2,1)S(1)}, bf16[36,256,256]{2,1,0:T(8,128)(2,1)}, u32[]{:S(2)}) copy-start(bf16[36,256,256]{2,1,0:T(8,128)(2,1)} %copy-done) | copy-start | bytes 14155780
  72.0 2.3 %copy-start.8 = (bf16[36,256,256]{2,1,0:T(8,128)(2,1)S(1)}, bf16[36,256,256]{2,1,0:T(8,128)(2,1)}, u32[]{:S(2)}) copy-start(bf16[36,256,256]{2,1,0:T(8,128)(2,1)} %copy-done) | copy-start | bytes 14155780

commit v3 on v0

v3 whole, which is shorter than its diff:
```python
import functools

import jax
import jax.numpy as jnp
from jax import lax
from jax.experimental import pallas as pl
from jax.experimental.pallas import tpu as pltpu
from jax.sharding import PartitionSpec as P

PRODUCTS = 4
REACH = 4
LEVELS = 3
SPAN = 2 * REACH + 1

F32 = jnp.float32
BF16 = jnp.bfloat16
IN_VMEM = pl.BlockSpec(memory_space=pltpu.VMEM)
IN_SMEM = pl.BlockSpec(memory_space=pltpu.SMEM)
IN_HBM = pl.BlockSpec(memory_space=pltpu.HBM)
ANYWHERE = pl.BlockSpec(memory_space=pl.ANY)


def dot_nt(a, b):
    return lax.dot_general(a, b, (((1,), (1,)), ((), ())), preferred_element_type=F32)


def dot_nn(a, b):
    return lax.dot_general(a, b, (((1,), (0,)), ((), ())), preferred_element_type=F32)


def halves(value):
    upper = value.astype(BF16)
    return upper, (value - upper.astype(F32)).astype(BF16)


class Plan:
    def __init__(self, block_shape, tile_shape, coupling_shape, members, loop_size):
        self.rhs, self.shard_len = block_shape
        self.tiles, self.size, _ = tile_shape
        self.slots, self.rank, _ = coupling_shape
        self.members, self.loop_size = members, loop_size
        self.per_device = self.shard_len // self.size
        self.width = self.per_device * self.rank
        self.cells = self.per_device * SPAN
        self.block_clusters = self.per_device * members
        distances = [d % loop_size for d in (2, loop_size - 2, loop_size // 2)]
        self.hops = sorted(set(distances))
        self.sets = [[i for i, d in enumerate(distances) if d == hop] for hop in self.hops]
        self.paired = len(self.hops) == 1 and 2 * self.hops[0] == loop_size and members == 4
        devices = members * loop_size
        self.near = [(i, i ^ 1) for i in range(devices)]
        self.over = [(i, (i + 1 if i % 2 else i - 1) % devices) for i in range(devices)]
        places = [(l, m) for l in range(loop_size) for m in range(members)]
        self.across = [
            (l * members + m, (l + self.hops[0]) % loop_size * members + (m ^ (m % 2 * 2)))
            for l, m in places
        ]
        self.routes = [
            [(l * members + m, (l + hop) % loop_size * members + (m + step) % members) for l, m in places]
            for hop in self.hops
            for step in range(members)
        ]

    def panel(self, ref, c):
        return ref[:, c * self.size : (c + 1) * self.size]

    def member(self, index_ref):
        return lax.rem(index_ref[0], self.members)

    def send_far(self, index_ref, x, cb_ref, g_ref, out_refs):
        coeffs = dot_nt(x, cb_ref[...]).astype(BF16)
        totals = [sum(dot_nt(coeffs, g_ref[level]) for level in levels) for levels in self.sets]
        if not self.paired:
            for i, out_ref in enumerate(out_refs):
                step = i % self.members * self.width
                out_ref[...] = totals[i // self.members][:, step : step + self.width].astype(BF16)
            return
        message_ref, keep_ref = out_refs
        (total,) = totals
        member = self.member(index_ref)
        second = lax.rem(member, 2) != lax.div(member, 2)
        first, last = total[:, : 2 * self.width], total[:, 2 * self.width :]
        keep_ref[...] = jnp.where(second, last, first)
        upper, lower = halves(jnp.where(second, first, last))
        message_ref[:, : self.shard_len] = x
        message_ref[:, self.shard_len : self.shard_len + 2 * self.width] = upper
        message_ref[:, self.shard_len + 2 * self.width :] = lower

    def relay_far(self, keep_ref, message_ref, out_ref):
        upper = message_ref[:, self.shard_len : self.shard_len + 2 * self.width].astype(F32)
        lower = message_ref[:, self.shard_len + 2 * self.width :].astype(F32)
        out_ref[...] = (keep_ref[...] + (upper + lower)).astype(BF16)

    def far_sum(self, index_ref, far_refs):
        if not self.paired:
            return sum(ref[...].astype(F32) for ref in far_refs)
        both = far_refs[0][...].astype(F32) + far_refs[1][...].astype(F32)
        second = lax.rem(index_ref[0], 2) == 1
        return jnp.where(second, both[:, self.width :], both[:, : self.width])

    def own_sums(self, x_ref, d_ref, acc_ref):
        panels = [self.panel(x_ref, c) for c in range(self.per_device)]
        for r in range(self.per_device):
            acc_ref[:, r * self.size : (r + 1) * self.size] = sum(
                dot_nt(panels[c], d_ref[r * SPAN + c - r + REACH]) for c in range(self.per_device)
            )

    def next_block(self, index_ref, acc_ref, near_ref, over_ref, d_ref, rb_ref, far_refs):
        both = jnp.concatenate(halves(self.far_sum(index_ref, far_refs)), axis=1)
        odd = lax.rem(index_ref[0], 2) == 1
        low, high = [], []
        for c in range(self.per_device):
            near, over = self.panel(near_ref, c), self.panel(over_ref, c)
            low.append(jnp.where(odd, near, over))
            high.append(jnp.where(odd, over, near))
        parts = []
        for r in range(self.per_device):
            value = self.panel(acc_ref, r) + dot_nn(both, self.panel(rb_ref, r))
            for c in range(self.per_device):
                for panel, place in ((low[c], c - self.per_device), (high[c], c + self.per_device)):
                    offset = place - r
                    if -REACH <= offset <= REACH:
                        value = value + dot_nt(panel, d_ref[r * SPAN + offset + REACH])
            parts.append(value.astype(BF16))
        return jnp.concatenate(parts, axis=1)


def prepare_kernel(plan, index_ref, *refs):
    sources, refs = refs[:9], refs[9:]
    x_ref, d_ref, g_ref, cb_ref, rb_ref = refs[:5]
    sends, held, (present, sems, tile_sems) = refs[5:-10], refs[-10:-3], refs[-3:]
    rows_ref, cols_ref, near_rows_ref, offsets_ref, col_ref, coup_ref, row_ref = held
    tiles_hbm = sources[8]
    targets = (near_rows_ref, offsets_ref, rows_ref, cols_ref, x_ref, col_ref, coup_ref, row_ref)
    copies = [
        pltpu.make_async_copy(source, target, sems.at[i])
        for i, (source, target) in enumerate(zip(sources[:8], targets))
    ]
    for copy in copies:
        copy.start()
    rank, size = plan.rank, plan.size
    cb_ref[...] = jnp.zeros_like(cb_ref)
    rb_ref[...] = jnp.zeros_like(rb_ref)
    g_ref[...] = jnp.zeros_like(g_ref)
    for cell in range(plan.cells):
        present[cell] = 0
    copies[0].wait()
    copies[1].wait()
    tiles = []
    for s in range(plan.tiles):
        cell = near_rows_ref[s] * SPAN + offsets_ref[s] + REACH
        present[cell] = 1
        tiles.append(pltpu.make_async_copy(tiles_hbm.at[s], d_ref.at[cell], tile_sems.at[s]))
        tiles[-1].start()
    for copy in copies[2:]:
        copy.wait()
    for c in range(plan.per_device):
        columns = slice(c * size, (c + 1) * size)
        cb_ref[c * rank : (c + 1) * rank, columns] = col_ref[c]
        for start in (c * rank, plan.width + c * rank):
            rb_ref[start : start + rank, columns] = row_ref[c]
    column = lax.broadcasted_iota(jnp.int32, (rank, plan.width), 1) // rank
    shift = 0 if plan.paired else plan.member(index_ref)
    for s in range(plan.slots):
        level = lax.div(rows_ref[s], plan.block_clusters)
        row = lax.rem(rows_ref[s], plan.block_clusters)
        step = lax.rem(lax.div(row, plan.per_device) - shift + plan.members, plan.members)
        place = step * plan.per_device + lax.rem(row, plan.per_device)
        where = (level, pl.ds(pl.multiple_of(place * rank, rank), rank), slice(None))
        tile = coup_ref[s].astype(F32)
        wide = jnp.where(column == cols_ref[s], jnp.concatenate([tile] * plan.per_device, axis=1), 0.0)
        g_ref[where] = g_ref[where] + wide.astype(BF16)
    plan.send_far(index_ref, x_ref[...], cb_ref, g_ref, sends)
    for copy in tiles:
        copy.wait()

    @pl.loop(0, plan.cells)
    def _(cell):
        @pl.when(present[cell] == 0)
        def _():
            d_ref[cell] = jnp.zeros(d_ref.shape[1:], d_ref.dtype)


def own_kernel(plan, slot, *refs):
    x_ref, d_ref, *refs = refs
    if plan.paired:
        keep_ref, message_ref, *refs = refs
    if slot is not None:
        *refs, sem = refs
        krylov_ref = refs[-1]
        copy = pltpu.make_async_copy(x_ref, krylov_ref.at[slot], sem)
        copy.start()
        refs = refs[1:-1] if slot else refs[:-1]
    if plan.paired:
        plan.relay_far(keep_ref, message_ref, refs[1])
    plan.own_sums(x_ref, d_ref, refs[0])
    if slot is not None:
        copy.wait()


def finish_kernel(plan, fars, *refs):
    index_ref, acc_ref, near_ref, over_ref, d_ref, rb_ref, cb_ref, g_ref = refs[:8]
    far_refs, (x_ref, *sends) = refs[8 : 8 + fars], refs[8 + fars :]
    x = plan.next_block(index_ref, acc_ref, near_ref, over_ref, d_ref, rb_ref, far_refs)
    x_ref[...] = x
    plan.send_far(index_ref, x, cb_ref, g_ref, sends)


def last_kernel(plan, fars, slot, *refs):
    index_ref, acc_ref, near_ref, over_ref, d_ref, rb_ref = refs[:6]
    far_refs, (_, krylov_ref, x_ref, sem) = refs[6 : 6 + fars], refs[6 + fars :]
    x_ref[...] = plan.next_block(index_ref, acc_ref, near_ref, over_ref, d_ref, rb_ref, far_refs)
    copy = pltpu.make_async_copy(x_ref, krylov_ref.at[slot], sem)
    copy.start()
    copy.wait()


def call(kernel, name, ins, specs, outs, out_specs=None, scratch=(), aliases=None):
    spaces = {id(IN_VMEM): pltpu.VMEM, id(IN_HBM): pltpu.HBM}
    ins = [
        pltpu.with_memory_space_constraint(v, spaces[id(spec)]) if id(spec) in spaces else v
        for v, spec in zip(ins, specs)
    ]
    return pl.pallas_call(
        kernel,
        in_specs=list(specs),
        out_specs=out_specs or [IN_VMEM] * len(outs),
        out_shape=list(outs),
        scratch_shapes=list(scratch),
        input_output_aliases=aliases or {},
        compiler_params=pltpu.CompilerParams(vmem_limit_bytes=16 * 2**20),
        cost_estimate=pl.CostEstimate(flops=10**9, bytes_accessed=2**22, transcendentals=0),
        name=name,
    )(*ins)


def on_device(
    block, near_tiles, near_rows, near_offsets, col_basis, couplings, far_rows, far_cols, row_basis
):
    axes = ("loop", "far")
    plan = Plan(
        block.shape, near_tiles.shape, couplings.shape, lax.axis_size("far"), lax.axis_size("loop")
    )
    rhs, shard_len, width = plan.rhs, plan.shard_len, plan.width
    block_out = pltpu.VMEM((rhs, shard_len), BF16)
    acc_out = pltpu.VMEM((rhs, shard_len), F32)
    relay_out = pltpu.VMEM((rhs, 2 * width), BF16)
    krylov_out = jax.ShapeDtypeStruct((PRODUCTS, rhs, shard_len), BF16)
    if plan.paired:
        sends_out = [
            pltpu.VMEM((rhs, shard_len + 4 * width), BF16),
            pltpu.VMEM((rhs, 2 * width), F32),
        ]
    else:
        sends_out = [pltpu.VMEM((rhs, width), BF16)] * len(plan.routes)
    index = lax.axis_index(axes).astype(jnp.int32).reshape(1)
    smem = [pltpu.SMEM(v.shape, jnp.int32) for v in (far_rows, far_cols, near_rows, near_offsets)]
    vmem = [pltpu.VMEM(v.shape, BF16) for v in (col_basis, couplings, row_basis)]

    current = block
    krylov = None
    for product in range(PRODUCTS):
        over = lax.ppermute(current, axes, plan.over)
        if product == 0:
            ins = [near_rows, near_offsets, far_rows, far_cols]
            ins += [block, col_basis, couplings, row_basis, near_tiles]
            current, dense, coupled, col_wide, row_wide, *sends = call(
                functools.partial(prepare_kernel, plan),
                "prepare",
                [index, *ins],
                [IN_SMEM] + [IN_HBM] * 9,
                [
                    block_out,
                    pltpu.VMEM((plan.cells, plan.size, plan.size), BF16),
                    pltpu.VMEM((LEVELS, plan.members * width, width), BF16),
                    pltpu.VMEM((width, shard_len), BF16),
                    pltpu.VMEM((2 * width, shard_len), BF16),
                    *sends_out,
                ],
                scratch=[
                    *smem,
                    *vmem,
                    pltpu.SMEM((plan.cells,), jnp.int32),
                    pltpu.SemaphoreType.DMA((8,)),
                    pltpu.SemaphoreType.DMA((plan.tiles,)),
                ],
            )
        ins, outs = [current, dense], [acc_out]
        if plan.paired:
            message, keep = sends
            near = lax.ppermute(message, axes, plan.near)
            ins, outs = ins + [keep, near], outs + [relay_out]
        else:
            near = lax.ppermute(current, axes, plan.near)
            fars = [lax.ppermute(s, axes, route) for s, route in zip(sends, plan.routes)]
        specs, out_specs, scratch, aliases = [IN_VMEM] * len(ins), [IN_VMEM] * len(outs), [], None
        if product > 0:
            scratch, out_specs, outs = [pltpu.SemaphoreType.DMA], out_specs + [ANYWHERE], outs + [krylov_out]
        if product > 1:
            aliases = {len(ins): len(outs) - 1}
            ins, specs = ins + [krylov], specs + [ANYWHERE]
        slot = product - 1 if product else None
        acc, *rest = call(
            functools.partial(own_kernel, plan, slot), "own", ins, specs, outs, out_specs, scratch, aliases
        )
        if product > 0:
            *rest, krylov = rest
        if plan.paired:
            received = lax.ppermute(rest[0], axes, plan.across)
            fars = [received, lax.ppermute(received, axes, plan.near)]
        ins = [index, acc, near, over, dense, row_wide]
        if product < PRODUCTS - 1:
            ins += [col_wide, coupled, *fars]
            current, *sends = call(
                functools.partial(finish_kernel, plan, len(fars)),
                "finish",
                ins,
                [IN_SMEM] + [IN_VMEM] * (len(ins) - 1),
                [block_out, *sends_out],
            )
        else:
            ins += [*fars, krylov]
            (krylov,) = call(
                functools.partial(last_kernel, plan, len(fars), product),
                "last",
                ins,
                [IN_SMEM] + [IN_VMEM] * (len(ins) - 2) + [ANYWHERE],
                [krylov_out],
                [ANYWHERE],
                [pltpu.VMEM((rhs, shard_len), BF16), pltpu.SemaphoreType.DMA],
                {len(ins) - 1: 0},
            )
    return krylov


def solution(mesh):
    split = ("groups", "loop", "far")
    wide, narrow = P(split, None, None), P(split)
    in_specs = (P(None, split), wide, narrow, narrow, wide, wide, narrow, narrow, wide)
    return jax.shard_map(
        on_device, mesh=mesh, in_specs=in_specs, out_specs=P(None, None, split), check_vma=False
    )
```

time: 247 us -> 53.3 us (0.22)
  waiting for transfers between devices: 150 us -> 24 us
  matrix products: 30.4 us -> 0 us
  starting transfers between devices: 35.4 us -> 15.2 us
  local copies, waits for them, and re-layouts: 14.3 us -> 0.01 us
  between operations: 14.3 us -> 0.1 us
  Pallas kernels: 0 us -> 13.8 us
    unnamed x8 -> x0, waiting for transfers between devices: 127 us -> none
    dot_general x24 -> x0, matrix products: 30.4 us -> none  [the longest x4 14.3 us: on_device(): jnp.einsum('esq,spq->sep', chosen, near_tiles, preferred_element_type=jnp...]
    ppermute x20 -> x16, starting transfers between devices: 35.3 us -> 15.2 us  [the longest x4 13.7 us: on_device(): over = lax.ppermute(current, axes, plan.over)]
    pallas_call x0 -> x9, Pallas kernels: none -> 13.8 us  [call(): pl.pallas_call(kernel, in_specs=list(specs), out_specs=out_specs or [IN_V...]
    gather x8 -> x0, local copies, waits for them, and re-layouts: 4.88 us -> none  [the longest x4 2.46 us: on_device(): chosen = jnp.take(panels, window_pos, axis=1)]
    reshape x8 -> x0, local copies, waits for them, and re-layouts: 4.79 us -> none  [the longest x4 4.67 us: on_device(): partial_value.reshape(level_count, block_clusters, rank_size, rhs_count)]
    squeeze x4 -> x0, local copies, waits for them, and re-layouts: 3.66 us -> none  [on_device(): summed[level]]
    ppermute x20 -> x16, waiting for transfers between devices: 22.6 us -> 24 us  [the longest x4 19.2 us: on_device(): received = lax.ppermute(rest[0], axes, plan.across)]
  transfers between devices with their start and end apart: 24 -> 16, of which waited for: 19 -> 8; matrix products, arithmetic and copies ran while one was open for 13% -> 0% of each run, Pallas kernels for 0% -> 8%
where the time goes in v3:
time: 53.3 us; the launch traced here: 53.1 us
  waiting for transfers between devices  24 us (45%)
  starting transfers between devices  15.2 us (29%)
  Pallas kernels  13.8 us (26%)
    ppermute x4, waiting for transfers between devices, on_device(): received = lax.ppermute(rest[0], axes, plan.across)  19.2 us
    pallas_call x9, Pallas kernels, call(): pl.pallas_call(kernel, in_specs=list(specs), out_specs=out_specs or [IN_V...  13.8 us
    ppermute x4, starting transfers between devices, on_device(): over = lax.ppermute(current, axes, plan.over)  13.7 us
    ppermute x4, waiting for transfers between devices, on_device(): fars = [received, lax.ppermute(received, axes, plan.near)]  4.81 us
    ppermute x4, starting transfers between devices, on_device(): near = lax.ppermute(message, axes, plan.near)  1.14 us
  transfers between devices with their start and end apart: 16, of which 8 were waited for; matrix products, arithmetic and copies ran while one was open for 0% of the time, Pallas kernels for 8%

profile of v3, /device:TPU:0, one launch (start us, length us, event | category | flops | bytes accessed | tf_op | source)
XLA Modules:
  0.0 53.1 jit_solution(9572296462461830548)
XLA Ops:
  0.0 0.0 copy-start
  0.0 3.7 %prepare.1 = (bf16[64,1024]{1,0:T(8,128)(2,1)S(1)}, bf16[36,256,256]{2,1,0:T(8,128)(2,1)S(1)}, bf16[3,512,128]{2,1,0:T(8,128)(2,1)S(1)}, bf16[128,1024]{1,0:T(8,...) custom-call(s32[1]{0:T(128)} %bitcast.index_ref.refs_0_, ...), custom_call_target="tpu_custom_call" | custom-call | flops 1000000000 | bytes 4194304 | tf_op jit(solution)/shard_map/prepare/pallas_call | solution.py:224
  3.7 0.5 collective-permute-start
  4.2 0.0 copy-done
  4.2 5.7 %collective-permute-start.1 = (bf16[64,1024]{1,0:T(8,128)(2,1)S(1)}, bf16[64,1024]{1,0:T(8,128)(2,1)S(1)}, u32[]{:S(2)}, u32[]{:S(2)}) collective-permute-start(bf16[64,1024]{1,0:T(8,128)(2,1)S(1)} %copy-done), channel_id=1, source_target_pairs={{0,15},{1,2},{2,1},{3,4},{4,3},{5,6},{6,5},{7,8},{8,7},{9,10},{10,... | collective-permute-start | bytes 393224 | tf_op jit(solution)/shard_map/ppermute | solution.py:263
  9.9 0.0 collective-permute-done.refs_3_.refs_2_
  9.9 0.8 %own.4 = (f32[64,1024]{1,0:T(8,128)S(1)}, bf16[64,256]{1,0:T(8,128)(2,1)S(1)}) custom-call(bf16[64,1024]{1,0:T(8,128)(2,1)S(1)} %get-tuple-element.32.refs_0_, bf16[36,256,256]{2,1,0:T(8,128)(2,1)S(1)} %get-tuple-element.33.refs_1_.refs_4_, f32[64,256]{1,0:T(8,128)S(1)} %get-tuple-element.34.refs_2_, bf16[64,1536]{1,0:T(8,128)(2,1)S(1)} %collective-permute-done.refs_3_.refs_2_), custom_call_target="tpu_custom_call" | custom-call | flops 1000000000 | bytes 4194304 | tf_op jit(solution)/shard_map/own/pallas_call | solution.py:224
  10.7 0.1 collective-permute-start.2
  10.7 4.8 %collective-permute-done.2.refs_8_ = bf16[64,256]{1,0:T(8,128)(2,1)S(1)} collective-permute-done((bf16[64,256]{1,0:T(8,128)(2,1)S(1)}, bf16[64,256]{1,0:T(8,128)(2,1)S(1)}, u32[]{:S(2)}, u32[]{:S(2)}) %collective-permute-start.2) | collective-permute-done | bytes 32800 | tf_op jit(solution)/shard_map/ppermute | solution.py:309
  15.5 0.0 collective-permute-start.3
  15.5 0.0 collective-permute-done.1.refs_3_
  15.5 1.2 %collective-permute-done.3.refs_9_ = bf16[64,256]{1,0:T(8,128)(2,1)S(1)} collective-permute-done((bf16[64,256]{1,0:T(8,128)(2,1)S(1)}, bf16[64,256]{1,0:T(8,128)(2,1)S(1)}, u32[]{:S(2)}, u32[]{:S(2)}) %collective-permute-start.3) | collective-permute-done | bytes 32800 | tf_op jit(solution)/shard_map/ppermute | solution.py:310
  16.7 1.5 %finish.3 = (bf16[64,1024]{1,0:T(8,128)(2,1)S(1)}, bf16[64,1536]{1,0:T(8,128)(2,1)S(1)}, f32[64,256]{1,0:T(8,128)S(1)}) custom-call(s32[1]{0:T(128)} %bitcast.index_ref.refs_0_, f32[64,1024]{1,0:T(8,128)S(1)} %get-tuple-element.36.refs_1_, bf16[64,1536]{1,0:T(8,128)(2,1)S(1)} %collective-permute-done.refs_3_.refs_2_, ...), custom_call_target="tpu_custom_call" | custom-call | flops 1000000000 | bytes 4194304 | tf_op jit(solution)/shard_map/finish/pallas_call | solution.py:224
  18.2 0.2 collective-permute-start.4
  18.4 2.9 %collective-permute-start.5 = (bf16[64,1024]{1,0:T(8,128)(2,1)S(1)}, bf16[64,1024]{1,0:T(8,128)(2,1)S(1)}, u32[]{:S(2)}, u32[]{:S(2)}) collective-permute-start(bf16[64,1024]{1,0:T(8,128)(2,1)S(1)} %get-tuple-element.41.refs_0_), channel_id=1, source_target_pairs={{0,15},{1,2},{2,1},{3,4},{4,3},{5,6},{6,5},{7,8},{8,7},{9,10},{10,... | collective-permute-start | bytes 393224 | tf_op jit(solution)/shard_map/ppermute | solution.py:263
  21.3 0.0 collective-permute-done.4.refs_3_.refs_2_
  21.3 0.8 %own.5 = (f32[64,1024]{1,0:T(8,128)S(1)}, bf16[64,256]{1,0:T(8,128)(2,1)S(1)}, bf16[4,64,1024]{2,1,0:T(8,128)(2,1)}) custom-call(bf16[64,1024]{1,0:T(8,128)(2,1)S(1)} %get-tuple-element.41.refs_0_, bf16[36,256,256]{2,1,0:T(8,128)(2,1)S(1)} %get-tuple-element.33.refs_1_.refs_4_, f32[64,256]{1,0:T(8,128)S(1)} %get-tuple-element.42.refs_2_, ...), custom_call_target="tpu_custom_call" | custom-call | flops 1000000000 | bytes 4194304 | tf_op jit(solution)/shard_map/own/pallas_call | solution.py:224
  22.1 0.1 collective-permute-start.6
  22.1 4.8 %collective-permute-done.6.refs_8_ = bf16[64,256]{1,0:T(8,128)(2,1)S(1)} collective-permute-done((bf16[64,256]{1,0:T(8,128)(2,1)S(1)}, bf16[64,256]{1,0:T(8,128)(2,1)S(1)}, u32[]{:S(2)}, u32[]{:S(2)}) %collective-permute-start.6) | collective-permute-done | bytes 32800 | tf_op jit(solution)/shard_map/ppermute | solution.py:309
  26.9 0.0 collective-permute-start.7
  26.9 0.0 collective-permute-done.5.refs_3_
  26.9 1.2 %collective-permute-done.7.refs_9_ = bf16[64,256]{1,0:T(8,128)(2,1)S(1)} collective-permute-done((bf16[64,256]{1,0:T(8,128)(2,1)S(1)}, bf16[64,256]{1,0:T(8,128)(2,1)S(1)}, u32[]{:S(2)}, u32[]{:S(2)}) %collective-permute-start.7) | collective-permute-done | bytes 32800 | tf_op jit(solution)/shard_map/ppermute | solution.py:310
  28.1 1.4 %finish.4 = (bf16[64,1024]{1,0:T(8,128)(2,1)S(1)}, bf16[64,1536]{1,0:T(8,128)(2,1)S(1)}, f32[64,256]{1,0:T(8,128)S(1)}) custom-call(s32[1]{0:T(128)} %bitcast.index_ref.refs_0_, f32[64,1024]{1,0:T(8,128)S(1)} %get-tuple-element.44.refs_1_, bf16[64,1536]{1,0:T(8,128)(2,1)S(1)} %collective-permute-done.4.refs_3_.refs_2_, ...), custom_call_target="tpu_custom_call" | custom-call | flops 1000000000 | bytes 4194304 | tf_op jit(solution)/shard_map/finish/pallas_call | solution.py:224
  29.6 0.2 collective-permute-start.8
  29.8 2.8 %collective-permute-start.9 = (bf16[64,1024]{1,0:T(8,128)(2,1)S(1)}, bf16[64,1024]{1,0:T(8,128)(2,1)S(1)}, u32[]{:S(2)}, u32[]{:S(2)}) collective-permute-start(bf16[64,1024]{1,0:T(8,128)(2,1)S(1)} %get-tuple-element.46.refs_0_), channel_id=1, source_target_pairs={{0,15},{1,2},{2,1},{3,4},{4,3},{5,6},{6,5},{7,8},{8,7},{9,10},{10,... | collective-permute-start | bytes 393224 | tf_op jit(solution)/shard_map/ppermute | solution.py:263
  32.7 0.0 collective-permute-done.8.refs_3_.refs_2_
  32.7 1.3 %own.6 = (f32[64,1024]{1,0:T(8,128)S(1)}, bf16[64,256]{1,0:T(8,128)(2,1)S(1)}, bf16[4,64,1024]{2,1,0:T(8,128)(2,1)}) custom-call(bf16[64,1024]{1,0:T(8,128)(2,1)S(1)} %get-tuple-element.46.refs_0_, bf16[36,256,256]{2,1,0:T(8,128)(2,1)S(1)} %get-tuple-element.33.refs_1_.refs_4_, ...), custom_call_target="tpu_custom_call", output_to_operand_aliasing={{2}: (4, {})} | custom-call | flops 1000000000 | bytes 4194304 | tf_op jit(solution)/shard_map/own/pallas_call | solution.py:224
  34.0 0.1 collective-permute-start.10
  34.0 4.8 %collective-permute-done.10.refs_8_ = bf16[64,256]{1,0:T(8,128)(2,1)S(1)} collective-permute-done((bf16[64,256]{1,0:T(8,128)(2,1)S(1)}, bf16[64,256]{1,0:T(8,128)(2,1)S(1)}, u32[]{:S(2)}, u32[]{:S(2)}) %collective-permute-start.10) | collective-permute-done | bytes 32800 | tf_op jit(solution)/shard_map/ppermute | solution.py:309
  38.8 0.0 collective-permute-start.11
  38.8 0.0 collective-permute-done.9.refs_3_
  38.9 1.2 %collective-permute-done.11.refs_9_ = bf16[64,256]{1,0:T(8,128)(2,1)S(1)} collective-permute-done((bf16[64,256]{1,0:T(8,128)(2,1)S(1)}, bf16[64,256]{1,0:T(8,128)(2,1)S(1)}, u32[]{:S(2)}, u32[]{:S(2)}) %collective-permute-start.11) | collective-permute-done | bytes 32800 | tf_op jit(solution)/shard_map/ppermute | solution.py:310
  40.1 1.5 %finish.5 = (bf16[64,1024]{1,0:T(8,128)(2,1)S(1)}, bf16[64,1536]{1,0:T(8,128)(2,1)S(1)}, f32[64,256]{1,0:T(8,128)S(1)}) custom-call(s32[1]{0:T(128)} %bitcast.index_ref.refs_0_, f32[64,1024]{1,0:T(8,128)S(1)} %get-tuple-element.50.refs_1_, bf16[64,1536]{1,0:T(8,128)(2,1)S(1)} %collective-permute-done.8.refs_3_.refs_2_, ...), custom_call_target="tpu_custom_call" | custom-call | flops 1000000000 | bytes 4194304 | tf_op jit(solution)/shard_map/finish/pallas_call | solution.py:224
  41.5 0.2 collective-permute-start.12
  41.7 2.3 %collective-permute-start.13 = (bf16[64,1024]{1,0:T(8,128)(2,1)S(1)}, bf16[64,1024]{1,0:T(8,128)(2,1)S(1)}, u32[]{:S(2)}, u32[]{:S(2)}) collective-permute-start(bf16[64,1024]{1,0:T(8,128)(2,1)S(1)} %get-tuple-element.52.refs_0_), channel_id=1, source_target_pairs={{0,15},{1,2},{2,1},{3,4},{4,3},{5,6},{6,5},{7,8},{8,7},{9,10},{10,... | collective-permute-start | bytes 393224 | tf_op jit(solution)/shard_map/ppermute | solution.py:263
  44.1 0.0 collective-permute-done.12.refs_3_.refs_2_
  44.1 1.3 %own.7 = (f32[64,1024]{1,0:T(8,128)S(1)}, bf16[64,256]{1,0:T(8,128)(2,1)S(1)}, bf16[4,64,1024]{2,1,0:T(8,128)(2,1)}) custom-call(bf16[64,1024]{1,0:T(8,128)(2,1)S(1)} %get-tuple-element.52.refs_0_, bf16[36,256,256]{2,1,0:T(8,128)(2,1)S(1)} %get-tuple-element.33.refs_1_.refs_4_, ...), custom_call_target="tpu_custom_call", output_to_operand_aliasing={{2}: (4, {})} | custom-call | flops 1000000000 | bytes 4194304 | tf_op jit(solution)/shard_map/own/pallas_call | solution.py:224
  45.4 0.1 collective-permute-start.14
  45.4 4.8 %collective-permute-done.14.refs_6_ = bf16[64,256]{1,0:T(8,128)(2,1)S(1)} collective-permute-done((bf16[64,256]{1,0:T(8,128)(2,1)S(1)}, bf16[64,256]{1,0:T(8,128)(2,1)S(1)}, u32[]{:S(2)}, u32[]{:S(2)}) %collective-permute-start.14) | collective-permute-done | bytes 32800 | tf_op jit(solution)/shard_map/ppermute | solution.py:309
  50.2 0.0 collective-permute-start.15
  50.2 0.0 collective-permute-done.13.refs_3_
  50.2 1.2 %collective-permute-done.15.refs_7_ = bf16[64,256]{1,0:T(8,128)(2,1)S(1)} collective-permute-done((bf16[64,256]{1,0:T(8,128)(2,1)S(1)}, bf16[64,256]{1,0:T(8,128)(2,1)S(1)}, u32[]{:S(2)}, u32[]{:S(2)}) %collective-permute-start.15) | collective-permute-done | bytes 32800 | tf_op jit(solution)/shard_map/ppermute | solution.py:310
  51.4 1.7 %last.1 = bf16[4,64,1024]{2,1,0:T(8,128)(2,1)} custom-call(s32[1]{0:T(128)} %bitcast.index_ref.refs_0_, f32[64,1024]{1,0:T(8,128)S(1)} %get-tuple-element.56.refs_1_, bf16[64,1536]{1,0:T(8,128)(2,1)S(1)} %collective-permute-done.12.refs_3_.refs_2_, bf16[64,1024]{1,0:T(8,128)(2,1)S(1)} %collective-permute-done.13.refs_3_, ...), custom_call_target="tpu_custom_call", output_to_operand_aliasing={{}: (8, {})} | custom-call | flops 1000000000 | bytes 4194304 | tf_op jit(solution)/shard_map/last/pallas_call | solution.py:224
Async XLA Ops:
  0.0 4.2 %copy-start = (bf16[64,1024]{1,0:T(8,128)(2,1)S(1)}, bf16[64,1024]{1,0:T(8,128)(2,1)}, u32[]{:S(2)}) copy-start(bf16[64,1024]{1,0:T(8,128)(2,1)} %refs_4_.1) | copy-start | bytes 393220
  3.7 6.2 %collective-permute-start = (bf16[64,1536]{1,0:T(8,128)(2,1)S(1)}, bf16[64,1536]{1,0:T(8,128)(2,1)S(1)}, u32[]{:S(2)}, u32[]{:S(2)}) collective-permute-start(bf16[64,1536]{1,0:T(8,128)(2,1)S(1)} %get-tuple-element.35), channel_id=1, source_target_pairs={{0,1},{1,0},{2,3},{3,2},{4,5},{5,4},{6,7},{7,6},{8,9},{9,8},{10,11... | collective-permute-start | bytes 589832 | tf_op jit(solution)/shard_map/ppermute | solution.py:291
  4.2 11.3 %collective-permute-start.1 = (bf16[64,1024]{1,0:T(8,128)(2,1)S(1)}, bf16[64,1024]{1,0:T(8,128)(2,1)S(1)}, u32[]{:S(2)}, u32[]{:S(2)}) collective-permute-start(bf16[64,1024]{1,0:T(8,128)(2,1)S(1)} %copy-done), channel_id=1, source_target_pairs={{0,15},{1,2},{2,1},{3,4},{4,3},{5,6},{6,5},{7,8},{8,7},{9,10},{10,... | collective-permute-start | bytes 393224 | tf_op jit(solution)/shard_map/ppermute | solution.py:263
  10.7 4.9 %collective-permute-start.2 = (bf16[64,256]{1,0:T(8,128)(2,1)S(1)}, bf16[64,256]{1,0:T(8,128)(2,1)S(1)}, u32[]{:S(2)}, u32[]{:S(2)}) collective-permute-start(bf16[64,256]{1,0:T(8,128)(2,1)S(1)} %get-tuple-element.40), channel_id=1, source_target_pairs={{0,8},{1,11},{2,10},{3,9},{4,12},{5,15},{6,14},{7,13},{8,0},{9,3},... | collective-permute-start | bytes 98312 | tf_op jit(solution)/shard_map/ppermute | solution.py:309
  15.5 1.2 %collective-permute-start.3 = (bf16[64,256]{1,0:T(8,128)(2,1)S(1)}, bf16[64,256]{1,0:T(8,128)(2,1)S(1)}, u32[]{:S(2)}, u32[]{:S(2)}) collective-permute-start(bf16[64,256]{1,0:T(8,128)(2,1)S(1)} %collective-permute-done.2.refs_8_), channel_id=1, source_target_pairs={{0,1},{1,0},{2,3},{3,2},{4,5},{5,4},{6,7},{7,6},{8,9},{9,8},{10,11... | collective-permute-start | bytes 98312 | tf_op jit(solution)/shard_map/ppermute | solution.py:310
  18.2 3.1 %collective-permute-start.4 = (bf16[64,1536]{1,0:T(8,128)(2,1)S(1)}, bf16[64,1536]{1,0:T(8,128)(2,1)S(1)}, u32[]{:S(2)}, u32[]{:S(2)}) collective-permute-start(bf16[64,1536]{1,0:T(8,128)(2,1)S(1)} %get-tuple-element.43), channel_id=1, source_target_pairs={{0,1},{1,0},{2,3},{3,2},{4,5},{5,4},{6,7},{7,6},{8,9},{9,8},{10,11... | collective-permute-start | bytes 589832 | tf_op jit(solution)/shard_map/ppermute | solution.py:291
  18.4 8.5 %collective-permute-start.5 = (bf16[64,1024]{1,0:T(8,128)(2,1)S(1)}, bf16[64,1024]{1,0:T(8,128)(2,1)S(1)}, u32[]{:S(2)}, u32[]{:S(2)}) collective-permute-start(bf16[64,1024]{1,0:T(8,128)(2,1)S(1)} %get-tuple-element.41.refs_0_), channel_id=1, source_target_pairs={{0,15},{1,2},{2,1},{3,4},{4,3},{5,6},{6,5},{7,8},{8,7},{9,10},{10,... | collective-permute-start | bytes 393224 | tf_op jit(solution)/shard_map/ppermute | solution.py:263
  22.1 4.9 %collective-permute-start.6 = (bf16[64,256]{1,0:T(8,128)(2,1)S(1)}, bf16[64,256]{1,0:T(8,128)(2,1)S(1)}, u32[]{:S(2)}, u32[]{:S(2)}) collective-permute-start(bf16[64,256]{1,0:T(8,128)(2,1)S(1)} %get-tuple-element.45), channel_id=1, source_target_pairs={{0,8},{1,11},{2,10},{3,9},{4,12},{5,15},{6,14},{7,13},{8,0},{9,3},... | collective-permute-start | bytes 98312 | tf_op jit(solution)/shard_map/ppermute | solution.py:309
  26.9 1.2 %collective-permute-start.7 = (bf16[64,256]{1,0:T(8,128)(2,1)S(1)}, bf16[64,256]{1,0:T(8,128)(2,1)S(1)}, u32[]{:S(2)}, u32[]{:S(2)}) collective-permute-start(bf16[64,256]{1,0:T(8,128)(2,1)S(1)} %collective-permute-done.6.refs_8_), channel_id=1, source_target_pairs={{0,1},{1,0},{2,3},{3,2},{4,5},{5,4},{6,7},{7,6},{8,9},{9,8},{10,11... | collective-permute-start | bytes 98312 | tf_op jit(solution)/shard_map/ppermute | solution.py:310
  29.6 3.1 %collective-permute-start.8 = (bf16[64,1536]{1,0:T(8,128)(2,1)S(1)}, bf16[64,1536]{1,0:T(8,128)(2,1)S(1)}, u32[]{:S(2)}, u32[]{:S(2)}) collective-permute-start(bf16[64,1536]{1,0:T(8,128)(2,1)S(1)} %get-tuple-element.48), channel_id=1, source_target_pairs={{0,1},{1,0},{2,3},{3,2},{4,5},{5,4},{6,7},{7,6},{8,9},{9,8},{10,11... | collective-permute-start | bytes 589832 | tf_op jit(solution)/shard_map/ppermute | solution.py:291
  29.8 9.0 %collective-permute-start.9 = (bf16[64,1024]{1,0:T(8,128)(2,1)S(1)}, bf16[64,1024]{1,0:T(8,128)(2,1)S(1)}, u32[]{:S(2)}, u32[]{:S(2)}) collective-permute-start(bf16[64,1024]{1,0:T(8,128)(2,1)S(1)} %get-tuple-element.46.refs_0_), channel_id=1, source_target_pairs={{0,15},{1,2},{2,1},{3,4},{4,3},{5,6},{6,5},{7,8},{8,7},{9,10},{10,... | collective-permute-start | bytes 393224 | tf_op jit(solution)/shard_map/ppermute | solution.py:263
  34.0 4.9 %collective-permute-start.10 = (bf16[64,256]{1,0:T(8,128)(2,1)S(1)}, bf16[64,256]{1,0:T(8,128)(2,1)S(1)}, u32[]{:S(2)}, u32[]{:S(2)}) collective-permute-start(bf16[64,256]{1,0:T(8,128)(2,1)S(1)} %get-tuple-element.51), channel_id=1, source_target_pairs={{0,8},{1,11},{2,10},{3,9},{4,12},{5,15},{6,14},{7,13},{8,0},{9,3},... | collective-permute-start | bytes 98312 | tf_op jit(solution)/shard_map/ppermute | solution.py:309
  38.8 1.2 %collective-permute-start.11 = (bf16[64,256]{1,0:T(8,128)(2,1)S(1)}, bf16[64,256]{1,0:T(8,128)(2,1)S(1)}, u32[]{:S(2)}, u32[]{:S(2)}) collective-permute-start(bf16[64,256]{1,0:T(8,128)(2,1)S(1)} %collective-permute-done.10.refs_8_), channel_id=1, source_target_pairs={{0,1},{1,0},{2,3},{3,2},{4,5},{5,4},{6,7},{7,6},{8,9},{9,8},{10,11... | collective-permute-start | bytes 98312 | tf_op jit(solution)/shard_map/ppermute | solution.py:310
  41.5 2.5 %collective-permute-start.12 = (bf16[64,1536]{1,0:T(8,128)(2,1)S(1)}, bf16[64,1536]{1,0:T(8,128)(2,1)S(1)}, u32[]{:S(2)}, u32[]{:S(2)}) collective-permute-start(bf16[64,1536]{1,0:T(8,128)(2,1)S(1)} %get-tuple-element.54), channel_id=1, source_target_pairs={{0,1},{1,0},{2,3},{3,2},{4,5},{5,4},{6,7},{7,6},{8,9},{9,8},{10,11... | collective-permute-start | bytes 589832 | tf_op jit(solution)/shard_map/ppermute | solution.py:291
  41.7 8.5 %collective-permute-start.13 = (bf16[64,1024]{1,0:T(8,128)(2,1)S(1)}, bf16[64,1024]{1,0:T(8,128)(2,1)S(1)}, u32[]{:S(2)}, u32[]{:S(2)}) collective-permute-start(bf16[64,1024]{1,0:T(8,128)(2,1)S(1)} %get-tuple-element.52.refs_0_), channel_id=1, source_target_pairs={{0,15},{1,2},{2,1},{3,4},{4,3},{5,6},{6,5},{7,8},{8,7},{9,10},{10,... | collective-permute-start | bytes 393224 | tf_op jit(solution)/shard_map/ppermute | solution.py:263
  45.4 4.9 %collective-permute-start.14 = (bf16[64,256]{1,0:T(8,128)(2,1)S(1)}, bf16[64,256]{1,0:T(8,128)(2,1)S(1)}, u32[]{:S(2)}, u32[]{:S(2)}) collective-permute-start(bf16[64,256]{1,0:T(8,128)(2,1)S(1)} %get-tuple-element.57), channel_id=1, source_target_pairs={{0,8},{1,11},{2,10},{3,9},{4,12},{5,15},{6,14},{7,13},{8,0},{9,3},... | collective-permute-start | bytes 98312 | tf_op jit(solution)/shard_map/ppermute | solution.py:309
  50.2 1.2 %collective-permute-start.15 = (bf16[64,256]{1,0:T(8,128)(2,1)S(1)}, bf16[64,256]{1,0:T(8,128)(2,1)S(1)}, u32[]{:S(2)}, u32[]{:S(2)}) collective-permute-start(bf16[64,256]{1,0:T(8,128)(2,1)S(1)} %collective-permute-done.14.refs_6_), channel_id=1, source_target_pairs={{0,1},{1,0},{2,3},{3,2},{4,5},{5,4},{6,7},{7,6},{8,9},{9,8},{10,11... | collective-permute-start | bytes 98312 | tf_op jit(solution)/shard_map/ppermute | solution.py:310

commit v4 on v3

--- a/solution.py
+++ b/solution.py
@@ -105,60 +105,45 @@
                 dot_nt(panels[c], d_ref[r * SPAN + c - r + REACH]) for c in range(self.per_device)
             )
 
-    def next_block(self, index_ref, acc_ref, near_ref, over_ref, d_ref, rb_ref, far_refs):
-        both = jnp.concatenate(halves(self.far_sum(index_ref, far_refs)), axis=1)
+    def halo_sums(self, index_ref, acc_ref, near_ref, over_ref, d_ref, out_ref):
         odd = lax.rem(index_ref[0], 2) == 1
         low, high = [], []
         for c in range(self.per_device):
             near, over = self.panel(near_ref, c), self.panel(over_ref, c)
             low.append(jnp.where(odd, near, over))
             high.append(jnp.where(odd, over, near))
-        parts = []
         for r in range(self.per_device):
-            value = self.panel(acc_ref, r) + dot_nn(both, self.panel(rb_ref, r))
+            value = self.panel(acc_ref, r)
             for c in range(self.per_device):
                 for panel, place in ((low[c], c - self.per_device), (high[c], c + self.per_device)):
                     offset = place - r
                     if -REACH <= offset <= REACH:
                         value = value + dot_nt(panel, d_ref[r * SPAN + offset + REACH])
-            parts.append(value.astype(BF16))
-        return jnp.concatenate(parts, axis=1)
+            out_ref[:, r * self.size : (r + 1) * self.size] = value
+
+    def next_block(self, index_ref, acc_ref, rb_ref, far_refs):
+        both = jnp.concatenate(halves(self.far_sum(index_ref, far_refs)), axis=1)
+        return (acc_ref[...] + dot_nn(both, rb_ref[...])).astype(BF16)
 
 
 def prepare_kernel(plan, index_ref, *refs):
-    sources, refs = refs[:9], refs[9:]
-    x_ref, d_ref, g_ref, cb_ref, rb_ref = refs[:5]
-    sends, held, (present, sems, tile_sems) = refs[5:-10], refs[-10:-3], refs[-3:]
-    rows_ref, cols_ref, near_rows_ref, offsets_ref, col_ref, coup_ref, row_ref = held
-    tiles_hbm = sources[8]
-    targets = (near_rows_ref, offsets_ref, rows_ref, cols_ref, x_ref, col_ref, coup_ref, row_ref)
+    sources, refs = refs[:5], refs[5:]
+    x_ref, g_ref, cb_ref = refs[:3]
+    sends, (rows_ref, cols_ref, col_ref, coup_ref, sems) = refs[3:-5], refs[-5:]
+    targets = (rows_ref, cols_ref, x_ref, col_ref, coup_ref)
     copies = [
         pltpu.make_async_copy(source, target, sems.at[i])
-        for i, (source, target) in enumerate(zip(sources[:8], targets))
+        for i, (source, target) in enumerate(zip(sources, targets))
     ]
     for copy in copies:
         copy.start()
     rank, size = plan.rank, plan.size
     cb_ref[...] = jnp.zeros_like(cb_ref)
-    rb_ref[...] = jnp.zeros_like(rb_ref)
     g_ref[...] = jnp.zeros_like(g_ref)
-    for cell in range(plan.cells):
-        present[cell] = 0
-    copies[0].wait()
-    copies[1].wait()
-    tiles = []
-    for s in range(plan.tiles):
-        cell = near_rows_ref[s] * SPAN + offsets_ref[s] + REACH
-        present[cell] = 1
-        tiles.append(pltpu.make_async_copy(tiles_hbm.at[s], d_ref.at[cell], tile_sems.at[s]))
-        tiles[-1].start()
-    for copy in copies[2:]:
+    for copy in copies:
         copy.wait()
     for c in range(plan.per_device):
-        columns = slice(c * size, (c + 1) * size)
-        cb_ref[c * rank : (c + 1) * rank, columns] = col_ref[c]
-        for start in (c * rank, plan.width + c * rank):
-            rb_ref[start : start + rank, columns] = row_ref[c]
+        cb_ref[c * rank : (c + 1) * rank, c * size : (c + 1) * size] = col_ref[c]
     column = lax.broadcasted_iota(jnp.int32, (rank, plan.width), 1) // rank
     shift = 0 if plan.paired else plan.member(index_ref)
     for s in range(plan.slots):
@@ -171,6 +156,35 @@
         wide = jnp.where(column == cols_ref[s], jnp.concatenate([tile] * plan.per_device, axis=1), 0.0)
         g_ref[where] = g_ref[where] + wide.astype(BF16)
     plan.send_far(index_ref, x_ref[...], cb_ref, g_ref, sends)
+
+
+def relay_kernel(plan, keep_ref, message_ref, out_ref):
+    plan.relay_far(keep_ref, message_ref, out_ref)
+
+
+def first_own_kernel(plan, *refs):
+    x_ref, rows_hbm, offsets_hbm, row_hbm, tiles_hbm = refs[:5]
+    acc_ref, d_ref, rb_ref, rows_ref, offsets_ref, row_ref, present, sems, tile_sems = refs[-9:]
+    pairs = ((rows_hbm, rows_ref), (offsets_hbm, offsets_ref), (row_hbm, row_ref))
+    copies = [pltpu.make_async_copy(*pair, sems.at[i]) for i, pair in enumerate(pairs)]
+    for copy in copies:
+        copy.start()
+    rb_ref[...] = jnp.zeros_like(rb_ref)
+    for cell in range(plan.cells):
+        present[cell] = 0
+    copies[0].wait()
+    copies[1].wait()
+    tiles = []
+    for s in range(plan.tiles):
+        cell = rows_ref[s] * SPAN + offsets_ref[s] + REACH
+        present[cell] = 1
+        tiles.append(pltpu.make_async_copy(tiles_hbm.at[s], d_ref.at[cell], tile_sems.at[s]))
+        tiles[-1].start()
+    copies[2].wait()
+    rank, size = plan.rank, plan.size
+    for c in range(plan.per_device):
+        for start in (c * rank, plan.width + c * rank):
+            rb_ref[start : start + rank, c * size : (c + 1) * size] = row_ref[c]
     for copy in tiles:
         copy.wait()
 
@@ -180,36 +194,34 @@
         def _():
             d_ref[cell] = jnp.zeros(d_ref.shape[1:], d_ref.dtype)
 
+    plan.own_sums(x_ref, d_ref, acc_ref)
+
 
 def own_kernel(plan, slot, *refs):
-    x_ref, d_ref, *refs = refs
-    if plan.paired:
-        keep_ref, message_ref, *refs = refs
-    if slot is not None:
-        *refs, sem = refs
-        krylov_ref = refs[-1]
-        copy = pltpu.make_async_copy(x_ref, krylov_ref.at[slot], sem)
-        copy.start()
-        refs = refs[1:-1] if slot else refs[:-1]
-    if plan.paired:
-        plan.relay_far(keep_ref, message_ref, refs[1])
-    plan.own_sums(x_ref, d_ref, refs[0])
-    if slot is not None:
-        copy.wait()
+    x_ref, d_ref = refs[:2]
+    acc_ref, krylov_ref, sem = refs[-3:]
+    copy = pltpu.make_async_copy(x_ref, krylov_ref.at[slot], sem)
+    copy.start()
+    plan.own_sums(x_ref, d_ref, acc_ref)
+    copy.wait()
+
+
+def halo_kernel(plan, index_ref, acc_ref, near_ref, over_ref, d_ref, *refs):
+    plan.halo_sums(index_ref, acc_ref, near_ref, over_ref, d_ref, refs[-1])
 
 
 def finish_kernel(plan, fars, *refs):
-    index_ref, acc_ref, near_ref, over_ref, d_ref, rb_ref, cb_ref, g_ref = refs[:8]
-    far_refs, (x_ref, *sends) = refs[8 : 8 + fars], refs[8 + fars :]
-    x = plan.next_block(index_ref, acc_ref, near_ref, over_ref, d_ref, rb_ref, far_refs)
+    index_ref, acc_ref, rb_ref, cb_ref, g_ref = refs[:5]
+    far_refs, (x_ref, *sends) = refs[5 : 5 + fars], refs[5 + fars :]
+    x = plan.next_block(index_ref, acc_ref, rb_ref, far_refs)
     x_ref[...] = x
     plan.send_far(index_ref, x, cb_ref, g_ref, sends)
 
 
 def last_kernel(plan, fars, slot, *refs):
-    index_ref, acc_ref, near_ref, over_ref, d_ref, rb_ref = refs[:6]
-    far_refs, (_, krylov_ref, x_ref, sem) = refs[6 : 6 + fars], refs[6 + fars :]
-    x_ref[...] = plan.next_block(index_ref, acc_ref, near_ref, over_ref, d_ref, rb_ref, far_refs)
+    index_ref, acc_ref, rb_ref = refs[:3]
+    far_refs, (_, krylov_ref, x_ref, sem) = refs[3 : 3 + fars], refs[3 + fars :]
+    x_ref[...] = plan.next_block(index_ref, acc_ref, rb_ref, far_refs)
     copy = pltpu.make_async_copy(x_ref, krylov_ref.at[slot], sem)
     copy.start()
     copy.wait()
@@ -254,63 +266,83 @@
     else:
         sends_out = [pltpu.VMEM((rhs, width), BF16)] * len(plan.routes)
     index = lax.axis_index(axes).astype(jnp.int32).reshape(1)
-    smem = [pltpu.SMEM(v.shape, jnp.int32) for v in (far_rows, far_cols, near_rows, near_offsets)]
-    vmem = [pltpu.VMEM(v.shape, BF16) for v in (col_basis, couplings, row_basis)]
-
-    current = block
-    krylov = None
+
+    def scratch_for(*arrays):
+        return [
+            pltpu.SMEM(v.shape, v.dtype) if v.dtype == jnp.int32 else pltpu.VMEM(v.shape, v.dtype)
+            for v in arrays
+        ]
+
+    current, sends, krylov = block, None, None
     for product in range(PRODUCTS):
-        over = lax.ppermute(current, axes, plan.over)
         if product == 0:
-            ins = [near_rows, near_offsets, far_rows, far_cols]
-            ins += [block, col_basis, couplings, row_basis, near_tiles]
-            current, dense, coupled, col_wide, row_wide, *sends = call(
+            ins = [far_rows, far_cols, block, col_basis, couplings]
+            current, coupled, col_wide, *sends = call(
                 functools.partial(prepare_kernel, plan),
                 "prepare",
                 [index, *ins],
-                [IN_SMEM] + [IN_HBM] * 9,
+                [IN_SMEM] + [IN_HBM] * 5,
                 [
                     block_out,
-                    pltpu.VMEM((plan.cells, plan.size, plan.size), BF16),
                     pltpu.VMEM((LEVELS, plan.members * width, width), BF16),
                     pltpu.VMEM((width, shard_len), BF16),
-                    pltpu.VMEM((2 * width, shard_len), BF16),
                     *sends_out,
                 ],
-                scratch=[
-                    *smem,
-                    *vmem,
+                scratch=scratch_for(far_rows, far_cols, col_basis, couplings)
+                + [pltpu.SemaphoreType.DMA((5,))],
+            )
+        near = lax.ppermute(sends[0] if plan.paired else current, axes, plan.near)
+        over = lax.ppermute(block if product == 0 else current, axes, plan.over)
+        if plan.paired:
+            (relayed,) = call(
+                functools.partial(relay_kernel, plan), "relay", [sends[1], near], [IN_VMEM] * 2, [relay_out]
+            )
+            fars = [lax.ppermute(relayed, axes, plan.across)]
+        else:
+            fars = [lax.ppermute(s, axes, route) for s, route in zip(sends, plan.routes)]
+        after = [relayed] if plan.paired else []
+        if product == 0:
+            acc, dense, row_wide = call(
+                functools.partial(first_own_kernel, plan),
+                "first_own",
+                [current, near_rows, near_offsets, row_basis, near_tiles, *after],
+                [IN_VMEM] + [IN_HBM] * 4 + [ANYWHERE] * len(after),
+                [
+                    acc_out,
+                    pltpu.VMEM((plan.cells, plan.size, plan.size), BF16),
+                    pltpu.VMEM((2 * width, shard_len), BF16),
+                ],
+                scratch=scratch_for(near_rows, near_offsets, row_basis)
+                + [
                     pltpu.SMEM((plan.cells,), jnp.int32),
-                    pltpu.SemaphoreType.DMA((8,)),
+                    pltpu.SemaphoreType.DMA((3,)),
                     pltpu.SemaphoreType.DMA((plan.tiles,)),
                 ],
             )
-        ins, outs = [current, dense], [acc_out]
+        else:
+            ins = [current, dense, *after] + ([krylov] if product > 1 else [])
+            acc, krylov = call(
+                functools.partial(own_kernel, plan, product - 1),
+                "own",
+                ins,
+                [IN_VMEM] * 2 + [ANYWHERE] * (len(ins) - 2),
+                [acc_out, krylov_out],
+                [IN_VMEM, ANYWHERE],
+                [pltpu.SemaphoreType.DMA],
+                {len(ins) - 1: 1} if product > 1 else None,
+            )
+        after = list(fars) if plan.paired else []
         if plan.paired:
-            message, keep = sends
-            near = lax.ppermute(message, axes, plan.near)
-            ins, outs = ins + [keep, near], outs + [relay_out]
-        else:
-            near = lax.ppermute(current, axes, plan.near)
-            fars = [lax.ppermute(s, axes, route) for s, route in zip(sends, plan.routes)]
-        specs, out_specs, scratch, aliases = [IN_VMEM] * len(ins), [IN_VMEM] * len(outs), [], None
-        if product > 0:
-            scratch, out_specs, outs = [pltpu.SemaphoreType.DMA], out_specs + [ANYWHERE], outs + [krylov_out]
-        if product > 1:
-            aliases = {len(ins): len(outs) - 1}
-            ins, specs = ins + [krylov], specs + [ANYWHERE]
-        slot = product - 1 if product else None
-        acc, *rest = call(
-            functools.partial(own_kernel, plan, slot), "own", ins, specs, outs, out_specs, scratch, aliases
+            fars.append(lax.ppermute(fars[0], axes, plan.near))
+        (acc,) = call(
+            functools.partial(halo_kernel, plan),
+            "halo",
+            [index, acc, near, over, dense, *after],
+            [IN_SMEM] + [IN_VMEM] * 4 + [ANYWHERE] * len(after),
+            [acc_out],
         )
-        if product > 0:
-            *rest, krylov = rest
-        if plan.paired:
-            received = lax.ppermute(rest[0], axes, plan.across)
-            fars = [received, lax.ppermute(received, axes, plan.near)]
-        ins = [index, acc, near, over, dense, row_wide]
         if product < PRODUCTS - 1:
-            ins += [col_wide, coupled, *fars]
+            ins = [index, acc, row_wide, col_wide, coupled, *fars]
             current, *sends = call(
                 functools.partial(finish_kernel, plan, len(fars)),
                 "finish",
@@ -319,7 +351,7 @@
                 [block_out, *sends_out],
             )
         else:
-            ins += [*fars, krylov]
+            ins = [index, acc, row_wide, *fars, krylov]
             (krylov,) = call(
                 functools.partial(last_kernel, plan, len(fars), product),
                 "last",

time: 53.3 us -> 46 us (0.86)
  waiting for transfers between devices: 24 us -> 12.3 us
  starting transfers between devices: 15.2 us -> 18.2 us
  Pallas kernels: 13.8 us -> 15.1 us
    ppermute x16, waiting for transfers between devices: 24 us -> 12.3 us  [the longest x4 11.8 us: on_device(): fars = [lax.ppermute(relayed, axes, plan.across)]]
    ppermute x16, starting transfers between devices: 15.2 us -> 18.2 us  [the longest x4 15.2 us: on_device(): over = lax.ppermute(block if product == 0 else current, axes, plan.over)]
    pallas_call x9 -> x17, Pallas kernels: 13.8 us -> 15.1 us  [call(): pl.pallas_call(kernel, in_specs=list(specs), out_specs=out_specs or [IN_V...]
  transfers between devices with their start and end apart: 16 -> 16, of which waited for: 8 -> 7; matrix products, arithmetic and copies ran while one was open for 0% -> 0% of each run, Pallas kernels for 8% -> 23%
where the time goes in v4:
time: 46 us; the launch traced here: 45.8 us
  starting transfers between devices  18.2 us (40%)
  Pallas kernels  15.1 us (33%)
  waiting for transfers between devices  12.3 us (27%)
    ppermute x4, starting transfers between devices, on_device(): over = lax.ppermute(block if product == 0 else current, axes, plan.over)  15.2 us
    pallas_call x17, Pallas kernels, call(): pl.pallas_call(kernel, in_specs=list(specs), out_specs=out_specs or [IN_V...  15.1 us
    ppermute x4, waiting for transfers between devices, on_device(): fars = [lax.ppermute(relayed, axes, plan.across)]  11.8 us
    ppermute x4, starting transfers between devices, on_device(): near = lax.ppermute(sends[0] if plan.paired else current, axes, plan.near)  1.4 us
  transfers between devices with their start and end apart: 16, of which 7 were waited for; matrix products, arithmetic and copies ran while one was open for 0% of the time, Pallas kernels for 23%

profile of v4, /device:TPU:0, one launch (start us, length us, event | category | flops | bytes accessed | tf_op | source)
XLA Modules:
  0.0 45.8 jit_solution(5976306694069583572)
XLA Ops:
  0.0 1.8 %prepare.1 = (bf16[64,1024]{1,0:T(8,128)(2,1)S(1)}, bf16[3,512,128]{2,1,0:T(8,128)(2,1)S(1)}, bf16[128,1024]{1,0:T(8,128)(2,1)S(1)}, bf16[64,1536]{1,0:T(8,128)(2,1)S(1)}, f32[64,256]{1,0:T(8,128)S(1)}) custom-call(s32[1]{0:T(128)} %bitcast.index_ref.refs_0_, s32[32]{0:T(128)} %refs_0_.1, s32[32]{0:T(128)} %refs_1_.2, bf16[64,1024]{1,0:T(8,128)(2,1)} %refs_2_.2, ...), custom_call_target="tpu_custom_call" | custom-call | flops 1000000000 | bytes 4194304 | tf_op jit(solution)/shard_map/prepare/pallas_call | solution.py:236
  1.8 0.5 %collective-permute-start = (bf16[64,1536]{1,0:T(8,128)(2,1)S(1)}, bf16[64,1536]{1,0:T(8,128)(2,1)S(1)}, u32[]{:S(2)}, u32[]{:S(2)}) collective-permute-start(bf16[64,1536]{1,0:T(8,128)(2,1)S(1)} %get-tuple-element.30), channel_id=1, source_target_pairs={{0,1},{1,0},{2,3},{3,2},{4,5},{5,4},{6,7},{7,6},{8,9},{9,8},{10,11... | collective-permute-start | bytes 589832 | tf_op jit(solution)/shard_map/ppermute | solution.py:294
  2.3 5.6 %collective-permute-start.1 = (bf16[64,1024]{1,0:T(8,128)(2,1)}, bf16[64,1024]{1,0:T(8,128)(2,1)S(1)}, u32[]{:S(2)}, u32[]{:S(2)}) collective-permute-start(bf16[64,1024]{1,0:T(8,128)(2,1)} %refs_2_.2), channel_id=1, source_target_pairs={{0,15},{1,2},{2,1},{3,4},{4,3},{5,6},{6,5},{7,8},{8,7},{9,10},{10,... | collective-permute-start | bytes 393224 | tf_op jit(solution)/shard_map/ppermute | solution.py:295
  7.9 0.0 collective-permute-done.message_ref.near_ref
  7.9 0.1 collective-permute-start.2
  8.0 4.5 %first_own.1 = (f32[64,1024]{1,0:T(8,128)S(1)}, bf16[36,256,256]{2,1,0:T(8,128)(2,1)S(1)}, bf16[256,1024]{1,0:T(8,128)(2,1)S(1)}) custom-call(bf16[64,1024]{1,0:T(8,128)(2,1)S(1)} %get-tuple-element.28.refs_0_, s32[32]{0:T(128)} %refs_1_.3, s32[32]{0:T(128)} %refs_2_.3, bf16[4,32,256]{2,1,0:T(8,128)(2,1)} %refs_3_.3, bf16[32,256,256]{2,1,0:T(8,128)(2,1)} %refs_4_.3, ...), custom_call_target="tpu_custom_call" | custom-call | flops 1000000000 | bytes 4194304 | tf_op jit(solution)/shard_map/first_own/pallas_call | solution.py:236
  12.5 0.3 collective-permute-done.2.refs_0_.refs_5_
  12.8 0.1 collective-permute-start.3
  12.9 0.0 collective-permute-done.1.over_ref
  12.9 0.9 %halo.4.refs_1_ = f32[64,1024]{1,0:T(8,128)S(1)} custom-call(s32[1]{0:T(128)} %bitcast.index_ref.refs_0_, f32[64,1024]{1,0:T(8,128)S(1)} %get-tuple-element.31.acc_ref, bf16[64,1536]{1,0:T(8,128)(2,1)S(1)} %collective-permute-done.message_ref.near_ref, bf16[64,1024]{1,0:T(8,128)(2,1)S(1)} %collective-permute-done.1.over_ref, ...), custom_call_target="tpu_custom_call" | custom-call | flops 1000000000 | bytes 4194304 | tf_op jit(solution)/shard_map/halo/pallas_call | solution.py:236
  13.8 0.2 collective-permute-done.3.refs_6_
  14.0 0.7 %finish.3 = (bf16[64,1024]{1,0:T(8,128)(2,1)S(1)}, bf16[64,1536]{1,0:T(8,128)(2,1)S(1)}, f32[64,256]{1,0:T(8,128)S(1)}) custom-call(s32[1]{0:T(128)} %bitcast.index_ref.refs_0_, f32[64,1024]{1,0:T(8,128)S(1)} %halo.4.refs_1_, bf16[256,1024]{1,0:T(8,128)(2,1)S(1)} %get-tuple-element.33.refs_2_, bf16[128,1024]{1,0:T(8,128)(2,1)S(1)} %get-tuple-element.34.refs_3_, ...), custom_call_target="tpu_custom_call" | custom-call | flops 1000000000 | bytes 4194304 | tf_op jit(solution)/shard_map/finish/pallas_call | solution.py:236
  14.7 0.3 collective-permute-start.4
  15.0 3.2 %collective-permute-start.5 = (bf16[64,1024]{1,0:T(8,128)(2,1)S(1)}, bf16[64,1024]{1,0:T(8,128)(2,1)S(1)}, u32[]{:S(2)}, u32[]{:S(2)}) collective-permute-start(bf16[64,1024]{1,0:T(8,128)(2,1)S(1)} %get-tuple-element.36.refs_0_), channel_id=1, source_target_pairs={{0,15},{1,2},{2,1},{3,4},{4,3},{5,6},{6,5},{7,8},{8,7},{9,10},{10,... | collective-permute-start | bytes 393224 | tf_op jit(solution)/shard_map/ppermute | solution.py:295
  18.2 0.0 collective-permute-done.4.message_ref.near_ref
  18.3 0.7 %collective-permute-start.6 = (bf16[64,256]{1,0:T(8,128)(2,1)S(1)}, bf16[64,256]{1,0:T(8,128)(2,1)S(1)}, u32[]{:S(2)}, u32[]{:S(2)}) collective-permute-start(bf16[64,256]{1,0:T(8,128)(2,1)S(1)} %relay.5.refs_2_), channel_id=1, source_target_pairs={{0,8},{1,11},{2,10},{3,9},{4,12},{5,15},{6,14},{7,13},{8,0},{9,3},... | collective-permute-start | bytes 98312 | tf_op jit(solution)/shard_map/ppermute | solution.py:300
  19.0 0.8 %own.3 = (f32[64,1024]{1,0:T(8,128)S(1)}, bf16[4,64,1024]{2,1,0:T(8,128)(2,1)}) custom-call(bf16[64,1024]{1,0:T(8,128)(2,1)S(1)} %get-tuple-element.36.refs_0_, bf16[36,256,256]{2,1,0:T(8,128)(2,1)S(1)} %get-tuple-element.32.d_ref.refs_1_, bf16[64,256]{1,0:T(8,128)(2,1)S(1)} %relay.5.refs_2_), custom_call_target="tpu_custom_call" | custom-call | flops 1000000000 | bytes 4194304 | tf_op jit(solution)/shard_map/own/pallas_call | solution.py:236
  19.7 3.4 %collective-permute-done.6.refs_0_.refs_5_ = bf16[64,256]{1,0:T(8,128)(2,1)S(1)} collective-permute-done((bf16[64,256]{1,0:T(8,128)(2,1)S(1)}, bf16[64,256]{1,0:T(8,128)(2,1)S(1)}, u32[]{:S(2)}, u32[]{:S(2)}) %collective-permute-start.6) | collective-permute-done | bytes 32800 | tf_op jit(solution)/shard_map/ppermute | solution.py:300
  23.1 0.2 collective-permute-start.7
  23.3 0.0 collective-permute-done.5.over_ref
  23.3 0.9 %halo.5.refs_1_ = f32[64,1024]{1,0:T(8,128)S(1)} custom-call(s32[1]{0:T(128)} %bitcast.index_ref.refs_0_, f32[64,1024]{1,0:T(8,128)S(1)} %get-tuple-element.39.acc_ref, bf16[64,1536]{1,0:T(8,128)(2,1)S(1)} %collective-permute-done.4.message_ref.near_ref, bf16[64,1024]{1,0:T(8,128)(2,1)S(1)} %collective-permute-done.5.over_ref, ...), custom_call_target="tpu_custom_call" | custom-call | flops 1000000000 | bytes 4194304 | tf_op jit(solution)/shard_map/halo/pallas_call | solution.py:236
  24.3 0.1 collective-permute-done.7.refs_6_
  24.4 0.7 %finish.4 = (bf16[64,1024]{1,0:T(8,128)(2,1)S(1)}, bf16[64,1536]{1,0:T(8,128)(2,1)S(1)}, f32[64,256]{1,0:T(8,128)S(1)}) custom-call(s32[1]{0:T(128)} %bitcast.index_ref.refs_0_, f32[64,1024]{1,0:T(8,128)S(1)} %halo.5.refs_1_, bf16[256,1024]{1,0:T(8,128)(2,1)S(1)} %get-tuple-element.33.refs_2_, bf16[128,1024]{1,0:T(8,128)(2,1)S(1)} %get-tuple-element.34.refs_3_, ...), custom_call_target="tpu_custom_call" | custom-call | flops 1000000000 | bytes 4194304 | tf_op jit(solution)/shard_map/finish/pallas_call | solution.py:236
  25.1 0.3 collective-permute-start.8
  25.3 3.2 %collective-permute-start.9 = (bf16[64,1024]{1,0:T(8,128)(2,1)S(1)}, bf16[64,1024]{1,0:T(8,128)(2,1)S(1)}, u32[]{:S(2)}, u32[]{:S(2)}) collective-permute-start(bf16[64,1024]{1,0:T(8,128)(2,1)S(1)} %get-tuple-element.40.refs_0_), channel_id=1, source_target_pairs={{0,15},{1,2},{2,1},{3,4},{4,3},{5,6},{6,5},{7,8},{8,7},{9,10},{10,... | collective-permute-start | bytes 393224 | tf_op jit(solution)/shard_map/ppermute | solution.py:295
  28.6 0.0 collective-permute-done.8.message_ref.near_ref
  28.6 0.1 collective-permute-start.10
  28.7 0.8 %own.4 = (f32[64,1024]{1,0:T(8,128)S(1)}, bf16[4,64,1024]{2,1,0:T(8,128)(2,1)}) custom-call(bf16[64,1024]{1,0:T(8,128)(2,1)S(1)} %get-tuple-element.40.refs_0_, bf16[36,256,256]{2,1,0:T(8,128)(2,1)S(1)} %get-tuple-element.32.d_ref.refs_1_, bf16[64,256]{1,0:T(8,128)(2,1)S(1)} %relay.6.refs_2_, ...), custom_call_target="tpu_custom_call", output_to_operand_aliasing={{1}: (3, {})} | custom-call | flops 1000000000 | bytes 4194304 | tf_op jit(solution)/shard_map/own/pallas_call | solution.py:236
  29.4 4.0 %collective-permute-done.10.refs_0_.refs_5_ = bf16[64,256]{1,0:T(8,128)(2,1)S(1)} collective-permute-done((bf16[64,256]{1,0:T(8,128)(2,1)S(1)}, bf16[64,256]{1,0:T(8,128)(2,1)S(1)}, u32[]{:S(2)}, u32[]{:S(2)}) %collective-permute-start.10) | collective-permute-done | bytes 32800 | tf_op jit(solution)/shard_map/ppermute | solution.py:300
  33.5 0.2 collective-permute-start.11
  33.6 0.0 collective-permute-done.9.over_ref
  33.6 0.9 %halo.6.refs_1_ = f32[64,1024]{1,0:T(8,128)S(1)} custom-call(s32[1]{0:T(128)} %bitcast.index_ref.refs_0_, f32[64,1024]{1,0:T(8,128)S(1)} %get-tuple-element.44.acc_ref, bf16[64,1536]{1,0:T(8,128)(2,1)S(1)} %collective-permute-done.8.message_ref.near_ref, bf16[64,1024]{1,0:T(8,128)(2,1)S(1)} %collective-permute-done.9.over_ref, ...), custom_call_target="tpu_custom_call" | custom-call | flops 1000000000 | bytes 4194304 | tf_op jit(solution)/shard_map/halo/pallas_call | solution.py:236
  34.5 0.1 collective-permute-done.11.refs_6_
  34.7 0.7 %finish.5 = (bf16[64,1024]{1,0:T(8,128)(2,1)S(1)}, bf16[64,1536]{1,0:T(8,128)(2,1)S(1)}, f32[64,256]{1,0:T(8,128)S(1)}) custom-call(s32[1]{0:T(128)} %bitcast.index_ref.refs_0_, f32[64,1024]{1,0:T(8,128)S(1)} %halo.6.refs_1_, bf16[256,1024]{1,0:T(8,128)(2,1)S(1)} %get-tuple-element.33.refs_2_, bf16[128,1024]{1,0:T(8,128)(2,1)S(1)} %get-tuple-element.34.refs_3_, ...), custom_call_target="tpu_custom_call" | custom-call | flops 1000000000 | bytes 4194304 | tf_op jit(solution)/shard_map/finish/pallas_call | solution.py:236
  35.4 0.3 collective-permute-start.12
  35.7 3.1 %collective-permute-start.13 = (bf16[64,1024]{1,0:T(8,128)(2,1)S(1)}, bf16[64,1024]{1,0:T(8,128)(2,1)S(1)}, u32[]{:S(2)}, u32[]{:S(2)}) collective-permute-start(bf16[64,1024]{1,0:T(8,128)(2,1)S(1)} %get-tuple-element.45.refs_0_), channel_id=1, source_target_pairs={{0,15},{1,2},{2,1},{3,4},{4,3},{5,6},{6,5},{7,8},{8,7},{9,10},{10,... | collective-permute-start | bytes 393224 | tf_op jit(solution)/shard_map/ppermute | solution.py:295
  38.8 0.0 collective-permute-done.12.message_ref.near_ref
  38.8 0.1 collective-permute-start.14
  38.9 0.8 %own.5 = (f32[64,1024]{1,0:T(8,128)S(1)}, bf16[4,64,1024]{2,1,0:T(8,128)(2,1)}) custom-call(bf16[64,1024]{1,0:T(8,128)(2,1)S(1)} %get-tuple-element.45.refs_0_, bf16[36,256,256]{2,1,0:T(8,128)(2,1)S(1)} %get-tuple-element.32.d_ref.refs_1_, bf16[64,256]{1,0:T(8,128)(2,1)S(1)} %relay.7.refs_2_, ...), custom_call_target="tpu_custom_call", output_to_operand_aliasing={{1}: (3, {})} | custom-call | flops 1000000000 | bytes 4194304 | tf_op jit(solution)/shard_map/own/pallas_call | solution.py:236
  39.7 4.0 %collective-permute-done.14.refs_0_.refs_3_ = bf16[64,256]{1,0:T(8,128)(2,1)S(1)} collective-permute-done((bf16[64,256]{1,0:T(8,128)(2,1)S(1)}, bf16[64,256]{1,0:T(8,128)(2,1)S(1)}, u32[]{:S(2)}, u32[]{:S(2)}) %collective-permute-start.14) | collective-permute-done | bytes 32800 | tf_op jit(solution)/shard_map/ppermute | solution.py:300
  43.7 0.3 collective-permute-start.15
  44.0 0.0 collective-permute-done.13.over_ref
  44.0 0.9 %halo.7.refs_1_ = f32[64,1024]{1,0:T(8,128)S(1)} custom-call(s32[1]{0:T(128)} %bitcast.index_ref.refs_0_, f32[64,1024]{1,0:T(8,128)S(1)} %get-tuple-element.49.acc_ref, bf16[64,1536]{1,0:T(8,128)(2,1)S(1)} %collective-permute-done.12.message_ref.near_ref, bf16[64,1024]{1,0:T(8,128)(2,1)S(1)} %collective-permute-done.13.over_ref, ...), custom_call_target="tpu_custom_call" | custom-call | flops 1000000000 | bytes 4194304 | tf_op jit(solution)/shard_map/halo/pallas_call | solution.py:236
  44.9 0.0 collective-permute-done.15.refs_4_
  44.9 0.9 %last.1 = bf16[4,64,1024]{2,1,0:T(8,128)(2,1)} custom-call(s32[1]{0:T(128)} %bitcast.index_ref.refs_0_, f32[64,1024]{1,0:T(8,128)S(1)} %halo.7.refs_1_, bf16[256,1024]{1,0:T(8,128)(2,1)S(1)} %get-tuple-element.33.refs_2_, bf16[64,256]{1,0:T(8,128)(2,1)S(1)} %collective-permute-done.14.refs_0_.refs_3_, ...), custom_call_target="tpu_custom_call", output_to_operand_aliasing={{}: (5, {})} | custom-call | flops 1000000000 | bytes 4194304 | tf_op jit(solution)/shard_map/last/pallas_call | solution.py:236
  (4 shorter events, 0.1 us)
Async XLA Ops:
  1.8 6.2 %collective-permute-start = (bf16[64,1536]{1,0:T(8,128)(2,1)S(1)}, bf16[64,1536]{1,0:T(8,128)(2,1)S(1)}, u32[]{:S(2)}, u32[]{:S(2)}) collective-permute-start(bf16[64,1536]{1,0:T(8,128)(2,1)S(1)} %get-tuple-element.30), channel_id=1, source_target_pairs={{0,1},{1,0},{2,3},{3,2},{4,5},{5,4},{6,7},{7,6},{8,9},{9,8},{10,11... | collective-permute-start | bytes 589832 | tf_op jit(solution)/shard_map/ppermute | solution.py:294
  2.3 10.6 %collective-permute-start.1 = (bf16[64,1024]{1,0:T(8,128)(2,1)}, bf16[64,1024]{1,0:T(8,128)(2,1)S(1)}, u32[]{:S(2)}, u32[]{:S(2)}) collective-permute-start(bf16[64,1024]{1,0:T(8,128)(2,1)} %refs_2_.2), channel_id=1, source_target_pairs={{0,15},{1,2},{2,1},{3,4},{4,3},{5,6},{6,5},{7,8},{8,7},{9,10},{10,... | collective-permute-start | bytes 393224 | tf_op jit(solution)/shard_map/ppermute | solution.py:295
  7.9 4.9 %collective-permute-start.2 = (bf16[64,256]{1,0:T(8,128)(2,1)S(1)}, bf16[64,256]{1,0:T(8,128)(2,1)S(1)}, u32[]{:S(2)}, u32[]{:S(2)}) collective-permute-start(bf16[64,256]{1,0:T(8,128)(2,1)S(1)} %relay.4.refs_5_), channel_id=1, source_target_pairs={{0,8},{1,11},{2,10},{3,9},{4,12},{5,15},{6,14},{7,13},{8,0},{9,3},... | collective-permute-start | bytes 98312 | tf_op jit(solution)/shard_map/ppermute | solution.py:300
  12.8 1.2 %collective-permute-start.3 = (bf16[64,256]{1,0:T(8,128)(2,1)S(1)}, bf16[64,256]{1,0:T(8,128)(2,1)S(1)}, u32[]{:S(2)}, u32[]{:S(2)}) collective-permute-start(bf16[64,256]{1,0:T(8,128)(2,1)S(1)} %collective-permute-done.2.refs_0_.refs_5_), channel_id=1, source_target_pairs={{0,1},{1,0},{2,3},{3,2},{4,5},{5,4},{6,7},{7,6},{8,9},{9,8},{10,11... | collective-permute-start | bytes 98312 | tf_op jit(solution)/shard_map/ppermute | solution.py:336
  14.7 3.5 %collective-permute-start.4 = (bf16[64,1536]{1,0:T(8,128)(2,1)S(1)}, bf16[64,1536]{1,0:T(8,128)(2,1)S(1)}, u32[]{:S(2)}, u32[]{:S(2)}) collective-permute-start(bf16[64,1536]{1,0:T(8,128)(2,1)S(1)} %get-tuple-element.38), channel_id=1, source_target_pairs={{0,1},{1,0},{2,3},{3,2},{4,5},{5,4},{6,7},{7,6},{8,9},{9,8},{10,11... | collective-permute-start | bytes 589832 | tf_op jit(solution)/shard_map/ppermute | solution.py:294
  15.0 8.3 %collective-permute-start.5 = (bf16[64,1024]{1,0:T(8,128)(2,1)S(1)}, bf16[64,1024]{1,0:T(8,128)(2,1)S(1)}, u32[]{:S(2)}, u32[]{:S(2)}) collective-permute-start(bf16[64,1024]{1,0:T(8,128)(2,1)S(1)} %get-tuple-element.36.refs_0_), channel_id=1, source_target_pairs={{0,15},{1,2},{2,1},{3,4},{4,3},{5,6},{6,5},{7,8},{8,7},{9,10},{10,... | collective-permute-start | bytes 393224 | tf_op jit(solution)/shard_map/ppermute | solution.py:295
  18.3 4.9 %collective-permute-start.6 = (bf16[64,256]{1,0:T(8,128)(2,1)S(1)}, bf16[64,256]{1,0:T(8,128)(2,1)S(1)}, u32[]{:S(2)}, u32[]{:S(2)}) collective-permute-start(bf16[64,256]{1,0:T(8,128)(2,1)S(1)} %relay.5.refs_2_), channel_id=1, source_target_pairs={{0,8},{1,11},{2,10},{3,9},{4,12},{5,15},{6,14},{7,13},{8,0},{9,3},... | collective-permute-start | bytes 98312 | tf_op jit(solution)/shard_map/ppermute | solution.py:300
  23.1 1.2 %collective-permute-start.7 = (bf16[64,256]{1,0:T(8,128)(2,1)S(1)}, bf16[64,256]{1,0:T(8,128)(2,1)S(1)}, u32[]{:S(2)}, u32[]{:S(2)}) collective-permute-start(bf16[64,256]{1,0:T(8,128)(2,1)S(1)} %collective-permute-done.6.refs_0_.refs_5_), channel_id=1, source_target_pairs={{0,1},{1,0},{2,3},{3,2},{4,5},{5,4},{6,7},{7,6},{8,9},{9,8},{10,11... | collective-permute-start | bytes 98312 | tf_op jit(solution)/shard_map/ppermute | solution.py:336
  25.1 3.5 %collective-permute-start.8 = (bf16[64,1536]{1,0:T(8,128)(2,1)S(1)}, bf16[64,1536]{1,0:T(8,128)(2,1)S(1)}, u32[]{:S(2)}, u32[]{:S(2)}) collective-permute-start(bf16[64,1536]{1,0:T(8,128)(2,1)S(1)} %get-tuple-element.42), channel_id=1, source_target_pairs={{0,1},{1,0},{2,3},{3,2},{4,5},{5,4},{6,7},{7,6},{8,9},{9,8},{10,11... | collective-permute-start | bytes 589832 | tf_op jit(solution)/shard_map/ppermute | solution.py:294
  25.3 8.3 %collective-permute-start.9 = (bf16[64,1024]{1,0:T(8,128)(2,1)S(1)}, bf16[64,1024]{1,0:T(8,128)(2,1)S(1)}, u32[]{:S(2)}, u32[]{:S(2)}) collective-permute-start(bf16[64,1024]{1,0:T(8,128)(2,1)S(1)} %get-tuple-element.40.refs_0_), channel_id=1, source_target_pairs={{0,15},{1,2},{2,1},{3,4},{4,3},{5,6},{6,5},{7,8},{8,7},{9,10},{10,... | collective-permute-start | bytes 393224 | tf_op jit(solution)/shard_map/ppermute | solution.py:295
  28.6 4.9 %collective-permute-start.10 = (bf16[64,256]{1,0:T(8,128)(2,1)S(1)}, bf16[64,256]{1,0:T(8,128)(2,1)S(1)}, u32[]{:S(2)}, u32[]{:S(2)}) collective-permute-start(bf16[64,256]{1,0:T(8,128)(2,1)S(1)} %relay.6.refs_2_), channel_id=1, source_target_pairs={{0,8},{1,11},{2,10},{3,9},{4,12},{5,15},{6,14},{7,13},{8,0},{9,3},... | collective-permute-start | bytes 98312 | tf_op jit(solution)/shard_map/ppermute | solution.py:300
  33.5 1.2 %collective-permute-start.11 = (bf16[64,256]{1,0:T(8,128)(2,1)S(1)}, bf16[64,256]{1,0:T(8,128)(2,1)S(1)}, u32[]{:S(2)}, u32[]{:S(2)}) collective-permute-start(bf16[64,256]{1,0:T(8,128)(2,1)S(1)} %collective-permute-done.10.refs_0_.refs_5_), channel_id=1, source_target_pairs={{0,1},{1,0},{2,3},{3,2},{4,5},{5,4},{6,7},{7,6},{8,9},{9,8},{10,11... | collective-permute-start | bytes 98312 | tf_op jit(solution)/shard_map/ppermute | solution.py:336
  35.4 3.4 %collective-permute-start.12 = (bf16[64,1536]{1,0:T(8,128)(2,1)S(1)}, bf16[64,1536]{1,0:T(8,128)(2,1)S(1)}, u32[]{:S(2)}, u32[]{:S(2)}) collective-permute-start(bf16[64,1536]{1,0:T(8,128)(2,1)S(1)} %get-tuple-element.47), channel_id=1, source_target_pairs={{0,1},{1,0},{2,3},{3,2},{4,5},{5,4},{6,7},{7,6},{8,9},{9,8},{10,11... | collective-permute-start | bytes 589832 | tf_op jit(solution)/shard_map/ppermute | solution.py:294
  35.7 8.3 %collective-permute-start.13 = (bf16[64,1024]{1,0:T(8,128)(2,1)S(1)}, bf16[64,1024]{1,0:T(8,128)(2,1)S(1)}, u32[]{:S(2)}, u32[]{:S(2)}) collective-permute-start(bf16[64,1024]{1,0:T(8,128)(2,1)S(1)} %get-tuple-element.45.refs_0_), channel_id=1, source_target_pairs={{0,15},{1,2},{2,1},{3,4},{4,3},{5,6},{6,5},{7,8},{8,7},{9,10},{10,... | collective-permute-start | bytes 393224 | tf_op jit(solution)/shard_map/ppermute | solution.py:295
  38.8 4.9 %collective-permute-start.14 = (bf16[64,256]{1,0:T(8,128)(2,1)S(1)}, bf16[64,256]{1,0:T(8,128)(2,1)S(1)}, u32[]{:S(2)}, u32[]{:S(2)}) collective-permute-start(bf16[64,256]{1,0:T(8,128)(2,1)S(1)} %relay.7.refs_2_), channel_id=1, source_target_pairs={{0,8},{1,11},{2,10},{3,9},{4,12},{5,15},{6,14},{7,13},{8,0},{9,3},... | collective-permute-start | bytes 98312 | tf_op jit(solution)/shard_map/ppermute | solution.py:300
  43.7 1.2 %collective-permute-start.15 = (bf16[64,256]{1,0:T(8,128)(2,1)S(1)}, bf16[64,256]{1,0:T(8,128)(2,1)S(1)}, u32[]{:S(2)}, u32[]{:S(2)}) collective-permute-start(bf16[64,256]{1,0:T(8,128)(2,1)S(1)} %collective-permute-done.14.refs_0_.refs_3_), channel_id=1, source_target_pairs={{0,1},{1,0},{2,3},{3,2},{4,5},{5,4},{6,7},{7,6},{8,9},{9,8},{10,11... | collective-permute-start | bytes 98312 | tf_op jit(solution)/shard_map/ppermute | solution.py:336

commit v5 on v4

--- a/solution.py
+++ b/solution.py
@@ -98,28 +98,25 @@
         second = lax.rem(index_ref[0], 2) == 1
         return jnp.where(second, both[:, self.width :], both[:, : self.width])
 
-    def own_sums(self, x_ref, d_ref, acc_ref):
+    def near_sums(self, x_ref, d_ref, acc_ref, first, start_ref=None):
         panels = [self.panel(x_ref, c) for c in range(self.per_device)]
         for r in range(self.per_device):
-            acc_ref[:, r * self.size : (r + 1) * self.size] = sum(
-                dot_nt(panels[c], d_ref[r * SPAN + c - r + REACH]) for c in range(self.per_device)
-            )
-
-    def halo_sums(self, index_ref, acc_ref, near_ref, over_ref, d_ref, out_ref):
-        odd = lax.rem(index_ref[0], 2) == 1
-        low, high = [], []
-        for c in range(self.per_device):
-            near, over = self.panel(near_ref, c), self.panel(over_ref, c)
-            low.append(jnp.where(odd, near, over))
-            high.append(jnp.where(odd, over, near))
-        for r in range(self.per_device):
-            value = self.panel(acc_ref, r)
+            value = None if start_ref is None else self.panel(start_ref, r)
             for c in range(self.per_device):
-                for panel, place in ((low[c], c - self.per_device), (high[c], c + self.per_device)):
-                    offset = place - r
-                    if -REACH <= offset <= REACH:
-                        value = value + dot_nt(panel, d_ref[r * SPAN + offset + REACH])
-            out_ref[:, r * self.size : (r + 1) * self.size] = value
+                offset = first + c - r
+                if -REACH <= offset <= REACH:
+                    term = dot_nt(panels[c], d_ref[r * SPAN + offset + REACH])
+                    value = term if value is None else value + term
+            acc_ref[:, r * self.size : (r + 1) * self.size] = value
+
+    def halo_sums(self, below, x_ref, d_ref, acc_ref, start_ref):
+        @pl.when(below)
+        def _():
+            self.near_sums(x_ref, d_ref, acc_ref, -self.per_device, start_ref)
+
+        @pl.when(jnp.logical_not(below))
+        def _():
+            self.near_sums(x_ref, d_ref, acc_ref, self.per_device, start_ref)
 
     def next_block(self, index_ref, acc_ref, rb_ref, far_refs):
         both = jnp.concatenate(halves(self.far_sum(index_ref, far_refs)), axis=1)
@@ -163,7 +160,7 @@
 
 
 def first_own_kernel(plan, *refs):
-    x_ref, rows_hbm, offsets_hbm, row_hbm, tiles_hbm = refs[:5]
+    index_ref, x_ref, near_ref, rows_hbm, offsets_hbm, row_hbm, tiles_hbm = refs[:7]
     acc_ref, d_ref, rb_ref, rows_ref, offsets_ref, row_ref, present, sems, tile_sems = refs[-9:]
     pairs = ((rows_hbm, rows_ref), (offsets_hbm, offsets_ref), (row_hbm, row_ref))
     copies = [pltpu.make_async_copy(*pair, sems.at[i]) for i, pair in enumerate(pairs)]
@@ -194,20 +191,22 @@
         def _():
             d_ref[cell] = jnp.zeros(d_ref.shape[1:], d_ref.dtype)
 
-    plan.own_sums(x_ref, d_ref, acc_ref)
+    plan.near_sums(x_ref, d_ref, acc_ref, 0)
+    plan.halo_sums(lax.rem(index_ref[0], 2) == 1, near_ref, d_ref, acc_ref, acc_ref)
 
 
 def own_kernel(plan, slot, *refs):
-    x_ref, d_ref = refs[:2]
+    index_ref, x_ref, near_ref, d_ref = refs[:4]
     acc_ref, krylov_ref, sem = refs[-3:]
     copy = pltpu.make_async_copy(x_ref, krylov_ref.at[slot], sem)
     copy.start()
-    plan.own_sums(x_ref, d_ref, acc_ref)
+    plan.near_sums(x_ref, d_ref, acc_ref, 0)
+    plan.halo_sums(lax.rem(index_ref[0], 2) == 1, near_ref, d_ref, acc_ref, acc_ref)
     copy.wait()
 
 
-def halo_kernel(plan, index_ref, acc_ref, near_ref, over_ref, d_ref, *refs):
-    plan.halo_sums(index_ref, acc_ref, near_ref, over_ref, d_ref, refs[-1])
+def halo_kernel(plan, index_ref, acc_ref, over_ref, d_ref, *refs):
+    plan.halo_sums(lax.rem(index_ref[0], 2) == 0, over_ref, d_ref, refs[-1], acc_ref)
 
 
 def finish_kernel(plan, fars, *refs):
@@ -305,8 +304,8 @@
             acc, dense, row_wide = call(
                 functools.partial(first_own_kernel, plan),
                 "first_own",
-                [current, near_rows, near_offsets, row_basis, near_tiles, *after],
-                [IN_VMEM] + [IN_HBM] * 4 + [ANYWHERE] * len(after),
+                [index, current, near, near_rows, near_offsets, row_basis, near_tiles, *after],
+                [IN_SMEM] + [IN_VMEM] * 2 + [IN_HBM] * 4 + [ANYWHERE] * len(after),
                 [
                     acc_out,
                     pltpu.VMEM((plan.cells, plan.size, plan.size), BF16),
@@ -320,12 +319,12 @@
                 ],
             )
         else:
-            ins = [current, dense, *after] + ([krylov] if product > 1 else [])
+            ins = [index, current, near, dense, *after] + ([krylov] if product > 1 else [])
             acc, krylov = call(
                 functools.partial(own_kernel, plan, product - 1),
                 "own",
                 ins,
-                [IN_VMEM] * 2 + [ANYWHERE] * (len(ins) - 2),
+                [IN_SMEM] + [IN_VMEM] * 3 + [ANYWHERE] * (len(ins) - 4),
                 [acc_out, krylov_out],
                 [IN_VMEM, ANYWHERE],
                 [pltpu.SemaphoreType.DMA],
@@ -337,8 +336,8 @@
         (acc,) = call(
             functools.partial(halo_kernel, plan),
             "halo",
-            [index, acc, near, over, dense, *after],
-            [IN_SMEM] + [IN_VMEM] * 4 + [ANYWHERE] * len(after),
+            [index, acc, over, dense, *after],
+            [IN_SMEM] + [IN_VMEM] * 3 + [ANYWHERE] * len(after),
             [acc_out],
         )
         if product < PRODUCTS - 1:

time: 46 us -> 46.3 us (level)
  waiting for transfers between devices: 12.3 us -> 11.6 us
  starting transfers between devices: 18.2 us -> 18.8 us
  Pallas kernels: 15.1 us -> 15.6 us
    ppermute x4, waiting for transfers between devices: 11.8 us -> 9.64 us  [on_device(): fars = [lax.ppermute(relayed, axes, plan.across)]]
    ppermute x4, waiting for transfers between devices: 0.52 us -> 1.93 us  [on_device(): fars.append(lax.ppermute(fars[0], axes, plan.near))]
  transfers between devices with their start and end apart: 16 -> 16, of which waited for: 7 -> 7; matrix products, arithmetic and copies ran while one was open for 0% -> 0% of each run, Pallas kernels for 23% -> 24%
where the time goes in v5:
time: 46.3 us; the launch traced here: 46.1 us
  starting transfers between devices  18.8 us (41%)
  Pallas kernels  15.6 us (34%)
  waiting for transfers between devices  11.6 us (25%)
    pallas_call x17, Pallas kernels, call(): pl.pallas_call(kernel, in_specs=list(specs), out_specs=out_specs or [IN_V...  15.6 us
    ppermute x4, starting transfers between devices, on_device(): over = lax.ppermute(block if product == 0 else current, axes, plan.over)  15.2 us
    ppermute x4, waiting for transfers between devices, on_device(): fars = [lax.ppermute(relayed, axes, plan.across)]  9.64 us
    ppermute x4, waiting for transfers between devices, on_device(): fars.append(lax.ppermute(fars[0], axes, plan.near))  1.93 us
    ppermute x4, starting transfers between devices, on_device(): near = lax.ppermute(sends[0] if plan.paired else current, axes, plan.near)  1.45 us
    ppermute x4, starting transfers between devices, on_device(): fars = [lax.ppermute(relayed, axes, plan.across)]  1.31 us
  transfers between devices with their start and end apart: 16, of which 7 were waited for; matrix products, arithmetic and copies ran while one was open for 0% of the time, Pallas kernels for 24%

profile of v5, /device:TPU:0, one launch (start us, length us, event | category | flops | bytes accessed | tf_op | source)
XLA Modules:
  0.0 46.1 jit_solution(10394809930008469448)
XLA Ops:
  0.0 1.8 %prepare.1 = (bf16[64,1024]{1,0:T(8,128)(2,1)S(1)}, bf16[3,512,128]{2,1,0:T(8,128)(2,1)S(1)}, bf16[128,1024]{1,0:T(8,128)(2,1)S(1)}, bf16[64,1536]{1,0:T(8,128)(2,1)S(1)}, f32[64,256]{1,0:T(8,128)S(1)}) custom-call(s32[1]{0:T(128)} %bitcast.index_ref.refs_0_, s32[32]{0:T(128)} %refs_0_.1, s32[32]{0:T(128)} %refs_1_.1, bf16[64,1024]{1,0:T(8,128)(2,1)} %refs_2_.1, ...), custom_call_target="tpu_custom_call" | custom-call | flops 1000000000 | bytes 4194304 | tf_op jit(solution)/shard_map/prepare/pallas_call | solution.py:235
  1.8 0.5 %collective-permute-start = (bf16[64,1536]{1,0:T(8,128)(2,1)S(1)}, bf16[64,1536]{1,0:T(8,128)(2,1)S(1)}, u32[]{:S(2)}, u32[]{:S(2)}) collective-permute-start(bf16[64,1536]{1,0:T(8,128)(2,1)S(1)} %get-tuple-element.29), channel_id=1, source_target_pairs={{0,1},{1,0},{2,3},{3,2},{4,5},{5,4},{6,7},{7,6},{8,9},{9,8},{10,11... | collective-permute-start | bytes 589832 | tf_op jit(solution)/shard_map/ppermute | solution.py:293
  2.3 5.6 %collective-permute-start.1 = (bf16[64,1024]{1,0:T(8,128)(2,1)}, bf16[64,1024]{1,0:T(8,128)(2,1)S(1)}, u32[]{:S(2)}, u32[]{:S(2)}) collective-permute-start(bf16[64,1024]{1,0:T(8,128)(2,1)} %refs_2_.1), channel_id=1, source_target_pairs={{0,15},{1,2},{2,1},{3,4},{4,3},{5,6},{6,5},{7,8},{8,7},{9,10},{10,... | collective-permute-start | bytes 393224 | tf_op jit(solution)/shard_map/ppermute | solution.py:294
  7.9 0.0 collective-permute-done.message_ref.refs_2_
  7.9 0.1 collective-permute-start.2
  8.0 4.9 %first_own.1 = (f32[64,1024]{1,0:T(8,128)S(1)}, bf16[36,256,256]{2,1,0:T(8,128)(2,1)S(1)}, bf16[256,1024]{1,0:T(8,128)(2,1)S(1)}) custom-call(s32[1]{0:T(128)} %bitcast.index_ref.refs_0_, bf16[64,1024]{1,0:T(8,128)(2,1)S(1)} %get-tuple-element.28.refs_1_, bf16[64,1536]{1,0:T(8,128)(2,1)S(1)} %collective-permute-done.message_ref.refs_2_, s32[32]{0:T(128)} %refs_3_.3, ...), custom_call_target="tpu_custom_call" | custom-call | flops 1000000000 | bytes 4194304 | tf_op jit(solution)/shard_map/first_own/pallas_call | solution.py:235
  12.9 0.0 collective-permute-done.2.refs_0_.refs_5_
  12.9 0.3 collective-permute-start.3
  13.3 0.0 collective-permute-done.1.over_ref
  13.3 0.5 %halo.4.refs_1_ = f32[64,1024]{1,0:T(8,128)S(1)} custom-call(s32[1]{0:T(128)} %bitcast.index_ref.refs_0_, f32[64,1024]{1,0:T(8,128)S(1)} %get-tuple-element.31.acc_ref, bf16[64,1024]{1,0:T(8,128)(2,1)S(1)} %collective-permute-done.1.over_ref, bf16[36,256,256]{2,1,0:T(8,128)(2,1)S(1)} %get-tuple-element.32.d_ref.refs_3_, ...), custom_call_target="tpu_custom_call" | custom-call | flops 1000000000 | bytes 4194304 | tf_op jit(solution)/shard_map/halo/pallas_call | solution.py:235
  13.8 0.4 collective-permute-done.3.refs_6_
  14.2 0.7 %finish.3 = (bf16[64,1024]{1,0:T(8,128)(2,1)S(1)}, bf16[64,1536]{1,0:T(8,128)(2,1)S(1)}, f32[64,256]{1,0:T(8,128)S(1)}) custom-call(s32[1]{0:T(128)} %bitcast.index_ref.refs_0_, f32[64,1024]{1,0:T(8,128)S(1)} %halo.4.refs_1_, bf16[256,1024]{1,0:T(8,128)(2,1)S(1)} %get-tuple-element.33.refs_2_, bf16[128,1024]{1,0:T(8,128)(2,1)S(1)} %get-tuple-element.34.refs_3_, ...), custom_call_target="tpu_custom_call" | custom-call | flops 1000000000 | bytes 4194304 | tf_op jit(solution)/shard_map/finish/pallas_call | solution.py:235
  14.9 0.3 collective-permute-start.4
  15.2 3.0 %collective-permute-start.5 = (bf16[64,1024]{1,0:T(8,128)(2,1)S(1)}, bf16[64,1024]{1,0:T(8,128)(2,1)S(1)}, u32[]{:S(2)}, u32[]{:S(2)}) collective-permute-start(bf16[64,1024]{1,0:T(8,128)(2,1)S(1)} %get-tuple-element.36.refs_1_), channel_id=1, source_target_pairs={{0,15},{1,2},{2,1},{3,4},{4,3},{5,6},{6,5},{7,8},{8,7},{9,10},{10,... | collective-permute-start | bytes 393224 | tf_op jit(solution)/shard_map/ppermute | solution.py:294
  18.2 0.0 collective-permute-done.4.message_ref.refs_2_
  18.2 1.1 %collective-permute-start.6 = (bf16[64,256]{1,0:T(8,128)(2,1)S(1)}, bf16[64,256]{1,0:T(8,128)(2,1)S(1)}, u32[]{:S(2)}, u32[]{:S(2)}) collective-permute-start(bf16[64,256]{1,0:T(8,128)(2,1)S(1)} %relay.5.refs_4_), channel_id=1, source_target_pairs={{0,8},{1,11},{2,10},{3,9},{4,12},{5,15},{6,14},{7,13},{8,0},{9,3},... | collective-permute-start | bytes 98312 | tf_op jit(solution)/shard_map/ppermute | solution.py:299
  19.3 1.3 %own.3 = (f32[64,1024]{1,0:T(8,128)S(1)}, bf16[4,64,1024]{2,1,0:T(8,128)(2,1)}) custom-call(s32[1]{0:T(128)} %bitcast.index_ref.refs_0_, bf16[64,1024]{1,0:T(8,128)(2,1)S(1)} %get-tuple-element.36.refs_1_, bf16[64,1536]{1,0:T(8,128)(2,1)S(1)} %collective-permute-done.4.message_ref.refs_2_, bf16[36,256,256]{2,1,0:T(8,128)(2,1)S(1)} %get-tuple-element.32.d_ref.refs_3_, ...), custom_call_target="tpu_custom_call" | custom-call | flops 1000000000 | bytes 4194304 | tf_op jit(solution)/shard_map/own/pallas_call | solution.py:235
  20.6 2.6 %collective-permute-done.6.refs_0_.refs_5_ = bf16[64,256]{1,0:T(8,128)(2,1)S(1)} collective-permute-done((bf16[64,256]{1,0:T(8,128)(2,1)S(1)}, bf16[64,256]{1,0:T(8,128)(2,1)S(1)}, u32[]{:S(2)}, u32[]{:S(2)}) %collective-permute-start.6) | collective-permute-done | bytes 32800 | tf_op jit(solution)/shard_map/ppermute | solution.py:299
  23.2 0.3 collective-permute-start.7
  23.5 0.0 collective-permute-done.5.over_ref
  23.5 0.5 %halo.5.refs_1_ = f32[64,1024]{1,0:T(8,128)S(1)} custom-call(s32[1]{0:T(128)} %bitcast.index_ref.refs_0_, f32[64,1024]{1,0:T(8,128)S(1)} %get-tuple-element.39.acc_ref, bf16[64,1024]{1,0:T(8,128)(2,1)S(1)} %collective-permute-done.5.over_ref, bf16[36,256,256]{2,1,0:T(8,128)(2,1)S(1)} %get-tuple-element.32.d_ref.refs_3_, ...), custom_call_target="tpu_custom_call" | custom-call | flops 1000000000 | bytes 4194304 | tf_op jit(solution)/shard_map/halo/pallas_call | solution.py:235
  24.1 0.4 collective-permute-done.7.refs_6_
  24.4 0.7 %finish.4 = (bf16[64,1024]{1,0:T(8,128)(2,1)S(1)}, bf16[64,1536]{1,0:T(8,128)(2,1)S(1)}, f32[64,256]{1,0:T(8,128)S(1)}) custom-call(s32[1]{0:T(128)} %bitcast.index_ref.refs_0_, f32[64,1024]{1,0:T(8,128)S(1)} %halo.5.refs_1_, bf16[256,1024]{1,0:T(8,128)(2,1)S(1)} %get-tuple-element.33.refs_2_, bf16[128,1024]{1,0:T(8,128)(2,1)S(1)} %get-tuple-element.34.refs_3_, ...), custom_call_target="tpu_custom_call" | custom-call | flops 1000000000 | bytes 4194304 | tf_op jit(solution)/shard_map/finish/pallas_call | solution.py:235
  25.1 0.4 collective-permute-start.8
  25.5 3.3 %collective-permute-start.9 = (bf16[64,1024]{1,0:T(8,128)(2,1)S(1)}, bf16[64,1024]{1,0:T(8,128)(2,1)S(1)}, u32[]{:S(2)}, u32[]{:S(2)}) collective-permute-start(bf16[64,1024]{1,0:T(8,128)(2,1)S(1)} %get-tuple-element.40.refs_1_), channel_id=1, source_target_pairs={{0,15},{1,2},{2,1},{3,4},{4,3},{5,6},{6,5},{7,8},{8,7},{9,10},{10,... | collective-permute-start | bytes 393224 | tf_op jit(solution)/shard_map/ppermute | solution.py:294
  28.8 0.0 collective-permute-done.8.message_ref.refs_2_
  28.8 0.1 collective-permute-start.10
  28.9 1.3 %own.4 = (f32[64,1024]{1,0:T(8,128)S(1)}, bf16[4,64,1024]{2,1,0:T(8,128)(2,1)}) custom-call(s32[1]{0:T(128)} %bitcast.index_ref.refs_0_, bf16[64,1024]{1,0:T(8,128)(2,1)S(1)} %get-tuple-element.40.refs_1_, bf16[64,1536]{1,0:T(8,128)(2,1)S(1)} %collective-permute-done.8.message_ref.refs_2_, ...), custom_call_target="tpu_custom_call", output_to_operand_aliasing={{1}: (5, {})} | custom-call | flops 1000000000 | bytes 4194304 | tf_op jit(solution)/shard_map/own/pallas_call | solution.py:235
  30.2 3.5 %collective-permute-done.10.refs_0_.refs_5_ = bf16[64,256]{1,0:T(8,128)(2,1)S(1)} collective-permute-done((bf16[64,256]{1,0:T(8,128)(2,1)S(1)}, bf16[64,256]{1,0:T(8,128)(2,1)S(1)}, u32[]{:S(2)}, u32[]{:S(2)}) %collective-permute-start.10) | collective-permute-done | bytes 32800 | tf_op jit(solution)/shard_map/ppermute | solution.py:299
  33.7 0.1 collective-permute-start.11
  33.8 0.0 collective-permute-done.9.over_ref
  33.8 0.5 %halo.6.refs_1_ = f32[64,1024]{1,0:T(8,128)S(1)} custom-call(s32[1]{0:T(128)} %bitcast.index_ref.refs_0_, f32[64,1024]{1,0:T(8,128)S(1)} %get-tuple-element.44.acc_ref, bf16[64,1024]{1,0:T(8,128)(2,1)S(1)} %collective-permute-done.9.over_ref, bf16[36,256,256]{2,1,0:T(8,128)(2,1)S(1)} %get-tuple-element.32.d_ref.refs_3_, ...), custom_call_target="tpu_custom_call" | custom-call | flops 1000000000 | bytes 4194304 | tf_op jit(solution)/shard_map/halo/pallas_call | solution.py:235
  34.3 0.6 %collective-permute-done.11.refs_6_ = bf16[64,256]{1,0:T(8,128)(2,1)S(1)} collective-permute-done((bf16[64,256]{1,0:T(8,128)(2,1)S(1)}, bf16[64,256]{1,0:T(8,128)(2,1)S(1)}, u32[]{:S(2)}, u32[]{:S(2)}) %collective-permute-start.11) | collective-permute-done | bytes 32800 | tf_op jit(solution)/shard_map/ppermute | solution.py:335
  34.9 0.7 %finish.5 = (bf16[64,1024]{1,0:T(8,128)(2,1)S(1)}, bf16[64,1536]{1,0:T(8,128)(2,1)S(1)}, f32[64,256]{1,0:T(8,128)S(1)}) custom-call(s32[1]{0:T(128)} %bitcast.index_ref.refs_0_, f32[64,1024]{1,0:T(8,128)S(1)} %halo.6.refs_1_, bf16[256,1024]{1,0:T(8,128)(2,1)S(1)} %get-tuple-element.33.refs_2_, bf16[128,1024]{1,0:T(8,128)(2,1)S(1)} %get-tuple-element.34.refs_3_, ...), custom_call_target="tpu_custom_call" | custom-call | flops 1000000000 | bytes 4194304 | tf_op jit(solution)/shard_map/finish/pallas_call | solution.py:235
  35.6 0.2 collective-permute-start.12
  35.8 3.3 %collective-permute-start.13 = (bf16[64,1024]{1,0:T(8,128)(2,1)S(1)}, bf16[64,1024]{1,0:T(8,128)(2,1)S(1)}, u32[]{:S(2)}, u32[]{:S(2)}) collective-permute-start(bf16[64,1024]{1,0:T(8,128)(2,1)S(1)} %get-tuple-element.45.refs_1_), channel_id=1, source_target_pairs={{0,15},{1,2},{2,1},{3,4},{4,3},{5,6},{6,5},{7,8},{8,7},{9,10},{10,... | collective-permute-start | bytes 393224 | tf_op jit(solution)/shard_map/ppermute | solution.py:294
  39.1 0.0 collective-permute-done.12.message_ref.refs_2_
  39.1 0.1 collective-permute-start.14
  39.2 1.3 %own.5 = (f32[64,1024]{1,0:T(8,128)S(1)}, bf16[4,64,1024]{2,1,0:T(8,128)(2,1)}) custom-call(s32[1]{0:T(128)} %bitcast.index_ref.refs_0_, bf16[64,1024]{1,0:T(8,128)(2,1)S(1)} %get-tuple-element.45.refs_1_, bf16[64,1536]{1,0:T(8,128)(2,1)S(1)} %collective-permute-done.12.message_ref.refs_2_, ...), custom_call_target="tpu_custom_call", output_to_operand_aliasing={{1}: (5, {})} | custom-call | flops 1000000000 | bytes 4194304 | tf_op jit(solution)/shard_map/own/pallas_call | solution.py:235
  40.5 3.5 %collective-permute-done.14.refs_0_.refs_3_ = bf16[64,256]{1,0:T(8,128)(2,1)S(1)} collective-permute-done((bf16[64,256]{1,0:T(8,128)(2,1)S(1)}, bf16[64,256]{1,0:T(8,128)(2,1)S(1)}, u32[]{:S(2)}, u32[]{:S(2)}) %collective-permute-start.14) | collective-permute-done | bytes 32800 | tf_op jit(solution)/shard_map/ppermute | solution.py:299
  44.0 0.1 collective-permute-start.15
  44.1 0.0 collective-permute-done.13.over_ref
  44.1 0.5 %halo.7.refs_1_ = f32[64,1024]{1,0:T(8,128)S(1)} custom-call(s32[1]{0:T(128)} %bitcast.index_ref.refs_0_, f32[64,1024]{1,0:T(8,128)S(1)} %get-tuple-element.49.acc_ref, bf16[64,1024]{1,0:T(8,128)(2,1)S(1)} %collective-permute-done.13.over_ref, bf16[36,256,256]{2,1,0:T(8,128)(2,1)S(1)} %get-tuple-element.32.d_ref.refs_3_, ...), custom_call_target="tpu_custom_call" | custom-call | flops 1000000000 | bytes 4194304 | tf_op jit(solution)/shard_map/halo/pallas_call | solution.py:235
  44.6 0.6 %collective-permute-done.15.refs_4_ = bf16[64,256]{1,0:T(8,128)(2,1)S(1)} collective-permute-done((bf16[64,256]{1,0:T(8,128)(2,1)S(1)}, bf16[64,256]{1,0:T(8,128)(2,1)S(1)}, u32[]{:S(2)}, u32[]{:S(2)}) %collective-permute-start.15) | collective-permute-done | bytes 32800 | tf_op jit(solution)/shard_map/ppermute | solution.py:335
  45.2 0.9 %last.1 = bf16[4,64,1024]{2,1,0:T(8,128)(2,1)} custom-call(s32[1]{0:T(128)} %bitcast.index_ref.refs_0_, f32[64,1024]{1,0:T(8,128)S(1)} %halo.7.refs_1_, bf16[256,1024]{1,0:T(8,128)(2,1)S(1)} %get-tuple-element.33.refs_2_, bf16[64,256]{1,0:T(8,128)(2,1)S(1)} %collective-permute-done.14.refs_0_.refs_3_, ...), custom_call_target="tpu_custom_call", output_to_operand_aliasing={{}: (5, {})} | custom-call | flops 1000000000 | bytes 4194304 | tf_op jit(solution)/shard_map/last/pallas_call | solution.py:235
  (4 shorter events, 0.1 us)
Async XLA Ops:
  1.8 6.2 %collective-permute-start = (bf16[64,1536]{1,0:T(8,128)(2,1)S(1)}, bf16[64,1536]{1,0:T(8,128)(2,1)S(1)}, u32[]{:S(2)}, u32[]{:S(2)}) collective-permute-start(bf16[64,1536]{1,0:T(8,128)(2,1)S(1)} %get-tuple-element.29), channel_id=1, source_target_pairs={{0,1},{1,0},{2,3},{3,2},{4,5},{5,4},{6,7},{7,6},{8,9},{9,8},{10,11... | collective-permute-start | bytes 589832 | tf_op jit(solution)/shard_map/ppermute | solution.py:293
  2.3 11.0 %collective-permute-start.1 = (bf16[64,1024]{1,0:T(8,128)(2,1)}, bf16[64,1024]{1,0:T(8,128)(2,1)S(1)}, u32[]{:S(2)}, u32[]{:S(2)}) collective-permute-start(bf16[64,1024]{1,0:T(8,128)(2,1)} %refs_2_.1), channel_id=1, source_target_pairs={{0,15},{1,2},{2,1},{3,4},{4,3},{5,6},{6,5},{7,8},{8,7},{9,10},{10,... | collective-permute-start | bytes 393224 | tf_op jit(solution)/shard_map/ppermute | solution.py:294
  7.9 5.0 %collective-permute-start.2 = (bf16[64,256]{1,0:T(8,128)(2,1)S(1)}, bf16[64,256]{1,0:T(8,128)(2,1)S(1)}, u32[]{:S(2)}, u32[]{:S(2)}) collective-permute-start(bf16[64,256]{1,0:T(8,128)(2,1)S(1)} %relay.4.refs_7_), channel_id=1, source_target_pairs={{0,8},{1,11},{2,10},{3,9},{4,12},{5,15},{6,14},{7,13},{8,0},{9,3},... | collective-permute-start | bytes 98312 | tf_op jit(solution)/shard_map/ppermute | solution.py:299
  12.9 1.3 %collective-permute-start.3 = (bf16[64,256]{1,0:T(8,128)(2,1)S(1)}, bf16[64,256]{1,0:T(8,128)(2,1)S(1)}, u32[]{:S(2)}, u32[]{:S(2)}) collective-permute-start(bf16[64,256]{1,0:T(8,128)(2,1)S(1)} %collective-permute-done.2.refs_0_.refs_5_), channel_id=1, source_target_pairs={{0,1},{1,0},{2,3},{3,2},{4,5},{5,4},{6,7},{7,6},{8,9},{9,8},{10,11... | collective-permute-start | bytes 98312 | tf_op jit(solution)/shard_map/ppermute | solution.py:335
  14.9 3.3 %collective-permute-start.4 = (bf16[64,1536]{1,0:T(8,128)(2,1)S(1)}, bf16[64,1536]{1,0:T(8,128)(2,1)S(1)}, u32[]{:S(2)}, u32[]{:S(2)}) collective-permute-start(bf16[64,1536]{1,0:T(8,128)(2,1)S(1)} %get-tuple-element.37), channel_id=1, source_target_pairs={{0,1},{1,0},{2,3},{3,2},{4,5},{5,4},{6,7},{7,6},{8,9},{9,8},{10,11... | collective-permute-start | bytes 589832 | tf_op jit(solution)/shard_map/ppermute | solution.py:293
  15.2 8.3 %collective-permute-start.5 = (bf16[64,1024]{1,0:T(8,128)(2,1)S(1)}, bf16[64,1024]{1,0:T(8,128)(2,1)S(1)}, u32[]{:S(2)}, u32[]{:S(2)}) collective-permute-start(bf16[64,1024]{1,0:T(8,128)(2,1)S(1)} %get-tuple-element.36.refs_1_), channel_id=1, source_target_pairs={{0,15},{1,2},{2,1},{3,4},{4,3},{5,6},{6,5},{7,8},{8,7},{9,10},{10,... | collective-permute-start | bytes 393224 | tf_op jit(solution)/shard_map/ppermute | solution.py:294
  18.2 5.0 %collective-permute-start.6 = (bf16[64,256]{1,0:T(8,128)(2,1)S(1)}, bf16[64,256]{1,0:T(8,128)(2,1)S(1)}, u32[]{:S(2)}, u32[]{:S(2)}) collective-permute-start(bf16[64,256]{1,0:T(8,128)(2,1)S(1)} %relay.5.refs_4_), channel_id=1, source_target_pairs={{0,8},{1,11},{2,10},{3,9},{4,12},{5,15},{6,14},{7,13},{8,0},{9,3},... | collective-permute-start | bytes 98312 | tf_op jit(solution)/shard_map/ppermute | solution.py:299
  23.2 1.2 %collective-permute-start.7 = (bf16[64,256]{1,0:T(8,128)(2,1)S(1)}, bf16[64,256]{1,0:T(8,128)(2,1)S(1)}, u32[]{:S(2)}, u32[]{:S(2)}) collective-permute-start(bf16[64,256]{1,0:T(8,128)(2,1)S(1)} %collective-permute-done.6.refs_0_.refs_5_), channel_id=1, source_target_pairs={{0,1},{1,0},{2,3},{3,2},{4,5},{5,4},{6,7},{7,6},{8,9},{9,8},{10,11... | collective-permute-start | bytes 98312 | tf_op jit(solution)/shard_map/ppermute | solution.py:335
  25.1 3.7 %collective-permute-start.8 = (bf16[64,1536]{1,0:T(8,128)(2,1)S(1)}, bf16[64,1536]{1,0:T(8,128)(2,1)S(1)}, u32[]{:S(2)}, u32[]{:S(2)}) collective-permute-start(bf16[64,1536]{1,0:T(8,128)(2,1)S(1)} %get-tuple-element.41), channel_id=1, source_target_pairs={{0,1},{1,0},{2,3},{3,2},{4,5},{5,4},{6,7},{7,6},{8,9},{9,8},{10,11... | collective-permute-start | bytes 589832 | tf_op jit(solution)/shard_map/ppermute | solution.py:293
  25.5 8.3 %collective-permute-start.9 = (bf16[64,1024]{1,0:T(8,128)(2,1)S(1)}, bf16[64,1024]{1,0:T(8,128)(2,1)S(1)}, u32[]{:S(2)}, u32[]{:S(2)}) collective-permute-start(bf16[64,1024]{1,0:T(8,128)(2,1)S(1)} %get-tuple-element.40.refs_1_), channel_id=1, source_target_pairs={{0,15},{1,2},{2,1},{3,4},{4,3},{5,6},{6,5},{7,8},{8,7},{9,10},{10,... | collective-permute-start | bytes 393224 | tf_op jit(solution)/shard_map/ppermute | solution.py:294
  28.8 4.9 %collective-permute-start.10 = (bf16[64,256]{1,0:T(8,128)(2,1)S(1)}, bf16[64,256]{1,0:T(8,128)(2,1)S(1)}, u32[]{:S(2)}, u32[]{:S(2)}) collective-permute-start(bf16[64,256]{1,0:T(8,128)(2,1)S(1)} %relay.6.refs_4_), channel_id=1, source_target_pairs={{0,8},{1,11},{2,10},{3,9},{4,12},{5,15},{6,14},{7,13},{8,0},{9,3},... | collective-permute-start | bytes 98312 | tf_op jit(solution)/shard_map/ppermute | solution.py:299
  33.7 1.2 %collective-permute-start.11 = (bf16[64,256]{1,0:T(8,128)(2,1)S(1)}, bf16[64,256]{1,0:T(8,128)(2,1)S(1)}, u32[]{:S(2)}, u32[]{:S(2)}) collective-permute-start(bf16[64,256]{1,0:T(8,128)(2,1)S(1)} %collective-permute-done.10.refs_0_.refs_5_), channel_id=1, source_target_pairs={{0,1},{1,0},{2,3},{3,2},{4,5},{5,4},{6,7},{7,6},{8,9},{9,8},{10,11... | collective-permute-start | bytes 98312 | tf_op jit(solution)/shard_map/ppermute | solution.py:335
  35.6 3.5 %collective-permute-start.12 = (bf16[64,1536]{1,0:T(8,128)(2,1)S(1)}, bf16[64,1536]{1,0:T(8,128)(2,1)S(1)}, u32[]{:S(2)}, u32[]{:S(2)}) collective-permute-start(bf16[64,1536]{1,0:T(8,128)(2,1)S(1)} %get-tuple-element.46), channel_id=1, source_target_pairs={{0,1},{1,0},{2,3},{3,2},{4,5},{5,4},{6,7},{7,6},{8,9},{9,8},{10,11... | collective-permute-start | bytes 589832 | tf_op jit(solution)/shard_map/ppermute | solution.py:293
  35.8 8.3 %collective-permute-start.13 = (bf16[64,1024]{1,0:T(8,128)(2,1)S(1)}, bf16[64,1024]{1,0:T(8,128)(2,1)S(1)}, u32[]{:S(2)}, u32[]{:S(2)}) collective-permute-start(bf16[64,1024]{1,0:T(8,128)(2,1)S(1)} %get-tuple-element.45.refs_1_), channel_id=1, source_target_pairs={{0,15},{1,2},{2,1},{3,4},{4,3},{5,6},{6,5},{7,8},{8,7},{9,10},{10,... | collective-permute-start | bytes 393224 | tf_op jit(solution)/shard_map/ppermute | solution.py:294
  39.1 4.9 %collective-permute-start.14 = (bf16[64,256]{1,0:T(8,128)(2,1)S(1)}, bf16[64,256]{1,0:T(8,128)(2,1)S(1)}, u32[]{:S(2)}, u32[]{:S(2)}) collective-permute-start(bf16[64,256]{1,0:T(8,128)(2,1)S(1)} %relay.7.refs_4_), channel_id=1, source_target_pairs={{0,8},{1,11},{2,10},{3,9},{4,12},{5,15},{6,14},{7,13},{8,0},{9,3},... | collective-permute-start | bytes 98312 | tf_op jit(solution)/shard_map/ppermute | solution.py:299
  44.0 1.2 %collective-permute-start.15 = (bf16[64,256]{1,0:T(8,128)(2,1)S(1)}, bf16[64,256]{1,0:T(8,128)(2,1)S(1)}, u32[]{:S(2)}, u32[]{:S(2)}) collective-permute-start(bf16[64,256]{1,0:T(8,128)(2,1)S(1)} %collective-permute-done.14.refs_0_.refs_3_), channel_id=1, source_target_pairs={{0,1},{1,0},{2,3},{3,2},{4,5},{5,4},{6,7},{7,6},{8,9},{9,8},{10,11... | collective-permute-start | bytes 98312 | tf_op jit(solution)/shard_map/ppermute | solution.py:335

commit v6 on v5

--- a/solution.py
+++ b/solution.py
@@ -52,8 +52,11 @@
         self.over = [(i, (i + 1 if i % 2 else i - 1) % devices) for i in range(devices)]
         places = [(l, m) for l in range(loop_size) for m in range(members)]
         self.across = [
-            (l * members + m, (l + self.hops[0]) % loop_size * members + (m ^ (m % 2 * 2)))
-            for l, m in places
+            [
+                (l * members + m, (l + self.hops[0]) % loop_size * members + (m ^ (m % 2 * 2) ^ other))
+                for l, m in places
+            ]
+            for other in range(2)
         ]
         self.routes = [
             [(l * members + m, (l + hop) % loop_size * members + (m + step) % members) for l, m in places]
@@ -86,17 +89,17 @@
         message_ref[:, self.shard_len : self.shard_len + 2 * self.width] = upper
         message_ref[:, self.shard_len + 2 * self.width :] = lower
 
-    def relay_far(self, keep_ref, message_ref, out_ref):
+    def relay_far(self, index_ref, keep_ref, message_ref, out_refs):
         upper = message_ref[:, self.shard_len : self.shard_len + 2 * self.width].astype(F32)
         lower = message_ref[:, self.shard_len + 2 * self.width :].astype(F32)
-        out_ref[...] = (keep_ref[...] + (upper + lower)).astype(BF16)
-
-    def far_sum(self, index_ref, far_refs):
-        if not self.paired:
-            return sum(ref[...].astype(F32) for ref in far_refs)
-        both = far_refs[0][...].astype(F32) + far_refs[1][...].astype(F32)
+        total = (keep_ref[...] + (upper + lower)).astype(BF16)
         second = lax.rem(index_ref[0], 2) == 1
-        return jnp.where(second, both[:, self.width :], both[:, : self.width])
+        first, last = total[:, : self.width], total[:, self.width :]
+        out_refs[0][...] = jnp.where(second, last, first)
+        out_refs[1][...] = jnp.where(second, first, last)
+
+    def far_sum(self, far_refs):
+        return sum(ref[...].astype(F32) for ref in far_refs)
 
     def near_sums(self, x_ref, d_ref, acc_ref, first, start_ref=None):
         panels = [self.panel(x_ref, c) for c in range(self.per_device)]
@@ -118,8 +121,8 @@
         def _():
             self.near_sums(x_ref, d_ref, acc_ref, self.per_device, start_ref)
 
-    def next_block(self, index_ref, acc_ref, rb_ref, far_refs):
-        both = jnp.concatenate(halves(self.far_sum(index_ref, far_refs)), axis=1)
+    def next_block(self, acc_ref, rb_ref, far_refs):
+        both = jnp.concatenate(halves(self.far_sum(far_refs)), axis=1)
         return (acc_ref[...] + dot_nn(both, rb_ref[...])).astype(BF16)
 
 
@@ -155,8 +158,8 @@
     plan.send_far(index_ref, x_ref[...], cb_ref, g_ref, sends)
 
 
-def relay_kernel(plan, keep_ref, message_ref, out_ref):
-    plan.relay_far(keep_ref, message_ref, out_ref)
+def relay_kernel(plan, index_ref, keep_ref, message_ref, *out_refs):
+    plan.relay_far(index_ref, keep_ref, message_ref, out_refs)
 
 
 def first_own_kernel(plan, *refs):
@@ -212,15 +215,15 @@
 def finish_kernel(plan, fars, *refs):
     index_ref, acc_ref, rb_ref, cb_ref, g_ref = refs[:5]
     far_refs, (x_ref, *sends) = refs[5 : 5 + fars], refs[5 + fars :]
-    x = plan.next_block(index_ref, acc_ref, rb_ref, far_refs)
+    x = plan.next_block(acc_ref, rb_ref, far_refs)
     x_ref[...] = x
     plan.send_far(index_ref, x, cb_ref, g_ref, sends)
 
 
 def last_kernel(plan, fars, slot, *refs):
-    index_ref, acc_ref, rb_ref = refs[:3]
-    far_refs, (_, krylov_ref, x_ref, sem) = refs[3 : 3 + fars], refs[3 + fars :]
-    x_ref[...] = plan.next_block(index_ref, acc_ref, rb_ref, far_refs)
+    acc_ref, rb_ref = refs[:2]
+    far_refs, (_, krylov_ref, x_ref, sem) = refs[2 : 2 + fars], refs[2 + fars :]
+    x_ref[...] = plan.next_block(acc_ref, rb_ref, far_refs)
     copy = pltpu.make_async_copy(x_ref, krylov_ref.at[slot], sem)
     copy.start()
     copy.wait()
@@ -255,7 +258,7 @@
     rhs, shard_len, width = plan.rhs, plan.shard_len, plan.width
     block_out = pltpu.VMEM((rhs, shard_len), BF16)
     acc_out = pltpu.VMEM((rhs, shard_len), F32)
-    relay_out = pltpu.VMEM((rhs, 2 * width), BF16)
+    relay_out = pltpu.VMEM((rhs, width), BF16)
     krylov_out = jax.ShapeDtypeStruct((PRODUCTS, rhs, shard_len), BF16)
     if plan.paired:
         sends_out = [
@@ -293,13 +296,18 @@
         near = lax.ppermute(sends[0] if plan.paired else current, axes, plan.near)
         over = lax.ppermute(block if product == 0 else current, axes, plan.over)
         if plan.paired:
-            (relayed,) = call(
-                functools.partial(relay_kernel, plan), "relay", [sends[1], near], [IN_VMEM] * 2, [relay_out]
-            )
-            fars = [lax.ppermute(relayed, axes, plan.across)]
+            sends = call(
+                functools.partial(relay_kernel, plan),
+                "relay",
+                [index, sends[1], near],
+                [IN_SMEM] + [IN_VMEM] * 2,
+                [relay_out] * 2,
+            )
+            routes = plan.across
         else:
-            fars = [lax.ppermute(s, axes, route) for s, route in zip(sends, plan.routes)]
-        after = [relayed] if plan.paired else []
+            routes = plan.routes
+        fars = [lax.ppermute(s, axes, route) for s, route in zip(sends, routes)]
+        after = sends if plan.paired else []
         if product == 0:
             acc, dense, row_wide = call(
                 functools.partial(first_own_kernel, plan),
@@ -330,14 +338,11 @@
                 [pltpu.SemaphoreType.DMA],
                 {len(ins) - 1: 1} if product > 1 else None,
             )
-        after = list(fars) if plan.paired else []
-        if plan.paired:
-            fars.append(lax.ppermute(fars[0], axes, plan.near))
         (acc,) = call(
             functools.partial(halo_kernel, plan),
             "halo",
-            [index, acc, over, dense, *after],
-            [IN_SMEM] + [IN_VMEM] * 3 + [ANYWHERE] * len(after),
+            [index, acc, over, dense],
+            [IN_SMEM] + [IN_VMEM] * 3,
             [acc_out],
         )
         if product < PRODUCTS - 1:
@@ -350,12 +355,12 @@
                 [block_out, *sends_out],
             )
         else:
-            ins = [index, acc, row_wide, *fars, krylov]
+            ins = [acc, row_wide, *fars, krylov]
             (krylov,) = call(
                 functools.partial(last_kernel, plan, len(fars), product),
                 "last",
                 ins,
-                [IN_SMEM] + [IN_VMEM] * (len(ins) - 2) + [ANYWHERE],
+                [IN_VMEM] * (len(ins) - 1) + [ANYWHERE],
                 [krylov_out],
                 [ANYWHERE],
                 [pltpu.VMEM((rhs, shard_len), BF16), pltpu.SemaphoreType.DMA],

time: 46.3 us -> 44.4 us (0.959)
  waiting for transfers between devices: 11.6 us -> 4.27 us
  starting transfers between devices: 18.8 us -> 24.4 us
    ppermute x8, waiting for transfers between devices: 11.6 us -> 1.45 us  [on_device(): fars = [lax.ppermute(s, axes, route) for s, route in zip(sends, routes)]]
    ppermute x8, starting transfers between devices: 2.17 us -> 7.62 us  [on_device(): fars = [lax.ppermute(s, axes, route) for s, route in zip(sends, routes)]]
    ppermute x4, waiting for transfers between devices: 0.01 us -> 2.81 us  [on_device(): over = lax.ppermute(block if product == 0 else current, axes, plan.over)]
    ppermute x4, starting transfers between devices: 1.45 us -> 2.19 us  [on_device(): near = lax.ppermute(sends[0] if plan.paired else current, axes, plan.near)]
    ppermute x4, starting transfers between devices: 15.2 us -> 14.6 us  [on_device(): over = lax.ppermute(block if product == 0 else current, axes, plan.over)]
  transfers between devices with their start and end apart: 16 -> 16, of which waited for: 7 -> 4; matrix products, arithmetic and copies ran while one was open for 0% -> 0% of each run, Pallas kernels for 24% -> 24%
where the time goes in v6:
time: 44.4 us; the launch traced here: 44.3 us
  starting transfers between devices  24.4 us (55%)
  Pallas kernels  15.4 us (35%)
  waiting for transfers between devices  4.27 us (10%)
    pallas_call x17, Pallas kernels, call(): pl.pallas_call(kernel, in_specs=list(specs), out_specs=out_specs or [IN_V...  15.4 us
    ppermute x4, starting transfers between devices, on_device(): over = lax.ppermute(block if product == 0 else current, axes, plan.over)  14.6 us
    ppermute x8, starting transfers between devices, on_device(): fars = [lax.ppermute(s, axes, route) for s, route in zip(sends, routes)]  7.62 us
    ppermute x4, waiting for transfers between devices, on_device(): over = lax.ppermute(block if product == 0 else current, axes, plan.over)  2.81 us
    ppermute x4, starting transfers between devices, on_device(): near = lax.ppermute(sends[0] if plan.paired else current, axes, plan.near)  2.19 us
    ppermute x8, waiting for transfers between devices, on_device(): fars = [lax.ppermute(s, axes, route) for s, route in zip(sends, routes)]  1.45 us
  transfers between devices with their start and end apart: 16, of which 4 were waited for; matrix products, arithmetic and copies ran while one was open for 0% of the time, Pallas kernels for 24%

profile of v6, /device:TPU:0, one launch (start us, length us, event | category | flops | bytes accessed | tf_op | source)
XLA Modules:
  0.0 44.3 jit_solution(10458930232305138203)
XLA Ops:
  0.0 1.8 %prepare.1 = (bf16[64,1024]{1,0:T(8,128)(2,1)S(1)}, bf16[3,512,128]{2,1,0:T(8,128)(2,1)S(1)}, bf16[128,1024]{1,0:T(8,128)(2,1)S(1)}, bf16[64,1536]{1,0:T(8,128)(2,1)S(1)}, f32[64,256]{1,0:T(8,128)S(1)}) custom-call(s32[1]{0:T(128)} %bitcast.index_ref.refs_0_, s32[32]{0:T(128)} %refs_0_.1, s32[32]{0:T(128)} %refs_1_.1, bf16[64,1024]{1,0:T(8,128)(2,1)} %refs_2_.1, ...), custom_call_target="tpu_custom_call" | custom-call | flops 1000000000 | bytes 4194304 | tf_op jit(solution)/shard_map/prepare/pallas_call | solution.py:238
  1.8 0.5 %collective-permute-start = (bf16[64,1536]{1,0:T(8,128)(2,1)S(1)}, bf16[64,1536]{1,0:T(8,128)(2,1)S(1)}, u32[]{:S(2)}, u32[]{:S(2)}) collective-permute-start(bf16[64,1536]{1,0:T(8,128)(2,1)S(1)} %get-tuple-element.37), channel_id=1, source_target_pairs={{0,1},{1,0},{2,3},{3,2},{4,5},{5,4},{6,7},{7,6},{8,9},{9,8},{10,11... | collective-permute-start | bytes 589832 | tf_op jit(solution)/shard_map/ppermute | solution.py:296
  2.3 5.6 %collective-permute-start.1 = (bf16[64,1024]{1,0:T(8,128)(2,1)}, bf16[64,1024]{1,0:T(8,128)(2,1)S(1)}, u32[]{:S(2)}, u32[]{:S(2)}) collective-permute-start(bf16[64,1024]{1,0:T(8,128)(2,1)} %refs_2_.1), channel_id=1, source_target_pairs={{0,15},{1,2},{2,1},{3,4},{4,3},{5,6},{6,5},{7,8},{8,7},{9,10},{10,... | collective-permute-start | bytes 393224 | tf_op jit(solution)/shard_map/ppermute | solution.py:297
  7.9 0.0 collective-permute-done.message_ref.refs_2_
  8.0 0.1 collective-permute-start.2
  8.0 0.3 collective-permute-start.3
  8.3 4.7 %first_own.1 = (f32[64,1024]{1,0:T(8,128)S(1)}, bf16[36,256,256]{2,1,0:T(8,128)(2,1)S(1)}, bf16[256,1024]{1,0:T(8,128)(2,1)S(1)}) custom-call(s32[1]{0:T(128)} %bitcast.index_ref.refs_0_, bf16[64,1024]{1,0:T(8,128)(2,1)S(1)} %get-tuple-element.36.refs_1_, bf16[64,1536]{1,0:T(8,128)(2,1)S(1)} %collective-permute-done.message_ref.refs_2_, s32[32]{0:T(128)} %refs_3_.3, ...), custom_call_target="tpu_custom_call" | custom-call | flops 1000000000 | bytes 4194304 | tf_op jit(solution)/shard_map/first_own/pallas_call | solution.py:238
  13.0 0.0 collective-permute-done.1.over_ref
  13.0 0.5 %halo.4.refs_1_ = f32[64,1024]{1,0:T(8,128)S(1)} custom-call(s32[1]{0:T(128)} %bitcast.index_ref.refs_0_, f32[64,1024]{1,0:T(8,128)S(1)} %get-tuple-element.41.acc_ref, bf16[64,1024]{1,0:T(8,128)(2,1)S(1)} %collective-permute-done.1.over_ref, bf16[36,256,256]{2,1,0:T(8,128)(2,1)S(1)} %get-tuple-element.42.d_ref.refs_3_), custom_call_target="tpu_custom_call" | custom-call | flops 1000000000 | bytes 4194304 | tf_op jit(solution)/shard_map/halo/pallas_call | solution.py:238
  13.5 0.0 collective-permute-done.2.refs_5_
  13.5 0.0 collective-permute-done.3.refs_6_
  13.6 0.7 %finish.3 = (bf16[64,1024]{1,0:T(8,128)(2,1)S(1)}, bf16[64,1536]{1,0:T(8,128)(2,1)S(1)}, f32[64,256]{1,0:T(8,128)S(1)}) custom-call(s32[1]{0:T(128)} %bitcast.index_ref.refs_0_, f32[64,1024]{1,0:T(8,128)S(1)} %halo.4.refs_1_, bf16[256,1024]{1,0:T(8,128)(2,1)S(1)} %get-tuple-element.43.refs_2_.refs_1_, bf16[128,1024]{1,0:T(8,128)(2,1)S(1)} %get-tuple-element.44.refs_3_, ...), custom_call_target="tpu_custom_call" | custom-call | flops 1000000000 | bytes 4194304 | tf_op jit(solution)/shard_map/finish/pallas_call | solution.py:238
  14.3 0.7 %collective-permute-start.4 = (bf16[64,1536]{1,0:T(8,128)(2,1)S(1)}, bf16[64,1536]{1,0:T(8,128)(2,1)S(1)}, u32[]{:S(2)}, u32[]{:S(2)}) collective-permute-start(bf16[64,1536]{1,0:T(8,128)(2,1)S(1)} %get-tuple-element.47), channel_id=1, source_target_pairs={{0,1},{1,0},{2,3},{3,2},{4,5},{5,4},{6,7},{7,6},{8,9},{9,8},{10,11... | collective-permute-start | bytes 589832 | tf_op jit(solution)/shard_map/ppermute | solution.py:296
  14.9 3.4 %collective-permute-start.5 = (bf16[64,1024]{1,0:T(8,128)(2,1)S(1)}, bf16[64,1024]{1,0:T(8,128)(2,1)S(1)}, u32[]{:S(2)}, u32[]{:S(2)}) collective-permute-start(bf16[64,1024]{1,0:T(8,128)(2,1)S(1)} %get-tuple-element.46.refs_1_), channel_id=1, source_target_pairs={{0,15},{1,2},{2,1},{3,4},{4,3},{5,6},{6,5},{7,8},{8,7},{9,10},{10,... | collective-permute-start | bytes 393224 | tf_op jit(solution)/shard_map/ppermute | solution.py:297
  18.3 0.0 collective-permute-done.4.message_ref.refs_2_
  18.3 0.3 collective-permute-start.6
  18.6 3.4 %collective-permute-start.7 = (bf16[64,128]{1,0:T(8,128)(2,1)S(1)}, bf16[64,128]{1,0:T(8,128)(2,1)S(1)}, u32[]{:S(2)}, u32[]{:S(2)}) collective-permute-start(bf16[64,128]{1,0:T(8,128)(2,1)S(1)} %get-tuple-element.50.refs_5_), channel_id=1, source_target_pairs={{0,9},{1,10},{2,11},{3,8},{4,13},{5,14},{6,15},{7,12},{8,1},{9,2},... | collective-permute-start | bytes 49160 | tf_op jit(solution)/shard_map/ppermute | solution.py:309
  22.0 1.3 %own.3 = (f32[64,1024]{1,0:T(8,128)S(1)}, bf16[4,64,1024]{2,1,0:T(8,128)(2,1)}) custom-call(s32[1]{0:T(128)} %bitcast.index_ref.refs_0_, bf16[64,1024]{1,0:T(8,128)(2,1)S(1)} %get-tuple-element.46.refs_1_, bf16[64,1536]{1,0:T(8,128)(2,1)S(1)} %collective-permute-done.4.message_ref.refs_2_, bf16[36,256,256]{2,1,0:T(8,128)(2,1)S(1)} %get-tuple-element.42.d_ref.refs_3_, ...), custom_call_target="tpu_custom_call" | custom-call | flops 1000000000 | bytes 4194304 | tf_op jit(solution)/shard_map/own/pallas_call | solution.py:238
  23.3 0.0 collective-permute-done.5.over_ref
  23.3 0.5 %halo.5.refs_1_ = f32[64,1024]{1,0:T(8,128)S(1)} custom-call(s32[1]{0:T(128)} %bitcast.index_ref.refs_0_, f32[64,1024]{1,0:T(8,128)S(1)} %get-tuple-element.51.acc_ref, bf16[64,1024]{1,0:T(8,128)(2,1)S(1)} %collective-permute-done.5.over_ref, bf16[36,256,256]{2,1,0:T(8,128)(2,1)S(1)} %get-tuple-element.42.d_ref.refs_3_), custom_call_target="tpu_custom_call" | custom-call | flops 1000000000 | bytes 4194304 | tf_op jit(solution)/shard_map/halo/pallas_call | solution.py:238
  23.8 0.0 collective-permute-done.6.refs_5_
  23.9 0.0 collective-permute-done.7.refs_6_
  23.9 0.7 %finish.4 = (bf16[64,1024]{1,0:T(8,128)(2,1)S(1)}, bf16[64,1536]{1,0:T(8,128)(2,1)S(1)}, f32[64,256]{1,0:T(8,128)S(1)}) custom-call(s32[1]{0:T(128)} %bitcast.index_ref.refs_0_, f32[64,1024]{1,0:T(8,128)S(1)} %halo.5.refs_1_, bf16[256,1024]{1,0:T(8,128)(2,1)S(1)} %get-tuple-element.43.refs_2_.refs_1_, bf16[128,1024]{1,0:T(8,128)(2,1)S(1)} %get-tuple-element.44.refs_3_, ...), custom_call_target="tpu_custom_call" | custom-call | flops 1000000000 | bytes 4194304 | tf_op jit(solution)/shard_map/finish/pallas_call | solution.py:238
  24.6 0.5 %collective-permute-start.8 = (bf16[64,1536]{1,0:T(8,128)(2,1)S(1)}, bf16[64,1536]{1,0:T(8,128)(2,1)S(1)}, u32[]{:S(2)}, u32[]{:S(2)}) collective-permute-start(bf16[64,1536]{1,0:T(8,128)(2,1)S(1)} %get-tuple-element.53), channel_id=1, source_target_pairs={{0,1},{1,0},{2,3},{3,2},{4,5},{5,4},{6,7},{7,6},{8,9},{9,8},{10,11... | collective-permute-start | bytes 589832 | tf_op jit(solution)/shard_map/ppermute | solution.py:296
  25.0 2.7 %collective-permute-start.9 = (bf16[64,1024]{1,0:T(8,128)(2,1)S(1)}, bf16[64,1024]{1,0:T(8,128)(2,1)S(1)}, u32[]{:S(2)}, u32[]{:S(2)}) collective-permute-start(bf16[64,1024]{1,0:T(8,128)(2,1)S(1)} %get-tuple-element.52.refs_1_), channel_id=1, source_target_pairs={{0,15},{1,2},{2,1},{3,4},{4,3},{5,6},{6,5},{7,8},{8,7},{9,10},{10,... | collective-permute-start | bytes 393224 | tf_op jit(solution)/shard_map/ppermute | solution.py:297
  27.8 0.0 collective-permute-done.8.message_ref.refs_2_
  27.8 0.8 %collective-permute-start.10 = (bf16[64,128]{1,0:T(8,128)(2,1)S(1)}, bf16[64,128]{1,0:T(8,128)(2,1)S(1)}, u32[]{:S(2)}, u32[]{:S(2)}) collective-permute-start(bf16[64,128]{1,0:T(8,128)(2,1)S(1)} %get-tuple-element.55.refs_4_), channel_id=1, source_target_pairs={{0,8},{1,11},{2,10},{3,9},{4,12},{5,15},{6,14},{7,13},{8,0},{9,3},... | collective-permute-start | bytes 49160 | tf_op jit(solution)/shard_map/ppermute | solution.py:309
  28.6 0.9 %collective-permute-start.11 = (bf16[64,128]{1,0:T(8,128)(2,1)S(1)}, bf16[64,128]{1,0:T(8,128)(2,1)S(1)}, u32[]{:S(2)}, u32[]{:S(2)}) collective-permute-start(bf16[64,128]{1,0:T(8,128)(2,1)S(1)} %get-tuple-element.56.refs_5_), channel_id=1, source_target_pairs={{0,9},{1,10},{2,11},{3,8},{4,13},{5,14},{6,15},{7,12},{8,1},{9,2},... | collective-permute-start | bytes 49160 | tf_op jit(solution)/shard_map/ppermute | solution.py:309
  29.5 1.3 %own.4 = (f32[64,1024]{1,0:T(8,128)S(1)}, bf16[4,64,1024]{2,1,0:T(8,128)(2,1)}) custom-call(s32[1]{0:T(128)} %bitcast.index_ref.refs_0_, bf16[64,1024]{1,0:T(8,128)(2,1)S(1)} %get-tuple-element.52.refs_1_, bf16[64,1536]{1,0:T(8,128)(2,1)S(1)} %collective-permute-done.8.message_ref.refs_2_, ...), custom_call_target="tpu_custom_call", output_to_operand_aliasing={{1}: (6, {})} | custom-call | flops 1000000000 | bytes 4194304 | tf_op jit(solution)/shard_map/own/pallas_call | solution.py:238
  30.8 1.6 %collective-permute-done.9.over_ref = bf16[64,1024]{1,0:T(8,128)(2,1)S(1)} collective-permute-done((bf16[64,1024]{1,0:T(8,128)(2,1)S(1)}, bf16[64,1024]{1,0:T(8,128)(2,1)S(1)}, u32[]{:S(2)}, u32[]{:S(2)}) %collective-permute-start.9) | collective-permute-done | bytes 131104 | tf_op jit(solution)/shard_map/ppermute | solution.py:297
  32.4 0.5 %halo.6.refs_1_ = f32[64,1024]{1,0:T(8,128)S(1)} custom-call(s32[1]{0:T(128)} %bitcast.index_ref.refs_0_, f32[64,1024]{1,0:T(8,128)S(1)} %get-tuple-element.58.acc_ref, bf16[64,1024]{1,0:T(8,128)(2,1)S(1)} %collective-permute-done.9.over_ref, bf16[36,256,256]{2,1,0:T(8,128)(2,1)S(1)} %get-tuple-element.42.d_ref.refs_3_), custom_call_target="tpu_custom_call" | custom-call | flops 1000000000 | bytes 4194304 | tf_op jit(solution)/shard_map/halo/pallas_call | solution.py:238
  32.9 0.0 collective-permute-done.10.refs_5_
  32.9 0.6 %collective-permute-done.11.refs_6_ = bf16[64,128]{1,0:T(8,128)(2,1)S(1)} collective-permute-done((bf16[64,128]{1,0:T(8,128)(2,1)S(1)}, bf16[64,128]{1,0:T(8,128)(2,1)S(1)}, u32[]{:S(2)}, u32[]{:S(2)}) %collective-permute-start.11) | collective-permute-done | bytes 16416 | tf_op jit(solution)/shard_map/ppermute | solution.py:309
  33.5 0.7 %finish.5 = (bf16[64,1024]{1,0:T(8,128)(2,1)S(1)}, bf16[64,1536]{1,0:T(8,128)(2,1)S(1)}, f32[64,256]{1,0:T(8,128)S(1)}) custom-call(s32[1]{0:T(128)} %bitcast.index_ref.refs_0_, f32[64,1024]{1,0:T(8,128)S(1)} %halo.6.refs_1_, bf16[256,1024]{1,0:T(8,128)(2,1)S(1)} %get-tuple-element.43.refs_2_.refs_1_, bf16[128,1024]{1,0:T(8,128)(2,1)S(1)} %get-tuple-element.44.refs_3_, ...), custom_call_target="tpu_custom_call" | custom-call | flops 1000000000 | bytes 4194304 | tf_op jit(solution)/shard_map/finish/pallas_call | solution.py:238
  34.2 0.5 %collective-permute-start.12 = (bf16[64,1536]{1,0:T(8,128)(2,1)S(1)}, bf16[64,1536]{1,0:T(8,128)(2,1)S(1)}, u32[]{:S(2)}, u32[]{:S(2)}) collective-permute-start(bf16[64,1536]{1,0:T(8,128)(2,1)S(1)} %get-tuple-element.60), channel_id=1, source_target_pairs={{0,1},{1,0},{2,3},{3,2},{4,5},{5,4},{6,7},{7,6},{8,9},{9,8},{10,11... | collective-permute-start | bytes 589832 | tf_op jit(solution)/shard_map/ppermute | solution.py:296
  34.8 2.9 %collective-permute-start.13 = (bf16[64,1024]{1,0:T(8,128)(2,1)S(1)}, bf16[64,1024]{1,0:T(8,128)(2,1)S(1)}, u32[]{:S(2)}, u32[]{:S(2)}) collective-permute-start(bf16[64,1024]{1,0:T(8,128)(2,1)S(1)} %get-tuple-element.59.refs_1_), channel_id=1, source_target_pairs={{0,15},{1,2},{2,1},{3,4},{4,3},{5,6},{6,5},{7,8},{8,7},{9,10},{10,... | collective-permute-start | bytes 393224 | tf_op jit(solution)/shard_map/ppermute | solution.py:297
  37.6 0.0 collective-permute-done.12.message_ref.refs_2_
  37.6 0.4 collective-permute-start.14
  38.0 1.6 %collective-permute-start.15 = (bf16[64,128]{1,0:T(8,128)(2,1)S(1)}, bf16[64,128]{1,0:T(8,128)(2,1)S(1)}, u32[]{:S(2)}, u32[]{:S(2)}) collective-permute-start(bf16[64,128]{1,0:T(8,128)(2,1)S(1)} %get-tuple-element.63.refs_5_), channel_id=1, source_target_pairs={{0,9},{1,10},{2,11},{3,8},{4,13},{5,14},{6,15},{7,12},{8,1},{9,2},... | collective-permute-start | bytes 49160 | tf_op jit(solution)/shard_map/ppermute | solution.py:309
  39.6 1.3 %own.5 = (f32[64,1024]{1,0:T(8,128)S(1)}, bf16[4,64,1024]{2,1,0:T(8,128)(2,1)}) custom-call(s32[1]{0:T(128)} %bitcast.index_ref.refs_0_, bf16[64,1024]{1,0:T(8,128)(2,1)S(1)} %get-tuple-element.59.refs_1_, bf16[64,1536]{1,0:T(8,128)(2,1)S(1)} %collective-permute-done.12.message_ref.refs_2_, ...), custom_call_target="tpu_custom_call", output_to_operand_aliasing={{1}: (6, {})} | custom-call | flops 1000000000 | bytes 4194304 | tf_op jit(solution)/shard_map/own/pallas_call | solution.py:238
  40.9 1.2 %collective-permute-done.13.over_ref = bf16[64,1024]{1,0:T(8,128)(2,1)S(1)} collective-permute-done((bf16[64,1024]{1,0:T(8,128)(2,1)S(1)}, bf16[64,1024]{1,0:T(8,128)(2,1)S(1)}, u32[]{:S(2)}, u32[]{:S(2)}) %collective-permute-start.13) | collective-permute-done | bytes 131104 | tf_op jit(solution)/shard_map/ppermute | solution.py:297
  42.0 0.5 %halo.7.refs_0_ = f32[64,1024]{1,0:T(8,128)S(1)} custom-call(s32[1]{0:T(128)} %bitcast.index_ref.refs_0_, f32[64,1024]{1,0:T(8,128)S(1)} %get-tuple-element.65.acc_ref, bf16[64,1024]{1,0:T(8,128)(2,1)S(1)} %collective-permute-done.13.over_ref, bf16[36,256,256]{2,1,0:T(8,128)(2,1)S(1)} %get-tuple-element.42.d_ref.refs_3_), custom_call_target="tpu_custom_call" | custom-call | flops 1000000000 | bytes 4194304 | tf_op jit(solution)/shard_map/halo/pallas_call | solution.py:238
  42.6 0.0 collective-permute-done.14.refs_2_
  42.6 0.8 %collective-permute-done.15.refs_3_ = bf16[64,128]{1,0:T(8,128)(2,1)S(1)} collective-permute-done((bf16[64,128]{1,0:T(8,128)(2,1)S(1)}, bf16[64,128]{1,0:T(8,128)(2,1)S(1)}, u32[]{:S(2)}, u32[]{:S(2)}) %collective-permute-start.15) | collective-permute-done | bytes 16416 | tf_op jit(solution)/shard_map/ppermute | solution.py:309
  43.4 0.9 %last.1 = bf16[4,64,1024]{2,1,0:T(8,128)(2,1)} custom-call(f32[64,1024]{1,0:T(8,128)S(1)} %halo.7.refs_0_, bf16[256,1024]{1,0:T(8,128)(2,1)S(1)} %get-tuple-element.43.refs_2_.refs_1_, bf16[64,128]{1,0:T(8,128)(2,1)S(1)} %collective-permute-done.14.refs_2_, bf16[64,128]{1,0:T(8,128)(2,1)S(1)} %collective-permute-done.15.refs_3_, ...), custom_call_target="tpu_custom_call", output_to_operand_aliasing={{}: (4, {})} | custom-call | flops 1000000000 | bytes 4194304 | tf_op jit(solution)/shard_map/last/pallas_call | solution.py:238
  (4 shorter events, 0.1 us)
Async XLA Ops:
  1.8 6.2 %collective-permute-start = (bf16[64,1536]{1,0:T(8,128)(2,1)S(1)}, bf16[64,1536]{1,0:T(8,128)(2,1)S(1)}, u32[]{:S(2)}, u32[]{:S(2)}) collective-permute-start(bf16[64,1536]{1,0:T(8,128)(2,1)S(1)} %get-tuple-element.37), channel_id=1, source_target_pairs={{0,1},{1,0},{2,3},{3,2},{4,5},{5,4},{6,7},{7,6},{8,9},{9,8},{10,11... | collective-permute-start | bytes 589832 | tf_op jit(solution)/shard_map/ppermute | solution.py:296
  2.3 10.7 %collective-permute-start.1 = (bf16[64,1024]{1,0:T(8,128)(2,1)}, bf16[64,1024]{1,0:T(8,128)(2,1)S(1)}, u32[]{:S(2)}, u32[]{:S(2)}) collective-permute-start(bf16[64,1024]{1,0:T(8,128)(2,1)} %refs_2_.1), channel_id=1, source_target_pairs={{0,15},{1,2},{2,1},{3,4},{4,3},{5,6},{6,5},{7,8},{8,7},{9,10},{10,... | collective-permute-start | bytes 393224 | tf_op jit(solution)/shard_map/ppermute | solution.py:297
  8.0 5.6 %collective-permute-start.2 = (bf16[64,128]{1,0:T(8,128)(2,1)S(1)}, bf16[64,128]{1,0:T(8,128)(2,1)S(1)}, u32[]{:S(2)}, u32[]{:S(2)}) collective-permute-start(bf16[64,128]{1,0:T(8,128)(2,1)S(1)} %get-tuple-element.39.refs_7_), channel_id=1, source_target_pairs={{0,8},{1,11},{2,10},{3,9},{4,12},{5,15},{6,14},{7,13},{8,0},{9,3},... | collective-permute-start | bytes 49160 | tf_op jit(solution)/shard_map/ppermute | solution.py:309
  8.0 5.5 %collective-permute-start.3 = (bf16[64,128]{1,0:T(8,128)(2,1)S(1)}, bf16[64,128]{1,0:T(8,128)(2,1)S(1)}, u32[]{:S(2)}, u32[]{:S(2)}) collective-permute-start(bf16[64,128]{1,0:T(8,128)(2,1)S(1)} %get-tuple-element.40.refs_8_), channel_id=1, source_target_pairs={{0,9},{1,10},{2,11},{3,8},{4,13},{5,14},{6,15},{7,12},{8,1},{9,2},... | collective-permute-start | bytes 49160 | tf_op jit(solution)/shard_map/ppermute | solution.py:309
  14.3 4.1 %collective-permute-start.4 = (bf16[64,1536]{1,0:T(8,128)(2,1)S(1)}, bf16[64,1536]{1,0:T(8,128)(2,1)S(1)}, u32[]{:S(2)}, u32[]{:S(2)}) collective-permute-start(bf16[64,1536]{1,0:T(8,128)(2,1)S(1)} %get-tuple-element.47), channel_id=1, source_target_pairs={{0,1},{1,0},{2,3},{3,2},{4,5},{5,4},{6,7},{7,6},{8,9},{9,8},{10,11... | collective-permute-start | bytes 589832 | tf_op jit(solution)/shard_map/ppermute | solution.py:296
  14.9 8.4 %collective-permute-start.5 = (bf16[64,1024]{1,0:T(8,128)(2,1)S(1)}, bf16[64,1024]{1,0:T(8,128)(2,1)S(1)}, u32[]{:S(2)}, u32[]{:S(2)}) collective-permute-start(bf16[64,1024]{1,0:T(8,128)(2,1)S(1)} %get-tuple-element.46.refs_1_), channel_id=1, source_target_pairs={{0,15},{1,2},{2,1},{3,4},{4,3},{5,6},{6,5},{7,8},{8,7},{9,10},{10,... | collective-permute-start | bytes 393224 | tf_op jit(solution)/shard_map/ppermute | solution.py:297
  18.3 5.5 %collective-permute-start.6 = (bf16[64,128]{1,0:T(8,128)(2,1)S(1)}, bf16[64,128]{1,0:T(8,128)(2,1)S(1)}, u32[]{:S(2)}, u32[]{:S(2)}) collective-permute-start(bf16[64,128]{1,0:T(8,128)(2,1)S(1)} %get-tuple-element.49.refs_4_), channel_id=1, source_target_pairs={{0,8},{1,11},{2,10},{3,9},{4,12},{5,15},{6,14},{7,13},{8,0},{9,3},... | collective-permute-start | bytes 49160 | tf_op jit(solution)/shard_map/ppermute | solution.py:309
  18.6 5.2 %collective-permute-start.7 = (bf16[64,128]{1,0:T(8,128)(2,1)S(1)}, bf16[64,128]{1,0:T(8,128)(2,1)S(1)}, u32[]{:S(2)}, u32[]{:S(2)}) collective-permute-start(bf16[64,128]{1,0:T(8,128)(2,1)S(1)} %get-tuple-element.50.refs_5_), channel_id=1, source_target_pairs={{0,9},{1,10},{2,11},{3,8},{4,13},{5,14},{6,15},{7,12},{8,1},{9,2},... | collective-permute-start | bytes 49160 | tf_op jit(solution)/shard_map/ppermute | solution.py:309
  24.6 3.2 %collective-permute-start.8 = (bf16[64,1536]{1,0:T(8,128)(2,1)S(1)}, bf16[64,1536]{1,0:T(8,128)(2,1)S(1)}, u32[]{:S(2)}, u32[]{:S(2)}) collective-permute-start(bf16[64,1536]{1,0:T(8,128)(2,1)S(1)} %get-tuple-element.53), channel_id=1, source_target_pairs={{0,1},{1,0},{2,3},{3,2},{4,5},{5,4},{6,7},{7,6},{8,9},{9,8},{10,11... | collective-permute-start | bytes 589832 | tf_op jit(solution)/shard_map/ppermute | solution.py:296
  25.0 7.4 %collective-permute-start.9 = (bf16[64,1024]{1,0:T(8,128)(2,1)S(1)}, bf16[64,1024]{1,0:T(8,128)(2,1)S(1)}, u32[]{:S(2)}, u32[]{:S(2)}) collective-permute-start(bf16[64,1024]{1,0:T(8,128)(2,1)S(1)} %get-tuple-element.52.refs_1_), channel_id=1, source_target_pairs={{0,15},{1,2},{2,1},{3,4},{4,3},{5,6},{6,5},{7,8},{8,7},{9,10},{10,... | collective-permute-start | bytes 393224 | tf_op jit(solution)/shard_map/ppermute | solution.py:297
  27.8 5.1 %collective-permute-start.10 = (bf16[64,128]{1,0:T(8,128)(2,1)S(1)}, bf16[64,128]{1,0:T(8,128)(2,1)S(1)}, u32[]{:S(2)}, u32[]{:S(2)}) collective-permute-start(bf16[64,128]{1,0:T(8,128)(2,1)S(1)} %get-tuple-element.55.refs_4_), channel_id=1, source_target_pairs={{0,8},{1,11},{2,10},{3,9},{4,12},{5,15},{6,14},{7,13},{8,0},{9,3},... | collective-permute-start | bytes 49160 | tf_op jit(solution)/shard_map/ppermute | solution.py:309
  28.6 5.0 %collective-permute-start.11 = (bf16[64,128]{1,0:T(8,128)(2,1)S(1)}, bf16[64,128]{1,0:T(8,128)(2,1)S(1)}, u32[]{:S(2)}, u32[]{:S(2)}) collective-permute-start(bf16[64,128]{1,0:T(8,128)(2,1)S(1)} %get-tuple-element.56.refs_5_), channel_id=1, source_target_pairs={{0,9},{1,10},{2,11},{3,8},{4,13},{5,14},{6,15},{7,12},{8,1},{9,2},... | collective-permute-start | bytes 49160 | tf_op jit(solution)/shard_map/ppermute | solution.py:309
  34.2 3.4 %collective-permute-start.12 = (bf16[64,1536]{1,0:T(8,128)(2,1)S(1)}, bf16[64,1536]{1,0:T(8,128)(2,1)S(1)}, u32[]{:S(2)}, u32[]{:S(2)}) collective-permute-start(bf16[64,1536]{1,0:T(8,128)(2,1)S(1)} %get-tuple-element.60), channel_id=1, source_target_pairs={{0,1},{1,0},{2,3},{3,2},{4,5},{5,4},{6,7},{7,6},{8,9},{9,8},{10,11... | collective-permute-start | bytes 589832 | tf_op jit(solution)/shard_map/ppermute | solution.py:296
  34.8 7.3 %collective-permute-start.13 = (bf16[64,1024]{1,0:T(8,128)(2,1)S(1)}, bf16[64,1024]{1,0:T(8,128)(2,1)S(1)}, u32[]{:S(2)}, u32[]{:S(2)}) collective-permute-start(bf16[64,1024]{1,0:T(8,128)(2,1)S(1)} %get-tuple-element.59.refs_1_), channel_id=1, source_target_pairs={{0,15},{1,2},{2,1},{3,4},{4,3},{5,6},{6,5},{7,8},{8,7},{9,10},{10,... | collective-permute-start | bytes 393224 | tf_op jit(solution)/shard_map/ppermute | solution.py:297
  37.6 4.9 %collective-permute-start.14 = (bf16[64,128]{1,0:T(8,128)(2,1)S(1)}, bf16[64,128]{1,0:T(8,128)(2,1)S(1)}, u32[]{:S(2)}, u32[]{:S(2)}) collective-permute-start(bf16[64,128]{1,0:T(8,128)(2,1)S(1)} %get-tuple-element.62.refs_4_), channel_id=1, source_target_pairs={{0,8},{1,11},{2,10},{3,9},{4,12},{5,15},{6,14},{7,13},{8,0},{9,3},... | collective-permute-start | bytes 49160 | tf_op jit(solution)/shard_map/ppermute | solution.py:309
  38.0 5.4 %collective-permute-start.15 = (bf16[64,128]{1,0:T(8,128)(2,1)S(1)}, bf16[64,128]{1,0:T(8,128)(2,1)S(1)}, u32[]{:S(2)}, u32[]{:S(2)}) collective-permute-start(bf16[64,128]{1,0:T(8,128)(2,1)S(1)} %get-tuple-element.63.refs_5_), channel_id=1, source_target_pairs={{0,9},{1,10},{2,11},{3,8},{4,13},{5,14},{6,15},{7,12},{8,1},{9,2},... | collective-permute-start | bytes 49160 | tf_op jit(solution)/shard_map/ppermute | solution.py:309

commit v7 on v6

--- a/solution.py
+++ b/solution.py
@@ -53,10 +53,10 @@
         places = [(l, m) for l in range(loop_size) for m in range(members)]
         self.across = [
             [
-                (l * members + m, (l + self.hops[0]) % loop_size * members + (m ^ (m % 2 * 2) ^ other))
+                (l * members + m, (l + self.hops[0]) % loop_size * members + (m ^ other))
                 for l, m in places
             ]
-            for other in range(2)
+            for other in (2, 0)
         ]
         self.routes = [
             [(l * members + m, (l + hop) % loop_size * members + (m + step) % members) for l, m in places]
@@ -80,11 +80,12 @@
             return
         message_ref, keep_ref = out_refs
         (total,) = totals
-        member = self.member(index_ref)
-        second = lax.rem(member, 2) != lax.div(member, 2)
-        first, last = total[:, : 2 * self.width], total[:, 2 * self.width :]
-        keep_ref[...] = jnp.where(second, last, first)
-        upper, lower = halves(jnp.where(second, first, last))
+        pieces = [total[:, i * self.width : (i + 1) * self.width] for i in range(self.members)]
+        even = jnp.concatenate(pieces[0::2], axis=1)
+        odd = jnp.concatenate(pieces[1::2], axis=1)
+        second = lax.rem(index_ref[0], 2) == 1
+        keep_ref[...] = jnp.where(second, odd, even)
+        upper, lower = halves(jnp.where(second, even, odd))
         message_ref[:, : self.shard_len] = x
         message_ref[:, self.shard_len : self.shard_len + 2 * self.width] = upper
         message_ref[:, self.shard_len + 2 * self.width :] = lower
@@ -93,10 +94,10 @@
         upper = message_ref[:, self.shard_len : self.shard_len + 2 * self.width].astype(F32)
         lower = message_ref[:, self.shard_len + 2 * self.width :].astype(F32)
         total = (keep_ref[...] + (upper + lower)).astype(BF16)
-        second = lax.rem(index_ref[0], 2) == 1
+        second = self.member(index_ref) >= 2
         first, last = total[:, : self.width], total[:, self.width :]
-        out_refs[0][...] = jnp.where(second, last, first)
-        out_refs[1][...] = jnp.where(second, first, last)
+        out_refs[0][...] = jnp.where(second, first, last)
+        out_refs[1][...] = jnp.where(second, last, first)
 
     def far_sum(self, far_refs):
         return sum(ref[...].astype(F32) for ref in far_refs)

time: 44.4 us -> 45.8 us (1.032)
  waiting for transfers between devices: 4.27 us -> 5.28 us
    ppermute x8, waiting for transfers between devices: 1.45 us -> 3.25 us  [on_device(): fars = [lax.ppermute(s, axes, route) for s, route in zip(sends, routes)]]
    ppermute x4, starting transfers between devices: 14.6 us -> 16.2 us  [on_device(): over = lax.ppermute(block if product == 0 else current, axes, plan.over)]
    ppermute x4, starting transfers between devices: 2.19 us -> 0.74 us  [on_device(): near = lax.ppermute(sends[0] if plan.paired else current, axes, plan.near)]
    ppermute x4, waiting for transfers between devices: 2.81 us -> 2.02 us  [on_device(): over = lax.ppermute(block if product == 0 else current, axes, plan.over)]
  transfers between devices with their start and end apart: 16 -> 16, of which waited for: 4 -> 6; matrix products, arithmetic and copies ran while one was open for 0% -> 0% of each run, Pallas kernels for 24% -> 24%
where the time goes in v7:
time: 45.8 us; the launch traced here: 45.6 us
  starting transfers between devices  24.5 us (53%)
  Pallas kernels  15.7 us (34%)
  waiting for transfers between devices  5.28 us (12%)
    ppermute x4, starting transfers between devices, on_device(): over = lax.ppermute(block if product == 0 else current, axes, plan.over)  16.2 us
    pallas_call x17, Pallas kernels, call(): pl.pallas_call(kernel, in_specs=list(specs), out_specs=out_specs or [IN_V...  15.7 us
    ppermute x8, starting transfers between devices, on_device(): fars = [lax.ppermute(s, axes, route) for s, route in zip(sends, routes)]  7.63 us
    ppermute x8, waiting for transfers between devices, on_device(): fars = [lax.ppermute(s, axes, route) for s, route in zip(sends, routes)]  3.25 us
    ppermute x4, waiting for transfers between devices, on_device(): over = lax.ppermute(block if product == 0 else current, axes, plan.over)  2.02 us
  transfers between devices with their start and end apart: 16, of which 6 were waited for; matrix products, arithmetic and copies ran while one was open for 0% of the time, Pallas kernels for 24%

profile of v7, /device:TPU:0, one launch (start us, length us, event | category | flops | bytes accessed | tf_op | source)
XLA Modules:
  0.0 45.6 jit_solution(14781916909066513726)
XLA Ops:
  0.0 1.8 %prepare.1 = (bf16[64,1024]{1,0:T(8,128)(2,1)S(1)}, bf16[3,512,128]{2,1,0:T(8,128)(2,1)S(1)}, bf16[128,1024]{1,0:T(8,128)(2,1)S(1)}, bf16[64,1536]{1,0:T(8,128)(2,1)S(1)}, f32[64,256]{1,0:T(8,128)S(1)}) custom-call(s32[1]{0:T(128)} %bitcast.index_ref.refs_0_, s32[32]{0:T(128)} %refs_0_.1, s32[32]{0:T(128)} %refs_1_.1, bf16[64,1024]{1,0:T(8,128)(2,1)} %refs_2_.1, ...), custom_call_target="tpu_custom_call" | custom-call | flops 1000000000 | bytes 4194304 | tf_op jit(solution)/shard_map/prepare/pallas_call | solution.py:239
  1.8 0.5 %collective-permute-start = (bf16[64,1536]{1,0:T(8,128)(2,1)S(1)}, bf16[64,1536]{1,0:T(8,128)(2,1)S(1)}, u32[]{:S(2)}, u32[]{:S(2)}) collective-permute-start(bf16[64,1536]{1,0:T(8,128)(2,1)S(1)} %get-tuple-element.37), channel_id=1, source_target_pairs={{0,1},{1,0},{2,3},{3,2},{4,5},{5,4},{6,7},{7,6},{8,9},{9,8},{10,11... | collective-permute-start | bytes 589832 | tf_op jit(solution)/shard_map/ppermute | solution.py:297
  2.3 5.6 %collective-permute-start.1 = (bf16[64,1024]{1,0:T(8,128)(2,1)}, bf16[64,1024]{1,0:T(8,128)(2,1)S(1)}, u32[]{:S(2)}, u32[]{:S(2)}) collective-permute-start(bf16[64,1024]{1,0:T(8,128)(2,1)} %refs_2_.1), channel_id=1, source_target_pairs={{0,15},{1,2},{2,1},{3,4},{4,3},{5,6},{6,5},{7,8},{8,7},{9,10},{10,... | collective-permute-start | bytes 393224 | tf_op jit(solution)/shard_map/ppermute | solution.py:298
  7.9 0.0 collective-permute-done.message_ref.refs_2_
  8.0 0.4 collective-permute-start.2
  8.3 0.3 collective-permute-start.3
  8.7 5.0 %first_own.1 = (f32[64,1024]{1,0:T(8,128)S(1)}, bf16[36,256,256]{2,1,0:T(8,128)(2,1)S(1)}, bf16[256,1024]{1,0:T(8,128)(2,1)S(1)}) custom-call(s32[1]{0:T(128)} %bitcast.index_ref.refs_0_, bf16[64,1024]{1,0:T(8,128)(2,1)S(1)} %get-tuple-element.36.refs_1_, bf16[64,1536]{1,0:T(8,128)(2,1)S(1)} %collective-permute-done.message_ref.refs_2_, s32[32]{0:T(128)} %refs_3_.3, ...), custom_call_target="tpu_custom_call" | custom-call | flops 1000000000 | bytes 4194304 | tf_op jit(solution)/shard_map/first_own/pallas_call | solution.py:239
  13.7 0.0 collective-permute-done.1.over_ref
  13.7 0.5 %halo.4.refs_1_ = f32[64,1024]{1,0:T(8,128)S(1)} custom-call(s32[1]{0:T(128)} %bitcast.index_ref.refs_0_, f32[64,1024]{1,0:T(8,128)S(1)} %get-tuple-element.41.acc_ref, bf16[64,1024]{1,0:T(8,128)(2,1)S(1)} %collective-permute-done.1.over_ref, bf16[36,256,256]{2,1,0:T(8,128)(2,1)S(1)} %get-tuple-element.42.d_ref.refs_3_), custom_call_target="tpu_custom_call" | custom-call | flops 1000000000 | bytes 4194304 | tf_op jit(solution)/shard_map/halo/pallas_call | solution.py:239
  14.2 0.0 collective-permute-done.2.refs_5_
  14.2 0.0 collective-permute-done.3.refs_6_
  14.2 0.7 %finish.3 = (bf16[64,1024]{1,0:T(8,128)(2,1)S(1)}, bf16[64,1536]{1,0:T(8,128)(2,1)S(1)}, f32[64,256]{1,0:T(8,128)S(1)}) custom-call(s32[1]{0:T(128)} %bitcast.index_ref.refs_0_, f32[64,1024]{1,0:T(8,128)S(1)} %halo.4.refs_1_, bf16[256,1024]{1,0:T(8,128)(2,1)S(1)} %get-tuple-element.43.refs_2_.refs_1_, bf16[128,1024]{1,0:T(8,128)(2,1)S(1)} %get-tuple-element.44.refs_3_, ...), custom_call_target="tpu_custom_call" | custom-call | flops 1000000000 | bytes 4194304 | tf_op jit(solution)/shard_map/finish/pallas_call | solution.py:239
  14.9 0.1 collective-permute-start.4
  15.0 3.7 %collective-permute-start.5 = (bf16[64,1024]{1,0:T(8,128)(2,1)S(1)}, bf16[64,1024]{1,0:T(8,128)(2,1)S(1)}, u32[]{:S(2)}, u32[]{:S(2)}) collective-permute-start(bf16[64,1024]{1,0:T(8,128)(2,1)S(1)} %get-tuple-element.46.refs_1_), channel_id=1, source_target_pairs={{0,15},{1,2},{2,1},{3,4},{4,3},{5,6},{6,5},{7,8},{8,7},{9,10},{10,... | collective-permute-start | bytes 393224 | tf_op jit(solution)/shard_map/ppermute | solution.py:298
  18.6 0.0 collective-permute-done.4.message_ref.refs_2_
  18.7 1.0 %collective-permute-start.6 = (bf16[64,128]{1,0:T(8,128)(2,1)S(1)}, bf16[64,128]{1,0:T(8,128)(2,1)S(1)}, u32[]{:S(2)}, u32[]{:S(2)}) collective-permute-start(bf16[64,128]{1,0:T(8,128)(2,1)S(1)} %get-tuple-element.49.refs_4_), channel_id=1, source_target_pairs={{0,10},{1,11},{2,8},{3,9},{4,14},{5,15},{6,12},{7,13},{8,2},{9,3},... | collective-permute-start | bytes 49160 | tf_op jit(solution)/shard_map/ppermute | solution.py:310
  19.7 2.9 %collective-permute-start.7 = (bf16[64,128]{1,0:T(8,128)(2,1)S(1)}, bf16[64,128]{1,0:T(8,128)(2,1)S(1)}, u32[]{:S(2)}, u32[]{:S(2)}) collective-permute-start(bf16[64,128]{1,0:T(8,128)(2,1)S(1)} %get-tuple-element.50.refs_5_), channel_id=1, source_target_pairs={{0,8},{1,9},{2,10},{3,11},{4,12},{5,13},{6,14},{7,15},{8,0},{9,1},... | collective-permute-start | bytes 49160 | tf_op jit(solution)/shard_map/ppermute | solution.py:310
  22.6 1.3 %own.3 = (f32[64,1024]{1,0:T(8,128)S(1)}, bf16[4,64,1024]{2,1,0:T(8,128)(2,1)}) custom-call(s32[1]{0:T(128)} %bitcast.index_ref.refs_0_, bf16[64,1024]{1,0:T(8,128)(2,1)S(1)} %get-tuple-element.46.refs_1_, bf16[64,1536]{1,0:T(8,128)(2,1)S(1)} %collective-permute-done.4.message_ref.refs_2_, bf16[36,256,256]{2,1,0:T(8,128)(2,1)S(1)} %get-tuple-element.42.d_ref.refs_3_, ...), custom_call_target="tpu_custom_call" | custom-call | flops 1000000000 | bytes 4194304 | tf_op jit(solution)/shard_map/own/pallas_call | solution.py:239
  23.9 0.0 collective-permute-done.5.over_ref
  23.9 0.5 %halo.5.refs_1_ = f32[64,1024]{1,0:T(8,128)S(1)} custom-call(s32[1]{0:T(128)} %bitcast.index_ref.refs_0_, f32[64,1024]{1,0:T(8,128)S(1)} %get-tuple-element.51.acc_ref, bf16[64,1024]{1,0:T(8,128)(2,1)S(1)} %collective-permute-done.5.over_ref, bf16[36,256,256]{2,1,0:T(8,128)(2,1)S(1)} %get-tuple-element.42.d_ref.refs_3_), custom_call_target="tpu_custom_call" | custom-call | flops 1000000000 | bytes 4194304 | tf_op jit(solution)/shard_map/halo/pallas_call | solution.py:239
  24.4 0.0 collective-permute-done.6.refs_5_
  24.4 0.1 collective-permute-done.7.refs_6_
  24.5 0.7 %finish.4 = (bf16[64,1024]{1,0:T(8,128)(2,1)S(1)}, bf16[64,1536]{1,0:T(8,128)(2,1)S(1)}, f32[64,256]{1,0:T(8,128)S(1)}) custom-call(s32[1]{0:T(128)} %bitcast.index_ref.refs_0_, f32[64,1024]{1,0:T(8,128)S(1)} %halo.5.refs_1_, bf16[256,1024]{1,0:T(8,128)(2,1)S(1)} %get-tuple-element.43.refs_2_.refs_1_, bf16[128,1024]{1,0:T(8,128)(2,1)S(1)} %get-tuple-element.44.refs_3_, ...), custom_call_target="tpu_custom_call" | custom-call | flops 1000000000 | bytes 4194304 | tf_op jit(solution)/shard_map/finish/pallas_call | solution.py:239
  25.2 0.1 collective-permute-start.8
  25.2 3.9 %collective-permute-start.9 = (bf16[64,1024]{1,0:T(8,128)(2,1)S(1)}, bf16[64,1024]{1,0:T(8,128)(2,1)S(1)}, u32[]{:S(2)}, u32[]{:S(2)}) collective-permute-start(bf16[64,1024]{1,0:T(8,128)(2,1)S(1)} %get-tuple-element.52.refs_1_), channel_id=1, source_target_pairs={{0,15},{1,2},{2,1},{3,4},{4,3},{5,6},{6,5},{7,8},{8,7},{9,10},{10,... | collective-permute-start | bytes 393224 | tf_op jit(solution)/shard_map/ppermute | solution.py:298
  29.1 0.0 collective-permute-done.8.message_ref.refs_2_
  29.2 0.5 %collective-permute-start.10 = (bf16[64,128]{1,0:T(8,128)(2,1)S(1)}, bf16[64,128]{1,0:T(8,128)(2,1)S(1)}, u32[]{:S(2)}, u32[]{:S(2)}) collective-permute-start(bf16[64,128]{1,0:T(8,128)(2,1)S(1)} %get-tuple-element.55.refs_4_), channel_id=1, source_target_pairs={{0,10},{1,11},{2,8},{3,9},{4,14},{5,15},{6,12},{7,13},{8,2},{9,3},... | collective-permute-start | bytes 49160 | tf_op jit(solution)/shard_map/ppermute | solution.py:310
  29.7 0.8 %collective-permute-start.11 = (bf16[64,128]{1,0:T(8,128)(2,1)S(1)}, bf16[64,128]{1,0:T(8,128)(2,1)S(1)}, u32[]{:S(2)}, u32[]{:S(2)}) collective-permute-start(bf16[64,128]{1,0:T(8,128)(2,1)S(1)} %get-tuple-element.56.refs_5_), channel_id=1, source_target_pairs={{0,8},{1,9},{2,10},{3,11},{4,12},{5,13},{6,14},{7,15},{8,0},{9,1},... | collective-permute-start | bytes 49160 | tf_op jit(solution)/shard_map/ppermute | solution.py:310
  30.4 1.3 %own.4 = (f32[64,1024]{1,0:T(8,128)S(1)}, bf16[4,64,1024]{2,1,0:T(8,128)(2,1)}) custom-call(s32[1]{0:T(128)} %bitcast.index_ref.refs_0_, bf16[64,1024]{1,0:T(8,128)(2,1)S(1)} %get-tuple-element.52.refs_1_, bf16[64,1536]{1,0:T(8,128)(2,1)S(1)} %collective-permute-done.8.message_ref.refs_2_, ...), custom_call_target="tpu_custom_call", output_to_operand_aliasing={{1}: (6, {})} | custom-call | flops 1000000000 | bytes 4194304 | tf_op jit(solution)/shard_map/own/pallas_call | solution.py:239
  31.7 0.8 %collective-permute-done.9.over_ref = bf16[64,1024]{1,0:T(8,128)(2,1)S(1)} collective-permute-done((bf16[64,1024]{1,0:T(8,128)(2,1)S(1)}, bf16[64,1024]{1,0:T(8,128)(2,1)S(1)}, u32[]{:S(2)}, u32[]{:S(2)}) %collective-permute-start.9) | collective-permute-done | bytes 131104 | tf_op jit(solution)/shard_map/ppermute | solution.py:298
  32.5 0.5 %halo.6.refs_1_ = f32[64,1024]{1,0:T(8,128)S(1)} custom-call(s32[1]{0:T(128)} %bitcast.index_ref.refs_0_, f32[64,1024]{1,0:T(8,128)S(1)} %get-tuple-element.58.acc_ref, bf16[64,1024]{1,0:T(8,128)(2,1)S(1)} %collective-permute-done.9.over_ref, bf16[36,256,256]{2,1,0:T(8,128)(2,1)S(1)} %get-tuple-element.42.d_ref.refs_3_), custom_call_target="tpu_custom_call" | custom-call | flops 1000000000 | bytes 4194304 | tf_op jit(solution)/shard_map/halo/pallas_call | solution.py:239
  33.0 1.7 %collective-permute-done.10.refs_5_ = bf16[64,128]{1,0:T(8,128)(2,1)S(1)} collective-permute-done((bf16[64,128]{1,0:T(8,128)(2,1)S(1)}, bf16[64,128]{1,0:T(8,128)(2,1)S(1)}, u32[]{:S(2)}, u32[]{:S(2)}) %collective-permute-start.10) | collective-permute-done | bytes 16416 | tf_op jit(solution)/shard_map/ppermute | solution.py:310
  34.8 0.0 collective-permute-done.11.refs_6_
  34.8 0.7 %finish.5 = (bf16[64,1024]{1,0:T(8,128)(2,1)S(1)}, bf16[64,1536]{1,0:T(8,128)(2,1)S(1)}, f32[64,256]{1,0:T(8,128)S(1)}) custom-call(s32[1]{0:T(128)} %bitcast.index_ref.refs_0_, f32[64,1024]{1,0:T(8,128)S(1)} %halo.6.refs_1_, bf16[256,1024]{1,0:T(8,128)(2,1)S(1)} %get-tuple-element.43.refs_2_.refs_1_, bf16[128,1024]{1,0:T(8,128)(2,1)S(1)} %get-tuple-element.44.refs_3_, ...), custom_call_target="tpu_custom_call" | custom-call | flops 1000000000 | bytes 4194304 | tf_op jit(solution)/shard_map/finish/pallas_call | solution.py:239
  35.5 0.1 collective-permute-start.12
  35.5 3.0 %collective-permute-start.13 = (bf16[64,1024]{1,0:T(8,128)(2,1)S(1)}, bf16[64,1024]{1,0:T(8,128)(2,1)S(1)}, u32[]{:S(2)}, u32[]{:S(2)}) collective-permute-start(bf16[64,1024]{1,0:T(8,128)(2,1)S(1)} %get-tuple-element.59.refs_1_), channel_id=1, source_target_pairs={{0,15},{1,2},{2,1},{3,4},{4,3},{5,6},{6,5},{7,8},{8,7},{9,10},{10,... | collective-permute-start | bytes 393224 | tf_op jit(solution)/shard_map/ppermute | solution.py:298
  38.5 0.0 collective-permute-done.12.message_ref.refs_2_
  38.6 1.4 %collective-permute-start.14 = (bf16[64,128]{1,0:T(8,128)(2,1)S(1)}, bf16[64,128]{1,0:T(8,128)(2,1)S(1)}, u32[]{:S(2)}, u32[]{:S(2)}) collective-permute-start(bf16[64,128]{1,0:T(8,128)(2,1)S(1)} %get-tuple-element.62.refs_4_), channel_id=1, source_target_pairs={{0,10},{1,11},{2,8},{3,9},{4,14},{5,15},{6,12},{7,13},{8,2},{9,3},... | collective-permute-start | bytes 49160 | tf_op jit(solution)/shard_map/ppermute | solution.py:310
  40.0 0.3 collective-permute-start.15
  40.3 1.3 %own.5 = (f32[64,1024]{1,0:T(8,128)S(1)}, bf16[4,64,1024]{2,1,0:T(8,128)(2,1)}) custom-call(s32[1]{0:T(128)} %bitcast.index_ref.refs_0_, bf16[64,1024]{1,0:T(8,128)(2,1)S(1)} %get-tuple-element.59.refs_1_, bf16[64,1536]{1,0:T(8,128)(2,1)S(1)} %collective-permute-done.12.message_ref.refs_2_, ...), custom_call_target="tpu_custom_call", output_to_operand_aliasing={{1}: (6, {})} | custom-call | flops 1000000000 | bytes 4194304 | tf_op jit(solution)/shard_map/own/pallas_call | solution.py:239
  41.6 1.2 %collective-permute-done.13.over_ref = bf16[64,1024]{1,0:T(8,128)(2,1)S(1)} collective-permute-done((bf16[64,1024]{1,0:T(8,128)(2,1)S(1)}, bf16[64,1024]{1,0:T(8,128)(2,1)S(1)}, u32[]{:S(2)}, u32[]{:S(2)}) %collective-permute-start.13) | collective-permute-done | bytes 131104 | tf_op jit(solution)/shard_map/ppermute | solution.py:298
  42.8 0.5 %halo.7.refs_0_ = f32[64,1024]{1,0:T(8,128)S(1)} custom-call(s32[1]{0:T(128)} %bitcast.index_ref.refs_0_, f32[64,1024]{1,0:T(8,128)S(1)} %get-tuple-element.65.acc_ref, bf16[64,1024]{1,0:T(8,128)(2,1)S(1)} %collective-permute-done.13.over_ref, bf16[36,256,256]{2,1,0:T(8,128)(2,1)S(1)} %get-tuple-element.42.d_ref.refs_3_), custom_call_target="tpu_custom_call" | custom-call | flops 1000000000 | bytes 4194304 | tf_op jit(solution)/shard_map/halo/pallas_call | solution.py:239
  43.3 0.8 %collective-permute-done.14.refs_2_ = bf16[64,128]{1,0:T(8,128)(2,1)S(1)} collective-permute-done((bf16[64,128]{1,0:T(8,128)(2,1)S(1)}, bf16[64,128]{1,0:T(8,128)(2,1)S(1)}, u32[]{:S(2)}, u32[]{:S(2)}) %collective-permute-start.14) | collective-permute-done | bytes 16416 | tf_op jit(solution)/shard_map/ppermute | solution.py:310
  44.2 0.6 %collective-permute-done.15.refs_3_ = bf16[64,128]{1,0:T(8,128)(2,1)S(1)} collective-permute-done((bf16[64,128]{1,0:T(8,128)(2,1)S(1)}, bf16[64,128]{1,0:T(8,128)(2,1)S(1)}, u32[]{:S(2)}, u32[]{:S(2)}) %collective-permute-start.15) | collective-permute-done | bytes 16416 | tf_op jit(solution)/shard_map/ppermute | solution.py:310
  44.8 0.9 %last.1 = bf16[4,64,1024]{2,1,0:T(8,128)(2,1)} custom-call(f32[64,1024]{1,0:T(8,128)S(1)} %halo.7.refs_0_, bf16[256,1024]{1,0:T(8,128)(2,1)S(1)} %get-tuple-element.43.refs_2_.refs_1_, bf16[64,128]{1,0:T(8,128)(2,1)S(1)} %collective-permute-done.14.refs_2_, bf16[64,128]{1,0:T(8,128)(2,1)S(1)} %collective-permute-done.15.refs_3_, ...), custom_call_target="tpu_custom_call", output_to_operand_aliasing={{}: (4, {})} | custom-call | flops 1000000000 | bytes 4194304 | tf_op jit(solution)/shard_map/last/pallas_call | solution.py:239
  (4 shorter events, 0.1 us)
Async XLA Ops:
  1.8 6.2 %collective-permute-start = (bf16[64,1536]{1,0:T(8,128)(2,1)S(1)}, bf16[64,1536]{1,0:T(8,128)(2,1)S(1)}, u32[]{:S(2)}, u32[]{:S(2)}) collective-permute-start(bf16[64,1536]{1,0:T(8,128)(2,1)S(1)} %get-tuple-element.37), channel_id=1, source_target_pairs={{0,1},{1,0},{2,3},{3,2},{4,5},{5,4},{6,7},{7,6},{8,9},{9,8},{10,11... | collective-permute-start | bytes 589832 | tf_op jit(solution)/shard_map/ppermute | solution.py:297
  2.3 11.4 %collective-permute-start.1 = (bf16[64,1024]{1,0:T(8,128)(2,1)}, bf16[64,1024]{1,0:T(8,128)(2,1)S(1)}, u32[]{:S(2)}, u32[]{:S(2)}) collective-permute-start(bf16[64,1024]{1,0:T(8,128)(2,1)} %refs_2_.1), channel_id=1, source_target_pairs={{0,15},{1,2},{2,1},{3,4},{4,3},{5,6},{6,5},{7,8},{8,7},{9,10},{10,... | collective-permute-start | bytes 393224 | tf_op jit(solution)/shard_map/ppermute | solution.py:298
  8.0 6.2 %collective-permute-start.2 = (bf16[64,128]{1,0:T(8,128)(2,1)S(1)}, bf16[64,128]{1,0:T(8,128)(2,1)S(1)}, u32[]{:S(2)}, u32[]{:S(2)}) collective-permute-start(bf16[64,128]{1,0:T(8,128)(2,1)S(1)} %get-tuple-element.39.refs_7_), channel_id=1, source_target_pairs={{0,10},{1,11},{2,8},{3,9},{4,14},{5,15},{6,12},{7,13},{8,2},{9,3},... | collective-permute-start | bytes 49160 | tf_op jit(solution)/shard_map/ppermute | solution.py:310
  8.3 5.9 %collective-permute-start.3 = (bf16[64,128]{1,0:T(8,128)(2,1)S(1)}, bf16[64,128]{1,0:T(8,128)(2,1)S(1)}, u32[]{:S(2)}, u32[]{:S(2)}) collective-permute-start(bf16[64,128]{1,0:T(8,128)(2,1)S(1)} %get-tuple-element.40.refs_8_), channel_id=1, source_target_pairs={{0,8},{1,9},{2,10},{3,11},{4,12},{5,13},{6,14},{7,15},{8,0},{9,1},... | collective-permute-start | bytes 49160 | tf_op jit(solution)/shard_map/ppermute | solution.py:310
  14.9 3.7 %collective-permute-start.4 = (bf16[64,1536]{1,0:T(8,128)(2,1)S(1)}, bf16[64,1536]{1,0:T(8,128)(2,1)S(1)}, u32[]{:S(2)}, u32[]{:S(2)}) collective-permute-start(bf16[64,1536]{1,0:T(8,128)(2,1)S(1)} %get-tuple-element.47), channel_id=1, source_target_pairs={{0,1},{1,0},{2,3},{3,2},{4,5},{5,4},{6,7},{7,6},{8,9},{9,8},{10,11... | collective-permute-start | bytes 589832 | tf_op jit(solution)/shard_map/ppermute | solution.py:297
  15.0 8.9 %collective-permute-start.5 = (bf16[64,1024]{1,0:T(8,128)(2,1)S(1)}, bf16[64,1024]{1,0:T(8,128)(2,1)S(1)}, u32[]{:S(2)}, u32[]{:S(2)}) collective-permute-start(bf16[64,1024]{1,0:T(8,128)(2,1)S(1)} %get-tuple-element.46.refs_1_), channel_id=1, source_target_pairs={{0,15},{1,2},{2,1},{3,4},{4,3},{5,6},{6,5},{7,8},{8,7},{9,10},{10,... | collective-permute-start | bytes 393224 | tf_op jit(solution)/shard_map/ppermute | solution.py:298
  18.7 5.8 %collective-permute-start.6 = (bf16[64,128]{1,0:T(8,128)(2,1)S(1)}, bf16[64,128]{1,0:T(8,128)(2,1)S(1)}, u32[]{:S(2)}, u32[]{:S(2)}) collective-permute-start(bf16[64,128]{1,0:T(8,128)(2,1)S(1)} %get-tuple-element.49.refs_4_), channel_id=1, source_target_pairs={{0,10},{1,11},{2,8},{3,9},{4,14},{5,15},{6,12},{7,13},{8,2},{9,3},... | collective-permute-start | bytes 49160 | tf_op jit(solution)/shard_map/ppermute | solution.py:310
  19.7 4.8 %collective-permute-start.7 = (bf16[64,128]{1,0:T(8,128)(2,1)S(1)}, bf16[64,128]{1,0:T(8,128)(2,1)S(1)}, u32[]{:S(2)}, u32[]{:S(2)}) collective-permute-start(bf16[64,128]{1,0:T(8,128)(2,1)S(1)} %get-tuple-element.50.refs_5_), channel_id=1, source_target_pairs={{0,8},{1,9},{2,10},{3,11},{4,12},{5,13},{6,14},{7,15},{8,0},{9,1},... | collective-permute-start | bytes 49160 | tf_op jit(solution)/shard_map/ppermute | solution.py:310
  25.2 4.0 %collective-permute-start.8 = (bf16[64,1536]{1,0:T(8,128)(2,1)S(1)}, bf16[64,1536]{1,0:T(8,128)(2,1)S(1)}, u32[]{:S(2)}, u32[]{:S(2)}) collective-permute-start(bf16[64,1536]{1,0:T(8,128)(2,1)S(1)} %get-tuple-element.53), channel_id=1, source_target_pairs={{0,1},{1,0},{2,3},{3,2},{4,5},{5,4},{6,7},{7,6},{8,9},{9,8},{10,11... | collective-permute-start | bytes 589832 | tf_op jit(solution)/shard_map/ppermute | solution.py:297
  25.2 7.3 %collective-permute-start.9 = (bf16[64,1024]{1,0:T(8,128)(2,1)S(1)}, bf16[64,1024]{1,0:T(8,128)(2,1)S(1)}, u32[]{:S(2)}, u32[]{:S(2)}) collective-permute-start(bf16[64,1024]{1,0:T(8,128)(2,1)S(1)} %get-tuple-element.52.refs_1_), channel_id=1, source_target_pairs={{0,15},{1,2},{2,1},{3,4},{4,3},{5,6},{6,5},{7,8},{8,7},{9,10},{10,... | collective-permute-start | bytes 393224 | tf_op jit(solution)/shard_map/ppermute | solution.py:298
  29.2 5.6 %collective-permute-start.10 = (bf16[64,128]{1,0:T(8,128)(2,1)S(1)}, bf16[64,128]{1,0:T(8,128)(2,1)S(1)}, u32[]{:S(2)}, u32[]{:S(2)}) collective-permute-start(bf16[64,128]{1,0:T(8,128)(2,1)S(1)} %get-tuple-element.55.refs_4_), channel_id=1, source_target_pairs={{0,10},{1,11},{2,8},{3,9},{4,14},{5,15},{6,12},{7,13},{8,2},{9,3},... | collective-permute-start | bytes 49160 | tf_op jit(solution)/shard_map/ppermute | solution.py:310
  29.7 5.1 %collective-permute-start.11 = (bf16[64,128]{1,0:T(8,128)(2,1)S(1)}, bf16[64,128]{1,0:T(8,128)(2,1)S(1)}, u32[]{:S(2)}, u32[]{:S(2)}) collective-permute-start(bf16[64,128]{1,0:T(8,128)(2,1)S(1)} %get-tuple-element.56.refs_5_), channel_id=1, source_target_pairs={{0,8},{1,9},{2,10},{3,11},{4,12},{5,13},{6,14},{7,15},{8,0},{9,1},... | collective-permute-start | bytes 49160 | tf_op jit(solution)/shard_map/ppermute | solution.py:310
  35.5 3.1 %collective-permute-start.12 = (bf16[64,1536]{1,0:T(8,128)(2,1)S(1)}, bf16[64,1536]{1,0:T(8,128)(2,1)S(1)}, u32[]{:S(2)}, u32[]{:S(2)}) collective-permute-start(bf16[64,1536]{1,0:T(8,128)(2,1)S(1)} %get-tuple-element.60), channel_id=1, source_target_pairs={{0,1},{1,0},{2,3},{3,2},{4,5},{5,4},{6,7},{7,6},{8,9},{9,8},{10,11... | collective-permute-start | bytes 589832 | tf_op jit(solution)/shard_map/ppermute | solution.py:297
  35.5 7.3 %collective-permute-start.13 = (bf16[64,1024]{1,0:T(8,128)(2,1)S(1)}, bf16[64,1024]{1,0:T(8,128)(2,1)S(1)}, u32[]{:S(2)}, u32[]{:S(2)}) collective-permute-start(bf16[64,1024]{1,0:T(8,128)(2,1)S(1)} %get-tuple-element.59.refs_1_), channel_id=1, source_target_pairs={{0,15},{1,2},{2,1},{3,4},{4,3},{5,6},{6,5},{7,8},{8,7},{9,10},{10,... | collective-permute-start | bytes 393224 | tf_op jit(solution)/shard_map/ppermute | solution.py:298
  38.6 5.6 %collective-permute-start.14 = (bf16[64,128]{1,0:T(8,128)(2,1)S(1)}, bf16[64,128]{1,0:T(8,128)(2,1)S(1)}, u32[]{:S(2)}, u32[]{:S(2)}) collective-permute-start(bf16[64,128]{1,0:T(8,128)(2,1)S(1)} %get-tuple-element.62.refs_4_), channel_id=1, source_target_pairs={{0,10},{1,11},{2,8},{3,9},{4,14},{5,15},{6,12},{7,13},{8,2},{9,3},... | collective-permute-start | bytes 49160 | tf_op jit(solution)/shard_map/ppermute | solution.py:310
  40.0 4.8 %collective-permute-start.15 = (bf16[64,128]{1,0:T(8,128)(2,1)S(1)}, bf16[64,128]{1,0:T(8,128)(2,1)S(1)}, u32[]{:S(2)}, u32[]{:S(2)}) collective-permute-start(bf16[64,128]{1,0:T(8,128)(2,1)S(1)} %get-tuple-element.63.refs_5_), channel_id=1, source_target_pairs={{0,8},{1,9},{2,10},{3,11},{4,12},{5,13},{6,14},{7,15},{8,0},{9,1},... | collective-permute-start | bytes 49160 | tf_op jit(solution)/shard_map/ppermute | solution.py:310

commit v8 on v6

--- a/solution.py
+++ b/solution.py
@@ -121,16 +121,23 @@
         def _():
             self.near_sums(x_ref, d_ref, acc_ref, self.per_device, start_ref)
 
+    def far_halves(self, far_refs):
+        return jnp.concatenate(halves(self.far_sum(far_refs)), axis=1)
+
+    def next_panel(self, acc_ref, rb_ref, both, c):
+        return (self.panel(acc_ref, c) + dot_nn(both, self.panel(rb_ref, c))).astype(BF16)
+
     def next_block(self, acc_ref, rb_ref, far_refs):
-        both = jnp.concatenate(halves(self.far_sum(far_refs)), axis=1)
-        return (acc_ref[...] + dot_nn(both, rb_ref[...])).astype(BF16)
+        both = self.far_halves(far_refs)
+        panels = [self.next_panel(acc_ref, rb_ref, both, c) for c in range(self.per_device)]
+        return jnp.concatenate(panels, axis=1)
 
 
 def prepare_kernel(plan, index_ref, *refs):
-    sources, refs = refs[:5], refs[5:]
-    x_ref, g_ref, cb_ref = refs[:3]
-    sends, (rows_ref, cols_ref, col_ref, coup_ref, sems) = refs[3:-5], refs[-5:]
-    targets = (rows_ref, cols_ref, x_ref, col_ref, coup_ref)
+    sources, refs = refs[:7], refs[7:]
+    x_ref, g_ref, cb_ref, order_ref = refs[:4]
+    sends, (near_ref, offsets_ref, rows_ref, cols_ref, col_ref, coup_ref, sems) = refs[4:-7], refs[-7:]
+    targets = (near_ref, offsets_ref, rows_ref, cols_ref, x_ref, col_ref, coup_ref)
     copies = [
         pltpu.make_async_copy(source, target, sems.at[i])
         for i, (source, target) in enumerate(zip(sources, targets))
@@ -142,6 +149,15 @@
     g_ref[...] = jnp.zeros_like(g_ref)
     for copy in copies:
         copy.wait()
+    first, last = jnp.int32(0), jnp.int32(plan.tiles - 1)
+    for s in range(plan.tiles):
+        place = near_ref[s] + offsets_ref[s]
+        own = jnp.logical_and(place >= 0, place < plan.per_device).astype(jnp.int32)
+        where = jnp.where(own == 1, first, last)
+        order_ref[where] = s
+        order_ref[plan.tiles + where] = near_ref[s] * SPAN + offsets_ref[s] + REACH
+        first, last = first + own, last - (1 - own)
+    order_ref[2 * plan.tiles] = first
     for c in range(plan.per_device):
         cb_ref[c * rank : (c + 1) * rank, c * size : (c + 1) * size] = col_ref[c]
     column = lax.broadcasted_iota(jnp.int32, (rank, plan.width), 1) // rank
@@ -163,38 +179,46 @@
 
 
 def first_own_kernel(plan, *refs):
-    index_ref, x_ref, near_ref, rows_hbm, offsets_hbm, row_hbm, tiles_hbm = refs[:7]
-    acc_ref, d_ref, rb_ref, rows_ref, offsets_ref, row_ref, present, sems, tile_sems = refs[-9:]
-    pairs = ((rows_hbm, rows_ref), (offsets_hbm, offsets_ref), (row_hbm, row_ref))
-    copies = [pltpu.make_async_copy(*pair, sems.at[i]) for i, pair in enumerate(pairs)]
-    for copy in copies:
-        copy.start()
+    index_ref, order_ref, x_ref, near_ref, row_hbm, tiles_hbm = refs[:6]
+    acc_ref, d_ref, rb_ref, row_ref, empty, sem, tile_sems = refs[-7:]
+    rank, size = plan.rank, plan.size
+
+    def tile_copy(place):
+        source, cell = order_ref[place], order_ref[plan.tiles + place]
+        return pltpu.make_async_copy(tiles_hbm.at[source], d_ref.at[cell], tile_sems.at[place])
+
+    def wait_for(first, last):
+        @pl.loop(first, last)
+        def _(place):
+            tile_copy(place).wait()
+
+    for place in range(plan.tiles):
+        tile_copy(place).start()
+    copy = pltpu.make_async_copy(row_hbm, row_ref, sem)
+    copy.start()
+    for cell in range(plan.cells):
+        empty[cell] = 1
+    for place in range(plan.tiles):
+        empty[order_ref[plan.tiles + place]] = 0
+    count = jnp.int32(0)
+    for cell in range(plan.cells):
+        missing = empty[cell]
+        empty[plan.cells + count] = cell
+        count = count + missing
+
+    @pl.loop(0, count)
+    def _(place):
+        d_ref[empty[plan.cells + place]] = jnp.zeros(d_ref.shape[1:], d_ref.dtype)
+
     rb_ref[...] = jnp.zeros_like(rb_ref)
-    for cell in range(plan.cells):
-        present[cell] = 0
-    copies[0].wait()
-    copies[1].wait()
-    tiles = []
-    for s in range(plan.tiles):
-        cell = rows_ref[s] * SPAN + offsets_ref[s] + REACH
-        present[cell] = 1
-        tiles.append(pltpu.make_async_copy(tiles_hbm.at[s], d_ref.at[cell], tile_sems.at[s]))
-        tiles[-1].start()
-    copies[2].wait()
-    rank, size = plan.rank, plan.size
+    copy.wait()
     for c in range(plan.per_device):
         for start in (c * rank, plan.width + c * rank):
             rb_ref[start : start + rank, c * size : (c + 1) * size] = row_ref[c]
-    for copy in tiles:
-        copy.wait()
-
-    @pl.loop(0, plan.cells)
-    def _(cell):
-        @pl.when(present[cell] == 0)
-        def _():
-            d_ref[cell] = jnp.zeros(d_ref.shape[1:], d_ref.dtype)
-
+    own = order_ref[2 * plan.tiles]
+    wait_for(0, own)
     plan.near_sums(x_ref, d_ref, acc_ref, 0)
+    wait_for(own, plan.tiles)
     plan.halo_sums(lax.rem(index_ref[0], 2) == 1, near_ref, d_ref, acc_ref, acc_ref)
 
 
@@ -223,10 +247,17 @@
 def last_kernel(plan, fars, slot, *refs):
     acc_ref, rb_ref = refs[:2]
     far_refs, (_, krylov_ref, x_ref, sem) = refs[2 : 2 + fars], refs[2 + fars :]
-    x_ref[...] = plan.next_block(acc_ref, rb_ref, far_refs)
-    copy = pltpu.make_async_copy(x_ref, krylov_ref.at[slot], sem)
-    copy.start()
-    copy.wait()
+    both = plan.far_halves(far_refs)
+    copies = []
+    for c in range(plan.per_device):
+        columns = pl.ds(c * plan.size, plan.size)
+        x_ref[:, columns] = plan.next_panel(acc_ref, rb_ref, both, c)
+        copies.append(
+            pltpu.make_async_copy(x_ref.at[:, columns], krylov_ref.at[slot, :, columns], sem.at[c])
+        )
+        copies[-1].start()
+    for copy in copies:
+        copy.wait()
 
 
 def call(kernel, name, ins, specs, outs, out_specs=None, scratch=(), aliases=None):
@@ -278,20 +309,22 @@
     current, sends, krylov = block, None, None
     for product in range(PRODUCTS):
         if product == 0:
-            ins = [far_rows, far_cols, block, col_basis, couplings]
-            current, coupled, col_wide, *sends = call(
+            ins = [near_rows, near_offsets, far_rows, far_cols, block, col_basis, couplings]
+            current, coupled, col_wide, order, *sends = call(
                 functools.partial(prepare_kernel, plan),
                 "prepare",
                 [index, *ins],
-                [IN_SMEM] + [IN_HBM] * 5,
+                [IN_SMEM] + [IN_HBM] * 7,
                 [
                     block_out,
                     pltpu.VMEM((LEVELS, plan.members * width, width), BF16),
                     pltpu.VMEM((width, shard_len), BF16),
+                    pltpu.SMEM((2 * plan.tiles + 1,), jnp.int32),
                     *sends_out,
                 ],
-                scratch=scratch_for(far_rows, far_cols, col_basis, couplings)
-                + [pltpu.SemaphoreType.DMA((5,))],
+                [IN_VMEM] * 3 + [IN_SMEM] + [IN_VMEM] * len(sends_out),
+                scratch=scratch_for(near_rows, near_offsets, far_rows, far_cols, col_basis, couplings)
+                + [pltpu.SemaphoreType.DMA((7,))],
             )
         near = lax.ppermute(sends[0] if plan.paired else current, axes, plan.near)
         over = lax.ppermute(block if product == 0 else current, axes, plan.over)
@@ -312,17 +345,17 @@
             acc, dense, row_wide = call(
                 functools.partial(first_own_kernel, plan),
                 "first_own",
-                [index, current, near, near_rows, near_offsets, row_basis, near_tiles, *after],
-                [IN_SMEM] + [IN_VMEM] * 2 + [IN_HBM] * 4 + [ANYWHERE] * len(after),
+                [index, order, current, near, row_basis, near_tiles, *after],
+                [IN_SMEM] * 2 + [IN_VMEM] * 2 + [IN_HBM] * 2 + [ANYWHERE] * len(after),
                 [
                     acc_out,
                     pltpu.VMEM((plan.cells, plan.size, plan.size), BF16),
                     pltpu.VMEM((2 * width, shard_len), BF16),
                 ],
-                scratch=scratch_for(near_rows, near_offsets, row_basis)
+                scratch=scratch_for(row_basis)
                 + [
-                    pltpu.SMEM((plan.cells,), jnp.int32),
-                    pltpu.SemaphoreType.DMA((3,)),
+                    pltpu.SMEM((2 * plan.cells + 1,), jnp.int32),
+                    pltpu.SemaphoreType.DMA,
                     pltpu.SemaphoreType.DMA((plan.tiles,)),
                 ],
             )
@@ -363,7 +396,10 @@
                 [IN_VMEM] * (len(ins) - 1) + [ANYWHERE],
                 [krylov_out],
                 [ANYWHERE],
-                [pltpu.VMEM((rhs, shard_len), BF16), pltpu.SemaphoreType.DMA],
+                [
+                    pltpu.VMEM((rhs, shard_len), BF16),
+                    pltpu.SemaphoreType.DMA((plan.per_device,)),
+                ],
                 {len(ins) - 1: 0},
             )
     return krylov

time: 44.4 us -> 43.7 us (0.984)
  starting transfers between devices: 24.4 us -> 23.4 us
  waiting for transfers between devices: 4.27 us -> 5.1 us
  Pallas kernels: 15.4 us -> 14.8 us
    ppermute x4, starting transfers between devices: 2.19 us -> 1.4 us  [on_device(): near = lax.ppermute(sends[0] if plan.paired else current, axes, plan.near)]
    ppermute x8, waiting for transfers between devices: 1.45 us -> 2.24 us  [on_device(): fars = [lax.ppermute(s, axes, route) for s, route in zip(sends, routes)]]
    pallas_call x17, Pallas kernels: 15.4 us -> 14.8 us  [call(): pl.pallas_call(kernel, in_specs=list(specs), out_specs=out_specs or [IN_V...]
  transfers between devices with their start and end apart: 16 -> 16, of which waited for: 4 -> 6; matrix products, arithmetic and copies ran while one was open for 0% -> 0% of each run, Pallas kernels for 24% -> 23%
where the time goes in v8:
time: 43.7 us; the launch traced here: 43.5 us
  starting transfers between devices  23.4 us (54%)
  Pallas kernels  14.8 us (34%)
  waiting for transfers between devices  5.1 us (12%)
    pallas_call x17, Pallas kernels, call(): pl.pallas_call(kernel, in_specs=list(specs), out_specs=out_specs or [IN_V...  14.8 us
    ppermute x4, starting transfers between devices, on_device(): over = lax.ppermute(block if product == 0 else current, axes, plan.over)  14.3 us
    ppermute x8, starting transfers between devices, on_device(): fars = [lax.ppermute(s, axes, route) for s, route in zip(sends, routes)]  7.74 us
    ppermute x4, waiting for transfers between devices, on_device(): over = lax.ppermute(block if product == 0 else current, axes, plan.over)  2.85 us
    ppermute x8, waiting for transfers between devices, on_device(): fars = [lax.ppermute(s, axes, route) for s, route in zip(sends, routes)]  2.24 us
    ppermute x4, starting transfers between devices, on_device(): near = lax.ppermute(sends[0] if plan.paired else current, axes, plan.near)  1.4 us
  transfers between devices with their start and end apart: 16, of which 6 were waited for; matrix products, arithmetic and copies ran while one was open for 0% of the time, Pallas kernels for 23%

profile of v8, /device:TPU:0, one launch (start us, length us, event | category | flops | bytes accessed | tf_op | source)
XLA Modules:
  0.0 43.5 jit_solution(14787025432966741193)
XLA Ops:
  0.0 1.9 %prepare.1 = (bf16[64,1024]{1,0:T(8,128)(2,1)S(1)}, bf16[3,512,128]{2,1,0:T(8,128)(2,1)S(1)}, bf16[128,1024]{1,0:T(8,128)(2,1)S(1)}, s32[65]{0:T(128)S(4)}, bf16...) custom-call(s32[1]{0:T(128)} %bitcast.index_ref.refs_0_, s32[32]{0:T(128)} %refs_0_.1, s32[32]{0:T(128)} %refs_1_.1, ...), custom_call_target="tpu_custom_call" | custom-call | flops 1000000000 | bytes 4194304 | tf_op jit(solution)/shard_map/prepare/pallas_call | solution.py:269
  1.9 0.5 %collective-permute-start = (bf16[64,1536]{1,0:T(8,128)(2,1)S(1)}, bf16[64,1536]{1,0:T(8,128)(2,1)S(1)}, u32[]{:S(2)}, u32[]{:S(2)}) collective-permute-start(bf16[64,1536]{1,0:T(8,128)(2,1)S(1)} %get-tuple-element.39), channel_id=1, source_target_pairs={{0,1},{1,0},{2,3},{3,2},{4,5},{5,4},{6,7},{7,6},{8,9},{9,8},{10,11... | collective-permute-start | bytes 589832 | tf_op jit(solution)/shard_map/ppermute | solution.py:329
  2.5 5.6 %collective-permute-start.1 = (bf16[64,1024]{1,0:T(8,128)(2,1)}, bf16[64,1024]{1,0:T(8,128)(2,1)S(1)}, u32[]{:S(2)}, u32[]{:S(2)}) collective-permute-start(bf16[64,1024]{1,0:T(8,128)(2,1)} %refs_4_.2), channel_id=1, source_target_pairs={{0,15},{1,2},{2,1},{3,4},{4,3},{5,6},{6,5},{7,8},{8,7},{9,10},{10,... | collective-permute-start | bytes 393224 | tf_op jit(solution)/shard_map/ppermute | solution.py:330
  8.1 0.0 collective-permute-done.message_ref.refs_3_
  8.1 0.1 collective-permute-start.2
  8.2 0.3 collective-permute-start.3
  8.5 4.0 %first_own.1 = (f32[64,1024]{1,0:T(8,128)S(1)}, bf16[36,256,256]{2,1,0:T(8,128)(2,1)S(1)}, bf16[256,1024]{1,0:T(8,128)(2,1)S(1)}) custom-call(s32[1]{0:T(128)} %bitcast.index_ref.refs_0_, s32[65]{0:T(128)S(4)} %get-tuple-element.37.refs_1_, bf16[64,1024]{1,0:T(8,128)(2,1)S(1)} %get-tuple-element.38.refs_2_, ...), custom_call_target="tpu_custom_call" | custom-call | flops 1000000000 | bytes 4194304 | tf_op jit(solution)/shard_map/first_own/pallas_call | solution.py:269
  12.4 0.0 collective-permute-done.1.over_ref
  12.5 0.5 %halo.4.refs_1_ = f32[64,1024]{1,0:T(8,128)S(1)} custom-call(s32[1]{0:T(128)} %bitcast.index_ref.refs_0_, f32[64,1024]{1,0:T(8,128)S(1)} %get-tuple-element.43.acc_ref, bf16[64,1024]{1,0:T(8,128)(2,1)S(1)} %collective-permute-done.1.over_ref, bf16[36,256,256]{2,1,0:T(8,128)(2,1)S(1)} %get-tuple-element.44.d_ref.refs_3_), custom_call_target="tpu_custom_call" | custom-call | flops 1000000000 | bytes 4194304 | tf_op jit(solution)/shard_map/halo/pallas_call | solution.py:269
  13.0 0.0 collective-permute-done.2.refs_5_
  13.0 0.2 collective-permute-done.3.refs_6_
  13.2 0.7 %finish.3 = (bf16[64,1024]{1,0:T(8,128)(2,1)S(1)}, bf16[64,1536]{1,0:T(8,128)(2,1)S(1)}, f32[64,256]{1,0:T(8,128)S(1)}) custom-call(s32[1]{0:T(128)} %bitcast.index_ref.refs_0_, f32[64,1024]{1,0:T(8,128)S(1)} %halo.4.refs_1_, bf16[256,1024]{1,0:T(8,128)(2,1)S(1)} %get-tuple-element.45.refs_2_.refs_1_, bf16[128,1024]{1,0:T(8,128)(2,1)S(1)} %get-tuple-element.46.refs_3_, ...), custom_call_target="tpu_custom_call" | custom-call | flops 1000000000 | bytes 4194304 | tf_op jit(solution)/shard_map/finish/pallas_call | solution.py:269
  13.9 0.3 collective-permute-start.4
  14.2 3.4 %collective-permute-start.5 = (bf16[64,1024]{1,0:T(8,128)(2,1)S(1)}, bf16[64,1024]{1,0:T(8,128)(2,1)S(1)}, u32[]{:S(2)}, u32[]{:S(2)}) collective-permute-start(bf16[64,1024]{1,0:T(8,128)(2,1)S(1)} %get-tuple-element.48.refs_1_), channel_id=1, source_target_pairs={{0,15},{1,2},{2,1},{3,4},{4,3},{5,6},{6,5},{7,8},{8,7},{9,10},{10,... | collective-permute-start | bytes 393224 | tf_op jit(solution)/shard_map/ppermute | solution.py:330
  17.7 0.0 collective-permute-done.4.message_ref.refs_2_
  17.7 0.7 %collective-permute-start.6 = (bf16[64,128]{1,0:T(8,128)(2,1)S(1)}, bf16[64,128]{1,0:T(8,128)(2,1)S(1)}, u32[]{:S(2)}, u32[]{:S(2)}) collective-permute-start(bf16[64,128]{1,0:T(8,128)(2,1)S(1)} %get-tuple-element.51.refs_4_), channel_id=1, source_target_pairs={{0,8},{1,11},{2,10},{3,9},{4,12},{5,15},{6,14},{7,13},{8,0},{9,3},... | collective-permute-start | bytes 49160 | tf_op jit(solution)/shard_map/ppermute | solution.py:342
  18.4 2.8 %collective-permute-start.7 = (bf16[64,128]{1,0:T(8,128)(2,1)S(1)}, bf16[64,128]{1,0:T(8,128)(2,1)S(1)}, u32[]{:S(2)}, u32[]{:S(2)}) collective-permute-start(bf16[64,128]{1,0:T(8,128)(2,1)S(1)} %get-tuple-element.52.refs_5_), channel_id=1, source_target_pairs={{0,9},{1,10},{2,11},{3,8},{4,13},{5,14},{6,15},{7,12},{8,1},{9,2},... | collective-permute-start | bytes 49160 | tf_op jit(solution)/shard_map/ppermute | solution.py:342
  21.2 1.3 %own.3 = (f32[64,1024]{1,0:T(8,128)S(1)}, bf16[4,64,1024]{2,1,0:T(8,128)(2,1)}) custom-call(s32[1]{0:T(128)} %bitcast.index_ref.refs_0_, bf16[64,1024]{1,0:T(8,128)(2,1)S(1)} %get-tuple-element.48.refs_1_, bf16[64,1536]{1,0:T(8,128)(2,1)S(1)} %collective-permute-done.4.message_ref.refs_2_, bf16[36,256,256]{2,1,0:T(8,128)(2,1)S(1)} %get-tuple-element.44.d_ref.refs_3_, ...), custom_call_target="tpu_custom_call" | custom-call | flops 1000000000 | bytes 4194304 | tf_op jit(solution)/shard_map/own/pallas_call | solution.py:269
  22.5 0.0 collective-permute-done.5.over_ref
  22.5 0.5 %halo.5.refs_1_ = f32[64,1024]{1,0:T(8,128)S(1)} custom-call(s32[1]{0:T(128)} %bitcast.index_ref.refs_0_, f32[64,1024]{1,0:T(8,128)S(1)} %get-tuple-element.53.acc_ref, bf16[64,1024]{1,0:T(8,128)(2,1)S(1)} %collective-permute-done.5.over_ref, bf16[36,256,256]{2,1,0:T(8,128)(2,1)S(1)} %get-tuple-element.44.d_ref.refs_3_), custom_call_target="tpu_custom_call" | custom-call | flops 1000000000 | bytes 4194304 | tf_op jit(solution)/shard_map/halo/pallas_call | solution.py:269
  23.0 0.0 collective-permute-done.6.refs_5_
  23.0 0.5 %collective-permute-done.7.refs_6_ = bf16[64,128]{1,0:T(8,128)(2,1)S(1)} collective-permute-done((bf16[64,128]{1,0:T(8,128)(2,1)S(1)}, bf16[64,128]{1,0:T(8,128)(2,1)S(1)}, u32[]{:S(2)}, u32[]{:S(2)}) %collective-permute-start.7) | collective-permute-done | bytes 16416 | tf_op jit(solution)/shard_map/ppermute | solution.py:342
  23.5 0.7 %finish.4 = (bf16[64,1024]{1,0:T(8,128)(2,1)S(1)}, bf16[64,1536]{1,0:T(8,128)(2,1)S(1)}, f32[64,256]{1,0:T(8,128)S(1)}) custom-call(s32[1]{0:T(128)} %bitcast.index_ref.refs_0_, f32[64,1024]{1,0:T(8,128)S(1)} %halo.5.refs_1_, bf16[256,1024]{1,0:T(8,128)(2,1)S(1)} %get-tuple-element.45.refs_2_.refs_1_, bf16[128,1024]{1,0:T(8,128)(2,1)S(1)} %get-tuple-element.46.refs_3_, ...), custom_call_target="tpu_custom_call" | custom-call | flops 1000000000 | bytes 4194304 | tf_op jit(solution)/shard_map/finish/pallas_call | solution.py:269
  24.2 0.2 collective-permute-start.8
  24.4 2.6 %collective-permute-start.9 = (bf16[64,1024]{1,0:T(8,128)(2,1)S(1)}, bf16[64,1024]{1,0:T(8,128)(2,1)S(1)}, u32[]{:S(2)}, u32[]{:S(2)}) collective-permute-start(bf16[64,1024]{1,0:T(8,128)(2,1)S(1)} %get-tuple-element.54.refs_1_), channel_id=1, source_target_pairs={{0,15},{1,2},{2,1},{3,4},{4,3},{5,6},{6,5},{7,8},{8,7},{9,10},{10,... | collective-permute-start | bytes 393224 | tf_op jit(solution)/shard_map/ppermute | solution.py:330
  27.0 0.0 collective-permute-done.8.message_ref.refs_2_
  27.0 1.1 %collective-permute-start.10 = (bf16[64,128]{1,0:T(8,128)(2,1)S(1)}, bf16[64,128]{1,0:T(8,128)(2,1)S(1)}, u32[]{:S(2)}, u32[]{:S(2)}) collective-permute-start(bf16[64,128]{1,0:T(8,128)(2,1)S(1)} %get-tuple-element.57.refs_4_), channel_id=1, source_target_pairs={{0,8},{1,11},{2,10},{3,9},{4,12},{5,15},{6,14},{7,13},{8,0},{9,3},... | collective-permute-start | bytes 49160 | tf_op jit(solution)/shard_map/ppermute | solution.py:342
  28.0 0.7 %collective-permute-start.11 = (bf16[64,128]{1,0:T(8,128)(2,1)S(1)}, bf16[64,128]{1,0:T(8,128)(2,1)S(1)}, u32[]{:S(2)}, u32[]{:S(2)}) collective-permute-start(bf16[64,128]{1,0:T(8,128)(2,1)S(1)} %get-tuple-element.58.refs_5_), channel_id=1, source_target_pairs={{0,9},{1,10},{2,11},{3,8},{4,13},{5,14},{6,15},{7,12},{8,1},{9,2},... | collective-permute-start | bytes 49160 | tf_op jit(solution)/shard_map/ppermute | solution.py:342
  28.7 1.3 %own.4 = (f32[64,1024]{1,0:T(8,128)S(1)}, bf16[4,64,1024]{2,1,0:T(8,128)(2,1)}) custom-call(s32[1]{0:T(128)} %bitcast.index_ref.refs_0_, bf16[64,1024]{1,0:T(8,128)(2,1)S(1)} %get-tuple-element.54.refs_1_, bf16[64,1536]{1,0:T(8,128)(2,1)S(1)} %collective-permute-done.8.message_ref.refs_2_, ...), custom_call_target="tpu_custom_call", output_to_operand_aliasing={{1}: (6, {})} | custom-call | flops 1000000000 | bytes 4194304 | tf_op jit(solution)/shard_map/own/pallas_call | solution.py:269
  30.0 1.7 %collective-permute-done.9.over_ref = bf16[64,1024]{1,0:T(8,128)(2,1)S(1)} collective-permute-done((bf16[64,1024]{1,0:T(8,128)(2,1)S(1)}, bf16[64,1024]{1,0:T(8,128)(2,1)S(1)}, u32[]{:S(2)}, u32[]{:S(2)}) %collective-permute-start.9) | collective-permute-done | bytes 131104 | tf_op jit(solution)/shard_map/ppermute | solution.py:330
  31.7 0.5 %halo.6.refs_1_ = f32[64,1024]{1,0:T(8,128)S(1)} custom-call(s32[1]{0:T(128)} %bitcast.index_ref.refs_0_, f32[64,1024]{1,0:T(8,128)S(1)} %get-tuple-element.60.acc_ref, bf16[64,1024]{1,0:T(8,128)(2,1)S(1)} %collective-permute-done.9.over_ref, bf16[36,256,256]{2,1,0:T(8,128)(2,1)S(1)} %get-tuple-element.44.d_ref.refs_3_), custom_call_target="tpu_custom_call" | custom-call | flops 1000000000 | bytes 4194304 | tf_op jit(solution)/shard_map/halo/pallas_call | solution.py:269
  32.2 0.0 collective-permute-done.10.refs_5_
  32.3 0.9 %collective-permute-done.11.refs_6_ = bf16[64,128]{1,0:T(8,128)(2,1)S(1)} collective-permute-done((bf16[64,128]{1,0:T(8,128)(2,1)S(1)}, bf16[64,128]{1,0:T(8,128)(2,1)S(1)}, u32[]{:S(2)}, u32[]{:S(2)}) %collective-permute-start.11) | collective-permute-done | bytes 16416 | tf_op jit(solution)/shard_map/ppermute | solution.py:342
  33.1 0.7 %finish.5 = (bf16[64,1024]{1,0:T(8,128)(2,1)S(1)}, bf16[64,1536]{1,0:T(8,128)(2,1)S(1)}, f32[64,256]{1,0:T(8,128)S(1)}) custom-call(s32[1]{0:T(128)} %bitcast.index_ref.refs_0_, f32[64,1024]{1,0:T(8,128)S(1)} %halo.6.refs_1_, bf16[256,1024]{1,0:T(8,128)(2,1)S(1)} %get-tuple-element.45.refs_2_.refs_1_, bf16[128,1024]{1,0:T(8,128)(2,1)S(1)} %get-tuple-element.46.refs_3_, ...), custom_call_target="tpu_custom_call" | custom-call | flops 1000000000 | bytes 4194304 | tf_op jit(solution)/shard_map/finish/pallas_call | solution.py:269
  33.8 0.4 collective-permute-start.12
  34.2 2.6 %collective-permute-start.13 = (bf16[64,1024]{1,0:T(8,128)(2,1)S(1)}, bf16[64,1024]{1,0:T(8,128)(2,1)S(1)}, u32[]{:S(2)}, u32[]{:S(2)}) collective-permute-start(bf16[64,1024]{1,0:T(8,128)(2,1)S(1)} %get-tuple-element.61.refs_1_), channel_id=1, source_target_pairs={{0,15},{1,2},{2,1},{3,4},{4,3},{5,6},{6,5},{7,8},{8,7},{9,10},{10,... | collective-permute-start | bytes 393224 | tf_op jit(solution)/shard_map/ppermute | solution.py:330
  36.8 0.0 collective-permute-done.12.message_ref.refs_2_
  36.8 0.5 %collective-permute-start.14 = (bf16[64,128]{1,0:T(8,128)(2,1)S(1)}, bf16[64,128]{1,0:T(8,128)(2,1)S(1)}, u32[]{:S(2)}, u32[]{:S(2)}) collective-permute-start(bf16[64,128]{1,0:T(8,128)(2,1)S(1)} %get-tuple-element.64.refs_4_), channel_id=1, source_target_pairs={{0,8},{1,11},{2,10},{3,9},{4,12},{5,15},{6,14},{7,13},{8,0},{9,3},... | collective-permute-start | bytes 49160 | tf_op jit(solution)/shard_map/ppermute | solution.py:342
  37.3 1.7 %collective-permute-start.15 = (bf16[64,128]{1,0:T(8,128)(2,1)S(1)}, bf16[64,128]{1,0:T(8,128)(2,1)S(1)}, u32[]{:S(2)}, u32[]{:S(2)}) collective-permute-start(bf16[64,128]{1,0:T(8,128)(2,1)S(1)} %get-tuple-element.65.refs_5_), channel_id=1, source_target_pairs={{0,9},{1,10},{2,11},{3,8},{4,13},{5,14},{6,15},{7,12},{8,1},{9,2},... | collective-permute-start | bytes 49160 | tf_op jit(solution)/shard_map/ppermute | solution.py:342
  39.0 1.3 %own.5 = (f32[64,1024]{1,0:T(8,128)S(1)}, bf16[4,64,1024]{2,1,0:T(8,128)(2,1)}) custom-call(s32[1]{0:T(128)} %bitcast.index_ref.refs_0_, bf16[64,1024]{1,0:T(8,128)(2,1)S(1)} %get-tuple-element.61.refs_1_, bf16[64,1536]{1,0:T(8,128)(2,1)S(1)} %collective-permute-done.12.message_ref.refs_2_, ...), custom_call_target="tpu_custom_call", output_to_operand_aliasing={{1}: (6, {})} | custom-call | flops 1000000000 | bytes 4194304 | tf_op jit(solution)/shard_map/own/pallas_call | solution.py:269
  40.3 1.1 %collective-permute-done.13.over_ref = bf16[64,1024]{1,0:T(8,128)(2,1)S(1)} collective-permute-done((bf16[64,1024]{1,0:T(8,128)(2,1)S(1)}, bf16[64,1024]{1,0:T(8,128)(2,1)S(1)}, u32[]{:S(2)}, u32[]{:S(2)}) %collective-permute-start.13) | collective-permute-done | bytes 131104 | tf_op jit(solution)/shard_map/ppermute | solution.py:330
  41.4 0.5 %halo.7.refs_0_ = f32[64,1024]{1,0:T(8,128)S(1)} custom-call(s32[1]{0:T(128)} %bitcast.index_ref.refs_0_, f32[64,1024]{1,0:T(8,128)S(1)} %get-tuple-element.67.acc_ref, bf16[64,1024]{1,0:T(8,128)(2,1)S(1)} %collective-permute-done.13.over_ref, bf16[36,256,256]{2,1,0:T(8,128)(2,1)S(1)} %get-tuple-element.44.d_ref.refs_3_), custom_call_target="tpu_custom_call" | custom-call | flops 1000000000 | bytes 4194304 | tf_op jit(solution)/shard_map/halo/pallas_call | solution.py:269
  42.0 0.0 collective-permute-done.14.refs_2_
  42.0 0.7 %collective-permute-done.15.refs_3_ = bf16[64,128]{1,0:T(8,128)(2,1)S(1)} collective-permute-done((bf16[64,128]{1,0:T(8,128)(2,1)S(1)}, bf16[64,128]{1,0:T(8,128)(2,1)S(1)}, u32[]{:S(2)}, u32[]{:S(2)}) %collective-permute-start.15) | collective-permute-done | bytes 16416 | tf_op jit(solution)/shard_map/ppermute | solution.py:342
  42.6 0.9 %last.1 = bf16[4,64,1024]{2,1,0:T(8,128)(2,1)} custom-call(f32[64,1024]{1,0:T(8,128)S(1)} %halo.7.refs_0_, bf16[256,1024]{1,0:T(8,128)(2,1)S(1)} %get-tuple-element.45.refs_2_.refs_1_, bf16[64,128]{1,0:T(8,128)(2,1)S(1)} %collective-permute-done.14.refs_2_, bf16[64,128]{1,0:T(8,128)(2,1)S(1)} %collective-permute-done.15.refs_3_, ...), custom_call_target="tpu_custom_call", output_to_operand_aliasing={{}: (4, {})} | custom-call | flops 1000000000 | bytes 4194304 | tf_op jit(solution)/shard_map/last/pallas_call | solution.py:269
  (4 shorter events, 0.1 us)
Async XLA Ops:
  1.9 6.2 %collective-permute-start = (bf16[64,1536]{1,0:T(8,128)(2,1)S(1)}, bf16[64,1536]{1,0:T(8,128)(2,1)S(1)}, u32[]{:S(2)}, u32[]{:S(2)}) collective-permute-start(bf16[64,1536]{1,0:T(8,128)(2,1)S(1)} %get-tuple-element.39), channel_id=1, source_target_pairs={{0,1},{1,0},{2,3},{3,2},{4,5},{5,4},{6,7},{7,6},{8,9},{9,8},{10,11... | collective-permute-start | bytes 589832 | tf_op jit(solution)/shard_map/ppermute | solution.py:329
  2.5 10.0 %collective-permute-start.1 = (bf16[64,1024]{1,0:T(8,128)(2,1)}, bf16[64,1024]{1,0:T(8,128)(2,1)S(1)}, u32[]{:S(2)}, u32[]{:S(2)}) collective-permute-start(bf16[64,1024]{1,0:T(8,128)(2,1)} %refs_4_.2), channel_id=1, source_target_pairs={{0,15},{1,2},{2,1},{3,4},{4,3},{5,6},{6,5},{7,8},{8,7},{9,10},{10,... | collective-permute-start | bytes 393224 | tf_op jit(solution)/shard_map/ppermute | solution.py:330
  8.1 4.9 %collective-permute-start.2 = (bf16[64,128]{1,0:T(8,128)(2,1)S(1)}, bf16[64,128]{1,0:T(8,128)(2,1)S(1)}, u32[]{:S(2)}, u32[]{:S(2)}) collective-permute-start(bf16[64,128]{1,0:T(8,128)(2,1)S(1)} %get-tuple-element.41.refs_6_), channel_id=1, source_target_pairs={{0,8},{1,11},{2,10},{3,9},{4,12},{5,15},{6,14},{7,13},{8,0},{9,3},... | collective-permute-start | bytes 49160 | tf_op jit(solution)/shard_map/ppermute | solution.py:342
  8.2 5.0 %collective-permute-start.3 = (bf16[64,128]{1,0:T(8,128)(2,1)S(1)}, bf16[64,128]{1,0:T(8,128)(2,1)S(1)}, u32[]{:S(2)}, u32[]{:S(2)}) collective-permute-start(bf16[64,128]{1,0:T(8,128)(2,1)S(1)} %get-tuple-element.42.refs_7_), channel_id=1, source_target_pairs={{0,9},{1,10},{2,11},{3,8},{4,13},{5,14},{6,15},{7,12},{8,1},{9,2},... | collective-permute-start | bytes 49160 | tf_op jit(solution)/shard_map/ppermute | solution.py:342
  13.9 3.8 %collective-permute-start.4 = (bf16[64,1536]{1,0:T(8,128)(2,1)S(1)}, bf16[64,1536]{1,0:T(8,128)(2,1)S(1)}, u32[]{:S(2)}, u32[]{:S(2)}) collective-permute-start(bf16[64,1536]{1,0:T(8,128)(2,1)S(1)} %get-tuple-element.49), channel_id=1, source_target_pairs={{0,1},{1,0},{2,3},{3,2},{4,5},{5,4},{6,7},{7,6},{8,9},{9,8},{10,11... | collective-permute-start | bytes 589832 | tf_op jit(solution)/shard_map/ppermute | solution.py:329
  14.2 8.2 %collective-permute-start.5 = (bf16[64,1024]{1,0:T(8,128)(2,1)S(1)}, bf16[64,1024]{1,0:T(8,128)(2,1)S(1)}, u32[]{:S(2)}, u32[]{:S(2)}) collective-permute-start(bf16[64,1024]{1,0:T(8,128)(2,1)S(1)} %get-tuple-element.48.refs_1_), channel_id=1, source_target_pairs={{0,15},{1,2},{2,1},{3,4},{4,3},{5,6},{6,5},{7,8},{8,7},{9,10},{10,... | collective-permute-start | bytes 393224 | tf_op jit(solution)/shard_map/ppermute | solution.py:330
  17.7 5.3 %collective-permute-start.6 = (bf16[64,128]{1,0:T(8,128)(2,1)S(1)}, bf16[64,128]{1,0:T(8,128)(2,1)S(1)}, u32[]{:S(2)}, u32[]{:S(2)}) collective-permute-start(bf16[64,128]{1,0:T(8,128)(2,1)S(1)} %get-tuple-element.51.refs_4_), channel_id=1, source_target_pairs={{0,8},{1,11},{2,10},{3,9},{4,12},{5,15},{6,14},{7,13},{8,0},{9,3},... | collective-permute-start | bytes 49160 | tf_op jit(solution)/shard_map/ppermute | solution.py:342
  18.4 5.1 %collective-permute-start.7 = (bf16[64,128]{1,0:T(8,128)(2,1)S(1)}, bf16[64,128]{1,0:T(8,128)(2,1)S(1)}, u32[]{:S(2)}, u32[]{:S(2)}) collective-permute-start(bf16[64,128]{1,0:T(8,128)(2,1)S(1)} %get-tuple-element.52.refs_5_), channel_id=1, source_target_pairs={{0,9},{1,10},{2,11},{3,8},{4,13},{5,14},{6,15},{7,12},{8,1},{9,2},... | collective-permute-start | bytes 49160 | tf_op jit(solution)/shard_map/ppermute | solution.py:342
  24.2 2.8 %collective-permute-start.8 = (bf16[64,1536]{1,0:T(8,128)(2,1)S(1)}, bf16[64,1536]{1,0:T(8,128)(2,1)S(1)}, u32[]{:S(2)}, u32[]{:S(2)}) collective-permute-start(bf16[64,1536]{1,0:T(8,128)(2,1)S(1)} %get-tuple-element.55), channel_id=1, source_target_pairs={{0,1},{1,0},{2,3},{3,2},{4,5},{5,4},{6,7},{7,6},{8,9},{9,8},{10,11... | collective-permute-start | bytes 589832 | tf_op jit(solution)/shard_map/ppermute | solution.py:329
  24.4 7.4 %collective-permute-start.9 = (bf16[64,1024]{1,0:T(8,128)(2,1)S(1)}, bf16[64,1024]{1,0:T(8,128)(2,1)S(1)}, u32[]{:S(2)}, u32[]{:S(2)}) collective-permute-start(bf16[64,1024]{1,0:T(8,128)(2,1)S(1)} %get-tuple-element.54.refs_1_), channel_id=1, source_target_pairs={{0,15},{1,2},{2,1},{3,4},{4,3},{5,6},{6,5},{7,8},{8,7},{9,10},{10,... | collective-permute-start | bytes 393224 | tf_op jit(solution)/shard_map/ppermute | solution.py:330
  27.0 5.3 %collective-permute-start.10 = (bf16[64,128]{1,0:T(8,128)(2,1)S(1)}, bf16[64,128]{1,0:T(8,128)(2,1)S(1)}, u32[]{:S(2)}, u32[]{:S(2)}) collective-permute-start(bf16[64,128]{1,0:T(8,128)(2,1)S(1)} %get-tuple-element.57.refs_4_), channel_id=1, source_target_pairs={{0,8},{1,11},{2,10},{3,9},{4,12},{5,15},{6,14},{7,13},{8,0},{9,3},... | collective-permute-start | bytes 49160 | tf_op jit(solution)/shard_map/ppermute | solution.py:342
  28.0 5.1 %collective-permute-start.11 = (bf16[64,128]{1,0:T(8,128)(2,1)S(1)}, bf16[64,128]{1,0:T(8,128)(2,1)S(1)}, u32[]{:S(2)}, u32[]{:S(2)}) collective-permute-start(bf16[64,128]{1,0:T(8,128)(2,1)S(1)} %get-tuple-element.58.refs_5_), channel_id=1, source_target_pairs={{0,9},{1,10},{2,11},{3,8},{4,13},{5,14},{6,15},{7,12},{8,1},{9,2},... | collective-permute-start | bytes 49160 | tf_op jit(solution)/shard_map/ppermute | solution.py:342
  33.8 3.0 %collective-permute-start.12 = (bf16[64,1536]{1,0:T(8,128)(2,1)S(1)}, bf16[64,1536]{1,0:T(8,128)(2,1)S(1)}, u32[]{:S(2)}, u32[]{:S(2)}) collective-permute-start(bf16[64,1536]{1,0:T(8,128)(2,1)S(1)} %get-tuple-element.62), channel_id=1, source_target_pairs={{0,1},{1,0},{2,3},{3,2},{4,5},{5,4},{6,7},{7,6},{8,9},{9,8},{10,11... | collective-permute-start | bytes 589832 | tf_op jit(solution)/shard_map/ppermute | solution.py:329
  34.2 7.3 %collective-permute-start.13 = (bf16[64,1024]{1,0:T(8,128)(2,1)S(1)}, bf16[64,1024]{1,0:T(8,128)(2,1)S(1)}, u32[]{:S(2)}, u32[]{:S(2)}) collective-permute-start(bf16[64,1024]{1,0:T(8,128)(2,1)S(1)} %get-tuple-element.61.refs_1_), channel_id=1, source_target_pairs={{0,15},{1,2},{2,1},{3,4},{4,3},{5,6},{6,5},{7,8},{8,7},{9,10},{10,... | collective-permute-start | bytes 393224 | tf_op jit(solution)/shard_map/ppermute | solution.py:330
  36.8 5.1 %collective-permute-start.14 = (bf16[64,128]{1,0:T(8,128)(2,1)S(1)}, bf16[64,128]{1,0:T(8,128)(2,1)S(1)}, u32[]{:S(2)}, u32[]{:S(2)}) collective-permute-start(bf16[64,128]{1,0:T(8,128)(2,1)S(1)} %get-tuple-element.64.refs_4_), channel_id=1, source_target_pairs={{0,8},{1,11},{2,10},{3,9},{4,12},{5,15},{6,14},{7,13},{8,0},{9,3},... | collective-permute-start | bytes 49160 | tf_op jit(solution)/shard_map/ppermute | solution.py:342
  37.3 5.3 %collective-permute-start.15 = (bf16[64,128]{1,0:T(8,128)(2,1)S(1)}, bf16[64,128]{1,0:T(8,128)(2,1)S(1)}, u32[]{:S(2)}, u32[]{:S(2)}) collective-permute-start(bf16[64,128]{1,0:T(8,128)(2,1)S(1)} %get-tuple-element.65.refs_5_), channel_id=1, source_target_pairs={{0,9},{1,10},{2,11},{3,8},{4,13},{5,14},{6,15},{7,12},{8,1},{9,2},... | collective-permute-start | bytes 49160 | tf_op jit(solution)/shard_map/ppermute | solution.py:342

commit v9 on v8

--- a/solution.py
+++ b/solution.py
@@ -134,10 +134,11 @@
 
 
 def prepare_kernel(plan, index_ref, *refs):
-    sources, refs = refs[:7], refs[7:]
-    x_ref, g_ref, cb_ref, order_ref = refs[:4]
-    sends, (near_ref, offsets_ref, rows_ref, cols_ref, col_ref, coup_ref, sems) = refs[4:-7], refs[-7:]
-    targets = (near_ref, offsets_ref, rows_ref, cols_ref, x_ref, col_ref, coup_ref)
+    sources, tiles_hbm, refs = refs[:8], refs[8], refs[9:]
+    x_ref, d_ref, g_ref, cb_ref, rb_ref = refs[:5]
+    sends, held = refs[5:-11], refs[-11:]
+    near_ref, offsets_ref, rows_ref, cols_ref, col_ref, coup_ref, row_ref, taken, empty, sems, tile_sems = held
+    targets = (near_ref, offsets_ref, rows_ref, cols_ref, x_ref, col_ref, coup_ref, row_ref)
     copies = [
         pltpu.make_async_copy(source, target, sems.at[i])
         for i, (source, target) in enumerate(zip(sources, targets))
@@ -145,21 +146,32 @@
     for copy in copies:
         copy.start()
     rank, size = plan.rank, plan.size
+    for cell in range(plan.cells):
+        taken[cell] = 0
     cb_ref[...] = jnp.zeros_like(cb_ref)
+    rb_ref[...] = jnp.zeros_like(rb_ref)
     g_ref[...] = jnp.zeros_like(g_ref)
-    for copy in copies:
+    copies[0].wait()
+    copies[1].wait()
+    tiles = []
+    for s in range(plan.tiles):
+        cell = near_ref[s] * SPAN + offsets_ref[s] + REACH
+        taken[cell] = 1
+        tiles.append(pltpu.make_async_copy(tiles_hbm.at[s], d_ref.at[cell], tile_sems.at[s]))
+        tiles[-1].start()
+    for copy in copies[2:]:
         copy.wait()
-    first, last = jnp.int32(0), jnp.int32(plan.tiles - 1)
-    for s in range(plan.tiles):
-        place = near_ref[s] + offsets_ref[s]
-        own = jnp.logical_and(place >= 0, place < plan.per_device).astype(jnp.int32)
-        where = jnp.where(own == 1, first, last)
-        order_ref[where] = s
-        order_ref[plan.tiles + where] = near_ref[s] * SPAN + offsets_ref[s] + REACH
-        first, last = first + own, last - (1 - own)
-    order_ref[2 * plan.tiles] = first
+    count = jnp.int32(0)
+    for cell in range(plan.cells):
+        empty[count] = cell
+        count = count + 1 - taken[cell]
+    for place in range(plan.cells - plan.tiles):
+        d_ref[empty[place]] = jnp.zeros(d_ref.shape[1:], d_ref.dtype)
     for c in range(plan.per_device):
-        cb_ref[c * rank : (c + 1) * rank, c * size : (c + 1) * size] = col_ref[c]
+        columns = slice(c * size, (c + 1) * size)
+        cb_ref[c * rank : (c + 1) * rank, columns] = col_ref[c]
+        for start in (c * rank, plan.width + c * rank):
+            rb_ref[start : start + rank, columns] = row_ref[c]
     column = lax.broadcasted_iota(jnp.int32, (rank, plan.width), 1) // rank
     shift = 0 if plan.paired else plan.member(index_ref)
     for s in range(plan.slots):
@@ -172,64 +184,24 @@
         wide = jnp.where(column == cols_ref[s], jnp.concatenate([tile] * plan.per_device, axis=1), 0.0)
         g_ref[where] = g_ref[where] + wide.astype(BF16)
     plan.send_far(index_ref, x_ref[...], cb_ref, g_ref, sends)
+    for copy in tiles:
+        copy.wait()
 
 
 def relay_kernel(plan, index_ref, keep_ref, message_ref, *out_refs):
     plan.relay_far(index_ref, keep_ref, message_ref, out_refs)
 
 
-def first_own_kernel(plan, *refs):
-    index_ref, order_ref, x_ref, near_ref, row_hbm, tiles_hbm = refs[:6]
-    acc_ref, d_ref, rb_ref, row_ref, empty, sem, tile_sems = refs[-7:]
-    rank, size = plan.rank, plan.size
-
-    def tile_copy(place):
-        source, cell = order_ref[place], order_ref[plan.tiles + place]
-        return pltpu.make_async_copy(tiles_hbm.at[source], d_ref.at[cell], tile_sems.at[place])
-
-    def wait_for(first, last):
-        @pl.loop(first, last)
-        def _(place):
-            tile_copy(place).wait()
-
-    for place in range(plan.tiles):
-        tile_copy(place).start()
-    copy = pltpu.make_async_copy(row_hbm, row_ref, sem)
-    copy.start()
-    for cell in range(plan.cells):
-        empty[cell] = 1
-    for place in range(plan.tiles):
-        empty[order_ref[plan.tiles + place]] = 0
-    count = jnp.int32(0)
-    for cell in range(plan.cells):
-        missing = empty[cell]
-        empty[plan.cells + count] = cell
-        count = count + missing
-
-    @pl.loop(0, count)
-    def _(place):
-        d_ref[empty[plan.cells + place]] = jnp.zeros(d_ref.shape[1:], d_ref.dtype)
-
-    rb_ref[...] = jnp.zeros_like(rb_ref)
-    copy.wait()
-    for c in range(plan.per_device):
-        for start in (c * rank, plan.width + c * rank):
-            rb_ref[start : start + rank, c * size : (c + 1) * size] = row_ref[c]
-    own = order_ref[2 * plan.tiles]
-    wait_for(0, own)
-    plan.near_sums(x_ref, d_ref, acc_ref, 0)
-    wait_for(own, plan.tiles)
-    plan.halo_sums(lax.rem(index_ref[0], 2) == 1, near_ref, d_ref, acc_ref, acc_ref)
-
-
 def own_kernel(plan, slot, *refs):
     index_ref, x_ref, near_ref, d_ref = refs[:4]
-    acc_ref, krylov_ref, sem = refs[-3:]
-    copy = pltpu.make_async_copy(x_ref, krylov_ref.at[slot], sem)
-    copy.start()
+    acc_ref = refs[-1] if slot is None else refs[-3]
+    if slot is not None:
+        copy = pltpu.make_async_copy(x_ref, refs[-2].at[slot], refs[-1])
+        copy.start()
     plan.near_sums(x_ref, d_ref, acc_ref, 0)
     plan.halo_sums(lax.rem(index_ref[0], 2) == 1, near_ref, d_ref, acc_ref, acc_ref)
-    copy.wait()
+    if slot is not None:
+        copy.wait()
 
 
 def halo_kernel(plan, index_ref, acc_ref, over_ref, d_ref, *refs):
@@ -309,22 +281,28 @@
     current, sends, krylov = block, None, None
     for product in range(PRODUCTS):
         if product == 0:
-            ins = [near_rows, near_offsets, far_rows, far_cols, block, col_basis, couplings]
-            current, coupled, col_wide, order, *sends = call(
+            small = [near_rows, near_offsets, far_rows, far_cols]
+            bases = [col_basis, couplings, row_basis]
+            current, dense, coupled, col_wide, row_wide, *sends = call(
                 functools.partial(prepare_kernel, plan),
                 "prepare",
-                [index, *ins],
-                [IN_SMEM] + [IN_HBM] * 7,
+                [index, *small, block, *bases, near_tiles],
+                [IN_SMEM] + [IN_HBM] * 9,
                 [
                     block_out,
+                    pltpu.VMEM((plan.cells, plan.size, plan.size), BF16),
                     pltpu.VMEM((LEVELS, plan.members * width, width), BF16),
                     pltpu.VMEM((width, shard_len), BF16),
-                    pltpu.SMEM((2 * plan.tiles + 1,), jnp.int32),
+                    pltpu.VMEM((2 * width, shard_len), BF16),
                     *sends_out,
                 ],
-                [IN_VMEM] * 3 + [IN_SMEM] + [IN_VMEM] * len(sends_out),
-                scratch=scratch_for(near_rows, near_offsets, far_rows, far_cols, col_basis, couplings)
-                + [pltpu.SemaphoreType.DMA((7,))],
+                scratch=scratch_for(*small, *bases)
+                + [
+                    pltpu.SMEM((plan.cells,), jnp.int32),
+                    pltpu.SMEM((plan.cells,), jnp.int32),
+                    pltpu.SemaphoreType.DMA((8,)),
+                    pltpu.SemaphoreType.DMA((plan.tiles,)),
+                ],
             )
         near = lax.ppermute(sends[0] if plan.paired else current, axes, plan.near)
         over = lax.ppermute(block if product == 0 else current, axes, plan.over)
@@ -341,36 +319,19 @@
             routes = plan.routes
         fars = [lax.ppermute(s, axes, route) for s, route in zip(sends, routes)]
         after = sends if plan.paired else []
-        if product == 0:
-            acc, dense, row_wide = call(
-                functools.partial(first_own_kernel, plan),
-                "first_own",
-                [index, order, current, near, row_basis, near_tiles, *after],
-                [IN_SMEM] * 2 + [IN_VMEM] * 2 + [IN_HBM] * 2 + [ANYWHERE] * len(after),
-                [
-                    acc_out,
-                    pltpu.VMEM((plan.cells, plan.size, plan.size), BF16),
-                    pltpu.VMEM((2 * width, shard_len), BF16),
-                ],
-                scratch=scratch_for(row_basis)
-                + [
-                    pltpu.SMEM((2 * plan.cells + 1,), jnp.int32),
-                    pltpu.SemaphoreType.DMA,
-                    pltpu.SemaphoreType.DMA((plan.tiles,)),
-                ],
-            )
-        else:
-            ins = [index, current, near, dense, *after] + ([krylov] if product > 1 else [])
-            acc, krylov = call(
-                functools.partial(own_kernel, plan, product - 1),
-                "own",
-                ins,
-                [IN_SMEM] + [IN_VMEM] * 3 + [ANYWHERE] * (len(ins) - 4),
-                [acc_out, krylov_out],
-                [IN_VMEM, ANYWHERE],
-                [pltpu.SemaphoreType.DMA],
-                {len(ins) - 1: 1} if product > 1 else None,
-            )
+        ins, outs = [index, current, near, dense, *after], [acc_out]
+        specs = [IN_SMEM] + [IN_VMEM] * 3 + [ANYWHERE] * len(after)
+        out_specs, scratch, aliases = [IN_VMEM], [], None
+        if product > 0:
+            outs, out_specs, scratch = outs + [krylov_out], out_specs + [ANYWHERE], [pltpu.SemaphoreType.DMA]
+        if product > 1:
+            aliases = {len(ins): 1}
+            ins, specs = ins + [krylov], specs + [ANYWHERE]
+        slot = product - 1 if product else None
+        acc, *rest = call(
+            functools.partial(own_kernel, plan, slot), "own", ins, specs, outs, out_specs, scratch, aliases
+        )
+        krylov = rest[0] if rest else None
         (acc,) = call(
             functools.partial(halo_kernel, plan),
             "halo",

time: 43.7 us -> 44.9 us (1.027)
  waiting for transfers between devices: 5.1 us -> 12.1 us
  starting transfers between devices: 23.4 us -> 19 us
  Pallas kernels: 14.8 us -> 13.5 us
    ppermute x8, starting transfers between devices: 7.74 us -> 3.61 us  [on_device(): fars = [lax.ppermute(s, axes, route) for s, route in zip(sends, routes)]]
    ppermute x4, waiting for transfers between devices: 2.85 us -> 6.94 us  [on_device(): over = lax.ppermute(block if product == 0 else current, axes, plan.over)]
    ppermute x8, waiting for transfers between devices: 2.24 us -> 5.15 us  [on_device(): fars = [lax.ppermute(s, axes, route) for s, route in zip(sends, routes)]]
    pallas_call x17, Pallas kernels: 14.8 us -> 13.5 us  [call(): pl.pallas_call(kernel, in_specs=list(specs), out_specs=out_specs or [IN_V...]
    ppermute x4, starting transfers between devices: 1.4 us -> 0.73 us  [on_device(): near = lax.ppermute(sends[0] if plan.paired else current, axes, plan.near)]
  transfers between devices with their start and end apart: 16 -> 16, of which waited for: 6 -> 10; matrix products, arithmetic and copies ran while one was open for 0% -> 0% of each run, Pallas kernels for 23% -> 16%
where the time goes in v9:
time: 44.9 us; the launch traced here: 44.8 us
  starting transfers between devices  19 us (42%)
  Pallas kernels  13.5 us (30%)
  waiting for transfers between devices  12.1 us (27%)
    ppermute x4, starting transfers between devices, on_device(): over = lax.ppermute(block if product == 0 else current, axes, plan.over)  14.7 us
    pallas_call x17, Pallas kernels, call(): pl.pallas_call(kernel, in_specs=list(specs), out_specs=out_specs or [IN_V...  13.5 us
    ppermute x4, waiting for transfers between devices, on_device(): over = lax.ppermute(block if product == 0 else current, axes, plan.over)  6.94 us
    ppermute x8, waiting for transfers between devices, on_device(): fars = [lax.ppermute(s, axes, route) for s, route in zip(sends, routes)]  5.15 us
    ppermute x8, starting transfers between devices, on_device(): fars = [lax.ppermute(s, axes, route) for s, route in zip(sends, routes)]  3.61 us
  transfers between devices with their start and end apart: 16, of which 10 were waited for; matrix products, arithmetic and copies ran while one was open for 0% of the time, Pallas kernels for 16%

profile of v9, /device:TPU:0, one launch (start us, length us, event | category | flops | bytes accessed | tf_op | source)
XLA Modules:
  0.0 44.8 jit_solution(10218374746310498539)
XLA Ops:
  0.0 0.0 copy-start
  0.0 3.3 %prepare.1 = (bf16[64,1024]{1,0:T(8,128)(2,1)S(1)}, bf16[36,256,256]{2,1,0:T(8,128)(2,1)S(1)}, bf16[3,512,128]{2,1,0:T(8,128)(2,1)S(1)}, bf16[128,1024]{1,0:T(8,...) custom-call(s32[1]{0:T(128)} %bitcast.index_ref.refs_0_, ...), custom_call_target="tpu_custom_call" | custom-call | flops 1000000000 | bytes 4194304 | tf_op jit(solution)/shard_map/prepare/pallas_call | solution.py:241
  3.3 0.5 %collective-permute-start = (bf16[64,1536]{1,0:T(8,128)(2,1)S(1)}, bf16[64,1536]{1,0:T(8,128)(2,1)S(1)}, u32[]{:S(2)}, u32[]{:S(2)}) collective-permute-start(bf16[64,1536]{1,0:T(8,128)(2,1)S(1)} %get-tuple-element.36), channel_id=1, source_target_pairs={{0,1},{1,0},{2,3},{3,2},{4,5},{5,4},{6,7},{7,6},{8,9},{9,8},{10,11... | collective-permute-start | bytes 589832 | tf_op jit(solution)/shard_map/ppermute | solution.py:307
  3.9 0.0 copy-done
  3.9 5.6 %collective-permute-start.1 = (bf16[64,1024]{1,0:T(8,128)(2,1)S(1)}, bf16[64,1024]{1,0:T(8,128)(2,1)S(1)}, u32[]{:S(2)}, u32[]{:S(2)}) collective-permute-start(bf16[64,1024]{1,0:T(8,128)(2,1)S(1)} %copy-done), channel_id=1, source_target_pairs={{0,15},{1,2},{2,1},{3,4},{4,3},{5,6},{6,5},{7,8},{8,7},{9,10},{10,... | collective-permute-start | bytes 393224 | tf_op jit(solution)/shard_map/ppermute | solution.py:308
  9.5 0.0 collective-permute-done.message_ref.refs_2_
  9.5 0.1 collective-permute-start.2
  9.6 0.3 collective-permute-start.3
  9.9 1.3 %own.4.acc_ref = f32[64,1024]{1,0:T(8,128)S(1)} custom-call(s32[1]{0:T(128)} %bitcast.index_ref.refs_0_, bf16[64,1024]{1,0:T(8,128)(2,1)S(1)} %get-tuple-element.35.refs_1_, bf16[64,1536]{1,0:T(8,128)(2,1)S(1)} %collective-permute-done.message_ref.refs_2_, bf16[36,256,256]{2,1,0:T(8,128)(2,1)S(1)} %get-tuple-element.37.refs_3_.d_ref, ...), custom_call_target="tpu_custom_call" | custom-call | flops 1000000000 | bytes 4194304 | tf_op jit(solution)/shard_map/own/pallas_call | solution.py:241
  11.1 1.1 %collective-permute-done.1.over_ref = bf16[64,1024]{1,0:T(8,128)(2,1)S(1)} collective-permute-done((bf16[64,1024]{1,0:T(8,128)(2,1)S(1)}, bf16[64,1024]{1,0:T(8,128)(2,1)S(1)}, u32[]{:S(2)}, u32[]{:S(2)}) %collective-permute-start.1) | collective-permute-done | bytes 131104 | tf_op jit(solution)/shard_map/ppermute | solution.py:308
  12.3 0.5 %halo.4.refs_1_ = f32[64,1024]{1,0:T(8,128)S(1)} custom-call(s32[1]{0:T(128)} %bitcast.index_ref.refs_0_, f32[64,1024]{1,0:T(8,128)S(1)} %own.4.acc_ref, bf16[64,1024]{1,0:T(8,128)(2,1)S(1)} %collective-permute-done.1.over_ref, bf16[36,256,256]{2,1,0:T(8,128)(2,1)S(1)} %get-tuple-element.37.refs_3_.d_ref), custom_call_target="tpu_custom_call" | custom-call | flops 1000000000 | bytes 4194304 | tf_op jit(solution)/shard_map/halo/pallas_call | solution.py:241
  12.8 1.5 %collective-permute-done.2.refs_5_ = bf16[64,128]{1,0:T(8,128)(2,1)S(1)} collective-permute-done((bf16[64,128]{1,0:T(8,128)(2,1)S(1)}, bf16[64,128]{1,0:T(8,128)(2,1)S(1)}, u32[]{:S(2)}, u32[]{:S(2)}) %collective-permute-start.2) | collective-permute-done | bytes 16416 | tf_op jit(solution)/shard_map/ppermute | solution.py:320
  14.2 0.4 collective-permute-done.3.refs_6_
  14.6 0.7 %finish.3 = (bf16[64,1024]{1,0:T(8,128)(2,1)S(1)}, bf16[64,1536]{1,0:T(8,128)(2,1)S(1)}, f32[64,256]{1,0:T(8,128)S(1)}) custom-call(s32[1]{0:T(128)} %bitcast.index_ref.refs_0_, f32[64,1024]{1,0:T(8,128)S(1)} %halo.4.refs_1_, bf16[256,1024]{1,0:T(8,128)(2,1)S(1)} %get-tuple-element.41.refs_2_.refs_1_, bf16[128,1024]{1,0:T(8,128)(2,1)S(1)} %get-tuple-element.42.refs_3_, ...), custom_call_target="tpu_custom_call" | custom-call | flops 1000000000 | bytes 4194304 | tf_op jit(solution)/shard_map/finish/pallas_call | solution.py:241
  15.3 0.1 collective-permute-start.4
  15.4 3.7 %collective-permute-start.5 = (bf16[64,1024]{1,0:T(8,128)(2,1)S(1)}, bf16[64,1024]{1,0:T(8,128)(2,1)S(1)}, u32[]{:S(2)}, u32[]{:S(2)}) collective-permute-start(bf16[64,1024]{1,0:T(8,128)(2,1)S(1)} %get-tuple-element.44.refs_1_), channel_id=1, source_target_pairs={{0,15},{1,2},{2,1},{3,4},{4,3},{5,6},{6,5},{7,8},{8,7},{9,10},{10,... | collective-permute-start | bytes 393224 | tf_op jit(solution)/shard_map/ppermute | solution.py:308
  19.1 0.0 collective-permute-done.4.message_ref.refs_2_
  19.1 0.7 %collective-permute-start.6 = (bf16[64,128]{1,0:T(8,128)(2,1)S(1)}, bf16[64,128]{1,0:T(8,128)(2,1)S(1)}, u32[]{:S(2)}, u32[]{:S(2)}) collective-permute-start(bf16[64,128]{1,0:T(8,128)(2,1)S(1)} %get-tuple-element.47.refs_4_), channel_id=1, source_target_pairs={{0,8},{1,11},{2,10},{3,9},{4,12},{5,15},{6,14},{7,13},{8,0},{9,3},... | collective-permute-start | bytes 49160 | tf_op jit(solution)/shard_map/ppermute | solution.py:320
  19.8 0.1 collective-permute-start.7
  19.9 1.3 %own.5 = (f32[64,1024]{1,0:T(8,128)S(1)}, bf16[4,64,1024]{2,1,0:T(8,128)(2,1)}) custom-call(s32[1]{0:T(128)} %bitcast.index_ref.refs_0_, bf16[64,1024]{1,0:T(8,128)(2,1)S(1)} %get-tuple-element.44.refs_1_, bf16[64,1536]{1,0:T(8,128)(2,1)S(1)} %collective-permute-done.4.message_ref.refs_2_, bf16[36,256,256]{2,1,0:T(8,128)(2,1)S(1)} %get-tuple-element.37.refs_3_.d_ref, ...), custom_call_target="tpu_custom_call" | custom-call | flops 1000000000 | bytes 4194304 | tf_op jit(solution)/shard_map/own/pallas_call | solution.py:241
  21.2 1.5 %collective-permute-done.5.over_ref = bf16[64,1024]{1,0:T(8,128)(2,1)S(1)} collective-permute-done((bf16[64,1024]{1,0:T(8,128)(2,1)S(1)}, bf16[64,1024]{1,0:T(8,128)(2,1)S(1)}, u32[]{:S(2)}, u32[]{:S(2)}) %collective-permute-start.5) | collective-permute-done | bytes 131104 | tf_op jit(solution)/shard_map/ppermute | solution.py:308
  22.6 0.5 %halo.5.refs_1_ = f32[64,1024]{1,0:T(8,128)S(1)} custom-call(s32[1]{0:T(128)} %bitcast.index_ref.refs_0_, f32[64,1024]{1,0:T(8,128)S(1)} %get-tuple-element.49.acc_ref, bf16[64,1024]{1,0:T(8,128)(2,1)S(1)} %collective-permute-done.5.over_ref, bf16[36,256,256]{2,1,0:T(8,128)(2,1)S(1)} %get-tuple-element.37.refs_3_.d_ref), custom_call_target="tpu_custom_call" | custom-call | flops 1000000000 | bytes 4194304 | tf_op jit(solution)/shard_map/halo/pallas_call | solution.py:241
  23.2 0.7 %collective-permute-done.6.refs_5_ = bf16[64,128]{1,0:T(8,128)(2,1)S(1)} collective-permute-done((bf16[64,128]{1,0:T(8,128)(2,1)S(1)}, bf16[64,128]{1,0:T(8,128)(2,1)S(1)}, u32[]{:S(2)}, u32[]{:S(2)}) %collective-permute-start.6) | collective-permute-done | bytes 16416 | tf_op jit(solution)/shard_map/ppermute | solution.py:320
  23.8 1.2 %collective-permute-done.7.refs_6_ = bf16[64,128]{1,0:T(8,128)(2,1)S(1)} collective-permute-done((bf16[64,128]{1,0:T(8,128)(2,1)S(1)}, bf16[64,128]{1,0:T(8,128)(2,1)S(1)}, u32[]{:S(2)}, u32[]{:S(2)}) %collective-permute-start.7) | collective-permute-done | bytes 16416 | tf_op jit(solution)/shard_map/ppermute | solution.py:320
  25.0 0.7 %finish.4 = (bf16[64,1024]{1,0:T(8,128)(2,1)S(1)}, bf16[64,1536]{1,0:T(8,128)(2,1)S(1)}, f32[64,256]{1,0:T(8,128)S(1)}) custom-call(s32[1]{0:T(128)} %bitcast.index_ref.refs_0_, f32[64,1024]{1,0:T(8,128)S(1)} %halo.5.refs_1_, bf16[256,1024]{1,0:T(8,128)(2,1)S(1)} %get-tuple-element.41.refs_2_.refs_1_, bf16[128,1024]{1,0:T(8,128)(2,1)S(1)} %get-tuple-element.42.refs_3_, ...), custom_call_target="tpu_custom_call" | custom-call | flops 1000000000 | bytes 4194304 | tf_op jit(solution)/shard_map/finish/pallas_call | solution.py:241
  25.7 0.1 collective-permute-start.8
  25.8 2.6 %collective-permute-start.9 = (bf16[64,1024]{1,0:T(8,128)(2,1)S(1)}, bf16[64,1024]{1,0:T(8,128)(2,1)S(1)}, u32[]{:S(2)}, u32[]{:S(2)}) collective-permute-start(bf16[64,1024]{1,0:T(8,128)(2,1)S(1)} %get-tuple-element.50.refs_1_), channel_id=1, source_target_pairs={{0,15},{1,2},{2,1},{3,4},{4,3},{5,6},{6,5},{7,8},{8,7},{9,10},{10,... | collective-permute-start | bytes 393224 | tf_op jit(solution)/shard_map/ppermute | solution.py:308
  28.4 0.0 collective-permute-done.8.message_ref.refs_2_
  28.4 0.9 %collective-permute-start.10 = (bf16[64,128]{1,0:T(8,128)(2,1)S(1)}, bf16[64,128]{1,0:T(8,128)(2,1)S(1)}, u32[]{:S(2)}, u32[]{:S(2)}) collective-permute-start(bf16[64,128]{1,0:T(8,128)(2,1)S(1)} %get-tuple-element.53.refs_4_), channel_id=1, source_target_pairs={{0,8},{1,11},{2,10},{3,9},{4,12},{5,15},{6,14},{7,13},{8,0},{9,3},... | collective-permute-start | bytes 49160 | tf_op jit(solution)/shard_map/ppermute | solution.py:320
  29.3 0.4 collective-permute-start.11
  29.7 1.3 %own.6 = (f32[64,1024]{1,0:T(8,128)S(1)}, bf16[4,64,1024]{2,1,0:T(8,128)(2,1)}) custom-call(s32[1]{0:T(128)} %bitcast.index_ref.refs_0_, bf16[64,1024]{1,0:T(8,128)(2,1)S(1)} %get-tuple-element.50.refs_1_, bf16[64,1536]{1,0:T(8,128)(2,1)S(1)} %collective-permute-done.8.message_ref.refs_2_, ...), custom_call_target="tpu_custom_call", output_to_operand_aliasing={{1}: (6, {})} | custom-call | flops 1000000000 | bytes 4194304 | tf_op jit(solution)/shard_map/own/pallas_call | solution.py:241
  31.0 2.2 %collective-permute-done.9.over_ref = bf16[64,1024]{1,0:T(8,128)(2,1)S(1)} collective-permute-done((bf16[64,1024]{1,0:T(8,128)(2,1)S(1)}, bf16[64,1024]{1,0:T(8,128)(2,1)S(1)}, u32[]{:S(2)}, u32[]{:S(2)}) %collective-permute-start.9) | collective-permute-done | bytes 131104 | tf_op jit(solution)/shard_map/ppermute | solution.py:308
  33.2 0.5 %halo.6.refs_1_ = f32[64,1024]{1,0:T(8,128)S(1)} custom-call(s32[1]{0:T(128)} %bitcast.index_ref.refs_0_, f32[64,1024]{1,0:T(8,128)S(1)} %get-tuple-element.56.acc_ref, bf16[64,1024]{1,0:T(8,128)(2,1)S(1)} %collective-permute-done.9.over_ref, bf16[36,256,256]{2,1,0:T(8,128)(2,1)S(1)} %get-tuple-element.37.refs_3_.d_ref), custom_call_target="tpu_custom_call" | custom-call | flops 1000000000 | bytes 4194304 | tf_op jit(solution)/shard_map/halo/pallas_call | solution.py:241
  33.7 0.0 collective-permute-done.10.refs_5_
  33.8 0.7 %collective-permute-done.11.refs_6_ = bf16[64,128]{1,0:T(8,128)(2,1)S(1)} collective-permute-done((bf16[64,128]{1,0:T(8,128)(2,1)S(1)}, bf16[64,128]{1,0:T(8,128)(2,1)S(1)}, u32[]{:S(2)}, u32[]{:S(2)}) %collective-permute-start.11) | collective-permute-done | bytes 16416 | tf_op jit(solution)/shard_map/ppermute | solution.py:320
  34.4 0.7 %finish.5 = (bf16[64,1024]{1,0:T(8,128)(2,1)S(1)}, bf16[64,1536]{1,0:T(8,128)(2,1)S(1)}, f32[64,256]{1,0:T(8,128)S(1)}) custom-call(s32[1]{0:T(128)} %bitcast.index_ref.refs_0_, f32[64,1024]{1,0:T(8,128)S(1)} %halo.6.refs_1_, bf16[256,1024]{1,0:T(8,128)(2,1)S(1)} %get-tuple-element.41.refs_2_.refs_1_, bf16[128,1024]{1,0:T(8,128)(2,1)S(1)} %get-tuple-element.42.refs_3_, ...), custom_call_target="tpu_custom_call" | custom-call | flops 1000000000 | bytes 4194304 | tf_op jit(solution)/shard_map/finish/pallas_call | solution.py:241
  35.1 0.1 collective-permute-start.12
  35.2 2.8 %collective-permute-start.13 = (bf16[64,1024]{1,0:T(8,128)(2,1)S(1)}, bf16[64,1024]{1,0:T(8,128)(2,1)S(1)}, u32[]{:S(2)}, u32[]{:S(2)}) collective-permute-start(bf16[64,1024]{1,0:T(8,128)(2,1)S(1)} %get-tuple-element.57.refs_1_), channel_id=1, source_target_pairs={{0,15},{1,2},{2,1},{3,4},{4,3},{5,6},{6,5},{7,8},{8,7},{9,10},{10,... | collective-permute-start | bytes 393224 | tf_op jit(solution)/shard_map/ppermute | solution.py:308
  38.0 0.0 collective-permute-done.12.message_ref.refs_2_
  38.0 0.7 %collective-permute-start.14 = (bf16[64,128]{1,0:T(8,128)(2,1)S(1)}, bf16[64,128]{1,0:T(8,128)(2,1)S(1)}, u32[]{:S(2)}, u32[]{:S(2)}) collective-permute-start(bf16[64,128]{1,0:T(8,128)(2,1)S(1)} %get-tuple-element.60.refs_4_), channel_id=1, source_target_pairs={{0,8},{1,11},{2,10},{3,9},{4,12},{5,15},{6,14},{7,13},{8,0},{9,3},... | collective-permute-start | bytes 49160 | tf_op jit(solution)/shard_map/ppermute | solution.py:320
  38.7 0.6 %collective-permute-start.15 = (bf16[64,128]{1,0:T(8,128)(2,1)S(1)}, bf16[64,128]{1,0:T(8,128)(2,1)S(1)}, u32[]{:S(2)}, u32[]{:S(2)}) collective-permute-start(bf16[64,128]{1,0:T(8,128)(2,1)S(1)} %get-tuple-element.61.refs_5_), channel_id=1, source_target_pairs={{0,9},{1,10},{2,11},{3,8},{4,13},{5,14},{6,15},{7,12},{8,1},{9,2},... | collective-permute-start | bytes 49160 | tf_op jit(solution)/shard_map/ppermute | solution.py:320
  39.2 1.3 %own.7 = (f32[64,1024]{1,0:T(8,128)S(1)}, bf16[4,64,1024]{2,1,0:T(8,128)(2,1)}) custom-call(s32[1]{0:T(128)} %bitcast.index_ref.refs_0_, bf16[64,1024]{1,0:T(8,128)(2,1)S(1)} %get-tuple-element.57.refs_1_, bf16[64,1536]{1,0:T(8,128)(2,1)S(1)} %collective-permute-done.12.message_ref.refs_2_, ...), custom_call_target="tpu_custom_call", output_to_operand_aliasing={{1}: (6, {})} | custom-call | flops 1000000000 | bytes 4194304 | tf_op jit(solution)/shard_map/own/pallas_call | solution.py:241
  40.5 2.1 %collective-permute-done.13.over_ref = bf16[64,1024]{1,0:T(8,128)(2,1)S(1)} collective-permute-done((bf16[64,1024]{1,0:T(8,128)(2,1)S(1)}, bf16[64,1024]{1,0:T(8,128)(2,1)S(1)}, u32[]{:S(2)}, u32[]{:S(2)}) %collective-permute-start.13) | collective-permute-done | bytes 131104 | tf_op jit(solution)/shard_map/ppermute | solution.py:308
  42.6 0.5 %halo.7.refs_0_ = f32[64,1024]{1,0:T(8,128)S(1)} custom-call(s32[1]{0:T(128)} %bitcast.index_ref.refs_0_, f32[64,1024]{1,0:T(8,128)S(1)} %get-tuple-element.63.acc_ref, bf16[64,1024]{1,0:T(8,128)(2,1)S(1)} %collective-permute-done.13.over_ref, bf16[36,256,256]{2,1,0:T(8,128)(2,1)S(1)} %get-tuple-element.37.refs_3_.d_ref), custom_call_target="tpu_custom_call" | custom-call | flops 1000000000 | bytes 4194304 | tf_op jit(solution)/shard_map/halo/pallas_call | solution.py:241
  43.2 0.0 collective-permute-done.14.refs_2_
  43.2 0.8 %collective-permute-done.15.refs_3_ = bf16[64,128]{1,0:T(8,128)(2,1)S(1)} collective-permute-done((bf16[64,128]{1,0:T(8,128)(2,1)S(1)}, bf16[64,128]{1,0:T(8,128)(2,1)S(1)}, u32[]{:S(2)}, u32[]{:S(2)}) %collective-permute-start.15) | collective-permute-done | bytes 16416 | tf_op jit(solution)/shard_map/ppermute | solution.py:320
  43.9 0.9 %last.1 = bf16[4,64,1024]{2,1,0:T(8,128)(2,1)} custom-call(f32[64,1024]{1,0:T(8,128)S(1)} %halo.7.refs_0_, bf16[256,1024]{1,0:T(8,128)(2,1)S(1)} %get-tuple-element.41.refs_2_.refs_1_, bf16[64,128]{1,0:T(8,128)(2,1)S(1)} %collective-permute-done.14.refs_2_, bf16[64,128]{1,0:T(8,128)(2,1)S(1)} %collective-permute-done.15.refs_3_, ...), custom_call_target="tpu_custom_call", output_to_operand_aliasing={{}: (4, {})} | custom-call | flops 1000000000 | bytes 4194304 | tf_op jit(solution)/shard_map/last/pallas_call | solution.py:241
  (4 shorter events, 0.1 us)
Async XLA Ops:
  0.0 3.9 %copy-start = (bf16[64,1024]{1,0:T(8,128)(2,1)S(1)}, bf16[64,1024]{1,0:T(8,128)(2,1)}, u32[]{:S(2)}) copy-start(bf16[64,1024]{1,0:T(8,128)(2,1)} %refs_4_.1) | copy-start | bytes 393220
  3.3 6.2 %collective-permute-start = (bf16[64,1536]{1,0:T(8,128)(2,1)S(1)}, bf16[64,1536]{1,0:T(8,128)(2,1)S(1)}, u32[]{:S(2)}, u32[]{:S(2)}) collective-permute-start(bf16[64,1536]{1,0:T(8,128)(2,1)S(1)} %get-tuple-element.36), channel_id=1, source_target_pairs={{0,1},{1,0},{2,3},{3,2},{4,5},{5,4},{6,7},{7,6},{8,9},{9,8},{10,11... | collective-permute-start | bytes 589832 | tf_op jit(solution)/shard_map/ppermute | solution.py:307
  3.9 8.4 %collective-permute-start.1 = (bf16[64,1024]{1,0:T(8,128)(2,1)S(1)}, bf16[64,1024]{1,0:T(8,128)(2,1)S(1)}, u32[]{:S(2)}, u32[]{:S(2)}) collective-permute-start(bf16[64,1024]{1,0:T(8,128)(2,1)S(1)} %copy-done), channel_id=1, source_target_pairs={{0,15},{1,2},{2,1},{3,4},{4,3},{5,6},{6,5},{7,8},{8,7},{9,10},{10,... | collective-permute-start | bytes 393224 | tf_op jit(solution)/shard_map/ppermute | solution.py:308
  9.5 4.7 %collective-permute-start.2 = (bf16[64,128]{1,0:T(8,128)(2,1)S(1)}, bf16[64,128]{1,0:T(8,128)(2,1)S(1)}, u32[]{:S(2)}, u32[]{:S(2)}) collective-permute-start(bf16[64,128]{1,0:T(8,128)(2,1)S(1)} %get-tuple-element.39.refs_4_), channel_id=1, source_target_pairs={{0,8},{1,11},{2,10},{3,9},{4,12},{5,15},{6,14},{7,13},{8,0},{9,3},... | collective-permute-start | bytes 49160 | tf_op jit(solution)/shard_map/ppermute | solution.py:320
  9.6 5.0 %collective-permute-start.3 = (bf16[64,128]{1,0:T(8,128)(2,1)S(1)}, bf16[64,128]{1,0:T(8,128)(2,1)S(1)}, u32[]{:S(2)}, u32[]{:S(2)}) collective-permute-start(bf16[64,128]{1,0:T(8,128)(2,1)S(1)} %get-tuple-element.40.refs_5_), channel_id=1, source_target_pairs={{0,9},{1,10},{2,11},{3,8},{4,13},{5,14},{6,15},{7,12},{8,1},{9,2},... | collective-permute-start | bytes 49160 | tf_op jit(solution)/shard_map/ppermute | solution.py:320
  15.3 3.8 %collective-permute-start.4 = (bf16[64,1536]{1,0:T(8,128)(2,1)S(1)}, bf16[64,1536]{1,0:T(8,128)(2,1)S(1)}, u32[]{:S(2)}, u32[]{:S(2)}) collective-permute-start(bf16[64,1536]{1,0:T(8,128)(2,1)S(1)} %get-tuple-element.45), channel_id=1, source_target_pairs={{0,1},{1,0},{2,3},{3,2},{4,5},{5,4},{6,7},{7,6},{8,9},{9,8},{10,11... | collective-permute-start | bytes 589832 | tf_op jit(solution)/shard_map/ppermute | solution.py:307
  15.4 7.3 %collective-permute-start.5 = (bf16[64,1024]{1,0:T(8,128)(2,1)S(1)}, bf16[64,1024]{1,0:T(8,128)(2,1)S(1)}, u32[]{:S(2)}, u32[]{:S(2)}) collective-permute-start(bf16[64,1024]{1,0:T(8,128)(2,1)S(1)} %get-tuple-element.44.refs_1_), channel_id=1, source_target_pairs={{0,15},{1,2},{2,1},{3,4},{4,3},{5,6},{6,5},{7,8},{8,7},{9,10},{10,... | collective-permute-start | bytes 393224 | tf_op jit(solution)/shard_map/ppermute | solution.py:308
  19.1 4.7 %collective-permute-start.6 = (bf16[64,128]{1,0:T(8,128)(2,1)S(1)}, bf16[64,128]{1,0:T(8,128)(2,1)S(1)}, u32[]{:S(2)}, u32[]{:S(2)}) collective-permute-start(bf16[64,128]{1,0:T(8,128)(2,1)S(1)} %get-tuple-element.47.refs_4_), channel_id=1, source_target_pairs={{0,8},{1,11},{2,10},{3,9},{4,12},{5,15},{6,14},{7,13},{8,0},{9,3},... | collective-permute-start | bytes 49160 | tf_op jit(solution)/shard_map/ppermute | solution.py:320
  19.8 5.3 %collective-permute-start.7 = (bf16[64,128]{1,0:T(8,128)(2,1)S(1)}, bf16[64,128]{1,0:T(8,128)(2,1)S(1)}, u32[]{:S(2)}, u32[]{:S(2)}) collective-permute-start(bf16[64,128]{1,0:T(8,128)(2,1)S(1)} %get-tuple-element.48.refs_5_), channel_id=1, source_target_pairs={{0,9},{1,10},{2,11},{3,8},{4,13},{5,14},{6,15},{7,12},{8,1},{9,2},... | collective-permute-start | bytes 49160 | tf_op jit(solution)/shard_map/ppermute | solution.py:320
  25.7 2.7 %collective-permute-start.8 = (bf16[64,1536]{1,0:T(8,128)(2,1)S(1)}, bf16[64,1536]{1,0:T(8,128)(2,1)S(1)}, u32[]{:S(2)}, u32[]{:S(2)}) collective-permute-start(bf16[64,1536]{1,0:T(8,128)(2,1)S(1)} %get-tuple-element.51), channel_id=1, source_target_pairs={{0,1},{1,0},{2,3},{3,2},{4,5},{5,4},{6,7},{7,6},{8,9},{9,8},{10,11... | collective-permute-start | bytes 589832 | tf_op jit(solution)/shard_map/ppermute | solution.py:307
  25.8 7.4 %collective-permute-start.9 = (bf16[64,1024]{1,0:T(8,128)(2,1)S(1)}, bf16[64,1024]{1,0:T(8,128)(2,1)S(1)}, u32[]{:S(2)}, u32[]{:S(2)}) collective-permute-start(bf16[64,1024]{1,0:T(8,128)(2,1)S(1)} %get-tuple-element.50.refs_1_), channel_id=1, source_target_pairs={{0,15},{1,2},{2,1},{3,4},{4,3},{5,6},{6,5},{7,8},{8,7},{9,10},{10,... | collective-permute-start | bytes 393224 | tf_op jit(solution)/shard_map/ppermute | solution.py:308
  28.4 5.3 %collective-permute-start.10 = (bf16[64,128]{1,0:T(8,128)(2,1)S(1)}, bf16[64,128]{1,0:T(8,128)(2,1)S(1)}, u32[]{:S(2)}, u32[]{:S(2)}) collective-permute-start(bf16[64,128]{1,0:T(8,128)(2,1)S(1)} %get-tuple-element.53.refs_4_), channel_id=1, source_target_pairs={{0,8},{1,11},{2,10},{3,9},{4,12},{5,15},{6,14},{7,13},{8,0},{9,3},... | collective-permute-start | bytes 49160 | tf_op jit(solution)/shard_map/ppermute | solution.py:320
  29.3 5.1 %collective-permute-start.11 = (bf16[64,128]{1,0:T(8,128)(2,1)S(1)}, bf16[64,128]{1,0:T(8,128)(2,1)S(1)}, u32[]{:S(2)}, u32[]{:S(2)}) collective-permute-start(bf16[64,128]{1,0:T(8,128)(2,1)S(1)} %get-tuple-element.54.refs_5_), channel_id=1, source_target_pairs={{0,9},{1,10},{2,11},{3,8},{4,13},{5,14},{6,15},{7,12},{8,1},{9,2},... | collective-permute-start | bytes 49160 | tf_op jit(solution)/shard_map/ppermute | solution.py:320
  35.1 2.9 %collective-permute-start.12 = (bf16[64,1536]{1,0:T(8,128)(2,1)S(1)}, bf16[64,1536]{1,0:T(8,128)(2,1)S(1)}, u32[]{:S(2)}, u32[]{:S(2)}) collective-permute-start(bf16[64,1536]{1,0:T(8,128)(2,1)S(1)} %get-tuple-element.58), channel_id=1, source_target_pairs={{0,1},{1,0},{2,3},{3,2},{4,5},{5,4},{6,7},{7,6},{8,9},{9,8},{10,11... | collective-permute-start | bytes 589832 | tf_op jit(solution)/shard_map/ppermute | solution.py:307
  35.2 7.4 %collective-permute-start.13 = (bf16[64,1024]{1,0:T(8,128)(2,1)S(1)}, bf16[64,1024]{1,0:T(8,128)(2,1)S(1)}, u32[]{:S(2)}, u32[]{:S(2)}) collective-permute-start(bf16[64,1024]{1,0:T(8,128)(2,1)S(1)} %get-tuple-element.57.refs_1_), channel_id=1, source_target_pairs={{0,15},{1,2},{2,1},{3,4},{4,3},{5,6},{6,5},{7,8},{8,7},{9,10},{10,... | collective-permute-start | bytes 393224 | tf_op jit(solution)/shard_map/ppermute | solution.py:308
  38.0 5.2 %collective-permute-start.14 = (bf16[64,128]{1,0:T(8,128)(2,1)S(1)}, bf16[64,128]{1,0:T(8,128)(2,1)S(1)}, u32[]{:S(2)}, u32[]{:S(2)}) collective-permute-start(bf16[64,128]{1,0:T(8,128)(2,1)S(1)} %get-tuple-element.60.refs_4_), channel_id=1, source_target_pairs={{0,8},{1,11},{2,10},{3,9},{4,12},{5,15},{6,14},{7,13},{8,0},{9,3},... | collective-permute-start | bytes 49160 | tf_op jit(solution)/shard_map/ppermute | solution.py:320
  38.7 5.3 %collective-permute-start.15 = (bf16[64,128]{1,0:T(8,128)(2,1)S(1)}, bf16[64,128]{1,0:T(8,128)(2,1)S(1)}, u32[]{:S(2)}, u32[]{:S(2)}) collective-permute-start(bf16[64,128]{1,0:T(8,128)(2,1)S(1)} %get-tuple-element.61.refs_5_), channel_id=1, source_target_pairs={{0,9},{1,10},{2,11},{3,8},{4,13},{5,14},{6,15},{7,12},{8,1},{9,2},... | collective-permute-start | bytes 49160 | tf_op jit(solution)/shard_map/ppermute | solution.py:320

commit v10 on v8

--- a/solution.py
+++ b/solution.py
@@ -135,8 +135,8 @@
 
 def prepare_kernel(plan, index_ref, *refs):
     sources, refs = refs[:7], refs[7:]
-    x_ref, g_ref, cb_ref, order_ref = refs[:4]
-    sends, (near_ref, offsets_ref, rows_ref, cols_ref, col_ref, coup_ref, sems) = refs[4:-7], refs[-7:]
+    x_ref, d_ref, g_ref, cb_ref, near_ref, offsets_ref = refs[:6]
+    sends, (rows_ref, cols_ref, col_ref, coup_ref, sems) = refs[6:-5], refs[-5:]
     targets = (near_ref, offsets_ref, rows_ref, cols_ref, x_ref, col_ref, coup_ref)
     copies = [
         pltpu.make_async_copy(source, target, sems.at[i])
@@ -147,17 +147,10 @@
     rank, size = plan.rank, plan.size
     cb_ref[...] = jnp.zeros_like(cb_ref)
     g_ref[...] = jnp.zeros_like(g_ref)
+    for cell in range(plan.cells):
+        d_ref[cell] = jnp.zeros(d_ref.shape[1:], d_ref.dtype)
     for copy in copies:
         copy.wait()
-    first, last = jnp.int32(0), jnp.int32(plan.tiles - 1)
-    for s in range(plan.tiles):
-        place = near_ref[s] + offsets_ref[s]
-        own = jnp.logical_and(place >= 0, place < plan.per_device).astype(jnp.int32)
-        where = jnp.where(own == 1, first, last)
-        order_ref[where] = s
-        order_ref[plan.tiles + where] = near_ref[s] * SPAN + offsets_ref[s] + REACH
-        first, last = first + own, last - (1 - own)
-    order_ref[2 * plan.tiles] = first
     for c in range(plan.per_device):
         cb_ref[c * rank : (c + 1) * rank, c * size : (c + 1) * size] = col_ref[c]
     column = lax.broadcasted_iota(jnp.int32, (rank, plan.width), 1) // rank
@@ -179,46 +172,24 @@
 
 
 def first_own_kernel(plan, *refs):
-    index_ref, order_ref, x_ref, near_ref, row_hbm, tiles_hbm = refs[:6]
-    acc_ref, d_ref, rb_ref, row_ref, empty, sem, tile_sems = refs[-7:]
+    index_ref, rows_ref, offsets_ref, x_ref, near_ref, row_hbm, tiles_hbm = refs[:7]
+    acc_ref, d_ref, rb_ref, row_ref, sem, tile_sems = refs[-6:]
     rank, size = plan.rank, plan.size
-
-    def tile_copy(place):
-        source, cell = order_ref[place], order_ref[plan.tiles + place]
-        return pltpu.make_async_copy(tiles_hbm.at[source], d_ref.at[cell], tile_sems.at[place])
-
-    def wait_for(first, last):
-        @pl.loop(first, last)
-        def _(place):
-            tile_copy(place).wait()
-
-    for place in range(plan.tiles):
-        tile_copy(place).start()
+    copies = []
+    for s in range(plan.tiles):
+        cell = rows_ref[s] * SPAN + offsets_ref[s] + REACH
+        copies.append(pltpu.make_async_copy(tiles_hbm.at[s], d_ref.at[cell], tile_sems.at[s]))
+        copies[-1].start()
     copy = pltpu.make_async_copy(row_hbm, row_ref, sem)
     copy.start()
-    for cell in range(plan.cells):
-        empty[cell] = 1
-    for place in range(plan.tiles):
-        empty[order_ref[plan.tiles + place]] = 0
-    count = jnp.int32(0)
-    for cell in range(plan.cells):
-        missing = empty[cell]
-        empty[plan.cells + count] = cell
-        count = count + missing
-
-    @pl.loop(0, count)
-    def _(place):
-        d_ref[empty[plan.cells + place]] = jnp.zeros(d_ref.shape[1:], d_ref.dtype)
-
     rb_ref[...] = jnp.zeros_like(rb_ref)
     copy.wait()
     for c in range(plan.per_device):
         for start in (c * rank, plan.width + c * rank):
             rb_ref[start : start + rank, c * size : (c + 1) * size] = row_ref[c]
-    own = order_ref[2 * plan.tiles]
-    wait_for(0, own)
+    for copy in copies:
+        copy.wait()
     plan.near_sums(x_ref, d_ref, acc_ref, 0)
-    wait_for(own, plan.tiles)
     plan.halo_sums(lax.rem(index_ref[0], 2) == 1, near_ref, d_ref, acc_ref, acc_ref)
 
 
@@ -310,20 +281,21 @@
     for product in range(PRODUCTS):
         if product == 0:
             ins = [near_rows, near_offsets, far_rows, far_cols, block, col_basis, couplings]
-            current, coupled, col_wide, order, *sends = call(
+            current, dense, coupled, col_wide, row_slots, offset_slots, *sends = call(
                 functools.partial(prepare_kernel, plan),
                 "prepare",
                 [index, *ins],
                 [IN_SMEM] + [IN_HBM] * 7,
                 [
                     block_out,
+                    pltpu.VMEM((plan.cells, plan.size, plan.size), BF16),
                     pltpu.VMEM((LEVELS, plan.members * width, width), BF16),
                     pltpu.VMEM((width, shard_len), BF16),
-                    pltpu.SMEM((2 * plan.tiles + 1,), jnp.int32),
+                    *scratch_for(near_rows, near_offsets),
                     *sends_out,
                 ],
-                [IN_VMEM] * 3 + [IN_SMEM] + [IN_VMEM] * len(sends_out),
-                scratch=scratch_for(near_rows, near_offsets, far_rows, far_cols, col_basis, couplings)
+                [IN_VMEM] * 4 + [IN_SMEM] * 2 + [IN_VMEM] * len(sends_out),
+                scratch=scratch_for(far_rows, far_cols, col_basis, couplings)
                 + [pltpu.SemaphoreType.DMA((7,))],
             )
         near = lax.ppermute(sends[0] if plan.paired else current, axes, plan.near)
@@ -342,22 +314,20 @@
         fars = [lax.ppermute(s, axes, route) for s, route in zip(sends, routes)]
         after = sends if plan.paired else []
         if product == 0:
+            ins = [index, row_slots, offset_slots, current, near, row_basis, near_tiles, dense, *after]
             acc, dense, row_wide = call(
                 functools.partial(first_own_kernel, plan),
                 "first_own",
-                [index, order, current, near, row_basis, near_tiles, *after],
-                [IN_SMEM] * 2 + [IN_VMEM] * 2 + [IN_HBM] * 2 + [ANYWHERE] * len(after),
+                ins,
+                [IN_SMEM] * 3 + [IN_VMEM] * 2 + [IN_HBM] * 2 + [IN_VMEM] + [ANYWHERE] * len(after),
                 [
                     acc_out,
                     pltpu.VMEM((plan.cells, plan.size, plan.size), BF16),
                     pltpu.VMEM((2 * width, shard_len), BF16),
                 ],
                 scratch=scratch_for(row_basis)
-                + [
-                    pltpu.SMEM((2 * plan.cells + 1,), jnp.int32),
-                    pltpu.SemaphoreType.DMA,
-                    pltpu.SemaphoreType.DMA((plan.tiles,)),
-                ],
+                + [pltpu.SemaphoreType.DMA, pltpu.SemaphoreType.DMA((plan.tiles,))],
+                aliases={7: 1},
             )
         else:
             ins = [index, current, near, dense, *after] + ([krylov] if product > 1 else [])

time: 43.7 us -> 43.8 us (level)
  waiting for transfers between devices: 5.1 us -> 5.89 us
  starting transfers between devices: 23.4 us -> 22.7 us
    ppermute x8, starting transfers between devices: 7.74 us -> 6.88 us  [on_device(): fars = [lax.ppermute(s, axes, route) for s, route in zip(sends, routes)]]
    ppermute x4, starting transfers between devices: 14.3 us -> 14.9 us  [on_device(): over = lax.ppermute(block if product == 0 else current, axes, plan.over)]
where the time goes in v10:
time: 43.8 us; the launch traced here: 43.7 us
  starting transfers between devices  22.7 us (52%)
  Pallas kernels  14.9 us (34%)
  waiting for transfers between devices  5.89 us (13%)
    pallas_call x17, Pallas kernels, call(): pl.pallas_call(kernel, in_specs=list(specs), out_specs=out_specs or [IN_V...  14.9 us
    ppermute x4, starting transfers between devices, on_device(): over = lax.ppermute(block if product == 0 else current, axes, plan.over)  14.9 us
    ppermute x8, starting transfers between devices, on_device(): fars = [lax.ppermute(s, axes, route) for s, route in zip(sends, routes)]  6.88 us
    ppermute x4, waiting for transfers between devices, on_device(): over = lax.ppermute(block if product == 0 else current, axes, plan.over)  3.28 us
    ppermute x8, waiting for transfers between devices, on_device(): fars = [lax.ppermute(s, axes, route) for s, route in zip(sends, routes)]  2.61 us
    ppermute x4, starting transfers between devices, on_device(): near = lax.ppermute(sends[0] if plan.paired else current, axes, plan.near)  0.96 us
  transfers between devices with their start and end apart: 16, of which 6 were waited for; matrix products, arithmetic and copies ran while one was open for 0% of the time, Pallas kernels for 23%

profile of v10, /device:TPU:0, one launch (start us, length us, event | category | flops | bytes accessed | tf_op | source)
XLA Modules:
  0.0 43.7 jit_solution(13140513326527507750)
XLA Ops:
  0.0 2.1 %prepare.1 = (bf16[64,1024]{1,0:T(8,128)(2,1)S(1)}, bf16[36,256,256]{2,1,0:T(8,128)(2,1)S(1)}, bf16[3,512,128]{2,1,0:T(8,128)(2,1)S(1)}, bf16[128,1024]{1,0:T(8,...) custom-call(s32[1]{0:T(128)} %bitcast.index_ref.refs_0_, ...), custom_call_target="tpu_custom_call" | custom-call | flops 1000000000 | bytes 4194304 | tf_op jit(solution)/shard_map/prepare/pallas_call | solution.py:240
  2.2 0.5 %collective-permute-start = (bf16[64,1536]{1,0:T(8,128)(2,1)S(1)}, bf16[64,1536]{1,0:T(8,128)(2,1)S(1)}, u32[]{:S(2)}, u32[]{:S(2)}) collective-permute-start(bf16[64,1536]{1,0:T(8,128)(2,1)S(1)} %get-tuple-element.42), channel_id=1, source_target_pairs={{0,1},{1,0},{2,3},{3,2},{4,5},{5,4},{6,7},{7,6},{8,9},{9,8},{10,11... | collective-permute-start | bytes 589832 | tf_op jit(solution)/shard_map/ppermute | solution.py:301
  2.7 5.6 %collective-permute-start.1 = (bf16[64,1024]{1,0:T(8,128)(2,1)}, bf16[64,1024]{1,0:T(8,128)(2,1)S(1)}, u32[]{:S(2)}, u32[]{:S(2)}) collective-permute-start(bf16[64,1024]{1,0:T(8,128)(2,1)} %refs_4_.1), channel_id=1, source_target_pairs={{0,15},{1,2},{2,1},{3,4},{4,3},{5,6},{6,5},{7,8},{8,7},{9,10},{10,... | collective-permute-start | bytes 393224 | tf_op jit(solution)/shard_map/ppermute | solution.py:302
  8.3 0.0 collective-permute-done.message_ref.refs_4_
  8.3 0.1 collective-permute-start.2
  8.4 0.3 collective-permute-start.3
  8.7 3.8 %first_own.1 = (f32[64,1024]{1,0:T(8,128)S(1)}, bf16[36,256,256]{2,1,0:T(8,128)(2,1)S(1)}, bf16[256,1024]{1,0:T(8,128)(2,1)S(1)}) custom-call(s32[1]{0:T(128)} %bitcast.index_ref.refs_0_, s32[32]{0:T(128)S(4)} %get-tuple-element.39.refs_1_, s32[32]{0:T(128)S(4)} %get-tuple-element.40.refs_2_, ...), custom_call_target="tpu_custom_call", output_to_operand_aliasing={{1}: (7, {})} | custom-call | flops 1000000000 | bytes 4194304 | tf_op jit(solution)/shard_map/first_own/pallas_call | solution.py:240
  12.5 0.0 collective-permute-done.1.over_ref
  12.5 0.5 %halo.4.refs_1_ = f32[64,1024]{1,0:T(8,128)S(1)} custom-call(s32[1]{0:T(128)} %bitcast.index_ref.refs_0_, f32[64,1024]{1,0:T(8,128)S(1)} %get-tuple-element.47.acc_ref, bf16[64,1024]{1,0:T(8,128)(2,1)S(1)} %collective-permute-done.1.over_ref, bf16[36,256,256]{2,1,0:T(8,128)(2,1)S(1)} %get-tuple-element.48.d_ref.refs_3_), custom_call_target="tpu_custom_call" | custom-call | flops 1000000000 | bytes 4194304 | tf_op jit(solution)/shard_map/halo/pallas_call | solution.py:240
  13.1 0.0 collective-permute-done.2.refs_5_
  13.1 0.4 collective-permute-done.3.refs_6_
  13.4 0.7 %finish.3 = (bf16[64,1024]{1,0:T(8,128)(2,1)S(1)}, bf16[64,1536]{1,0:T(8,128)(2,1)S(1)}, f32[64,256]{1,0:T(8,128)S(1)}) custom-call(s32[1]{0:T(128)} %bitcast.index_ref.refs_0_, f32[64,1024]{1,0:T(8,128)S(1)} %halo.4.refs_1_, bf16[256,1024]{1,0:T(8,128)(2,1)S(1)} %get-tuple-element.49.refs_2_.refs_1_, bf16[128,1024]{1,0:T(8,128)(2,1)S(1)} %get-tuple-element.50.refs_3_, ...), custom_call_target="tpu_custom_call" | custom-call | flops 1000000000 | bytes 4194304 | tf_op jit(solution)/shard_map/finish/pallas_call | solution.py:240
  14.1 0.2 collective-permute-start.4
  14.3 3.6 %collective-permute-start.5 = (bf16[64,1024]{1,0:T(8,128)(2,1)S(1)}, bf16[64,1024]{1,0:T(8,128)(2,1)S(1)}, u32[]{:S(2)}, u32[]{:S(2)}) collective-permute-start(bf16[64,1024]{1,0:T(8,128)(2,1)S(1)} %get-tuple-element.52.refs_1_), channel_id=1, source_target_pairs={{0,15},{1,2},{2,1},{3,4},{4,3},{5,6},{6,5},{7,8},{8,7},{9,10},{10,... | collective-permute-start | bytes 393224 | tf_op jit(solution)/shard_map/ppermute | solution.py:302
  17.9 0.0 collective-permute-done.4.message_ref.refs_2_
  17.9 0.7 %collective-permute-start.6 = (bf16[64,128]{1,0:T(8,128)(2,1)S(1)}, bf16[64,128]{1,0:T(8,128)(2,1)S(1)}, u32[]{:S(2)}, u32[]{:S(2)}) collective-permute-start(bf16[64,128]{1,0:T(8,128)(2,1)S(1)} %get-tuple-element.55.refs_4_), channel_id=1, source_target_pairs={{0,8},{1,11},{2,10},{3,9},{4,12},{5,15},{6,14},{7,13},{8,0},{9,3},... | collective-permute-start | bytes 49160 | tf_op jit(solution)/shard_map/ppermute | solution.py:314
  18.6 2.7 %collective-permute-start.7 = (bf16[64,128]{1,0:T(8,128)(2,1)S(1)}, bf16[64,128]{1,0:T(8,128)(2,1)S(1)}, u32[]{:S(2)}, u32[]{:S(2)}) collective-permute-start(bf16[64,128]{1,0:T(8,128)(2,1)S(1)} %get-tuple-element.56.refs_5_), channel_id=1, source_target_pairs={{0,9},{1,10},{2,11},{3,8},{4,13},{5,14},{6,15},{7,12},{8,1},{9,2},... | collective-permute-start | bytes 49160 | tf_op jit(solution)/shard_map/ppermute | solution.py:314
  21.2 1.3 %own.3 = (f32[64,1024]{1,0:T(8,128)S(1)}, bf16[4,64,1024]{2,1,0:T(8,128)(2,1)}) custom-call(s32[1]{0:T(128)} %bitcast.index_ref.refs_0_, bf16[64,1024]{1,0:T(8,128)(2,1)S(1)} %get-tuple-element.52.refs_1_, bf16[64,1536]{1,0:T(8,128)(2,1)S(1)} %collective-permute-done.4.message_ref.refs_2_, bf16[36,256,256]{2,1,0:T(8,128)(2,1)S(1)} %get-tuple-element.48.d_ref.refs_3_, ...), custom_call_target="tpu_custom_call" | custom-call | flops 1000000000 | bytes 4194304 | tf_op jit(solution)/shard_map/own/pallas_call | solution.py:240
  22.5 0.0 collective-permute-done.5.over_ref
  22.5 0.5 %halo.5.refs_1_ = f32[64,1024]{1,0:T(8,128)S(1)} custom-call(s32[1]{0:T(128)} %bitcast.index_ref.refs_0_, f32[64,1024]{1,0:T(8,128)S(1)} %get-tuple-element.57.acc_ref, bf16[64,1024]{1,0:T(8,128)(2,1)S(1)} %collective-permute-done.5.over_ref, bf16[36,256,256]{2,1,0:T(8,128)(2,1)S(1)} %get-tuple-element.48.d_ref.refs_3_), custom_call_target="tpu_custom_call" | custom-call | flops 1000000000 | bytes 4194304 | tf_op jit(solution)/shard_map/halo/pallas_call | solution.py:240
  23.1 0.0 collective-permute-done.6.refs_5_
  23.1 0.6 %collective-permute-done.7.refs_6_ = bf16[64,128]{1,0:T(8,128)(2,1)S(1)} collective-permute-done((bf16[64,128]{1,0:T(8,128)(2,1)S(1)}, bf16[64,128]{1,0:T(8,128)(2,1)S(1)}, u32[]{:S(2)}, u32[]{:S(2)}) %collective-permute-start.7) | collective-permute-done | bytes 16416 | tf_op jit(solution)/shard_map/ppermute | solution.py:314
  23.7 0.7 %finish.4 = (bf16[64,1024]{1,0:T(8,128)(2,1)S(1)}, bf16[64,1536]{1,0:T(8,128)(2,1)S(1)}, f32[64,256]{1,0:T(8,128)S(1)}) custom-call(s32[1]{0:T(128)} %bitcast.index_ref.refs_0_, f32[64,1024]{1,0:T(8,128)S(1)} %halo.5.refs_1_, bf16[256,1024]{1,0:T(8,128)(2,1)S(1)} %get-tuple-element.49.refs_2_.refs_1_, bf16[128,1024]{1,0:T(8,128)(2,1)S(1)} %get-tuple-element.50.refs_3_, ...), custom_call_target="tpu_custom_call" | custom-call | flops 1000000000 | bytes 4194304 | tf_op jit(solution)/shard_map/finish/pallas_call | solution.py:240
  24.4 0.2 collective-permute-start.8
  24.5 2.6 %collective-permute-start.9 = (bf16[64,1024]{1,0:T(8,128)(2,1)S(1)}, bf16[64,1024]{1,0:T(8,128)(2,1)S(1)}, u32[]{:S(2)}, u32[]{:S(2)}) collective-permute-start(bf16[64,1024]{1,0:T(8,128)(2,1)S(1)} %get-tuple-element.58.refs_1_), channel_id=1, source_target_pairs={{0,15},{1,2},{2,1},{3,4},{4,3},{5,6},{6,5},{7,8},{8,7},{9,10},{10,... | collective-permute-start | bytes 393224 | tf_op jit(solution)/shard_map/ppermute | solution.py:302
  27.2 0.0 collective-permute-done.8.message_ref.refs_2_
  27.2 1.0 %collective-permute-start.10 = (bf16[64,128]{1,0:T(8,128)(2,1)S(1)}, bf16[64,128]{1,0:T(8,128)(2,1)S(1)}, u32[]{:S(2)}, u32[]{:S(2)}) collective-permute-start(bf16[64,128]{1,0:T(8,128)(2,1)S(1)} %get-tuple-element.61.refs_4_), channel_id=1, source_target_pairs={{0,8},{1,11},{2,10},{3,9},{4,12},{5,15},{6,14},{7,13},{8,0},{9,3},... | collective-permute-start | bytes 49160 | tf_op jit(solution)/shard_map/ppermute | solution.py:314
  28.2 0.6 %collective-permute-start.11 = (bf16[64,128]{1,0:T(8,128)(2,1)S(1)}, bf16[64,128]{1,0:T(8,128)(2,1)S(1)}, u32[]{:S(2)}, u32[]{:S(2)}) collective-permute-start(bf16[64,128]{1,0:T(8,128)(2,1)S(1)} %get-tuple-element.62.refs_5_), channel_id=1, source_target_pairs={{0,9},{1,10},{2,11},{3,8},{4,13},{5,14},{6,15},{7,12},{8,1},{9,2},... | collective-permute-start | bytes 49160 | tf_op jit(solution)/shard_map/ppermute | solution.py:314
  28.7 1.3 %own.4 = (f32[64,1024]{1,0:T(8,128)S(1)}, bf16[4,64,1024]{2,1,0:T(8,128)(2,1)}) custom-call(s32[1]{0:T(128)} %bitcast.index_ref.refs_0_, bf16[64,1024]{1,0:T(8,128)(2,1)S(1)} %get-tuple-element.58.refs_1_, bf16[64,1536]{1,0:T(8,128)(2,1)S(1)} %collective-permute-done.8.message_ref.refs_2_, ...), custom_call_target="tpu_custom_call", output_to_operand_aliasing={{1}: (6, {})} | custom-call | flops 1000000000 | bytes 4194304 | tf_op jit(solution)/shard_map/own/pallas_call | solution.py:240
  30.0 1.9 %collective-permute-done.9.over_ref = bf16[64,1024]{1,0:T(8,128)(2,1)S(1)} collective-permute-done((bf16[64,1024]{1,0:T(8,128)(2,1)S(1)}, bf16[64,1024]{1,0:T(8,128)(2,1)S(1)}, u32[]{:S(2)}, u32[]{:S(2)}) %collective-permute-start.9) | collective-permute-done | bytes 131104 | tf_op jit(solution)/shard_map/ppermute | solution.py:302
  31.9 0.5 %halo.6.refs_1_ = f32[64,1024]{1,0:T(8,128)S(1)} custom-call(s32[1]{0:T(128)} %bitcast.index_ref.refs_0_, f32[64,1024]{1,0:T(8,128)S(1)} %get-tuple-element.64.acc_ref, bf16[64,1024]{1,0:T(8,128)(2,1)S(1)} %collective-permute-done.9.over_ref, bf16[36,256,256]{2,1,0:T(8,128)(2,1)S(1)} %get-tuple-element.48.d_ref.refs_3_), custom_call_target="tpu_custom_call" | custom-call | flops 1000000000 | bytes 4194304 | tf_op jit(solution)/shard_map/halo/pallas_call | solution.py:240
  32.4 0.0 collective-permute-done.10.refs_5_
  32.4 0.9 %collective-permute-done.11.refs_6_ = bf16[64,128]{1,0:T(8,128)(2,1)S(1)} collective-permute-done((bf16[64,128]{1,0:T(8,128)(2,1)S(1)}, bf16[64,128]{1,0:T(8,128)(2,1)S(1)}, u32[]{:S(2)}, u32[]{:S(2)}) %collective-permute-start.11) | collective-permute-done | bytes 16416 | tf_op jit(solution)/shard_map/ppermute | solution.py:314
  33.3 0.7 %finish.5 = (bf16[64,1024]{1,0:T(8,128)(2,1)S(1)}, bf16[64,1536]{1,0:T(8,128)(2,1)S(1)}, f32[64,256]{1,0:T(8,128)S(1)}) custom-call(s32[1]{0:T(128)} %bitcast.index_ref.refs_0_, f32[64,1024]{1,0:T(8,128)S(1)} %halo.6.refs_1_, bf16[256,1024]{1,0:T(8,128)(2,1)S(1)} %get-tuple-element.49.refs_2_.refs_1_, bf16[128,1024]{1,0:T(8,128)(2,1)S(1)} %get-tuple-element.50.refs_3_, ...), custom_call_target="tpu_custom_call" | custom-call | flops 1000000000 | bytes 4194304 | tf_op jit(solution)/shard_map/finish/pallas_call | solution.py:240
  34.0 0.1 collective-permute-start.12
  34.1 3.0 %collective-permute-start.13 = (bf16[64,1024]{1,0:T(8,128)(2,1)S(1)}, bf16[64,1024]{1,0:T(8,128)(2,1)S(1)}, u32[]{:S(2)}, u32[]{:S(2)}) collective-permute-start(bf16[64,1024]{1,0:T(8,128)(2,1)S(1)} %get-tuple-element.65.refs_1_), channel_id=1, source_target_pairs={{0,15},{1,2},{2,1},{3,4},{4,3},{5,6},{6,5},{7,8},{8,7},{9,10},{10,... | collective-permute-start | bytes 393224 | tf_op jit(solution)/shard_map/ppermute | solution.py:302
  37.1 0.0 collective-permute-done.12.message_ref.refs_2_
  37.1 0.3 collective-permute-start.14
  37.4 1.4 %collective-permute-start.15 = (bf16[64,128]{1,0:T(8,128)(2,1)S(1)}, bf16[64,128]{1,0:T(8,128)(2,1)S(1)}, u32[]{:S(2)}, u32[]{:S(2)}) collective-permute-start(bf16[64,128]{1,0:T(8,128)(2,1)S(1)} %get-tuple-element.69.refs_5_), channel_id=1, source_target_pairs={{0,9},{1,10},{2,11},{3,8},{4,13},{5,14},{6,15},{7,12},{8,1},{9,2},... | collective-permute-start | bytes 49160 | tf_op jit(solution)/shard_map/ppermute | solution.py:314
  38.8 1.3 %own.5 = (f32[64,1024]{1,0:T(8,128)S(1)}, bf16[4,64,1024]{2,1,0:T(8,128)(2,1)}) custom-call(s32[1]{0:T(128)} %bitcast.index_ref.refs_0_, bf16[64,1024]{1,0:T(8,128)(2,1)S(1)} %get-tuple-element.65.refs_1_, bf16[64,1536]{1,0:T(8,128)(2,1)S(1)} %collective-permute-done.12.message_ref.refs_2_, ...), custom_call_target="tpu_custom_call", output_to_operand_aliasing={{1}: (6, {})} | custom-call | flops 1000000000 | bytes 4194304 | tf_op jit(solution)/shard_map/own/pallas_call | solution.py:240
  40.1 1.4 %collective-permute-done.13.over_ref = bf16[64,1024]{1,0:T(8,128)(2,1)S(1)} collective-permute-done((bf16[64,1024]{1,0:T(8,128)(2,1)S(1)}, bf16[64,1024]{1,0:T(8,128)(2,1)S(1)}, u32[]{:S(2)}, u32[]{:S(2)}) %collective-permute-start.13) | collective-permute-done | bytes 131104 | tf_op jit(solution)/shard_map/ppermute | solution.py:302
  41.5 0.5 %halo.7.refs_0_ = f32[64,1024]{1,0:T(8,128)S(1)} custom-call(s32[1]{0:T(128)} %bitcast.index_ref.refs_0_, f32[64,1024]{1,0:T(8,128)S(1)} %get-tuple-element.71.acc_ref, bf16[64,1024]{1,0:T(8,128)(2,1)S(1)} %collective-permute-done.13.over_ref, bf16[36,256,256]{2,1,0:T(8,128)(2,1)S(1)} %get-tuple-element.48.d_ref.refs_3_), custom_call_target="tpu_custom_call" | custom-call | flops 1000000000 | bytes 4194304 | tf_op jit(solution)/shard_map/halo/pallas_call | solution.py:240
  42.0 0.0 collective-permute-done.14.refs_2_
  42.0 0.8 %collective-permute-done.15.refs_3_ = bf16[64,128]{1,0:T(8,128)(2,1)S(1)} collective-permute-done((bf16[64,128]{1,0:T(8,128)(2,1)S(1)}, bf16[64,128]{1,0:T(8,128)(2,1)S(1)}, u32[]{:S(2)}, u32[]{:S(2)}) %collective-permute-start.15) | collective-permute-done | bytes 16416 | tf_op jit(solution)/shard_map/ppermute | solution.py:314
  42.8 0.9 %last.1 = bf16[4,64,1024]{2,1,0:T(8,128)(2,1)} custom-call(f32[64,1024]{1,0:T(8,128)S(1)} %halo.7.refs_0_, bf16[256,1024]{1,0:T(8,128)(2,1)S(1)} %get-tuple-element.49.refs_2_.refs_1_, bf16[64,128]{1,0:T(8,128)(2,1)S(1)} %collective-permute-done.14.refs_2_, bf16[64,128]{1,0:T(8,128)(2,1)S(1)} %collective-permute-done.15.refs_3_, ...), custom_call_target="tpu_custom_call", output_to_operand_aliasing={{}: (4, {})} | custom-call | flops 1000000000 | bytes 4194304 | tf_op jit(solution)/shard_map/last/pallas_call | solution.py:240
  (4 shorter events, 0.1 us)
Async XLA Ops:
  2.2 6.2 %collective-permute-start = (bf16[64,1536]{1,0:T(8,128)(2,1)S(1)}, bf16[64,1536]{1,0:T(8,128)(2,1)S(1)}, u32[]{:S(2)}, u32[]{:S(2)}) collective-permute-start(bf16[64,1536]{1,0:T(8,128)(2,1)S(1)} %get-tuple-element.42), channel_id=1, source_target_pairs={{0,1},{1,0},{2,3},{3,2},{4,5},{5,4},{6,7},{7,6},{8,9},{9,8},{10,11... | collective-permute-start | bytes 589832 | tf_op jit(solution)/shard_map/ppermute | solution.py:301
  2.7 9.9 %collective-permute-start.1 = (bf16[64,1024]{1,0:T(8,128)(2,1)}, bf16[64,1024]{1,0:T(8,128)(2,1)S(1)}, u32[]{:S(2)}, u32[]{:S(2)}) collective-permute-start(bf16[64,1024]{1,0:T(8,128)(2,1)} %refs_4_.1), channel_id=1, source_target_pairs={{0,15},{1,2},{2,1},{3,4},{4,3},{5,6},{6,5},{7,8},{8,7},{9,10},{10,... | collective-permute-start | bytes 393224 | tf_op jit(solution)/shard_map/ppermute | solution.py:302
  8.3 4.7 %collective-permute-start.2 = (bf16[64,128]{1,0:T(8,128)(2,1)S(1)}, bf16[64,128]{1,0:T(8,128)(2,1)S(1)}, u32[]{:S(2)}, u32[]{:S(2)}) collective-permute-start(bf16[64,128]{1,0:T(8,128)(2,1)S(1)} %get-tuple-element.45.refs_8_), channel_id=1, source_target_pairs={{0,8},{1,11},{2,10},{3,9},{4,12},{5,15},{6,14},{7,13},{8,0},{9,3},... | collective-permute-start | bytes 49160 | tf_op jit(solution)/shard_map/ppermute | solution.py:314
  8.4 5.0 %collective-permute-start.3 = (bf16[64,128]{1,0:T(8,128)(2,1)S(1)}, bf16[64,128]{1,0:T(8,128)(2,1)S(1)}, u32[]{:S(2)}, u32[]{:S(2)}) collective-permute-start(bf16[64,128]{1,0:T(8,128)(2,1)S(1)} %get-tuple-element.46.refs_9_), channel_id=1, source_target_pairs={{0,9},{1,10},{2,11},{3,8},{4,13},{5,14},{6,15},{7,12},{8,1},{9,2},... | collective-permute-start | bytes 49160 | tf_op jit(solution)/shard_map/ppermute | solution.py:314
  14.1 3.8 %collective-permute-start.4 = (bf16[64,1536]{1,0:T(8,128)(2,1)S(1)}, bf16[64,1536]{1,0:T(8,128)(2,1)S(1)}, u32[]{:S(2)}, u32[]{:S(2)}) collective-permute-start(bf16[64,1536]{1,0:T(8,128)(2,1)S(1)} %get-tuple-element.53), channel_id=1, source_target_pairs={{0,1},{1,0},{2,3},{3,2},{4,5},{5,4},{6,7},{7,6},{8,9},{9,8},{10,11... | collective-permute-start | bytes 589832 | tf_op jit(solution)/shard_map/ppermute | solution.py:301
  14.3 8.2 %collective-permute-start.5 = (bf16[64,1024]{1,0:T(8,128)(2,1)S(1)}, bf16[64,1024]{1,0:T(8,128)(2,1)S(1)}, u32[]{:S(2)}, u32[]{:S(2)}) collective-permute-start(bf16[64,1024]{1,0:T(8,128)(2,1)S(1)} %get-tuple-element.52.refs_1_), channel_id=1, source_target_pairs={{0,15},{1,2},{2,1},{3,4},{4,3},{5,6},{6,5},{7,8},{8,7},{9,10},{10,... | collective-permute-start | bytes 393224 | tf_op jit(solution)/shard_map/ppermute | solution.py:302
  17.9 5.1 %collective-permute-start.6 = (bf16[64,128]{1,0:T(8,128)(2,1)S(1)}, bf16[64,128]{1,0:T(8,128)(2,1)S(1)}, u32[]{:S(2)}, u32[]{:S(2)}) collective-permute-start(bf16[64,128]{1,0:T(8,128)(2,1)S(1)} %get-tuple-element.55.refs_4_), channel_id=1, source_target_pairs={{0,8},{1,11},{2,10},{3,9},{4,12},{5,15},{6,14},{7,13},{8,0},{9,3},... | collective-permute-start | bytes 49160 | tf_op jit(solution)/shard_map/ppermute | solution.py:314
  18.6 5.1 %collective-permute-start.7 = (bf16[64,128]{1,0:T(8,128)(2,1)S(1)}, bf16[64,128]{1,0:T(8,128)(2,1)S(1)}, u32[]{:S(2)}, u32[]{:S(2)}) collective-permute-start(bf16[64,128]{1,0:T(8,128)(2,1)S(1)} %get-tuple-element.56.refs_5_), channel_id=1, source_target_pairs={{0,9},{1,10},{2,11},{3,8},{4,13},{5,14},{6,15},{7,12},{8,1},{9,2},... | collective-permute-start | bytes 49160 | tf_op jit(solution)/shard_map/ppermute | solution.py:314
  24.4 2.8 %collective-permute-start.8 = (bf16[64,1536]{1,0:T(8,128)(2,1)S(1)}, bf16[64,1536]{1,0:T(8,128)(2,1)S(1)}, u32[]{:S(2)}, u32[]{:S(2)}) collective-permute-start(bf16[64,1536]{1,0:T(8,128)(2,1)S(1)} %get-tuple-element.59), channel_id=1, source_target_pairs={{0,1},{1,0},{2,3},{3,2},{4,5},{5,4},{6,7},{7,6},{8,9},{9,8},{10,11... | collective-permute-start | bytes 589832 | tf_op jit(solution)/shard_map/ppermute | solution.py:301
  24.5 7.4 %collective-permute-start.9 = (bf16[64,1024]{1,0:T(8,128)(2,1)S(1)}, bf16[64,1024]{1,0:T(8,128)(2,1)S(1)}, u32[]{:S(2)}, u32[]{:S(2)}) collective-permute-start(bf16[64,1024]{1,0:T(8,128)(2,1)S(1)} %get-tuple-element.58.refs_1_), channel_id=1, source_target_pairs={{0,15},{1,2},{2,1},{3,4},{4,3},{5,6},{6,5},{7,8},{8,7},{9,10},{10,... | collective-permute-start | bytes 393224 | tf_op jit(solution)/shard_map/ppermute | solution.py:302
  27.2 5.2 %collective-permute-start.10 = (bf16[64,128]{1,0:T(8,128)(2,1)S(1)}, bf16[64,128]{1,0:T(8,128)(2,1)S(1)}, u32[]{:S(2)}, u32[]{:S(2)}) collective-permute-start(bf16[64,128]{1,0:T(8,128)(2,1)S(1)} %get-tuple-element.61.refs_4_), channel_id=1, source_target_pairs={{0,8},{1,11},{2,10},{3,9},{4,12},{5,15},{6,14},{7,13},{8,0},{9,3},... | collective-permute-start | bytes 49160 | tf_op jit(solution)/shard_map/ppermute | solution.py:314
  28.2 5.1 %collective-permute-start.11 = (bf16[64,128]{1,0:T(8,128)(2,1)S(1)}, bf16[64,128]{1,0:T(8,128)(2,1)S(1)}, u32[]{:S(2)}, u32[]{:S(2)}) collective-permute-start(bf16[64,128]{1,0:T(8,128)(2,1)S(1)} %get-tuple-element.62.refs_5_), channel_id=1, source_target_pairs={{0,9},{1,10},{2,11},{3,8},{4,13},{5,14},{6,15},{7,12},{8,1},{9,2},... | collective-permute-start | bytes 49160 | tf_op jit(solution)/shard_map/ppermute | solution.py:314
  34.0 3.1 %collective-permute-start.12 = (bf16[64,1536]{1,0:T(8,128)(2,1)S(1)}, bf16[64,1536]{1,0:T(8,128)(2,1)S(1)}, u32[]{:S(2)}, u32[]{:S(2)}) collective-permute-start(bf16[64,1536]{1,0:T(8,128)(2,1)S(1)} %get-tuple-element.66), channel_id=1, source_target_pairs={{0,1},{1,0},{2,3},{3,2},{4,5},{5,4},{6,7},{7,6},{8,9},{9,8},{10,11... | collective-permute-start | bytes 589832 | tf_op jit(solution)/shard_map/ppermute | solution.py:301
  34.1 7.4 %collective-permute-start.13 = (bf16[64,1024]{1,0:T(8,128)(2,1)S(1)}, bf16[64,1024]{1,0:T(8,128)(2,1)S(1)}, u32[]{:S(2)}, u32[]{:S(2)}) collective-permute-start(bf16[64,1024]{1,0:T(8,128)(2,1)S(1)} %get-tuple-element.65.refs_1_), channel_id=1, source_target_pairs={{0,15},{1,2},{2,1},{3,4},{4,3},{5,6},{6,5},{7,8},{8,7},{9,10},{10,... | collective-permute-start | bytes 393224 | tf_op jit(solution)/shard_map/ppermute | solution.py:302
  37.1 4.9 %collective-permute-start.14 = (bf16[64,128]{1,0:T(8,128)(2,1)S(1)}, bf16[64,128]{1,0:T(8,128)(2,1)S(1)}, u32[]{:S(2)}, u32[]{:S(2)}) collective-permute-start(bf16[64,128]{1,0:T(8,128)(2,1)S(1)} %get-tuple-element.68.refs_4_), channel_id=1, source_target_pairs={{0,8},{1,11},{2,10},{3,9},{4,12},{5,15},{6,14},{7,13},{8,0},{9,3},... | collective-permute-start | bytes 49160 | tf_op jit(solution)/shard_map/ppermute | solution.py:314
  37.4 5.4 %collective-permute-start.15 = (bf16[64,128]{1,0:T(8,128)(2,1)S(1)}, bf16[64,128]{1,0:T(8,128)(2,1)S(1)}, u32[]{:S(2)}, u32[]{:S(2)}) collective-permute-start(bf16[64,128]{1,0:T(8,128)(2,1)S(1)} %get-tuple-element.69.refs_5_), channel_id=1, source_target_pairs={{0,9},{1,10},{2,11},{3,8},{4,13},{5,14},{6,15},{7,12},{8,1},{9,2},... | collective-permute-start | bytes 49160 | tf_op jit(solution)/shard_map/ppermute | solution.py:314

commit v11 on v10

--- a/solution.py
+++ b/solution.py
@@ -15,6 +15,7 @@
 F32 = jnp.float32
 BF16 = jnp.bfloat16
 IN_VMEM = pl.BlockSpec(memory_space=pltpu.VMEM)
+PREFETCHED = pl.BlockSpec(memory_space=pltpu.VMEM)
 IN_SMEM = pl.BlockSpec(memory_space=pltpu.SMEM)
 IN_HBM = pl.BlockSpec(memory_space=pltpu.HBM)
 ANYWHERE = pl.BlockSpec(memory_space=pl.ANY)
@@ -172,23 +173,15 @@
 
 
 def first_own_kernel(plan, *refs):
-    index_ref, rows_ref, offsets_ref, x_ref, near_ref, row_hbm, tiles_hbm = refs[:7]
-    acc_ref, d_ref, rb_ref, row_ref, sem, tile_sems = refs[-6:]
+    index_ref, rows_ref, offsets_ref, x_ref, near_ref, row_ref, tiles_ref = refs[:7]
+    acc_ref, d_ref, rb_ref = refs[-3:]
     rank, size = plan.rank, plan.size
-    copies = []
     for s in range(plan.tiles):
-        cell = rows_ref[s] * SPAN + offsets_ref[s] + REACH
-        copies.append(pltpu.make_async_copy(tiles_hbm.at[s], d_ref.at[cell], tile_sems.at[s]))
-        copies[-1].start()
-    copy = pltpu.make_async_copy(row_hbm, row_ref, sem)
-    copy.start()
+        d_ref[rows_ref[s] * SPAN + offsets_ref[s] + REACH] = tiles_ref[s]
     rb_ref[...] = jnp.zeros_like(rb_ref)
-    copy.wait()
     for c in range(plan.per_device):
         for start in (c * rank, plan.width + c * rank):
             rb_ref[start : start + rank, c * size : (c + 1) * size] = row_ref[c]
-    for copy in copies:
-        copy.wait()
     plan.near_sums(x_ref, d_ref, acc_ref, 0)
     plan.halo_sums(lax.rem(index_ref[0], 2) == 1, near_ref, d_ref, acc_ref, acc_ref)
 
@@ -319,14 +312,12 @@
                 functools.partial(first_own_kernel, plan),
                 "first_own",
                 ins,
-                [IN_SMEM] * 3 + [IN_VMEM] * 2 + [IN_HBM] * 2 + [IN_VMEM] + [ANYWHERE] * len(after),
+                [IN_SMEM] * 3 + [IN_VMEM] * 2 + [PREFETCHED] * 2 + [IN_VMEM] + [ANYWHERE] * len(after),
                 [
                     acc_out,
                     pltpu.VMEM((plan.cells, plan.size, plan.size), BF16),
                     pltpu.VMEM((2 * width, shard_len), BF16),
                 ],
-                scratch=scratch_for(row_basis)
-                + [pltpu.SemaphoreType.DMA, pltpu.SemaphoreType.DMA((plan.tiles,))],
                 aliases={7: 1},
             )
         else:

time: 43.8 us -> 44 us (level)
  waiting for transfers between devices: 5.89 us -> 11.5 us
  starting transfers between devices: 22.7 us -> 19.3 us
  Pallas kernels: 14.9 us -> 12.8 us
    ppermute x4, waiting for transfers between devices: 3.28 us -> 6.54 us  [on_device(): over = lax.ppermute(block if product == 0 else current, axes, plan.over)]
    ppermute x8, starting transfers between devices: 6.88 us -> 3.9 us  [on_device(): fars = [lax.ppermute(s, axes, route) for s, route in zip(sends, routes)]]
    ppermute x8, waiting for transfers between devices: 2.61 us -> 4.95 us  [on_device(): fars = [lax.ppermute(s, axes, route) for s, route in zip(sends, routes)]]
    pallas_call x17, Pallas kernels: 14.9 us -> 12.8 us  [call(): pl.pallas_call(kernel, in_specs=list(specs), out_specs=out_specs or [IN_V...]
  transfers between devices with their start and end apart: 16 -> 16, of which waited for: 6 -> 10; matrix products, arithmetic and copies ran while one was open for 0% -> 0% of each run, Pallas kernels for 23% -> 17%
where the time goes in v11:
time: 44 us; the launch traced here: 43.8 us
  starting transfers between devices  19.3 us (44%)
  Pallas kernels  12.8 us (29%)
  waiting for transfers between devices  11.5 us (26%)
    ppermute x4, starting transfers between devices, on_device(): over = lax.ppermute(block if product == 0 else current, axes, plan.over)  14.7 us
    pallas_call x17, Pallas kernels, call(): pl.pallas_call(kernel, in_specs=list(specs), out_specs=out_specs or [IN_V...  12.8 us
    ppermute x4, waiting for transfers between devices, on_device(): over = lax.ppermute(block if product == 0 else current, axes, plan.over)  6.54 us
    ppermute x8, waiting for transfers between devices, on_device(): fars = [lax.ppermute(s, axes, route) for s, route in zip(sends, routes)]  4.95 us
    ppermute x8, starting transfers between devices, on_device(): fars = [lax.ppermute(s, axes, route) for s, route in zip(sends, routes)]  3.9 us
  transfers between devices with their start and end apart: 16, of which 10 were waited for; matrix products, arithmetic and copies ran while one was open for 0% of the time, Pallas kernels for 17%

profile of v11, /device:TPU:0, one launch (start us, length us, event | category | flops | bytes accessed | tf_op | source)
XLA Modules:
  0.0 43.8 jit_solution(16182686382921828365)
XLA Ops:
  0.0 0.0 copy-start.1
  0.0 0.0 copy-start
  0.0 2.3 %prepare.1 = (bf16[64,1024]{1,0:T(8,128)(2,1)S(1)}, bf16[36,256,256]{2,1,0:T(8,128)(2,1)S(1)}, bf16[3,512,128]{2,1,0:T(8,128)(2,1)S(1)}, bf16[128,1024]{1,0:T(8,...) custom-call(s32[1]{0:T(128)} %bitcast.index_ref.refs_0_, ...), custom_call_target="tpu_custom_call" | custom-call | flops 1000000000 | bytes 4194304 | tf_op jit(solution)/shard_map/prepare/pallas_call | solution.py:233
  2.4 0.5 %collective-permute-start = (bf16[64,1536]{1,0:T(8,128)(2,1)S(1)}, bf16[64,1536]{1,0:T(8,128)(2,1)S(1)}, u32[]{:S(2)}, u32[]{:S(2)}) collective-permute-start(bf16[64,1536]{1,0:T(8,128)(2,1)S(1)} %get-tuple-element.42), channel_id=1, source_target_pairs={{0,1},{1,0},{2,3},{3,2},{4,5},{5,4},{6,7},{7,6},{8,9},{9,8},{10,11... | collective-permute-start | bytes 589832 | tf_op jit(solution)/shard_map/ppermute | solution.py:294
  2.9 5.6 %collective-permute-start.1 = (bf16[64,1024]{1,0:T(8,128)(2,1)}, bf16[64,1024]{1,0:T(8,128)(2,1)S(1)}, u32[]{:S(2)}, u32[]{:S(2)}) collective-permute-start(bf16[64,1024]{1,0:T(8,128)(2,1)} %refs_4_.1), channel_id=1, source_target_pairs={{0,15},{1,2},{2,1},{3,4},{4,3},{5,6},{6,5},{7,8},{8,7},{9,10},{10,... | collective-permute-start | bytes 393224 | tf_op jit(solution)/shard_map/ppermute | solution.py:295
  8.5 0.0 collective-permute-done.message_ref.refs_4_
  8.5 0.1 collective-permute-start.2
  8.6 0.3 collective-permute-start.3
  8.9 0.0 copy-done.1
  8.9 0.0 copy-done
  8.9 1.6 %first_own.1 = (f32[64,1024]{1,0:T(8,128)S(1)}, bf16[36,256,256]{2,1,0:T(8,128)(2,1)S(1)}, bf16[256,1024]{1,0:T(8,128)(2,1)S(1)}) custom-call(s32[1]{0:T(128)} %bitcast.index_ref.refs_0_, s32[32]{0:T(128)S(4)} %get-tuple-element.39.refs_1_, s32[32]{0:T(128)S(4)} %get-tuple-element.40.refs_2_, ...), custom_call_target="tpu_custom_call", output_to_operand_aliasing={{1}: (7, {})} | custom-call | flops 1000000000 | bytes 4194304 | tf_op jit(solution)/shard_map/first_own/pallas_call | solution.py:233
  10.5 1.0 %collective-permute-done.1.over_ref = bf16[64,1024]{1,0:T(8,128)(2,1)S(1)} collective-permute-done((bf16[64,1024]{1,0:T(8,128)(2,1)}, bf16[64,1024]{1,0:T(8,128)(2,1)S(1)}, u32[]{:S(2)}, u32[]{:S(2)}) %collective-permute-start.1) | collective-permute-done | bytes 131104 | tf_op jit(solution)/shard_map/ppermute | solution.py:295
  11.5 0.5 %halo.4.refs_1_ = f32[64,1024]{1,0:T(8,128)S(1)} custom-call(s32[1]{0:T(128)} %bitcast.index_ref.refs_0_, f32[64,1024]{1,0:T(8,128)S(1)} %get-tuple-element.47.acc_ref, bf16[64,1024]{1,0:T(8,128)(2,1)S(1)} %collective-permute-done.1.over_ref, bf16[36,256,256]{2,1,0:T(8,128)(2,1)S(1)} %get-tuple-element.48.d_ref.refs_3_), custom_call_target="tpu_custom_call" | custom-call | flops 1000000000 | bytes 4194304 | tf_op jit(solution)/shard_map/halo/pallas_call | solution.py:233
  12.0 1.2 %collective-permute-done.2.refs_5_ = bf16[64,128]{1,0:T(8,128)(2,1)S(1)} collective-permute-done((bf16[64,128]{1,0:T(8,128)(2,1)S(1)}, bf16[64,128]{1,0:T(8,128)(2,1)S(1)}, u32[]{:S(2)}, u32[]{:S(2)}) %collective-permute-start.2) | collective-permute-done | bytes 16416 | tf_op jit(solution)/shard_map/ppermute | solution.py:307
  13.2 0.4 collective-permute-done.3.refs_6_
  13.6 0.7 %finish.3 = (bf16[64,1024]{1,0:T(8,128)(2,1)S(1)}, bf16[64,1536]{1,0:T(8,128)(2,1)S(1)}, f32[64,256]{1,0:T(8,128)S(1)}) custom-call(s32[1]{0:T(128)} %bitcast.index_ref.refs_0_, f32[64,1024]{1,0:T(8,128)S(1)} %halo.4.refs_1_, bf16[256,1024]{1,0:T(8,128)(2,1)S(1)} %get-tuple-element.49.refs_2_.refs_1_, bf16[128,1024]{1,0:T(8,128)(2,1)S(1)} %get-tuple-element.50.refs_3_, ...), custom_call_target="tpu_custom_call" | custom-call | flops 1000000000 | bytes 4194304 | tf_op jit(solution)/shard_map/finish/pallas_call | solution.py:233
  14.3 0.1 collective-permute-start.4
  14.4 3.7 %collective-permute-start.5 = (bf16[64,1024]{1,0:T(8,128)(2,1)S(1)}, bf16[64,1024]{1,0:T(8,128)(2,1)S(1)}, u32[]{:S(2)}, u32[]{:S(2)}) collective-permute-start(bf16[64,1024]{1,0:T(8,128)(2,1)S(1)} %get-tuple-element.52.refs_1_), channel_id=1, source_target_pairs={{0,15},{1,2},{2,1},{3,4},{4,3},{5,6},{6,5},{7,8},{8,7},{9,10},{10,... | collective-permute-start | bytes 393224 | tf_op jit(solution)/shard_map/ppermute | solution.py:295
  18.1 0.0 collective-permute-done.4.message_ref.refs_2_
  18.1 0.7 %collective-permute-start.6 = (bf16[64,128]{1,0:T(8,128)(2,1)S(1)}, bf16[64,128]{1,0:T(8,128)(2,1)S(1)}, u32[]{:S(2)}, u32[]{:S(2)}) collective-permute-start(bf16[64,128]{1,0:T(8,128)(2,1)S(1)} %get-tuple-element.55.refs_4_), channel_id=1, source_target_pairs={{0,8},{1,11},{2,10},{3,9},{4,12},{5,15},{6,14},{7,13},{8,0},{9,3},... | collective-permute-start | bytes 49160 | tf_op jit(solution)/shard_map/ppermute | solution.py:307
  18.8 0.4 collective-permute-start.7
  19.2 1.3 %own.3 = (f32[64,1024]{1,0:T(8,128)S(1)}, bf16[4,64,1024]{2,1,0:T(8,128)(2,1)}) custom-call(s32[1]{0:T(128)} %bitcast.index_ref.refs_0_, bf16[64,1024]{1,0:T(8,128)(2,1)S(1)} %get-tuple-element.52.refs_1_, bf16[64,1536]{1,0:T(8,128)(2,1)S(1)} %collective-permute-done.4.message_ref.refs_2_, bf16[36,256,256]{2,1,0:T(8,128)(2,1)S(1)} %get-tuple-element.48.d_ref.refs_3_, ...), custom_call_target="tpu_custom_call" | custom-call | flops 1000000000 | bytes 4194304 | tf_op jit(solution)/shard_map/own/pallas_call | solution.py:233
  20.5 1.2 %collective-permute-done.5.over_ref = bf16[64,1024]{1,0:T(8,128)(2,1)S(1)} collective-permute-done((bf16[64,1024]{1,0:T(8,128)(2,1)S(1)}, bf16[64,1024]{1,0:T(8,128)(2,1)S(1)}, u32[]{:S(2)}, u32[]{:S(2)}) %collective-permute-start.5) | collective-permute-done | bytes 131104 | tf_op jit(solution)/shard_map/ppermute | solution.py:295
  21.7 0.5 %halo.5.refs_1_ = f32[64,1024]{1,0:T(8,128)S(1)} custom-call(s32[1]{0:T(128)} %bitcast.index_ref.refs_0_, f32[64,1024]{1,0:T(8,128)S(1)} %get-tuple-element.57.acc_ref, bf16[64,1024]{1,0:T(8,128)(2,1)S(1)} %collective-permute-done.5.over_ref, bf16[36,256,256]{2,1,0:T(8,128)(2,1)S(1)} %get-tuple-element.48.d_ref.refs_3_), custom_call_target="tpu_custom_call" | custom-call | flops 1000000000 | bytes 4194304 | tf_op jit(solution)/shard_map/halo/pallas_call | solution.py:233
  22.2 0.7 %collective-permute-done.6.refs_5_ = bf16[64,128]{1,0:T(8,128)(2,1)S(1)} collective-permute-done((bf16[64,128]{1,0:T(8,128)(2,1)S(1)}, bf16[64,128]{1,0:T(8,128)(2,1)S(1)}, u32[]{:S(2)}, u32[]{:S(2)}) %collective-permute-start.6) | collective-permute-done | bytes 16416 | tf_op jit(solution)/shard_map/ppermute | solution.py:307
  22.8 1.2 %collective-permute-done.7.refs_6_ = bf16[64,128]{1,0:T(8,128)(2,1)S(1)} collective-permute-done((bf16[64,128]{1,0:T(8,128)(2,1)S(1)}, bf16[64,128]{1,0:T(8,128)(2,1)S(1)}, u32[]{:S(2)}, u32[]{:S(2)}) %collective-permute-start.7) | collective-permute-done | bytes 16416 | tf_op jit(solution)/shard_map/ppermute | solution.py:307
  24.0 0.7 %finish.4 = (bf16[64,1024]{1,0:T(8,128)(2,1)S(1)}, bf16[64,1536]{1,0:T(8,128)(2,1)S(1)}, f32[64,256]{1,0:T(8,128)S(1)}) custom-call(s32[1]{0:T(128)} %bitcast.index_ref.refs_0_, f32[64,1024]{1,0:T(8,128)S(1)} %halo.5.refs_1_, bf16[256,1024]{1,0:T(8,128)(2,1)S(1)} %get-tuple-element.49.refs_2_.refs_1_, bf16[128,1024]{1,0:T(8,128)(2,1)S(1)} %get-tuple-element.50.refs_3_, ...), custom_call_target="tpu_custom_call" | custom-call | flops 1000000000 | bytes 4194304 | tf_op jit(solution)/shard_map/finish/pallas_call | solution.py:233
  24.7 0.1 collective-permute-start.8
  24.8 2.6 %collective-permute-start.9 = (bf16[64,1024]{1,0:T(8,128)(2,1)S(1)}, bf16[64,1024]{1,0:T(8,128)(2,1)S(1)}, u32[]{:S(2)}, u32[]{:S(2)}) collective-permute-start(bf16[64,1024]{1,0:T(8,128)(2,1)S(1)} %get-tuple-element.58.refs_1_), channel_id=1, source_target_pairs={{0,15},{1,2},{2,1},{3,4},{4,3},{5,6},{6,5},{7,8},{8,7},{9,10},{10,... | collective-permute-start | bytes 393224 | tf_op jit(solution)/shard_map/ppermute | solution.py:295
  27.4 0.0 collective-permute-done.8.message_ref.refs_2_
  27.4 0.9 %collective-permute-start.10 = (bf16[64,128]{1,0:T(8,128)(2,1)S(1)}, bf16[64,128]{1,0:T(8,128)(2,1)S(1)}, u32[]{:S(2)}, u32[]{:S(2)}) collective-permute-start(bf16[64,128]{1,0:T(8,128)(2,1)S(1)} %get-tuple-element.61.refs_4_), channel_id=1, source_target_pairs={{0,8},{1,11},{2,10},{3,9},{4,12},{5,15},{6,14},{7,13},{8,0},{9,3},... | collective-permute-start | bytes 49160 | tf_op jit(solution)/shard_map/ppermute | solution.py:307
  28.4 0.4 collective-permute-start.11
  28.7 1.3 %own.4 = (f32[64,1024]{1,0:T(8,128)S(1)}, bf16[4,64,1024]{2,1,0:T(8,128)(2,1)}) custom-call(s32[1]{0:T(128)} %bitcast.index_ref.refs_0_, bf16[64,1024]{1,0:T(8,128)(2,1)S(1)} %get-tuple-element.58.refs_1_, bf16[64,1536]{1,0:T(8,128)(2,1)S(1)} %collective-permute-done.8.message_ref.refs_2_, ...), custom_call_target="tpu_custom_call", output_to_operand_aliasing={{1}: (6, {})} | custom-call | flops 1000000000 | bytes 4194304 | tf_op jit(solution)/shard_map/own/pallas_call | solution.py:233
  30.0 2.2 %collective-permute-done.9.over_ref = bf16[64,1024]{1,0:T(8,128)(2,1)S(1)} collective-permute-done((bf16[64,1024]{1,0:T(8,128)(2,1)S(1)}, bf16[64,1024]{1,0:T(8,128)(2,1)S(1)}, u32[]{:S(2)}, u32[]{:S(2)}) %collective-permute-start.9) | collective-permute-done | bytes 131104 | tf_op jit(solution)/shard_map/ppermute | solution.py:295
  32.2 0.5 %halo.6.refs_1_ = f32[64,1024]{1,0:T(8,128)S(1)} custom-call(s32[1]{0:T(128)} %bitcast.index_ref.refs_0_, f32[64,1024]{1,0:T(8,128)S(1)} %get-tuple-element.64.acc_ref, bf16[64,1024]{1,0:T(8,128)(2,1)S(1)} %collective-permute-done.9.over_ref, bf16[36,256,256]{2,1,0:T(8,128)(2,1)S(1)} %get-tuple-element.48.d_ref.refs_3_), custom_call_target="tpu_custom_call" | custom-call | flops 1000000000 | bytes 4194304 | tf_op jit(solution)/shard_map/halo/pallas_call | solution.py:233
  32.8 0.0 collective-permute-done.10.refs_5_
  32.8 0.7 %collective-permute-done.11.refs_6_ = bf16[64,128]{1,0:T(8,128)(2,1)S(1)} collective-permute-done((bf16[64,128]{1,0:T(8,128)(2,1)S(1)}, bf16[64,128]{1,0:T(8,128)(2,1)S(1)}, u32[]{:S(2)}, u32[]{:S(2)}) %collective-permute-start.11) | collective-permute-done | bytes 16416 | tf_op jit(solution)/shard_map/ppermute | solution.py:307
  33.5 0.7 %finish.5 = (bf16[64,1024]{1,0:T(8,128)(2,1)S(1)}, bf16[64,1536]{1,0:T(8,128)(2,1)S(1)}, f32[64,256]{1,0:T(8,128)S(1)}) custom-call(s32[1]{0:T(128)} %bitcast.index_ref.refs_0_, f32[64,1024]{1,0:T(8,128)S(1)} %halo.6.refs_1_, bf16[256,1024]{1,0:T(8,128)(2,1)S(1)} %get-tuple-element.49.refs_2_.refs_1_, bf16[128,1024]{1,0:T(8,128)(2,1)S(1)} %get-tuple-element.50.refs_3_, ...), custom_call_target="tpu_custom_call" | custom-call | flops 1000000000 | bytes 4194304 | tf_op jit(solution)/shard_map/finish/pallas_call | solution.py:233
  34.1 0.1 collective-permute-start.12
  34.2 2.8 %collective-permute-start.13 = (bf16[64,1024]{1,0:T(8,128)(2,1)S(1)}, bf16[64,1024]{1,0:T(8,128)(2,1)S(1)}, u32[]{:S(2)}, u32[]{:S(2)}) collective-permute-start(bf16[64,1024]{1,0:T(8,128)(2,1)S(1)} %get-tuple-element.65.refs_1_), channel_id=1, source_target_pairs={{0,15},{1,2},{2,1},{3,4},{4,3},{5,6},{6,5},{7,8},{8,7},{9,10},{10,... | collective-permute-start | bytes 393224 | tf_op jit(solution)/shard_map/ppermute | solution.py:295
  37.0 0.0 collective-permute-done.12.message_ref.refs_2_
  37.0 0.7 %collective-permute-start.14 = (bf16[64,128]{1,0:T(8,128)(2,1)S(1)}, bf16[64,128]{1,0:T(8,128)(2,1)S(1)}, u32[]{:S(2)}, u32[]{:S(2)}) collective-permute-start(bf16[64,128]{1,0:T(8,128)(2,1)S(1)} %get-tuple-element.68.refs_4_), channel_id=1, source_target_pairs={{0,8},{1,11},{2,10},{3,9},{4,12},{5,15},{6,14},{7,13},{8,0},{9,3},... | collective-permute-start | bytes 49160 | tf_op jit(solution)/shard_map/ppermute | solution.py:307
  37.7 0.6 %collective-permute-start.15 = (bf16[64,128]{1,0:T(8,128)(2,1)S(1)}, bf16[64,128]{1,0:T(8,128)(2,1)S(1)}, u32[]{:S(2)}, u32[]{:S(2)}) collective-permute-start(bf16[64,128]{1,0:T(8,128)(2,1)S(1)} %get-tuple-element.69.refs_5_), channel_id=1, source_target_pairs={{0,9},{1,10},{2,11},{3,8},{4,13},{5,14},{6,15},{7,12},{8,1},{9,2},... | collective-permute-start | bytes 49160 | tf_op jit(solution)/shard_map/ppermute | solution.py:307
  38.3 1.3 %own.5 = (f32[64,1024]{1,0:T(8,128)S(1)}, bf16[4,64,1024]{2,1,0:T(8,128)(2,1)}) custom-call(s32[1]{0:T(128)} %bitcast.index_ref.refs_0_, bf16[64,1024]{1,0:T(8,128)(2,1)S(1)} %get-tuple-element.65.refs_1_, bf16[64,1536]{1,0:T(8,128)(2,1)S(1)} %collective-permute-done.12.message_ref.refs_2_, ...), custom_call_target="tpu_custom_call", output_to_operand_aliasing={{1}: (6, {})} | custom-call | flops 1000000000 | bytes 4194304 | tf_op jit(solution)/shard_map/own/pallas_call | solution.py:233
  39.5 2.1 %collective-permute-done.13.over_ref = bf16[64,1024]{1,0:T(8,128)(2,1)S(1)} collective-permute-done((bf16[64,1024]{1,0:T(8,128)(2,1)S(1)}, bf16[64,1024]{1,0:T(8,128)(2,1)S(1)}, u32[]{:S(2)}, u32[]{:S(2)}) %collective-permute-start.13) | collective-permute-done | bytes 131104 | tf_op jit(solution)/shard_map/ppermute | solution.py:295
  41.7 0.5 %halo.7.refs_0_ = f32[64,1024]{1,0:T(8,128)S(1)} custom-call(s32[1]{0:T(128)} %bitcast.index_ref.refs_0_, f32[64,1024]{1,0:T(8,128)S(1)} %get-tuple-element.71.acc_ref, bf16[64,1024]{1,0:T(8,128)(2,1)S(1)} %collective-permute-done.13.over_ref, bf16[36,256,256]{2,1,0:T(8,128)(2,1)S(1)} %get-tuple-element.48.d_ref.refs_3_), custom_call_target="tpu_custom_call" | custom-call | flops 1000000000 | bytes 4194304 | tf_op jit(solution)/shard_map/halo/pallas_call | solution.py:233
  42.2 0.0 collective-permute-done.14.refs_2_
  42.2 0.8 %collective-permute-done.15.refs_3_ = bf16[64,128]{1,0:T(8,128)(2,1)S(1)} collective-permute-done((bf16[64,128]{1,0:T(8,128)(2,1)S(1)}, bf16[64,128]{1,0:T(8,128)(2,1)S(1)}, u32[]{:S(2)}, u32[]{:S(2)}) %collective-permute-start.15) | collective-permute-done | bytes 16416 | tf_op jit(solution)/shard_map/ppermute | solution.py:307
  42.9 0.9 %last.1 = bf16[4,64,1024]{2,1,0:T(8,128)(2,1)} custom-call(f32[64,1024]{1,0:T(8,128)S(1)} %halo.7.refs_0_, bf16[256,1024]{1,0:T(8,128)(2,1)S(1)} %get-tuple-element.49.refs_2_.refs_1_, bf16[64,128]{1,0:T(8,128)(2,1)S(1)} %collective-permute-done.14.refs_2_, bf16[64,128]{1,0:T(8,128)(2,1)S(1)} %collective-permute-done.15.refs_3_, ...), custom_call_target="tpu_custom_call", output_to_operand_aliasing={{}: (4, {})} | custom-call | flops 1000000000 | bytes 4194304 | tf_op jit(solution)/shard_map/last/pallas_call | solution.py:233
  (4 shorter events, 0.1 us)
Async XLA Ops:
  0.0 8.9 %copy-start.1 = (bf16[4,32,256]{2,1,0:T(8,128)(2,1)S(1)}, bf16[4,32,256]{2,1,0:T(8,128)(2,1)}, u32[]{:S(2)}) copy-start(bf16[4,32,256]{2,1,0:T(8,128)(2,1)} %refs_5_.3) | copy-start | bytes 196612
  0.0 8.9 %copy-start = (bf16[32,256,256]{2,1,0:T(8,128)(2,1)S(1)}, bf16[32,256,256]{2,1,0:T(8,128)(2,1)}, u32[]{:S(2)}) copy-start(bf16[32,256,256]{2,1,0:T(8,128)(2,1)} %refs_6_.3) | copy-start | bytes 12582916
  2.4 6.2 %collective-permute-start = (bf16[64,1536]{1,0:T(8,128)(2,1)S(1)}, bf16[64,1536]{1,0:T(8,128)(2,1)S(1)}, u32[]{:S(2)}, u32[]{:S(2)}) collective-permute-start(bf16[64,1536]{1,0:T(8,128)(2,1)S(1)} %get-tuple-element.42), channel_id=1, source_target_pairs={{0,1},{1,0},{2,3},{3,2},{4,5},{5,4},{6,7},{7,6},{8,9},{9,8},{10,11... | collective-permute-start | bytes 589832 | tf_op jit(solution)/shard_map/ppermute | solution.py:294
  2.9 8.6 %collective-permute-start.1 = (bf16[64,1024]{1,0:T(8,128)(2,1)}, bf16[64,1024]{1,0:T(8,128)(2,1)S(1)}, u32[]{:S(2)}, u32[]{:S(2)}) collective-permute-start(bf16[64,1024]{1,0:T(8,128)(2,1)} %refs_4_.1), channel_id=1, source_target_pairs={{0,15},{1,2},{2,1},{3,4},{4,3},{5,6},{6,5},{7,8},{8,7},{9,10},{10,... | collective-permute-start | bytes 393224 | tf_op jit(solution)/shard_map/ppermute | solution.py:295
  8.5 4.7 %collective-permute-start.2 = (bf16[64,128]{1,0:T(8,128)(2,1)S(1)}, bf16[64,128]{1,0:T(8,128)(2,1)S(1)}, u32[]{:S(2)}, u32[]{:S(2)}) collective-permute-start(bf16[64,128]{1,0:T(8,128)(2,1)S(1)} %get-tuple-element.45.refs_8_), channel_id=1, source_target_pairs={{0,8},{1,11},{2,10},{3,9},{4,12},{5,15},{6,14},{7,13},{8,0},{9,3},... | collective-permute-start | bytes 49160 | tf_op jit(solution)/shard_map/ppermute | solution.py:307
  8.6 5.0 %collective-permute-start.3 = (bf16[64,128]{1,0:T(8,128)(2,1)S(1)}, bf16[64,128]{1,0:T(8,128)(2,1)S(1)}, u32[]{:S(2)}, u32[]{:S(2)}) collective-permute-start(bf16[64,128]{1,0:T(8,128)(2,1)S(1)} %get-tuple-element.46.refs_9_), channel_id=1, source_target_pairs={{0,9},{1,10},{2,11},{3,8},{4,13},{5,14},{6,15},{7,12},{8,1},{9,2},... | collective-permute-start | bytes 49160 | tf_op jit(solution)/shard_map/ppermute | solution.py:307
  14.3 3.8 %collective-permute-start.4 = (bf16[64,1536]{1,0:T(8,128)(2,1)S(1)}, bf16[64,1536]{1,0:T(8,128)(2,1)S(1)}, u32[]{:S(2)}, u32[]{:S(2)}) collective-permute-start(bf16[64,1536]{1,0:T(8,128)(2,1)S(1)} %get-tuple-element.53), channel_id=1, source_target_pairs={{0,1},{1,0},{2,3},{3,2},{4,5},{5,4},{6,7},{7,6},{8,9},{9,8},{10,11... | collective-permute-start | bytes 589832 | tf_op jit(solution)/shard_map/ppermute | solution.py:294
  14.4 7.3 %collective-permute-start.5 = (bf16[64,1024]{1,0:T(8,128)(2,1)S(1)}, bf16[64,1024]{1,0:T(8,128)(2,1)S(1)}, u32[]{:S(2)}, u32[]{:S(2)}) collective-permute-start(bf16[64,1024]{1,0:T(8,128)(2,1)S(1)} %get-tuple-element.52.refs_1_), channel_id=1, source_target_pairs={{0,15},{1,2},{2,1},{3,4},{4,3},{5,6},{6,5},{7,8},{8,7},{9,10},{10,... | collective-permute-start | bytes 393224 | tf_op jit(solution)/shard_map/ppermute | solution.py:295
  18.1 4.7 %collective-permute-start.6 = (bf16[64,128]{1,0:T(8,128)(2,1)S(1)}, bf16[64,128]{1,0:T(8,128)(2,1)S(1)}, u32[]{:S(2)}, u32[]{:S(2)}) collective-permute-start(bf16[64,128]{1,0:T(8,128)(2,1)S(1)} %get-tuple-element.55.refs_4_), channel_id=1, source_target_pairs={{0,8},{1,11},{2,10},{3,9},{4,12},{5,15},{6,14},{7,13},{8,0},{9,3},... | collective-permute-start | bytes 49160 | tf_op jit(solution)/shard_map/ppermute | solution.py:307
  18.8 5.3 %collective-permute-start.7 = (bf16[64,128]{1,0:T(8,128)(2,1)S(1)}, bf16[64,128]{1,0:T(8,128)(2,1)S(1)}, u32[]{:S(2)}, u32[]{:S(2)}) collective-permute-start(bf16[64,128]{1,0:T(8,128)(2,1)S(1)} %get-tuple-element.56.refs_5_), channel_id=1, source_target_pairs={{0,9},{1,10},{2,11},{3,8},{4,13},{5,14},{6,15},{7,12},{8,1},{9,2},... | collective-permute-start | bytes 49160 | tf_op jit(solution)/shard_map/ppermute | solution.py:307
  24.7 2.7 %collective-permute-start.8 = (bf16[64,1536]{1,0:T(8,128)(2,1)S(1)}, bf16[64,1536]{1,0:T(8,128)(2,1)S(1)}, u32[]{:S(2)}, u32[]{:S(2)}) collective-permute-start(bf16[64,1536]{1,0:T(8,128)(2,1)S(1)} %get-tuple-element.59), channel_id=1, source_target_pairs={{0,1},{1,0},{2,3},{3,2},{4,5},{5,4},{6,7},{7,6},{8,9},{9,8},{10,11... | collective-permute-start | bytes 589832 | tf_op jit(solution)/shard_map/ppermute | solution.py:294
  24.8 7.4 %collective-permute-start.9 = (bf16[64,1024]{1,0:T(8,128)(2,1)S(1)}, bf16[64,1024]{1,0:T(8,128)(2,1)S(1)}, u32[]{:S(2)}, u32[]{:S(2)}) collective-permute-start(bf16[64,1024]{1,0:T(8,128)(2,1)S(1)} %get-tuple-element.58.refs_1_), channel_id=1, source_target_pairs={{0,15},{1,2},{2,1},{3,4},{4,3},{5,6},{6,5},{7,8},{8,7},{9,10},{10,... | collective-permute-start | bytes 393224 | tf_op jit(solution)/shard_map/ppermute | solution.py:295
  27.4 5.3 %collective-permute-start.10 = (bf16[64,128]{1,0:T(8,128)(2,1)S(1)}, bf16[64,128]{1,0:T(8,128)(2,1)S(1)}, u32[]{:S(2)}, u32[]{:S(2)}) collective-permute-start(bf16[64,128]{1,0:T(8,128)(2,1)S(1)} %get-tuple-element.61.refs_4_), channel_id=1, source_target_pairs={{0,8},{1,11},{2,10},{3,9},{4,12},{5,15},{6,14},{7,13},{8,0},{9,3},... | collective-permute-start | bytes 49160 | tf_op jit(solution)/shard_map/ppermute | solution.py:307
  28.4 5.1 %collective-permute-start.11 = (bf16[64,128]{1,0:T(8,128)(2,1)S(1)}, bf16[64,128]{1,0:T(8,128)(2,1)S(1)}, u32[]{:S(2)}, u32[]{:S(2)}) collective-permute-start(bf16[64,128]{1,0:T(8,128)(2,1)S(1)} %get-tuple-element.62.refs_5_), channel_id=1, source_target_pairs={{0,9},{1,10},{2,11},{3,8},{4,13},{5,14},{6,15},{7,12},{8,1},{9,2},... | collective-permute-start | bytes 49160 | tf_op jit(solution)/shard_map/ppermute | solution.py:307
  34.1 2.9 %collective-permute-start.12 = (bf16[64,1536]{1,0:T(8,128)(2,1)S(1)}, bf16[64,1536]{1,0:T(8,128)(2,1)S(1)}, u32[]{:S(2)}, u32[]{:S(2)}) collective-permute-start(bf16[64,1536]{1,0:T(8,128)(2,1)S(1)} %get-tuple-element.66), channel_id=1, source_target_pairs={{0,1},{1,0},{2,3},{3,2},{4,5},{5,4},{6,7},{7,6},{8,9},{9,8},{10,11... | collective-permute-start | bytes 589832 | tf_op jit(solution)/shard_map/ppermute | solution.py:294
  34.2 7.4 %collective-permute-start.13 = (bf16[64,1024]{1,0:T(8,128)(2,1)S(1)}, bf16[64,1024]{1,0:T(8,128)(2,1)S(1)}, u32[]{:S(2)}, u32[]{:S(2)}) collective-permute-start(bf16[64,1024]{1,0:T(8,128)(2,1)S(1)} %get-tuple-element.65.refs_1_), channel_id=1, source_target_pairs={{0,15},{1,2},{2,1},{3,4},{4,3},{5,6},{6,5},{7,8},{8,7},{9,10},{10,... | collective-permute-start | bytes 393224 | tf_op jit(solution)/shard_map/ppermute | solution.py:295
  37.0 5.2 %collective-permute-start.14 = (bf16[64,128]{1,0:T(8,128)(2,1)S(1)}, bf16[64,128]{1,0:T(8,128)(2,1)S(1)}, u32[]{:S(2)}, u32[]{:S(2)}) collective-permute-start(bf16[64,128]{1,0:T(8,128)(2,1)S(1)} %get-tuple-element.68.refs_4_), channel_id=1, source_target_pairs={{0,8},{1,11},{2,10},{3,9},{4,12},{5,15},{6,14},{7,13},{8,0},{9,3},... | collective-permute-start | bytes 49160 | tf_op jit(solution)/shard_map/ppermute | solution.py:307
  37.7 5.3 %collective-permute-start.15 = (bf16[64,128]{1,0:T(8,128)(2,1)S(1)}, bf16[64,128]{1,0:T(8,128)(2,1)S(1)}, u32[]{:S(2)}, u32[]{:S(2)}) collective-permute-start(bf16[64,128]{1,0:T(8,128)(2,1)S(1)} %get-tuple-element.69.refs_5_), channel_id=1, source_target_pairs={{0,9},{1,10},{2,11},{3,8},{4,13},{5,14},{6,15},{7,12},{8,1},{9,2},... | collective-permute-start | bytes 49160 | tf_op jit(solution)/shard_map/ppermute | solution.py:307

commit v12 on v11

--- a/solution.py
+++ b/solution.py
@@ -11,6 +11,8 @@
 REACH = 4
 LEVELS = 3
 SPAN = 2 * REACH + 1
+
+BRIEF, USUAL, LONG, LOADING = (10**6, 2**16), (10**9, 2**22), (4 * 10**9, 2**22), (10**6, 2**23)
 
 F32 = jnp.float32
 BF16 = jnp.bfloat16
@@ -86,13 +88,16 @@
         first, last = total[:, : 2 * self.width], total[:, 2 * self.width :]
         keep_ref[...] = jnp.where(second, last, first)
         upper, lower = halves(jnp.where(second, first, last))
-        message_ref[:, : self.shard_len] = x
-        message_ref[:, self.shard_len : self.shard_len + 2 * self.width] = upper
-        message_ref[:, self.shard_len + 2 * self.width :] = lower
+        start = message_ref.shape[1] - 4 * self.width
+        if start:
+            message_ref[:, :start] = x
+        message_ref[:, start : start + 2 * self.width] = upper
+        message_ref[:, start + 2 * self.width :] = lower
 
     def relay_far(self, index_ref, keep_ref, message_ref, out_refs):
-        upper = message_ref[:, self.shard_len : self.shard_len + 2 * self.width].astype(F32)
-        lower = message_ref[:, self.shard_len + 2 * self.width :].astype(F32)
+        start = message_ref.shape[1] - 4 * self.width
+        upper = message_ref[:, start : start + 2 * self.width].astype(F32)
+        lower = message_ref[:, start + 2 * self.width :].astype(F32)
         total = (keep_ref[...] + (upper + lower)).astype(BF16)
         second = lax.rem(index_ref[0], 2) == 1
         first, last = total[:, : self.width], total[:, self.width :]
@@ -136,8 +141,8 @@
 
 def prepare_kernel(plan, index_ref, *refs):
     sources, refs = refs[:7], refs[7:]
-    x_ref, d_ref, g_ref, cb_ref, near_ref, offsets_ref = refs[:6]
-    sends, (rows_ref, cols_ref, col_ref, coup_ref, sems) = refs[6:-5], refs[-5:]
+    x_ref, g_ref, cb_ref, near_ref, offsets_ref = refs[:5]
+    sends, (rows_ref, cols_ref, col_ref, coup_ref, sems) = refs[5:-5], refs[-5:]
     targets = (near_ref, offsets_ref, rows_ref, cols_ref, x_ref, col_ref, coup_ref)
     copies = [
         pltpu.make_async_copy(source, target, sems.at[i])
@@ -148,8 +153,6 @@
     rank, size = plan.rank, plan.size
     cb_ref[...] = jnp.zeros_like(cb_ref)
     g_ref[...] = jnp.zeros_like(g_ref)
-    for cell in range(plan.cells):
-        d_ref[cell] = jnp.zeros(d_ref.shape[1:], d_ref.dtype)
     for copy in copies:
         copy.wait()
     for c in range(plan.per_device):
@@ -176,6 +179,8 @@
     index_ref, rows_ref, offsets_ref, x_ref, near_ref, row_ref, tiles_ref = refs[:7]
     acc_ref, d_ref, rb_ref = refs[-3:]
     rank, size = plan.rank, plan.size
+    for cell in range(plan.cells):
+        d_ref[cell] = jnp.zeros(d_ref.shape[1:], d_ref.dtype)
     for s in range(plan.tiles):
         d_ref[rows_ref[s] * SPAN + offsets_ref[s] + REACH] = tiles_ref[s]
     rb_ref[...] = jnp.zeros_like(rb_ref)
@@ -224,7 +229,7 @@
         copy.wait()
 
 
-def call(kernel, name, ins, specs, outs, out_specs=None, scratch=(), aliases=None):
+def call(kernel, name, ins, specs, outs, out_specs=None, scratch=(), aliases=None, cost=USUAL):
     spaces = {id(IN_VMEM): pltpu.VMEM, id(IN_HBM): pltpu.HBM}
     ins = [
         pltpu.with_memory_space_constraint(v, spaces[id(spec)]) if id(spec) in spaces else v
@@ -238,7 +243,7 @@
         scratch_shapes=list(scratch),
         input_output_aliases=aliases or {},
         compiler_params=pltpu.CompilerParams(vmem_limit_bytes=16 * 2**20),
-        cost_estimate=pl.CostEstimate(flops=10**9, bytes_accessed=2**22, transcendentals=0),
+        cost_estimate=pl.CostEstimate(flops=cost[0], bytes_accessed=cost[1], transcendentals=0),
         name=name,
     )(*ins)
 
@@ -256,12 +261,11 @@
     relay_out = pltpu.VMEM((rhs, width), BF16)
     krylov_out = jax.ShapeDtypeStruct((PRODUCTS, rhs, shard_len), BF16)
     if plan.paired:
-        sends_out = [
-            pltpu.VMEM((rhs, shard_len + 4 * width), BF16),
-            pltpu.VMEM((rhs, 2 * width), F32),
-        ]
+        kept = pltpu.VMEM((rhs, 2 * width), F32)
+        first_out = [pltpu.VMEM((rhs, 4 * width), BF16), kept]
+        sends_out = [pltpu.VMEM((rhs, shard_len + 4 * width), BF16), kept]
     else:
-        sends_out = [pltpu.VMEM((rhs, width), BF16)] * len(plan.routes)
+        first_out = sends_out = [pltpu.VMEM((rhs, width), BF16)] * len(plan.routes)
     index = lax.axis_index(axes).astype(jnp.int32).reshape(1)
 
     def scratch_for(*arrays):
@@ -273,33 +277,39 @@
     current, sends, krylov = block, None, None
     for product in range(PRODUCTS):
         if product == 0:
+            near = lax.ppermute(block, axes, plan.near)
+            over = lax.ppermute(block, axes, plan.over)
             ins = [near_rows, near_offsets, far_rows, far_cols, block, col_basis, couplings]
-            current, dense, coupled, col_wide, row_slots, offset_slots, *sends = call(
+            current, coupled, col_wide, row_slots, offset_slots, *sends = call(
                 functools.partial(prepare_kernel, plan),
                 "prepare",
                 [index, *ins],
                 [IN_SMEM] + [IN_HBM] * 7,
                 [
                     block_out,
-                    pltpu.VMEM((plan.cells, plan.size, plan.size), BF16),
                     pltpu.VMEM((LEVELS, plan.members * width, width), BF16),
                     pltpu.VMEM((width, shard_len), BF16),
                     *scratch_for(near_rows, near_offsets),
-                    *sends_out,
+                    *first_out,
                 ],
-                [IN_VMEM] * 4 + [IN_SMEM] * 2 + [IN_VMEM] * len(sends_out),
+                [IN_VMEM] * 3 + [IN_SMEM] * 2 + [IN_VMEM] * len(sends_out),
                 scratch=scratch_for(far_rows, far_cols, col_basis, couplings)
                 + [pltpu.SemaphoreType.DMA((7,))],
-            )
-        near = lax.ppermute(sends[0] if plan.paired else current, axes, plan.near)
-        over = lax.ppermute(block if product == 0 else current, axes, plan.over)
+                cost=LONG,
+            )
+        if product > 0:
+            over = lax.ppermute(current, axes, plan.over)
+            near = message = lax.ppermute(sends[0] if plan.paired else current, axes, plan.near)
+        elif plan.paired:
+            message = lax.ppermute(sends[0], axes, plan.near)
         if plan.paired:
             sends = call(
                 functools.partial(relay_kernel, plan),
                 "relay",
-                [index, sends[1], near],
+                [index, sends[1], message],
                 [IN_SMEM] + [IN_VMEM] * 2,
                 [relay_out] * 2,
+                cost=BRIEF if product == 0 else USUAL,
             )
             routes = plan.across
         else:
@@ -307,18 +317,18 @@
         fars = [lax.ppermute(s, axes, route) for s, route in zip(sends, routes)]
         after = sends if plan.paired else []
         if product == 0:
-            ins = [index, row_slots, offset_slots, current, near, row_basis, near_tiles, dense, *after]
+            ins = [index, row_slots, offset_slots, current, near, row_basis, near_tiles, *after]
             acc, dense, row_wide = call(
                 functools.partial(first_own_kernel, plan),
                 "first_own",
                 ins,
-                [IN_SMEM] * 3 + [IN_VMEM] * 2 + [PREFETCHED] * 2 + [IN_VMEM] + [ANYWHERE] * len(after),
+                [IN_SMEM] * 3 + [IN_VMEM] * 2 + [PREFETCHED] * 2 + [ANYWHERE] * len(after),
                 [
                     acc_out,
                     pltpu.VMEM((plan.cells, plan.size, plan.size), BF16),
                     pltpu.VMEM((2 * width, shard_len), BF16),
                 ],
-                aliases={7: 1},
+                cost=LOADING,
             )
         else:
             ins = [index, current, near, dense, *after] + ([krylov] if product > 1 else [])
@@ -338,6 +348,7 @@
             [index, acc, over, dense],
             [IN_SMEM] + [IN_VMEM] * 3,
             [acc_out],
+            cost=BRIEF if product == 0 else USUAL,
         )
         if product < PRODUCTS - 1:
             ins = [index, acc, row_wide, col_wide, coupled, *fars]

time: 44 us -> 44.3 us (level)
    ppermute x8, starting transfers between devices: 3.9 us -> 8.25 us  [on_device(): fars = [lax.ppermute(s, axes, route) for s, route in zip(sends, routes)]]
    ppermute x8 -> x9, starting transfers between devices: 15.4 us -> 11.2 us  [the longest x1 5.64 us: on_device(): over = lax.ppermute(block, axes, plan.over)]
    ppermute x8 -> x9, waiting for transfers between devices: 6.55 us -> 6.62 us  [the longest x3 4.97 us: on_device(): over = lax.ppermute(current, axes, plan.over)]
  transfers between devices with their start and end apart: 16 -> 17, of which waited for: 10 -> 10; matrix products, arithmetic and copies ran while one was open for 0% -> 0% of each run, Pallas kernels for 17% -> 22%
where the time goes in v12:
time: 44.3 us; the launch traced here: 44.2 us
  starting transfers between devices  19.5 us (44%)
  Pallas kernels  12.7 us (29%)
  waiting for transfers between devices  11.8 us (27%)
    pallas_call x17, Pallas kernels, call(): pl.pallas_call(kernel, in_specs=list(specs), out_specs=out_specs or [IN_V...  12.7 us
    ppermute x8, starting transfers between devices, on_device(): fars = [lax.ppermute(s, axes, route) for s, route in zip(sends, routes)]  8.25 us
    ppermute x1, starting transfers between devices, on_device(): over = lax.ppermute(block, axes, plan.over)  5.64 us
    ppermute x8, waiting for transfers between devices, on_device(): fars = [lax.ppermute(s, axes, route) for s, route in zip(sends, routes)]  5.2 us
    ppermute x3, waiting for transfers between devices, on_device(): over = lax.ppermute(current, axes, plan.over)  4.97 us
    ppermute x3, starting transfers between devices, on_device(): over = lax.ppermute(current, axes, plan.over)  4.72 us
    ppermute x1, waiting for transfers between devices, on_device(): message = lax.ppermute(sends[0], axes, plan.near)  1.24 us
  transfers between devices with their start and end apart: 17, of which 10 were waited for; matrix products, arithmetic and copies ran while one was open for 0% of the time, Pallas kernels for 22%

profile of v12, /device:TPU:0, one launch (start us, length us, event | category | flops | bytes accessed | tf_op | source)
XLA Modules:
  0.0 44.2 jit_solution(17378725662625813494)
XLA Ops:
  0.0 0.5 %collective-permute-start = (bf16[64,1024]{1,0:T(8,128)(2,1)}, bf16[64,1024]{1,0:T(8,128)(2,1)S(1)}, u32[]{:S(2)}, u32[]{:S(2)}) collective-permute-start(bf16[64,1024]{1,0:T(8,128)(2,1)} %refs_4_.1), channel_id=1, source_target_pairs={{0,1},{1,0},{2,3},{3,2},{4,5},{5,4},{6,7},{7,6},{8,9},{9,8},{10,11... | collective-permute-start | bytes 393224 | tf_op jit(solution)/shard_map/ppermute | solution.py:280
  0.5 5.6 %collective-permute-start.2 = (bf16[64,1024]{1,0:T(8,128)(2,1)}, bf16[64,1024]{1,0:T(8,128)(2,1)S(1)}, u32[]{:S(2)}, u32[]{:S(2)}) collective-permute-start(bf16[64,1024]{1,0:T(8,128)(2,1)} %refs_4_.1), channel_id=1, source_target_pairs={{0,15},{1,2},{2,1},{3,4},{4,3},{5,6},{6,5},{7,8},{8,7},{9,10},{10,... | collective-permute-start | bytes 393224 | tf_op jit(solution)/shard_map/ppermute | solution.py:281
  6.1 0.0 copy-start
  6.1 0.0 copy-start.1
  6.1 1.9 %prepare.1 = (bf16[64,1024]{1,0:T(8,128)(2,1)S(1)}, bf16[3,512,128]{2,1,0:T(8,128)(2,1)S(1)}, bf16[128,1024]{1,0:T(8,128)(2,1)S(1)}, s32[32]{0:T(128)S(4)}, s32[...) custom-call(s32[1]{0:T(128)} %bitcast.index_ref.refs_0_, s32[32]{0:T(128)} %refs_0_.1, s32[32]{0:T(128)} %refs_1_.1, ...), custom_call_target="tpu_custom_call" | custom-call | flops 4000000000 | bytes 4194304 | tf_op jit(solution)/shard_map/prepare/pallas_call | solution.py:238
  8.0 0.1 collective-permute-start.1
  8.1 1.2 %collective-permute-done.1.message_ref = bf16[64,512]{1,0:T(8,128)(2,1)S(1)} collective-permute-done((bf16[64,512]{1,0:T(8,128)(2,1)S(1)}, bf16[64,512]{1,0:T(8,128)(2,1)S(1)}, u32[]{:S(2)}, u32[]{:S(2)}) %collective-permute-start.1) | collective-permute-done | bytes 65568 | tf_op jit(solution)/shard_map/ppermute | solution.py:304
  9.4 0.1 collective-permute-start.3
  9.4 0.2 collective-permute-start.4
  9.6 0.0 collective-permute-done.refs_4_
  9.6 0.0 copy-done
  9.6 0.0 copy-done.1
  9.6 1.9 %first_own.1 = (f32[64,1024]{1,0:T(8,128)S(1)}, bf16[36,256,256]{2,1,0:T(8,128)(2,1)S(1)}, bf16[256,1024]{1,0:T(8,128)(2,1)S(1)}) custom-call(s32[1]{0:T(128)} %bitcast.index_ref.refs_0_, s32[32]{0:T(128)S(4)} %get-tuple-element.38.refs_1_, s32[32]{0:T(128)S(4)} %get-tuple-element.39.refs_2_, bf16[64,1024]{1,0:T(8,128)(2,1)S(1)} %get-tuple-element.40.refs_3_, ...), custom_call_target="tpu_custom_call" | custom-call | flops 1000000 | bytes 8388608 | tf_op jit(solution)/shard_map/first_own/pallas_call | solution.py:238
  11.5 0.0 collective-permute-done.2.over_ref
  11.5 0.5 %halo.4.refs_1_ = f32[64,1024]{1,0:T(8,128)S(1)} custom-call(s32[1]{0:T(128)} %bitcast.index_ref.refs_0_, f32[64,1024]{1,0:T(8,128)S(1)} %get-tuple-element.45.acc_ref, bf16[64,1024]{1,0:T(8,128)(2,1)S(1)} %collective-permute-done.2.over_ref, bf16[36,256,256]{2,1,0:T(8,128)(2,1)S(1)} %get-tuple-element.46.d_ref.refs_3_), custom_call_target="tpu_custom_call" | custom-call | flops 1000000 | bytes 65536 | tf_op jit(solution)/shard_map/halo/pallas_call | solution.py:238
  12.1 2.3 %collective-permute-done.3.refs_5_ = bf16[64,128]{1,0:T(8,128)(2,1)S(1)} collective-permute-done((bf16[64,128]{1,0:T(8,128)(2,1)S(1)}, bf16[64,128]{1,0:T(8,128)(2,1)S(1)}, u32[]{:S(2)}, u32[]{:S(2)}) %collective-permute-start.3) | collective-permute-done | bytes 16416 | tf_op jit(solution)/shard_map/ppermute | solution.py:317
  14.4 0.1 collective-permute-done.4.refs_6_
  14.5 0.7 %finish.3 = (bf16[64,1024]{1,0:T(8,128)(2,1)S(1)}, bf16[64,1536]{1,0:T(8,128)(2,1)S(1)}, f32[64,256]{1,0:T(8,128)S(1)}) custom-call(s32[1]{0:T(128)} %bitcast.index_ref.refs_0_, f32[64,1024]{1,0:T(8,128)S(1)} %halo.4.refs_1_, bf16[256,1024]{1,0:T(8,128)(2,1)S(1)} %get-tuple-element.47.refs_2_.refs_1_, bf16[128,1024]{1,0:T(8,128)(2,1)S(1)} %get-tuple-element.48.refs_3_, ...), custom_call_target="tpu_custom_call" | custom-call | flops 1000000000 | bytes 4194304 | tf_op jit(solution)/shard_map/finish/pallas_call | solution.py:238
  15.1 0.2 collective-permute-start.5
  15.3 2.1 %collective-permute-start.6 = (bf16[64,1024]{1,0:T(8,128)(2,1)S(1)}, bf16[64,1024]{1,0:T(8,128)(2,1)S(1)}, u32[]{:S(2)}, u32[]{:S(2)}) collective-permute-start(bf16[64,1024]{1,0:T(8,128)(2,1)S(1)} %get-tuple-element.50.refs_1_), channel_id=1, source_target_pairs={{0,15},{1,2},{2,1},{3,4},{4,3},{5,6},{6,5},{7,8},{8,7},{9,10},{10,... | collective-permute-start | bytes 393224 | tf_op jit(solution)/shard_map/ppermute | solution.py:301
  17.4 0.0 collective-permute-done.5.message_ref.refs_2_
  17.4 2.3 %collective-permute-start.7 = (bf16[64,128]{1,0:T(8,128)(2,1)S(1)}, bf16[64,128]{1,0:T(8,128)(2,1)S(1)}, u32[]{:S(2)}, u32[]{:S(2)}) collective-permute-start(bf16[64,128]{1,0:T(8,128)(2,1)S(1)} %get-tuple-element.53.refs_4_), channel_id=1, source_target_pairs={{0,8},{1,11},{2,10},{3,9},{4,12},{5,15},{6,14},{7,13},{8,0},{9,3},... | collective-permute-start | bytes 49160 | tf_op jit(solution)/shard_map/ppermute | solution.py:317
  19.7 0.6 %collective-permute-start.8 = (bf16[64,128]{1,0:T(8,128)(2,1)S(1)}, bf16[64,128]{1,0:T(8,128)(2,1)S(1)}, u32[]{:S(2)}, u32[]{:S(2)}) collective-permute-start(bf16[64,128]{1,0:T(8,128)(2,1)S(1)} %get-tuple-element.54.refs_5_), channel_id=1, source_target_pairs={{0,9},{1,10},{2,11},{3,8},{4,13},{5,14},{6,15},{7,12},{8,1},{9,2},... | collective-permute-start | bytes 49160 | tf_op jit(solution)/shard_map/ppermute | solution.py:317
  20.3 1.3 %own.3 = (f32[64,1024]{1,0:T(8,128)S(1)}, bf16[4,64,1024]{2,1,0:T(8,128)(2,1)}) custom-call(s32[1]{0:T(128)} %bitcast.index_ref.refs_0_, bf16[64,1024]{1,0:T(8,128)(2,1)S(1)} %get-tuple-element.50.refs_1_, bf16[64,1536]{1,0:T(8,128)(2,1)S(1)} %collective-permute-done.5.message_ref.refs_2_, bf16[36,256,256]{2,1,0:T(8,128)(2,1)S(1)} %get-tuple-element.46.d_ref.refs_3_, ...), custom_call_target="tpu_custom_call" | custom-call | flops 1000000000 | bytes 4194304 | tf_op jit(solution)/shard_map/own/pallas_call | solution.py:238
  21.6 1.1 %collective-permute-done.6.over_ref = bf16[64,1024]{1,0:T(8,128)(2,1)S(1)} collective-permute-done((bf16[64,1024]{1,0:T(8,128)(2,1)S(1)}, bf16[64,1024]{1,0:T(8,128)(2,1)S(1)}, u32[]{:S(2)}, u32[]{:S(2)}) %collective-permute-start.6) | collective-permute-done | bytes 131104 | tf_op jit(solution)/shard_map/ppermute | solution.py:301
  22.7 0.5 %halo.5.refs_1_ = f32[64,1024]{1,0:T(8,128)S(1)} custom-call(s32[1]{0:T(128)} %bitcast.index_ref.refs_0_, f32[64,1024]{1,0:T(8,128)S(1)} %get-tuple-element.55.acc_ref, bf16[64,1024]{1,0:T(8,128)(2,1)S(1)} %collective-permute-done.6.over_ref, bf16[36,256,256]{2,1,0:T(8,128)(2,1)S(1)} %get-tuple-element.46.d_ref.refs_3_), custom_call_target="tpu_custom_call" | custom-call | flops 1000000000 | bytes 4194304 | tf_op jit(solution)/shard_map/halo/pallas_call | solution.py:238
  23.2 0.0 collective-permute-done.7.refs_5_
  23.2 1.6 %collective-permute-done.8.refs_6_ = bf16[64,128]{1,0:T(8,128)(2,1)S(1)} collective-permute-done((bf16[64,128]{1,0:T(8,128)(2,1)S(1)}, bf16[64,128]{1,0:T(8,128)(2,1)S(1)}, u32[]{:S(2)}, u32[]{:S(2)}) %collective-permute-start.8) | collective-permute-done | bytes 16416 | tf_op jit(solution)/shard_map/ppermute | solution.py:317
  24.8 0.7 %finish.4 = (bf16[64,1024]{1,0:T(8,128)(2,1)S(1)}, bf16[64,1536]{1,0:T(8,128)(2,1)S(1)}, f32[64,256]{1,0:T(8,128)S(1)}) custom-call(s32[1]{0:T(128)} %bitcast.index_ref.refs_0_, f32[64,1024]{1,0:T(8,128)S(1)} %halo.5.refs_1_, bf16[256,1024]{1,0:T(8,128)(2,1)S(1)} %get-tuple-element.47.refs_2_.refs_1_, bf16[128,1024]{1,0:T(8,128)(2,1)S(1)} %get-tuple-element.48.refs_3_, ...), custom_call_target="tpu_custom_call" | custom-call | flops 1000000000 | bytes 4194304 | tf_op jit(solution)/shard_map/finish/pallas_call | solution.py:238
  25.5 0.1 collective-permute-start.9
  25.6 1.0 %collective-permute-start.10 = (bf16[64,1024]{1,0:T(8,128)(2,1)S(1)}, bf16[64,1024]{1,0:T(8,128)(2,1)S(1)}, u32[]{:S(2)}, u32[]{:S(2)}) collective-permute-start(bf16[64,1024]{1,0:T(8,128)(2,1)S(1)} %get-tuple-element.56.refs_1_), channel_id=1, source_target_pairs={{0,15},{1,2},{2,1},{3,4},{4,3},{5,6},{6,5},{7,8},{8,7},{9,10},{10,... | collective-permute-start | bytes 393224 | tf_op jit(solution)/shard_map/ppermute | solution.py:301
  26.6 0.4 collective-permute-done.9.message_ref.refs_2_
  27.0 0.6 %collective-permute-start.11 = (bf16[64,128]{1,0:T(8,128)(2,1)S(1)}, bf16[64,128]{1,0:T(8,128)(2,1)S(1)}, u32[]{:S(2)}, u32[]{:S(2)}) collective-permute-start(bf16[64,128]{1,0:T(8,128)(2,1)S(1)} %get-tuple-element.59.refs_4_), channel_id=1, source_target_pairs={{0,8},{1,11},{2,10},{3,9},{4,12},{5,15},{6,14},{7,13},{8,0},{9,3},... | collective-permute-start | bytes 49160 | tf_op jit(solution)/shard_map/ppermute | solution.py:317
  27.6 1.8 %collective-permute-start.12 = (bf16[64,128]{1,0:T(8,128)(2,1)S(1)}, bf16[64,128]{1,0:T(8,128)(2,1)S(1)}, u32[]{:S(2)}, u32[]{:S(2)}) collective-permute-start(bf16[64,128]{1,0:T(8,128)(2,1)S(1)} %get-tuple-element.60.refs_5_), channel_id=1, source_target_pairs={{0,9},{1,10},{2,11},{3,8},{4,13},{5,14},{6,15},{7,12},{8,1},{9,2},... | collective-permute-start | bytes 49160 | tf_op jit(solution)/shard_map/ppermute | solution.py:317
  29.5 1.3 %own.4 = (f32[64,1024]{1,0:T(8,128)S(1)}, bf16[4,64,1024]{2,1,0:T(8,128)(2,1)}) custom-call(s32[1]{0:T(128)} %bitcast.index_ref.refs_0_, bf16[64,1024]{1,0:T(8,128)(2,1)S(1)} %get-tuple-element.56.refs_1_, bf16[64,1536]{1,0:T(8,128)(2,1)S(1)} %collective-permute-done.9.message_ref.refs_2_, ...), custom_call_target="tpu_custom_call", output_to_operand_aliasing={{1}: (6, {})} | custom-call | flops 1000000000 | bytes 4194304 | tf_op jit(solution)/shard_map/own/pallas_call | solution.py:238
  30.8 2.1 %collective-permute-done.10.over_ref = bf16[64,1024]{1,0:T(8,128)(2,1)S(1)} collective-permute-done((bf16[64,1024]{1,0:T(8,128)(2,1)S(1)}, bf16[64,1024]{1,0:T(8,128)(2,1)S(1)}, u32[]{:S(2)}, u32[]{:S(2)}) %collective-permute-start.10) | collective-permute-done | bytes 131104 | tf_op jit(solution)/shard_map/ppermute | solution.py:301
  32.8 0.5 %halo.6.refs_1_ = f32[64,1024]{1,0:T(8,128)S(1)} custom-call(s32[1]{0:T(128)} %bitcast.index_ref.refs_0_, f32[64,1024]{1,0:T(8,128)S(1)} %get-tuple-element.62.acc_ref, bf16[64,1024]{1,0:T(8,128)(2,1)S(1)} %collective-permute-done.10.over_ref, bf16[36,256,256]{2,1,0:T(8,128)(2,1)S(1)} %get-tuple-element.46.d_ref.refs_3_), custom_call_target="tpu_custom_call" | custom-call | flops 1000000000 | bytes 4194304 | tf_op jit(solution)/shard_map/halo/pallas_call | solution.py:238
  33.4 0.0 collective-permute-done.11.refs_5_
  33.4 0.6 %collective-permute-done.12.refs_6_ = bf16[64,128]{1,0:T(8,128)(2,1)S(1)} collective-permute-done((bf16[64,128]{1,0:T(8,128)(2,1)S(1)}, bf16[64,128]{1,0:T(8,128)(2,1)S(1)}, u32[]{:S(2)}, u32[]{:S(2)}) %collective-permute-start.12) | collective-permute-done | bytes 16416 | tf_op jit(solution)/shard_map/ppermute | solution.py:317
  34.0 0.7 %finish.5 = (bf16[64,1024]{1,0:T(8,128)(2,1)S(1)}, bf16[64,1536]{1,0:T(8,128)(2,1)S(1)}, f32[64,256]{1,0:T(8,128)S(1)}) custom-call(s32[1]{0:T(128)} %bitcast.index_ref.refs_0_, f32[64,1024]{1,0:T(8,128)S(1)} %halo.6.refs_1_, bf16[256,1024]{1,0:T(8,128)(2,1)S(1)} %get-tuple-element.47.refs_2_.refs_1_, bf16[128,1024]{1,0:T(8,128)(2,1)S(1)} %get-tuple-element.48.refs_3_, ...), custom_call_target="tpu_custom_call" | custom-call | flops 1000000000 | bytes 4194304 | tf_op jit(solution)/shard_map/finish/pallas_call | solution.py:238
  34.6 0.1 collective-permute-start.13
  34.7 1.6 %collective-permute-start.14 = (bf16[64,1024]{1,0:T(8,128)(2,1)S(1)}, bf16[64,1024]{1,0:T(8,128)(2,1)S(1)}, u32[]{:S(2)}, u32[]{:S(2)}) collective-permute-start(bf16[64,1024]{1,0:T(8,128)(2,1)S(1)} %get-tuple-element.63.refs_1_), channel_id=1, source_target_pairs={{0,15},{1,2},{2,1},{3,4},{4,3},{5,6},{6,5},{7,8},{8,7},{9,10},{10,... | collective-permute-start | bytes 393224 | tf_op jit(solution)/shard_map/ppermute | solution.py:301
  36.4 0.0 collective-permute-done.13.message_ref.refs_2_
  36.4 1.0 %collective-permute-start.15 = (bf16[64,128]{1,0:T(8,128)(2,1)S(1)}, bf16[64,128]{1,0:T(8,128)(2,1)S(1)}, u32[]{:S(2)}, u32[]{:S(2)}) collective-permute-start(bf16[64,128]{1,0:T(8,128)(2,1)S(1)} %get-tuple-element.66.refs_4_), channel_id=1, source_target_pairs={{0,8},{1,11},{2,10},{3,9},{4,12},{5,15},{6,14},{7,13},{8,0},{9,3},... | collective-permute-start | bytes 49160 | tf_op jit(solution)/shard_map/ppermute | solution.py:317
  37.4 1.6 %collective-permute-start.16 = (bf16[64,128]{1,0:T(8,128)(2,1)S(1)}, bf16[64,128]{1,0:T(8,128)(2,1)S(1)}, u32[]{:S(2)}, u32[]{:S(2)}) collective-permute-start(bf16[64,128]{1,0:T(8,128)(2,1)S(1)} %get-tuple-element.67.refs_5_), channel_id=1, source_target_pairs={{0,9},{1,10},{2,11},{3,8},{4,13},{5,14},{6,15},{7,12},{8,1},{9,2},... | collective-permute-start | bytes 49160 | tf_op jit(solution)/shard_map/ppermute | solution.py:317
  39.0 1.3 %own.5 = (f32[64,1024]{1,0:T(8,128)S(1)}, bf16[4,64,1024]{2,1,0:T(8,128)(2,1)}) custom-call(s32[1]{0:T(128)} %bitcast.index_ref.refs_0_, bf16[64,1024]{1,0:T(8,128)(2,1)S(1)} %get-tuple-element.63.refs_1_, bf16[64,1536]{1,0:T(8,128)(2,1)S(1)} %collective-permute-done.13.message_ref.refs_2_, ...), custom_call_target="tpu_custom_call", output_to_operand_aliasing={{1}: (6, {})} | custom-call | flops 1000000000 | bytes 4194304 | tf_op jit(solution)/shard_map/own/pallas_call | solution.py:238
  40.3 1.8 %collective-permute-done.14.over_ref = bf16[64,1024]{1,0:T(8,128)(2,1)S(1)} collective-permute-done((bf16[64,1024]{1,0:T(8,128)(2,1)S(1)}, bf16[64,1024]{1,0:T(8,128)(2,1)S(1)}, u32[]{:S(2)}, u32[]{:S(2)}) %collective-permute-start.14) | collective-permute-done | bytes 131104 | tf_op jit(solution)/shard_map/ppermute | solution.py:301
  42.2 0.5 %halo.7.refs_0_ = f32[64,1024]{1,0:T(8,128)S(1)} custom-call(s32[1]{0:T(128)} %bitcast.index_ref.refs_0_, f32[64,1024]{1,0:T(8,128)S(1)} %get-tuple-element.69.acc_ref, bf16[64,1024]{1,0:T(8,128)(2,1)S(1)} %collective-permute-done.14.over_ref, bf16[36,256,256]{2,1,0:T(8,128)(2,1)S(1)} %get-tuple-element.46.d_ref.refs_3_), custom_call_target="tpu_custom_call" | custom-call | flops 1000000000 | bytes 4194304 | tf_op jit(solution)/shard_map/halo/pallas_call | solution.py:238
  42.7 0.0 collective-permute-done.15.refs_2_
  42.7 0.6 %collective-permute-done.16.refs_3_ = bf16[64,128]{1,0:T(8,128)(2,1)S(1)} collective-permute-done((bf16[64,128]{1,0:T(8,128)(2,1)S(1)}, bf16[64,128]{1,0:T(8,128)(2,1)S(1)}, u32[]{:S(2)}, u32[]{:S(2)}) %collective-permute-start.16) | collective-permute-done | bytes 16416 | tf_op jit(solution)/shard_map/ppermute | solution.py:317
  43.3 0.9 %last.1 = bf16[4,64,1024]{2,1,0:T(8,128)(2,1)} custom-call(f32[64,1024]{1,0:T(8,128)S(1)} %halo.7.refs_0_, bf16[256,1024]{1,0:T(8,128)(2,1)S(1)} %get-tuple-element.47.refs_2_.refs_1_, bf16[64,128]{1,0:T(8,128)(2,1)S(1)} %collective-permute-done.15.refs_2_, bf16[64,128]{1,0:T(8,128)(2,1)S(1)} %collective-permute-done.16.refs_3_, ...), custom_call_target="tpu_custom_call", output_to_operand_aliasing={{}: (4, {})} | custom-call | flops 1000000000 | bytes 4194304 | tf_op jit(solution)/shard_map/last/pallas_call | solution.py:238
  (4 shorter events, 0.1 us)
Async XLA Ops:
  0.0 9.6 %collective-permute-start = (bf16[64,1024]{1,0:T(8,128)(2,1)}, bf16[64,1024]{1,0:T(8,128)(2,1)S(1)}, u32[]{:S(2)}, u32[]{:S(2)}) collective-permute-start(bf16[64,1024]{1,0:T(8,128)(2,1)} %refs_4_.1), channel_id=1, source_target_pairs={{0,1},{1,0},{2,3},{3,2},{4,5},{5,4},{6,7},{7,6},{8,9},{9,8},{10,11... | collective-permute-start | bytes 393224 | tf_op jit(solution)/shard_map/ppermute | solution.py:280
  0.5 11.1 %collective-permute-start.2 = (bf16[64,1024]{1,0:T(8,128)(2,1)}, bf16[64,1024]{1,0:T(8,128)(2,1)S(1)}, u32[]{:S(2)}, u32[]{:S(2)}) collective-permute-start(bf16[64,1024]{1,0:T(8,128)(2,1)} %refs_4_.1), channel_id=1, source_target_pairs={{0,15},{1,2},{2,1},{3,4},{4,3},{5,6},{6,5},{7,8},{8,7},{9,10},{10,... | collective-permute-start | bytes 393224 | tf_op jit(solution)/shard_map/ppermute | solution.py:281
  6.1 3.5 %copy-start = (bf16[32,256,256]{2,1,0:T(8,128)(2,1)S(1)}, bf16[32,256,256]{2,1,0:T(8,128)(2,1)}, u32[]{:S(2)}) copy-start(bf16[32,256,256]{2,1,0:T(8,128)(2,1)} %refs_6_.3) | copy-start | bytes 12582916
  6.1 3.5 %copy-start.1 = (bf16[4,32,256]{2,1,0:T(8,128)(2,1)S(1)}, bf16[4,32,256]{2,1,0:T(8,128)(2,1)}, u32[]{:S(2)}) copy-start(bf16[4,32,256]{2,1,0:T(8,128)(2,1)} %refs_5_.3) | copy-start | bytes 196612
  8.0 1.3 %collective-permute-start.1 = (bf16[64,512]{1,0:T(8,128)(2,1)S(1)}, bf16[64,512]{1,0:T(8,128)(2,1)S(1)}, u32[]{:S(2)}, u32[]{:S(2)}) collective-permute-start(bf16[64,512]{1,0:T(8,128)(2,1)S(1)} %get-tuple-element.42), channel_id=1, source_target_pairs={{0,1},{1,0},{2,3},{3,2},{4,5},{5,4},{6,7},{7,6},{8,9},{9,8},{10,11... | collective-permute-start | bytes 196616 | tf_op jit(solution)/shard_map/ppermute | solution.py:304
  9.4 5.0 %collective-permute-start.3 = (bf16[64,128]{1,0:T(8,128)(2,1)S(1)}, bf16[64,128]{1,0:T(8,128)(2,1)S(1)}, u32[]{:S(2)}, u32[]{:S(2)}) collective-permute-start(bf16[64,128]{1,0:T(8,128)(2,1)S(1)} %get-tuple-element.43.refs_7_), channel_id=1, source_target_pairs={{0,8},{1,11},{2,10},{3,9},{4,12},{5,15},{6,14},{7,13},{8,0},{9,3},... | collective-permute-start | bytes 49160 | tf_op jit(solution)/shard_map/ppermute | solution.py:317
  9.4 5.0 %collective-permute-start.4 = (bf16[64,128]{1,0:T(8,128)(2,1)S(1)}, bf16[64,128]{1,0:T(8,128)(2,1)S(1)}, u32[]{:S(2)}, u32[]{:S(2)}) collective-permute-start(bf16[64,128]{1,0:T(8,128)(2,1)S(1)} %get-tuple-element.44.refs_8_), channel_id=1, source_target_pairs={{0,9},{1,10},{2,11},{3,8},{4,13},{5,14},{6,15},{7,12},{8,1},{9,2},... | collective-permute-start | bytes 49160 | tf_op jit(solution)/shard_map/ppermute | solution.py:317
  15.1 2.2 %collective-permute-start.5 = (bf16[64,1536]{1,0:T(8,128)(2,1)S(1)}, bf16[64,1536]{1,0:T(8,128)(2,1)S(1)}, u32[]{:S(2)}, u32[]{:S(2)}) collective-permute-start(bf16[64,1536]{1,0:T(8,128)(2,1)S(1)} %get-tuple-element.51), channel_id=1, source_target_pairs={{0,1},{1,0},{2,3},{3,2},{4,5},{5,4},{6,7},{7,6},{8,9},{9,8},{10,11... | collective-permute-start | bytes 589832 | tf_op jit(solution)/shard_map/ppermute | solution.py:302
  15.3 7.4 %collective-permute-start.6 = (bf16[64,1024]{1,0:T(8,128)(2,1)S(1)}, bf16[64,1024]{1,0:T(8,128)(2,1)S(1)}, u32[]{:S(2)}, u32[]{:S(2)}) collective-permute-start(bf16[64,1024]{1,0:T(8,128)(2,1)S(1)} %get-tuple-element.50.refs_1_), channel_id=1, source_target_pairs={{0,15},{1,2},{2,1},{3,4},{4,3},{5,6},{6,5},{7,8},{8,7},{9,10},{10,... | collective-permute-start | bytes 393224 | tf_op jit(solution)/shard_map/ppermute | solution.py:301
  17.4 5.8 %collective-permute-start.7 = (bf16[64,128]{1,0:T(8,128)(2,1)S(1)}, bf16[64,128]{1,0:T(8,128)(2,1)S(1)}, u32[]{:S(2)}, u32[]{:S(2)}) collective-permute-start(bf16[64,128]{1,0:T(8,128)(2,1)S(1)} %get-tuple-element.53.refs_4_), channel_id=1, source_target_pairs={{0,8},{1,11},{2,10},{3,9},{4,12},{5,15},{6,14},{7,13},{8,0},{9,3},... | collective-permute-start | bytes 49160 | tf_op jit(solution)/shard_map/ppermute | solution.py:317
  19.7 5.1 %collective-permute-start.8 = (bf16[64,128]{1,0:T(8,128)(2,1)S(1)}, bf16[64,128]{1,0:T(8,128)(2,1)S(1)}, u32[]{:S(2)}, u32[]{:S(2)}) collective-permute-start(bf16[64,128]{1,0:T(8,128)(2,1)S(1)} %get-tuple-element.54.refs_5_), channel_id=1, source_target_pairs={{0,9},{1,10},{2,11},{3,8},{4,13},{5,14},{6,15},{7,12},{8,1},{9,2},... | collective-permute-start | bytes 49160 | tf_op jit(solution)/shard_map/ppermute | solution.py:317
  25.5 1.5 %collective-permute-start.9 = (bf16[64,1536]{1,0:T(8,128)(2,1)S(1)}, bf16[64,1536]{1,0:T(8,128)(2,1)S(1)}, u32[]{:S(2)}, u32[]{:S(2)}) collective-permute-start(bf16[64,1536]{1,0:T(8,128)(2,1)S(1)} %get-tuple-element.57), channel_id=1, source_target_pairs={{0,1},{1,0},{2,3},{3,2},{4,5},{5,4},{6,7},{7,6},{8,9},{9,8},{10,11... | collective-permute-start | bytes 589832 | tf_op jit(solution)/shard_map/ppermute | solution.py:302
  25.6 7.3 %collective-permute-start.10 = (bf16[64,1024]{1,0:T(8,128)(2,1)S(1)}, bf16[64,1024]{1,0:T(8,128)(2,1)S(1)}, u32[]{:S(2)}, u32[]{:S(2)}) collective-permute-start(bf16[64,1024]{1,0:T(8,128)(2,1)S(1)} %get-tuple-element.56.refs_1_), channel_id=1, source_target_pairs={{0,15},{1,2},{2,1},{3,4},{4,3},{5,6},{6,5},{7,8},{8,7},{9,10},{10,... | collective-permute-start | bytes 393224 | tf_op jit(solution)/shard_map/ppermute | solution.py:301
  27.0 6.3 %collective-permute-start.11 = (bf16[64,128]{1,0:T(8,128)(2,1)S(1)}, bf16[64,128]{1,0:T(8,128)(2,1)S(1)}, u32[]{:S(2)}, u32[]{:S(2)}) collective-permute-start(bf16[64,128]{1,0:T(8,128)(2,1)S(1)} %get-tuple-element.59.refs_4_), channel_id=1, source_target_pairs={{0,8},{1,11},{2,10},{3,9},{4,12},{5,15},{6,14},{7,13},{8,0},{9,3},... | collective-permute-start | bytes 49160 | tf_op jit(solution)/shard_map/ppermute | solution.py:317
  27.6 6.3 %collective-permute-start.12 = (bf16[64,128]{1,0:T(8,128)(2,1)S(1)}, bf16[64,128]{1,0:T(8,128)(2,1)S(1)}, u32[]{:S(2)}, u32[]{:S(2)}) collective-permute-start(bf16[64,128]{1,0:T(8,128)(2,1)S(1)} %get-tuple-element.60.refs_5_), channel_id=1, source_target_pairs={{0,9},{1,10},{2,11},{3,8},{4,13},{5,14},{6,15},{7,12},{8,1},{9,2},... | collective-permute-start | bytes 49160 | tf_op jit(solution)/shard_map/ppermute | solution.py:317
  34.6 1.7 %collective-permute-start.13 = (bf16[64,1536]{1,0:T(8,128)(2,1)S(1)}, bf16[64,1536]{1,0:T(8,128)(2,1)S(1)}, u32[]{:S(2)}, u32[]{:S(2)}) collective-permute-start(bf16[64,1536]{1,0:T(8,128)(2,1)S(1)} %get-tuple-element.64), channel_id=1, source_target_pairs={{0,1},{1,0},{2,3},{3,2},{4,5},{5,4},{6,7},{7,6},{8,9},{9,8},{10,11... | collective-permute-start | bytes 589832 | tf_op jit(solution)/shard_map/ppermute | solution.py:302
  34.7 7.4 %collective-permute-start.14 = (bf16[64,1024]{1,0:T(8,128)(2,1)S(1)}, bf16[64,1024]{1,0:T(8,128)(2,1)S(1)}, u32[]{:S(2)}, u32[]{:S(2)}) collective-permute-start(bf16[64,1024]{1,0:T(8,128)(2,1)S(1)} %get-tuple-element.63.refs_1_), channel_id=1, source_target_pairs={{0,15},{1,2},{2,1},{3,4},{4,3},{5,6},{6,5},{7,8},{8,7},{9,10},{10,... | collective-permute-start | bytes 393224 | tf_op jit(solution)/shard_map/ppermute | solution.py:301
  36.4 6.3 %collective-permute-start.15 = (bf16[64,128]{1,0:T(8,128)(2,1)S(1)}, bf16[64,128]{1,0:T(8,128)(2,1)S(1)}, u32[]{:S(2)}, u32[]{:S(2)}) collective-permute-start(bf16[64,128]{1,0:T(8,128)(2,1)S(1)} %get-tuple-element.66.refs_4_), channel_id=1, source_target_pairs={{0,8},{1,11},{2,10},{3,9},{4,12},{5,15},{6,14},{7,13},{8,0},{9,3},... | collective-permute-start | bytes 49160 | tf_op jit(solution)/shard_map/ppermute | solution.py:317
  37.4 5.9 %collective-permute-start.16 = (bf16[64,128]{1,0:T(8,128)(2,1)S(1)}, bf16[64,128]{1,0:T(8,128)(2,1)S(1)}, u32[]{:S(2)}, u32[]{:S(2)}) collective-permute-start(bf16[64,128]{1,0:T(8,128)(2,1)S(1)} %get-tuple-element.67.refs_5_), channel_id=1, source_target_pairs={{0,9},{1,10},{2,11},{3,8},{4,13},{5,14},{6,15},{7,12},{8,1},{9,2},... | collective-permute-start | bytes 49160 | tf_op jit(solution)/shard_map/ppermute | solution.py:317

commit v13 on v12

--- a/solution.py
+++ b/solution.py
@@ -48,7 +48,7 @@
         self.block_clusters = self.per_device * members
         distances = [d % loop_size for d in (2, loop_size - 2, loop_size // 2)]
         self.hops = sorted(set(distances))
-        self.sets = [[i for i, d in enumerate(distances) if d == hop] for hop in self.hops]
+        self.set_of = [self.hops.index(d) for d in distances]
         self.paired = len(self.hops) == 1 and 2 * self.hops[0] == loop_size and members == 4
         devices = members * loop_size
         self.near = [(i, i ^ 1) for i in range(devices)]
@@ -75,7 +75,8 @@
 
     def send_far(self, index_ref, x, cb_ref, g_ref, out_refs):
         coeffs = dot_nt(x, cb_ref[...]).astype(BF16)
-        totals = [sum(dot_nt(coeffs, g_ref[level]) for level in levels) for levels in self.sets]
+        twice = jnp.concatenate([coeffs, coeffs], axis=1)
+        totals = [dot_nt(twice, g_ref[index]) for index in range(len(self.hops))]
         if not self.paired:
             for i, out_ref in enumerate(out_refs):
                 step = i % self.members * self.width
@@ -141,8 +142,7 @@
 
 def prepare_kernel(plan, index_ref, *refs):
     sources, refs = refs[:7], refs[7:]
-    x_ref, g_ref, cb_ref, near_ref, offsets_ref = refs[:5]
-    sends, (rows_ref, cols_ref, col_ref, coup_ref, sems) = refs[5:-5], refs[-5:]
+    x_ref, g_ref, cb_ref, near_ref, offsets_ref, rows_ref, cols_ref, col_ref, coup_ref, sum_ref, sems = refs
     targets = (near_ref, offsets_ref, rows_ref, cols_ref, x_ref, col_ref, coup_ref)
     copies = [
         pltpu.make_async_copy(source, target, sems.at[i])
@@ -152,7 +152,7 @@
         copy.start()
     rank, size = plan.rank, plan.size
     cb_ref[...] = jnp.zeros_like(cb_ref)
-    g_ref[...] = jnp.zeros_like(g_ref)
+    sum_ref[...] = jnp.zeros_like(sum_ref)
     for copy in copies:
         copy.wait()
     for c in range(plan.per_device):
@@ -160,15 +160,26 @@
     column = lax.broadcasted_iota(jnp.int32, (rank, plan.width), 1) // rank
     shift = 0 if plan.paired else plan.member(index_ref)
     for s in range(plan.slots):
-        level = lax.div(rows_ref[s], plan.block_clusters)
         row = lax.rem(rows_ref[s], plan.block_clusters)
         step = lax.rem(lax.div(row, plan.per_device) - shift + plan.members, plan.members)
         place = step * plan.per_device + lax.rem(row, plan.per_device)
-        where = (level, pl.ds(pl.multiple_of(place * rank, rank), rank), slice(None))
+        if len(plan.hops) > 1:
+            level = lax.div(rows_ref[s], plan.block_clusters)
+            index = sum(jnp.where(level == i, index, 0) for i, index in enumerate(plan.set_of))
+        else:
+            index = 0
+        where = (index, pl.ds(pl.multiple_of(place * rank, rank), rank), slice(None))
         tile = coup_ref[s].astype(F32)
         wide = jnp.where(column == cols_ref[s], jnp.concatenate([tile] * plan.per_device, axis=1), 0.0)
-        g_ref[where] = g_ref[where] + wide.astype(BF16)
-    plan.send_far(index_ref, x_ref[...], cb_ref, g_ref, sends)
+        sum_ref[where] = sum_ref[where] + wide
+    for index in range(len(plan.hops)):
+        g_ref[index] = jnp.concatenate(halves(sum_ref[index]), axis=1)
+
+
+def first_far_kernel(plan, index_ref, x_ref, cb_ref, g_ref, copy_ref, *out_refs):
+    x = x_ref[...]
+    plan.send_far(index_ref, x, cb_ref, g_ref, out_refs)
+    copy_ref[...] = x
 
 
 def relay_kernel(plan, index_ref, keep_ref, message_ref, *out_refs):
@@ -277,31 +288,38 @@
     current, sends, krylov = block, None, None
     for product in range(PRODUCTS):
         if product == 0:
-            near = lax.ppermute(block, axes, plan.near)
-            over = lax.ppermute(block, axes, plan.over)
             ins = [near_rows, near_offsets, far_rows, far_cols, block, col_basis, couplings]
-            current, coupled, col_wide, row_slots, offset_slots, *sends = call(
+            matrix = (len(plan.hops), plan.members * width, 2 * width)
+            current, coupled, col_wide, row_slots, offset_slots = call(
                 functools.partial(prepare_kernel, plan),
                 "prepare",
                 [index, *ins],
                 [IN_SMEM] + [IN_HBM] * 7,
                 [
                     block_out,
-                    pltpu.VMEM((LEVELS, plan.members * width, width), BF16),
+                    pltpu.VMEM(matrix, BF16),
                     pltpu.VMEM((width, shard_len), BF16),
                     *scratch_for(near_rows, near_offsets),
-                    *first_out,
                 ],
-                [IN_VMEM] * 3 + [IN_SMEM] * 2 + [IN_VMEM] * len(sends_out),
+                [IN_VMEM] * 3 + [IN_SMEM] * 2,
                 scratch=scratch_for(far_rows, far_cols, col_basis, couplings)
-                + [pltpu.SemaphoreType.DMA((7,))],
+                + [pltpu.VMEM(matrix[:2] + (width,), F32), pltpu.SemaphoreType.DMA((7,))],
+            )
+            over = lax.ppermute(current, axes, plan.over)
+            current, *sends = call(
+                functools.partial(first_far_kernel, plan),
+                "first_far",
+                [index, current, col_wide, coupled],
+                [IN_SMEM] + [IN_VMEM] * 3,
+                [block_out, *first_out],
                 cost=LONG,
             )
         if product > 0:
             over = lax.ppermute(current, axes, plan.over)
             near = message = lax.ppermute(sends[0] if plan.paired else current, axes, plan.near)
-        elif plan.paired:
-            message = lax.ppermute(sends[0], axes, plan.near)
+        else:
+            message = lax.ppermute(sends[0], axes, plan.near) if plan.paired else None
+            near = lax.ppermute(current, axes, plan.near)
         if plan.paired:
             sends = call(
                 functools.partial(relay_kernel, plan),

time: 44.3 us -> 44.1 us (level)
    ppermute x3 -> x4, starting transfers between devices: 4.72 us -> 13 us  [on_device(): over = lax.ppermute(current, axes, plan.over)]
    ppermute x3 -> x2, starting transfers between devices: 6.16 us -> 0.52 us  [the longest x1 0.52 us: on_device(): near = lax.ppermute(current, axes, plan.near)]
    ppermute x8, starting transfers between devices: 8.25 us -> 6.1 us  [on_device(): fars = [lax.ppermute(s, axes, route) for s, route in zip(sends, routes)]]
    pallas_call x17 -> x18, Pallas kernels: 12.7 us -> 12.4 us  [call(): pl.pallas_call(kernel, in_specs=list(specs), out_specs=out_specs or [IN_V...]
    ppermute x3 -> x2, waiting for transfers between devices: 1.25 us -> 1.25 us  [the longest x1 1.25 us: on_device(): message = lax.ppermute(sends[0], axes, plan.near) if plan.paired else None]
    ppermute x3 -> x4, waiting for transfers between devices: 4.97 us -> 4.98 us  [on_device(): over = lax.ppermute(current, axes, plan.over)]
  transfers between devices with their start and end apart: 17 -> 17, of which waited for: 10 -> 9; matrix products, arithmetic and copies ran while one was open for 0% -> 0% of each run, Pallas kernels for 22% -> 18%
where the time goes in v13:
time: 44.1 us; the launch traced here: 43.9 us
  starting transfers between devices  19.9 us (45%)
  Pallas kernels  12.4 us (28%)
  waiting for transfers between devices  11.4 us (26%)
    ppermute x4, starting transfers between devices, on_device(): over = lax.ppermute(current, axes, plan.over)  13 us
    pallas_call x18, Pallas kernels, call(): pl.pallas_call(kernel, in_specs=list(specs), out_specs=out_specs or [IN_V...  12.4 us
    ppermute x8, starting transfers between devices, on_device(): fars = [lax.ppermute(s, axes, route) for s, route in zip(sends, routes)]  6.1 us
    ppermute x8, waiting for transfers between devices, on_device(): fars = [lax.ppermute(s, axes, route) for s, route in zip(sends, routes)]  5.12 us
    ppermute x4, waiting for transfers between devices, on_device(): over = lax.ppermute(current, axes, plan.over)  4.98 us
    ppermute x1, waiting for transfers between devices, on_device(): message = lax.ppermute(sends[0], axes, plan.near) if plan.paired else None  1.25 us
  transfers between devices with their start and end apart: 17, of which 9 were waited for; matrix products, arithmetic and copies ran while one was open for 0% of the time, Pallas kernels for 18%

profile of v13, /device:TPU:0, one launch (start us, length us, event | category | flops | bytes accessed | tf_op | source)
XLA Modules:
  0.0 43.9 jit_solution(7906652923503063948)
XLA Ops:
  0.0 1.5 %prepare.1 = (bf16[64,1024]{1,0:T(8,128)(2,1)S(1)}, bf16[1,512,256]{2,1,0:T(8,128)(2,1)S(1)}, bf16[128,1024]{1,0:T(8,128)(2,1)S(1)}, s32[32]{0:T(128)S(4)}, s32[32]{0:T(128)S(4)}) custom-call(s32[1]{0:T(128)} %bitcast.index_ref.refs_0_, s32[32]{0:T(128)} %refs_0_.1, s32[32]{0:T(128)} %refs_1_.1, s32[32]{0:T(128)} %refs_2_.1, s32[32]{0:T(128)} %refs_3_.1, ...), custom_call_target="tpu_custom_call" | custom-call | flops 1000000000 | bytes 4194304 | tf_op jit(solution)/shard_map/prepare/pallas_call | solution.py:249
  1.5 0.0 copy-start
  1.5 0.0 copy-start.1
  1.5 0.5 %first_far.1 = (bf16[64,1024]{1,0:T(8,128)(2,1)S(1)}, bf16[64,512]{1,0:T(8,128)(2,1)S(1)}, f32[64,256]{1,0:T(8,128)S(1)}) custom-call(s32[1]{0:T(128)} %bitcast.index_ref.refs_0_, bf16[64,1024]{1,0:T(8,128)(2,1)S(1)} %get-tuple-element.41.x_ref, bf16[128,1024]{1,0:T(8,128)(2,1)S(1)} %get-tuple-element.42.cb_ref.refs_3_, ...), custom_call_target="tpu_custom_call" | custom-call | flops 4000000000 | bytes 4194304 | tf_op jit(solution)/shard_map/first_far/pallas_call | solution.py:249
  2.0 0.5 %collective-permute-start = (bf16[64,1024]{1,0:T(8,128)(2,1)S(1)}, bf16[64,1024]{1,0:T(8,128)(2,1)S(1)}, u32[]{:S(2)}, u32[]{:S(2)}) collective-permute-start(bf16[64,1024]{1,0:T(8,128)(2,1)S(1)} %get-tuple-element.44.refs_3_), channel_id=1, source_target_pairs={{0,1},{1,0},{2,3},{3,2},{4,5},{5,4},{6,7},{7,6},{8,9},{9,8},{10,11... | collective-permute-start | bytes 393224 | tf_op jit(solution)/shard_map/ppermute | solution.py:322
  2.5 5.6 %collective-permute-start.2 = (bf16[64,1024]{1,0:T(8,128)(2,1)S(1)}, bf16[64,1024]{1,0:T(8,128)(2,1)S(1)}, u32[]{:S(2)}, u32[]{:S(2)}) collective-permute-start(bf16[64,1024]{1,0:T(8,128)(2,1)S(1)} %get-tuple-element.41.x_ref), channel_id=1, source_target_pairs={{0,15},{1,2},{2,1},{3,4},{4,3},{5,6},{6,5},{7,8},{8,7},{9,10},{10,... | collective-permute-start | bytes 393224 | tf_op jit(solution)/shard_map/ppermute | solution.py:308
  8.2 0.0 collective-permute-start.1
  8.2 1.3 %collective-permute-done.1.message_ref = bf16[64,512]{1,0:T(8,128)(2,1)S(1)} collective-permute-done((bf16[64,512]{1,0:T(8,128)(2,1)S(1)}, bf16[64,512]{1,0:T(8,128)(2,1)S(1)}, u32[]{:S(2)}, u32[]{:S(2)}) %collective-permute-start.1) | collective-permute-done | bytes 65568 | tf_op jit(solution)/shard_map/ppermute | solution.py:321
  9.4 0.1 collective-permute-start.3
  9.5 0.3 collective-permute-start.4
  9.8 0.0 collective-permute-done.refs_4_
  9.8 0.0 copy-done
  9.8 0.0 copy-done.1
  9.8 1.9 %first_own.1 = (f32[64,1024]{1,0:T(8,128)S(1)}, bf16[36,256,256]{2,1,0:T(8,128)(2,1)S(1)}, bf16[256,1024]{1,0:T(8,128)(2,1)S(1)}) custom-call(s32[1]{0:T(128)} %bitcast.index_ref.refs_0_, s32[32]{0:T(128)S(4)} %get-tuple-element.39.refs_1_, s32[32]{0:T(128)S(4)} %get-tuple-element.40.refs_2_, bf16[64,1024]{1,0:T(8,128)(2,1)S(1)} %get-tuple-element.44.refs_3_, ...), custom_call_target="tpu_custom_call" | custom-call | flops 1000000 | bytes 8388608 | tf_op jit(solution)/shard_map/first_own/pallas_call | solution.py:249
  11.7 0.0 collective-permute-done.2.over_ref
  11.7 0.5 %halo.4.refs_1_ = f32[64,1024]{1,0:T(8,128)S(1)} custom-call(s32[1]{0:T(128)} %bitcast.index_ref.refs_0_, f32[64,1024]{1,0:T(8,128)S(1)} %get-tuple-element.49.acc_ref, bf16[64,1024]{1,0:T(8,128)(2,1)S(1)} %collective-permute-done.2.over_ref, bf16[36,256,256]{2,1,0:T(8,128)(2,1)S(1)} %get-tuple-element.50.d_ref.refs_3_), custom_call_target="tpu_custom_call" | custom-call | flops 1000000 | bytes 65536 | tf_op jit(solution)/shard_map/halo/pallas_call | solution.py:249
  12.2 2.2 %collective-permute-done.3.refs_5_ = bf16[64,128]{1,0:T(8,128)(2,1)S(1)} collective-permute-done((bf16[64,128]{1,0:T(8,128)(2,1)S(1)}, bf16[64,128]{1,0:T(8,128)(2,1)S(1)}, u32[]{:S(2)}, u32[]{:S(2)}) %collective-permute-start.3) | collective-permute-done | bytes 16416 | tf_op jit(solution)/shard_map/ppermute | solution.py:335
  14.4 0.1 collective-permute-done.4.refs_6_
  14.5 0.6 %finish.3 = (bf16[64,1024]{1,0:T(8,128)(2,1)S(1)}, bf16[64,1536]{1,0:T(8,128)(2,1)S(1)}, f32[64,256]{1,0:T(8,128)S(1)}) custom-call(s32[1]{0:T(128)} %bitcast.index_ref.refs_0_, f32[64,1024]{1,0:T(8,128)S(1)} %halo.4.refs_1_, bf16[256,1024]{1,0:T(8,128)(2,1)S(1)} %get-tuple-element.51.refs_2_.refs_1_, ...), custom_call_target="tpu_custom_call" | custom-call | flops 1000000000 | bytes 4194304 | tf_op jit(solution)/shard_map/finish/pallas_call | solution.py:249
  15.1 0.2 collective-permute-start.5
  15.3 2.6 %collective-permute-start.6 = (bf16[64,1024]{1,0:T(8,128)(2,1)S(1)}, bf16[64,1024]{1,0:T(8,128)(2,1)S(1)}, u32[]{:S(2)}, u32[]{:S(2)}) collective-permute-start(bf16[64,1024]{1,0:T(8,128)(2,1)S(1)} %get-tuple-element.52.refs_1_), channel_id=1, source_target_pairs={{0,15},{1,2},{2,1},{3,4},{4,3},{5,6},{6,5},{7,8},{8,7},{9,10},{10,... | collective-permute-start | bytes 393224 | tf_op jit(solution)/shard_map/ppermute | solution.py:318
  17.9 0.0 collective-permute-done.5.message_ref.refs_2_
  17.9 1.7 %collective-permute-start.7 = (bf16[64,128]{1,0:T(8,128)(2,1)S(1)}, bf16[64,128]{1,0:T(8,128)(2,1)S(1)}, u32[]{:S(2)}, u32[]{:S(2)}) collective-permute-start(bf16[64,128]{1,0:T(8,128)(2,1)S(1)} %get-tuple-element.55.refs_4_), channel_id=1, source_target_pairs={{0,8},{1,11},{2,10},{3,9},{4,12},{5,15},{6,14},{7,13},{8,0},{9,3},... | collective-permute-start | bytes 49160 | tf_op jit(solution)/shard_map/ppermute | solution.py:335
  19.7 0.6 %collective-permute-start.8 = (bf16[64,128]{1,0:T(8,128)(2,1)S(1)}, bf16[64,128]{1,0:T(8,128)(2,1)S(1)}, u32[]{:S(2)}, u32[]{:S(2)}) collective-permute-start(bf16[64,128]{1,0:T(8,128)(2,1)S(1)} %get-tuple-element.56.refs_5_), channel_id=1, source_target_pairs={{0,9},{1,10},{2,11},{3,8},{4,13},{5,14},{6,15},{7,12},{8,1},{9,2},... | collective-permute-start | bytes 49160 | tf_op jit(solution)/shard_map/ppermute | solution.py:335
  20.3 1.3 %own.3 = (f32[64,1024]{1,0:T(8,128)S(1)}, bf16[4,64,1024]{2,1,0:T(8,128)(2,1)}) custom-call(s32[1]{0:T(128)} %bitcast.index_ref.refs_0_, bf16[64,1024]{1,0:T(8,128)(2,1)S(1)} %get-tuple-element.52.refs_1_, bf16[64,1536]{1,0:T(8,128)(2,1)S(1)} %collective-permute-done.5.message_ref.refs_2_, bf16[36,256,256]{2,1,0:T(8,128)(2,1)S(1)} %get-tuple-element.50.d_ref.refs_3_, ...), custom_call_target="tpu_custom_call" | custom-call | flops 1000000000 | bytes 4194304 | tf_op jit(solution)/shard_map/own/pallas_call | solution.py:249
  21.6 1.1 %collective-permute-done.6.over_ref = bf16[64,1024]{1,0:T(8,128)(2,1)S(1)} collective-permute-done((bf16[64,1024]{1,0:T(8,128)(2,1)S(1)}, bf16[64,1024]{1,0:T(8,128)(2,1)S(1)}, u32[]{:S(2)}, u32[]{:S(2)}) %collective-permute-start.6) | collective-permute-done | bytes 131104 | tf_op jit(solution)/shard_map/ppermute | solution.py:318
  22.7 0.5 %halo.5.refs_1_ = f32[64,1024]{1,0:T(8,128)S(1)} custom-call(s32[1]{0:T(128)} %bitcast.index_ref.refs_0_, f32[64,1024]{1,0:T(8,128)S(1)} %get-tuple-element.57.acc_ref, bf16[64,1024]{1,0:T(8,128)(2,1)S(1)} %collective-permute-done.6.over_ref, bf16[36,256,256]{2,1,0:T(8,128)(2,1)S(1)} %get-tuple-element.50.d_ref.refs_3_), custom_call_target="tpu_custom_call" | custom-call | flops 1000000000 | bytes 4194304 | tf_op jit(solution)/shard_map/halo/pallas_call | solution.py:249
  23.2 0.0 collective-permute-done.7.refs_5_
  23.2 1.6 %collective-permute-done.8.refs_6_ = bf16[64,128]{1,0:T(8,128)(2,1)S(1)} collective-permute-done((bf16[64,128]{1,0:T(8,128)(2,1)S(1)}, bf16[64,128]{1,0:T(8,128)(2,1)S(1)}, u32[]{:S(2)}, u32[]{:S(2)}) %collective-permute-start.8) | collective-permute-done | bytes 16416 | tf_op jit(solution)/shard_map/ppermute | solution.py:335
  24.8 0.6 %finish.4 = (bf16[64,1024]{1,0:T(8,128)(2,1)S(1)}, bf16[64,1536]{1,0:T(8,128)(2,1)S(1)}, f32[64,256]{1,0:T(8,128)S(1)}) custom-call(s32[1]{0:T(128)} %bitcast.index_ref.refs_0_, f32[64,1024]{1,0:T(8,128)S(1)} %halo.5.refs_1_, bf16[256,1024]{1,0:T(8,128)(2,1)S(1)} %get-tuple-element.51.refs_2_.refs_1_, ...), custom_call_target="tpu_custom_call" | custom-call | flops 1000000000 | bytes 4194304 | tf_op jit(solution)/shard_map/finish/pallas_call | solution.py:249
  25.4 0.1 collective-permute-start.9
  25.4 2.1 %collective-permute-start.10 = (bf16[64,1024]{1,0:T(8,128)(2,1)S(1)}, bf16[64,1024]{1,0:T(8,128)(2,1)S(1)}, u32[]{:S(2)}, u32[]{:S(2)}) collective-permute-start(bf16[64,1024]{1,0:T(8,128)(2,1)S(1)} %get-tuple-element.58.refs_1_), channel_id=1, source_target_pairs={{0,15},{1,2},{2,1},{3,4},{4,3},{5,6},{6,5},{7,8},{8,7},{9,10},{10,... | collective-permute-start | bytes 393224 | tf_op jit(solution)/shard_map/ppermute | solution.py:318
  27.6 0.0 collective-permute-done.9.message_ref.refs_2_
  27.6 0.5 %collective-permute-start.11 = (bf16[64,128]{1,0:T(8,128)(2,1)S(1)}, bf16[64,128]{1,0:T(8,128)(2,1)S(1)}, u32[]{:S(2)}, u32[]{:S(2)}) collective-permute-start(bf16[64,128]{1,0:T(8,128)(2,1)S(1)} %get-tuple-element.61.refs_4_), channel_id=1, source_target_pairs={{0,8},{1,11},{2,10},{3,9},{4,12},{5,15},{6,14},{7,13},{8,0},{9,3},... | collective-permute-start | bytes 49160 | tf_op jit(solution)/shard_map/ppermute | solution.py:335
  28.1 1.3 %collective-permute-start.12 = (bf16[64,128]{1,0:T(8,128)(2,1)S(1)}, bf16[64,128]{1,0:T(8,128)(2,1)S(1)}, u32[]{:S(2)}, u32[]{:S(2)}) collective-permute-start(bf16[64,128]{1,0:T(8,128)(2,1)S(1)} %get-tuple-element.62.refs_5_), channel_id=1, source_target_pairs={{0,9},{1,10},{2,11},{3,8},{4,13},{5,14},{6,15},{7,12},{8,1},{9,2},... | collective-permute-start | bytes 49160 | tf_op jit(solution)/shard_map/ppermute | solution.py:335
  29.4 1.3 %own.4 = (f32[64,1024]{1,0:T(8,128)S(1)}, bf16[4,64,1024]{2,1,0:T(8,128)(2,1)}) custom-call(s32[1]{0:T(128)} %bitcast.index_ref.refs_0_, bf16[64,1024]{1,0:T(8,128)(2,1)S(1)} %get-tuple-element.58.refs_1_, bf16[64,1536]{1,0:T(8,128)(2,1)S(1)} %collective-permute-done.9.message_ref.refs_2_, ...), custom_call_target="tpu_custom_call", output_to_operand_aliasing={{1}: (6, {})} | custom-call | flops 1000000000 | bytes 4194304 | tf_op jit(solution)/shard_map/own/pallas_call | solution.py:249
  30.6 2.1 %collective-permute-done.10.over_ref = bf16[64,1024]{1,0:T(8,128)(2,1)S(1)} collective-permute-done((bf16[64,1024]{1,0:T(8,128)(2,1)S(1)}, bf16[64,1024]{1,0:T(8,128)(2,1)S(1)}, u32[]{:S(2)}, u32[]{:S(2)}) %collective-permute-start.10) | collective-permute-done | bytes 131104 | tf_op jit(solution)/shard_map/ppermute | solution.py:318
  32.7 0.5 %halo.6.refs_1_ = f32[64,1024]{1,0:T(8,128)S(1)} custom-call(s32[1]{0:T(128)} %bitcast.index_ref.refs_0_, f32[64,1024]{1,0:T(8,128)S(1)} %get-tuple-element.64.acc_ref, bf16[64,1024]{1,0:T(8,128)(2,1)S(1)} %collective-permute-done.10.over_ref, bf16[36,256,256]{2,1,0:T(8,128)(2,1)S(1)} %get-tuple-element.50.d_ref.refs_3_), custom_call_target="tpu_custom_call" | custom-call | flops 1000000000 | bytes 4194304 | tf_op jit(solution)/shard_map/halo/pallas_call | solution.py:249
  33.2 0.0 collective-permute-done.11.refs_5_
  33.2 0.6 %collective-permute-done.12.refs_6_ = bf16[64,128]{1,0:T(8,128)(2,1)S(1)} collective-permute-done((bf16[64,128]{1,0:T(8,128)(2,1)S(1)}, bf16[64,128]{1,0:T(8,128)(2,1)S(1)}, u32[]{:S(2)}, u32[]{:S(2)}) %collective-permute-start.12) | collective-permute-done | bytes 16416 | tf_op jit(solution)/shard_map/ppermute | solution.py:335
  33.8 0.6 %finish.5 = (bf16[64,1024]{1,0:T(8,128)(2,1)S(1)}, bf16[64,1536]{1,0:T(8,128)(2,1)S(1)}, f32[64,256]{1,0:T(8,128)S(1)}) custom-call(s32[1]{0:T(128)} %bitcast.index_ref.refs_0_, f32[64,1024]{1,0:T(8,128)S(1)} %halo.6.refs_1_, bf16[256,1024]{1,0:T(8,128)(2,1)S(1)} %get-tuple-element.51.refs_2_.refs_1_, ...), custom_call_target="tpu_custom_call" | custom-call | flops 1000000000 | bytes 4194304 | tf_op jit(solution)/shard_map/finish/pallas_call | solution.py:249
  34.4 0.1 collective-permute-start.13
  34.5 2.6 %collective-permute-start.14 = (bf16[64,1024]{1,0:T(8,128)(2,1)S(1)}, bf16[64,1024]{1,0:T(8,128)(2,1)S(1)}, u32[]{:S(2)}, u32[]{:S(2)}) collective-permute-start(bf16[64,1024]{1,0:T(8,128)(2,1)S(1)} %get-tuple-element.65.refs_1_), channel_id=1, source_target_pairs={{0,15},{1,2},{2,1},{3,4},{4,3},{5,6},{6,5},{7,8},{8,7},{9,10},{10,... | collective-permute-start | bytes 393224 | tf_op jit(solution)/shard_map/ppermute | solution.py:318
  37.1 0.0 collective-permute-done.13.message_ref.refs_2_
  37.1 0.6 %collective-permute-start.15 = (bf16[64,128]{1,0:T(8,128)(2,1)S(1)}, bf16[64,128]{1,0:T(8,128)(2,1)S(1)}, u32[]{:S(2)}, u32[]{:S(2)}) collective-permute-start(bf16[64,128]{1,0:T(8,128)(2,1)S(1)} %get-tuple-element.68.refs_4_), channel_id=1, source_target_pairs={{0,8},{1,11},{2,10},{3,9},{4,12},{5,15},{6,14},{7,13},{8,0},{9,3},... | collective-permute-start | bytes 49160 | tf_op jit(solution)/shard_map/ppermute | solution.py:335
  37.7 1.0 %collective-permute-start.16 = (bf16[64,128]{1,0:T(8,128)(2,1)S(1)}, bf16[64,128]{1,0:T(8,128)(2,1)S(1)}, u32[]{:S(2)}, u32[]{:S(2)}) collective-permute-start(bf16[64,128]{1,0:T(8,128)(2,1)S(1)} %get-tuple-element.69.refs_5_), channel_id=1, source_target_pairs={{0,9},{1,10},{2,11},{3,8},{4,13},{5,14},{6,15},{7,12},{8,1},{9,2},... | collective-permute-start | bytes 49160 | tf_op jit(solution)/shard_map/ppermute | solution.py:335
  38.8 1.3 %own.5 = (f32[64,1024]{1,0:T(8,128)S(1)}, bf16[4,64,1024]{2,1,0:T(8,128)(2,1)}) custom-call(s32[1]{0:T(128)} %bitcast.index_ref.refs_0_, bf16[64,1024]{1,0:T(8,128)(2,1)S(1)} %get-tuple-element.65.refs_1_, bf16[64,1536]{1,0:T(8,128)(2,1)S(1)} %collective-permute-done.13.message_ref.refs_2_, ...), custom_call_target="tpu_custom_call", output_to_operand_aliasing={{1}: (6, {})} | custom-call | flops 1000000000 | bytes 4194304 | tf_op jit(solution)/shard_map/own/pallas_call | solution.py:249
  40.1 1.8 %collective-permute-done.14.over_ref = bf16[64,1024]{1,0:T(8,128)(2,1)S(1)} collective-permute-done((bf16[64,1024]{1,0:T(8,128)(2,1)S(1)}, bf16[64,1024]{1,0:T(8,128)(2,1)S(1)}, u32[]{:S(2)}, u32[]{:S(2)}) %collective-permute-start.14) | collective-permute-done | bytes 131104 | tf_op jit(solution)/shard_map/ppermute | solution.py:318
  41.9 0.5 %halo.7.refs_0_ = f32[64,1024]{1,0:T(8,128)S(1)} custom-call(s32[1]{0:T(128)} %bitcast.index_ref.refs_0_, f32[64,1024]{1,0:T(8,128)S(1)} %get-tuple-element.71.acc_ref, bf16[64,1024]{1,0:T(8,128)(2,1)S(1)} %collective-permute-done.14.over_ref, bf16[36,256,256]{2,1,0:T(8,128)(2,1)S(1)} %get-tuple-element.50.d_ref.refs_3_), custom_call_target="tpu_custom_call" | custom-call | flops 1000000000 | bytes 4194304 | tf_op jit(solution)/shard_map/halo/pallas_call | solution.py:249
  42.4 0.0 collective-permute-done.15.refs_2_
  42.5 0.6 %collective-permute-done.16.refs_3_ = bf16[64,128]{1,0:T(8,128)(2,1)S(1)} collective-permute-done((bf16[64,128]{1,0:T(8,128)(2,1)S(1)}, bf16[64,128]{1,0:T(8,128)(2,1)S(1)}, u32[]{:S(2)}, u32[]{:S(2)}) %collective-permute-start.16) | collective-permute-done | bytes 16416 | tf_op jit(solution)/shard_map/ppermute | solution.py:335
  43.1 0.9 %last.1 = bf16[4,64,1024]{2,1,0:T(8,128)(2,1)} custom-call(f32[64,1024]{1,0:T(8,128)S(1)} %halo.7.refs_0_, bf16[256,1024]{1,0:T(8,128)(2,1)S(1)} %get-tuple-element.51.refs_2_.refs_1_, bf16[64,128]{1,0:T(8,128)(2,1)S(1)} %collective-permute-done.15.refs_2_, bf16[64,128]{1,0:T(8,128)(2,1)S(1)} %collective-permute-done.16.refs_3_, ...), custom_call_target="tpu_custom_call", output_to_operand_aliasing={{}: (4, {})} | custom-call | flops 1000000000 | bytes 4194304 | tf_op jit(solution)/shard_map/last/pallas_call | solution.py:249
  (4 shorter events, 0.1 us)
Async XLA Ops:
  1.5 8.3 %copy-start = (bf16[32,256,256]{2,1,0:T(8,128)(2,1)S(1)}, bf16[32,256,256]{2,1,0:T(8,128)(2,1)}, u32[]{:S(2)}) copy-start(bf16[32,256,256]{2,1,0:T(8,128)(2,1)} %refs_6_.3) | copy-start | bytes 12582916
  1.5 8.3 %copy-start.1 = (bf16[4,32,256]{2,1,0:T(8,128)(2,1)S(1)}, bf16[4,32,256]{2,1,0:T(8,128)(2,1)}, u32[]{:S(2)}) copy-start(bf16[4,32,256]{2,1,0:T(8,128)(2,1)} %refs_5_.3) | copy-start | bytes 196612
  2.0 7.8 %collective-permute-start = (bf16[64,1024]{1,0:T(8,128)(2,1)S(1)}, bf16[64,1024]{1,0:T(8,128)(2,1)S(1)}, u32[]{:S(2)}, u32[]{:S(2)}) collective-permute-start(bf16[64,1024]{1,0:T(8,128)(2,1)S(1)} %get-tuple-element.44.refs_3_), channel_id=1, source_target_pairs={{0,1},{1,0},{2,3},{3,2},{4,5},{5,4},{6,7},{7,6},{8,9},{9,8},{10,11... | collective-permute-start | bytes 393224 | tf_op jit(solution)/shard_map/ppermute | solution.py:322
  2.5 9.1 %collective-permute-start.2 = (bf16[64,1024]{1,0:T(8,128)(2,1)S(1)}, bf16[64,1024]{1,0:T(8,128)(2,1)S(1)}, u32[]{:S(2)}, u32[]{:S(2)}) collective-permute-start(bf16[64,1024]{1,0:T(8,128)(2,1)S(1)} %get-tuple-element.41.x_ref), channel_id=1, source_target_pairs={{0,15},{1,2},{2,1},{3,4},{4,3},{5,6},{6,5},{7,8},{8,7},{9,10},{10,... | collective-permute-start | bytes 393224 | tf_op jit(solution)/shard_map/ppermute | solution.py:308
  8.2 1.3 %collective-permute-start.1 = (bf16[64,512]{1,0:T(8,128)(2,1)S(1)}, bf16[64,512]{1,0:T(8,128)(2,1)S(1)}, u32[]{:S(2)}, u32[]{:S(2)}) collective-permute-start(bf16[64,512]{1,0:T(8,128)(2,1)S(1)} %get-tuple-element.46), channel_id=1, source_target_pairs={{0,1},{1,0},{2,3},{3,2},{4,5},{5,4},{6,7},{7,6},{8,9},{9,8},{10,11... | collective-permute-start | bytes 196616 | tf_op jit(solution)/shard_map/ppermute | solution.py:321
  9.4 5.0 %collective-permute-start.3 = (bf16[64,128]{1,0:T(8,128)(2,1)S(1)}, bf16[64,128]{1,0:T(8,128)(2,1)S(1)}, u32[]{:S(2)}, u32[]{:S(2)}) collective-permute-start(bf16[64,128]{1,0:T(8,128)(2,1)S(1)} %get-tuple-element.47.refs_7_), channel_id=1, source_target_pairs={{0,8},{1,11},{2,10},{3,9},{4,12},{5,15},{6,14},{7,13},{8,0},{9,3},... | collective-permute-start | bytes 49160 | tf_op jit(solution)/shard_map/ppermute | solution.py:335
  9.5 5.0 %collective-permute-start.4 = (bf16[64,128]{1,0:T(8,128)(2,1)S(1)}, bf16[64,128]{1,0:T(8,128)(2,1)S(1)}, u32[]{:S(2)}, u32[]{:S(2)}) collective-permute-start(bf16[64,128]{1,0:T(8,128)(2,1)S(1)} %get-tuple-element.48.refs_8_), channel_id=1, source_target_pairs={{0,9},{1,10},{2,11},{3,8},{4,13},{5,14},{6,15},{7,12},{8,1},{9,2},... | collective-permute-start | bytes 49160 | tf_op jit(solution)/shard_map/ppermute | solution.py:335
  15.1 2.8 %collective-permute-start.5 = (bf16[64,1536]{1,0:T(8,128)(2,1)S(1)}, bf16[64,1536]{1,0:T(8,128)(2,1)S(1)}, u32[]{:S(2)}, u32[]{:S(2)}) collective-permute-start(bf16[64,1536]{1,0:T(8,128)(2,1)S(1)} %get-tuple-element.53), channel_id=1, source_target_pairs={{0,1},{1,0},{2,3},{3,2},{4,5},{5,4},{6,7},{7,6},{8,9},{9,8},{10,11... | collective-permute-start | bytes 589832 | tf_op jit(solution)/shard_map/ppermute | solution.py:319
  15.3 7.4 %collective-permute-start.6 = (bf16[64,1024]{1,0:T(8,128)(2,1)S(1)}, bf16[64,1024]{1,0:T(8,128)(2,1)S(1)}, u32[]{:S(2)}, u32[]{:S(2)}) collective-permute-start(bf16[64,1024]{1,0:T(8,128)(2,1)S(1)} %get-tuple-element.52.refs_1_), channel_id=1, source_target_pairs={{0,15},{1,2},{2,1},{3,4},{4,3},{5,6},{6,5},{7,8},{8,7},{9,10},{10,... | collective-permute-start | bytes 393224 | tf_op jit(solution)/shard_map/ppermute | solution.py:318
  17.9 5.2 %collective-permute-start.7 = (bf16[64,128]{1,0:T(8,128)(2,1)S(1)}, bf16[64,128]{1,0:T(8,128)(2,1)S(1)}, u32[]{:S(2)}, u32[]{:S(2)}) collective-permute-start(bf16[64,128]{1,0:T(8,128)(2,1)S(1)} %get-tuple-element.55.refs_4_), channel_id=1, source_target_pairs={{0,8},{1,11},{2,10},{3,9},{4,12},{5,15},{6,14},{7,13},{8,0},{9,3},... | collective-permute-start | bytes 49160 | tf_op jit(solution)/shard_map/ppermute | solution.py:335
  19.7 5.1 %collective-permute-start.8 = (bf16[64,128]{1,0:T(8,128)(2,1)S(1)}, bf16[64,128]{1,0:T(8,128)(2,1)S(1)}, u32[]{:S(2)}, u32[]{:S(2)}) collective-permute-start(bf16[64,128]{1,0:T(8,128)(2,1)S(1)} %get-tuple-element.56.refs_5_), channel_id=1, source_target_pairs={{0,9},{1,10},{2,11},{3,8},{4,13},{5,14},{6,15},{7,12},{8,1},{9,2},... | collective-permute-start | bytes 49160 | tf_op jit(solution)/shard_map/ppermute | solution.py:335
  25.4 2.2 %collective-permute-start.9 = (bf16[64,1536]{1,0:T(8,128)(2,1)S(1)}, bf16[64,1536]{1,0:T(8,128)(2,1)S(1)}, u32[]{:S(2)}, u32[]{:S(2)}) collective-permute-start(bf16[64,1536]{1,0:T(8,128)(2,1)S(1)} %get-tuple-element.59), channel_id=1, source_target_pairs={{0,1},{1,0},{2,3},{3,2},{4,5},{5,4},{6,7},{7,6},{8,9},{9,8},{10,11... | collective-permute-start | bytes 589832 | tf_op jit(solution)/shard_map/ppermute | solution.py:319
  25.4 7.3 %collective-permute-start.10 = (bf16[64,1024]{1,0:T(8,128)(2,1)S(1)}, bf16[64,1024]{1,0:T(8,128)(2,1)S(1)}, u32[]{:S(2)}, u32[]{:S(2)}) collective-permute-start(bf16[64,1024]{1,0:T(8,128)(2,1)S(1)} %get-tuple-element.58.refs_1_), channel_id=1, source_target_pairs={{0,15},{1,2},{2,1},{3,4},{4,3},{5,6},{6,5},{7,8},{8,7},{9,10},{10,... | collective-permute-start | bytes 393224 | tf_op jit(solution)/shard_map/ppermute | solution.py:318
  27.6 5.6 %collective-permute-start.11 = (bf16[64,128]{1,0:T(8,128)(2,1)S(1)}, bf16[64,128]{1,0:T(8,128)(2,1)S(1)}, u32[]{:S(2)}, u32[]{:S(2)}) collective-permute-start(bf16[64,128]{1,0:T(8,128)(2,1)S(1)} %get-tuple-element.61.refs_4_), channel_id=1, source_target_pairs={{0,8},{1,11},{2,10},{3,9},{4,12},{5,15},{6,14},{7,13},{8,0},{9,3},... | collective-permute-start | bytes 49160 | tf_op jit(solution)/shard_map/ppermute | solution.py:335
  28.1 5.7 %collective-permute-start.12 = (bf16[64,128]{1,0:T(8,128)(2,1)S(1)}, bf16[64,128]{1,0:T(8,128)(2,1)S(1)}, u32[]{:S(2)}, u32[]{:S(2)}) collective-permute-start(bf16[64,128]{1,0:T(8,128)(2,1)S(1)} %get-tuple-element.62.refs_5_), channel_id=1, source_target_pairs={{0,9},{1,10},{2,11},{3,8},{4,13},{5,14},{6,15},{7,12},{8,1},{9,2},... | collective-permute-start | bytes 49160 | tf_op jit(solution)/shard_map/ppermute | solution.py:335
  34.4 2.7 %collective-permute-start.13 = (bf16[64,1536]{1,0:T(8,128)(2,1)S(1)}, bf16[64,1536]{1,0:T(8,128)(2,1)S(1)}, u32[]{:S(2)}, u32[]{:S(2)}) collective-permute-start(bf16[64,1536]{1,0:T(8,128)(2,1)S(1)} %get-tuple-element.66), channel_id=1, source_target_pairs={{0,1},{1,0},{2,3},{3,2},{4,5},{5,4},{6,7},{7,6},{8,9},{9,8},{10,11... | collective-permute-start | bytes 589832 | tf_op jit(solution)/shard_map/ppermute | solution.py:319
  34.5 7.4 %collective-permute-start.14 = (bf16[64,1024]{1,0:T(8,128)(2,1)S(1)}, bf16[64,1024]{1,0:T(8,128)(2,1)S(1)}, u32[]{:S(2)}, u32[]{:S(2)}) collective-permute-start(bf16[64,1024]{1,0:T(8,128)(2,1)S(1)} %get-tuple-element.65.refs_1_), channel_id=1, source_target_pairs={{0,15},{1,2},{2,1},{3,4},{4,3},{5,6},{6,5},{7,8},{8,7},{9,10},{10,... | collective-permute-start | bytes 393224 | tf_op jit(solution)/shard_map/ppermute | solution.py:318
  37.1 5.3 %collective-permute-start.15 = (bf16[64,128]{1,0:T(8,128)(2,1)S(1)}, bf16[64,128]{1,0:T(8,128)(2,1)S(1)}, u32[]{:S(2)}, u32[]{:S(2)}) collective-permute-start(bf16[64,128]{1,0:T(8,128)(2,1)S(1)} %get-tuple-element.68.refs_4_), channel_id=1, source_target_pairs={{0,8},{1,11},{2,10},{3,9},{4,12},{5,15},{6,14},{7,13},{8,0},{9,3},... | collective-permute-start | bytes 49160 | tf_op jit(solution)/shard_map/ppermute | solution.py:335
  37.7 5.3 %collective-permute-start.16 = (bf16[64,128]{1,0:T(8,128)(2,1)S(1)}, bf16[64,128]{1,0:T(8,128)(2,1)S(1)}, u32[]{:S(2)}, u32[]{:S(2)}) collective-permute-start(bf16[64,128]{1,0:T(8,128)(2,1)S(1)} %get-tuple-element.69.refs_5_), channel_id=1, source_target_pairs={{0,9},{1,10},{2,11},{3,8},{4,13},{5,14},{6,15},{7,12},{8,1},{9,2},... | collective-permute-start | bytes 49160 | tf_op jit(solution)/shard_map/ppermute | solution.py:335

commit v14 on v11

--- a/solution.py
+++ b/solution.py
@@ -46,7 +46,7 @@
         self.block_clusters = self.per_device * members
         distances = [d % loop_size for d in (2, loop_size - 2, loop_size // 2)]
         self.hops = sorted(set(distances))
-        self.sets = [[i for i, d in enumerate(distances) if d == hop] for hop in self.hops]
+        self.set_of = [self.hops.index(d) for d in distances]
         self.paired = len(self.hops) == 1 and 2 * self.hops[0] == loop_size and members == 4
         devices = members * loop_size
         self.near = [(i, i ^ 1) for i in range(devices)]
@@ -73,7 +73,8 @@
 
     def send_far(self, index_ref, x, cb_ref, g_ref, out_refs):
         coeffs = dot_nt(x, cb_ref[...]).astype(BF16)
-        totals = [sum(dot_nt(coeffs, g_ref[level]) for level in levels) for levels in self.sets]
+        twice = jnp.concatenate([coeffs, coeffs], axis=1)
+        totals = [dot_nt(twice, g_ref[index]) for index in range(len(self.hops))]
         if not self.paired:
             for i, out_ref in enumerate(out_refs):
                 step = i % self.members * self.width
@@ -136,8 +137,8 @@
 
 def prepare_kernel(plan, index_ref, *refs):
     sources, refs = refs[:7], refs[7:]
-    x_ref, d_ref, g_ref, cb_ref, near_ref, offsets_ref = refs[:6]
-    sends, (rows_ref, cols_ref, col_ref, coup_ref, sems) = refs[6:-5], refs[-5:]
+    x_ref, g_ref, cb_ref, near_ref, offsets_ref = refs[:5]
+    sends, (rows_ref, cols_ref, col_ref, coup_ref, sum_ref, sems) = refs[5:-6], refs[-6:]
     targets = (near_ref, offsets_ref, rows_ref, cols_ref, x_ref, col_ref, coup_ref)
     copies = [
         pltpu.make_async_copy(source, target, sems.at[i])
@@ -147,9 +148,7 @@
         copy.start()
     rank, size = plan.rank, plan.size
     cb_ref[...] = jnp.zeros_like(cb_ref)
-    g_ref[...] = jnp.zeros_like(g_ref)
-    for cell in range(plan.cells):
-        d_ref[cell] = jnp.zeros(d_ref.shape[1:], d_ref.dtype)
+    sum_ref[...] = jnp.zeros_like(sum_ref)
     for copy in copies:
         copy.wait()
     for c in range(plan.per_device):
@@ -157,14 +156,20 @@
     column = lax.broadcasted_iota(jnp.int32, (rank, plan.width), 1) // rank
     shift = 0 if plan.paired else plan.member(index_ref)
     for s in range(plan.slots):
-        level = lax.div(rows_ref[s], plan.block_clusters)
         row = lax.rem(rows_ref[s], plan.block_clusters)
         step = lax.rem(lax.div(row, plan.per_device) - shift + plan.members, plan.members)
         place = step * plan.per_device + lax.rem(row, plan.per_device)
-        where = (level, pl.ds(pl.multiple_of(place * rank, rank), rank), slice(None))
+        if len(plan.hops) > 1:
+            level = lax.div(rows_ref[s], plan.block_clusters)
+            index = sum(jnp.where(level == i, index, 0) for i, index in enumerate(plan.set_of))
+        else:
+            index = 0
+        where = (index, pl.ds(pl.multiple_of(place * rank, rank), rank), slice(None))
         tile = coup_ref[s].astype(F32)
         wide = jnp.where(column == cols_ref[s], jnp.concatenate([tile] * plan.per_device, axis=1), 0.0)
-        g_ref[where] = g_ref[where] + wide.astype(BF16)
+        sum_ref[where] = sum_ref[where] + wide
+    for index in range(len(plan.hops)):
+        g_ref[index] = jnp.concatenate(halves(sum_ref[index]), axis=1)
     plan.send_far(index_ref, x_ref[...], cb_ref, g_ref, sends)
 
 
@@ -176,6 +181,8 @@
     index_ref, rows_ref, offsets_ref, x_ref, near_ref, row_ref, tiles_ref = refs[:7]
     acc_ref, d_ref, rb_ref = refs[-3:]
     rank, size = plan.rank, plan.size
+    for cell in range(plan.cells):
+        d_ref[cell] = jnp.zeros(d_ref.shape[1:], d_ref.dtype)
     for s in range(plan.tiles):
         d_ref[rows_ref[s] * SPAN + offsets_ref[s] + REACH] = tiles_ref[s]
     rb_ref[...] = jnp.zeros_like(rb_ref)
@@ -274,25 +281,25 @@
     for product in range(PRODUCTS):
         if product == 0:
             ins = [near_rows, near_offsets, far_rows, far_cols, block, col_basis, couplings]
-            current, dense, coupled, col_wide, row_slots, offset_slots, *sends = call(
+            matrix = (len(plan.hops), plan.members * width, 2 * width)
+            current, coupled, col_wide, row_slots, offset_slots, *sends = call(
                 functools.partial(prepare_kernel, plan),
                 "prepare",
                 [index, *ins],
                 [IN_SMEM] + [IN_HBM] * 7,
                 [
                     block_out,
-                    pltpu.VMEM((plan.cells, plan.size, plan.size), BF16),
-                    pltpu.VMEM((LEVELS, plan.members * width, width), BF16),
+                    pltpu.VMEM(matrix, BF16),
                     pltpu.VMEM((width, shard_len), BF16),
                     *scratch_for(near_rows, near_offsets),
                     *sends_out,
                 ],
-                [IN_VMEM] * 4 + [IN_SMEM] * 2 + [IN_VMEM] * len(sends_out),
+                [IN_VMEM] * 3 + [IN_SMEM] * 2 + [IN_VMEM] * len(sends_out),
                 scratch=scratch_for(far_rows, far_cols, col_basis, couplings)
-                + [pltpu.SemaphoreType.DMA((7,))],
-            )
+                + [pltpu.VMEM(matrix[:2] + (width,), F32), pltpu.SemaphoreType.DMA((7,))],
+            )
+        over = lax.ppermute(block if product == 0 else current, axes, plan.over)
         near = lax.ppermute(sends[0] if plan.paired else current, axes, plan.near)
-        over = lax.ppermute(block if product == 0 else current, axes, plan.over)
         if plan.paired:
             sends = call(
                 functools.partial(relay_kernel, plan),
@@ -307,18 +314,17 @@
         fars = [lax.ppermute(s, axes, route) for s, route in zip(sends, routes)]
         after = sends if plan.paired else []
         if product == 0:
-            ins = [index, row_slots, offset_slots, current, near, row_basis, near_tiles, dense, *after]
+            ins = [index, row_slots, offset_slots, current, near, row_basis, near_tiles, *after]
             acc, dense, row_wide = call(
                 functools.partial(first_own_kernel, plan),
                 "first_own",
                 ins,
-                [IN_SMEM] * 3 + [IN_VMEM] * 2 + [PREFETCHED] * 2 + [IN_VMEM] + [ANYWHERE] * len(after),
+                [IN_SMEM] * 3 + [IN_VMEM] * 2 + [PREFETCHED] * 2 + [ANYWHERE] * len(after),
                 [
                     acc_out,
                     pltpu.VMEM((plan.cells, plan.size, plan.size), BF16),
                     pltpu.VMEM((2 * width, shard_len), BF16),
                 ],
-                aliases={7: 1},
             )
         else:
             ins = [index, current, near, dense, *after] + ([krylov] if product > 1 else [])

time: 44 us -> 43.1 us (0.980)
  waiting for transfers between devices: 11.5 us -> 10.9 us
  Pallas kernels: 12.8 us -> 12.3 us
    ppermute x4, waiting for transfers between devices: 6.54 us -> 5.92 us  [on_device(): over = lax.ppermute(block if product == 0 else current, axes, plan.over)]
    pallas_call x17, Pallas kernels: 12.8 us -> 12.3 us  [call(): pl.pallas_call(kernel, in_specs=list(specs), out_specs=out_specs or [IN_V...]
  transfers between devices with their start and end apart: 16 -> 16, of which waited for: 10 -> 10; matrix products, arithmetic and copies ran while one was open for 0% -> 0% of each run, Pallas kernels for 17% -> 18%
where the time goes in v14:
time: 43.1 us; the launch traced here: 43 us
  starting transfers between devices  19.6 us (45%)
  Pallas kernels  12.3 us (29%)
  waiting for transfers between devices  10.9 us (25%)
    ppermute x4, starting transfers between devices, on_device(): over = lax.ppermute(block if product == 0 else current, axes, plan.over)  14.7 us
    pallas_call x17, Pallas kernels, call(): pl.pallas_call(kernel, in_specs=list(specs), out_specs=out_specs or [IN_V...  12.3 us
    ppermute x4, waiting for transfers between devices, on_device(): over = lax.ppermute(block if product == 0 else current, axes, plan.over)  5.92 us
    ppermute x8, waiting for transfers between devices, on_device(): fars = [lax.ppermute(s, axes, route) for s, route in zip(sends, routes)]  4.97 us
    ppermute x8, starting transfers between devices, on_device(): fars = [lax.ppermute(s, axes, route) for s, route in zip(sends, routes)]  4.21 us
  transfers between devices with their start and end apart: 16, of which 10 were waited for; matrix products, arithmetic and copies ran while one was open for 0% of the time, Pallas kernels for 18%

profile of v14, /device:TPU:0, one launch (start us, length us, event | category | flops | bytes accessed | tf_op | source)
XLA Modules:
  0.0 43.0 jit_solution(11287079843620669071)
XLA Ops:
  0.0 0.0 copy-start.1
  0.0 0.0 copy-start
  0.0 1.8 %prepare.1 = (bf16[64,1024]{1,0:T(8,128)(2,1)S(1)}, bf16[1,512,256]{2,1,0:T(8,128)(2,1)S(1)}, bf16[128,1024]{1,0:T(8,128)(2,1)S(1)}, s32[32]{0:T(128)S(4)}, s32[...) custom-call(s32[1]{0:T(128)} %bitcast.index_ref.refs_0_, s32[32]{0:T(128)} %refs_0_.1, s32[32]{0:T(128)} %refs_1_.1, ...), custom_call_target="tpu_custom_call" | custom-call | flops 1000000000 | bytes 4194304 | tf_op jit(solution)/shard_map/prepare/pallas_call | solution.py:240
  1.8 0.5 %collective-permute-start = (bf16[64,1536]{1,0:T(8,128)(2,1)S(1)}, bf16[64,1536]{1,0:T(8,128)(2,1)S(1)}, u32[]{:S(2)}, u32[]{:S(2)}) collective-permute-start(bf16[64,1536]{1,0:T(8,128)(2,1)S(1)} %get-tuple-element.41), channel_id=1, source_target_pairs={{0,1},{1,0},{2,3},{3,2},{4,5},{5,4},{6,7},{7,6},{8,9},{9,8},{10,11... | collective-permute-start | bytes 589832 | tf_op jit(solution)/shard_map/ppermute | solution.py:302
  2.4 5.6 %collective-permute-start.1 = (bf16[64,1024]{1,0:T(8,128)(2,1)}, bf16[64,1024]{1,0:T(8,128)(2,1)S(1)}, u32[]{:S(2)}, u32[]{:S(2)}) collective-permute-start(bf16[64,1024]{1,0:T(8,128)(2,1)} %refs_4_.1), channel_id=1, source_target_pairs={{0,15},{1,2},{2,1},{3,4},{4,3},{5,6},{6,5},{7,8},{8,7},{9,10},{10,... | collective-permute-start | bytes 393224 | tf_op jit(solution)/shard_map/ppermute | solution.py:301
  8.0 0.0 collective-permute-done.message_ref.refs_4_
  8.0 0.1 collective-permute-start.2
  8.1 0.3 collective-permute-start.3
  8.4 0.0 copy-done.1
  8.4 0.0 copy-done
  8.4 1.9 %first_own.1 = (f32[64,1024]{1,0:T(8,128)S(1)}, bf16[36,256,256]{2,1,0:T(8,128)(2,1)S(1)}, bf16[256,1024]{1,0:T(8,128)(2,1)S(1)}) custom-call(s32[1]{0:T(128)} %bitcast.index_ref.refs_0_, s32[32]{0:T(128)S(4)} %get-tuple-element.38.refs_1_, s32[32]{0:T(128)S(4)} %get-tuple-element.39.refs_2_, bf16[64,1024]{1,0:T(8,128)(2,1)S(1)} %get-tuple-element.40.refs_3_, ...), custom_call_target="tpu_custom_call" | custom-call | flops 1000000000 | bytes 4194304 | tf_op jit(solution)/shard_map/first_own/pallas_call | solution.py:240
  10.3 0.7 %collective-permute-done.1.over_ref = bf16[64,1024]{1,0:T(8,128)(2,1)S(1)} collective-permute-done((bf16[64,1024]{1,0:T(8,128)(2,1)}, bf16[64,1024]{1,0:T(8,128)(2,1)S(1)}, u32[]{:S(2)}, u32[]{:S(2)}) %collective-permute-start.1) | collective-permute-done | bytes 131104 | tf_op jit(solution)/shard_map/ppermute | solution.py:301
  11.0 0.5 %halo.4.refs_1_ = f32[64,1024]{1,0:T(8,128)S(1)} custom-call(s32[1]{0:T(128)} %bitcast.index_ref.refs_0_, f32[64,1024]{1,0:T(8,128)S(1)} %get-tuple-element.45.acc_ref, bf16[64,1024]{1,0:T(8,128)(2,1)S(1)} %collective-permute-done.1.over_ref, bf16[36,256,256]{2,1,0:T(8,128)(2,1)S(1)} %get-tuple-element.46.d_ref.refs_3_), custom_call_target="tpu_custom_call" | custom-call | flops 1000000000 | bytes 4194304 | tf_op jit(solution)/shard_map/halo/pallas_call | solution.py:240
  11.5 1.2 %collective-permute-done.2.refs_5_ = bf16[64,128]{1,0:T(8,128)(2,1)S(1)} collective-permute-done((bf16[64,128]{1,0:T(8,128)(2,1)S(1)}, bf16[64,128]{1,0:T(8,128)(2,1)S(1)}, u32[]{:S(2)}, u32[]{:S(2)}) %collective-permute-start.2) | collective-permute-done | bytes 16416 | tf_op jit(solution)/shard_map/ppermute | solution.py:314
  12.7 0.4 collective-permute-done.3.refs_6_
  13.1 0.6 %finish.3 = (bf16[64,1024]{1,0:T(8,128)(2,1)S(1)}, bf16[64,1536]{1,0:T(8,128)(2,1)S(1)}, f32[64,256]{1,0:T(8,128)S(1)}) custom-call(s32[1]{0:T(128)} %bitcast.index_ref.refs_0_, f32[64,1024]{1,0:T(8,128)S(1)} %halo.4.refs_1_, bf16[256,1024]{1,0:T(8,128)(2,1)S(1)} %get-tuple-element.47.refs_2_.refs_1_, bf16[128,1024]{1,0:T(8,128)(2,1)S(1)} %get-tuple-element.48.refs_3_, ...), custom_call_target="tpu_custom_call" | custom-call | flops 1000000000 | bytes 4194304 | tf_op jit(solution)/shard_map/finish/pallas_call | solution.py:240
  13.7 0.1 collective-permute-start.4
  13.8 3.7 %collective-permute-start.5 = (bf16[64,1024]{1,0:T(8,128)(2,1)S(1)}, bf16[64,1024]{1,0:T(8,128)(2,1)S(1)}, u32[]{:S(2)}, u32[]{:S(2)}) collective-permute-start(bf16[64,1024]{1,0:T(8,128)(2,1)S(1)} %get-tuple-element.50.refs_1_), channel_id=1, source_target_pairs={{0,15},{1,2},{2,1},{3,4},{4,3},{5,6},{6,5},{7,8},{8,7},{9,10},{10,... | collective-permute-start | bytes 393224 | tf_op jit(solution)/shard_map/ppermute | solution.py:301
  17.5 0.0 collective-permute-done.4.message_ref.refs_2_
  17.5 0.7 %collective-permute-start.6 = (bf16[64,128]{1,0:T(8,128)(2,1)S(1)}, bf16[64,128]{1,0:T(8,128)(2,1)S(1)}, u32[]{:S(2)}, u32[]{:S(2)}) collective-permute-start(bf16[64,128]{1,0:T(8,128)(2,1)S(1)} %get-tuple-element.53.refs_4_), channel_id=1, source_target_pairs={{0,8},{1,11},{2,10},{3,9},{4,12},{5,15},{6,14},{7,13},{8,0},{9,3},... | collective-permute-start | bytes 49160 | tf_op jit(solution)/shard_map/ppermute | solution.py:314
  18.2 0.7 %collective-permute-start.7 = (bf16[64,128]{1,0:T(8,128)(2,1)S(1)}, bf16[64,128]{1,0:T(8,128)(2,1)S(1)}, u32[]{:S(2)}, u32[]{:S(2)}) collective-permute-start(bf16[64,128]{1,0:T(8,128)(2,1)S(1)} %get-tuple-element.54.refs_5_), channel_id=1, source_target_pairs={{0,9},{1,10},{2,11},{3,8},{4,13},{5,14},{6,15},{7,12},{8,1},{9,2},... | collective-permute-start | bytes 49160 | tf_op jit(solution)/shard_map/ppermute | solution.py:314
  18.9 1.3 %own.3 = (f32[64,1024]{1,0:T(8,128)S(1)}, bf16[4,64,1024]{2,1,0:T(8,128)(2,1)}) custom-call(s32[1]{0:T(128)} %bitcast.index_ref.refs_0_, bf16[64,1024]{1,0:T(8,128)(2,1)S(1)} %get-tuple-element.50.refs_1_, bf16[64,1536]{1,0:T(8,128)(2,1)S(1)} %collective-permute-done.4.message_ref.refs_2_, bf16[36,256,256]{2,1,0:T(8,128)(2,1)S(1)} %get-tuple-element.46.d_ref.refs_3_, ...), custom_call_target="tpu_custom_call" | custom-call | flops 1000000000 | bytes 4194304 | tf_op jit(solution)/shard_map/own/pallas_call | solution.py:240
  20.2 0.9 %collective-permute-done.5.over_ref = bf16[64,1024]{1,0:T(8,128)(2,1)S(1)} collective-permute-done((bf16[64,1024]{1,0:T(8,128)(2,1)S(1)}, bf16[64,1024]{1,0:T(8,128)(2,1)S(1)}, u32[]{:S(2)}, u32[]{:S(2)}) %collective-permute-start.5) | collective-permute-done | bytes 131104 | tf_op jit(solution)/shard_map/ppermute | solution.py:301
  21.0 0.5 %halo.5.refs_1_ = f32[64,1024]{1,0:T(8,128)S(1)} custom-call(s32[1]{0:T(128)} %bitcast.index_ref.refs_0_, f32[64,1024]{1,0:T(8,128)S(1)} %get-tuple-element.55.acc_ref, bf16[64,1024]{1,0:T(8,128)(2,1)S(1)} %collective-permute-done.5.over_ref, bf16[36,256,256]{2,1,0:T(8,128)(2,1)S(1)} %get-tuple-element.46.d_ref.refs_3_), custom_call_target="tpu_custom_call" | custom-call | flops 1000000000 | bytes 4194304 | tf_op jit(solution)/shard_map/halo/pallas_call | solution.py:240
  21.5 0.7 %collective-permute-done.6.refs_5_ = bf16[64,128]{1,0:T(8,128)(2,1)S(1)} collective-permute-done((bf16[64,128]{1,0:T(8,128)(2,1)S(1)}, bf16[64,128]{1,0:T(8,128)(2,1)S(1)}, u32[]{:S(2)}, u32[]{:S(2)}) %collective-permute-start.6) | collective-permute-done | bytes 16416 | tf_op jit(solution)/shard_map/ppermute | solution.py:314
  22.2 1.2 %collective-permute-done.7.refs_6_ = bf16[64,128]{1,0:T(8,128)(2,1)S(1)} collective-permute-done((bf16[64,128]{1,0:T(8,128)(2,1)S(1)}, bf16[64,128]{1,0:T(8,128)(2,1)S(1)}, u32[]{:S(2)}, u32[]{:S(2)}) %collective-permute-start.7) | collective-permute-done | bytes 16416 | tf_op jit(solution)/shard_map/ppermute | solution.py:314
  23.4 0.6 %finish.4 = (bf16[64,1024]{1,0:T(8,128)(2,1)S(1)}, bf16[64,1536]{1,0:T(8,128)(2,1)S(1)}, f32[64,256]{1,0:T(8,128)S(1)}) custom-call(s32[1]{0:T(128)} %bitcast.index_ref.refs_0_, f32[64,1024]{1,0:T(8,128)S(1)} %halo.5.refs_1_, bf16[256,1024]{1,0:T(8,128)(2,1)S(1)} %get-tuple-element.47.refs_2_.refs_1_, bf16[128,1024]{1,0:T(8,128)(2,1)S(1)} %get-tuple-element.48.refs_3_, ...), custom_call_target="tpu_custom_call" | custom-call | flops 1000000000 | bytes 4194304 | tf_op jit(solution)/shard_map/finish/pallas_call | solution.py:240
  24.0 0.1 collective-permute-start.8
  24.1 2.6 %collective-permute-start.9 = (bf16[64,1024]{1,0:T(8,128)(2,1)S(1)}, bf16[64,1024]{1,0:T(8,128)(2,1)S(1)}, u32[]{:S(2)}, u32[]{:S(2)}) collective-permute-start(bf16[64,1024]{1,0:T(8,128)(2,1)S(1)} %get-tuple-element.56.refs_1_), channel_id=1, source_target_pairs={{0,15},{1,2},{2,1},{3,4},{4,3},{5,6},{6,5},{7,8},{8,7},{9,10},{10,... | collective-permute-start | bytes 393224 | tf_op jit(solution)/shard_map/ppermute | solution.py:301
  26.7 0.0 collective-permute-done.8.message_ref.refs_2_
  26.7 0.9 %collective-permute-start.10 = (bf16[64,128]{1,0:T(8,128)(2,1)S(1)}, bf16[64,128]{1,0:T(8,128)(2,1)S(1)}, u32[]{:S(2)}, u32[]{:S(2)}) collective-permute-start(bf16[64,128]{1,0:T(8,128)(2,1)S(1)} %get-tuple-element.59.refs_4_), channel_id=1, source_target_pairs={{0,8},{1,11},{2,10},{3,9},{4,12},{5,15},{6,14},{7,13},{8,0},{9,3},... | collective-permute-start | bytes 49160 | tf_op jit(solution)/shard_map/ppermute | solution.py:314
  27.6 0.4 collective-permute-start.11
  28.0 1.3 %own.4 = (f32[64,1024]{1,0:T(8,128)S(1)}, bf16[4,64,1024]{2,1,0:T(8,128)(2,1)}) custom-call(s32[1]{0:T(128)} %bitcast.index_ref.refs_0_, bf16[64,1024]{1,0:T(8,128)(2,1)S(1)} %get-tuple-element.56.refs_1_, bf16[64,1536]{1,0:T(8,128)(2,1)S(1)} %collective-permute-done.8.message_ref.refs_2_, ...), custom_call_target="tpu_custom_call", output_to_operand_aliasing={{1}: (6, {})} | custom-call | flops 1000000000 | bytes 4194304 | tf_op jit(solution)/shard_map/own/pallas_call | solution.py:240
  29.3 2.2 %collective-permute-done.9.over_ref = bf16[64,1024]{1,0:T(8,128)(2,1)S(1)} collective-permute-done((bf16[64,1024]{1,0:T(8,128)(2,1)S(1)}, bf16[64,1024]{1,0:T(8,128)(2,1)S(1)}, u32[]{:S(2)}, u32[]{:S(2)}) %collective-permute-start.9) | collective-permute-done | bytes 131104 | tf_op jit(solution)/shard_map/ppermute | solution.py:301
  31.5 0.5 %halo.6.refs_1_ = f32[64,1024]{1,0:T(8,128)S(1)} custom-call(s32[1]{0:T(128)} %bitcast.index_ref.refs_0_, f32[64,1024]{1,0:T(8,128)S(1)} %get-tuple-element.62.acc_ref, bf16[64,1024]{1,0:T(8,128)(2,1)S(1)} %collective-permute-done.9.over_ref, bf16[36,256,256]{2,1,0:T(8,128)(2,1)S(1)} %get-tuple-element.46.d_ref.refs_3_), custom_call_target="tpu_custom_call" | custom-call | flops 1000000000 | bytes 4194304 | tf_op jit(solution)/shard_map/halo/pallas_call | solution.py:240
  32.0 0.0 collective-permute-done.10.refs_5_
  32.1 0.7 %collective-permute-done.11.refs_6_ = bf16[64,128]{1,0:T(8,128)(2,1)S(1)} collective-permute-done((bf16[64,128]{1,0:T(8,128)(2,1)S(1)}, bf16[64,128]{1,0:T(8,128)(2,1)S(1)}, u32[]{:S(2)}, u32[]{:S(2)}) %collective-permute-start.11) | collective-permute-done | bytes 16416 | tf_op jit(solution)/shard_map/ppermute | solution.py:314
  32.7 0.6 %finish.5 = (bf16[64,1024]{1,0:T(8,128)(2,1)S(1)}, bf16[64,1536]{1,0:T(8,128)(2,1)S(1)}, f32[64,256]{1,0:T(8,128)S(1)}) custom-call(s32[1]{0:T(128)} %bitcast.index_ref.refs_0_, f32[64,1024]{1,0:T(8,128)S(1)} %halo.6.refs_1_, bf16[256,1024]{1,0:T(8,128)(2,1)S(1)} %get-tuple-element.47.refs_2_.refs_1_, bf16[128,1024]{1,0:T(8,128)(2,1)S(1)} %get-tuple-element.48.refs_3_, ...), custom_call_target="tpu_custom_call" | custom-call | flops 1000000000 | bytes 4194304 | tf_op jit(solution)/shard_map/finish/pallas_call | solution.py:240
  33.3 0.1 collective-permute-start.12
  33.4 2.8 %collective-permute-start.13 = (bf16[64,1024]{1,0:T(8,128)(2,1)S(1)}, bf16[64,1024]{1,0:T(8,128)(2,1)S(1)}, u32[]{:S(2)}, u32[]{:S(2)}) collective-permute-start(bf16[64,1024]{1,0:T(8,128)(2,1)S(1)} %get-tuple-element.63.refs_1_), channel_id=1, source_target_pairs={{0,15},{1,2},{2,1},{3,4},{4,3},{5,6},{6,5},{7,8},{8,7},{9,10},{10,... | collective-permute-start | bytes 393224 | tf_op jit(solution)/shard_map/ppermute | solution.py:301
  36.2 0.0 collective-permute-done.12.message_ref.refs_2_
  36.2 0.6 %collective-permute-start.14 = (bf16[64,128]{1,0:T(8,128)(2,1)S(1)}, bf16[64,128]{1,0:T(8,128)(2,1)S(1)}, u32[]{:S(2)}, u32[]{:S(2)}) collective-permute-start(bf16[64,128]{1,0:T(8,128)(2,1)S(1)} %get-tuple-element.66.refs_4_), channel_id=1, source_target_pairs={{0,8},{1,11},{2,10},{3,9},{4,12},{5,15},{6,14},{7,13},{8,0},{9,3},... | collective-permute-start | bytes 49160 | tf_op jit(solution)/shard_map/ppermute | solution.py:314
  36.9 0.6 %collective-permute-start.15 = (bf16[64,128]{1,0:T(8,128)(2,1)S(1)}, bf16[64,128]{1,0:T(8,128)(2,1)S(1)}, u32[]{:S(2)}, u32[]{:S(2)}) collective-permute-start(bf16[64,128]{1,0:T(8,128)(2,1)S(1)} %get-tuple-element.67.refs_5_), channel_id=1, source_target_pairs={{0,9},{1,10},{2,11},{3,8},{4,13},{5,14},{6,15},{7,12},{8,1},{9,2},... | collective-permute-start | bytes 49160 | tf_op jit(solution)/shard_map/ppermute | solution.py:314
  37.4 1.3 %own.5 = (f32[64,1024]{1,0:T(8,128)S(1)}, bf16[4,64,1024]{2,1,0:T(8,128)(2,1)}) custom-call(s32[1]{0:T(128)} %bitcast.index_ref.refs_0_, bf16[64,1024]{1,0:T(8,128)(2,1)S(1)} %get-tuple-element.63.refs_1_, bf16[64,1536]{1,0:T(8,128)(2,1)S(1)} %collective-permute-done.12.message_ref.refs_2_, ...), custom_call_target="tpu_custom_call", output_to_operand_aliasing={{1}: (6, {})} | custom-call | flops 1000000000 | bytes 4194304 | tf_op jit(solution)/shard_map/own/pallas_call | solution.py:240
  38.7 2.1 %collective-permute-done.13.over_ref = bf16[64,1024]{1,0:T(8,128)(2,1)S(1)} collective-permute-done((bf16[64,1024]{1,0:T(8,128)(2,1)S(1)}, bf16[64,1024]{1,0:T(8,128)(2,1)S(1)}, u32[]{:S(2)}, u32[]{:S(2)}) %collective-permute-start.13) | collective-permute-done | bytes 131104 | tf_op jit(solution)/shard_map/ppermute | solution.py:301
  40.8 0.5 %halo.7.refs_0_ = f32[64,1024]{1,0:T(8,128)S(1)} custom-call(s32[1]{0:T(128)} %bitcast.index_ref.refs_0_, f32[64,1024]{1,0:T(8,128)S(1)} %get-tuple-element.69.acc_ref, bf16[64,1024]{1,0:T(8,128)(2,1)S(1)} %collective-permute-done.13.over_ref, bf16[36,256,256]{2,1,0:T(8,128)(2,1)S(1)} %get-tuple-element.46.d_ref.refs_3_), custom_call_target="tpu_custom_call" | custom-call | flops 1000000000 | bytes 4194304 | tf_op jit(solution)/shard_map/halo/pallas_call | solution.py:240
  41.4 0.0 collective-permute-done.14.refs_2_
  41.4 0.8 %collective-permute-done.15.refs_3_ = bf16[64,128]{1,0:T(8,128)(2,1)S(1)} collective-permute-done((bf16[64,128]{1,0:T(8,128)(2,1)S(1)}, bf16[64,128]{1,0:T(8,128)(2,1)S(1)}, u32[]{:S(2)}, u32[]{:S(2)}) %collective-permute-start.15) | collective-permute-done | bytes 16416 | tf_op jit(solution)/shard_map/ppermute | solution.py:314
  42.1 0.9 %last.1 = bf16[4,64,1024]{2,1,0:T(8,128)(2,1)} custom-call(f32[64,1024]{1,0:T(8,128)S(1)} %halo.7.refs_0_, bf16[256,1024]{1,0:T(8,128)(2,1)S(1)} %get-tuple-element.47.refs_2_.refs_1_, bf16[64,128]{1,0:T(8,128)(2,1)S(1)} %collective-permute-done.14.refs_2_, bf16[64,128]{1,0:T(8,128)(2,1)S(1)} %collective-permute-done.15.refs_3_, ...), custom_call_target="tpu_custom_call", output_to_operand_aliasing={{}: (4, {})} | custom-call | flops 1000000000 | bytes 4194304 | tf_op jit(solution)/shard_map/last/pallas_call | solution.py:240
  (4 shorter events, 0.1 us)
Async XLA Ops:
  0.0 8.4 %copy-start.1 = (bf16[4,32,256]{2,1,0:T(8,128)(2,1)S(1)}, bf16[4,32,256]{2,1,0:T(8,128)(2,1)}, u32[]{:S(2)}) copy-start(bf16[4,32,256]{2,1,0:T(8,128)(2,1)} %refs_5_.3) | copy-start | bytes 196612
  0.0 8.4 %copy-start = (bf16[32,256,256]{2,1,0:T(8,128)(2,1)S(1)}, bf16[32,256,256]{2,1,0:T(8,128)(2,1)}, u32[]{:S(2)}) copy-start(bf16[32,256,256]{2,1,0:T(8,128)(2,1)} %refs_6_.3) | copy-start | bytes 12582916
  1.8 6.2 %collective-permute-start = (bf16[64,1536]{1,0:T(8,128)(2,1)S(1)}, bf16[64,1536]{1,0:T(8,128)(2,1)S(1)}, u32[]{:S(2)}, u32[]{:S(2)}) collective-permute-start(bf16[64,1536]{1,0:T(8,128)(2,1)S(1)} %get-tuple-element.41), channel_id=1, source_target_pairs={{0,1},{1,0},{2,3},{3,2},{4,5},{5,4},{6,7},{7,6},{8,9},{9,8},{10,11... | collective-permute-start | bytes 589832 | tf_op jit(solution)/shard_map/ppermute | solution.py:302
  2.4 8.6 %collective-permute-start.1 = (bf16[64,1024]{1,0:T(8,128)(2,1)}, bf16[64,1024]{1,0:T(8,128)(2,1)S(1)}, u32[]{:S(2)}, u32[]{:S(2)}) collective-permute-start(bf16[64,1024]{1,0:T(8,128)(2,1)} %refs_4_.1), channel_id=1, source_target_pairs={{0,15},{1,2},{2,1},{3,4},{4,3},{5,6},{6,5},{7,8},{8,7},{9,10},{10,... | collective-permute-start | bytes 393224 | tf_op jit(solution)/shard_map/ppermute | solution.py:301
  8.0 4.7 %collective-permute-start.2 = (bf16[64,128]{1,0:T(8,128)(2,1)S(1)}, bf16[64,128]{1,0:T(8,128)(2,1)S(1)}, u32[]{:S(2)}, u32[]{:S(2)}) collective-permute-start(bf16[64,128]{1,0:T(8,128)(2,1)S(1)} %get-tuple-element.43.refs_7_), channel_id=1, source_target_pairs={{0,8},{1,11},{2,10},{3,9},{4,12},{5,15},{6,14},{7,13},{8,0},{9,3},... | collective-permute-start | bytes 49160 | tf_op jit(solution)/shard_map/ppermute | solution.py:314
  8.1 5.0 %collective-permute-start.3 = (bf16[64,128]{1,0:T(8,128)(2,1)S(1)}, bf16[64,128]{1,0:T(8,128)(2,1)S(1)}, u32[]{:S(2)}, u32[]{:S(2)}) collective-permute-start(bf16[64,128]{1,0:T(8,128)(2,1)S(1)} %get-tuple-element.44.refs_8_), channel_id=1, source_target_pairs={{0,9},{1,10},{2,11},{3,8},{4,13},{5,14},{6,15},{7,12},{8,1},{9,2},... | collective-permute-start | bytes 49160 | tf_op jit(solution)/shard_map/ppermute | solution.py:314
  13.7 3.8 %collective-permute-start.4 = (bf16[64,1536]{1,0:T(8,128)(2,1)S(1)}, bf16[64,1536]{1,0:T(8,128)(2,1)S(1)}, u32[]{:S(2)}, u32[]{:S(2)}) collective-permute-start(bf16[64,1536]{1,0:T(8,128)(2,1)S(1)} %get-tuple-element.51), channel_id=1, source_target_pairs={{0,1},{1,0},{2,3},{3,2},{4,5},{5,4},{6,7},{7,6},{8,9},{9,8},{10,11... | collective-permute-start | bytes 589832 | tf_op jit(solution)/shard_map/ppermute | solution.py:302
  13.8 7.2 %collective-permute-start.5 = (bf16[64,1024]{1,0:T(8,128)(2,1)S(1)}, bf16[64,1024]{1,0:T(8,128)(2,1)S(1)}, u32[]{:S(2)}, u32[]{:S(2)}) collective-permute-start(bf16[64,1024]{1,0:T(8,128)(2,1)S(1)} %get-tuple-element.50.refs_1_), channel_id=1, source_target_pairs={{0,15},{1,2},{2,1},{3,4},{4,3},{5,6},{6,5},{7,8},{8,7},{9,10},{10,... | collective-permute-start | bytes 393224 | tf_op jit(solution)/shard_map/ppermute | solution.py:301
  17.5 4.7 %collective-permute-start.6 = (bf16[64,128]{1,0:T(8,128)(2,1)S(1)}, bf16[64,128]{1,0:T(8,128)(2,1)S(1)}, u32[]{:S(2)}, u32[]{:S(2)}) collective-permute-start(bf16[64,128]{1,0:T(8,128)(2,1)S(1)} %get-tuple-element.53.refs_4_), channel_id=1, source_target_pairs={{0,8},{1,11},{2,10},{3,9},{4,12},{5,15},{6,14},{7,13},{8,0},{9,3},... | collective-permute-start | bytes 49160 | tf_op jit(solution)/shard_map/ppermute | solution.py:314
  18.2 5.3 %collective-permute-start.7 = (bf16[64,128]{1,0:T(8,128)(2,1)S(1)}, bf16[64,128]{1,0:T(8,128)(2,1)S(1)}, u32[]{:S(2)}, u32[]{:S(2)}) collective-permute-start(bf16[64,128]{1,0:T(8,128)(2,1)S(1)} %get-tuple-element.54.refs_5_), channel_id=1, source_target_pairs={{0,9},{1,10},{2,11},{3,8},{4,13},{5,14},{6,15},{7,12},{8,1},{9,2},... | collective-permute-start | bytes 49160 | tf_op jit(solution)/shard_map/ppermute | solution.py:314
  24.0 2.7 %collective-permute-start.8 = (bf16[64,1536]{1,0:T(8,128)(2,1)S(1)}, bf16[64,1536]{1,0:T(8,128)(2,1)S(1)}, u32[]{:S(2)}, u32[]{:S(2)}) collective-permute-start(bf16[64,1536]{1,0:T(8,128)(2,1)S(1)} %get-tuple-element.57), channel_id=1, source_target_pairs={{0,1},{1,0},{2,3},{3,2},{4,5},{5,4},{6,7},{7,6},{8,9},{9,8},{10,11... | collective-permute-start | bytes 589832 | tf_op jit(solution)/shard_map/ppermute | solution.py:302
  24.1 7.4 %collective-permute-start.9 = (bf16[64,1024]{1,0:T(8,128)(2,1)S(1)}, bf16[64,1024]{1,0:T(8,128)(2,1)S(1)}, u32[]{:S(2)}, u32[]{:S(2)}) collective-permute-start(bf16[64,1024]{1,0:T(8,128)(2,1)S(1)} %get-tuple-element.56.refs_1_), channel_id=1, source_target_pairs={{0,15},{1,2},{2,1},{3,4},{4,3},{5,6},{6,5},{7,8},{8,7},{9,10},{10,... | collective-permute-start | bytes 393224 | tf_op jit(solution)/shard_map/ppermute | solution.py:301
  26.7 5.3 %collective-permute-start.10 = (bf16[64,128]{1,0:T(8,128)(2,1)S(1)}, bf16[64,128]{1,0:T(8,128)(2,1)S(1)}, u32[]{:S(2)}, u32[]{:S(2)}) collective-permute-start(bf16[64,128]{1,0:T(8,128)(2,1)S(1)} %get-tuple-element.59.refs_4_), channel_id=1, source_target_pairs={{0,8},{1,11},{2,10},{3,9},{4,12},{5,15},{6,14},{7,13},{8,0},{9,3},... | collective-permute-start | bytes 49160 | tf_op jit(solution)/shard_map/ppermute | solution.py:314
  27.6 5.1 %collective-permute-start.11 = (bf16[64,128]{1,0:T(8,128)(2,1)S(1)}, bf16[64,128]{1,0:T(8,128)(2,1)S(1)}, u32[]{:S(2)}, u32[]{:S(2)}) collective-permute-start(bf16[64,128]{1,0:T(8,128)(2,1)S(1)} %get-tuple-element.60.refs_5_), channel_id=1, source_target_pairs={{0,9},{1,10},{2,11},{3,8},{4,13},{5,14},{6,15},{7,12},{8,1},{9,2},... | collective-permute-start | bytes 49160 | tf_op jit(solution)/shard_map/ppermute | solution.py:314
  33.3 2.9 %collective-permute-start.12 = (bf16[64,1536]{1,0:T(8,128)(2,1)S(1)}, bf16[64,1536]{1,0:T(8,128)(2,1)S(1)}, u32[]{:S(2)}, u32[]{:S(2)}) collective-permute-start(bf16[64,1536]{1,0:T(8,128)(2,1)S(1)} %get-tuple-element.64), channel_id=1, source_target_pairs={{0,1},{1,0},{2,3},{3,2},{4,5},{5,4},{6,7},{7,6},{8,9},{9,8},{10,11... | collective-permute-start | bytes 589832 | tf_op jit(solution)/shard_map/ppermute | solution.py:302
  33.4 7.4 %collective-permute-start.13 = (bf16[64,1024]{1,0:T(8,128)(2,1)S(1)}, bf16[64,1024]{1,0:T(8,128)(2,1)S(1)}, u32[]{:S(2)}, u32[]{:S(2)}) collective-permute-start(bf16[64,1024]{1,0:T(8,128)(2,1)S(1)} %get-tuple-element.63.refs_1_), channel_id=1, source_target_pairs={{0,15},{1,2},{2,1},{3,4},{4,3},{5,6},{6,5},{7,8},{8,7},{9,10},{10,... | collective-permute-start | bytes 393224 | tf_op jit(solution)/shard_map/ppermute | solution.py:301
  36.2 5.2 %collective-permute-start.14 = (bf16[64,128]{1,0:T(8,128)(2,1)S(1)}, bf16[64,128]{1,0:T(8,128)(2,1)S(1)}, u32[]{:S(2)}, u32[]{:S(2)}) collective-permute-start(bf16[64,128]{1,0:T(8,128)(2,1)S(1)} %get-tuple-element.66.refs_4_), channel_id=1, source_target_pairs={{0,8},{1,11},{2,10},{3,9},{4,12},{5,15},{6,14},{7,13},{8,0},{9,3},... | collective-permute-start | bytes 49160 | tf_op jit(solution)/shard_map/ppermute | solution.py:314
  36.9 5.3 %collective-permute-start.15 = (bf16[64,128]{1,0:T(8,128)(2,1)S(1)}, bf16[64,128]{1,0:T(8,128)(2,1)S(1)}, u32[]{:S(2)}, u32[]{:S(2)}) collective-permute-start(bf16[64,128]{1,0:T(8,128)(2,1)S(1)} %get-tuple-element.67.refs_5_), channel_id=1, source_target_pairs={{0,9},{1,10},{2,11},{3,8},{4,13},{5,14},{6,15},{7,12},{8,1},{9,2},... | collective-permute-start | bytes 49160 | tf_op jit(solution)/shard_map/ppermute | solution.py:314

commit v15 on v14

--- a/solution.py
+++ b/solution.py
@@ -57,7 +57,7 @@
                 (l * members + m, (l + self.hops[0]) % loop_size * members + (m ^ (m % 2 * 2) ^ other))
                 for l, m in places
             ]
-            for other in range(2)
+            for other in (1, 0)
         ]
         self.routes = [
             [(l * members + m, (l + hop) % loop_size * members + (m + step) % members) for l, m in places]
@@ -97,8 +97,8 @@
         total = (keep_ref[...] + (upper + lower)).astype(BF16)
         second = lax.rem(index_ref[0], 2) == 1
         first, last = total[:, : self.width], total[:, self.width :]
-        out_refs[0][...] = jnp.where(second, last, first)
-        out_refs[1][...] = jnp.where(second, first, last)
+        out_refs[0][...] = jnp.where(second, first, last)
+        out_refs[1][...] = jnp.where(second, last, first)
 
     def far_sum(self, far_refs):
         return sum(ref[...].astype(F32) for ref in far_refs)

time: 43.1 us -> 41.7 us (0.968)
  waiting for transfers between devices: 10.9 us -> 8.49 us
  starting transfers between devices: 19.6 us -> 20.5 us
    ppermute x8, waiting for transfers between devices: 4.97 us -> 1.67 us  [on_device(): fars = [lax.ppermute(s, axes, route) for s, route in zip(sends, routes)]]
    ppermute x4, starting transfers between devices: 0.73 us -> 2.69 us  [on_device(): near = lax.ppermute(sends[0] if plan.paired else current, axes, plan.near)]
    ppermute x4, starting transfers between devices: 14.7 us -> 12.8 us  [on_device(): over = lax.ppermute(block if product == 0 else current, axes, plan.over)]
    ppermute x4, waiting for transfers between devices: 5.92 us -> 6.8 us  [on_device(): over = lax.ppermute(block if product == 0 else current, axes, plan.over)]
    ppermute x8, starting transfers between devices: 4.21 us -> 5.02 us  [on_device(): fars = [lax.ppermute(s, axes, route) for s, route in zip(sends, routes)]]
  transfers between devices with their start and end apart: 16 -> 16, of which waited for: 10 -> 5; matrix products, arithmetic and copies ran while one was open for 0% -> 0% of each run, Pallas kernels for 18% -> 19%
where the time goes in v15:
time: 41.7 us; the launch traced here: 41.5 us
  starting transfers between devices  20.5 us (49%)
  Pallas kernels  12.3 us (29%)
  waiting for transfers between devices  8.49 us (20%)
    ppermute x4, starting transfers between devices, on_device(): over = lax.ppermute(block if product == 0 else current, axes, plan.over)  12.8 us
    pallas_call x17, Pallas kernels, call(): pl.pallas_call(kernel, in_specs=list(specs), out_specs=out_specs or [IN_V...  12.3 us
    ppermute x4, waiting for transfers between devices, on_device(): over = lax.ppermute(block if product == 0 else current, axes, plan.over)  6.8 us
    ppermute x8, starting transfers between devices, on_device(): fars = [lax.ppermute(s, axes, route) for s, route in zip(sends, routes)]  5.02 us
    ppermute x4, starting transfers between devices, on_device(): near = lax.ppermute(sends[0] if plan.paired else current, axes, plan.near)  2.69 us
    ppermute x8, waiting for transfers between devices, on_device(): fars = [lax.ppermute(s, axes, route) for s, route in zip(sends, routes)]  1.67 us
  transfers between devices with their start and end apart: 16, of which 5 were waited for; matrix products, arithmetic and copies ran while one was open for 0% of the time, Pallas kernels for 19%

profile of v15, /device:TPU:0, one launch (start us, length us, event | category | flops | bytes accessed | tf_op | source)
XLA Modules:
  0.0 41.5 jit_solution(3572719299007899675)
XLA Ops:
  0.0 0.0 copy-start.1
  0.0 0.0 copy-start
  0.0 1.8 %prepare.1 = (bf16[64,1024]{1,0:T(8,128)(2,1)S(1)}, bf16[1,512,256]{2,1,0:T(8,128)(2,1)S(1)}, bf16[128,1024]{1,0:T(8,128)(2,1)S(1)}, s32[32]{0:T(128)S(4)}, s32[...) custom-call(s32[1]{0:T(128)} %bitcast.index_ref.refs_0_, s32[32]{0:T(128)} %refs_0_.1, s32[32]{0:T(128)} %refs_1_.1, ...), custom_call_target="tpu_custom_call" | custom-call | flops 1000000000 | bytes 4194304 | tf_op jit(solution)/shard_map/prepare/pallas_call | solution.py:240
  1.8 0.5 %collective-permute-start = (bf16[64,1536]{1,0:T(8,128)(2,1)S(1)}, bf16[64,1536]{1,0:T(8,128)(2,1)S(1)}, u32[]{:S(2)}, u32[]{:S(2)}) collective-permute-start(bf16[64,1536]{1,0:T(8,128)(2,1)S(1)} %get-tuple-element.41), channel_id=1, source_target_pairs={{0,1},{1,0},{2,3},{3,2},{4,5},{5,4},{6,7},{7,6},{8,9},{9,8},{10,11... | collective-permute-start | bytes 589832 | tf_op jit(solution)/shard_map/ppermute | solution.py:302
  2.4 5.6 %collective-permute-start.1 = (bf16[64,1024]{1,0:T(8,128)(2,1)}, bf16[64,1024]{1,0:T(8,128)(2,1)S(1)}, u32[]{:S(2)}, u32[]{:S(2)}) collective-permute-start(bf16[64,1024]{1,0:T(8,128)(2,1)} %refs_4_.1), channel_id=1, source_target_pairs={{0,15},{1,2},{2,1},{3,4},{4,3},{5,6},{6,5},{7,8},{8,7},{9,10},{10,... | collective-permute-start | bytes 393224 | tf_op jit(solution)/shard_map/ppermute | solution.py:301
  8.0 0.0 collective-permute-done.message_ref.refs_4_
  8.0 0.1 collective-permute-start.2
  8.1 0.1 collective-permute-start.3
  8.2 0.0 copy-done.1
  8.2 0.0 copy-done
  8.2 1.9 %first_own.1 = (f32[64,1024]{1,0:T(8,128)S(1)}, bf16[36,256,256]{2,1,0:T(8,128)(2,1)S(1)}, bf16[256,1024]{1,0:T(8,128)(2,1)S(1)}) custom-call(s32[1]{0:T(128)} %bitcast.index_ref.refs_0_, s32[32]{0:T(128)S(4)} %get-tuple-element.38.refs_1_, s32[32]{0:T(128)S(4)} %get-tuple-element.39.refs_2_, bf16[64,1024]{1,0:T(8,128)(2,1)S(1)} %get-tuple-element.40.refs_3_, ...), custom_call_target="tpu_custom_call" | custom-call | flops 1000000000 | bytes 4194304 | tf_op jit(solution)/shard_map/first_own/pallas_call | solution.py:240
  10.1 0.9 %collective-permute-done.1.over_ref = bf16[64,1024]{1,0:T(8,128)(2,1)S(1)} collective-permute-done((bf16[64,1024]{1,0:T(8,128)(2,1)}, bf16[64,1024]{1,0:T(8,128)(2,1)S(1)}, u32[]{:S(2)}, u32[]{:S(2)}) %collective-permute-start.1) | collective-permute-done | bytes 131104 | tf_op jit(solution)/shard_map/ppermute | solution.py:301
  10.9 0.5 %halo.4.refs_1_ = f32[64,1024]{1,0:T(8,128)S(1)} custom-call(s32[1]{0:T(128)} %bitcast.index_ref.refs_0_, f32[64,1024]{1,0:T(8,128)S(1)} %get-tuple-element.45.acc_ref, bf16[64,1024]{1,0:T(8,128)(2,1)S(1)} %collective-permute-done.1.over_ref, bf16[36,256,256]{2,1,0:T(8,128)(2,1)S(1)} %get-tuple-element.46.d_ref.refs_3_), custom_call_target="tpu_custom_call" | custom-call | flops 1000000000 | bytes 4194304 | tf_op jit(solution)/shard_map/halo/pallas_call | solution.py:240
  11.5 1.7 %collective-permute-done.2.refs_5_ = bf16[64,128]{1,0:T(8,128)(2,1)S(1)} collective-permute-done((bf16[64,128]{1,0:T(8,128)(2,1)S(1)}, bf16[64,128]{1,0:T(8,128)(2,1)S(1)}, u32[]{:S(2)}, u32[]{:S(2)}) %collective-permute-start.2) | collective-permute-done | bytes 16416 | tf_op jit(solution)/shard_map/ppermute | solution.py:314
  13.1 0.0 collective-permute-done.3.refs_6_
  13.1 0.6 %finish.3 = (bf16[64,1024]{1,0:T(8,128)(2,1)S(1)}, bf16[64,1536]{1,0:T(8,128)(2,1)S(1)}, f32[64,256]{1,0:T(8,128)S(1)}) custom-call(s32[1]{0:T(128)} %bitcast.index_ref.refs_0_, f32[64,1024]{1,0:T(8,128)S(1)} %halo.4.refs_1_, bf16[256,1024]{1,0:T(8,128)(2,1)S(1)} %get-tuple-element.47.refs_2_.refs_1_, bf16[128,1024]{1,0:T(8,128)(2,1)S(1)} %get-tuple-element.48.refs_3_, ...), custom_call_target="tpu_custom_call" | custom-call | flops 1000000000 | bytes 4194304 | tf_op jit(solution)/shard_map/finish/pallas_call | solution.py:240
  13.7 1.1 %collective-permute-start.4 = (bf16[64,1536]{1,0:T(8,128)(2,1)S(1)}, bf16[64,1536]{1,0:T(8,128)(2,1)S(1)}, u32[]{:S(2)}, u32[]{:S(2)}) collective-permute-start(bf16[64,1536]{1,0:T(8,128)(2,1)S(1)} %get-tuple-element.51), channel_id=1, source_target_pairs={{0,1},{1,0},{2,3},{3,2},{4,5},{5,4},{6,7},{7,6},{8,9},{9,8},{10,11... | collective-permute-start | bytes 589832 | tf_op jit(solution)/shard_map/ppermute | solution.py:302
  14.8 2.3 %collective-permute-start.5 = (bf16[64,1024]{1,0:T(8,128)(2,1)S(1)}, bf16[64,1024]{1,0:T(8,128)(2,1)S(1)}, u32[]{:S(2)}, u32[]{:S(2)}) collective-permute-start(bf16[64,1024]{1,0:T(8,128)(2,1)S(1)} %get-tuple-element.50.refs_1_), channel_id=1, source_target_pairs={{0,15},{1,2},{2,1},{3,4},{4,3},{5,6},{6,5},{7,8},{8,7},{9,10},{10,... | collective-permute-start | bytes 393224 | tf_op jit(solution)/shard_map/ppermute | solution.py:301
  17.1 0.0 collective-permute-done.4.message_ref.refs_2_
  17.1 0.3 collective-permute-start.6
  17.4 1.4 %collective-permute-start.7 = (bf16[64,128]{1,0:T(8,128)(2,1)S(1)}, bf16[64,128]{1,0:T(8,128)(2,1)S(1)}, u32[]{:S(2)}, u32[]{:S(2)}) collective-permute-start(bf16[64,128]{1,0:T(8,128)(2,1)S(1)} %get-tuple-element.54.refs_5_), channel_id=1, source_target_pairs={{0,8},{1,11},{2,10},{3,9},{4,12},{5,15},{6,14},{7,13},{8,0},{9,3},... | collective-permute-start | bytes 49160 | tf_op jit(solution)/shard_map/ppermute | solution.py:314
  18.8 1.3 %own.3 = (f32[64,1024]{1,0:T(8,128)S(1)}, bf16[4,64,1024]{2,1,0:T(8,128)(2,1)}) custom-call(s32[1]{0:T(128)} %bitcast.index_ref.refs_0_, bf16[64,1024]{1,0:T(8,128)(2,1)S(1)} %get-tuple-element.50.refs_1_, bf16[64,1536]{1,0:T(8,128)(2,1)S(1)} %collective-permute-done.4.message_ref.refs_2_, bf16[36,256,256]{2,1,0:T(8,128)(2,1)S(1)} %get-tuple-element.46.d_ref.refs_3_, ...), custom_call_target="tpu_custom_call" | custom-call | flops 1000000000 | bytes 4194304 | tf_op jit(solution)/shard_map/own/pallas_call | solution.py:240
  20.1 1.9 %collective-permute-done.5.over_ref = bf16[64,1024]{1,0:T(8,128)(2,1)S(1)} collective-permute-done((bf16[64,1024]{1,0:T(8,128)(2,1)S(1)}, bf16[64,1024]{1,0:T(8,128)(2,1)S(1)}, u32[]{:S(2)}, u32[]{:S(2)}) %collective-permute-start.5) | collective-permute-done | bytes 131104 | tf_op jit(solution)/shard_map/ppermute | solution.py:301
  22.0 0.5 %halo.5.refs_1_ = f32[64,1024]{1,0:T(8,128)S(1)} custom-call(s32[1]{0:T(128)} %bitcast.index_ref.refs_0_, f32[64,1024]{1,0:T(8,128)S(1)} %get-tuple-element.55.acc_ref, bf16[64,1024]{1,0:T(8,128)(2,1)S(1)} %collective-permute-done.5.over_ref, bf16[36,256,256]{2,1,0:T(8,128)(2,1)S(1)} %get-tuple-element.46.d_ref.refs_3_), custom_call_target="tpu_custom_call" | custom-call | flops 1000000000 | bytes 4194304 | tf_op jit(solution)/shard_map/halo/pallas_call | solution.py:240
  22.5 0.0 collective-permute-done.6.refs_5_
  22.5 0.0 collective-permute-done.7.refs_6_
  22.6 0.6 %finish.4 = (bf16[64,1024]{1,0:T(8,128)(2,1)S(1)}, bf16[64,1536]{1,0:T(8,128)(2,1)S(1)}, f32[64,256]{1,0:T(8,128)S(1)}) custom-call(s32[1]{0:T(128)} %bitcast.index_ref.refs_0_, f32[64,1024]{1,0:T(8,128)S(1)} %halo.5.refs_1_, bf16[256,1024]{1,0:T(8,128)(2,1)S(1)} %get-tuple-element.47.refs_2_.refs_1_, bf16[128,1024]{1,0:T(8,128)(2,1)S(1)} %get-tuple-element.48.refs_3_, ...), custom_call_target="tpu_custom_call" | custom-call | flops 1000000000 | bytes 4194304 | tf_op jit(solution)/shard_map/finish/pallas_call | solution.py:240
  23.1 0.3 collective-permute-start.8
  23.5 2.4 %collective-permute-start.9 = (bf16[64,1024]{1,0:T(8,128)(2,1)S(1)}, bf16[64,1024]{1,0:T(8,128)(2,1)S(1)}, u32[]{:S(2)}, u32[]{:S(2)}) collective-permute-start(bf16[64,1024]{1,0:T(8,128)(2,1)S(1)} %get-tuple-element.56.refs_1_), channel_id=1, source_target_pairs={{0,15},{1,2},{2,1},{3,4},{4,3},{5,6},{6,5},{7,8},{8,7},{9,10},{10,... | collective-permute-start | bytes 393224 | tf_op jit(solution)/shard_map/ppermute | solution.py:301
  25.9 0.0 collective-permute-done.8.message_ref.refs_2_
  25.9 0.6 %collective-permute-start.10 = (bf16[64,128]{1,0:T(8,128)(2,1)S(1)}, bf16[64,128]{1,0:T(8,128)(2,1)S(1)}, u32[]{:S(2)}, u32[]{:S(2)}) collective-permute-start(bf16[64,128]{1,0:T(8,128)(2,1)S(1)} %get-tuple-element.59.refs_4_), channel_id=1, source_target_pairs={{0,9},{1,10},{2,11},{3,8},{4,13},{5,14},{6,15},{7,12},{8,1},{9,2},... | collective-permute-start | bytes 49160 | tf_op jit(solution)/shard_map/ppermute | solution.py:314
  26.5 1.0 %collective-permute-start.11 = (bf16[64,128]{1,0:T(8,128)(2,1)S(1)}, bf16[64,128]{1,0:T(8,128)(2,1)S(1)}, u32[]{:S(2)}, u32[]{:S(2)}) collective-permute-start(bf16[64,128]{1,0:T(8,128)(2,1)S(1)} %get-tuple-element.60.refs_5_), channel_id=1, source_target_pairs={{0,8},{1,11},{2,10},{3,9},{4,12},{5,15},{6,14},{7,13},{8,0},{9,3},... | collective-permute-start | bytes 49160 | tf_op jit(solution)/shard_map/ppermute | solution.py:314
  27.5 1.3 %own.4 = (f32[64,1024]{1,0:T(8,128)S(1)}, bf16[4,64,1024]{2,1,0:T(8,128)(2,1)}) custom-call(s32[1]{0:T(128)} %bitcast.index_ref.refs_0_, bf16[64,1024]{1,0:T(8,128)(2,1)S(1)} %get-tuple-element.56.refs_1_, bf16[64,1536]{1,0:T(8,128)(2,1)S(1)} %collective-permute-done.8.message_ref.refs_2_, ...), custom_call_target="tpu_custom_call", output_to_operand_aliasing={{1}: (6, {})} | custom-call | flops 1000000000 | bytes 4194304 | tf_op jit(solution)/shard_map/own/pallas_call | solution.py:240
  28.8 2.0 %collective-permute-done.9.over_ref = bf16[64,1024]{1,0:T(8,128)(2,1)S(1)} collective-permute-done((bf16[64,1024]{1,0:T(8,128)(2,1)S(1)}, bf16[64,1024]{1,0:T(8,128)(2,1)S(1)}, u32[]{:S(2)}, u32[]{:S(2)}) %collective-permute-start.9) | collective-permute-done | bytes 131104 | tf_op jit(solution)/shard_map/ppermute | solution.py:301
  30.8 0.5 %halo.6.refs_1_ = f32[64,1024]{1,0:T(8,128)S(1)} custom-call(s32[1]{0:T(128)} %bitcast.index_ref.refs_0_, f32[64,1024]{1,0:T(8,128)S(1)} %get-tuple-element.62.acc_ref, bf16[64,1024]{1,0:T(8,128)(2,1)S(1)} %collective-permute-done.9.over_ref, bf16[36,256,256]{2,1,0:T(8,128)(2,1)S(1)} %get-tuple-element.46.d_ref.refs_3_), custom_call_target="tpu_custom_call" | custom-call | flops 1000000000 | bytes 4194304 | tf_op jit(solution)/shard_map/halo/pallas_call | solution.py:240
  31.4 0.0 collective-permute-done.10.refs_5_
  31.4 0.0 collective-permute-done.11.refs_6_
  31.4 0.6 %finish.5 = (bf16[64,1024]{1,0:T(8,128)(2,1)S(1)}, bf16[64,1536]{1,0:T(8,128)(2,1)S(1)}, f32[64,256]{1,0:T(8,128)S(1)}) custom-call(s32[1]{0:T(128)} %bitcast.index_ref.refs_0_, f32[64,1024]{1,0:T(8,128)S(1)} %halo.6.refs_1_, bf16[256,1024]{1,0:T(8,128)(2,1)S(1)} %get-tuple-element.47.refs_2_.refs_1_, bf16[128,1024]{1,0:T(8,128)(2,1)S(1)} %get-tuple-element.48.refs_3_, ...), custom_call_target="tpu_custom_call" | custom-call | flops 1000000000 | bytes 4194304 | tf_op jit(solution)/shard_map/finish/pallas_call | solution.py:240
  32.0 0.8 %collective-permute-start.12 = (bf16[64,1536]{1,0:T(8,128)(2,1)S(1)}, bf16[64,1536]{1,0:T(8,128)(2,1)S(1)}, u32[]{:S(2)}, u32[]{:S(2)}) collective-permute-start(bf16[64,1536]{1,0:T(8,128)(2,1)S(1)} %get-tuple-element.64), channel_id=1, source_target_pairs={{0,1},{1,0},{2,3},{3,2},{4,5},{5,4},{6,7},{7,6},{8,9},{9,8},{10,11... | collective-permute-start | bytes 589832 | tf_op jit(solution)/shard_map/ppermute | solution.py:302
  32.7 2.5 %collective-permute-start.13 = (bf16[64,1024]{1,0:T(8,128)(2,1)S(1)}, bf16[64,1024]{1,0:T(8,128)(2,1)S(1)}, u32[]{:S(2)}, u32[]{:S(2)}) collective-permute-start(bf16[64,1024]{1,0:T(8,128)(2,1)S(1)} %get-tuple-element.63.refs_1_), channel_id=1, source_target_pairs={{0,15},{1,2},{2,1},{3,4},{4,3},{5,6},{6,5},{7,8},{8,7},{9,10},{10,... | collective-permute-start | bytes 393224 | tf_op jit(solution)/shard_map/ppermute | solution.py:301
  35.2 0.0 collective-permute-done.12.message_ref.refs_2_
  35.2 0.1 collective-permute-start.14
  35.3 1.5 %collective-permute-start.15 = (bf16[64,128]{1,0:T(8,128)(2,1)S(1)}, bf16[64,128]{1,0:T(8,128)(2,1)S(1)}, u32[]{:S(2)}, u32[]{:S(2)}) collective-permute-start(bf16[64,128]{1,0:T(8,128)(2,1)S(1)} %get-tuple-element.67.refs_5_), channel_id=1, source_target_pairs={{0,8},{1,11},{2,10},{3,9},{4,12},{5,15},{6,14},{7,13},{8,0},{9,3},... | collective-permute-start | bytes 49160 | tf_op jit(solution)/shard_map/ppermute | solution.py:314
  36.8 1.3 %own.5 = (f32[64,1024]{1,0:T(8,128)S(1)}, bf16[4,64,1024]{2,1,0:T(8,128)(2,1)}) custom-call(s32[1]{0:T(128)} %bitcast.index_ref.refs_0_, bf16[64,1024]{1,0:T(8,128)(2,1)S(1)} %get-tuple-element.63.refs_1_, bf16[64,1536]{1,0:T(8,128)(2,1)S(1)} %collective-permute-done.12.message_ref.refs_2_, ...), custom_call_target="tpu_custom_call", output_to_operand_aliasing={{1}: (6, {})} | custom-call | flops 1000000000 | bytes 4194304 | tf_op jit(solution)/shard_map/own/pallas_call | solution.py:240
  38.1 2.0 %collective-permute-done.13.over_ref = bf16[64,1024]{1,0:T(8,128)(2,1)S(1)} collective-permute-done((bf16[64,1024]{1,0:T(8,128)(2,1)S(1)}, bf16[64,1024]{1,0:T(8,128)(2,1)S(1)}, u32[]{:S(2)}, u32[]{:S(2)}) %collective-permute-start.13) | collective-permute-done | bytes 131104 | tf_op jit(solution)/shard_map/ppermute | solution.py:301
  40.1 0.5 %halo.7.refs_0_ = f32[64,1024]{1,0:T(8,128)S(1)} custom-call(s32[1]{0:T(128)} %bitcast.index_ref.refs_0_, f32[64,1024]{1,0:T(8,128)S(1)} %get-tuple-element.69.acc_ref, bf16[64,1024]{1,0:T(8,128)(2,1)S(1)} %collective-permute-done.13.over_ref, bf16[36,256,256]{2,1,0:T(8,128)(2,1)S(1)} %get-tuple-element.46.d_ref.refs_3_), custom_call_target="tpu_custom_call" | custom-call | flops 1000000000 | bytes 4194304 | tf_op jit(solution)/shard_map/halo/pallas_call | solution.py:240
  40.6 0.0 collective-permute-done.14.refs_2_
  40.6 0.0 collective-permute-done.15.refs_3_
  40.6 0.9 %last.1 = bf16[4,64,1024]{2,1,0:T(8,128)(2,1)} custom-call(f32[64,1024]{1,0:T(8,128)S(1)} %halo.7.refs_0_, bf16[256,1024]{1,0:T(8,128)(2,1)S(1)} %get-tuple-element.47.refs_2_.refs_1_, bf16[64,128]{1,0:T(8,128)(2,1)S(1)} %collective-permute-done.14.refs_2_, bf16[64,128]{1,0:T(8,128)(2,1)S(1)} %collective-permute-done.15.refs_3_, ...), custom_call_target="tpu_custom_call", output_to_operand_aliasing={{}: (4, {})} | custom-call | flops 1000000000 | bytes 4194304 | tf_op jit(solution)/shard_map/last/pallas_call | solution.py:240
  (4 shorter events, 0.1 us)
Async XLA Ops:
  0.0 8.2 %copy-start.1 = (bf16[4,32,256]{2,1,0:T(8,128)(2,1)S(1)}, bf16[4,32,256]{2,1,0:T(8,128)(2,1)}, u32[]{:S(2)}) copy-start(bf16[4,32,256]{2,1,0:T(8,128)(2,1)} %refs_5_.3) | copy-start | bytes 196612
  0.0 8.2 %copy-start = (bf16[32,256,256]{2,1,0:T(8,128)(2,1)S(1)}, bf16[32,256,256]{2,1,0:T(8,128)(2,1)}, u32[]{:S(2)}) copy-start(bf16[32,256,256]{2,1,0:T(8,128)(2,1)} %refs_6_.3) | copy-start | bytes 12582916
  1.8 6.2 %collective-permute-start = (bf16[64,1536]{1,0:T(8,128)(2,1)S(1)}, bf16[64,1536]{1,0:T(8,128)(2,1)S(1)}, u32[]{:S(2)}, u32[]{:S(2)}) collective-permute-start(bf16[64,1536]{1,0:T(8,128)(2,1)S(1)} %get-tuple-element.41), channel_id=1, source_target_pairs={{0,1},{1,0},{2,3},{3,2},{4,5},{5,4},{6,7},{7,6},{8,9},{9,8},{10,11... | collective-permute-start | bytes 589832 | tf_op jit(solution)/shard_map/ppermute | solution.py:302
  2.4 8.6 %collective-permute-start.1 = (bf16[64,1024]{1,0:T(8,128)(2,1)}, bf16[64,1024]{1,0:T(8,128)(2,1)S(1)}, u32[]{:S(2)}, u32[]{:S(2)}) collective-permute-start(bf16[64,1024]{1,0:T(8,128)(2,1)} %refs_4_.1), channel_id=1, source_target_pairs={{0,15},{1,2},{2,1},{3,4},{4,3},{5,6},{6,5},{7,8},{8,7},{9,10},{10,... | collective-permute-start | bytes 393224 | tf_op jit(solution)/shard_map/ppermute | solution.py:301
  8.0 5.1 %collective-permute-start.2 = (bf16[64,128]{1,0:T(8,128)(2,1)S(1)}, bf16[64,128]{1,0:T(8,128)(2,1)S(1)}, u32[]{:S(2)}, u32[]{:S(2)}) collective-permute-start(bf16[64,128]{1,0:T(8,128)(2,1)S(1)} %get-tuple-element.43.refs_7_), channel_id=1, source_target_pairs={{0,9},{1,10},{2,11},{3,8},{4,13},{5,14},{6,15},{7,12},{8,1},{9,2},... | collective-permute-start | bytes 49160 | tf_op jit(solution)/shard_map/ppermute | solution.py:314
  8.1 5.0 %collective-permute-start.3 = (bf16[64,128]{1,0:T(8,128)(2,1)S(1)}, bf16[64,128]{1,0:T(8,128)(2,1)S(1)}, u32[]{:S(2)}, u32[]{:S(2)}) collective-permute-start(bf16[64,128]{1,0:T(8,128)(2,1)S(1)} %get-tuple-element.44.refs_8_), channel_id=1, source_target_pairs={{0,8},{1,11},{2,10},{3,9},{4,12},{5,15},{6,14},{7,13},{8,0},{9,3},... | collective-permute-start | bytes 49160 | tf_op jit(solution)/shard_map/ppermute | solution.py:314
  13.7 3.4 %collective-permute-start.4 = (bf16[64,1536]{1,0:T(8,128)(2,1)S(1)}, bf16[64,1536]{1,0:T(8,128)(2,1)S(1)}, u32[]{:S(2)}, u32[]{:S(2)}) collective-permute-start(bf16[64,1536]{1,0:T(8,128)(2,1)S(1)} %get-tuple-element.51), channel_id=1, source_target_pairs={{0,1},{1,0},{2,3},{3,2},{4,5},{5,4},{6,7},{7,6},{8,9},{9,8},{10,11... | collective-permute-start | bytes 589832 | tf_op jit(solution)/shard_map/ppermute | solution.py:302
  14.8 7.2 %collective-permute-start.5 = (bf16[64,1024]{1,0:T(8,128)(2,1)S(1)}, bf16[64,1024]{1,0:T(8,128)(2,1)S(1)}, u32[]{:S(2)}, u32[]{:S(2)}) collective-permute-start(bf16[64,1024]{1,0:T(8,128)(2,1)S(1)} %get-tuple-element.50.refs_1_), channel_id=1, source_target_pairs={{0,15},{1,2},{2,1},{3,4},{4,3},{5,6},{6,5},{7,8},{8,7},{9,10},{10,... | collective-permute-start | bytes 393224 | tf_op jit(solution)/shard_map/ppermute | solution.py:301
  17.1 5.4 %collective-permute-start.6 = (bf16[64,128]{1,0:T(8,128)(2,1)S(1)}, bf16[64,128]{1,0:T(8,128)(2,1)S(1)}, u32[]{:S(2)}, u32[]{:S(2)}) collective-permute-start(bf16[64,128]{1,0:T(8,128)(2,1)S(1)} %get-tuple-element.53.refs_4_), channel_id=1, source_target_pairs={{0,9},{1,10},{2,11},{3,8},{4,13},{5,14},{6,15},{7,12},{8,1},{9,2},... | collective-permute-start | bytes 49160 | tf_op jit(solution)/shard_map/ppermute | solution.py:314
  17.4 5.1 %collective-permute-start.7 = (bf16[64,128]{1,0:T(8,128)(2,1)S(1)}, bf16[64,128]{1,0:T(8,128)(2,1)S(1)}, u32[]{:S(2)}, u32[]{:S(2)}) collective-permute-start(bf16[64,128]{1,0:T(8,128)(2,1)S(1)} %get-tuple-element.54.refs_5_), channel_id=1, source_target_pairs={{0,8},{1,11},{2,10},{3,9},{4,12},{5,15},{6,14},{7,13},{8,0},{9,3},... | collective-permute-start | bytes 49160 | tf_op jit(solution)/shard_map/ppermute | solution.py:314
  23.1 2.7 %collective-permute-start.8 = (bf16[64,1536]{1,0:T(8,128)(2,1)S(1)}, bf16[64,1536]{1,0:T(8,128)(2,1)S(1)}, u32[]{:S(2)}, u32[]{:S(2)}) collective-permute-start(bf16[64,1536]{1,0:T(8,128)(2,1)S(1)} %get-tuple-element.57), channel_id=1, source_target_pairs={{0,1},{1,0},{2,3},{3,2},{4,5},{5,4},{6,7},{7,6},{8,9},{9,8},{10,11... | collective-permute-start | bytes 589832 | tf_op jit(solution)/shard_map/ppermute | solution.py:302
  23.5 7.4 %collective-permute-start.9 = (bf16[64,1024]{1,0:T(8,128)(2,1)S(1)}, bf16[64,1024]{1,0:T(8,128)(2,1)S(1)}, u32[]{:S(2)}, u32[]{:S(2)}) collective-permute-start(bf16[64,1024]{1,0:T(8,128)(2,1)S(1)} %get-tuple-element.56.refs_1_), channel_id=1, source_target_pairs={{0,15},{1,2},{2,1},{3,4},{4,3},{5,6},{6,5},{7,8},{8,7},{9,10},{10,... | collective-permute-start | bytes 393224 | tf_op jit(solution)/shard_map/ppermute | solution.py:301
  25.9 5.4 %collective-permute-start.10 = (bf16[64,128]{1,0:T(8,128)(2,1)S(1)}, bf16[64,128]{1,0:T(8,128)(2,1)S(1)}, u32[]{:S(2)}, u32[]{:S(2)}) collective-permute-start(bf16[64,128]{1,0:T(8,128)(2,1)S(1)} %get-tuple-element.59.refs_4_), channel_id=1, source_target_pairs={{0,9},{1,10},{2,11},{3,8},{4,13},{5,14},{6,15},{7,12},{8,1},{9,2},... | collective-permute-start | bytes 49160 | tf_op jit(solution)/shard_map/ppermute | solution.py:314
  26.5 4.9 %collective-permute-start.11 = (bf16[64,128]{1,0:T(8,128)(2,1)S(1)}, bf16[64,128]{1,0:T(8,128)(2,1)S(1)}, u32[]{:S(2)}, u32[]{:S(2)}) collective-permute-start(bf16[64,128]{1,0:T(8,128)(2,1)S(1)} %get-tuple-element.60.refs_5_), channel_id=1, source_target_pairs={{0,8},{1,11},{2,10},{3,9},{4,12},{5,15},{6,14},{7,13},{8,0},{9,3},... | collective-permute-start | bytes 49160 | tf_op jit(solution)/shard_map/ppermute | solution.py:314
  32.0 3.2 %collective-permute-start.12 = (bf16[64,1536]{1,0:T(8,128)(2,1)S(1)}, bf16[64,1536]{1,0:T(8,128)(2,1)S(1)}, u32[]{:S(2)}, u32[]{:S(2)}) collective-permute-start(bf16[64,1536]{1,0:T(8,128)(2,1)S(1)} %get-tuple-element.64), channel_id=1, source_target_pairs={{0,1},{1,0},{2,3},{3,2},{4,5},{5,4},{6,7},{7,6},{8,9},{9,8},{10,11... | collective-permute-start | bytes 589832 | tf_op jit(solution)/shard_map/ppermute | solution.py:302
  32.7 7.4 %collective-permute-start.13 = (bf16[64,1024]{1,0:T(8,128)(2,1)S(1)}, bf16[64,1024]{1,0:T(8,128)(2,1)S(1)}, u32[]{:S(2)}, u32[]{:S(2)}) collective-permute-start(bf16[64,1024]{1,0:T(8,128)(2,1)S(1)} %get-tuple-element.63.refs_1_), channel_id=1, source_target_pairs={{0,15},{1,2},{2,1},{3,4},{4,3},{5,6},{6,5},{7,8},{8,7},{9,10},{10,... | collective-permute-start | bytes 393224 | tf_op jit(solution)/shard_map/ppermute | solution.py:301
  35.2 5.4 %collective-permute-start.14 = (bf16[64,128]{1,0:T(8,128)(2,1)S(1)}, bf16[64,128]{1,0:T(8,128)(2,1)S(1)}, u32[]{:S(2)}, u32[]{:S(2)}) collective-permute-start(bf16[64,128]{1,0:T(8,128)(2,1)S(1)} %get-tuple-element.66.refs_4_), channel_id=1, source_target_pairs={{0,9},{1,10},{2,11},{3,8},{4,13},{5,14},{6,15},{7,12},{8,1},{9,2},... | collective-permute-start | bytes 49160 | tf_op jit(solution)/shard_map/ppermute | solution.py:314
  35.3 5.3 %collective-permute-start.15 = (bf16[64,128]{1,0:T(8,128)(2,1)S(1)}, bf16[64,128]{1,0:T(8,128)(2,1)S(1)}, u32[]{:S(2)}, u32[]{:S(2)}) collective-permute-start(bf16[64,128]{1,0:T(8,128)(2,1)S(1)} %get-tuple-element.67.refs_5_), channel_id=1, source_target_pairs={{0,8},{1,11},{2,10},{3,9},{4,12},{5,15},{6,14},{7,13},{8,0},{9,3},... | collective-permute-start | bytes 49160 | tf_op jit(solution)/shard_map/ppermute | solution.py:314

commit v16 on v14

--- a/solution.py
+++ b/solution.py
@@ -54,10 +54,10 @@
         places = [(l, m) for l in range(loop_size) for m in range(members)]
         self.across = [
             [
-                (l * members + m, (l + self.hops[0]) % loop_size * members + (m ^ (m % 2 * 2) ^ other))
+                (l * members + m, (l + self.hops[0]) % loop_size * members + (m ^ other))
                 for l, m in places
             ]
-            for other in range(2)
+            for other in (0, 2)
         ]
         self.routes = [
             [(l * members + m, (l + hop) % loop_size * members + (m + step) % members) for l, m in places]
@@ -82,11 +82,12 @@
             return
         message_ref, keep_ref = out_refs
         (total,) = totals
-        member = self.member(index_ref)
-        second = lax.rem(member, 2) != lax.div(member, 2)
-        first, last = total[:, : 2 * self.width], total[:, 2 * self.width :]
-        keep_ref[...] = jnp.where(second, last, first)
-        upper, lower = halves(jnp.where(second, first, last))
+        pieces = [total[:, i * self.width : (i + 1) * self.width] for i in range(self.members)]
+        even = jnp.concatenate(pieces[0::2], axis=1)
+        odd = jnp.concatenate(pieces[1::2], axis=1)
+        second = lax.rem(index_ref[0], 2) == 1
+        keep_ref[...] = jnp.where(second, odd, even)
+        upper, lower = halves(jnp.where(second, even, odd))
         message_ref[:, : self.shard_len] = x
         message_ref[:, self.shard_len : self.shard_len + 2 * self.width] = upper
         message_ref[:, self.shard_len + 2 * self.width :] = lower
@@ -95,7 +96,7 @@
         upper = message_ref[:, self.shard_len : self.shard_len + 2 * self.width].astype(F32)
         lower = message_ref[:, self.shard_len + 2 * self.width :].astype(F32)
         total = (keep_ref[...] + (upper + lower)).astype(BF16)
-        second = lax.rem(index_ref[0], 2) == 1
+        second = self.member(index_ref) >= 2
         first, last = total[:, : self.width], total[:, self.width :]
         out_refs[0][...] = jnp.where(second, last, first)
         out_refs[1][...] = jnp.where(second, first, last)

time: 43.1 us -> 43.8 us (1.016)
  starting transfers between devices: 19.6 us -> 21.3 us
  waiting for transfers between devices: 10.9 us -> 9.9 us
    ppermute x8, starting transfers between devices: 4.21 us -> 8.72 us  [on_device(): fars = [lax.ppermute(s, axes, route) for s, route in zip(sends, routes)]]
    ppermute x4, starting transfers between devices: 14.7 us -> 11.9 us  [on_device(): over = lax.ppermute(block if product == 0 else current, axes, plan.over)]
    ppermute x4, waiting for transfers between devices: 5.92 us -> 4.25 us  [on_device(): over = lax.ppermute(block if product == 0 else current, axes, plan.over)]
    ppermute x8, waiting for transfers between devices: 4.97 us -> 5.64 us  [on_device(): fars = [lax.ppermute(s, axes, route) for s, route in zip(sends, routes)]]
  transfers between devices with their start and end apart: 16 -> 16, of which waited for: 10 -> 9; matrix products, arithmetic and copies ran while one was open for 0% -> 0% of each run, Pallas kernels for 18% -> 18%
where the time goes in v16:
time: 43.8 us; the launch traced here: 43.7 us
  starting transfers between devices  21.3 us (49%)
  Pallas kernels  12.3 us (28%)
  waiting for transfers between devices  9.9 us (23%)
    pallas_call x17, Pallas kernels, call(): pl.pallas_call(kernel, in_specs=list(specs), out_specs=out_specs or [IN_V...  12.3 us
    ppermute x4, starting transfers between devices, on_device(): over = lax.ppermute(block if product == 0 else current, axes, plan.over)  11.9 us
    ppermute x8, starting transfers between devices, on_device(): fars = [lax.ppermute(s, axes, route) for s, route in zip(sends, routes)]  8.72 us
    ppermute x8, waiting for transfers between devices, on_device(): fars = [lax.ppermute(s, axes, route) for s, route in zip(sends, routes)]  5.64 us
    ppermute x4, waiting for transfers between devices, on_device(): over = lax.ppermute(block if product == 0 else current, axes, plan.over)  4.25 us
  transfers between devices with their start and end apart: 16, of which 9 were waited for; matrix products, arithmetic and copies ran while one was open for 0% of the time, Pallas kernels for 18%

profile of v16, /device:TPU:0, one launch (start us, length us, event | category | flops | bytes accessed | tf_op | source)
XLA Modules:
  0.0 43.7 jit_solution(15021140277555464063)
XLA Ops:
  0.0 0.0 copy-start.1
  0.0 0.0 copy-start
  0.0 1.8 %prepare.1 = (bf16[64,1024]{1,0:T(8,128)(2,1)S(1)}, bf16[1,512,256]{2,1,0:T(8,128)(2,1)S(1)}, bf16[128,1024]{1,0:T(8,128)(2,1)S(1)}, s32[32]{0:T(128)S(4)}, s32[...) custom-call(s32[1]{0:T(128)} %bitcast.index_ref.refs_0_, s32[32]{0:T(128)} %refs_0_.1, s32[32]{0:T(128)} %refs_1_.1, ...), custom_call_target="tpu_custom_call" | custom-call | flops 1000000000 | bytes 4194304 | tf_op jit(solution)/shard_map/prepare/pallas_call | solution.py:241
  1.8 0.5 %collective-permute-start = (bf16[64,1536]{1,0:T(8,128)(2,1)S(1)}, bf16[64,1536]{1,0:T(8,128)(2,1)S(1)}, u32[]{:S(2)}, u32[]{:S(2)}) collective-permute-start(bf16[64,1536]{1,0:T(8,128)(2,1)S(1)} %get-tuple-element.41), channel_id=1, source_target_pairs={{0,1},{1,0},{2,3},{3,2},{4,5},{5,4},{6,7},{7,6},{8,9},{9,8},{10,11... | collective-permute-start | bytes 589832 | tf_op jit(solution)/shard_map/ppermute | solution.py:303
  2.4 5.6 %collective-permute-start.1 = (bf16[64,1024]{1,0:T(8,128)(2,1)}, bf16[64,1024]{1,0:T(8,128)(2,1)S(1)}, u32[]{:S(2)}, u32[]{:S(2)}) collective-permute-start(bf16[64,1024]{1,0:T(8,128)(2,1)} %refs_4_.1), channel_id=1, source_target_pairs={{0,15},{1,2},{2,1},{3,4},{4,3},{5,6},{6,5},{7,8},{8,7},{9,10},{10,... | collective-permute-start | bytes 393224 | tf_op jit(solution)/shard_map/ppermute | solution.py:302
  8.0 0.0 collective-permute-done.message_ref.refs_4_
  8.0 0.1 collective-permute-start.2
  8.1 0.6 %collective-permute-start.3 = (bf16[64,128]{1,0:T(8,128)(2,1)S(1)}, bf16[64,128]{1,0:T(8,128)(2,1)S(1)}, u32[]{:S(2)}, u32[]{:S(2)}) collective-permute-start(bf16[64,128]{1,0:T(8,128)(2,1)S(1)} %get-tuple-element.44.refs_8_), channel_id=1, source_target_pairs={{0,10},{1,11},{2,8},{3,9},{4,14},{5,15},{6,12},{7,13},{8,2},{9,3},... | collective-permute-start | bytes 49160 | tf_op jit(solution)/shard_map/ppermute | solution.py:315
  8.7 0.0 copy-done.1
  8.7 0.0 copy-done
  8.7 1.9 %first_own.1 = (f32[64,1024]{1,0:T(8,128)S(1)}, bf16[36,256,256]{2,1,0:T(8,128)(2,1)S(1)}, bf16[256,1024]{1,0:T(8,128)(2,1)S(1)}) custom-call(s32[1]{0:T(128)} %bitcast.index_ref.refs_0_, s32[32]{0:T(128)S(4)} %get-tuple-element.38.refs_1_, s32[32]{0:T(128)S(4)} %get-tuple-element.39.refs_2_, bf16[64,1024]{1,0:T(8,128)(2,1)S(1)} %get-tuple-element.40.refs_3_, ...), custom_call_target="tpu_custom_call" | custom-call | flops 1000000000 | bytes 4194304 | tf_op jit(solution)/shard_map/first_own/pallas_call | solution.py:241
  10.6 0.3 collective-permute-done.1.over_ref
  11.0 0.5 %halo.4.refs_1_ = f32[64,1024]{1,0:T(8,128)S(1)} custom-call(s32[1]{0:T(128)} %bitcast.index_ref.refs_0_, f32[64,1024]{1,0:T(8,128)S(1)} %get-tuple-element.45.acc_ref, bf16[64,1024]{1,0:T(8,128)(2,1)S(1)} %collective-permute-done.1.over_ref, bf16[36,256,256]{2,1,0:T(8,128)(2,1)S(1)} %get-tuple-element.46.d_ref.refs_3_), custom_call_target="tpu_custom_call" | custom-call | flops 1000000000 | bytes 4194304 | tf_op jit(solution)/shard_map/halo/pallas_call | solution.py:241
  11.5 1.2 %collective-permute-done.2.refs_5_ = bf16[64,128]{1,0:T(8,128)(2,1)S(1)} collective-permute-done((bf16[64,128]{1,0:T(8,128)(2,1)S(1)}, bf16[64,128]{1,0:T(8,128)(2,1)S(1)}, u32[]{:S(2)}, u32[]{:S(2)}) %collective-permute-start.2) | collective-permute-done | bytes 16416 | tf_op jit(solution)/shard_map/ppermute | solution.py:315
  12.7 1.0 %collective-permute-done.3.refs_6_ = bf16[64,128]{1,0:T(8,128)(2,1)S(1)} collective-permute-done((bf16[64,128]{1,0:T(8,128)(2,1)S(1)}, bf16[64,128]{1,0:T(8,128)(2,1)S(1)}, u32[]{:S(2)}, u32[]{:S(2)}) %collective-permute-start.3) | collective-permute-done | bytes 16416 | tf_op jit(solution)/shard_map/ppermute | solution.py:315
  13.7 0.6 %finish.3 = (bf16[64,1024]{1,0:T(8,128)(2,1)S(1)}, bf16[64,1536]{1,0:T(8,128)(2,1)S(1)}, f32[64,256]{1,0:T(8,128)S(1)}) custom-call(s32[1]{0:T(128)} %bitcast.index_ref.refs_0_, f32[64,1024]{1,0:T(8,128)S(1)} %halo.4.refs_1_, bf16[256,1024]{1,0:T(8,128)(2,1)S(1)} %get-tuple-element.47.refs_2_.refs_1_, bf16[128,1024]{1,0:T(8,128)(2,1)S(1)} %get-tuple-element.48.refs_3_, ...), custom_call_target="tpu_custom_call" | custom-call | flops 1000000000 | bytes 4194304 | tf_op jit(solution)/shard_map/finish/pallas_call | solution.py:241
  14.3 0.1 collective-permute-start.4
  14.4 2.8 %collective-permute-start.5 = (bf16[64,1024]{1,0:T(8,128)(2,1)S(1)}, bf16[64,1024]{1,0:T(8,128)(2,1)S(1)}, u32[]{:S(2)}, u32[]{:S(2)}) collective-permute-start(bf16[64,1024]{1,0:T(8,128)(2,1)S(1)} %get-tuple-element.50.refs_1_), channel_id=1, source_target_pairs={{0,15},{1,2},{2,1},{3,4},{4,3},{5,6},{6,5},{7,8},{8,7},{9,10},{10,... | collective-permute-start | bytes 393224 | tf_op jit(solution)/shard_map/ppermute | solution.py:302
  17.2 0.0 collective-permute-done.4.message_ref.refs_2_
  17.2 1.5 %collective-permute-start.6 = (bf16[64,128]{1,0:T(8,128)(2,1)S(1)}, bf16[64,128]{1,0:T(8,128)(2,1)S(1)}, u32[]{:S(2)}, u32[]{:S(2)}) collective-permute-start(bf16[64,128]{1,0:T(8,128)(2,1)S(1)} %get-tuple-element.53.refs_4_), channel_id=1, source_target_pairs={{0,8},{1,9},{2,10},{3,11},{4,12},{5,13},{6,14},{7,15},{8,0},{9,1},... | collective-permute-start | bytes 49160 | tf_op jit(solution)/shard_map/ppermute | solution.py:315
  18.7 0.7 %collective-permute-start.7 = (bf16[64,128]{1,0:T(8,128)(2,1)S(1)}, bf16[64,128]{1,0:T(8,128)(2,1)S(1)}, u32[]{:S(2)}, u32[]{:S(2)}) collective-permute-start(bf16[64,128]{1,0:T(8,128)(2,1)S(1)} %get-tuple-element.54.refs_5_), channel_id=1, source_target_pairs={{0,10},{1,11},{2,8},{3,9},{4,14},{5,15},{6,12},{7,13},{8,2},{9,3},... | collective-permute-start | bytes 49160 | tf_op jit(solution)/shard_map/ppermute | solution.py:315
  19.5 1.3 %own.3 = (f32[64,1024]{1,0:T(8,128)S(1)}, bf16[4,64,1024]{2,1,0:T(8,128)(2,1)}) custom-call(s32[1]{0:T(128)} %bitcast.index_ref.refs_0_, bf16[64,1024]{1,0:T(8,128)(2,1)S(1)} %get-tuple-element.50.refs_1_, bf16[64,1536]{1,0:T(8,128)(2,1)S(1)} %collective-permute-done.4.message_ref.refs_2_, bf16[36,256,256]{2,1,0:T(8,128)(2,1)S(1)} %get-tuple-element.46.d_ref.refs_3_, ...), custom_call_target="tpu_custom_call" | custom-call | flops 1000000000 | bytes 4194304 | tf_op jit(solution)/shard_map/own/pallas_call | solution.py:241
  20.8 0.9 %collective-permute-done.5.over_ref = bf16[64,1024]{1,0:T(8,128)(2,1)S(1)} collective-permute-done((bf16[64,1024]{1,0:T(8,128)(2,1)S(1)}, bf16[64,1024]{1,0:T(8,128)(2,1)S(1)}, u32[]{:S(2)}, u32[]{:S(2)}) %collective-permute-start.5) | collective-permute-done | bytes 131104 | tf_op jit(solution)/shard_map/ppermute | solution.py:302
  21.6 0.5 %halo.5.refs_1_ = f32[64,1024]{1,0:T(8,128)S(1)} custom-call(s32[1]{0:T(128)} %bitcast.index_ref.refs_0_, f32[64,1024]{1,0:T(8,128)S(1)} %get-tuple-element.55.acc_ref, bf16[64,1024]{1,0:T(8,128)(2,1)S(1)} %collective-permute-done.5.over_ref, bf16[36,256,256]{2,1,0:T(8,128)(2,1)S(1)} %get-tuple-element.46.d_ref.refs_3_), custom_call_target="tpu_custom_call" | custom-call | flops 1000000000 | bytes 4194304 | tf_op jit(solution)/shard_map/halo/pallas_call | solution.py:241
  22.1 0.0 collective-permute-done.6.refs_5_
  22.2 2.1 %collective-permute-done.7.refs_6_ = bf16[64,128]{1,0:T(8,128)(2,1)S(1)} collective-permute-done((bf16[64,128]{1,0:T(8,128)(2,1)S(1)}, bf16[64,128]{1,0:T(8,128)(2,1)S(1)}, u32[]{:S(2)}, u32[]{:S(2)}) %collective-permute-start.7) | collective-permute-done | bytes 16416 | tf_op jit(solution)/shard_map/ppermute | solution.py:315
  24.3 0.6 %finish.4 = (bf16[64,1024]{1,0:T(8,128)(2,1)S(1)}, bf16[64,1536]{1,0:T(8,128)(2,1)S(1)}, f32[64,256]{1,0:T(8,128)S(1)}) custom-call(s32[1]{0:T(128)} %bitcast.index_ref.refs_0_, f32[64,1024]{1,0:T(8,128)S(1)} %halo.5.refs_1_, bf16[256,1024]{1,0:T(8,128)(2,1)S(1)} %get-tuple-element.47.refs_2_.refs_1_, bf16[128,1024]{1,0:T(8,128)(2,1)S(1)} %get-tuple-element.48.refs_3_, ...), custom_call_target="tpu_custom_call" | custom-call | flops 1000000000 | bytes 4194304 | tf_op jit(solution)/shard_map/finish/pallas_call | solution.py:241
  24.9 0.1 collective-permute-start.8
  24.9 1.6 %collective-permute-start.9 = (bf16[64,1024]{1,0:T(8,128)(2,1)S(1)}, bf16[64,1024]{1,0:T(8,128)(2,1)S(1)}, u32[]{:S(2)}, u32[]{:S(2)}) collective-permute-start(bf16[64,1024]{1,0:T(8,128)(2,1)S(1)} %get-tuple-element.56.refs_1_), channel_id=1, source_target_pairs={{0,15},{1,2},{2,1},{3,4},{4,3},{5,6},{6,5},{7,8},{8,7},{9,10},{10,... | collective-permute-start | bytes 393224 | tf_op jit(solution)/shard_map/ppermute | solution.py:302
  26.5 0.0 collective-permute-done.8.message_ref.refs_2_
  26.6 1.3 %collective-permute-start.10 = (bf16[64,128]{1,0:T(8,128)(2,1)S(1)}, bf16[64,128]{1,0:T(8,128)(2,1)S(1)}, u32[]{:S(2)}, u32[]{:S(2)}) collective-permute-start(bf16[64,128]{1,0:T(8,128)(2,1)S(1)} %get-tuple-element.59.refs_4_), channel_id=1, source_target_pairs={{0,8},{1,9},{2,10},{3,11},{4,12},{5,13},{6,14},{7,15},{8,0},{9,1},... | collective-permute-start | bytes 49160 | tf_op jit(solution)/shard_map/ppermute | solution.py:315
  27.9 1.6 %collective-permute-start.11 = (bf16[64,128]{1,0:T(8,128)(2,1)S(1)}, bf16[64,128]{1,0:T(8,128)(2,1)S(1)}, u32[]{:S(2)}, u32[]{:S(2)}) collective-permute-start(bf16[64,128]{1,0:T(8,128)(2,1)S(1)} %get-tuple-element.60.refs_5_), channel_id=1, source_target_pairs={{0,10},{1,11},{2,8},{3,9},{4,14},{5,15},{6,12},{7,13},{8,2},{9,3},... | collective-permute-start | bytes 49160 | tf_op jit(solution)/shard_map/ppermute | solution.py:315
  29.5 1.3 %own.4 = (f32[64,1024]{1,0:T(8,128)S(1)}, bf16[4,64,1024]{2,1,0:T(8,128)(2,1)}) custom-call(s32[1]{0:T(128)} %bitcast.index_ref.refs_0_, bf16[64,1024]{1,0:T(8,128)(2,1)S(1)} %get-tuple-element.56.refs_1_, bf16[64,1536]{1,0:T(8,128)(2,1)S(1)} %collective-permute-done.8.message_ref.refs_2_, ...), custom_call_target="tpu_custom_call", output_to_operand_aliasing={{1}: (6, {})} | custom-call | flops 1000000000 | bytes 4194304 | tf_op jit(solution)/shard_map/own/pallas_call | solution.py:241
  30.8 1.6 %collective-permute-done.9.over_ref = bf16[64,1024]{1,0:T(8,128)(2,1)S(1)} collective-permute-done((bf16[64,1024]{1,0:T(8,128)(2,1)S(1)}, bf16[64,1024]{1,0:T(8,128)(2,1)S(1)}, u32[]{:S(2)}, u32[]{:S(2)}) %collective-permute-start.9) | collective-permute-done | bytes 131104 | tf_op jit(solution)/shard_map/ppermute | solution.py:302
  32.4 0.5 %halo.6.refs_1_ = f32[64,1024]{1,0:T(8,128)S(1)} custom-call(s32[1]{0:T(128)} %bitcast.index_ref.refs_0_, f32[64,1024]{1,0:T(8,128)S(1)} %get-tuple-element.62.acc_ref, bf16[64,1024]{1,0:T(8,128)(2,1)S(1)} %collective-permute-done.9.over_ref, bf16[36,256,256]{2,1,0:T(8,128)(2,1)S(1)} %get-tuple-element.46.d_ref.refs_3_), custom_call_target="tpu_custom_call" | custom-call | flops 1000000000 | bytes 4194304 | tf_op jit(solution)/shard_map/halo/pallas_call | solution.py:241
  32.9 0.0 collective-permute-done.10.refs_5_
  32.9 0.5 %collective-permute-done.11.refs_6_ = bf16[64,128]{1,0:T(8,128)(2,1)S(1)} collective-permute-done((bf16[64,128]{1,0:T(8,128)(2,1)S(1)}, bf16[64,128]{1,0:T(8,128)(2,1)S(1)}, u32[]{:S(2)}, u32[]{:S(2)}) %collective-permute-start.11) | collective-permute-done | bytes 16416 | tf_op jit(solution)/shard_map/ppermute | solution.py:315
  33.4 0.6 %finish.5 = (bf16[64,1024]{1,0:T(8,128)(2,1)S(1)}, bf16[64,1536]{1,0:T(8,128)(2,1)S(1)}, f32[64,256]{1,0:T(8,128)S(1)}) custom-call(s32[1]{0:T(128)} %bitcast.index_ref.refs_0_, f32[64,1024]{1,0:T(8,128)S(1)} %halo.6.refs_1_, bf16[256,1024]{1,0:T(8,128)(2,1)S(1)} %get-tuple-element.47.refs_2_.refs_1_, bf16[128,1024]{1,0:T(8,128)(2,1)S(1)} %get-tuple-element.48.refs_3_, ...), custom_call_target="tpu_custom_call" | custom-call | flops 1000000000 | bytes 4194304 | tf_op jit(solution)/shard_map/finish/pallas_call | solution.py:241
  34.0 0.1 collective-permute-start.12
  34.1 1.8 %collective-permute-start.13 = (bf16[64,1024]{1,0:T(8,128)(2,1)S(1)}, bf16[64,1024]{1,0:T(8,128)(2,1)S(1)}, u32[]{:S(2)}, u32[]{:S(2)}) collective-permute-start(bf16[64,1024]{1,0:T(8,128)(2,1)S(1)} %get-tuple-element.63.refs_1_), channel_id=1, source_target_pairs={{0,15},{1,2},{2,1},{3,4},{4,3},{5,6},{6,5},{7,8},{8,7},{9,10},{10,... | collective-permute-start | bytes 393224 | tf_op jit(solution)/shard_map/ppermute | solution.py:302
  36.0 0.0 collective-permute-done.12.message_ref.refs_2_
  36.0 1.3 %collective-permute-start.14 = (bf16[64,128]{1,0:T(8,128)(2,1)S(1)}, bf16[64,128]{1,0:T(8,128)(2,1)S(1)}, u32[]{:S(2)}, u32[]{:S(2)}) collective-permute-start(bf16[64,128]{1,0:T(8,128)(2,1)S(1)} %get-tuple-element.66.refs_4_), channel_id=1, source_target_pairs={{0,8},{1,9},{2,10},{3,11},{4,12},{5,13},{6,14},{7,15},{8,0},{9,1},... | collective-permute-start | bytes 49160 | tf_op jit(solution)/shard_map/ppermute | solution.py:315
  37.3 1.5 %collective-permute-start.15 = (bf16[64,128]{1,0:T(8,128)(2,1)S(1)}, bf16[64,128]{1,0:T(8,128)(2,1)S(1)}, u32[]{:S(2)}, u32[]{:S(2)}) collective-permute-start(bf16[64,128]{1,0:T(8,128)(2,1)S(1)} %get-tuple-element.67.refs_5_), channel_id=1, source_target_pairs={{0,10},{1,11},{2,8},{3,9},{4,14},{5,15},{6,12},{7,13},{8,2},{9,3},... | collective-permute-start | bytes 49160 | tf_op jit(solution)/shard_map/ppermute | solution.py:315
  38.8 1.3 %own.5 = (f32[64,1024]{1,0:T(8,128)S(1)}, bf16[4,64,1024]{2,1,0:T(8,128)(2,1)}) custom-call(s32[1]{0:T(128)} %bitcast.index_ref.refs_0_, bf16[64,1024]{1,0:T(8,128)(2,1)S(1)} %get-tuple-element.63.refs_1_, bf16[64,1536]{1,0:T(8,128)(2,1)S(1)} %collective-permute-done.12.message_ref.refs_2_, ...), custom_call_target="tpu_custom_call", output_to_operand_aliasing={{1}: (6, {})} | custom-call | flops 1000000000 | bytes 4194304 | tf_op jit(solution)/shard_map/own/pallas_call | solution.py:241
  40.1 1.5 %collective-permute-done.13.over_ref = bf16[64,1024]{1,0:T(8,128)(2,1)S(1)} collective-permute-done((bf16[64,1024]{1,0:T(8,128)(2,1)S(1)}, bf16[64,1024]{1,0:T(8,128)(2,1)S(1)}, u32[]{:S(2)}, u32[]{:S(2)}) %collective-permute-start.13) | collective-permute-done | bytes 131104 | tf_op jit(solution)/shard_map/ppermute | solution.py:302
  41.5 0.5 %halo.7.refs_0_ = f32[64,1024]{1,0:T(8,128)S(1)} custom-call(s32[1]{0:T(128)} %bitcast.index_ref.refs_0_, f32[64,1024]{1,0:T(8,128)S(1)} %get-tuple-element.69.acc_ref, bf16[64,1024]{1,0:T(8,128)(2,1)S(1)} %collective-permute-done.13.over_ref, bf16[36,256,256]{2,1,0:T(8,128)(2,1)S(1)} %get-tuple-element.46.d_ref.refs_3_), custom_call_target="tpu_custom_call" | custom-call | flops 1000000000 | bytes 4194304 | tf_op jit(solution)/shard_map/halo/pallas_call | solution.py:241
  42.1 0.0 collective-permute-done.14.refs_2_
  42.1 0.7 %collective-permute-done.15.refs_3_ = bf16[64,128]{1,0:T(8,128)(2,1)S(1)} collective-permute-done((bf16[64,128]{1,0:T(8,128)(2,1)S(1)}, bf16[64,128]{1,0:T(8,128)(2,1)S(1)}, u32[]{:S(2)}, u32[]{:S(2)}) %collective-permute-start.15) | collective-permute-done | bytes 16416 | tf_op jit(solution)/shard_map/ppermute | solution.py:315
  42.8 0.9 %last.1 = bf16[4,64,1024]{2,1,0:T(8,128)(2,1)} custom-call(f32[64,1024]{1,0:T(8,128)S(1)} %halo.7.refs_0_, bf16[256,1024]{1,0:T(8,128)(2,1)S(1)} %get-tuple-element.47.refs_2_.refs_1_, bf16[64,128]{1,0:T(8,128)(2,1)S(1)} %collective-permute-done.14.refs_2_, bf16[64,128]{1,0:T(8,128)(2,1)S(1)} %collective-permute-done.15.refs_3_, ...), custom_call_target="tpu_custom_call", output_to_operand_aliasing={{}: (4, {})} | custom-call | flops 1000000000 | bytes 4194304 | tf_op jit(solution)/shard_map/last/pallas_call | solution.py:241
  (4 shorter events, 0.1 us)
Async XLA Ops:
  0.0 8.7 %copy-start.1 = (bf16[4,32,256]{2,1,0:T(8,128)(2,1)S(1)}, bf16[4,32,256]{2,1,0:T(8,128)(2,1)}, u32[]{:S(2)}) copy-start(bf16[4,32,256]{2,1,0:T(8,128)(2,1)} %refs_5_.3) | copy-start | bytes 196612
  0.0 8.7 %copy-start = (bf16[32,256,256]{2,1,0:T(8,128)(2,1)S(1)}, bf16[32,256,256]{2,1,0:T(8,128)(2,1)}, u32[]{:S(2)}) copy-start(bf16[32,256,256]{2,1,0:T(8,128)(2,1)} %refs_6_.3) | copy-start | bytes 12582916
  1.8 6.2 %collective-permute-start = (bf16[64,1536]{1,0:T(8,128)(2,1)S(1)}, bf16[64,1536]{1,0:T(8,128)(2,1)S(1)}, u32[]{:S(2)}, u32[]{:S(2)}) collective-permute-start(bf16[64,1536]{1,0:T(8,128)(2,1)S(1)} %get-tuple-element.41), channel_id=1, source_target_pairs={{0,1},{1,0},{2,3},{3,2},{4,5},{5,4},{6,7},{7,6},{8,9},{9,8},{10,11... | collective-permute-start | bytes 589832 | tf_op jit(solution)/shard_map/ppermute | solution.py:303
  2.4 8.6 %collective-permute-start.1 = (bf16[64,1024]{1,0:T(8,128)(2,1)}, bf16[64,1024]{1,0:T(8,128)(2,1)S(1)}, u32[]{:S(2)}, u32[]{:S(2)}) collective-permute-start(bf16[64,1024]{1,0:T(8,128)(2,1)} %refs_4_.1), channel_id=1, source_target_pairs={{0,15},{1,2},{2,1},{3,4},{4,3},{5,6},{6,5},{7,8},{8,7},{9,10},{10,... | collective-permute-start | bytes 393224 | tf_op jit(solution)/shard_map/ppermute | solution.py:302
  8.0 4.7 %collective-permute-start.2 = (bf16[64,128]{1,0:T(8,128)(2,1)S(1)}, bf16[64,128]{1,0:T(8,128)(2,1)S(1)}, u32[]{:S(2)}, u32[]{:S(2)}) collective-permute-start(bf16[64,128]{1,0:T(8,128)(2,1)S(1)} %get-tuple-element.43.refs_7_), channel_id=1, source_target_pairs={{0,8},{1,9},{2,10},{3,11},{4,12},{5,13},{6,14},{7,15},{8,0},{9,1},... | collective-permute-start | bytes 49160 | tf_op jit(solution)/shard_map/ppermute | solution.py:315
  8.1 5.6 %collective-permute-start.3 = (bf16[64,128]{1,0:T(8,128)(2,1)S(1)}, bf16[64,128]{1,0:T(8,128)(2,1)S(1)}, u32[]{:S(2)}, u32[]{:S(2)}) collective-permute-start(bf16[64,128]{1,0:T(8,128)(2,1)S(1)} %get-tuple-element.44.refs_8_), channel_id=1, source_target_pairs={{0,10},{1,11},{2,8},{3,9},{4,14},{5,15},{6,12},{7,13},{8,2},{9,3},... | collective-permute-start | bytes 49160 | tf_op jit(solution)/shard_map/ppermute | solution.py:315
  14.3 2.9 %collective-permute-start.4 = (bf16[64,1536]{1,0:T(8,128)(2,1)S(1)}, bf16[64,1536]{1,0:T(8,128)(2,1)S(1)}, u32[]{:S(2)}, u32[]{:S(2)}) collective-permute-start(bf16[64,1536]{1,0:T(8,128)(2,1)S(1)} %get-tuple-element.51), channel_id=1, source_target_pairs={{0,1},{1,0},{2,3},{3,2},{4,5},{5,4},{6,7},{7,6},{8,9},{9,8},{10,11... | collective-permute-start | bytes 589832 | tf_op jit(solution)/shard_map/ppermute | solution.py:303
  14.4 7.3 %collective-permute-start.5 = (bf16[64,1024]{1,0:T(8,128)(2,1)S(1)}, bf16[64,1024]{1,0:T(8,128)(2,1)S(1)}, u32[]{:S(2)}, u32[]{:S(2)}) collective-permute-start(bf16[64,1024]{1,0:T(8,128)(2,1)S(1)} %get-tuple-element.50.refs_1_), channel_id=1, source_target_pairs={{0,15},{1,2},{2,1},{3,4},{4,3},{5,6},{6,5},{7,8},{8,7},{9,10},{10,... | collective-permute-start | bytes 393224 | tf_op jit(solution)/shard_map/ppermute | solution.py:302
  17.2 5.0 %collective-permute-start.6 = (bf16[64,128]{1,0:T(8,128)(2,1)S(1)}, bf16[64,128]{1,0:T(8,128)(2,1)S(1)}, u32[]{:S(2)}, u32[]{:S(2)}) collective-permute-start(bf16[64,128]{1,0:T(8,128)(2,1)S(1)} %get-tuple-element.53.refs_4_), channel_id=1, source_target_pairs={{0,8},{1,9},{2,10},{3,11},{4,12},{5,13},{6,14},{7,15},{8,0},{9,1},... | collective-permute-start | bytes 49160 | tf_op jit(solution)/shard_map/ppermute | solution.py:315
  18.7 5.5 %collective-permute-start.7 = (bf16[64,128]{1,0:T(8,128)(2,1)S(1)}, bf16[64,128]{1,0:T(8,128)(2,1)S(1)}, u32[]{:S(2)}, u32[]{:S(2)}) collective-permute-start(bf16[64,128]{1,0:T(8,128)(2,1)S(1)} %get-tuple-element.54.refs_5_), channel_id=1, source_target_pairs={{0,10},{1,11},{2,8},{3,9},{4,14},{5,15},{6,12},{7,13},{8,2},{9,3},... | collective-permute-start | bytes 49160 | tf_op jit(solution)/shard_map/ppermute | solution.py:315
  24.9 1.7 %collective-permute-start.8 = (bf16[64,1536]{1,0:T(8,128)(2,1)S(1)}, bf16[64,1536]{1,0:T(8,128)(2,1)S(1)}, u32[]{:S(2)}, u32[]{:S(2)}) collective-permute-start(bf16[64,1536]{1,0:T(8,128)(2,1)S(1)} %get-tuple-element.57), channel_id=1, source_target_pairs={{0,1},{1,0},{2,3},{3,2},{4,5},{5,4},{6,7},{7,6},{8,9},{9,8},{10,11... | collective-permute-start | bytes 589832 | tf_op jit(solution)/shard_map/ppermute | solution.py:303
  24.9 7.4 %collective-permute-start.9 = (bf16[64,1024]{1,0:T(8,128)(2,1)S(1)}, bf16[64,1024]{1,0:T(8,128)(2,1)S(1)}, u32[]{:S(2)}, u32[]{:S(2)}) collective-permute-start(bf16[64,1024]{1,0:T(8,128)(2,1)S(1)} %get-tuple-element.56.refs_1_), channel_id=1, source_target_pairs={{0,15},{1,2},{2,1},{3,4},{4,3},{5,6},{6,5},{7,8},{8,7},{9,10},{10,... | collective-permute-start | bytes 393224 | tf_op jit(solution)/shard_map/ppermute | solution.py:302
  26.6 6.3 %collective-permute-start.10 = (bf16[64,128]{1,0:T(8,128)(2,1)S(1)}, bf16[64,128]{1,0:T(8,128)(2,1)S(1)}, u32[]{:S(2)}, u32[]{:S(2)}) collective-permute-start(bf16[64,128]{1,0:T(8,128)(2,1)S(1)} %get-tuple-element.59.refs_4_), channel_id=1, source_target_pairs={{0,8},{1,9},{2,10},{3,11},{4,12},{5,13},{6,14},{7,15},{8,0},{9,1},... | collective-permute-start | bytes 49160 | tf_op jit(solution)/shard_map/ppermute | solution.py:315
  27.9 5.5 %collective-permute-start.11 = (bf16[64,128]{1,0:T(8,128)(2,1)S(1)}, bf16[64,128]{1,0:T(8,128)(2,1)S(1)}, u32[]{:S(2)}, u32[]{:S(2)}) collective-permute-start(bf16[64,128]{1,0:T(8,128)(2,1)S(1)} %get-tuple-element.60.refs_5_), channel_id=1, source_target_pairs={{0,10},{1,11},{2,8},{3,9},{4,14},{5,15},{6,12},{7,13},{8,2},{9,3},... | collective-permute-start | bytes 49160 | tf_op jit(solution)/shard_map/ppermute | solution.py:315
  34.0 1.9 %collective-permute-start.12 = (bf16[64,1536]{1,0:T(8,128)(2,1)S(1)}, bf16[64,1536]{1,0:T(8,128)(2,1)S(1)}, u32[]{:S(2)}, u32[]{:S(2)}) collective-permute-start(bf16[64,1536]{1,0:T(8,128)(2,1)S(1)} %get-tuple-element.64), channel_id=1, source_target_pairs={{0,1},{1,0},{2,3},{3,2},{4,5},{5,4},{6,7},{7,6},{8,9},{9,8},{10,11... | collective-permute-start | bytes 589832 | tf_op jit(solution)/shard_map/ppermute | solution.py:303
  34.1 7.4 %collective-permute-start.13 = (bf16[64,1024]{1,0:T(8,128)(2,1)S(1)}, bf16[64,1024]{1,0:T(8,128)(2,1)S(1)}, u32[]{:S(2)}, u32[]{:S(2)}) collective-permute-start(bf16[64,1024]{1,0:T(8,128)(2,1)S(1)} %get-tuple-element.63.refs_1_), channel_id=1, source_target_pairs={{0,15},{1,2},{2,1},{3,4},{4,3},{5,6},{6,5},{7,8},{8,7},{9,10},{10,... | collective-permute-start | bytes 393224 | tf_op jit(solution)/shard_map/ppermute | solution.py:302
  36.0 6.1 %collective-permute-start.14 = (bf16[64,128]{1,0:T(8,128)(2,1)S(1)}, bf16[64,128]{1,0:T(8,128)(2,1)S(1)}, u32[]{:S(2)}, u32[]{:S(2)}) collective-permute-start(bf16[64,128]{1,0:T(8,128)(2,1)S(1)} %get-tuple-element.66.refs_4_), channel_id=1, source_target_pairs={{0,8},{1,9},{2,10},{3,11},{4,12},{5,13},{6,14},{7,15},{8,0},{9,1},... | collective-permute-start | bytes 49160 | tf_op jit(solution)/shard_map/ppermute | solution.py:315
  37.3 5.5 %collective-permute-start.15 = (bf16[64,128]{1,0:T(8,128)(2,1)S(1)}, bf16[64,128]{1,0:T(8,128)(2,1)S(1)}, u32[]{:S(2)}, u32[]{:S(2)}) collective-permute-start(bf16[64,128]{1,0:T(8,128)(2,1)S(1)} %get-tuple-element.67.refs_5_), channel_id=1, source_target_pairs={{0,10},{1,11},{2,8},{3,9},{4,14},{5,15},{6,12},{7,13},{8,2},{9,3},... | collective-permute-start | bytes 49160 | tf_op jit(solution)/shard_map/ppermute | solution.py:315

commit v17 on v14

--- a/solution.py
+++ b/solution.py
@@ -54,16 +54,20 @@
         places = [(l, m) for l in range(loop_size) for m in range(members)]
         self.across = [
             [
-                (l * members + m, (l + self.hops[0]) % loop_size * members + (m ^ (m % 2 * 2) ^ other))
+                (l * members + m, (l + self.hops[0]) % loop_size * members + self.far_target(m, other))
                 for l, m in places
             ]
-            for other in range(2)
+            for other in (0, 1)
         ]
         self.routes = [
             [(l * members + m, (l + hop) % loop_size * members + (m + step) % members) for l, m in places]
             for hop in self.hops
             for step in range(members)
         ]
+
+    def far_target(self, member, other):
+        pair, core = divmod(member, 2)
+        return 2 * (pair ^ core) + (pair ^ other)
 
     def panel(self, ref, c):
         return ref[:, c * self.size : (c + 1) * self.size]
@@ -95,7 +99,7 @@
         upper = message_ref[:, self.shard_len : self.shard_len + 2 * self.width].astype(F32)
         lower = message_ref[:, self.shard_len + 2 * self.width :].astype(F32)
         total = (keep_ref[...] + (upper + lower)).astype(BF16)
-        second = lax.rem(index_ref[0], 2) == 1
+        second = self.member(index_ref) >= 2
         first, last = total[:, : self.width], total[:, self.width :]
         out_refs[0][...] = jnp.where(second, last, first)
         out_refs[1][...] = jnp.where(second, first, last)

time: 43.1 us -> 42.4 us (0.984)
  waiting for transfers between devices: 10.9 us -> 9.46 us
  starting transfers between devices: 19.6 us -> 20.4 us
    ppermute x8, starting transfers between devices: 4.21 us -> 5.6 us  [on_device(): fars = [lax.ppermute(s, axes, route) for s, route in zip(sends, routes)]]
    ppermute x4, waiting for transfers between devices: 5.92 us -> 4.87 us  [on_device(): over = lax.ppermute(block if product == 0 else current, axes, plan.over)]
    ppermute x4, starting transfers between devices: 14.7 us -> 14 us  [on_device(): over = lax.ppermute(block if product == 0 else current, axes, plan.over)]
  transfers between devices with their start and end apart: 16 -> 16, of which waited for: 10 -> 10; matrix products, arithmetic and copies ran while one was open for 0% -> 0% of each run, Pallas kernels for 18% -> 19%
where the time goes in v17:
time: 42.4 us; the launch traced here: 42.3 us
  starting transfers between devices  20.4 us (48%)
  Pallas kernels  12.3 us (29%)
  waiting for transfers between devices  9.46 us (22%)
    ppermute x4, starting transfers between devices, on_device(): over = lax.ppermute(block if product == 0 else current, axes, plan.over)  14 us
    pallas_call x17, Pallas kernels, call(): pl.pallas_call(kernel, in_specs=list(specs), out_specs=out_specs or [IN_V...  12.3 us
    ppermute x8, starting transfers between devices, on_device(): fars = [lax.ppermute(s, axes, route) for s, route in zip(sends, routes)]  5.6 us
    ppermute x4, waiting for transfers between devices, on_device(): over = lax.ppermute(block if product == 0 else current, axes, plan.over)  4.87 us
    ppermute x8, waiting for transfers between devices, on_device(): fars = [lax.ppermute(s, axes, route) for s, route in zip(sends, routes)]  4.58 us
  transfers between devices with their start and end apart: 16, of which 10 were waited for; matrix products, arithmetic and copies ran while one was open for 0% of the time, Pallas kernels for 19%

profile of v17, /device:TPU:0, one launch (start us, length us, event | category | flops | bytes accessed | tf_op | source)
XLA Modules:
  0.0 42.3 jit_solution(6956227431934432507)
XLA Ops:
  0.0 0.0 copy-start.1
  0.0 0.0 copy-start
  0.0 1.8 %prepare.1 = (bf16[64,1024]{1,0:T(8,128)(2,1)S(1)}, bf16[1,512,256]{2,1,0:T(8,128)(2,1)S(1)}, bf16[128,1024]{1,0:T(8,128)(2,1)S(1)}, s32[32]{0:T(128)S(4)}, s32[...) custom-call(s32[1]{0:T(128)} %bitcast.index_ref.refs_0_, s32[32]{0:T(128)} %refs_0_.1, s32[32]{0:T(128)} %refs_1_.1, ...), custom_call_target="tpu_custom_call" | custom-call | flops 1000000000 | bytes 4194304 | tf_op jit(solution)/shard_map/prepare/pallas_call | solution.py:244
  1.8 0.5 %collective-permute-start = (bf16[64,1536]{1,0:T(8,128)(2,1)S(1)}, bf16[64,1536]{1,0:T(8,128)(2,1)S(1)}, u32[]{:S(2)}, u32[]{:S(2)}) collective-permute-start(bf16[64,1536]{1,0:T(8,128)(2,1)S(1)} %get-tuple-element.41), channel_id=1, source_target_pairs={{0,1},{1,0},{2,3},{3,2},{4,5},{5,4},{6,7},{7,6},{8,9},{9,8},{10,11... | collective-permute-start | bytes 589832 | tf_op jit(solution)/shard_map/ppermute | solution.py:306
  2.4 5.6 %collective-permute-start.1 = (bf16[64,1024]{1,0:T(8,128)(2,1)}, bf16[64,1024]{1,0:T(8,128)(2,1)S(1)}, u32[]{:S(2)}, u32[]{:S(2)}) collective-permute-start(bf16[64,1024]{1,0:T(8,128)(2,1)} %refs_4_.1), channel_id=1, source_target_pairs={{0,15},{1,2},{2,1},{3,4},{4,3},{5,6},{6,5},{7,8},{8,7},{9,10},{10,... | collective-permute-start | bytes 393224 | tf_op jit(solution)/shard_map/ppermute | solution.py:305
  8.0 0.0 collective-permute-done.message_ref.refs_4_
  8.0 0.1 collective-permute-start.2
  8.1 0.4 collective-permute-start.3
  8.5 0.0 copy-done.1
  8.5 0.0 copy-done
  8.5 1.9 %first_own.1 = (f32[64,1024]{1,0:T(8,128)S(1)}, bf16[36,256,256]{2,1,0:T(8,128)(2,1)S(1)}, bf16[256,1024]{1,0:T(8,128)(2,1)S(1)}) custom-call(s32[1]{0:T(128)} %bitcast.index_ref.refs_0_, s32[32]{0:T(128)S(4)} %get-tuple-element.38.refs_1_, s32[32]{0:T(128)S(4)} %get-tuple-element.39.refs_2_, bf16[64,1024]{1,0:T(8,128)(2,1)S(1)} %get-tuple-element.40.refs_3_, ...), custom_call_target="tpu_custom_call" | custom-call | flops 1000000000 | bytes 4194304 | tf_op jit(solution)/shard_map/first_own/pallas_call | solution.py:244
  10.3 0.6 %collective-permute-done.1.over_ref = bf16[64,1024]{1,0:T(8,128)(2,1)S(1)} collective-permute-done((bf16[64,1024]{1,0:T(8,128)(2,1)}, bf16[64,1024]{1,0:T(8,128)(2,1)S(1)}, u32[]{:S(2)}, u32[]{:S(2)}) %collective-permute-start.1) | collective-permute-done | bytes 131104 | tf_op jit(solution)/shard_map/ppermute | solution.py:305
  11.0 0.5 %halo.4.refs_1_ = f32[64,1024]{1,0:T(8,128)S(1)} custom-call(s32[1]{0:T(128)} %bitcast.index_ref.refs_0_, f32[64,1024]{1,0:T(8,128)S(1)} %get-tuple-element.45.acc_ref, bf16[64,1024]{1,0:T(8,128)(2,1)S(1)} %collective-permute-done.1.over_ref, bf16[36,256,256]{2,1,0:T(8,128)(2,1)S(1)} %get-tuple-element.46.d_ref.refs_3_), custom_call_target="tpu_custom_call" | custom-call | flops 1000000000 | bytes 4194304 | tf_op jit(solution)/shard_map/halo/pallas_call | solution.py:244
  11.5 1.2 %collective-permute-done.2.refs_5_ = bf16[64,128]{1,0:T(8,128)(2,1)S(1)} collective-permute-done((bf16[64,128]{1,0:T(8,128)(2,1)S(1)}, bf16[64,128]{1,0:T(8,128)(2,1)S(1)}, u32[]{:S(2)}, u32[]{:S(2)}) %collective-permute-start.2) | collective-permute-done | bytes 16416 | tf_op jit(solution)/shard_map/ppermute | solution.py:318
  12.7 0.4 collective-permute-done.3.refs_6_
  13.1 0.6 %finish.3 = (bf16[64,1024]{1,0:T(8,128)(2,1)S(1)}, bf16[64,1536]{1,0:T(8,128)(2,1)S(1)}, f32[64,256]{1,0:T(8,128)S(1)}) custom-call(s32[1]{0:T(128)} %bitcast.index_ref.refs_0_, f32[64,1024]{1,0:T(8,128)S(1)} %halo.4.refs_1_, bf16[256,1024]{1,0:T(8,128)(2,1)S(1)} %get-tuple-element.47.refs_2_.refs_1_, bf16[128,1024]{1,0:T(8,128)(2,1)S(1)} %get-tuple-element.48.refs_3_, ...), custom_call_target="tpu_custom_call" | custom-call | flops 1000000000 | bytes 4194304 | tf_op jit(solution)/shard_map/finish/pallas_call | solution.py:244
  13.7 0.1 collective-permute-start.4
  13.8 3.5 %collective-permute-start.5 = (bf16[64,1024]{1,0:T(8,128)(2,1)S(1)}, bf16[64,1024]{1,0:T(8,128)(2,1)S(1)}, u32[]{:S(2)}, u32[]{:S(2)}) collective-permute-start(bf16[64,1024]{1,0:T(8,128)(2,1)S(1)} %get-tuple-element.50.refs_1_), channel_id=1, source_target_pairs={{0,15},{1,2},{2,1},{3,4},{4,3},{5,6},{6,5},{7,8},{8,7},{9,10},{10,... | collective-permute-start | bytes 393224 | tf_op jit(solution)/shard_map/ppermute | solution.py:305
  17.3 0.0 collective-permute-done.4.message_ref.refs_2_
  17.3 0.8 %collective-permute-start.6 = (bf16[64,128]{1,0:T(8,128)(2,1)S(1)}, bf16[64,128]{1,0:T(8,128)(2,1)S(1)}, u32[]{:S(2)}, u32[]{:S(2)}) collective-permute-start(bf16[64,128]{1,0:T(8,128)(2,1)S(1)} %get-tuple-element.53.refs_4_), channel_id=1, source_target_pairs={{0,8},{1,10},{2,11},{3,9},{4,12},{5,14},{6,15},{7,13},{8,0},{9,2},... | collective-permute-start | bytes 49160 | tf_op jit(solution)/shard_map/ppermute | solution.py:318
  18.1 0.7 %collective-permute-start.7 = (bf16[64,128]{1,0:T(8,128)(2,1)S(1)}, bf16[64,128]{1,0:T(8,128)(2,1)S(1)}, u32[]{:S(2)}, u32[]{:S(2)}) collective-permute-start(bf16[64,128]{1,0:T(8,128)(2,1)S(1)} %get-tuple-element.54.refs_5_), channel_id=1, source_target_pairs={{0,9},{1,11},{2,10},{3,8},{4,13},{5,15},{6,14},{7,12},{8,1},{9,3},... | collective-permute-start | bytes 49160 | tf_op jit(solution)/shard_map/ppermute | solution.py:318
  18.9 1.3 %own.3 = (f32[64,1024]{1,0:T(8,128)S(1)}, bf16[4,64,1024]{2,1,0:T(8,128)(2,1)}) custom-call(s32[1]{0:T(128)} %bitcast.index_ref.refs_0_, bf16[64,1024]{1,0:T(8,128)(2,1)S(1)} %get-tuple-element.50.refs_1_, bf16[64,1536]{1,0:T(8,128)(2,1)S(1)} %collective-permute-done.4.message_ref.refs_2_, bf16[36,256,256]{2,1,0:T(8,128)(2,1)S(1)} %get-tuple-element.46.d_ref.refs_3_, ...), custom_call_target="tpu_custom_call" | custom-call | flops 1000000000 | bytes 4194304 | tf_op jit(solution)/shard_map/own/pallas_call | solution.py:244
  20.2 0.9 %collective-permute-done.5.over_ref = bf16[64,1024]{1,0:T(8,128)(2,1)S(1)} collective-permute-done((bf16[64,1024]{1,0:T(8,128)(2,1)S(1)}, bf16[64,1024]{1,0:T(8,128)(2,1)S(1)}, u32[]{:S(2)}, u32[]{:S(2)}) %collective-permute-start.5) | collective-permute-done | bytes 131104 | tf_op jit(solution)/shard_map/ppermute | solution.py:305
  21.0 0.5 %halo.5.refs_1_ = f32[64,1024]{1,0:T(8,128)S(1)} custom-call(s32[1]{0:T(128)} %bitcast.index_ref.refs_0_, f32[64,1024]{1,0:T(8,128)S(1)} %get-tuple-element.55.acc_ref, bf16[64,1024]{1,0:T(8,128)(2,1)S(1)} %collective-permute-done.5.over_ref, bf16[36,256,256]{2,1,0:T(8,128)(2,1)S(1)} %get-tuple-element.46.d_ref.refs_3_), custom_call_target="tpu_custom_call" | custom-call | flops 1000000000 | bytes 4194304 | tf_op jit(solution)/shard_map/halo/pallas_call | solution.py:244
  21.5 0.4 %collective-permute-done.6.refs_5_ = bf16[64,128]{1,0:T(8,128)(2,1)S(1)} collective-permute-done((bf16[64,128]{1,0:T(8,128)(2,1)S(1)}, bf16[64,128]{1,0:T(8,128)(2,1)S(1)}, u32[]{:S(2)}, u32[]{:S(2)}) %collective-permute-start.6) | collective-permute-done | bytes 16416 | tf_op jit(solution)/shard_map/ppermute | solution.py:318
  22.0 1.2 %collective-permute-done.7.refs_6_ = bf16[64,128]{1,0:T(8,128)(2,1)S(1)} collective-permute-done((bf16[64,128]{1,0:T(8,128)(2,1)S(1)}, bf16[64,128]{1,0:T(8,128)(2,1)S(1)}, u32[]{:S(2)}, u32[]{:S(2)}) %collective-permute-start.7) | collective-permute-done | bytes 16416 | tf_op jit(solution)/shard_map/ppermute | solution.py:318
  23.2 0.6 %finish.4 = (bf16[64,1024]{1,0:T(8,128)(2,1)S(1)}, bf16[64,1536]{1,0:T(8,128)(2,1)S(1)}, f32[64,256]{1,0:T(8,128)S(1)}) custom-call(s32[1]{0:T(128)} %bitcast.index_ref.refs_0_, f32[64,1024]{1,0:T(8,128)S(1)} %halo.5.refs_1_, bf16[256,1024]{1,0:T(8,128)(2,1)S(1)} %get-tuple-element.47.refs_2_.refs_1_, bf16[128,1024]{1,0:T(8,128)(2,1)S(1)} %get-tuple-element.48.refs_3_, ...), custom_call_target="tpu_custom_call" | custom-call | flops 1000000000 | bytes 4194304 | tf_op jit(solution)/shard_map/finish/pallas_call | solution.py:244
  23.8 0.1 collective-permute-start.8
  23.9 2.4 %collective-permute-start.9 = (bf16[64,1024]{1,0:T(8,128)(2,1)S(1)}, bf16[64,1024]{1,0:T(8,128)(2,1)S(1)}, u32[]{:S(2)}, u32[]{:S(2)}) collective-permute-start(bf16[64,1024]{1,0:T(8,128)(2,1)S(1)} %get-tuple-element.56.refs_1_), channel_id=1, source_target_pairs={{0,15},{1,2},{2,1},{3,4},{4,3},{5,6},{6,5},{7,8},{8,7},{9,10},{10,... | collective-permute-start | bytes 393224 | tf_op jit(solution)/shard_map/ppermute | solution.py:305
  26.2 0.0 collective-permute-done.8.message_ref.refs_2_
  26.3 1.1 %collective-permute-start.10 = (bf16[64,128]{1,0:T(8,128)(2,1)S(1)}, bf16[64,128]{1,0:T(8,128)(2,1)S(1)}, u32[]{:S(2)}, u32[]{:S(2)}) collective-permute-start(bf16[64,128]{1,0:T(8,128)(2,1)S(1)} %get-tuple-element.59.refs_4_), channel_id=1, source_target_pairs={{0,8},{1,10},{2,11},{3,9},{4,12},{5,14},{6,15},{7,13},{8,0},{9,2},... | collective-permute-start | bytes 49160 | tf_op jit(solution)/shard_map/ppermute | solution.py:318
  27.4 0.8 %collective-permute-start.11 = (bf16[64,128]{1,0:T(8,128)(2,1)S(1)}, bf16[64,128]{1,0:T(8,128)(2,1)S(1)}, u32[]{:S(2)}, u32[]{:S(2)}) collective-permute-start(bf16[64,128]{1,0:T(8,128)(2,1)S(1)} %get-tuple-element.60.refs_5_), channel_id=1, source_target_pairs={{0,9},{1,11},{2,10},{3,8},{4,13},{5,15},{6,14},{7,12},{8,1},{9,3},... | collective-permute-start | bytes 49160 | tf_op jit(solution)/shard_map/ppermute | solution.py:318
  28.2 1.3 %own.4 = (f32[64,1024]{1,0:T(8,128)S(1)}, bf16[4,64,1024]{2,1,0:T(8,128)(2,1)}) custom-call(s32[1]{0:T(128)} %bitcast.index_ref.refs_0_, bf16[64,1024]{1,0:T(8,128)(2,1)S(1)} %get-tuple-element.56.refs_1_, bf16[64,1536]{1,0:T(8,128)(2,1)S(1)} %collective-permute-done.8.message_ref.refs_2_, ...), custom_call_target="tpu_custom_call", output_to_operand_aliasing={{1}: (6, {})} | custom-call | flops 1000000000 | bytes 4194304 | tf_op jit(solution)/shard_map/own/pallas_call | solution.py:244
  29.5 1.7 %collective-permute-done.9.over_ref = bf16[64,1024]{1,0:T(8,128)(2,1)S(1)} collective-permute-done((bf16[64,1024]{1,0:T(8,128)(2,1)S(1)}, bf16[64,1024]{1,0:T(8,128)(2,1)S(1)}, u32[]{:S(2)}, u32[]{:S(2)}) %collective-permute-start.9) | collective-permute-done | bytes 131104 | tf_op jit(solution)/shard_map/ppermute | solution.py:305
  31.2 0.5 %halo.6.refs_1_ = f32[64,1024]{1,0:T(8,128)S(1)} custom-call(s32[1]{0:T(128)} %bitcast.index_ref.refs_0_, f32[64,1024]{1,0:T(8,128)S(1)} %get-tuple-element.62.acc_ref, bf16[64,1024]{1,0:T(8,128)(2,1)S(1)} %collective-permute-done.9.over_ref, bf16[36,256,256]{2,1,0:T(8,128)(2,1)S(1)} %get-tuple-element.46.d_ref.refs_3_), custom_call_target="tpu_custom_call" | custom-call | flops 1000000000 | bytes 4194304 | tf_op jit(solution)/shard_map/halo/pallas_call | solution.py:244
  31.7 0.0 collective-permute-done.10.refs_5_
  31.7 0.7 %collective-permute-done.11.refs_6_ = bf16[64,128]{1,0:T(8,128)(2,1)S(1)} collective-permute-done((bf16[64,128]{1,0:T(8,128)(2,1)S(1)}, bf16[64,128]{1,0:T(8,128)(2,1)S(1)}, u32[]{:S(2)}, u32[]{:S(2)}) %collective-permute-start.11) | collective-permute-done | bytes 16416 | tf_op jit(solution)/shard_map/ppermute | solution.py:318
  32.4 0.6 %finish.5 = (bf16[64,1024]{1,0:T(8,128)(2,1)S(1)}, bf16[64,1536]{1,0:T(8,128)(2,1)S(1)}, f32[64,256]{1,0:T(8,128)S(1)}) custom-call(s32[1]{0:T(128)} %bitcast.index_ref.refs_0_, f32[64,1024]{1,0:T(8,128)S(1)} %halo.6.refs_1_, bf16[256,1024]{1,0:T(8,128)(2,1)S(1)} %get-tuple-element.47.refs_2_.refs_1_, bf16[128,1024]{1,0:T(8,128)(2,1)S(1)} %get-tuple-element.48.refs_3_, ...), custom_call_target="tpu_custom_call" | custom-call | flops 1000000000 | bytes 4194304 | tf_op jit(solution)/shard_map/finish/pallas_call | solution.py:244
  33.0 0.1 collective-permute-start.12
  33.0 2.6 %collective-permute-start.13 = (bf16[64,1024]{1,0:T(8,128)(2,1)S(1)}, bf16[64,1024]{1,0:T(8,128)(2,1)S(1)}, u32[]{:S(2)}, u32[]{:S(2)}) collective-permute-start(bf16[64,1024]{1,0:T(8,128)(2,1)S(1)} %get-tuple-element.63.refs_1_), channel_id=1, source_target_pairs={{0,15},{1,2},{2,1},{3,4},{4,3},{5,6},{6,5},{7,8},{8,7},{9,10},{10,... | collective-permute-start | bytes 393224 | tf_op jit(solution)/shard_map/ppermute | solution.py:305
  35.6 0.0 collective-permute-done.12.message_ref.refs_2_
  35.6 0.8 %collective-permute-start.14 = (bf16[64,128]{1,0:T(8,128)(2,1)S(1)}, bf16[64,128]{1,0:T(8,128)(2,1)S(1)}, u32[]{:S(2)}, u32[]{:S(2)}) collective-permute-start(bf16[64,128]{1,0:T(8,128)(2,1)S(1)} %get-tuple-element.66.refs_4_), channel_id=1, source_target_pairs={{0,8},{1,10},{2,11},{3,9},{4,12},{5,14},{6,15},{7,13},{8,0},{9,2},... | collective-permute-start | bytes 49160 | tf_op jit(solution)/shard_map/ppermute | solution.py:318
  36.4 0.9 %collective-permute-start.15 = (bf16[64,128]{1,0:T(8,128)(2,1)S(1)}, bf16[64,128]{1,0:T(8,128)(2,1)S(1)}, u32[]{:S(2)}, u32[]{:S(2)}) collective-permute-start(bf16[64,128]{1,0:T(8,128)(2,1)S(1)} %get-tuple-element.67.refs_5_), channel_id=1, source_target_pairs={{0,9},{1,11},{2,10},{3,8},{4,13},{5,15},{6,14},{7,12},{8,1},{9,3},... | collective-permute-start | bytes 49160 | tf_op jit(solution)/shard_map/ppermute | solution.py:318
  37.3 1.3 %own.5 = (f32[64,1024]{1,0:T(8,128)S(1)}, bf16[4,64,1024]{2,1,0:T(8,128)(2,1)}) custom-call(s32[1]{0:T(128)} %bitcast.index_ref.refs_0_, bf16[64,1024]{1,0:T(8,128)(2,1)S(1)} %get-tuple-element.63.refs_1_, bf16[64,1536]{1,0:T(8,128)(2,1)S(1)} %collective-permute-done.12.message_ref.refs_2_, ...), custom_call_target="tpu_custom_call", output_to_operand_aliasing={{1}: (6, {})} | custom-call | flops 1000000000 | bytes 4194304 | tf_op jit(solution)/shard_map/own/pallas_call | solution.py:244
  38.6 1.7 %collective-permute-done.13.over_ref = bf16[64,1024]{1,0:T(8,128)(2,1)S(1)} collective-permute-done((bf16[64,1024]{1,0:T(8,128)(2,1)S(1)}, bf16[64,1024]{1,0:T(8,128)(2,1)S(1)}, u32[]{:S(2)}, u32[]{:S(2)}) %collective-permute-start.13) | collective-permute-done | bytes 131104 | tf_op jit(solution)/shard_map/ppermute | solution.py:305
  40.3 0.5 %halo.7.refs_0_ = f32[64,1024]{1,0:T(8,128)S(1)} custom-call(s32[1]{0:T(128)} %bitcast.index_ref.refs_0_, f32[64,1024]{1,0:T(8,128)S(1)} %get-tuple-element.69.acc_ref, bf16[64,1024]{1,0:T(8,128)(2,1)S(1)} %collective-permute-done.13.over_ref, bf16[36,256,256]{2,1,0:T(8,128)(2,1)S(1)} %get-tuple-element.46.d_ref.refs_3_), custom_call_target="tpu_custom_call" | custom-call | flops 1000000000 | bytes 4194304 | tf_op jit(solution)/shard_map/halo/pallas_call | solution.py:244
  40.8 0.0 collective-permute-done.14.refs_2_
  40.9 0.6 %collective-permute-done.15.refs_3_ = bf16[64,128]{1,0:T(8,128)(2,1)S(1)} collective-permute-done((bf16[64,128]{1,0:T(8,128)(2,1)S(1)}, bf16[64,128]{1,0:T(8,128)(2,1)S(1)}, u32[]{:S(2)}, u32[]{:S(2)}) %collective-permute-start.15) | collective-permute-done | bytes 16416 | tf_op jit(solution)/shard_map/ppermute | solution.py:318
  41.4 0.9 %last.1 = bf16[4,64,1024]{2,1,0:T(8,128)(2,1)} custom-call(f32[64,1024]{1,0:T(8,128)S(1)} %halo.7.refs_0_, bf16[256,1024]{1,0:T(8,128)(2,1)S(1)} %get-tuple-element.47.refs_2_.refs_1_, bf16[64,128]{1,0:T(8,128)(2,1)S(1)} %collective-permute-done.14.refs_2_, bf16[64,128]{1,0:T(8,128)(2,1)S(1)} %collective-permute-done.15.refs_3_, ...), custom_call_target="tpu_custom_call", output_to_operand_aliasing={{}: (4, {})} | custom-call | flops 1000000000 | bytes 4194304 | tf_op jit(solution)/shard_map/last/pallas_call | solution.py:244
  (4 shorter events, 0.1 us)
Async XLA Ops:
  0.0 8.5 %copy-start.1 = (bf16[4,32,256]{2,1,0:T(8,128)(2,1)S(1)}, bf16[4,32,256]{2,1,0:T(8,128)(2,1)}, u32[]{:S(2)}) copy-start(bf16[4,32,256]{2,1,0:T(8,128)(2,1)} %refs_5_.3) | copy-start | bytes 196612
  0.0 8.5 %copy-start = (bf16[32,256,256]{2,1,0:T(8,128)(2,1)S(1)}, bf16[32,256,256]{2,1,0:T(8,128)(2,1)}, u32[]{:S(2)}) copy-start(bf16[32,256,256]{2,1,0:T(8,128)(2,1)} %refs_6_.3) | copy-start | bytes 12582916
  1.8 6.2 %collective-permute-start = (bf16[64,1536]{1,0:T(8,128)(2,1)S(1)}, bf16[64,1536]{1,0:T(8,128)(2,1)S(1)}, u32[]{:S(2)}, u32[]{:S(2)}) collective-permute-start(bf16[64,1536]{1,0:T(8,128)(2,1)S(1)} %get-tuple-element.41), channel_id=1, source_target_pairs={{0,1},{1,0},{2,3},{3,2},{4,5},{5,4},{6,7},{7,6},{8,9},{9,8},{10,11... | collective-permute-start | bytes 589832 | tf_op jit(solution)/shard_map/ppermute | solution.py:306
  2.4 8.6 %collective-permute-start.1 = (bf16[64,1024]{1,0:T(8,128)(2,1)}, bf16[64,1024]{1,0:T(8,128)(2,1)S(1)}, u32[]{:S(2)}, u32[]{:S(2)}) collective-permute-start(bf16[64,1024]{1,0:T(8,128)(2,1)} %refs_4_.1), channel_id=1, source_target_pairs={{0,15},{1,2},{2,1},{3,4},{4,3},{5,6},{6,5},{7,8},{8,7},{9,10},{10,... | collective-permute-start | bytes 393224 | tf_op jit(solution)/shard_map/ppermute | solution.py:305
  8.0 4.7 %collective-permute-start.2 = (bf16[64,128]{1,0:T(8,128)(2,1)S(1)}, bf16[64,128]{1,0:T(8,128)(2,1)S(1)}, u32[]{:S(2)}, u32[]{:S(2)}) collective-permute-start(bf16[64,128]{1,0:T(8,128)(2,1)S(1)} %get-tuple-element.43.refs_7_), channel_id=1, source_target_pairs={{0,8},{1,10},{2,11},{3,9},{4,12},{5,14},{6,15},{7,13},{8,0},{9,2},... | collective-permute-start | bytes 49160 | tf_op jit(solution)/shard_map/ppermute | solution.py:318
  8.1 5.0 %collective-permute-start.3 = (bf16[64,128]{1,0:T(8,128)(2,1)S(1)}, bf16[64,128]{1,0:T(8,128)(2,1)S(1)}, u32[]{:S(2)}, u32[]{:S(2)}) collective-permute-start(bf16[64,128]{1,0:T(8,128)(2,1)S(1)} %get-tuple-element.44.refs_8_), channel_id=1, source_target_pairs={{0,9},{1,11},{2,10},{3,8},{4,13},{5,15},{6,14},{7,12},{8,1},{9,3},... | collective-permute-start | bytes 49160 | tf_op jit(solution)/shard_map/ppermute | solution.py:318
  13.7 3.6 %collective-permute-start.4 = (bf16[64,1536]{1,0:T(8,128)(2,1)S(1)}, bf16[64,1536]{1,0:T(8,128)(2,1)S(1)}, u32[]{:S(2)}, u32[]{:S(2)}) collective-permute-start(bf16[64,1536]{1,0:T(8,128)(2,1)S(1)} %get-tuple-element.51), channel_id=1, source_target_pairs={{0,1},{1,0},{2,3},{3,2},{4,5},{5,4},{6,7},{7,6},{8,9},{9,8},{10,11... | collective-permute-start | bytes 589832 | tf_op jit(solution)/shard_map/ppermute | solution.py:306
  13.8 7.2 %collective-permute-start.5 = (bf16[64,1024]{1,0:T(8,128)(2,1)S(1)}, bf16[64,1024]{1,0:T(8,128)(2,1)S(1)}, u32[]{:S(2)}, u32[]{:S(2)}) collective-permute-start(bf16[64,1024]{1,0:T(8,128)(2,1)S(1)} %get-tuple-element.50.refs_1_), channel_id=1, source_target_pairs={{0,15},{1,2},{2,1},{3,4},{4,3},{5,6},{6,5},{7,8},{8,7},{9,10},{10,... | collective-permute-start | bytes 393224 | tf_op jit(solution)/shard_map/ppermute | solution.py:305
  17.3 4.7 %collective-permute-start.6 = (bf16[64,128]{1,0:T(8,128)(2,1)S(1)}, bf16[64,128]{1,0:T(8,128)(2,1)S(1)}, u32[]{:S(2)}, u32[]{:S(2)}) collective-permute-start(bf16[64,128]{1,0:T(8,128)(2,1)S(1)} %get-tuple-element.53.refs_4_), channel_id=1, source_target_pairs={{0,8},{1,10},{2,11},{3,9},{4,12},{5,14},{6,15},{7,13},{8,0},{9,2},... | collective-permute-start | bytes 49160 | tf_op jit(solution)/shard_map/ppermute | solution.py:318
  18.1 5.1 %collective-permute-start.7 = (bf16[64,128]{1,0:T(8,128)(2,1)S(1)}, bf16[64,128]{1,0:T(8,128)(2,1)S(1)}, u32[]{:S(2)}, u32[]{:S(2)}) collective-permute-start(bf16[64,128]{1,0:T(8,128)(2,1)S(1)} %get-tuple-element.54.refs_5_), channel_id=1, source_target_pairs={{0,9},{1,11},{2,10},{3,8},{4,13},{5,15},{6,14},{7,12},{8,1},{9,3},... | collective-permute-start | bytes 49160 | tf_op jit(solution)/shard_map/ppermute | solution.py:318
  23.8 2.4 %collective-permute-start.8 = (bf16[64,1536]{1,0:T(8,128)(2,1)S(1)}, bf16[64,1536]{1,0:T(8,128)(2,1)S(1)}, u32[]{:S(2)}, u32[]{:S(2)}) collective-permute-start(bf16[64,1536]{1,0:T(8,128)(2,1)S(1)} %get-tuple-element.57), channel_id=1, source_target_pairs={{0,1},{1,0},{2,3},{3,2},{4,5},{5,4},{6,7},{7,6},{8,9},{9,8},{10,11... | collective-permute-start | bytes 589832 | tf_op jit(solution)/shard_map/ppermute | solution.py:306
  23.9 7.3 %collective-permute-start.9 = (bf16[64,1024]{1,0:T(8,128)(2,1)S(1)}, bf16[64,1024]{1,0:T(8,128)(2,1)S(1)}, u32[]{:S(2)}, u32[]{:S(2)}) collective-permute-start(bf16[64,1024]{1,0:T(8,128)(2,1)S(1)} %get-tuple-element.56.refs_1_), channel_id=1, source_target_pairs={{0,15},{1,2},{2,1},{3,4},{4,3},{5,6},{6,5},{7,8},{8,7},{9,10},{10,... | collective-permute-start | bytes 393224 | tf_op jit(solution)/shard_map/ppermute | solution.py:305
  26.3 5.4 %collective-permute-start.10 = (bf16[64,128]{1,0:T(8,128)(2,1)S(1)}, bf16[64,128]{1,0:T(8,128)(2,1)S(1)}, u32[]{:S(2)}, u32[]{:S(2)}) collective-permute-start(bf16[64,128]{1,0:T(8,128)(2,1)S(1)} %get-tuple-element.59.refs_4_), channel_id=1, source_target_pairs={{0,8},{1,10},{2,11},{3,9},{4,12},{5,14},{6,15},{7,13},{8,0},{9,2},... | collective-permute-start | bytes 49160 | tf_op jit(solution)/shard_map/ppermute | solution.py:318
  27.4 5.0 %collective-permute-start.11 = (bf16[64,128]{1,0:T(8,128)(2,1)S(1)}, bf16[64,128]{1,0:T(8,128)(2,1)S(1)}, u32[]{:S(2)}, u32[]{:S(2)}) collective-permute-start(bf16[64,128]{1,0:T(8,128)(2,1)S(1)} %get-tuple-element.60.refs_5_), channel_id=1, source_target_pairs={{0,9},{1,11},{2,10},{3,8},{4,13},{5,15},{6,14},{7,12},{8,1},{9,3},... | collective-permute-start | bytes 49160 | tf_op jit(solution)/shard_map/ppermute | solution.py:318
  33.0 2.7 %collective-permute-start.12 = (bf16[64,1536]{1,0:T(8,128)(2,1)S(1)}, bf16[64,1536]{1,0:T(8,128)(2,1)S(1)}, u32[]{:S(2)}, u32[]{:S(2)}) collective-permute-start(bf16[64,1536]{1,0:T(8,128)(2,1)S(1)} %get-tuple-element.64), channel_id=1, source_target_pairs={{0,1},{1,0},{2,3},{3,2},{4,5},{5,4},{6,7},{7,6},{8,9},{9,8},{10,11... | collective-permute-start | bytes 589832 | tf_op jit(solution)/shard_map/ppermute | solution.py:306
  33.0 7.3 %collective-permute-start.13 = (bf16[64,1024]{1,0:T(8,128)(2,1)S(1)}, bf16[64,1024]{1,0:T(8,128)(2,1)S(1)}, u32[]{:S(2)}, u32[]{:S(2)}) collective-permute-start(bf16[64,1024]{1,0:T(8,128)(2,1)S(1)} %get-tuple-element.63.refs_1_), channel_id=1, source_target_pairs={{0,15},{1,2},{2,1},{3,4},{4,3},{5,6},{6,5},{7,8},{8,7},{9,10},{10,... | collective-permute-start | bytes 393224 | tf_op jit(solution)/shard_map/ppermute | solution.py:305
  35.6 5.2 %collective-permute-start.14 = (bf16[64,128]{1,0:T(8,128)(2,1)S(1)}, bf16[64,128]{1,0:T(8,128)(2,1)S(1)}, u32[]{:S(2)}, u32[]{:S(2)}) collective-permute-start(bf16[64,128]{1,0:T(8,128)(2,1)S(1)} %get-tuple-element.66.refs_4_), channel_id=1, source_target_pairs={{0,8},{1,10},{2,11},{3,9},{4,12},{5,14},{6,15},{7,13},{8,0},{9,2},... | collective-permute-start | bytes 49160 | tf_op jit(solution)/shard_map/ppermute | solution.py:318
  36.4 5.0 %collective-permute-start.15 = (bf16[64,128]{1,0:T(8,128)(2,1)S(1)}, bf16[64,128]{1,0:T(8,128)(2,1)S(1)}, u32[]{:S(2)}, u32[]{:S(2)}) collective-permute-start(bf16[64,128]{1,0:T(8,128)(2,1)S(1)} %get-tuple-element.67.refs_5_), channel_id=1, source_target_pairs={{0,9},{1,11},{2,10},{3,8},{4,13},{5,15},{6,14},{7,12},{8,1},{9,3},... | collective-permute-start | bytes 49160 | tf_op jit(solution)/shard_map/ppermute | solution.py:318

commit v18 on v17

--- a/solution.py
+++ b/solution.py
@@ -57,7 +57,7 @@
                 (l * members + m, (l + self.hops[0]) % loop_size * members + self.far_target(m, other))
                 for l, m in places
             ]
-            for other in (0, 1)
+            for other in (1, 0)
         ]
         self.routes = [
             [(l * members + m, (l + hop) % loop_size * members + (m + step) % members) for l, m in places]
@@ -101,8 +101,8 @@
         total = (keep_ref[...] + (upper + lower)).astype(BF16)
         second = self.member(index_ref) >= 2
         first, last = total[:, : self.width], total[:, self.width :]
-        out_refs[0][...] = jnp.where(second, last, first)
-        out_refs[1][...] = jnp.where(second, first, last)
+        out_refs[0][...] = jnp.where(second, first, last)
+        out_refs[1][...] = jnp.where(second, last, first)
 
     def far_sum(self, far_refs):
         return sum(ref[...].astype(F32) for ref in far_refs)

time: 42.4 us -> 42.2 us (level)
  starting transfers between devices: 20.4 us -> 19.2 us
  waiting for transfers between devices: 9.46 us -> 10.5 us
    ppermute x8, starting transfers between devices: 5.6 us -> 2.01 us  [on_device(): fars = [lax.ppermute(s, axes, route) for s, route in zip(sends, routes)]]
    ppermute x4, starting transfers between devices: 14 us -> 16.1 us  [on_device(): over = lax.ppermute(block if product == 0 else current, axes, plan.over)]
    ppermute x4, waiting for transfers between devices: 4.87 us -> 6.03 us  [on_device(): over = lax.ppermute(block if product == 0 else current, axes, plan.over)]
  transfers between devices with their start and end apart: 16 -> 16, of which waited for: 10 -> 8; matrix products, arithmetic and copies ran while one was open for 0% -> 0% of each run, Pallas kernels for 19% -> 19%
where the time goes in v18:
time: 42.2 us; the launch traced here: 42.1 us
  starting transfers between devices  19.2 us (45%)
  Pallas kernels  12.3 us (29%)
  waiting for transfers between devices  10.5 us (25%)
    ppermute x4, starting transfers between devices, on_device(): over = lax.ppermute(block if product == 0 else current, axes, plan.over)  16.1 us
    pallas_call x17, Pallas kernels, call(): pl.pallas_call(kernel, in_specs=list(specs), out_specs=out_specs or [IN_V...  12.3 us
    ppermute x4, waiting for transfers between devices, on_device(): over = lax.ppermute(block if product == 0 else current, axes, plan.over)  6.03 us
    ppermute x8, waiting for transfers between devices, on_device(): fars = [lax.ppermute(s, axes, route) for s, route in zip(sends, routes)]  4.44 us
    ppermute x8, starting transfers between devices, on_device(): fars = [lax.ppermute(s, axes, route) for s, route in zip(sends, routes)]  2.01 us
    ppermute x4, starting transfers between devices, on_device(): near = lax.ppermute(sends[0] if plan.paired else current, axes, plan.near)  1.05 us
  transfers between devices with their start and end apart: 16, of which 8 were waited for; matrix products, arithmetic and copies ran while one was open for 0% of the time, Pallas kernels for 19%

profile of v18, /device:TPU:0, one launch (start us, length us, event | category | flops | bytes accessed | tf_op | source)
XLA Modules:
  0.0 42.1 jit_solution(4373106124337541768)
XLA Ops:
  0.0 0.0 copy-start.1
  0.0 0.0 copy-start
  0.0 1.8 %prepare.1 = (bf16[64,1024]{1,0:T(8,128)(2,1)S(1)}, bf16[1,512,256]{2,1,0:T(8,128)(2,1)S(1)}, bf16[128,1024]{1,0:T(8,128)(2,1)S(1)}, s32[32]{0:T(128)S(4)}, s32[...) custom-call(s32[1]{0:T(128)} %bitcast.index_ref.refs_0_, s32[32]{0:T(128)} %refs_0_.1, s32[32]{0:T(128)} %refs_1_.1, ...), custom_call_target="tpu_custom_call" | custom-call | flops 1000000000 | bytes 4194304 | tf_op jit(solution)/shard_map/prepare/pallas_call | solution.py:244
  1.8 0.5 %collective-permute-start = (bf16[64,1536]{1,0:T(8,128)(2,1)S(1)}, bf16[64,1536]{1,0:T(8,128)(2,1)S(1)}, u32[]{:S(2)}, u32[]{:S(2)}) collective-permute-start(bf16[64,1536]{1,0:T(8,128)(2,1)S(1)} %get-tuple-element.41), channel_id=1, source_target_pairs={{0,1},{1,0},{2,3},{3,2},{4,5},{5,4},{6,7},{7,6},{8,9},{9,8},{10,11... | collective-permute-start | bytes 589832 | tf_op jit(solution)/shard_map/ppermute | solution.py:306
  2.4 5.6 %collective-permute-start.1 = (bf16[64,1024]{1,0:T(8,128)(2,1)}, bf16[64,1024]{1,0:T(8,128)(2,1)S(1)}, u32[]{:S(2)}, u32[]{:S(2)}) collective-permute-start(bf16[64,1024]{1,0:T(8,128)(2,1)} %refs_4_.1), channel_id=1, source_target_pairs={{0,15},{1,2},{2,1},{3,4},{4,3},{5,6},{6,5},{7,8},{8,7},{9,10},{10,... | collective-permute-start | bytes 393224 | tf_op jit(solution)/shard_map/ppermute | solution.py:305
  8.0 0.0 collective-permute-done.message_ref.refs_4_
  8.0 0.1 collective-permute-start.2
  8.1 0.1 collective-permute-start.3
  8.2 0.0 copy-done.1
  8.2 0.0 copy-done
  8.2 1.9 %first_own.1 = (f32[64,1024]{1,0:T(8,128)S(1)}, bf16[36,256,256]{2,1,0:T(8,128)(2,1)S(1)}, bf16[256,1024]{1,0:T(8,128)(2,1)S(1)}) custom-call(s32[1]{0:T(128)} %bitcast.index_ref.refs_0_, s32[32]{0:T(128)S(4)} %get-tuple-element.38.refs_1_, s32[32]{0:T(128)S(4)} %get-tuple-element.39.refs_2_, bf16[64,1024]{1,0:T(8,128)(2,1)S(1)} %get-tuple-element.40.refs_3_, ...), custom_call_target="tpu_custom_call" | custom-call | flops 1000000000 | bytes 4194304 | tf_op jit(solution)/shard_map/first_own/pallas_call | solution.py:244
  10.1 0.9 %collective-permute-done.1.over_ref = bf16[64,1024]{1,0:T(8,128)(2,1)S(1)} collective-permute-done((bf16[64,1024]{1,0:T(8,128)(2,1)}, bf16[64,1024]{1,0:T(8,128)(2,1)S(1)}, u32[]{:S(2)}, u32[]{:S(2)}) %collective-permute-start.1) | collective-permute-done | bytes 131104 | tf_op jit(solution)/shard_map/ppermute | solution.py:305
  10.9 0.5 %halo.4.refs_1_ = f32[64,1024]{1,0:T(8,128)S(1)} custom-call(s32[1]{0:T(128)} %bitcast.index_ref.refs_0_, f32[64,1024]{1,0:T(8,128)S(1)} %get-tuple-element.45.acc_ref, bf16[64,1024]{1,0:T(8,128)(2,1)S(1)} %collective-permute-done.1.over_ref, bf16[36,256,256]{2,1,0:T(8,128)(2,1)S(1)} %get-tuple-element.46.d_ref.refs_3_), custom_call_target="tpu_custom_call" | custom-call | flops 1000000000 | bytes 4194304 | tf_op jit(solution)/shard_map/halo/pallas_call | solution.py:244
  11.4 1.6 %collective-permute-done.2.refs_5_ = bf16[64,128]{1,0:T(8,128)(2,1)S(1)} collective-permute-done((bf16[64,128]{1,0:T(8,128)(2,1)S(1)}, bf16[64,128]{1,0:T(8,128)(2,1)S(1)}, u32[]{:S(2)}, u32[]{:S(2)}) %collective-permute-start.2) | collective-permute-done | bytes 16416 | tf_op jit(solution)/shard_map/ppermute | solution.py:318
  13.0 0.0 collective-permute-done.3.refs_6_
  13.1 0.6 %finish.3 = (bf16[64,1024]{1,0:T(8,128)(2,1)S(1)}, bf16[64,1536]{1,0:T(8,128)(2,1)S(1)}, f32[64,256]{1,0:T(8,128)S(1)}) custom-call(s32[1]{0:T(128)} %bitcast.index_ref.refs_0_, f32[64,1024]{1,0:T(8,128)S(1)} %halo.4.refs_1_, bf16[256,1024]{1,0:T(8,128)(2,1)S(1)} %get-tuple-element.47.refs_2_.refs_1_, bf16[128,1024]{1,0:T(8,128)(2,1)S(1)} %get-tuple-element.48.refs_3_, ...), custom_call_target="tpu_custom_call" | custom-call | flops 1000000000 | bytes 4194304 | tf_op jit(solution)/shard_map/finish/pallas_call | solution.py:244
  13.6 0.2 collective-permute-start.4
  13.8 3.5 %collective-permute-start.5 = (bf16[64,1024]{1,0:T(8,128)(2,1)S(1)}, bf16[64,1024]{1,0:T(8,128)(2,1)S(1)}, u32[]{:S(2)}, u32[]{:S(2)}) collective-permute-start(bf16[64,1024]{1,0:T(8,128)(2,1)S(1)} %get-tuple-element.50.refs_1_), channel_id=1, source_target_pairs={{0,15},{1,2},{2,1},{3,4},{4,3},{5,6},{6,5},{7,8},{8,7},{9,10},{10,... | collective-permute-start | bytes 393224 | tf_op jit(solution)/shard_map/ppermute | solution.py:305
  17.3 0.0 collective-permute-done.4.message_ref.refs_2_
  17.4 0.1 collective-permute-start.6
  17.4 0.7 %collective-permute-start.7 = (bf16[64,128]{1,0:T(8,128)(2,1)S(1)}, bf16[64,128]{1,0:T(8,128)(2,1)S(1)}, u32[]{:S(2)}, u32[]{:S(2)}) collective-permute-start(bf16[64,128]{1,0:T(8,128)(2,1)S(1)} %get-tuple-element.54.refs_5_), channel_id=1, source_target_pairs={{0,8},{1,10},{2,11},{3,9},{4,12},{5,14},{6,15},{7,13},{8,0},{9,2},... | collective-permute-start | bytes 49160 | tf_op jit(solution)/shard_map/ppermute | solution.py:318
  18.1 1.3 %own.3 = (f32[64,1024]{1,0:T(8,128)S(1)}, bf16[4,64,1024]{2,1,0:T(8,128)(2,1)}) custom-call(s32[1]{0:T(128)} %bitcast.index_ref.refs_0_, bf16[64,1024]{1,0:T(8,128)(2,1)S(1)} %get-tuple-element.50.refs_1_, bf16[64,1536]{1,0:T(8,128)(2,1)S(1)} %collective-permute-done.4.message_ref.refs_2_, bf16[36,256,256]{2,1,0:T(8,128)(2,1)S(1)} %get-tuple-element.46.d_ref.refs_3_, ...), custom_call_target="tpu_custom_call" | custom-call | flops 1000000000 | bytes 4194304 | tf_op jit(solution)/shard_map/own/pallas_call | solution.py:244
  19.4 1.5 %collective-permute-done.5.over_ref = bf16[64,1024]{1,0:T(8,128)(2,1)S(1)} collective-permute-done((bf16[64,1024]{1,0:T(8,128)(2,1)S(1)}, bf16[64,1024]{1,0:T(8,128)(2,1)S(1)}, u32[]{:S(2)}, u32[]{:S(2)}) %collective-permute-start.5) | collective-permute-done | bytes 131104 | tf_op jit(solution)/shard_map/ppermute | solution.py:305
  20.9 0.5 %halo.5.refs_1_ = f32[64,1024]{1,0:T(8,128)S(1)} custom-call(s32[1]{0:T(128)} %bitcast.index_ref.refs_0_, f32[64,1024]{1,0:T(8,128)S(1)} %get-tuple-element.55.acc_ref, bf16[64,1024]{1,0:T(8,128)(2,1)S(1)} %collective-permute-done.5.over_ref, bf16[36,256,256]{2,1,0:T(8,128)(2,1)S(1)} %get-tuple-element.46.d_ref.refs_3_), custom_call_target="tpu_custom_call" | custom-call | flops 1000000000 | bytes 4194304 | tf_op jit(solution)/shard_map/halo/pallas_call | solution.py:244
  21.4 1.0 %collective-permute-done.6.refs_5_ = bf16[64,128]{1,0:T(8,128)(2,1)S(1)} collective-permute-done((bf16[64,128]{1,0:T(8,128)(2,1)S(1)}, bf16[64,128]{1,0:T(8,128)(2,1)S(1)}, u32[]{:S(2)}, u32[]{:S(2)}) %collective-permute-start.6) | collective-permute-done | bytes 16416 | tf_op jit(solution)/shard_map/ppermute | solution.py:318
  22.4 0.0 collective-permute-done.7.refs_6_
  22.4 0.6 %finish.4 = (bf16[64,1024]{1,0:T(8,128)(2,1)S(1)}, bf16[64,1536]{1,0:T(8,128)(2,1)S(1)}, f32[64,256]{1,0:T(8,128)S(1)}) custom-call(s32[1]{0:T(128)} %bitcast.index_ref.refs_0_, f32[64,1024]{1,0:T(8,128)S(1)} %halo.5.refs_1_, bf16[256,1024]{1,0:T(8,128)(2,1)S(1)} %get-tuple-element.47.refs_2_.refs_1_, bf16[128,1024]{1,0:T(8,128)(2,1)S(1)} %get-tuple-element.48.refs_3_, ...), custom_call_target="tpu_custom_call" | custom-call | flops 1000000000 | bytes 4194304 | tf_op jit(solution)/shard_map/finish/pallas_call | solution.py:244
  23.0 0.2 collective-permute-start.8
  23.2 3.6 %collective-permute-start.9 = (bf16[64,1024]{1,0:T(8,128)(2,1)S(1)}, bf16[64,1024]{1,0:T(8,128)(2,1)S(1)}, u32[]{:S(2)}, u32[]{:S(2)}) collective-permute-start(bf16[64,1024]{1,0:T(8,128)(2,1)S(1)} %get-tuple-element.56.refs_1_), channel_id=1, source_target_pairs={{0,15},{1,2},{2,1},{3,4},{4,3},{5,6},{6,5},{7,8},{8,7},{9,10},{10,... | collective-permute-start | bytes 393224 | tf_op jit(solution)/shard_map/ppermute | solution.py:305
  26.8 0.0 collective-permute-done.8.message_ref.refs_2_
  26.8 0.1 collective-permute-start.10
  26.9 0.4 collective-permute-start.11
  27.3 1.3 %own.4 = (f32[64,1024]{1,0:T(8,128)S(1)}, bf16[4,64,1024]{2,1,0:T(8,128)(2,1)}) custom-call(s32[1]{0:T(128)} %bitcast.index_ref.refs_0_, bf16[64,1024]{1,0:T(8,128)(2,1)S(1)} %get-tuple-element.56.refs_1_, bf16[64,1536]{1,0:T(8,128)(2,1)S(1)} %collective-permute-done.8.message_ref.refs_2_, ...), custom_call_target="tpu_custom_call", output_to_operand_aliasing={{1}: (6, {})} | custom-call | flops 1000000000 | bytes 4194304 | tf_op jit(solution)/shard_map/own/pallas_call | solution.py:244
  28.6 1.8 %collective-permute-done.9.over_ref = bf16[64,1024]{1,0:T(8,128)(2,1)S(1)} collective-permute-done((bf16[64,1024]{1,0:T(8,128)(2,1)S(1)}, bf16[64,1024]{1,0:T(8,128)(2,1)S(1)}, u32[]{:S(2)}, u32[]{:S(2)}) %collective-permute-start.9) | collective-permute-done | bytes 131104 | tf_op jit(solution)/shard_map/ppermute | solution.py:305
  30.4 0.5 %halo.6.refs_1_ = f32[64,1024]{1,0:T(8,128)S(1)} custom-call(s32[1]{0:T(128)} %bitcast.index_ref.refs_0_, f32[64,1024]{1,0:T(8,128)S(1)} %get-tuple-element.62.acc_ref, bf16[64,1024]{1,0:T(8,128)(2,1)S(1)} %collective-permute-done.9.over_ref, bf16[36,256,256]{2,1,0:T(8,128)(2,1)S(1)} %get-tuple-element.46.d_ref.refs_3_), custom_call_target="tpu_custom_call" | custom-call | flops 1000000000 | bytes 4194304 | tf_op jit(solution)/shard_map/halo/pallas_call | solution.py:244
  30.9 1.1 %collective-permute-done.10.refs_5_ = bf16[64,128]{1,0:T(8,128)(2,1)S(1)} collective-permute-done((bf16[64,128]{1,0:T(8,128)(2,1)S(1)}, bf16[64,128]{1,0:T(8,128)(2,1)S(1)}, u32[]{:S(2)}, u32[]{:S(2)}) %collective-permute-start.10) | collective-permute-done | bytes 16416 | tf_op jit(solution)/shard_map/ppermute | solution.py:318
  32.0 0.0 collective-permute-done.11.refs_6_
  32.0 0.6 %finish.5 = (bf16[64,1024]{1,0:T(8,128)(2,1)S(1)}, bf16[64,1536]{1,0:T(8,128)(2,1)S(1)}, f32[64,256]{1,0:T(8,128)S(1)}) custom-call(s32[1]{0:T(128)} %bitcast.index_ref.refs_0_, f32[64,1024]{1,0:T(8,128)S(1)} %halo.6.refs_1_, bf16[256,1024]{1,0:T(8,128)(2,1)S(1)} %get-tuple-element.47.refs_2_.refs_1_, bf16[128,1024]{1,0:T(8,128)(2,1)S(1)} %get-tuple-element.48.refs_3_, ...), custom_call_target="tpu_custom_call" | custom-call | flops 1000000000 | bytes 4194304 | tf_op jit(solution)/shard_map/finish/pallas_call | solution.py:244
  32.6 0.2 collective-permute-start.12
  32.8 3.4 %collective-permute-start.13 = (bf16[64,1024]{1,0:T(8,128)(2,1)S(1)}, bf16[64,1024]{1,0:T(8,128)(2,1)S(1)}, u32[]{:S(2)}, u32[]{:S(2)}) collective-permute-start(bf16[64,1024]{1,0:T(8,128)(2,1)S(1)} %get-tuple-element.63.refs_1_), channel_id=1, source_target_pairs={{0,15},{1,2},{2,1},{3,4},{4,3},{5,6},{6,5},{7,8},{8,7},{9,10},{10,... | collective-permute-start | bytes 393224 | tf_op jit(solution)/shard_map/ppermute | solution.py:305
  36.1 0.0 collective-permute-done.12.message_ref.refs_2_
  36.1 0.1 collective-permute-start.14
  36.2 0.6 %collective-permute-start.15 = (bf16[64,128]{1,0:T(8,128)(2,1)S(1)}, bf16[64,128]{1,0:T(8,128)(2,1)S(1)}, u32[]{:S(2)}, u32[]{:S(2)}) collective-permute-start(bf16[64,128]{1,0:T(8,128)(2,1)S(1)} %get-tuple-element.67.refs_5_), channel_id=1, source_target_pairs={{0,8},{1,10},{2,11},{3,9},{4,12},{5,14},{6,15},{7,13},{8,0},{9,2},... | collective-permute-start | bytes 49160 | tf_op jit(solution)/shard_map/ppermute | solution.py:318
  36.8 1.3 %own.5 = (f32[64,1024]{1,0:T(8,128)S(1)}, bf16[4,64,1024]{2,1,0:T(8,128)(2,1)}) custom-call(s32[1]{0:T(128)} %bitcast.index_ref.refs_0_, bf16[64,1024]{1,0:T(8,128)(2,1)S(1)} %get-tuple-element.63.refs_1_, bf16[64,1536]{1,0:T(8,128)(2,1)S(1)} %collective-permute-done.12.message_ref.refs_2_, ...), custom_call_target="tpu_custom_call", output_to_operand_aliasing={{1}: (6, {})} | custom-call | flops 1000000000 | bytes 4194304 | tf_op jit(solution)/shard_map/own/pallas_call | solution.py:244
  38.1 1.8 %collective-permute-done.13.over_ref = bf16[64,1024]{1,0:T(8,128)(2,1)S(1)} collective-permute-done((bf16[64,1024]{1,0:T(8,128)(2,1)S(1)}, bf16[64,1024]{1,0:T(8,128)(2,1)S(1)}, u32[]{:S(2)}, u32[]{:S(2)}) %collective-permute-start.13) | collective-permute-done | bytes 131104 | tf_op jit(solution)/shard_map/ppermute | solution.py:305
  39.9 0.5 %halo.7.refs_0_ = f32[64,1024]{1,0:T(8,128)S(1)} custom-call(s32[1]{0:T(128)} %bitcast.index_ref.refs_0_, f32[64,1024]{1,0:T(8,128)S(1)} %get-tuple-element.69.acc_ref, bf16[64,1024]{1,0:T(8,128)(2,1)S(1)} %collective-permute-done.13.over_ref, bf16[36,256,256]{2,1,0:T(8,128)(2,1)S(1)} %get-tuple-element.46.d_ref.refs_3_), custom_call_target="tpu_custom_call" | custom-call | flops 1000000000 | bytes 4194304 | tf_op jit(solution)/shard_map/halo/pallas_call | solution.py:244
  40.5 0.8 %collective-permute-done.14.refs_2_ = bf16[64,128]{1,0:T(8,128)(2,1)S(1)} collective-permute-done((bf16[64,128]{1,0:T(8,128)(2,1)S(1)}, bf16[64,128]{1,0:T(8,128)(2,1)S(1)}, u32[]{:S(2)}, u32[]{:S(2)}) %collective-permute-start.14) | collective-permute-done | bytes 16416 | tf_op jit(solution)/shard_map/ppermute | solution.py:318
  41.2 0.0 collective-permute-done.15.refs_3_
  41.2 0.9 %last.1 = bf16[4,64,1024]{2,1,0:T(8,128)(2,1)} custom-call(f32[64,1024]{1,0:T(8,128)S(1)} %halo.7.refs_0_, bf16[256,1024]{1,0:T(8,128)(2,1)S(1)} %get-tuple-element.47.refs_2_.refs_1_, bf16[64,128]{1,0:T(8,128)(2,1)S(1)} %collective-permute-done.14.refs_2_, bf16[64,128]{1,0:T(8,128)(2,1)S(1)} %collective-permute-done.15.refs_3_, ...), custom_call_target="tpu_custom_call", output_to_operand_aliasing={{}: (4, {})} | custom-call | flops 1000000000 | bytes 4194304 | tf_op jit(solution)/shard_map/last/pallas_call | solution.py:244
  (4 shorter events, 0.1 us)
Async XLA Ops:
  0.0 8.2 %copy-start.1 = (bf16[4,32,256]{2,1,0:T(8,128)(2,1)S(1)}, bf16[4,32,256]{2,1,0:T(8,128)(2,1)}, u32[]{:S(2)}) copy-start(bf16[4,32,256]{2,1,0:T(8,128)(2,1)} %refs_5_.3) | copy-start | bytes 196612
  0.0 8.2 %copy-start = (bf16[32,256,256]{2,1,0:T(8,128)(2,1)S(1)}, bf16[32,256,256]{2,1,0:T(8,128)(2,1)}, u32[]{:S(2)}) copy-start(bf16[32,256,256]{2,1,0:T(8,128)(2,1)} %refs_6_.3) | copy-start | bytes 12582916
  1.8 6.2 %collective-permute-start = (bf16[64,1536]{1,0:T(8,128)(2,1)S(1)}, bf16[64,1536]{1,0:T(8,128)(2,1)S(1)}, u32[]{:S(2)}, u32[]{:S(2)}) collective-permute-start(bf16[64,1536]{1,0:T(8,128)(2,1)S(1)} %get-tuple-element.41), channel_id=1, source_target_pairs={{0,1},{1,0},{2,3},{3,2},{4,5},{5,4},{6,7},{7,6},{8,9},{9,8},{10,11... | collective-permute-start | bytes 589832 | tf_op jit(solution)/shard_map/ppermute | solution.py:306
  2.4 8.6 %collective-permute-start.1 = (bf16[64,1024]{1,0:T(8,128)(2,1)}, bf16[64,1024]{1,0:T(8,128)(2,1)S(1)}, u32[]{:S(2)}, u32[]{:S(2)}) collective-permute-start(bf16[64,1024]{1,0:T(8,128)(2,1)} %refs_4_.1), channel_id=1, source_target_pairs={{0,15},{1,2},{2,1},{3,4},{4,3},{5,6},{6,5},{7,8},{8,7},{9,10},{10,... | collective-permute-start | bytes 393224 | tf_op jit(solution)/shard_map/ppermute | solution.py:305
  8.0 5.0 %collective-permute-start.2 = (bf16[64,128]{1,0:T(8,128)(2,1)S(1)}, bf16[64,128]{1,0:T(8,128)(2,1)S(1)}, u32[]{:S(2)}, u32[]{:S(2)}) collective-permute-start(bf16[64,128]{1,0:T(8,128)(2,1)S(1)} %get-tuple-element.43.refs_7_), channel_id=1, source_target_pairs={{0,9},{1,11},{2,10},{3,8},{4,13},{5,15},{6,14},{7,12},{8,1},{9,3},... | collective-permute-start | bytes 49160 | tf_op jit(solution)/shard_map/ppermute | solution.py:318
  8.1 5.0 %collective-permute-start.3 = (bf16[64,128]{1,0:T(8,128)(2,1)S(1)}, bf16[64,128]{1,0:T(8,128)(2,1)S(1)}, u32[]{:S(2)}, u32[]{:S(2)}) collective-permute-start(bf16[64,128]{1,0:T(8,128)(2,1)S(1)} %get-tuple-element.44.refs_8_), channel_id=1, source_target_pairs={{0,8},{1,10},{2,11},{3,9},{4,12},{5,14},{6,15},{7,13},{8,0},{9,2},... | collective-permute-start | bytes 49160 | tf_op jit(solution)/shard_map/ppermute | solution.py:318
  13.6 3.7 %collective-permute-start.4 = (bf16[64,1536]{1,0:T(8,128)(2,1)S(1)}, bf16[64,1536]{1,0:T(8,128)(2,1)S(1)}, u32[]{:S(2)}, u32[]{:S(2)}) collective-permute-start(bf16[64,1536]{1,0:T(8,128)(2,1)S(1)} %get-tuple-element.51), channel_id=1, source_target_pairs={{0,1},{1,0},{2,3},{3,2},{4,5},{5,4},{6,7},{7,6},{8,9},{9,8},{10,11... | collective-permute-start | bytes 589832 | tf_op jit(solution)/shard_map/ppermute | solution.py:306
  13.8 7.1 %collective-permute-start.5 = (bf16[64,1024]{1,0:T(8,128)(2,1)S(1)}, bf16[64,1024]{1,0:T(8,128)(2,1)S(1)}, u32[]{:S(2)}, u32[]{:S(2)}) collective-permute-start(bf16[64,1024]{1,0:T(8,128)(2,1)S(1)} %get-tuple-element.50.refs_1_), channel_id=1, source_target_pairs={{0,15},{1,2},{2,1},{3,4},{4,3},{5,6},{6,5},{7,8},{8,7},{9,10},{10,... | collective-permute-start | bytes 393224 | tf_op jit(solution)/shard_map/ppermute | solution.py:305
  17.4 5.1 %collective-permute-start.6 = (bf16[64,128]{1,0:T(8,128)(2,1)S(1)}, bf16[64,128]{1,0:T(8,128)(2,1)S(1)}, u32[]{:S(2)}, u32[]{:S(2)}) collective-permute-start(bf16[64,128]{1,0:T(8,128)(2,1)S(1)} %get-tuple-element.53.refs_4_), channel_id=1, source_target_pairs={{0,9},{1,11},{2,10},{3,8},{4,13},{5,15},{6,14},{7,12},{8,1},{9,3},... | collective-permute-start | bytes 49160 | tf_op jit(solution)/shard_map/ppermute | solution.py:318
  17.4 5.0 %collective-permute-start.7 = (bf16[64,128]{1,0:T(8,128)(2,1)S(1)}, bf16[64,128]{1,0:T(8,128)(2,1)S(1)}, u32[]{:S(2)}, u32[]{:S(2)}) collective-permute-start(bf16[64,128]{1,0:T(8,128)(2,1)S(1)} %get-tuple-element.54.refs_5_), channel_id=1, source_target_pairs={{0,8},{1,10},{2,11},{3,9},{4,12},{5,14},{6,15},{7,13},{8,0},{9,2},... | collective-permute-start | bytes 49160 | tf_op jit(solution)/shard_map/ppermute | solution.py:318
  23.0 3.7 %collective-permute-start.8 = (bf16[64,1536]{1,0:T(8,128)(2,1)S(1)}, bf16[64,1536]{1,0:T(8,128)(2,1)S(1)}, u32[]{:S(2)}, u32[]{:S(2)}) collective-permute-start(bf16[64,1536]{1,0:T(8,128)(2,1)S(1)} %get-tuple-element.57), channel_id=1, source_target_pairs={{0,1},{1,0},{2,3},{3,2},{4,5},{5,4},{6,7},{7,6},{8,9},{9,8},{10,11... | collective-permute-start | bytes 589832 | tf_op jit(solution)/shard_map/ppermute | solution.py:306
  23.2 7.2 %collective-permute-start.9 = (bf16[64,1024]{1,0:T(8,128)(2,1)S(1)}, bf16[64,1024]{1,0:T(8,128)(2,1)S(1)}, u32[]{:S(2)}, u32[]{:S(2)}) collective-permute-start(bf16[64,1024]{1,0:T(8,128)(2,1)S(1)} %get-tuple-element.56.refs_1_), channel_id=1, source_target_pairs={{0,15},{1,2},{2,1},{3,4},{4,3},{5,6},{6,5},{7,8},{8,7},{9,10},{10,... | collective-permute-start | bytes 393224 | tf_op jit(solution)/shard_map/ppermute | solution.py:305
  26.8 5.2 %collective-permute-start.10 = (bf16[64,128]{1,0:T(8,128)(2,1)S(1)}, bf16[64,128]{1,0:T(8,128)(2,1)S(1)}, u32[]{:S(2)}, u32[]{:S(2)}) collective-permute-start(bf16[64,128]{1,0:T(8,128)(2,1)S(1)} %get-tuple-element.59.refs_4_), channel_id=1, source_target_pairs={{0,9},{1,11},{2,10},{3,8},{4,13},{5,15},{6,14},{7,12},{8,1},{9,3},... | collective-permute-start | bytes 49160 | tf_op jit(solution)/shard_map/ppermute | solution.py:318
  26.9 5.1 %collective-permute-start.11 = (bf16[64,128]{1,0:T(8,128)(2,1)S(1)}, bf16[64,128]{1,0:T(8,128)(2,1)S(1)}, u32[]{:S(2)}, u32[]{:S(2)}) collective-permute-start(bf16[64,128]{1,0:T(8,128)(2,1)S(1)} %get-tuple-element.60.refs_5_), channel_id=1, source_target_pairs={{0,8},{1,10},{2,11},{3,9},{4,12},{5,14},{6,15},{7,13},{8,0},{9,2},... | collective-permute-start | bytes 49160 | tf_op jit(solution)/shard_map/ppermute | solution.py:318
  32.6 3.5 %collective-permute-start.12 = (bf16[64,1536]{1,0:T(8,128)(2,1)S(1)}, bf16[64,1536]{1,0:T(8,128)(2,1)S(1)}, u32[]{:S(2)}, u32[]{:S(2)}) collective-permute-start(bf16[64,1536]{1,0:T(8,128)(2,1)S(1)} %get-tuple-element.64), channel_id=1, source_target_pairs={{0,1},{1,0},{2,3},{3,2},{4,5},{5,4},{6,7},{7,6},{8,9},{9,8},{10,11... | collective-permute-start | bytes 589832 | tf_op jit(solution)/shard_map/ppermute | solution.py:306
  32.8 7.2 %collective-permute-start.13 = (bf16[64,1024]{1,0:T(8,128)(2,1)S(1)}, bf16[64,1024]{1,0:T(8,128)(2,1)S(1)}, u32[]{:S(2)}, u32[]{:S(2)}) collective-permute-start(bf16[64,1024]{1,0:T(8,128)(2,1)S(1)} %get-tuple-element.63.refs_1_), channel_id=1, source_target_pairs={{0,15},{1,2},{2,1},{3,4},{4,3},{5,6},{6,5},{7,8},{8,7},{9,10},{10,... | collective-permute-start | bytes 393224 | tf_op jit(solution)/shard_map/ppermute | solution.py:305
  36.1 5.1 %collective-permute-start.14 = (bf16[64,128]{1,0:T(8,128)(2,1)S(1)}, bf16[64,128]{1,0:T(8,128)(2,1)S(1)}, u32[]{:S(2)}, u32[]{:S(2)}) collective-permute-start(bf16[64,128]{1,0:T(8,128)(2,1)S(1)} %get-tuple-element.66.refs_4_), channel_id=1, source_target_pairs={{0,9},{1,11},{2,10},{3,8},{4,13},{5,15},{6,14},{7,12},{8,1},{9,3},... | collective-permute-start | bytes 49160 | tf_op jit(solution)/shard_map/ppermute | solution.py:318
  36.2 5.0 %collective-permute-start.15 = (bf16[64,128]{1,0:T(8,128)(2,1)S(1)}, bf16[64,128]{1,0:T(8,128)(2,1)S(1)}, u32[]{:S(2)}, u32[]{:S(2)}) collective-permute-start(bf16[64,128]{1,0:T(8,128)(2,1)S(1)} %get-tuple-element.67.refs_5_), channel_id=1, source_target_pairs={{0,8},{1,10},{2,11},{3,9},{4,12},{5,14},{6,15},{7,13},{8,0},{9,2},... | collective-permute-start | bytes 49160 | tf_op jit(solution)/shard_map/ppermute | solution.py:318

commit v19 on v16

--- a/solution.py
+++ b/solution.py
@@ -57,7 +57,7 @@
                 (l * members + m, (l + self.hops[0]) % loop_size * members + (m ^ other))
                 for l, m in places
             ]
-            for other in (0, 2)
+            for other in (2, 0)
         ]
         self.routes = [
             [(l * members + m, (l + hop) % loop_size * members + (m + step) % members) for l, m in places]
@@ -98,8 +98,8 @@
         total = (keep_ref[...] + (upper + lower)).astype(BF16)
         second = self.member(index_ref) >= 2
         first, last = total[:, : self.width], total[:, self.width :]
-        out_refs[0][...] = jnp.where(second, last, first)
-        out_refs[1][...] = jnp.where(second, first, last)
+        out_refs[0][...] = jnp.where(second, first, last)
+        out_refs[1][...] = jnp.where(second, last, first)
 
     def far_sum(self, far_refs):
         return sum(ref[...].astype(F32) for ref in far_refs)

time: 43.8 us -> 43.3 us (0.989)
  waiting for transfers between devices: 9.9 us -> 9.37 us
    ppermute x8, starting transfers between devices: 8.72 us -> 6.5 us  [on_device(): fars = [lax.ppermute(s, axes, route) for s, route in zip(sends, routes)]]
    ppermute x4, starting transfers between devices: 11.9 us -> 14.1 us  [on_device(): over = lax.ppermute(block if product == 0 else current, axes, plan.over)]
    ppermute x8, waiting for transfers between devices: 5.64 us -> 5.1 us  [on_device(): fars = [lax.ppermute(s, axes, route) for s, route in zip(sends, routes)]]
  transfers between devices with their start and end apart: 16 -> 16, of which waited for: 9 -> 11; matrix products, arithmetic and copies ran while one was open for 0% -> 0% of each run, Pallas kernels for 18% -> 18%
where the time goes in v19:
time: 43.3 us; the launch traced here: 43.1 us
  starting transfers between devices  21.3 us (49%)
  Pallas kernels  12.3 us (28%)
  waiting for transfers between devices  9.37 us (22%)
    ppermute x4, starting transfers between devices, on_device(): over = lax.ppermute(block if product == 0 else current, axes, plan.over)  14.1 us
    pallas_call x17, Pallas kernels, call(): pl.pallas_call(kernel, in_specs=list(specs), out_specs=out_specs or [IN_V...  12.3 us
    ppermute x8, starting transfers between devices, on_device(): fars = [lax.ppermute(s, axes, route) for s, route in zip(sends, routes)]  6.5 us
    ppermute x8, waiting for transfers between devices, on_device(): fars = [lax.ppermute(s, axes, route) for s, route in zip(sends, routes)]  5.1 us
    ppermute x4, waiting for transfers between devices, on_device(): over = lax.ppermute(block if product == 0 else current, axes, plan.over)  4.26 us
  transfers between devices with their start and end apart: 16, of which 11 were waited for; matrix products, arithmetic and copies ran while one was open for 0% of the time, Pallas kernels for 18%

profile of v19, /device:TPU:0, one launch (start us, length us, event | category | flops | bytes accessed | tf_op | source)
XLA Modules:
  0.0 43.1 jit_solution(4190517998875831524)
XLA Ops:
  0.0 0.0 copy-start.1
  0.0 0.0 copy-start
  0.0 1.8 %prepare.1 = (bf16[64,1024]{1,0:T(8,128)(2,1)S(1)}, bf16[1,512,256]{2,1,0:T(8,128)(2,1)S(1)}, bf16[128,1024]{1,0:T(8,128)(2,1)S(1)}, s32[32]{0:T(128)S(4)}, s32[...) custom-call(s32[1]{0:T(128)} %bitcast.index_ref.refs_0_, s32[32]{0:T(128)} %refs_0_.1, s32[32]{0:T(128)} %refs_1_.1, ...), custom_call_target="tpu_custom_call" | custom-call | flops 1000000000 | bytes 4194304 | tf_op jit(solution)/shard_map/prepare/pallas_call | solution.py:241
  1.8 0.5 %collective-permute-start = (bf16[64,1536]{1,0:T(8,128)(2,1)S(1)}, bf16[64,1536]{1,0:T(8,128)(2,1)S(1)}, u32[]{:S(2)}, u32[]{:S(2)}) collective-permute-start(bf16[64,1536]{1,0:T(8,128)(2,1)S(1)} %get-tuple-element.41), channel_id=1, source_target_pairs={{0,1},{1,0},{2,3},{3,2},{4,5},{5,4},{6,7},{7,6},{8,9},{9,8},{10,11... | collective-permute-start | bytes 589832 | tf_op jit(solution)/shard_map/ppermute | solution.py:303
  2.4 5.6 %collective-permute-start.1 = (bf16[64,1024]{1,0:T(8,128)(2,1)}, bf16[64,1024]{1,0:T(8,128)(2,1)S(1)}, u32[]{:S(2)}, u32[]{:S(2)}) collective-permute-start(bf16[64,1024]{1,0:T(8,128)(2,1)} %refs_4_.1), channel_id=1, source_target_pairs={{0,15},{1,2},{2,1},{3,4},{4,3},{5,6},{6,5},{7,8},{8,7},{9,10},{10,... | collective-permute-start | bytes 393224 | tf_op jit(solution)/shard_map/ppermute | solution.py:302
  8.0 0.0 collective-permute-done.message_ref.refs_4_
  8.0 0.4 collective-permute-start.2
  8.4 0.3 collective-permute-start.3
  8.7 0.0 copy-done.1
  8.7 0.0 copy-done
  8.7 1.9 %first_own.1 = (f32[64,1024]{1,0:T(8,128)S(1)}, bf16[36,256,256]{2,1,0:T(8,128)(2,1)S(1)}, bf16[256,1024]{1,0:T(8,128)(2,1)S(1)}) custom-call(s32[1]{0:T(128)} %bitcast.index_ref.refs_0_, s32[32]{0:T(128)S(4)} %get-tuple-element.38.refs_1_, s32[32]{0:T(128)S(4)} %get-tuple-element.39.refs_2_, bf16[64,1024]{1,0:T(8,128)(2,1)S(1)} %get-tuple-element.40.refs_3_, ...), custom_call_target="tpu_custom_call" | custom-call | flops 1000000000 | bytes 4194304 | tf_op jit(solution)/shard_map/first_own/pallas_call | solution.py:241
  10.6 0.3 collective-permute-done.1.over_ref
  11.0 0.5 %halo.4.refs_1_ = f32[64,1024]{1,0:T(8,128)S(1)} custom-call(s32[1]{0:T(128)} %bitcast.index_ref.refs_0_, f32[64,1024]{1,0:T(8,128)S(1)} %get-tuple-element.45.acc_ref, bf16[64,1024]{1,0:T(8,128)(2,1)S(1)} %collective-permute-done.1.over_ref, bf16[36,256,256]{2,1,0:T(8,128)(2,1)S(1)} %get-tuple-element.46.d_ref.refs_3_), custom_call_target="tpu_custom_call" | custom-call | flops 1000000000 | bytes 4194304 | tf_op jit(solution)/shard_map/halo/pallas_call | solution.py:241
  11.5 2.1 %collective-permute-done.2.refs_5_ = bf16[64,128]{1,0:T(8,128)(2,1)S(1)} collective-permute-done((bf16[64,128]{1,0:T(8,128)(2,1)S(1)}, bf16[64,128]{1,0:T(8,128)(2,1)S(1)}, u32[]{:S(2)}, u32[]{:S(2)}) %collective-permute-start.2) | collective-permute-done | bytes 16416 | tf_op jit(solution)/shard_map/ppermute | solution.py:315
  13.6 0.0 collective-permute-done.3.refs_6_
  13.6 0.6 %finish.3 = (bf16[64,1024]{1,0:T(8,128)(2,1)S(1)}, bf16[64,1536]{1,0:T(8,128)(2,1)S(1)}, f32[64,256]{1,0:T(8,128)S(1)}) custom-call(s32[1]{0:T(128)} %bitcast.index_ref.refs_0_, f32[64,1024]{1,0:T(8,128)S(1)} %halo.4.refs_1_, bf16[256,1024]{1,0:T(8,128)(2,1)S(1)} %get-tuple-element.47.refs_2_.refs_1_, bf16[128,1024]{1,0:T(8,128)(2,1)S(1)} %get-tuple-element.48.refs_3_, ...), custom_call_target="tpu_custom_call" | custom-call | flops 1000000000 | bytes 4194304 | tf_op jit(solution)/shard_map/finish/pallas_call | solution.py:241
  14.2 0.1 collective-permute-start.4
  14.3 3.1 %collective-permute-start.5 = (bf16[64,1024]{1,0:T(8,128)(2,1)S(1)}, bf16[64,1024]{1,0:T(8,128)(2,1)S(1)}, u32[]{:S(2)}, u32[]{:S(2)}) collective-permute-start(bf16[64,1024]{1,0:T(8,128)(2,1)S(1)} %get-tuple-element.50.refs_1_), channel_id=1, source_target_pairs={{0,15},{1,2},{2,1},{3,4},{4,3},{5,6},{6,5},{7,8},{8,7},{9,10},{10,... | collective-permute-start | bytes 393224 | tf_op jit(solution)/shard_map/ppermute | solution.py:302
  17.4 0.0 collective-permute-done.4.message_ref.refs_2_
  17.4 1.4 %collective-permute-start.6 = (bf16[64,128]{1,0:T(8,128)(2,1)S(1)}, bf16[64,128]{1,0:T(8,128)(2,1)S(1)}, u32[]{:S(2)}, u32[]{:S(2)}) collective-permute-start(bf16[64,128]{1,0:T(8,128)(2,1)S(1)} %get-tuple-element.53.refs_4_), channel_id=1, source_target_pairs={{0,10},{1,11},{2,8},{3,9},{4,14},{5,15},{6,12},{7,13},{8,2},{9,3},... | collective-permute-start | bytes 49160 | tf_op jit(solution)/shard_map/ppermute | solution.py:315
  18.7 0.7 %collective-permute-start.7 = (bf16[64,128]{1,0:T(8,128)(2,1)S(1)}, bf16[64,128]{1,0:T(8,128)(2,1)S(1)}, u32[]{:S(2)}, u32[]{:S(2)}) collective-permute-start(bf16[64,128]{1,0:T(8,128)(2,1)S(1)} %get-tuple-element.54.refs_5_), channel_id=1, source_target_pairs={{0,8},{1,9},{2,10},{3,11},{4,12},{5,13},{6,14},{7,15},{8,0},{9,1},... | collective-permute-start | bytes 49160 | tf_op jit(solution)/shard_map/ppermute | solution.py:315
  19.5 1.3 %own.3 = (f32[64,1024]{1,0:T(8,128)S(1)}, bf16[4,64,1024]{2,1,0:T(8,128)(2,1)}) custom-call(s32[1]{0:T(128)} %bitcast.index_ref.refs_0_, bf16[64,1024]{1,0:T(8,128)(2,1)S(1)} %get-tuple-element.50.refs_1_, bf16[64,1536]{1,0:T(8,128)(2,1)S(1)} %collective-permute-done.4.message_ref.refs_2_, bf16[36,256,256]{2,1,0:T(8,128)(2,1)S(1)} %get-tuple-element.46.d_ref.refs_3_, ...), custom_call_target="tpu_custom_call" | custom-call | flops 1000000000 | bytes 4194304 | tf_op jit(solution)/shard_map/own/pallas_call | solution.py:241
  20.8 0.8 %collective-permute-done.5.over_ref = bf16[64,1024]{1,0:T(8,128)(2,1)S(1)} collective-permute-done((bf16[64,1024]{1,0:T(8,128)(2,1)S(1)}, bf16[64,1024]{1,0:T(8,128)(2,1)S(1)}, u32[]{:S(2)}, u32[]{:S(2)}) %collective-permute-start.5) | collective-permute-done | bytes 131104 | tf_op jit(solution)/shard_map/ppermute | solution.py:302
  21.6 0.5 %halo.5.refs_1_ = f32[64,1024]{1,0:T(8,128)S(1)} custom-call(s32[1]{0:T(128)} %bitcast.index_ref.refs_0_, f32[64,1024]{1,0:T(8,128)S(1)} %get-tuple-element.55.acc_ref, bf16[64,1024]{1,0:T(8,128)(2,1)S(1)} %collective-permute-done.5.over_ref, bf16[36,256,256]{2,1,0:T(8,128)(2,1)S(1)} %get-tuple-element.46.d_ref.refs_3_), custom_call_target="tpu_custom_call" | custom-call | flops 1000000000 | bytes 4194304 | tf_op jit(solution)/shard_map/halo/pallas_call | solution.py:241
  22.1 0.9 %collective-permute-done.6.refs_5_ = bf16[64,128]{1,0:T(8,128)(2,1)S(1)} collective-permute-done((bf16[64,128]{1,0:T(8,128)(2,1)S(1)}, bf16[64,128]{1,0:T(8,128)(2,1)S(1)}, u32[]{:S(2)}, u32[]{:S(2)}) %collective-permute-start.6) | collective-permute-done | bytes 16416 | tf_op jit(solution)/shard_map/ppermute | solution.py:315
  23.0 0.6 %collective-permute-done.7.refs_6_ = bf16[64,128]{1,0:T(8,128)(2,1)S(1)} collective-permute-done((bf16[64,128]{1,0:T(8,128)(2,1)S(1)}, bf16[64,128]{1,0:T(8,128)(2,1)S(1)}, u32[]{:S(2)}, u32[]{:S(2)}) %collective-permute-start.7) | collective-permute-done | bytes 16416 | tf_op jit(solution)/shard_map/ppermute | solution.py:315
  23.6 0.6 %finish.4 = (bf16[64,1024]{1,0:T(8,128)(2,1)S(1)}, bf16[64,1536]{1,0:T(8,128)(2,1)S(1)}, f32[64,256]{1,0:T(8,128)S(1)}) custom-call(s32[1]{0:T(128)} %bitcast.index_ref.refs_0_, f32[64,1024]{1,0:T(8,128)S(1)} %halo.5.refs_1_, bf16[256,1024]{1,0:T(8,128)(2,1)S(1)} %get-tuple-element.47.refs_2_.refs_1_, bf16[128,1024]{1,0:T(8,128)(2,1)S(1)} %get-tuple-element.48.refs_3_, ...), custom_call_target="tpu_custom_call" | custom-call | flops 1000000000 | bytes 4194304 | tf_op jit(solution)/shard_map/finish/pallas_call | solution.py:241
  24.1 0.1 collective-permute-start.8
  24.2 2.7 %collective-permute-start.9 = (bf16[64,1024]{1,0:T(8,128)(2,1)S(1)}, bf16[64,1024]{1,0:T(8,128)(2,1)S(1)}, u32[]{:S(2)}, u32[]{:S(2)}) collective-permute-start(bf16[64,1024]{1,0:T(8,128)(2,1)S(1)} %get-tuple-element.56.refs_1_), channel_id=1, source_target_pairs={{0,15},{1,2},{2,1},{3,4},{4,3},{5,6},{6,5},{7,8},{8,7},{9,10},{10,... | collective-permute-start | bytes 393224 | tf_op jit(solution)/shard_map/ppermute | solution.py:302
  26.9 0.0 collective-permute-done.8.message_ref.refs_2_
  26.9 1.2 %collective-permute-start.10 = (bf16[64,128]{1,0:T(8,128)(2,1)S(1)}, bf16[64,128]{1,0:T(8,128)(2,1)S(1)}, u32[]{:S(2)}, u32[]{:S(2)}) collective-permute-start(bf16[64,128]{1,0:T(8,128)(2,1)S(1)} %get-tuple-element.59.refs_4_), channel_id=1, source_target_pairs={{0,10},{1,11},{2,8},{3,9},{4,14},{5,15},{6,12},{7,13},{8,2},{9,3},... | collective-permute-start | bytes 49160 | tf_op jit(solution)/shard_map/ppermute | solution.py:315
  28.1 0.7 %collective-permute-start.11 = (bf16[64,128]{1,0:T(8,128)(2,1)S(1)}, bf16[64,128]{1,0:T(8,128)(2,1)S(1)}, u32[]{:S(2)}, u32[]{:S(2)}) collective-permute-start(bf16[64,128]{1,0:T(8,128)(2,1)S(1)} %get-tuple-element.60.refs_5_), channel_id=1, source_target_pairs={{0,8},{1,9},{2,10},{3,11},{4,12},{5,13},{6,14},{7,15},{8,0},{9,1},... | collective-permute-start | bytes 49160 | tf_op jit(solution)/shard_map/ppermute | solution.py:315
  28.8 1.3 %own.4 = (f32[64,1024]{1,0:T(8,128)S(1)}, bf16[4,64,1024]{2,1,0:T(8,128)(2,1)}) custom-call(s32[1]{0:T(128)} %bitcast.index_ref.refs_0_, bf16[64,1024]{1,0:T(8,128)(2,1)S(1)} %get-tuple-element.56.refs_1_, bf16[64,1536]{1,0:T(8,128)(2,1)S(1)} %collective-permute-done.8.message_ref.refs_2_, ...), custom_call_target="tpu_custom_call", output_to_operand_aliasing={{1}: (6, {})} | custom-call | flops 1000000000 | bytes 4194304 | tf_op jit(solution)/shard_map/own/pallas_call | solution.py:241
  30.1 1.6 %collective-permute-done.9.over_ref = bf16[64,1024]{1,0:T(8,128)(2,1)S(1)} collective-permute-done((bf16[64,1024]{1,0:T(8,128)(2,1)S(1)}, bf16[64,1024]{1,0:T(8,128)(2,1)S(1)}, u32[]{:S(2)}, u32[]{:S(2)}) %collective-permute-start.9) | collective-permute-done | bytes 131104 | tf_op jit(solution)/shard_map/ppermute | solution.py:302
  31.7 0.5 %halo.6.refs_1_ = f32[64,1024]{1,0:T(8,128)S(1)} custom-call(s32[1]{0:T(128)} %bitcast.index_ref.refs_0_, f32[64,1024]{1,0:T(8,128)S(1)} %get-tuple-element.62.acc_ref, bf16[64,1024]{1,0:T(8,128)(2,1)S(1)} %collective-permute-done.9.over_ref, bf16[36,256,256]{2,1,0:T(8,128)(2,1)S(1)} %get-tuple-element.46.d_ref.refs_3_), custom_call_target="tpu_custom_call" | custom-call | flops 1000000000 | bytes 4194304 | tf_op jit(solution)/shard_map/halo/pallas_call | solution.py:241
  32.2 0.3 collective-permute-done.10.refs_5_
  32.5 0.4 %collective-permute-done.11.refs_6_ = bf16[64,128]{1,0:T(8,128)(2,1)S(1)} collective-permute-done((bf16[64,128]{1,0:T(8,128)(2,1)S(1)}, bf16[64,128]{1,0:T(8,128)(2,1)S(1)}, u32[]{:S(2)}, u32[]{:S(2)}) %collective-permute-start.11) | collective-permute-done | bytes 16416 | tf_op jit(solution)/shard_map/ppermute | solution.py:315
  33.0 0.6 %finish.5 = (bf16[64,1024]{1,0:T(8,128)(2,1)S(1)}, bf16[64,1536]{1,0:T(8,128)(2,1)S(1)}, f32[64,256]{1,0:T(8,128)S(1)}) custom-call(s32[1]{0:T(128)} %bitcast.index_ref.refs_0_, f32[64,1024]{1,0:T(8,128)S(1)} %halo.6.refs_1_, bf16[256,1024]{1,0:T(8,128)(2,1)S(1)} %get-tuple-element.47.refs_2_.refs_1_, bf16[128,1024]{1,0:T(8,128)(2,1)S(1)} %get-tuple-element.48.refs_3_, ...), custom_call_target="tpu_custom_call" | custom-call | flops 1000000000 | bytes 4194304 | tf_op jit(solution)/shard_map/finish/pallas_call | solution.py:241
  33.5 0.1 collective-permute-start.12
  33.6 2.7 %collective-permute-start.13 = (bf16[64,1024]{1,0:T(8,128)(2,1)S(1)}, bf16[64,1024]{1,0:T(8,128)(2,1)S(1)}, u32[]{:S(2)}, u32[]{:S(2)}) collective-permute-start(bf16[64,1024]{1,0:T(8,128)(2,1)S(1)} %get-tuple-element.63.refs_1_), channel_id=1, source_target_pairs={{0,15},{1,2},{2,1},{3,4},{4,3},{5,6},{6,5},{7,8},{8,7},{9,10},{10,... | collective-permute-start | bytes 393224 | tf_op jit(solution)/shard_map/ppermute | solution.py:302
  36.4 0.0 collective-permute-done.12.message_ref.refs_2_
  36.4 1.2 %collective-permute-start.14 = (bf16[64,128]{1,0:T(8,128)(2,1)S(1)}, bf16[64,128]{1,0:T(8,128)(2,1)S(1)}, u32[]{:S(2)}, u32[]{:S(2)}) collective-permute-start(bf16[64,128]{1,0:T(8,128)(2,1)S(1)} %get-tuple-element.66.refs_4_), channel_id=1, source_target_pairs={{0,10},{1,11},{2,8},{3,9},{4,14},{5,15},{6,12},{7,13},{8,2},{9,3},... | collective-permute-start | bytes 49160 | tf_op jit(solution)/shard_map/ppermute | solution.py:315
  37.6 0.6 %collective-permute-start.15 = (bf16[64,128]{1,0:T(8,128)(2,1)S(1)}, bf16[64,128]{1,0:T(8,128)(2,1)S(1)}, u32[]{:S(2)}, u32[]{:S(2)}) collective-permute-start(bf16[64,128]{1,0:T(8,128)(2,1)S(1)} %get-tuple-element.67.refs_5_), channel_id=1, source_target_pairs={{0,8},{1,9},{2,10},{3,11},{4,12},{5,13},{6,14},{7,15},{8,0},{9,1},... | collective-permute-start | bytes 49160 | tf_op jit(solution)/shard_map/ppermute | solution.py:315
  38.2 1.3 %own.5 = (f32[64,1024]{1,0:T(8,128)S(1)}, bf16[4,64,1024]{2,1,0:T(8,128)(2,1)}) custom-call(s32[1]{0:T(128)} %bitcast.index_ref.refs_0_, bf16[64,1024]{1,0:T(8,128)(2,1)S(1)} %get-tuple-element.63.refs_1_, bf16[64,1536]{1,0:T(8,128)(2,1)S(1)} %collective-permute-done.12.message_ref.refs_2_, ...), custom_call_target="tpu_custom_call", output_to_operand_aliasing={{1}: (6, {})} | custom-call | flops 1000000000 | bytes 4194304 | tf_op jit(solution)/shard_map/own/pallas_call | solution.py:241
  39.5 1.6 %collective-permute-done.13.over_ref = bf16[64,1024]{1,0:T(8,128)(2,1)S(1)} collective-permute-done((bf16[64,1024]{1,0:T(8,128)(2,1)S(1)}, bf16[64,1024]{1,0:T(8,128)(2,1)S(1)}, u32[]{:S(2)}, u32[]{:S(2)}) %collective-permute-start.13) | collective-permute-done | bytes 131104 | tf_op jit(solution)/shard_map/ppermute | solution.py:302
  41.1 0.5 %halo.7.refs_0_ = f32[64,1024]{1,0:T(8,128)S(1)} custom-call(s32[1]{0:T(128)} %bitcast.index_ref.refs_0_, f32[64,1024]{1,0:T(8,128)S(1)} %get-tuple-element.69.acc_ref, bf16[64,1024]{1,0:T(8,128)(2,1)S(1)} %collective-permute-done.13.over_ref, bf16[36,256,256]{2,1,0:T(8,128)(2,1)S(1)} %get-tuple-element.46.d_ref.refs_3_), custom_call_target="tpu_custom_call" | custom-call | flops 1000000000 | bytes 4194304 | tf_op jit(solution)/shard_map/halo/pallas_call | solution.py:241
  41.6 0.4 collective-permute-done.14.refs_2_
  42.0 0.3 collective-permute-done.15.refs_3_
  42.3 0.9 %last.1 = bf16[4,64,1024]{2,1,0:T(8,128)(2,1)} custom-call(f32[64,1024]{1,0:T(8,128)S(1)} %halo.7.refs_0_, bf16[256,1024]{1,0:T(8,128)(2,1)S(1)} %get-tuple-element.47.refs_2_.refs_1_, bf16[64,128]{1,0:T(8,128)(2,1)S(1)} %collective-permute-done.14.refs_2_, bf16[64,128]{1,0:T(8,128)(2,1)S(1)} %collective-permute-done.15.refs_3_, ...), custom_call_target="tpu_custom_call", output_to_operand_aliasing={{}: (4, {})} | custom-call | flops 1000000000 | bytes 4194304 | tf_op jit(solution)/shard_map/last/pallas_call | solution.py:241
  (4 shorter events, 0.1 us)
Async XLA Ops:
  0.0 8.7 %copy-start.1 = (bf16[4,32,256]{2,1,0:T(8,128)(2,1)S(1)}, bf16[4,32,256]{2,1,0:T(8,128)(2,1)}, u32[]{:S(2)}) copy-start(bf16[4,32,256]{2,1,0:T(8,128)(2,1)} %refs_5_.3) | copy-start | bytes 196612
  0.0 8.7 %copy-start = (bf16[32,256,256]{2,1,0:T(8,128)(2,1)S(1)}, bf16[32,256,256]{2,1,0:T(8,128)(2,1)}, u32[]{:S(2)}) copy-start(bf16[32,256,256]{2,1,0:T(8,128)(2,1)} %refs_6_.3) | copy-start | bytes 12582916
  1.8 6.2 %collective-permute-start = (bf16[64,1536]{1,0:T(8,128)(2,1)S(1)}, bf16[64,1536]{1,0:T(8,128)(2,1)S(1)}, u32[]{:S(2)}, u32[]{:S(2)}) collective-permute-start(bf16[64,1536]{1,0:T(8,128)(2,1)S(1)} %get-tuple-element.41), channel_id=1, source_target_pairs={{0,1},{1,0},{2,3},{3,2},{4,5},{5,4},{6,7},{7,6},{8,9},{9,8},{10,11... | collective-permute-start | bytes 589832 | tf_op jit(solution)/shard_map/ppermute | solution.py:303
  2.4 8.6 %collective-permute-start.1 = (bf16[64,1024]{1,0:T(8,128)(2,1)}, bf16[64,1024]{1,0:T(8,128)(2,1)S(1)}, u32[]{:S(2)}, u32[]{:S(2)}) collective-permute-start(bf16[64,1024]{1,0:T(8,128)(2,1)} %refs_4_.1), channel_id=1, source_target_pairs={{0,15},{1,2},{2,1},{3,4},{4,3},{5,6},{6,5},{7,8},{8,7},{9,10},{10,... | collective-permute-start | bytes 393224 | tf_op jit(solution)/shard_map/ppermute | solution.py:302
  8.0 5.6 %collective-permute-start.2 = (bf16[64,128]{1,0:T(8,128)(2,1)S(1)}, bf16[64,128]{1,0:T(8,128)(2,1)S(1)}, u32[]{:S(2)}, u32[]{:S(2)}) collective-permute-start(bf16[64,128]{1,0:T(8,128)(2,1)S(1)} %get-tuple-element.43.refs_7_), channel_id=1, source_target_pairs={{0,10},{1,11},{2,8},{3,9},{4,14},{5,15},{6,12},{7,13},{8,2},{9,3},... | collective-permute-start | bytes 49160 | tf_op jit(solution)/shard_map/ppermute | solution.py:315
  8.4 5.2 %collective-permute-start.3 = (bf16[64,128]{1,0:T(8,128)(2,1)S(1)}, bf16[64,128]{1,0:T(8,128)(2,1)S(1)}, u32[]{:S(2)}, u32[]{:S(2)}) collective-permute-start(bf16[64,128]{1,0:T(8,128)(2,1)S(1)} %get-tuple-element.44.refs_8_), channel_id=1, source_target_pairs={{0,8},{1,9},{2,10},{3,11},{4,12},{5,13},{6,14},{7,15},{8,0},{9,1},... | collective-permute-start | bytes 49160 | tf_op jit(solution)/shard_map/ppermute | solution.py:315
  14.2 3.1 %collective-permute-start.4 = (bf16[64,1536]{1,0:T(8,128)(2,1)S(1)}, bf16[64,1536]{1,0:T(8,128)(2,1)S(1)}, u32[]{:S(2)}, u32[]{:S(2)}) collective-permute-start(bf16[64,1536]{1,0:T(8,128)(2,1)S(1)} %get-tuple-element.51), channel_id=1, source_target_pairs={{0,1},{1,0},{2,3},{3,2},{4,5},{5,4},{6,7},{7,6},{8,9},{9,8},{10,11... | collective-permute-start | bytes 589832 | tf_op jit(solution)/shard_map/ppermute | solution.py:303
  14.3 7.3 %collective-permute-start.5 = (bf16[64,1024]{1,0:T(8,128)(2,1)S(1)}, bf16[64,1024]{1,0:T(8,128)(2,1)S(1)}, u32[]{:S(2)}, u32[]{:S(2)}) collective-permute-start(bf16[64,1024]{1,0:T(8,128)(2,1)S(1)} %get-tuple-element.50.refs_1_), channel_id=1, source_target_pairs={{0,15},{1,2},{2,1},{3,4},{4,3},{5,6},{6,5},{7,8},{8,7},{9,10},{10,... | collective-permute-start | bytes 393224 | tf_op jit(solution)/shard_map/ppermute | solution.py:302
  17.4 5.6 %collective-permute-start.6 = (bf16[64,128]{1,0:T(8,128)(2,1)S(1)}, bf16[64,128]{1,0:T(8,128)(2,1)S(1)}, u32[]{:S(2)}, u32[]{:S(2)}) collective-permute-start(bf16[64,128]{1,0:T(8,128)(2,1)S(1)} %get-tuple-element.53.refs_4_), channel_id=1, source_target_pairs={{0,10},{1,11},{2,8},{3,9},{4,14},{5,15},{6,12},{7,13},{8,2},{9,3},... | collective-permute-start | bytes 49160 | tf_op jit(solution)/shard_map/ppermute | solution.py:315
  18.7 4.8 %collective-permute-start.7 = (bf16[64,128]{1,0:T(8,128)(2,1)S(1)}, bf16[64,128]{1,0:T(8,128)(2,1)S(1)}, u32[]{:S(2)}, u32[]{:S(2)}) collective-permute-start(bf16[64,128]{1,0:T(8,128)(2,1)S(1)} %get-tuple-element.54.refs_5_), channel_id=1, source_target_pairs={{0,8},{1,9},{2,10},{3,11},{4,12},{5,13},{6,14},{7,15},{8,0},{9,1},... | collective-permute-start | bytes 49160 | tf_op jit(solution)/shard_map/ppermute | solution.py:315
  24.1 2.7 %collective-permute-start.8 = (bf16[64,1536]{1,0:T(8,128)(2,1)S(1)}, bf16[64,1536]{1,0:T(8,128)(2,1)S(1)}, u32[]{:S(2)}, u32[]{:S(2)}) collective-permute-start(bf16[64,1536]{1,0:T(8,128)(2,1)S(1)} %get-tuple-element.57), channel_id=1, source_target_pairs={{0,1},{1,0},{2,3},{3,2},{4,5},{5,4},{6,7},{7,6},{8,9},{9,8},{10,11... | collective-permute-start | bytes 589832 | tf_op jit(solution)/shard_map/ppermute | solution.py:303
  24.2 7.4 %collective-permute-start.9 = (bf16[64,1024]{1,0:T(8,128)(2,1)S(1)}, bf16[64,1024]{1,0:T(8,128)(2,1)S(1)}, u32[]{:S(2)}, u32[]{:S(2)}) collective-permute-start(bf16[64,1024]{1,0:T(8,128)(2,1)S(1)} %get-tuple-element.56.refs_1_), channel_id=1, source_target_pairs={{0,15},{1,2},{2,1},{3,4},{4,3},{5,6},{6,5},{7,8},{8,7},{9,10},{10,... | collective-permute-start | bytes 393224 | tf_op jit(solution)/shard_map/ppermute | solution.py:302
  26.9 5.6 %collective-permute-start.10 = (bf16[64,128]{1,0:T(8,128)(2,1)S(1)}, bf16[64,128]{1,0:T(8,128)(2,1)S(1)}, u32[]{:S(2)}, u32[]{:S(2)}) collective-permute-start(bf16[64,128]{1,0:T(8,128)(2,1)S(1)} %get-tuple-element.59.refs_4_), channel_id=1, source_target_pairs={{0,10},{1,11},{2,8},{3,9},{4,14},{5,15},{6,12},{7,13},{8,2},{9,3},... | collective-permute-start | bytes 49160 | tf_op jit(solution)/shard_map/ppermute | solution.py:315
  28.1 4.9 %collective-permute-start.11 = (bf16[64,128]{1,0:T(8,128)(2,1)S(1)}, bf16[64,128]{1,0:T(8,128)(2,1)S(1)}, u32[]{:S(2)}, u32[]{:S(2)}) collective-permute-start(bf16[64,128]{1,0:T(8,128)(2,1)S(1)} %get-tuple-element.60.refs_5_), channel_id=1, source_target_pairs={{0,8},{1,9},{2,10},{3,11},{4,12},{5,13},{6,14},{7,15},{8,0},{9,1},... | collective-permute-start | bytes 49160 | tf_op jit(solution)/shard_map/ppermute | solution.py:315
  33.5 2.8 %collective-permute-start.12 = (bf16[64,1536]{1,0:T(8,128)(2,1)S(1)}, bf16[64,1536]{1,0:T(8,128)(2,1)S(1)}, u32[]{:S(2)}, u32[]{:S(2)}) collective-permute-start(bf16[64,1536]{1,0:T(8,128)(2,1)S(1)} %get-tuple-element.64), channel_id=1, source_target_pairs={{0,1},{1,0},{2,3},{3,2},{4,5},{5,4},{6,7},{7,6},{8,9},{9,8},{10,11... | collective-permute-start | bytes 589832 | tf_op jit(solution)/shard_map/ppermute | solution.py:303
  33.6 7.4 %collective-permute-start.13 = (bf16[64,1024]{1,0:T(8,128)(2,1)S(1)}, bf16[64,1024]{1,0:T(8,128)(2,1)S(1)}, u32[]{:S(2)}, u32[]{:S(2)}) collective-permute-start(bf16[64,1024]{1,0:T(8,128)(2,1)S(1)} %get-tuple-element.63.refs_1_), channel_id=1, source_target_pairs={{0,15},{1,2},{2,1},{3,4},{4,3},{5,6},{6,5},{7,8},{8,7},{9,10},{10,... | collective-permute-start | bytes 393224 | tf_op jit(solution)/shard_map/ppermute | solution.py:302
  36.4 5.6 %collective-permute-start.14 = (bf16[64,128]{1,0:T(8,128)(2,1)S(1)}, bf16[64,128]{1,0:T(8,128)(2,1)S(1)}, u32[]{:S(2)}, u32[]{:S(2)}) collective-permute-start(bf16[64,128]{1,0:T(8,128)(2,1)S(1)} %get-tuple-element.66.refs_4_), channel_id=1, source_target_pairs={{0,10},{1,11},{2,8},{3,9},{4,14},{5,15},{6,12},{7,13},{8,2},{9,3},... | collective-permute-start | bytes 49160 | tf_op jit(solution)/shard_map/ppermute | solution.py:315
  37.6 4.6 %collective-permute-start.15 = (bf16[64,128]{1,0:T(8,128)(2,1)S(1)}, bf16[64,128]{1,0:T(8,128)(2,1)S(1)}, u32[]{:S(2)}, u32[]{:S(2)}) collective-permute-start(bf16[64,128]{1,0:T(8,128)(2,1)S(1)} %get-tuple-element.67.refs_5_), channel_id=1, source_target_pairs={{0,8},{1,9},{2,10},{3,11},{4,12},{5,13},{6,14},{7,15},{8,0},{9,1},... | collective-permute-start | bytes 49160 | tf_op jit(solution)/shard_map/ppermute | solution.py:315

commit v20 on v15

--- a/solution.py
+++ b/solution.py
@@ -11,6 +11,7 @@
 REACH = 4
 LEVELS = 3
 SPAN = 2 * REACH + 1
+OTHER_CORE_FIRST = 0b11011111
 
 F32 = jnp.float32
 BF16 = jnp.bfloat16
@@ -54,16 +55,31 @@
         places = [(l, m) for l in range(loop_size) for m in range(members)]
         self.across = [
             [
-                (l * members + m, (l + self.hops[0]) % loop_size * members + (m ^ (m % 2 * 2) ^ other))
+                (l * members + m, self.far_target(l, m)[turn])
                 for l, m in places
             ]
-            for other in (1, 0)
+            for turn in range(2)
         ]
         self.routes = [
             [(l * members + m, (l + hop) % loop_size * members + (m + step) % members) for l, m in places]
             for hop in self.hops
             for step in range(members)
         ]
+
+    def far_target(self, loop_index, member):
+        block = (loop_index + self.hops[0]) % self.loop_size
+        pair, core = divmod(member, 2)
+        chip = block * 2 + (pair ^ core)
+        first = core ^ (OTHER_CORE_FIRST >> chip & 1)
+        return 2 * chip + first, 2 * chip + (first ^ 1)
+
+    def first_is_odd(self, index_ref):
+        index = index_ref[0]
+        block = lax.rem(lax.div(index, self.members) + self.hops[0], self.loop_size)
+        pair, core = lax.div(self.member(index_ref), 2), lax.rem(index, 2)
+        chip = block * 2 + lax.bitwise_xor(pair, core)
+        swapped = lax.bitwise_and(lax.shift_right_logical(jnp.int32(OTHER_CORE_FIRST), chip), 1)
+        return lax.bitwise_xor(core, swapped) == 1
 
     def panel(self, ref, c):
         return ref[:, c * self.size : (c + 1) * self.size]
@@ -95,10 +111,10 @@
         upper = message_ref[:, self.shard_len : self.shard_len + 2 * self.width].astype(F32)
         lower = message_ref[:, self.shard_len + 2 * self.width :].astype(F32)
         total = (keep_ref[...] + (upper + lower)).astype(BF16)
-        second = lax.rem(index_ref[0], 2) == 1
+        odd = self.first_is_odd(index_ref)
         first, last = total[:, : self.width], total[:, self.width :]
-        out_refs[0][...] = jnp.where(second, first, last)
-        out_refs[1][...] = jnp.where(second, last, first)
+        out_refs[0][...] = jnp.where(odd, last, first)
+        out_refs[1][...] = jnp.where(odd, first, last)
 
     def far_sum(self, far_refs):
         return sum(ref[...].astype(F32) for ref in far_refs)

time: 41.7 us -> 41.9 us (level)
  waiting for transfers between devices: 8.49 us -> 9.83 us
  starting transfers between devices: 20.5 us -> 19.5 us
    ppermute x4, starting transfers between devices: 12.8 us -> 15.2 us  [on_device(): over = lax.ppermute(block if product == 0 else current, axes, plan.over)]
    ppermute x8, starting transfers between devices: 5.02 us -> 2.71 us  [on_device(): fars = [lax.ppermute(s, axes, route) for s, route in zip(sends, routes)]]
    ppermute x8, waiting for transfers between devices: 1.67 us -> 2.98 us  [on_device(): fars = [lax.ppermute(s, axes, route) for s, route in zip(sends, routes)]]
    ppermute x4, starting transfers between devices: 2.69 us -> 1.57 us  [on_device(): near = lax.ppermute(sends[0] if plan.paired else current, axes, plan.near)]
  transfers between devices with their start and end apart: 16 -> 16, of which waited for: 5 -> 8; matrix products, arithmetic and copies ran while one was open for 0% -> 0% of each run, Pallas kernels for 19% -> 19%
where the time goes in v20:
time: 41.9 us; the launch traced here: 41.8 us
  starting transfers between devices  19.5 us (47%)
  Pallas kernels  12.3 us (29%)
  waiting for transfers between devices  9.83 us (23%)
    ppermute x4, starting transfers between devices, on_device(): over = lax.ppermute(block if product == 0 else current, axes, plan.over)  15.2 us
    pallas_call x17, Pallas kernels, call(): pl.pallas_call(kernel, in_specs=list(specs), out_specs=out_specs or [IN_V...  12.3 us
    ppermute x4, waiting for transfers between devices, on_device(): over = lax.ppermute(block if product == 0 else current, axes, plan.over)  6.84 us
    ppermute x8, waiting for transfers between devices, on_device(): fars = [lax.ppermute(s, axes, route) for s, route in zip(sends, routes)]  2.98 us
    ppermute x8, starting transfers between devices, on_device(): fars = [lax.ppermute(s, axes, route) for s, route in zip(sends, routes)]  2.71 us
    ppermute x4, starting transfers between devices, on_device(): near = lax.ppermute(sends[0] if plan.paired else current, axes, plan.near)  1.57 us
  transfers between devices with their start and end apart: 16, of which 8 were waited for; matrix products, arithmetic and copies ran while one was open for 0% of the time, Pallas kernels for 19%

profile of v20, /device:TPU:0, one launch (start us, length us, event | category | flops | bytes accessed | tf_op | source)
XLA Modules:
  0.0 41.8 jit_solution(5637741618438846218)
XLA Ops:
  0.0 0.0 copy-start.1
  0.0 0.0 copy-start
  0.0 1.8 %prepare.1 = (bf16[64,1024]{1,0:T(8,128)(2,1)S(1)}, bf16[1,512,256]{2,1,0:T(8,128)(2,1)S(1)}, bf16[128,1024]{1,0:T(8,128)(2,1)S(1)}, s32[32]{0:T(128)S(4)}, s32[...) custom-call(s32[1]{0:T(128)} %bitcast.index_ref.refs_0_, s32[32]{0:T(128)} %refs_0_.1, s32[32]{0:T(128)} %refs_1_.1, ...), custom_call_target="tpu_custom_call" | custom-call | flops 1000000000 | bytes 4194304 | tf_op jit(solution)/shard_map/prepare/pallas_call | solution.py:256
  1.8 0.5 %collective-permute-start = (bf16[64,1536]{1,0:T(8,128)(2,1)S(1)}, bf16[64,1536]{1,0:T(8,128)(2,1)S(1)}, u32[]{:S(2)}, u32[]{:S(2)}) collective-permute-start(bf16[64,1536]{1,0:T(8,128)(2,1)S(1)} %get-tuple-element.41), channel_id=1, source_target_pairs={{0,1},{1,0},{2,3},{3,2},{4,5},{5,4},{6,7},{7,6},{8,9},{9,8},{10,11... | collective-permute-start | bytes 589832 | tf_op jit(solution)/shard_map/ppermute | solution.py:318
  2.4 5.6 %collective-permute-start.1 = (bf16[64,1024]{1,0:T(8,128)(2,1)}, bf16[64,1024]{1,0:T(8,128)(2,1)S(1)}, u32[]{:S(2)}, u32[]{:S(2)}) collective-permute-start(bf16[64,1024]{1,0:T(8,128)(2,1)} %refs_4_.1), channel_id=1, source_target_pairs={{0,15},{1,2},{2,1},{3,4},{4,3},{5,6},{6,5},{7,8},{8,7},{9,10},{10,... | collective-permute-start | bytes 393224 | tf_op jit(solution)/shard_map/ppermute | solution.py:317
  8.0 0.0 collective-permute-done.message_ref.refs_4_
  8.0 0.1 collective-permute-start.2
  8.1 0.1 collective-permute-start.3
  8.2 0.0 copy-done.1
  8.2 0.0 copy-done
  8.2 1.9 %first_own.1 = (f32[64,1024]{1,0:T(8,128)S(1)}, bf16[36,256,256]{2,1,0:T(8,128)(2,1)S(1)}, bf16[256,1024]{1,0:T(8,128)(2,1)S(1)}) custom-call(s32[1]{0:T(128)} %bitcast.index_ref.refs_0_, s32[32]{0:T(128)S(4)} %get-tuple-element.38.refs_1_, s32[32]{0:T(128)S(4)} %get-tuple-element.39.refs_2_, bf16[64,1024]{1,0:T(8,128)(2,1)S(1)} %get-tuple-element.40.refs_3_, ...), custom_call_target="tpu_custom_call" | custom-call | flops 1000000000 | bytes 4194304 | tf_op jit(solution)/shard_map/first_own/pallas_call | solution.py:256
  10.1 0.9 %collective-permute-done.1.over_ref = bf16[64,1024]{1,0:T(8,128)(2,1)S(1)} collective-permute-done((bf16[64,1024]{1,0:T(8,128)(2,1)}, bf16[64,1024]{1,0:T(8,128)(2,1)S(1)}, u32[]{:S(2)}, u32[]{:S(2)}) %collective-permute-start.1) | collective-permute-done | bytes 131104 | tf_op jit(solution)/shard_map/ppermute | solution.py:317
  10.9 0.5 %halo.4.refs_1_ = f32[64,1024]{1,0:T(8,128)S(1)} custom-call(s32[1]{0:T(128)} %bitcast.index_ref.refs_0_, f32[64,1024]{1,0:T(8,128)S(1)} %get-tuple-element.45.acc_ref, bf16[64,1024]{1,0:T(8,128)(2,1)S(1)} %collective-permute-done.1.over_ref, bf16[36,256,256]{2,1,0:T(8,128)(2,1)S(1)} %get-tuple-element.46.d_ref.refs_3_), custom_call_target="tpu_custom_call" | custom-call | flops 1000000000 | bytes 4194304 | tf_op jit(solution)/shard_map/halo/pallas_call | solution.py:256
  11.5 1.8 %collective-permute-done.2.refs_5_ = bf16[64,128]{1,0:T(8,128)(2,1)S(1)} collective-permute-done((bf16[64,128]{1,0:T(8,128)(2,1)S(1)}, bf16[64,128]{1,0:T(8,128)(2,1)S(1)}, u32[]{:S(2)}, u32[]{:S(2)}) %collective-permute-start.2) | collective-permute-done | bytes 16416 | tf_op jit(solution)/shard_map/ppermute | solution.py:330
  13.2 0.0 collective-permute-done.3.refs_6_
  13.2 0.6 %finish.3 = (bf16[64,1024]{1,0:T(8,128)(2,1)S(1)}, bf16[64,1536]{1,0:T(8,128)(2,1)S(1)}, f32[64,256]{1,0:T(8,128)S(1)}) custom-call(s32[1]{0:T(128)} %bitcast.index_ref.refs_0_, f32[64,1024]{1,0:T(8,128)S(1)} %halo.4.refs_1_, bf16[256,1024]{1,0:T(8,128)(2,1)S(1)} %get-tuple-element.47.refs_2_.refs_1_, bf16[128,1024]{1,0:T(8,128)(2,1)S(1)} %get-tuple-element.48.refs_3_, ...), custom_call_target="tpu_custom_call" | custom-call | flops 1000000000 | bytes 4194304 | tf_op jit(solution)/shard_map/finish/pallas_call | solution.py:256
  13.8 0.2 collective-permute-start.4
  14.0 3.2 %collective-permute-start.5 = (bf16[64,1024]{1,0:T(8,128)(2,1)S(1)}, bf16[64,1024]{1,0:T(8,128)(2,1)S(1)}, u32[]{:S(2)}, u32[]{:S(2)}) collective-permute-start(bf16[64,1024]{1,0:T(8,128)(2,1)S(1)} %get-tuple-element.50.refs_1_), channel_id=1, source_target_pairs={{0,15},{1,2},{2,1},{3,4},{4,3},{5,6},{6,5},{7,8},{8,7},{9,10},{10,... | collective-permute-start | bytes 393224 | tf_op jit(solution)/shard_map/ppermute | solution.py:317
  17.2 0.0 collective-permute-done.4.message_ref.refs_2_
  17.2 0.1 collective-permute-start.6
  17.3 0.8 %collective-permute-start.7 = (bf16[64,128]{1,0:T(8,128)(2,1)S(1)}, bf16[64,128]{1,0:T(8,128)(2,1)S(1)}, u32[]{:S(2)}, u32[]{:S(2)}) collective-permute-start(bf16[64,128]{1,0:T(8,128)(2,1)S(1)} %get-tuple-element.54.refs_5_), channel_id=1, source_target_pairs={{0,8},{1,10},{2,11},{3,9},{4,12},{5,15},{6,14},{7,13},{8,0},{9,3},... | collective-permute-start | bytes 49160 | tf_op jit(solution)/shard_map/ppermute | solution.py:330
  18.1 1.3 %own.3 = (f32[64,1024]{1,0:T(8,128)S(1)}, bf16[4,64,1024]{2,1,0:T(8,128)(2,1)}) custom-call(s32[1]{0:T(128)} %bitcast.index_ref.refs_0_, bf16[64,1024]{1,0:T(8,128)(2,1)S(1)} %get-tuple-element.50.refs_1_, bf16[64,1536]{1,0:T(8,128)(2,1)S(1)} %collective-permute-done.4.message_ref.refs_2_, bf16[36,256,256]{2,1,0:T(8,128)(2,1)S(1)} %get-tuple-element.46.d_ref.refs_3_, ...), custom_call_target="tpu_custom_call" | custom-call | flops 1000000000 | bytes 4194304 | tf_op jit(solution)/shard_map/own/pallas_call | solution.py:256
  19.4 1.9 %collective-permute-done.5.over_ref = bf16[64,1024]{1,0:T(8,128)(2,1)S(1)} collective-permute-done((bf16[64,1024]{1,0:T(8,128)(2,1)S(1)}, bf16[64,1024]{1,0:T(8,128)(2,1)S(1)}, u32[]{:S(2)}, u32[]{:S(2)}) %collective-permute-start.5) | collective-permute-done | bytes 131104 | tf_op jit(solution)/shard_map/ppermute | solution.py:317
  21.3 0.5 %halo.5.refs_1_ = f32[64,1024]{1,0:T(8,128)S(1)} custom-call(s32[1]{0:T(128)} %bitcast.index_ref.refs_0_, f32[64,1024]{1,0:T(8,128)S(1)} %get-tuple-element.55.acc_ref, bf16[64,1024]{1,0:T(8,128)(2,1)S(1)} %collective-permute-done.5.over_ref, bf16[36,256,256]{2,1,0:T(8,128)(2,1)S(1)} %get-tuple-element.46.d_ref.refs_3_), custom_call_target="tpu_custom_call" | custom-call | flops 1000000000 | bytes 4194304 | tf_op jit(solution)/shard_map/halo/pallas_call | solution.py:256
  21.8 0.4 %collective-permute-done.6.refs_5_ = bf16[64,128]{1,0:T(8,128)(2,1)S(1)} collective-permute-done((bf16[64,128]{1,0:T(8,128)(2,1)S(1)}, bf16[64,128]{1,0:T(8,128)(2,1)S(1)}, u32[]{:S(2)}, u32[]{:S(2)}) %collective-permute-start.6) | collective-permute-done | bytes 16416 | tf_op jit(solution)/shard_map/ppermute | solution.py:330
  22.3 0.0 collective-permute-done.7.refs_6_
  22.3 0.6 %finish.4 = (bf16[64,1024]{1,0:T(8,128)(2,1)S(1)}, bf16[64,1536]{1,0:T(8,128)(2,1)S(1)}, f32[64,256]{1,0:T(8,128)S(1)}) custom-call(s32[1]{0:T(128)} %bitcast.index_ref.refs_0_, f32[64,1024]{1,0:T(8,128)S(1)} %halo.5.refs_1_, bf16[256,1024]{1,0:T(8,128)(2,1)S(1)} %get-tuple-element.47.refs_2_.refs_1_, bf16[128,1024]{1,0:T(8,128)(2,1)S(1)} %get-tuple-element.48.refs_3_, ...), custom_call_target="tpu_custom_call" | custom-call | flops 1000000000 | bytes 4194304 | tf_op jit(solution)/shard_map/finish/pallas_call | solution.py:256
  22.9 0.3 collective-permute-start.8
  23.2 3.0 %collective-permute-start.9 = (bf16[64,1024]{1,0:T(8,128)(2,1)S(1)}, bf16[64,1024]{1,0:T(8,128)(2,1)S(1)}, u32[]{:S(2)}, u32[]{:S(2)}) collective-permute-start(bf16[64,1024]{1,0:T(8,128)(2,1)S(1)} %get-tuple-element.56.refs_1_), channel_id=1, source_target_pairs={{0,15},{1,2},{2,1},{3,4},{4,3},{5,6},{6,5},{7,8},{8,7},{9,10},{10,... | collective-permute-start | bytes 393224 | tf_op jit(solution)/shard_map/ppermute | solution.py:317
  26.2 0.0 collective-permute-done.8.message_ref.refs_2_
  26.2 0.1 collective-permute-start.10
  26.3 0.9 %collective-permute-start.11 = (bf16[64,128]{1,0:T(8,128)(2,1)S(1)}, bf16[64,128]{1,0:T(8,128)(2,1)S(1)}, u32[]{:S(2)}, u32[]{:S(2)}) collective-permute-start(bf16[64,128]{1,0:T(8,128)(2,1)S(1)} %get-tuple-element.60.refs_5_), channel_id=1, source_target_pairs={{0,8},{1,10},{2,11},{3,9},{4,12},{5,15},{6,14},{7,13},{8,0},{9,3},... | collective-permute-start | bytes 49160 | tf_op jit(solution)/shard_map/ppermute | solution.py:330
  27.2 1.3 %own.4 = (f32[64,1024]{1,0:T(8,128)S(1)}, bf16[4,64,1024]{2,1,0:T(8,128)(2,1)}) custom-call(s32[1]{0:T(128)} %bitcast.index_ref.refs_0_, bf16[64,1024]{1,0:T(8,128)(2,1)S(1)} %get-tuple-element.56.refs_1_, bf16[64,1536]{1,0:T(8,128)(2,1)S(1)} %collective-permute-done.8.message_ref.refs_2_, ...), custom_call_target="tpu_custom_call", output_to_operand_aliasing={{1}: (6, {})} | custom-call | flops 1000000000 | bytes 4194304 | tf_op jit(solution)/shard_map/own/pallas_call | solution.py:256
  28.5 2.0 %collective-permute-done.9.over_ref = bf16[64,1024]{1,0:T(8,128)(2,1)S(1)} collective-permute-done((bf16[64,1024]{1,0:T(8,128)(2,1)S(1)}, bf16[64,1024]{1,0:T(8,128)(2,1)S(1)}, u32[]{:S(2)}, u32[]{:S(2)}) %collective-permute-start.9) | collective-permute-done | bytes 131104 | tf_op jit(solution)/shard_map/ppermute | solution.py:317
  30.5 0.5 %halo.6.refs_1_ = f32[64,1024]{1,0:T(8,128)S(1)} custom-call(s32[1]{0:T(128)} %bitcast.index_ref.refs_0_, f32[64,1024]{1,0:T(8,128)S(1)} %get-tuple-element.62.acc_ref, bf16[64,1024]{1,0:T(8,128)(2,1)S(1)} %collective-permute-done.9.over_ref, bf16[36,256,256]{2,1,0:T(8,128)(2,1)S(1)} %get-tuple-element.46.d_ref.refs_3_), custom_call_target="tpu_custom_call" | custom-call | flops 1000000000 | bytes 4194304 | tf_op jit(solution)/shard_map/halo/pallas_call | solution.py:256
  31.1 0.2 collective-permute-done.10.refs_5_
  31.2 0.0 collective-permute-done.11.refs_6_
  31.2 0.6 %finish.5 = (bf16[64,1024]{1,0:T(8,128)(2,1)S(1)}, bf16[64,1536]{1,0:T(8,128)(2,1)S(1)}, f32[64,256]{1,0:T(8,128)S(1)}) custom-call(s32[1]{0:T(128)} %bitcast.index_ref.refs_0_, f32[64,1024]{1,0:T(8,128)S(1)} %halo.6.refs_1_, bf16[256,1024]{1,0:T(8,128)(2,1)S(1)} %get-tuple-element.47.refs_2_.refs_1_, bf16[128,1024]{1,0:T(8,128)(2,1)S(1)} %get-tuple-element.48.refs_3_, ...), custom_call_target="tpu_custom_call" | custom-call | flops 1000000000 | bytes 4194304 | tf_op jit(solution)/shard_map/finish/pallas_call | solution.py:256
  31.8 0.6 %collective-permute-start.12 = (bf16[64,1536]{1,0:T(8,128)(2,1)S(1)}, bf16[64,1536]{1,0:T(8,128)(2,1)S(1)}, u32[]{:S(2)}, u32[]{:S(2)}) collective-permute-start(bf16[64,1536]{1,0:T(8,128)(2,1)S(1)} %get-tuple-element.64), channel_id=1, source_target_pairs={{0,1},{1,0},{2,3},{3,2},{4,5},{5,4},{6,7},{7,6},{8,9},{9,8},{10,11... | collective-permute-start | bytes 589832 | tf_op jit(solution)/shard_map/ppermute | solution.py:318
  32.4 3.3 %collective-permute-start.13 = (bf16[64,1024]{1,0:T(8,128)(2,1)S(1)}, bf16[64,1024]{1,0:T(8,128)(2,1)S(1)}, u32[]{:S(2)}, u32[]{:S(2)}) collective-permute-start(bf16[64,1024]{1,0:T(8,128)(2,1)S(1)} %get-tuple-element.63.refs_1_), channel_id=1, source_target_pairs={{0,15},{1,2},{2,1},{3,4},{4,3},{5,6},{6,5},{7,8},{8,7},{9,10},{10,... | collective-permute-start | bytes 393224 | tf_op jit(solution)/shard_map/ppermute | solution.py:317
  35.7 0.0 collective-permute-done.12.message_ref.refs_2_
  35.7 0.1 collective-permute-start.14
  35.8 0.7 %collective-permute-start.15 = (bf16[64,128]{1,0:T(8,128)(2,1)S(1)}, bf16[64,128]{1,0:T(8,128)(2,1)S(1)}, u32[]{:S(2)}, u32[]{:S(2)}) collective-permute-start(bf16[64,128]{1,0:T(8,128)(2,1)S(1)} %get-tuple-element.67.refs_5_), channel_id=1, source_target_pairs={{0,8},{1,10},{2,11},{3,9},{4,12},{5,15},{6,14},{7,13},{8,0},{9,3},... | collective-permute-start | bytes 49160 | tf_op jit(solution)/shard_map/ppermute | solution.py:330
  36.5 1.3 %own.5 = (f32[64,1024]{1,0:T(8,128)S(1)}, bf16[4,64,1024]{2,1,0:T(8,128)(2,1)}) custom-call(s32[1]{0:T(128)} %bitcast.index_ref.refs_0_, bf16[64,1024]{1,0:T(8,128)(2,1)S(1)} %get-tuple-element.63.refs_1_, bf16[64,1536]{1,0:T(8,128)(2,1)S(1)} %collective-permute-done.12.message_ref.refs_2_, ...), custom_call_target="tpu_custom_call", output_to_operand_aliasing={{1}: (6, {})} | custom-call | flops 1000000000 | bytes 4194304 | tf_op jit(solution)/shard_map/own/pallas_call | solution.py:256
  37.7 2.0 %collective-permute-done.13.over_ref = bf16[64,1024]{1,0:T(8,128)(2,1)S(1)} collective-permute-done((bf16[64,1024]{1,0:T(8,128)(2,1)S(1)}, bf16[64,1024]{1,0:T(8,128)(2,1)S(1)}, u32[]{:S(2)}, u32[]{:S(2)}) %collective-permute-start.13) | collective-permute-done | bytes 131104 | tf_op jit(solution)/shard_map/ppermute | solution.py:317
  39.8 0.5 %halo.7.refs_0_ = f32[64,1024]{1,0:T(8,128)S(1)} custom-call(s32[1]{0:T(128)} %bitcast.index_ref.refs_0_, f32[64,1024]{1,0:T(8,128)S(1)} %get-tuple-element.69.acc_ref, bf16[64,1024]{1,0:T(8,128)(2,1)S(1)} %collective-permute-done.13.over_ref, bf16[36,256,256]{2,1,0:T(8,128)(2,1)S(1)} %get-tuple-element.46.d_ref.refs_3_), custom_call_target="tpu_custom_call" | custom-call | flops 1000000000 | bytes 4194304 | tf_op jit(solution)/shard_map/halo/pallas_call | solution.py:256
  40.3 0.6 %collective-permute-done.14.refs_2_ = bf16[64,128]{1,0:T(8,128)(2,1)S(1)} collective-permute-done((bf16[64,128]{1,0:T(8,128)(2,1)S(1)}, bf16[64,128]{1,0:T(8,128)(2,1)S(1)}, u32[]{:S(2)}, u32[]{:S(2)}) %collective-permute-start.14) | collective-permute-done | bytes 16416 | tf_op jit(solution)/shard_map/ppermute | solution.py:330
  40.9 0.0 collective-permute-done.15.refs_3_
  40.9 0.9 %last.1 = bf16[4,64,1024]{2,1,0:T(8,128)(2,1)} custom-call(f32[64,1024]{1,0:T(8,128)S(1)} %halo.7.refs_0_, bf16[256,1024]{1,0:T(8,128)(2,1)S(1)} %get-tuple-element.47.refs_2_.refs_1_, bf16[64,128]{1,0:T(8,128)(2,1)S(1)} %collective-permute-done.14.refs_2_, bf16[64,128]{1,0:T(8,128)(2,1)S(1)} %collective-permute-done.15.refs_3_, ...), custom_call_target="tpu_custom_call", output_to_operand_aliasing={{}: (4, {})} | custom-call | flops 1000000000 | bytes 4194304 | tf_op jit(solution)/shard_map/last/pallas_call | solution.py:256
  (4 shorter events, 0.1 us)
Async XLA Ops:
  0.0 8.2 %copy-start.1 = (bf16[4,32,256]{2,1,0:T(8,128)(2,1)S(1)}, bf16[4,32,256]{2,1,0:T(8,128)(2,1)}, u32[]{:S(2)}) copy-start(bf16[4,32,256]{2,1,0:T(8,128)(2,1)} %refs_5_.3) | copy-start | bytes 196612
  0.0 8.2 %copy-start = (bf16[32,256,256]{2,1,0:T(8,128)(2,1)S(1)}, bf16[32,256,256]{2,1,0:T(8,128)(2,1)}, u32[]{:S(2)}) copy-start(bf16[32,256,256]{2,1,0:T(8,128)(2,1)} %refs_6_.3) | copy-start | bytes 12582916
  1.8 6.2 %collective-permute-start = (bf16[64,1536]{1,0:T(8,128)(2,1)S(1)}, bf16[64,1536]{1,0:T(8,128)(2,1)S(1)}, u32[]{:S(2)}, u32[]{:S(2)}) collective-permute-start(bf16[64,1536]{1,0:T(8,128)(2,1)S(1)} %get-tuple-element.41), channel_id=1, source_target_pairs={{0,1},{1,0},{2,3},{3,2},{4,5},{5,4},{6,7},{7,6},{8,9},{9,8},{10,11... | collective-permute-start | bytes 589832 | tf_op jit(solution)/shard_map/ppermute | solution.py:318
  2.4 8.6 %collective-permute-start.1 = (bf16[64,1024]{1,0:T(8,128)(2,1)}, bf16[64,1024]{1,0:T(8,128)(2,1)S(1)}, u32[]{:S(2)}, u32[]{:S(2)}) collective-permute-start(bf16[64,1024]{1,0:T(8,128)(2,1)} %refs_4_.1), channel_id=1, source_target_pairs={{0,15},{1,2},{2,1},{3,4},{4,3},{5,6},{6,5},{7,8},{8,7},{9,10},{10,... | collective-permute-start | bytes 393224 | tf_op jit(solution)/shard_map/ppermute | solution.py:317
  8.0 5.2 %collective-permute-start.2 = (bf16[64,128]{1,0:T(8,128)(2,1)S(1)}, bf16[64,128]{1,0:T(8,128)(2,1)S(1)}, u32[]{:S(2)}, u32[]{:S(2)}) collective-permute-start(bf16[64,128]{1,0:T(8,128)(2,1)S(1)} %get-tuple-element.43.refs_7_), channel_id=1, source_target_pairs={{0,9},{1,11},{2,10},{3,8},{4,13},{5,14},{6,15},{7,12},{8,1},{9,2},... | collective-permute-start | bytes 49160 | tf_op jit(solution)/shard_map/ppermute | solution.py:330
  8.1 5.1 %collective-permute-start.3 = (bf16[64,128]{1,0:T(8,128)(2,1)S(1)}, bf16[64,128]{1,0:T(8,128)(2,1)S(1)}, u32[]{:S(2)}, u32[]{:S(2)}) collective-permute-start(bf16[64,128]{1,0:T(8,128)(2,1)S(1)} %get-tuple-element.44.refs_8_), channel_id=1, source_target_pairs={{0,8},{1,10},{2,11},{3,9},{4,12},{5,15},{6,14},{7,13},{8,0},{9,3},... | collective-permute-start | bytes 49160 | tf_op jit(solution)/shard_map/ppermute | solution.py:330
  13.8 3.4 %collective-permute-start.4 = (bf16[64,1536]{1,0:T(8,128)(2,1)S(1)}, bf16[64,1536]{1,0:T(8,128)(2,1)S(1)}, u32[]{:S(2)}, u32[]{:S(2)}) collective-permute-start(bf16[64,1536]{1,0:T(8,128)(2,1)S(1)} %get-tuple-element.51), channel_id=1, source_target_pairs={{0,1},{1,0},{2,3},{3,2},{4,5},{5,4},{6,7},{7,6},{8,9},{9,8},{10,11... | collective-permute-start | bytes 589832 | tf_op jit(solution)/shard_map/ppermute | solution.py:318
  14.0 7.3 %collective-permute-start.5 = (bf16[64,1024]{1,0:T(8,128)(2,1)S(1)}, bf16[64,1024]{1,0:T(8,128)(2,1)S(1)}, u32[]{:S(2)}, u32[]{:S(2)}) collective-permute-start(bf16[64,1024]{1,0:T(8,128)(2,1)S(1)} %get-tuple-element.50.refs_1_), channel_id=1, source_target_pairs={{0,15},{1,2},{2,1},{3,4},{4,3},{5,6},{6,5},{7,8},{8,7},{9,10},{10,... | collective-permute-start | bytes 393224 | tf_op jit(solution)/shard_map/ppermute | solution.py:317
  17.2 5.0 %collective-permute-start.6 = (bf16[64,128]{1,0:T(8,128)(2,1)S(1)}, bf16[64,128]{1,0:T(8,128)(2,1)S(1)}, u32[]{:S(2)}, u32[]{:S(2)}) collective-permute-start(bf16[64,128]{1,0:T(8,128)(2,1)S(1)} %get-tuple-element.53.refs_4_), channel_id=1, source_target_pairs={{0,9},{1,11},{2,10},{3,8},{4,13},{5,14},{6,15},{7,12},{8,1},{9,2},... | collective-permute-start | bytes 49160 | tf_op jit(solution)/shard_map/ppermute | solution.py:330
  17.3 5.0 %collective-permute-start.7 = (bf16[64,128]{1,0:T(8,128)(2,1)S(1)}, bf16[64,128]{1,0:T(8,128)(2,1)S(1)}, u32[]{:S(2)}, u32[]{:S(2)}) collective-permute-start(bf16[64,128]{1,0:T(8,128)(2,1)S(1)} %get-tuple-element.54.refs_5_), channel_id=1, source_target_pairs={{0,8},{1,10},{2,11},{3,9},{4,12},{5,15},{6,14},{7,13},{8,0},{9,3},... | collective-permute-start | bytes 49160 | tf_op jit(solution)/shard_map/ppermute | solution.py:330
  22.9 3.3 %collective-permute-start.8 = (bf16[64,1536]{1,0:T(8,128)(2,1)S(1)}, bf16[64,1536]{1,0:T(8,128)(2,1)S(1)}, u32[]{:S(2)}, u32[]{:S(2)}) collective-permute-start(bf16[64,1536]{1,0:T(8,128)(2,1)S(1)} %get-tuple-element.57), channel_id=1, source_target_pairs={{0,1},{1,0},{2,3},{3,2},{4,5},{5,4},{6,7},{7,6},{8,9},{9,8},{10,11... | collective-permute-start | bytes 589832 | tf_op jit(solution)/shard_map/ppermute | solution.py:318
  23.2 7.4 %collective-permute-start.9 = (bf16[64,1024]{1,0:T(8,128)(2,1)S(1)}, bf16[64,1024]{1,0:T(8,128)(2,1)S(1)}, u32[]{:S(2)}, u32[]{:S(2)}) collective-permute-start(bf16[64,1024]{1,0:T(8,128)(2,1)S(1)} %get-tuple-element.56.refs_1_), channel_id=1, source_target_pairs={{0,15},{1,2},{2,1},{3,4},{4,3},{5,6},{6,5},{7,8},{8,7},{9,10},{10,... | collective-permute-start | bytes 393224 | tf_op jit(solution)/shard_map/ppermute | solution.py:317
  26.2 5.0 %collective-permute-start.10 = (bf16[64,128]{1,0:T(8,128)(2,1)S(1)}, bf16[64,128]{1,0:T(8,128)(2,1)S(1)}, u32[]{:S(2)}, u32[]{:S(2)}) collective-permute-start(bf16[64,128]{1,0:T(8,128)(2,1)S(1)} %get-tuple-element.59.refs_4_), channel_id=1, source_target_pairs={{0,9},{1,11},{2,10},{3,8},{4,13},{5,14},{6,15},{7,12},{8,1},{9,2},... | collective-permute-start | bytes 49160 | tf_op jit(solution)/shard_map/ppermute | solution.py:330
  26.3 4.9 %collective-permute-start.11 = (bf16[64,128]{1,0:T(8,128)(2,1)S(1)}, bf16[64,128]{1,0:T(8,128)(2,1)S(1)}, u32[]{:S(2)}, u32[]{:S(2)}) collective-permute-start(bf16[64,128]{1,0:T(8,128)(2,1)S(1)} %get-tuple-element.60.refs_5_), channel_id=1, source_target_pairs={{0,8},{1,10},{2,11},{3,9},{4,12},{5,15},{6,14},{7,13},{8,0},{9,3},... | collective-permute-start | bytes 49160 | tf_op jit(solution)/shard_map/ppermute | solution.py:330
  31.8 3.8 %collective-permute-start.12 = (bf16[64,1536]{1,0:T(8,128)(2,1)S(1)}, bf16[64,1536]{1,0:T(8,128)(2,1)S(1)}, u32[]{:S(2)}, u32[]{:S(2)}) collective-permute-start(bf16[64,1536]{1,0:T(8,128)(2,1)S(1)} %get-tuple-element.64), channel_id=1, source_target_pairs={{0,1},{1,0},{2,3},{3,2},{4,5},{5,4},{6,7},{7,6},{8,9},{9,8},{10,11... | collective-permute-start | bytes 589832 | tf_op jit(solution)/shard_map/ppermute | solution.py:318
  32.4 7.4 %collective-permute-start.13 = (bf16[64,1024]{1,0:T(8,128)(2,1)S(1)}, bf16[64,1024]{1,0:T(8,128)(2,1)S(1)}, u32[]{:S(2)}, u32[]{:S(2)}) collective-permute-start(bf16[64,1024]{1,0:T(8,128)(2,1)S(1)} %get-tuple-element.63.refs_1_), channel_id=1, source_target_pairs={{0,15},{1,2},{2,1},{3,4},{4,3},{5,6},{6,5},{7,8},{8,7},{9,10},{10,... | collective-permute-start | bytes 393224 | tf_op jit(solution)/shard_map/ppermute | solution.py:317
  35.7 5.2 %collective-permute-start.14 = (bf16[64,128]{1,0:T(8,128)(2,1)S(1)}, bf16[64,128]{1,0:T(8,128)(2,1)S(1)}, u32[]{:S(2)}, u32[]{:S(2)}) collective-permute-start(bf16[64,128]{1,0:T(8,128)(2,1)S(1)} %get-tuple-element.66.refs_4_), channel_id=1, source_target_pairs={{0,9},{1,11},{2,10},{3,8},{4,13},{5,14},{6,15},{7,12},{8,1},{9,2},... | collective-permute-start | bytes 49160 | tf_op jit(solution)/shard_map/ppermute | solution.py:330
  35.8 5.1 %collective-permute-start.15 = (bf16[64,128]{1,0:T(8,128)(2,1)S(1)}, bf16[64,128]{1,0:T(8,128)(2,1)S(1)}, u32[]{:S(2)}, u32[]{:S(2)}) collective-permute-start(bf16[64,128]{1,0:T(8,128)(2,1)S(1)} %get-tuple-element.67.refs_5_), channel_id=1, source_target_pairs={{0,8},{1,10},{2,11},{3,9},{4,12},{5,15},{6,14},{7,13},{8,0},{9,3},... | collective-permute-start | bytes 49160 | tf_op jit(solution)/shard_map/ppermute | solution.py:330

commit v21 on v15

--- a/solution.py
+++ b/solution.py
@@ -154,6 +154,7 @@
     for c in range(plan.per_device):
         cb_ref[c * rank : (c + 1) * rank, c * size : (c + 1) * size] = col_ref[c]
     column = lax.broadcasted_iota(jnp.int32, (rank, plan.width), 1) // rank
+    wide = jnp.concatenate([coup_ref[...].astype(F32)] * plan.per_device, axis=2)
     shift = 0 if plan.paired else plan.member(index_ref)
     for s in range(plan.slots):
         row = lax.rem(rows_ref[s], plan.block_clusters)
@@ -165,9 +166,7 @@
         else:
             index = 0
         where = (index, pl.ds(pl.multiple_of(place * rank, rank), rank), slice(None))
-        tile = coup_ref[s].astype(F32)
-        wide = jnp.where(column == cols_ref[s], jnp.concatenate([tile] * plan.per_device, axis=1), 0.0)
-        sum_ref[where] = sum_ref[where] + wide
+        sum_ref[where] = sum_ref[where] + jnp.where(column == cols_ref[s], wide[s], 0.0)
     for index in range(len(plan.hops)):
         g_ref[index] = jnp.concatenate(halves(sum_ref[index]), axis=1)
     plan.send_far(index_ref, x_ref[...], cb_ref, g_ref, sends)
@@ -298,7 +297,7 @@
                 scratch=scratch_for(far_rows, far_cols, col_basis, couplings)
                 + [pltpu.VMEM(matrix[:2] + (width,), F32), pltpu.SemaphoreType.DMA((7,))],
             )
-        over = lax.ppermute(block if product == 0 else current, axes, plan.over)
+        over = lax.ppermute(current, axes, plan.over)
         near = lax.ppermute(sends[0] if plan.paired else current, axes, plan.near)
         if plan.paired:
             sends = call(

time: 41.7 us -> 41.7 us (level)
  no operation moved by 1% of the time
where the time goes in v21:
time: 41.7 us; the launch traced here: 41.5 us
  starting transfers between devices  20.6 us (49%)
  Pallas kernels  12.3 us (29%)
  waiting for transfers between devices  8.37 us (20%)
    ppermute x4, starting transfers between devices, on_device(): over = lax.ppermute(current, axes, plan.over)  12.8 us
    pallas_call x17, Pallas kernels, call(): pl.pallas_call(kernel, in_specs=list(specs), out_specs=out_specs or [IN_V...  12.3 us
    ppermute x4, waiting for transfers between devices, on_device(): over = lax.ppermute(current, axes, plan.over)  6.45 us
    ppermute x8, starting transfers between devices, on_device(): fars = [lax.ppermute(s, axes, route) for s, route in zip(sends, routes)]  5.04 us
    ppermute x4, starting transfers between devices, on_device(): near = lax.ppermute(sends[0] if plan.paired else current, axes, plan.near)  2.8 us
    ppermute x8, waiting for transfers between devices, on_device(): fars = [lax.ppermute(s, axes, route) for s, route in zip(sends, routes)]  1.9 us
  transfers between devices with their start and end apart: 16, of which 5 were waited for; matrix products, arithmetic and copies ran while one was open for 0% of the time, Pallas kernels for 19%

profile of v21, /device:TPU:0, one launch (start us, length us, event | category | flops | bytes accessed | tf_op | source)
XLA Modules:
  0.0 41.5 jit_solution(12187034482518965659)
XLA Ops:
  0.0 0.0 copy-start.1
  0.0 0.0 copy-start
  0.0 1.8 %prepare.1 = (bf16[64,1024]{1,0:T(8,128)(2,1)S(1)}, bf16[1,512,256]{2,1,0:T(8,128)(2,1)S(1)}, bf16[128,1024]{1,0:T(8,128)(2,1)S(1)}, s32[32]{0:T(128)S(4)}, s32[...) custom-call(s32[1]{0:T(128)} %bitcast.index_ref.refs_0_, s32[32]{0:T(128)} %refs_0_.1, s32[32]{0:T(128)} %refs_1_.1, ...), custom_call_target="tpu_custom_call" | custom-call | flops 1000000000 | bytes 4194304 | tf_op jit(solution)/shard_map/prepare/pallas_call | solution.py:239
  1.9 0.5 %collective-permute-start = (bf16[64,1536]{1,0:T(8,128)(2,1)S(1)}, bf16[64,1536]{1,0:T(8,128)(2,1)S(1)}, u32[]{:S(2)}, u32[]{:S(2)}) collective-permute-start(bf16[64,1536]{1,0:T(8,128)(2,1)S(1)} %get-tuple-element.41), channel_id=1, source_target_pairs={{0,1},{1,0},{2,3},{3,2},{4,5},{5,4},{6,7},{7,6},{8,9},{9,8},{10,11... | collective-permute-start | bytes 589832 | tf_op jit(solution)/shard_map/ppermute | solution.py:301
  2.4 5.6 %collective-permute-start.1 = (bf16[64,1024]{1,0:T(8,128)(2,1)S(1)}, bf16[64,1024]{1,0:T(8,128)(2,1)S(1)}, u32[]{:S(2)}, u32[]{:S(2)}) collective-permute-start(bf16[64,1024]{1,0:T(8,128)(2,1)S(1)} %get-tuple-element.40.refs_3_), channel_id=1, source_target_pairs={{0,15},{1,2},{2,1},{3,4},{4,3},{5,6},{6,5},{7,8},{8,7},{9,10},{10,... | collective-permute-start | bytes 393224 | tf_op jit(solution)/shard_map/ppermute | solution.py:300
  8.0 0.0 collective-permute-done.message_ref.refs_4_
  8.0 0.1 collective-permute-start.2
  8.1 0.1 collective-permute-start.3
  8.2 0.0 copy-done.1
  8.2 0.0 copy-done
  8.2 1.9 %first_own.1 = (f32[64,1024]{1,0:T(8,128)S(1)}, bf16[36,256,256]{2,1,0:T(8,128)(2,1)S(1)}, bf16[256,1024]{1,0:T(8,128)(2,1)S(1)}) custom-call(s32[1]{0:T(128)} %bitcast.index_ref.refs_0_, s32[32]{0:T(128)S(4)} %get-tuple-element.38.refs_1_, s32[32]{0:T(128)S(4)} %get-tuple-element.39.refs_2_, bf16[64,1024]{1,0:T(8,128)(2,1)S(1)} %get-tuple-element.40.refs_3_, ...), custom_call_target="tpu_custom_call" | custom-call | flops 1000000000 | bytes 4194304 | tf_op jit(solution)/shard_map/first_own/pallas_call | solution.py:239
  10.1 0.6 %collective-permute-done.1.over_ref = bf16[64,1024]{1,0:T(8,128)(2,1)S(1)} collective-permute-done((bf16[64,1024]{1,0:T(8,128)(2,1)S(1)}, bf16[64,1024]{1,0:T(8,128)(2,1)S(1)}, u32[]{:S(2)}, u32[]{:S(2)}) %collective-permute-start.1) | collective-permute-done | bytes 131104 | tf_op jit(solution)/shard_map/ppermute | solution.py:300
  10.7 0.5 %halo.4.refs_1_ = f32[64,1024]{1,0:T(8,128)S(1)} custom-call(s32[1]{0:T(128)} %bitcast.index_ref.refs_0_, f32[64,1024]{1,0:T(8,128)S(1)} %get-tuple-element.45.acc_ref, bf16[64,1024]{1,0:T(8,128)(2,1)S(1)} %collective-permute-done.1.over_ref, bf16[36,256,256]{2,1,0:T(8,128)(2,1)S(1)} %get-tuple-element.46.d_ref.refs_3_), custom_call_target="tpu_custom_call" | custom-call | flops 1000000000 | bytes 4194304 | tf_op jit(solution)/shard_map/halo/pallas_call | solution.py:239
  11.2 1.9 %collective-permute-done.2.refs_5_ = bf16[64,128]{1,0:T(8,128)(2,1)S(1)} collective-permute-done((bf16[64,128]{1,0:T(8,128)(2,1)S(1)}, bf16[64,128]{1,0:T(8,128)(2,1)S(1)}, u32[]{:S(2)}, u32[]{:S(2)}) %collective-permute-start.2) | collective-permute-done | bytes 16416 | tf_op jit(solution)/shard_map/ppermute | solution.py:313
  13.1 0.0 collective-permute-done.3.refs_6_
  13.1 0.6 %finish.3 = (bf16[64,1024]{1,0:T(8,128)(2,1)S(1)}, bf16[64,1536]{1,0:T(8,128)(2,1)S(1)}, f32[64,256]{1,0:T(8,128)S(1)}) custom-call(s32[1]{0:T(128)} %bitcast.index_ref.refs_0_, f32[64,1024]{1,0:T(8,128)S(1)} %halo.4.refs_1_, bf16[256,1024]{1,0:T(8,128)(2,1)S(1)} %get-tuple-element.47.refs_2_.refs_1_, bf16[128,1024]{1,0:T(8,128)(2,1)S(1)} %get-tuple-element.48.refs_3_, ...), custom_call_target="tpu_custom_call" | custom-call | flops 1000000000 | bytes 4194304 | tf_op jit(solution)/shard_map/finish/pallas_call | solution.py:239
  13.7 1.1 %collective-permute-start.4 = (bf16[64,1536]{1,0:T(8,128)(2,1)S(1)}, bf16[64,1536]{1,0:T(8,128)(2,1)S(1)}, u32[]{:S(2)}, u32[]{:S(2)}) collective-permute-start(bf16[64,1536]{1,0:T(8,128)(2,1)S(1)} %get-tuple-element.51), channel_id=1, source_target_pairs={{0,1},{1,0},{2,3},{3,2},{4,5},{5,4},{6,7},{7,6},{8,9},{9,8},{10,11... | collective-permute-start | bytes 589832 | tf_op jit(solution)/shard_map/ppermute | solution.py:301
  14.8 2.3 %collective-permute-start.5 = (bf16[64,1024]{1,0:T(8,128)(2,1)S(1)}, bf16[64,1024]{1,0:T(8,128)(2,1)S(1)}, u32[]{:S(2)}, u32[]{:S(2)}) collective-permute-start(bf16[64,1024]{1,0:T(8,128)(2,1)S(1)} %get-tuple-element.50.refs_1_), channel_id=1, source_target_pairs={{0,15},{1,2},{2,1},{3,4},{4,3},{5,6},{6,5},{7,8},{8,7},{9,10},{10,... | collective-permute-start | bytes 393224 | tf_op jit(solution)/shard_map/ppermute | solution.py:300
  17.1 0.0 collective-permute-done.4.message_ref.refs_2_
  17.1 0.3 collective-permute-start.6
  17.4 1.4 %collective-permute-start.7 = (bf16[64,128]{1,0:T(8,128)(2,1)S(1)}, bf16[64,128]{1,0:T(8,128)(2,1)S(1)}, u32[]{:S(2)}, u32[]{:S(2)}) collective-permute-start(bf16[64,128]{1,0:T(8,128)(2,1)S(1)} %get-tuple-element.54.refs_5_), channel_id=1, source_target_pairs={{0,8},{1,11},{2,10},{3,9},{4,12},{5,15},{6,14},{7,13},{8,0},{9,3},... | collective-permute-start | bytes 49160 | tf_op jit(solution)/shard_map/ppermute | solution.py:313
  18.8 1.3 %own.3 = (f32[64,1024]{1,0:T(8,128)S(1)}, bf16[4,64,1024]{2,1,0:T(8,128)(2,1)}) custom-call(s32[1]{0:T(128)} %bitcast.index_ref.refs_0_, bf16[64,1024]{1,0:T(8,128)(2,1)S(1)} %get-tuple-element.50.refs_1_, bf16[64,1536]{1,0:T(8,128)(2,1)S(1)} %collective-permute-done.4.message_ref.refs_2_, bf16[36,256,256]{2,1,0:T(8,128)(2,1)S(1)} %get-tuple-element.46.d_ref.refs_3_, ...), custom_call_target="tpu_custom_call" | custom-call | flops 1000000000 | bytes 4194304 | tf_op jit(solution)/shard_map/own/pallas_call | solution.py:239
  20.1 1.8 %collective-permute-done.5.over_ref = bf16[64,1024]{1,0:T(8,128)(2,1)S(1)} collective-permute-done((bf16[64,1024]{1,0:T(8,128)(2,1)S(1)}, bf16[64,1024]{1,0:T(8,128)(2,1)S(1)}, u32[]{:S(2)}, u32[]{:S(2)}) %collective-permute-start.5) | collective-permute-done | bytes 131104 | tf_op jit(solution)/shard_map/ppermute | solution.py:300
  21.9 0.5 %halo.5.refs_1_ = f32[64,1024]{1,0:T(8,128)S(1)} custom-call(s32[1]{0:T(128)} %bitcast.index_ref.refs_0_, f32[64,1024]{1,0:T(8,128)S(1)} %get-tuple-element.55.acc_ref, bf16[64,1024]{1,0:T(8,128)(2,1)S(1)} %collective-permute-done.5.over_ref, bf16[36,256,256]{2,1,0:T(8,128)(2,1)S(1)} %get-tuple-element.46.d_ref.refs_3_), custom_call_target="tpu_custom_call" | custom-call | flops 1000000000 | bytes 4194304 | tf_op jit(solution)/shard_map/halo/pallas_call | solution.py:239
  22.4 0.0 collective-permute-done.6.refs_5_
  22.4 0.0 collective-permute-done.7.refs_6_
  22.4 0.6 %finish.4 = (bf16[64,1024]{1,0:T(8,128)(2,1)S(1)}, bf16[64,1536]{1,0:T(8,128)(2,1)S(1)}, f32[64,256]{1,0:T(8,128)S(1)}) custom-call(s32[1]{0:T(128)} %bitcast.index_ref.refs_0_, f32[64,1024]{1,0:T(8,128)S(1)} %halo.5.refs_1_, bf16[256,1024]{1,0:T(8,128)(2,1)S(1)} %get-tuple-element.47.refs_2_.refs_1_, bf16[128,1024]{1,0:T(8,128)(2,1)S(1)} %get-tuple-element.48.refs_3_, ...), custom_call_target="tpu_custom_call" | custom-call | flops 1000000000 | bytes 4194304 | tf_op jit(solution)/shard_map/finish/pallas_call | solution.py:239
  23.0 0.5 %collective-permute-start.8 = (bf16[64,1536]{1,0:T(8,128)(2,1)S(1)}, bf16[64,1536]{1,0:T(8,128)(2,1)S(1)}, u32[]{:S(2)}, u32[]{:S(2)}) collective-permute-start(bf16[64,1536]{1,0:T(8,128)(2,1)S(1)} %get-tuple-element.57), channel_id=1, source_target_pairs={{0,1},{1,0},{2,3},{3,2},{4,5},{5,4},{6,7},{7,6},{8,9},{9,8},{10,11... | collective-permute-start | bytes 589832 | tf_op jit(solution)/shard_map/ppermute | solution.py:301
  23.5 2.4 %collective-permute-start.9 = (bf16[64,1024]{1,0:T(8,128)(2,1)S(1)}, bf16[64,1024]{1,0:T(8,128)(2,1)S(1)}, u32[]{:S(2)}, u32[]{:S(2)}) collective-permute-start(bf16[64,1024]{1,0:T(8,128)(2,1)S(1)} %get-tuple-element.56.refs_1_), channel_id=1, source_target_pairs={{0,15},{1,2},{2,1},{3,4},{4,3},{5,6},{6,5},{7,8},{8,7},{9,10},{10,... | collective-permute-start | bytes 393224 | tf_op jit(solution)/shard_map/ppermute | solution.py:300
  25.9 0.0 collective-permute-done.8.message_ref.refs_2_
  25.9 0.6 %collective-permute-start.10 = (bf16[64,128]{1,0:T(8,128)(2,1)S(1)}, bf16[64,128]{1,0:T(8,128)(2,1)S(1)}, u32[]{:S(2)}, u32[]{:S(2)}) collective-permute-start(bf16[64,128]{1,0:T(8,128)(2,1)S(1)} %get-tuple-element.59.refs_4_), channel_id=1, source_target_pairs={{0,9},{1,10},{2,11},{3,8},{4,13},{5,14},{6,15},{7,12},{8,1},{9,2},... | collective-permute-start | bytes 49160 | tf_op jit(solution)/shard_map/ppermute | solution.py:313
  26.5 1.0 %collective-permute-start.11 = (bf16[64,128]{1,0:T(8,128)(2,1)S(1)}, bf16[64,128]{1,0:T(8,128)(2,1)S(1)}, u32[]{:S(2)}, u32[]{:S(2)}) collective-permute-start(bf16[64,128]{1,0:T(8,128)(2,1)S(1)} %get-tuple-element.60.refs_5_), channel_id=1, source_target_pairs={{0,8},{1,11},{2,10},{3,9},{4,12},{5,15},{6,14},{7,13},{8,0},{9,3},... | collective-permute-start | bytes 49160 | tf_op jit(solution)/shard_map/ppermute | solution.py:313
  27.5 1.3 %own.4 = (f32[64,1024]{1,0:T(8,128)S(1)}, bf16[4,64,1024]{2,1,0:T(8,128)(2,1)}) custom-call(s32[1]{0:T(128)} %bitcast.index_ref.refs_0_, bf16[64,1024]{1,0:T(8,128)(2,1)S(1)} %get-tuple-element.56.refs_1_, bf16[64,1536]{1,0:T(8,128)(2,1)S(1)} %collective-permute-done.8.message_ref.refs_2_, ...), custom_call_target="tpu_custom_call", output_to_operand_aliasing={{1}: (6, {})} | custom-call | flops 1000000000 | bytes 4194304 | tf_op jit(solution)/shard_map/own/pallas_call | solution.py:239
  28.8 2.0 %collective-permute-done.9.over_ref = bf16[64,1024]{1,0:T(8,128)(2,1)S(1)} collective-permute-done((bf16[64,1024]{1,0:T(8,128)(2,1)S(1)}, bf16[64,1024]{1,0:T(8,128)(2,1)S(1)}, u32[]{:S(2)}, u32[]{:S(2)}) %collective-permute-start.9) | collective-permute-done | bytes 131104 | tf_op jit(solution)/shard_map/ppermute | solution.py:300
  30.8 0.5 %halo.6.refs_1_ = f32[64,1024]{1,0:T(8,128)S(1)} custom-call(s32[1]{0:T(128)} %bitcast.index_ref.refs_0_, f32[64,1024]{1,0:T(8,128)S(1)} %get-tuple-element.62.acc_ref, bf16[64,1024]{1,0:T(8,128)(2,1)S(1)} %collective-permute-done.9.over_ref, bf16[36,256,256]{2,1,0:T(8,128)(2,1)S(1)} %get-tuple-element.46.d_ref.refs_3_), custom_call_target="tpu_custom_call" | custom-call | flops 1000000000 | bytes 4194304 | tf_op jit(solution)/shard_map/halo/pallas_call | solution.py:239
  31.4 0.0 collective-permute-done.10.refs_5_
  31.4 0.0 collective-permute-done.11.refs_6_
  31.4 0.6 %finish.5 = (bf16[64,1024]{1,0:T(8,128)(2,1)S(1)}, bf16[64,1536]{1,0:T(8,128)(2,1)S(1)}, f32[64,256]{1,0:T(8,128)S(1)}) custom-call(s32[1]{0:T(128)} %bitcast.index_ref.refs_0_, f32[64,1024]{1,0:T(8,128)S(1)} %halo.6.refs_1_, bf16[256,1024]{1,0:T(8,128)(2,1)S(1)} %get-tuple-element.47.refs_2_.refs_1_, bf16[128,1024]{1,0:T(8,128)(2,1)S(1)} %get-tuple-element.48.refs_3_, ...), custom_call_target="tpu_custom_call" | custom-call | flops 1000000000 | bytes 4194304 | tf_op jit(solution)/shard_map/finish/pallas_call | solution.py:239
  32.0 0.7 %collective-permute-start.12 = (bf16[64,1536]{1,0:T(8,128)(2,1)S(1)}, bf16[64,1536]{1,0:T(8,128)(2,1)S(1)}, u32[]{:S(2)}, u32[]{:S(2)}) collective-permute-start(bf16[64,1536]{1,0:T(8,128)(2,1)S(1)} %get-tuple-element.64), channel_id=1, source_target_pairs={{0,1},{1,0},{2,3},{3,2},{4,5},{5,4},{6,7},{7,6},{8,9},{9,8},{10,11... | collective-permute-start | bytes 589832 | tf_op jit(solution)/shard_map/ppermute | solution.py:301
  32.7 2.5 %collective-permute-start.13 = (bf16[64,1024]{1,0:T(8,128)(2,1)S(1)}, bf16[64,1024]{1,0:T(8,128)(2,1)S(1)}, u32[]{:S(2)}, u32[]{:S(2)}) collective-permute-start(bf16[64,1024]{1,0:T(8,128)(2,1)S(1)} %get-tuple-element.63.refs_1_), channel_id=1, source_target_pairs={{0,15},{1,2},{2,1},{3,4},{4,3},{5,6},{6,5},{7,8},{8,7},{9,10},{10,... | collective-permute-start | bytes 393224 | tf_op jit(solution)/shard_map/ppermute | solution.py:300
  35.2 0.0 collective-permute-done.12.message_ref.refs_2_
  35.2 0.1 collective-permute-start.14
  35.3 1.5 %collective-permute-start.15 = (bf16[64,128]{1,0:T(8,128)(2,1)S(1)}, bf16[64,128]{1,0:T(8,128)(2,1)S(1)}, u32[]{:S(2)}, u32[]{:S(2)}) collective-permute-start(bf16[64,128]{1,0:T(8,128)(2,1)S(1)} %get-tuple-element.67.refs_5_), channel_id=1, source_target_pairs={{0,8},{1,11},{2,10},{3,9},{4,12},{5,15},{6,14},{7,13},{8,0},{9,3},... | collective-permute-start | bytes 49160 | tf_op jit(solution)/shard_map/ppermute | solution.py:313
  36.8 1.3 %own.5 = (f32[64,1024]{1,0:T(8,128)S(1)}, bf16[4,64,1024]{2,1,0:T(8,128)(2,1)}) custom-call(s32[1]{0:T(128)} %bitcast.index_ref.refs_0_, bf16[64,1024]{1,0:T(8,128)(2,1)S(1)} %get-tuple-element.63.refs_1_, bf16[64,1536]{1,0:T(8,128)(2,1)S(1)} %collective-permute-done.12.message_ref.refs_2_, ...), custom_call_target="tpu_custom_call", output_to_operand_aliasing={{1}: (6, {})} | custom-call | flops 1000000000 | bytes 4194304 | tf_op jit(solution)/shard_map/own/pallas_call | solution.py:239
  38.1 2.0 %collective-permute-done.13.over_ref = bf16[64,1024]{1,0:T(8,128)(2,1)S(1)} collective-permute-done((bf16[64,1024]{1,0:T(8,128)(2,1)S(1)}, bf16[64,1024]{1,0:T(8,128)(2,1)S(1)}, u32[]{:S(2)}, u32[]{:S(2)}) %collective-permute-start.13) | collective-permute-done | bytes 131104 | tf_op jit(solution)/shard_map/ppermute | solution.py:300
  40.1 0.5 %halo.7.refs_0_ = f32[64,1024]{1,0:T(8,128)S(1)} custom-call(s32[1]{0:T(128)} %bitcast.index_ref.refs_0_, f32[64,1024]{1,0:T(8,128)S(1)} %get-tuple-element.69.acc_ref, bf16[64,1024]{1,0:T(8,128)(2,1)S(1)} %collective-permute-done.13.over_ref, bf16[36,256,256]{2,1,0:T(8,128)(2,1)S(1)} %get-tuple-element.46.d_ref.refs_3_), custom_call_target="tpu_custom_call" | custom-call | flops 1000000000 | bytes 4194304 | tf_op jit(solution)/shard_map/halo/pallas_call | solution.py:239
  40.6 0.0 collective-permute-done.14.refs_2_
  40.6 0.0 collective-permute-done.15.refs_3_
  40.6 0.9 %last.1 = bf16[4,64,1024]{2,1,0:T(8,128)(2,1)} custom-call(f32[64,1024]{1,0:T(8,128)S(1)} %halo.7.refs_0_, bf16[256,1024]{1,0:T(8,128)(2,1)S(1)} %get-tuple-element.47.refs_2_.refs_1_, bf16[64,128]{1,0:T(8,128)(2,1)S(1)} %collective-permute-done.14.refs_2_, bf16[64,128]{1,0:T(8,128)(2,1)S(1)} %collective-permute-done.15.refs_3_, ...), custom_call_target="tpu_custom_call", output_to_operand_aliasing={{}: (4, {})} | custom-call | flops 1000000000 | bytes 4194304 | tf_op jit(solution)/shard_map/last/pallas_call | solution.py:239
  (4 shorter events, 0.1 us)
Async XLA Ops:
  0.0 8.2 %copy-start.1 = (bf16[4,32,256]{2,1,0:T(8,128)(2,1)S(1)}, bf16[4,32,256]{2,1,0:T(8,128)(2,1)}, u32[]{:S(2)}) copy-start(bf16[4,32,256]{2,1,0:T(8,128)(2,1)} %refs_5_.3) | copy-start | bytes 196612
  0.0 8.2 %copy-start = (bf16[32,256,256]{2,1,0:T(8,128)(2,1)S(1)}, bf16[32,256,256]{2,1,0:T(8,128)(2,1)}, u32[]{:S(2)}) copy-start(bf16[32,256,256]{2,1,0:T(8,128)(2,1)} %refs_6_.3) | copy-start | bytes 12582916
  1.9 6.2 %collective-permute-start = (bf16[64,1536]{1,0:T(8,128)(2,1)S(1)}, bf16[64,1536]{1,0:T(8,128)(2,1)S(1)}, u32[]{:S(2)}, u32[]{:S(2)}) collective-permute-start(bf16[64,1536]{1,0:T(8,128)(2,1)S(1)} %get-tuple-element.41), channel_id=1, source_target_pairs={{0,1},{1,0},{2,3},{3,2},{4,5},{5,4},{6,7},{7,6},{8,9},{9,8},{10,11... | collective-permute-start | bytes 589832 | tf_op jit(solution)/shard_map/ppermute | solution.py:301
  2.4 8.3 %collective-permute-start.1 = (bf16[64,1024]{1,0:T(8,128)(2,1)S(1)}, bf16[64,1024]{1,0:T(8,128)(2,1)S(1)}, u32[]{:S(2)}, u32[]{:S(2)}) collective-permute-start(bf16[64,1024]{1,0:T(8,128)(2,1)S(1)} %get-tuple-element.40.refs_3_), channel_id=1, source_target_pairs={{0,15},{1,2},{2,1},{3,4},{4,3},{5,6},{6,5},{7,8},{8,7},{9,10},{10,... | collective-permute-start | bytes 393224 | tf_op jit(solution)/shard_map/ppermute | solution.py:300
  8.0 5.1 %collective-permute-start.2 = (bf16[64,128]{1,0:T(8,128)(2,1)S(1)}, bf16[64,128]{1,0:T(8,128)(2,1)S(1)}, u32[]{:S(2)}, u32[]{:S(2)}) collective-permute-start(bf16[64,128]{1,0:T(8,128)(2,1)S(1)} %get-tuple-element.43.refs_7_), channel_id=1, source_target_pairs={{0,9},{1,10},{2,11},{3,8},{4,13},{5,14},{6,15},{7,12},{8,1},{9,2},... | collective-permute-start | bytes 49160 | tf_op jit(solution)/shard_map/ppermute | solution.py:313
  8.1 5.0 %collective-permute-start.3 = (bf16[64,128]{1,0:T(8,128)(2,1)S(1)}, bf16[64,128]{1,0:T(8,128)(2,1)S(1)}, u32[]{:S(2)}, u32[]{:S(2)}) collective-permute-start(bf16[64,128]{1,0:T(8,128)(2,1)S(1)} %get-tuple-element.44.refs_8_), channel_id=1, source_target_pairs={{0,8},{1,11},{2,10},{3,9},{4,12},{5,15},{6,14},{7,13},{8,0},{9,3},... | collective-permute-start | bytes 49160 | tf_op jit(solution)/shard_map/ppermute | solution.py:313
  13.7 3.4 %collective-permute-start.4 = (bf16[64,1536]{1,0:T(8,128)(2,1)S(1)}, bf16[64,1536]{1,0:T(8,128)(2,1)S(1)}, u32[]{:S(2)}, u32[]{:S(2)}) collective-permute-start(bf16[64,1536]{1,0:T(8,128)(2,1)S(1)} %get-tuple-element.51), channel_id=1, source_target_pairs={{0,1},{1,0},{2,3},{3,2},{4,5},{5,4},{6,7},{7,6},{8,9},{9,8},{10,11... | collective-permute-start | bytes 589832 | tf_op jit(solution)/shard_map/ppermute | solution.py:301
  14.8 7.1 %collective-permute-start.5 = (bf16[64,1024]{1,0:T(8,128)(2,1)S(1)}, bf16[64,1024]{1,0:T(8,128)(2,1)S(1)}, u32[]{:S(2)}, u32[]{:S(2)}) collective-permute-start(bf16[64,1024]{1,0:T(8,128)(2,1)S(1)} %get-tuple-element.50.refs_1_), channel_id=1, source_target_pairs={{0,15},{1,2},{2,1},{3,4},{4,3},{5,6},{6,5},{7,8},{8,7},{9,10},{10,... | collective-permute-start | bytes 393224 | tf_op jit(solution)/shard_map/ppermute | solution.py:300
  17.1 5.3 %collective-permute-start.6 = (bf16[64,128]{1,0:T(8,128)(2,1)S(1)}, bf16[64,128]{1,0:T(8,128)(2,1)S(1)}, u32[]{:S(2)}, u32[]{:S(2)}) collective-permute-start(bf16[64,128]{1,0:T(8,128)(2,1)S(1)} %get-tuple-element.53.refs_4_), channel_id=1, source_target_pairs={{0,9},{1,10},{2,11},{3,8},{4,13},{5,14},{6,15},{7,12},{8,1},{9,2},... | collective-permute-start | bytes 49160 | tf_op jit(solution)/shard_map/ppermute | solution.py:313
  17.4 5.0 %collective-permute-start.7 = (bf16[64,128]{1,0:T(8,128)(2,1)S(1)}, bf16[64,128]{1,0:T(8,128)(2,1)S(1)}, u32[]{:S(2)}, u32[]{:S(2)}) collective-permute-start(bf16[64,128]{1,0:T(8,128)(2,1)S(1)} %get-tuple-element.54.refs_5_), channel_id=1, source_target_pairs={{0,8},{1,11},{2,10},{3,9},{4,12},{5,15},{6,14},{7,13},{8,0},{9,3},... | collective-permute-start | bytes 49160 | tf_op jit(solution)/shard_map/ppermute | solution.py:313
  23.0 2.9 %collective-permute-start.8 = (bf16[64,1536]{1,0:T(8,128)(2,1)S(1)}, bf16[64,1536]{1,0:T(8,128)(2,1)S(1)}, u32[]{:S(2)}, u32[]{:S(2)}) collective-permute-start(bf16[64,1536]{1,0:T(8,128)(2,1)S(1)} %get-tuple-element.57), channel_id=1, source_target_pairs={{0,1},{1,0},{2,3},{3,2},{4,5},{5,4},{6,7},{7,6},{8,9},{9,8},{10,11... | collective-permute-start | bytes 589832 | tf_op jit(solution)/shard_map/ppermute | solution.py:301
  23.5 7.4 %collective-permute-start.9 = (bf16[64,1024]{1,0:T(8,128)(2,1)S(1)}, bf16[64,1024]{1,0:T(8,128)(2,1)S(1)}, u32[]{:S(2)}, u32[]{:S(2)}) collective-permute-start(bf16[64,1024]{1,0:T(8,128)(2,1)S(1)} %get-tuple-element.56.refs_1_), channel_id=1, source_target_pairs={{0,15},{1,2},{2,1},{3,4},{4,3},{5,6},{6,5},{7,8},{8,7},{9,10},{10,... | collective-permute-start | bytes 393224 | tf_op jit(solution)/shard_map/ppermute | solution.py:300
  25.9 5.5 %collective-permute-start.10 = (bf16[64,128]{1,0:T(8,128)(2,1)S(1)}, bf16[64,128]{1,0:T(8,128)(2,1)S(1)}, u32[]{:S(2)}, u32[]{:S(2)}) collective-permute-start(bf16[64,128]{1,0:T(8,128)(2,1)S(1)} %get-tuple-element.59.refs_4_), channel_id=1, source_target_pairs={{0,9},{1,10},{2,11},{3,8},{4,13},{5,14},{6,15},{7,12},{8,1},{9,2},... | collective-permute-start | bytes 49160 | tf_op jit(solution)/shard_map/ppermute | solution.py:313
  26.5 4.9 %collective-permute-start.11 = (bf16[64,128]{1,0:T(8,128)(2,1)S(1)}, bf16[64,128]{1,0:T(8,128)(2,1)S(1)}, u32[]{:S(2)}, u32[]{:S(2)}) collective-permute-start(bf16[64,128]{1,0:T(8,128)(2,1)S(1)} %get-tuple-element.60.refs_5_), channel_id=1, source_target_pairs={{0,8},{1,11},{2,10},{3,9},{4,12},{5,15},{6,14},{7,13},{8,0},{9,3},... | collective-permute-start | bytes 49160 | tf_op jit(solution)/shard_map/ppermute | solution.py:313
  32.0 3.2 %collective-permute-start.12 = (bf16[64,1536]{1,0:T(8,128)(2,1)S(1)}, bf16[64,1536]{1,0:T(8,128)(2,1)S(1)}, u32[]{:S(2)}, u32[]{:S(2)}) collective-permute-start(bf16[64,1536]{1,0:T(8,128)(2,1)S(1)} %get-tuple-element.64), channel_id=1, source_target_pairs={{0,1},{1,0},{2,3},{3,2},{4,5},{5,4},{6,7},{7,6},{8,9},{9,8},{10,11... | collective-permute-start | bytes 589832 | tf_op jit(solution)/shard_map/ppermute | solution.py:301
  32.7 7.4 %collective-permute-start.13 = (bf16[64,1024]{1,0:T(8,128)(2,1)S(1)}, bf16[64,1024]{1,0:T(8,128)(2,1)S(1)}, u32[]{:S(2)}, u32[]{:S(2)}) collective-permute-start(bf16[64,1024]{1,0:T(8,128)(2,1)S(1)} %get-tuple-element.63.refs_1_), channel_id=1, source_target_pairs={{0,15},{1,2},{2,1},{3,4},{4,3},{5,6},{6,5},{7,8},{8,7},{9,10},{10,... | collective-permute-start | bytes 393224 | tf_op jit(solution)/shard_map/ppermute | solution.py:300
  35.2 5.4 %collective-permute-start.14 = (bf16[64,128]{1,0:T(8,128)(2,1)S(1)}, bf16[64,128]{1,0:T(8,128)(2,1)S(1)}, u32[]{:S(2)}, u32[]{:S(2)}) collective-permute-start(bf16[64,128]{1,0:T(8,128)(2,1)S(1)} %get-tuple-element.66.refs_4_), channel_id=1, source_target_pairs={{0,9},{1,10},{2,11},{3,8},{4,13},{5,14},{6,15},{7,12},{8,1},{9,2},... | collective-permute-start | bytes 49160 | tf_op jit(solution)/shard_map/ppermute | solution.py:313
  35.3 5.3 %collective-permute-start.15 = (bf16[64,128]{1,0:T(8,128)(2,1)S(1)}, bf16[64,128]{1,0:T(8,128)(2,1)S(1)}, u32[]{:S(2)}, u32[]{:S(2)}) collective-permute-start(bf16[64,128]{1,0:T(8,128)(2,1)S(1)} %get-tuple-element.67.refs_5_), channel_id=1, source_target_pairs={{0,8},{1,11},{2,10},{3,9},{4,12},{5,15},{6,14},{7,13},{8,0},{9,3},... | collective-permute-start | bytes 49160 | tf_op jit(solution)/shard_map/ppermute | solution.py:313

commit v22 on v20

--- a/solution.py
+++ b/solution.py
@@ -11,7 +11,7 @@
 REACH = 4
 LEVELS = 3
 SPAN = 2 * REACH + 1
-OTHER_CORE_FIRST = 0b11011111
+TURNED = 0b00011000
 
 F32 = jnp.float32
 BF16 = jnp.bfloat16
@@ -55,7 +55,7 @@
         places = [(l, m) for l in range(loop_size) for m in range(members)]
         self.across = [
             [
-                (l * members + m, self.far_target(l, m)[turn])
+                (l * members + m, (l + self.hops[0]) % loop_size * members + self.far_target(l, m)[turn])
                 for l, m in places
             ]
             for turn in range(2)
@@ -69,17 +69,16 @@
     def far_target(self, loop_index, member):
         block = (loop_index + self.hops[0]) % self.loop_size
         pair, core = divmod(member, 2)
-        chip = block * 2 + (pair ^ core)
-        first = core ^ (OTHER_CORE_FIRST >> chip & 1)
-        return 2 * chip + first, 2 * chip + (first ^ 1)
+        chip = block * 2 + core
+        first = pair ^ (TURNED >> chip & 1)
+        return 2 * chip % self.members + first, 2 * chip % self.members + (first ^ 1)
 
     def first_is_odd(self, index_ref):
         index = index_ref[0]
         block = lax.rem(lax.div(index, self.members) + self.hops[0], self.loop_size)
         pair, core = lax.div(self.member(index_ref), 2), lax.rem(index, 2)
-        chip = block * 2 + lax.bitwise_xor(pair, core)
-        swapped = lax.bitwise_and(lax.shift_right_logical(jnp.int32(OTHER_CORE_FIRST), chip), 1)
-        return lax.bitwise_xor(core, swapped) == 1
+        turned = lax.bitwise_and(lax.shift_right_logical(jnp.int32(TURNED), block * 2 + core), 1)
+        return lax.bitwise_xor(pair, turned) == 1
 
     def panel(self, ref, c):
         return ref[:, c * self.size : (c + 1) * self.size]
@@ -99,7 +98,7 @@
         message_ref, keep_ref = out_refs
         (total,) = totals
         member = self.member(index_ref)
-        second = lax.rem(member, 2) != lax.div(member, 2)
+        second = lax.rem(member, 2) == 1
         first, last = total[:, : 2 * self.width], total[:, 2 * self.width :]
         keep_ref[...] = jnp.where(second, last, first)
         upper, lower = halves(jnp.where(second, first, last))
@@ -314,7 +313,7 @@
                 scratch=scratch_for(far_rows, far_cols, col_basis, couplings)
                 + [pltpu.VMEM(matrix[:2] + (width,), F32), pltpu.SemaphoreType.DMA((7,))],
             )
-        over = lax.ppermute(block if product == 0 else current, axes, plan.over)
+        over = lax.ppermute(current, axes, plan.over)
         near = lax.ppermute(sends[0] if plan.paired else current, axes, plan.near)
         if plan.paired:
             sends = call(

time: 41.9 us -> 42.3 us (level)
  starting transfers between devices: 19.5 us -> 25 us
  waiting for transfers between devices: 9.83 us -> 4.62 us
    ppermute x8, starting transfers between devices: 2.71 us -> 11.9 us  [on_device(): fars = [lax.ppermute(s, axes, route) for s, route in zip(sends, routes)]]
    ppermute x4, waiting for transfers between devices: 6.84 us -> 2.57 us  [on_device(): over = lax.ppermute(current, axes, plan.over)]
    ppermute x4, starting transfers between devices: 15.2 us -> 12.4 us  [on_device(): over = lax.ppermute(current, axes, plan.over)]
    ppermute x8, waiting for transfers between devices: 2.98 us -> 2.04 us  [on_device(): fars = [lax.ppermute(s, axes, route) for s, route in zip(sends, routes)]]
    ppermute x4, starting transfers between devices: 1.57 us -> 0.73 us  [on_device(): near = lax.ppermute(sends[0] if plan.paired else current, axes, plan.near)]
  transfers between devices with their start and end apart: 16 -> 16, of which waited for: 8 -> 7; matrix products, arithmetic and copies ran while one was open for 0% -> 0% of each run, Pallas kernels for 19% -> 19%
where the time goes in v22:
time: 42.3 us; the launch traced here: 42.1 us
  starting transfers between devices  25 us (59%)
  Pallas kernels  12.3 us (29%)
  waiting for transfers between devices  4.62 us (11%)
    ppermute x4, starting transfers between devices, on_device(): over = lax.ppermute(current, axes, plan.over)  12.4 us
    pallas_call x17, Pallas kernels, call(): pl.pallas_call(kernel, in_specs=list(specs), out_specs=out_specs or [IN_V...  12.3 us
    ppermute x8, starting transfers between devices, on_device(): fars = [lax.ppermute(s, axes, route) for s, route in zip(sends, routes)]  11.9 us
    ppermute x4, waiting for transfers between devices, on_device(): over = lax.ppermute(current, axes, plan.over)  2.57 us
    ppermute x8, waiting for transfers between devices, on_device(): fars = [lax.ppermute(s, axes, route) for s, route in zip(sends, routes)]  2.04 us
  transfers between devices with their start and end apart: 16, of which 7 were waited for; matrix products, arithmetic and copies ran while one was open for 0% of the time, Pallas kernels for 19%

profile of v22, /device:TPU:0, one launch (start us, length us, event | category | flops | bytes accessed | tf_op | source)
XLA Modules:
  0.0 42.1 jit_solution(62901069433972131)
XLA Ops:
  0.0 0.0 copy-start.1
  0.0 0.0 copy-start
  0.0 1.8 %prepare.1 = (bf16[64,1024]{1,0:T(8,128)(2,1)S(1)}, bf16[1,512,256]{2,1,0:T(8,128)(2,1)S(1)}, bf16[128,1024]{1,0:T(8,128)(2,1)S(1)}, s32[32]{0:T(128)S(4)}, s32[...) custom-call(s32[1]{0:T(128)} %bitcast.index_ref.refs_0_, s32[32]{0:T(128)} %refs_0_.1, s32[32]{0:T(128)} %refs_1_.1, ...), custom_call_target="tpu_custom_call" | custom-call | flops 1000000000 | bytes 4194304 | tf_op jit(solution)/shard_map/prepare/pallas_call | solution.py:255
  1.8 0.5 %collective-permute-start = (bf16[64,1536]{1,0:T(8,128)(2,1)S(1)}, bf16[64,1536]{1,0:T(8,128)(2,1)S(1)}, u32[]{:S(2)}, u32[]{:S(2)}) collective-permute-start(bf16[64,1536]{1,0:T(8,128)(2,1)S(1)} %get-tuple-element.41), channel_id=1, source_target_pairs={{0,1},{1,0},{2,3},{3,2},{4,5},{5,4},{6,7},{7,6},{8,9},{9,8},{10,11... | collective-permute-start | bytes 589832 | tf_op jit(solution)/shard_map/ppermute | solution.py:317
  2.4 5.6 %collective-permute-start.1 = (bf16[64,1024]{1,0:T(8,128)(2,1)S(1)}, bf16[64,1024]{1,0:T(8,128)(2,1)S(1)}, u32[]{:S(2)}, u32[]{:S(2)}) collective-permute-start(bf16[64,1024]{1,0:T(8,128)(2,1)S(1)} %get-tuple-element.40.refs_3_), channel_id=1, source_target_pairs={{0,15},{1,2},{2,1},{3,4},{4,3},{5,6},{6,5},{7,8},{8,7},{9,10},{10,... | collective-permute-start | bytes 393224 | tf_op jit(solution)/shard_map/ppermute | solution.py:316
  8.0 0.0 collective-permute-done.message_ref.refs_4_
  8.0 0.1 collective-permute-start.2
  8.1 2.9 %collective-permute-start.3 = (bf16[64,128]{1,0:T(8,128)(2,1)S(1)}, bf16[64,128]{1,0:T(8,128)(2,1)S(1)}, u32[]{:S(2)}, u32[]{:S(2)}) collective-permute-start(bf16[64,128]{1,0:T(8,128)(2,1)S(1)} %get-tuple-element.44.refs_8_), channel_id=1, source_target_pairs={{0,8},{1,11},{2,9},{3,10},{4,13},{5,15},{6,12},{7,14},{8,1},{9,3},... | collective-permute-start | bytes 49160 | tf_op jit(solution)/shard_map/ppermute | solution.py:329
  11.0 0.0 copy-done.1
  11.0 0.0 copy-done
  11.0 1.9 %first_own.1 = (f32[64,1024]{1,0:T(8,128)S(1)}, bf16[36,256,256]{2,1,0:T(8,128)(2,1)S(1)}, bf16[256,1024]{1,0:T(8,128)(2,1)S(1)}) custom-call(s32[1]{0:T(128)} %bitcast.index_ref.refs_0_, s32[32]{0:T(128)S(4)} %get-tuple-element.38.refs_1_, s32[32]{0:T(128)S(4)} %get-tuple-element.39.refs_2_, bf16[64,1024]{1,0:T(8,128)(2,1)S(1)} %get-tuple-element.40.refs_3_, ...), custom_call_target="tpu_custom_call" | custom-call | flops 1000000000 | bytes 4194304 | tf_op jit(solution)/shard_map/first_own/pallas_call | solution.py:255
  12.9 0.0 collective-permute-done.1.over_ref
  12.9 0.5 %halo.4.refs_1_ = f32[64,1024]{1,0:T(8,128)S(1)} custom-call(s32[1]{0:T(128)} %bitcast.index_ref.refs_0_, f32[64,1024]{1,0:T(8,128)S(1)} %get-tuple-element.45.acc_ref, bf16[64,1024]{1,0:T(8,128)(2,1)S(1)} %collective-permute-done.1.over_ref, bf16[36,256,256]{2,1,0:T(8,128)(2,1)S(1)} %get-tuple-element.46.d_ref.refs_3_), custom_call_target="tpu_custom_call" | custom-call | flops 1000000000 | bytes 4194304 | tf_op jit(solution)/shard_map/halo/pallas_call | solution.py:255
  13.4 0.0 collective-permute-done.2.refs_5_
  13.4 0.3 collective-permute-done.3.refs_6_
  13.7 0.6 %finish.3 = (bf16[64,1024]{1,0:T(8,128)(2,1)S(1)}, bf16[64,1536]{1,0:T(8,128)(2,1)S(1)}, f32[64,256]{1,0:T(8,128)S(1)}) custom-call(s32[1]{0:T(128)} %bitcast.index_ref.refs_0_, f32[64,1024]{1,0:T(8,128)S(1)} %halo.4.refs_1_, bf16[256,1024]{1,0:T(8,128)(2,1)S(1)} %get-tuple-element.47.refs_2_.refs_1_, bf16[128,1024]{1,0:T(8,128)(2,1)S(1)} %get-tuple-element.48.refs_3_, ...), custom_call_target="tpu_custom_call" | custom-call | flops 1000000000 | bytes 4194304 | tf_op jit(solution)/shard_map/finish/pallas_call | solution.py:255
  14.3 0.1 collective-permute-start.4
  14.4 2.7 %collective-permute-start.5 = (bf16[64,1024]{1,0:T(8,128)(2,1)S(1)}, bf16[64,1024]{1,0:T(8,128)(2,1)S(1)}, u32[]{:S(2)}, u32[]{:S(2)}) collective-permute-start(bf16[64,1024]{1,0:T(8,128)(2,1)S(1)} %get-tuple-element.50.refs_1_), channel_id=1, source_target_pairs={{0,15},{1,2},{2,1},{3,4},{4,3},{5,6},{6,5},{7,8},{8,7},{9,10},{10,... | collective-permute-start | bytes 393224 | tf_op jit(solution)/shard_map/ppermute | solution.py:316
  17.1 0.0 collective-permute-done.4.message_ref.refs_2_
  17.1 0.4 %collective-permute-start.6 = (bf16[64,128]{1,0:T(8,128)(2,1)S(1)}, bf16[64,128]{1,0:T(8,128)(2,1)S(1)}, u32[]{:S(2)}, u32[]{:S(2)}) collective-permute-start(bf16[64,128]{1,0:T(8,128)(2,1)S(1)} %get-tuple-element.53.refs_4_), channel_id=1, source_target_pairs={{0,9},{1,10},{2,8},{3,11},{4,12},{5,14},{6,13},{7,15},{8,0},{9,2},... | collective-permute-start | bytes 49160 | tf_op jit(solution)/shard_map/ppermute | solution.py:329
  17.6 2.5 %collective-permute-start.7 = (bf16[64,128]{1,0:T(8,128)(2,1)S(1)}, bf16[64,128]{1,0:T(8,128)(2,1)S(1)}, u32[]{:S(2)}, u32[]{:S(2)}) collective-permute-start(bf16[64,128]{1,0:T(8,128)(2,1)S(1)} %get-tuple-element.54.refs_5_), channel_id=1, source_target_pairs={{0,8},{1,11},{2,9},{3,10},{4,13},{5,15},{6,12},{7,14},{8,1},{9,3},... | collective-permute-start | bytes 49160 | tf_op jit(solution)/shard_map/ppermute | solution.py:329
  20.1 1.3 %own.3 = (f32[64,1024]{1,0:T(8,128)S(1)}, bf16[4,64,1024]{2,1,0:T(8,128)(2,1)}) custom-call(s32[1]{0:T(128)} %bitcast.index_ref.refs_0_, bf16[64,1024]{1,0:T(8,128)(2,1)S(1)} %get-tuple-element.50.refs_1_, bf16[64,1536]{1,0:T(8,128)(2,1)S(1)} %collective-permute-done.4.message_ref.refs_2_, bf16[36,256,256]{2,1,0:T(8,128)(2,1)S(1)} %get-tuple-element.46.d_ref.refs_3_, ...), custom_call_target="tpu_custom_call" | custom-call | flops 1000000000 | bytes 4194304 | tf_op jit(solution)/shard_map/own/pallas_call | solution.py:255
  21.4 0.3 collective-permute-done.5.over_ref
  21.7 0.5 %halo.5.refs_1_ = f32[64,1024]{1,0:T(8,128)S(1)} custom-call(s32[1]{0:T(128)} %bitcast.index_ref.refs_0_, f32[64,1024]{1,0:T(8,128)S(1)} %get-tuple-element.55.acc_ref, bf16[64,1024]{1,0:T(8,128)(2,1)S(1)} %collective-permute-done.5.over_ref, bf16[36,256,256]{2,1,0:T(8,128)(2,1)S(1)} %get-tuple-element.46.d_ref.refs_3_), custom_call_target="tpu_custom_call" | custom-call | flops 1000000000 | bytes 4194304 | tf_op jit(solution)/shard_map/halo/pallas_call | solution.py:255
  22.3 0.0 collective-permute-done.6.refs_5_
  22.3 0.9 %collective-permute-done.7.refs_6_ = bf16[64,128]{1,0:T(8,128)(2,1)S(1)} collective-permute-done((bf16[64,128]{1,0:T(8,128)(2,1)S(1)}, bf16[64,128]{1,0:T(8,128)(2,1)S(1)}, u32[]{:S(2)}, u32[]{:S(2)}) %collective-permute-start.7) | collective-permute-done | bytes 16416 | tf_op jit(solution)/shard_map/ppermute | solution.py:329
  23.2 0.6 %finish.4 = (bf16[64,1024]{1,0:T(8,128)(2,1)S(1)}, bf16[64,1536]{1,0:T(8,128)(2,1)S(1)}, f32[64,256]{1,0:T(8,128)S(1)}) custom-call(s32[1]{0:T(128)} %bitcast.index_ref.refs_0_, f32[64,1024]{1,0:T(8,128)S(1)} %halo.5.refs_1_, bf16[256,1024]{1,0:T(8,128)(2,1)S(1)} %get-tuple-element.47.refs_2_.refs_1_, bf16[128,1024]{1,0:T(8,128)(2,1)S(1)} %get-tuple-element.48.refs_3_, ...), custom_call_target="tpu_custom_call" | custom-call | flops 1000000000 | bytes 4194304 | tf_op jit(solution)/shard_map/finish/pallas_call | solution.py:255
  23.8 0.1 collective-permute-start.8
  23.9 2.0 %collective-permute-start.9 = (bf16[64,1024]{1,0:T(8,128)(2,1)S(1)}, bf16[64,1024]{1,0:T(8,128)(2,1)S(1)}, u32[]{:S(2)}, u32[]{:S(2)}) collective-permute-start(bf16[64,1024]{1,0:T(8,128)(2,1)S(1)} %get-tuple-element.56.refs_1_), channel_id=1, source_target_pairs={{0,15},{1,2},{2,1},{3,4},{4,3},{5,6},{6,5},{7,8},{8,7},{9,10},{10,... | collective-permute-start | bytes 393224 | tf_op jit(solution)/shard_map/ppermute | solution.py:316
  25.9 0.0 collective-permute-done.8.message_ref.refs_2_
  25.9 0.7 %collective-permute-start.10 = (bf16[64,128]{1,0:T(8,128)(2,1)S(1)}, bf16[64,128]{1,0:T(8,128)(2,1)S(1)}, u32[]{:S(2)}, u32[]{:S(2)}) collective-permute-start(bf16[64,128]{1,0:T(8,128)(2,1)S(1)} %get-tuple-element.59.refs_4_), channel_id=1, source_target_pairs={{0,9},{1,10},{2,8},{3,11},{4,12},{5,14},{6,13},{7,15},{8,0},{9,2},... | collective-permute-start | bytes 49160 | tf_op jit(solution)/shard_map/ppermute | solution.py:329
  26.7 2.3 %collective-permute-start.11 = (bf16[64,128]{1,0:T(8,128)(2,1)S(1)}, bf16[64,128]{1,0:T(8,128)(2,1)S(1)}, u32[]{:S(2)}, u32[]{:S(2)}) collective-permute-start(bf16[64,128]{1,0:T(8,128)(2,1)S(1)} %get-tuple-element.60.refs_5_), channel_id=1, source_target_pairs={{0,8},{1,11},{2,9},{3,10},{4,13},{5,15},{6,12},{7,14},{8,1},{9,3},... | collective-permute-start | bytes 49160 | tf_op jit(solution)/shard_map/ppermute | solution.py:329
  28.9 1.3 %own.4 = (f32[64,1024]{1,0:T(8,128)S(1)}, bf16[4,64,1024]{2,1,0:T(8,128)(2,1)}) custom-call(s32[1]{0:T(128)} %bitcast.index_ref.refs_0_, bf16[64,1024]{1,0:T(8,128)(2,1)S(1)} %get-tuple-element.56.refs_1_, bf16[64,1536]{1,0:T(8,128)(2,1)S(1)} %collective-permute-done.8.message_ref.refs_2_, ...), custom_call_target="tpu_custom_call", output_to_operand_aliasing={{1}: (6, {})} | custom-call | flops 1000000000 | bytes 4194304 | tf_op jit(solution)/shard_map/own/pallas_call | solution.py:255
  30.2 1.1 %collective-permute-done.9.over_ref = bf16[64,1024]{1,0:T(8,128)(2,1)S(1)} collective-permute-done((bf16[64,1024]{1,0:T(8,128)(2,1)S(1)}, bf16[64,1024]{1,0:T(8,128)(2,1)S(1)}, u32[]{:S(2)}, u32[]{:S(2)}) %collective-permute-start.9) | collective-permute-done | bytes 131104 | tf_op jit(solution)/shard_map/ppermute | solution.py:316
  31.3 0.5 %halo.6.refs_1_ = f32[64,1024]{1,0:T(8,128)S(1)} custom-call(s32[1]{0:T(128)} %bitcast.index_ref.refs_0_, f32[64,1024]{1,0:T(8,128)S(1)} %get-tuple-element.62.acc_ref, bf16[64,1024]{1,0:T(8,128)(2,1)S(1)} %collective-permute-done.9.over_ref, bf16[36,256,256]{2,1,0:T(8,128)(2,1)S(1)} %get-tuple-element.46.d_ref.refs_3_), custom_call_target="tpu_custom_call" | custom-call | flops 1000000000 | bytes 4194304 | tf_op jit(solution)/shard_map/halo/pallas_call | solution.py:255
  31.8 0.0 collective-permute-done.10.refs_5_
  31.8 0.7 %collective-permute-done.11.refs_6_ = bf16[64,128]{1,0:T(8,128)(2,1)S(1)} collective-permute-done((bf16[64,128]{1,0:T(8,128)(2,1)S(1)}, bf16[64,128]{1,0:T(8,128)(2,1)S(1)}, u32[]{:S(2)}, u32[]{:S(2)}) %collective-permute-start.11) | collective-permute-done | bytes 16416 | tf_op jit(solution)/shard_map/ppermute | solution.py:329
  32.5 0.6 %finish.5 = (bf16[64,1024]{1,0:T(8,128)(2,1)S(1)}, bf16[64,1536]{1,0:T(8,128)(2,1)S(1)}, f32[64,256]{1,0:T(8,128)S(1)}) custom-call(s32[1]{0:T(128)} %bitcast.index_ref.refs_0_, f32[64,1024]{1,0:T(8,128)S(1)} %halo.6.refs_1_, bf16[256,1024]{1,0:T(8,128)(2,1)S(1)} %get-tuple-element.47.refs_2_.refs_1_, bf16[128,1024]{1,0:T(8,128)(2,1)S(1)} %get-tuple-element.48.refs_3_, ...), custom_call_target="tpu_custom_call" | custom-call | flops 1000000000 | bytes 4194304 | tf_op jit(solution)/shard_map/finish/pallas_call | solution.py:255
  33.1 0.1 collective-permute-start.12
  33.2 2.0 %collective-permute-start.13 = (bf16[64,1024]{1,0:T(8,128)(2,1)S(1)}, bf16[64,1024]{1,0:T(8,128)(2,1)S(1)}, u32[]{:S(2)}, u32[]{:S(2)}) collective-permute-start(bf16[64,1024]{1,0:T(8,128)(2,1)S(1)} %get-tuple-element.63.refs_1_), channel_id=1, source_target_pairs={{0,15},{1,2},{2,1},{3,4},{4,3},{5,6},{6,5},{7,8},{8,7},{9,10},{10,... | collective-permute-start | bytes 393224 | tf_op jit(solution)/shard_map/ppermute | solution.py:316
  35.2 0.0 collective-permute-done.12.message_ref.refs_2_
  35.2 0.3 collective-permute-start.14
  35.5 2.7 %collective-permute-start.15 = (bf16[64,128]{1,0:T(8,128)(2,1)S(1)}, bf16[64,128]{1,0:T(8,128)(2,1)S(1)}, u32[]{:S(2)}, u32[]{:S(2)}) collective-permute-start(bf16[64,128]{1,0:T(8,128)(2,1)S(1)} %get-tuple-element.67.refs_5_), channel_id=1, source_target_pairs={{0,8},{1,11},{2,9},{3,10},{4,13},{5,15},{6,12},{7,14},{8,1},{9,3},... | collective-permute-start | bytes 49160 | tf_op jit(solution)/shard_map/ppermute | solution.py:329
  38.2 1.3 %own.5 = (f32[64,1024]{1,0:T(8,128)S(1)}, bf16[4,64,1024]{2,1,0:T(8,128)(2,1)}) custom-call(s32[1]{0:T(128)} %bitcast.index_ref.refs_0_, bf16[64,1024]{1,0:T(8,128)(2,1)S(1)} %get-tuple-element.63.refs_1_, bf16[64,1536]{1,0:T(8,128)(2,1)S(1)} %collective-permute-done.12.message_ref.refs_2_, ...), custom_call_target="tpu_custom_call", output_to_operand_aliasing={{1}: (6, {})} | custom-call | flops 1000000000 | bytes 4194304 | tf_op jit(solution)/shard_map/own/pallas_call | solution.py:255
  39.5 1.2 %collective-permute-done.13.over_ref = bf16[64,1024]{1,0:T(8,128)(2,1)S(1)} collective-permute-done((bf16[64,1024]{1,0:T(8,128)(2,1)S(1)}, bf16[64,1024]{1,0:T(8,128)(2,1)S(1)}, u32[]{:S(2)}, u32[]{:S(2)}) %collective-permute-start.13) | collective-permute-done | bytes 131104 | tf_op jit(solution)/shard_map/ppermute | solution.py:316
  40.6 0.5 %halo.7.refs_0_ = f32[64,1024]{1,0:T(8,128)S(1)} custom-call(s32[1]{0:T(128)} %bitcast.index_ref.refs_0_, f32[64,1024]{1,0:T(8,128)S(1)} %get-tuple-element.69.acc_ref, bf16[64,1024]{1,0:T(8,128)(2,1)S(1)} %collective-permute-done.13.over_ref, bf16[36,256,256]{2,1,0:T(8,128)(2,1)S(1)} %get-tuple-element.46.d_ref.refs_3_), custom_call_target="tpu_custom_call" | custom-call | flops 1000000000 | bytes 4194304 | tf_op jit(solution)/shard_map/halo/pallas_call | solution.py:255
  41.1 0.0 collective-permute-done.14.refs_2_
  41.2 0.1 collective-permute-done.15.refs_3_
  41.2 0.9 %last.1 = bf16[4,64,1024]{2,1,0:T(8,128)(2,1)} custom-call(f32[64,1024]{1,0:T(8,128)S(1)} %halo.7.refs_0_, bf16[256,1024]{1,0:T(8,128)(2,1)S(1)} %get-tuple-element.47.refs_2_.refs_1_, bf16[64,128]{1,0:T(8,128)(2,1)S(1)} %collective-permute-done.14.refs_2_, bf16[64,128]{1,0:T(8,128)(2,1)S(1)} %collective-permute-done.15.refs_3_, ...), custom_call_target="tpu_custom_call", output_to_operand_aliasing={{}: (4, {})} | custom-call | flops 1000000000 | bytes 4194304 | tf_op jit(solution)/shard_map/last/pallas_call | solution.py:255
  (4 shorter events, 0.1 us)
Async XLA Ops:
  0.0 11.0 %copy-start.1 = (bf16[4,32,256]{2,1,0:T(8,128)(2,1)S(1)}, bf16[4,32,256]{2,1,0:T(8,128)(2,1)}, u32[]{:S(2)}) copy-start(bf16[4,32,256]{2,1,0:T(8,128)(2,1)} %refs_5_.3) | copy-start | bytes 196612
  0.0 11.0 %copy-start = (bf16[32,256,256]{2,1,0:T(8,128)(2,1)S(1)}, bf16[32,256,256]{2,1,0:T(8,128)(2,1)}, u32[]{:S(2)}) copy-start(bf16[32,256,256]{2,1,0:T(8,128)(2,1)} %refs_6_.3) | copy-start | bytes 12582916
  1.8 6.2 %collective-permute-start = (bf16[64,1536]{1,0:T(8,128)(2,1)S(1)}, bf16[64,1536]{1,0:T(8,128)(2,1)S(1)}, u32[]{:S(2)}, u32[]{:S(2)}) collective-permute-start(bf16[64,1536]{1,0:T(8,128)(2,1)S(1)} %get-tuple-element.41), channel_id=1, source_target_pairs={{0,1},{1,0},{2,3},{3,2},{4,5},{5,4},{6,7},{7,6},{8,9},{9,8},{10,11... | collective-permute-start | bytes 589832 | tf_op jit(solution)/shard_map/ppermute | solution.py:317
  2.4 10.5 %collective-permute-start.1 = (bf16[64,1024]{1,0:T(8,128)(2,1)S(1)}, bf16[64,1024]{1,0:T(8,128)(2,1)S(1)}, u32[]{:S(2)}, u32[]{:S(2)}) collective-permute-start(bf16[64,1024]{1,0:T(8,128)(2,1)S(1)} %get-tuple-element.40.refs_3_), channel_id=1, source_target_pairs={{0,15},{1,2},{2,1},{3,4},{4,3},{5,6},{6,5},{7,8},{8,7},{9,10},{10,... | collective-permute-start | bytes 393224 | tf_op jit(solution)/shard_map/ppermute | solution.py:316
  8.0 5.4 %collective-permute-start.2 = (bf16[64,128]{1,0:T(8,128)(2,1)S(1)}, bf16[64,128]{1,0:T(8,128)(2,1)S(1)}, u32[]{:S(2)}, u32[]{:S(2)}) collective-permute-start(bf16[64,128]{1,0:T(8,128)(2,1)S(1)} %get-tuple-element.43.refs_7_), channel_id=1, source_target_pairs={{0,9},{1,10},{2,8},{3,11},{4,12},{5,14},{6,13},{7,15},{8,0},{9,2},... | collective-permute-start | bytes 49160 | tf_op jit(solution)/shard_map/ppermute | solution.py:329
  8.1 5.6 %collective-permute-start.3 = (bf16[64,128]{1,0:T(8,128)(2,1)S(1)}, bf16[64,128]{1,0:T(8,128)(2,1)S(1)}, u32[]{:S(2)}, u32[]{:S(2)}) collective-permute-start(bf16[64,128]{1,0:T(8,128)(2,1)S(1)} %get-tuple-element.44.refs_8_), channel_id=1, source_target_pairs={{0,8},{1,11},{2,9},{3,10},{4,13},{5,15},{6,12},{7,14},{8,1},{9,3},... | collective-permute-start | bytes 49160 | tf_op jit(solution)/shard_map/ppermute | solution.py:329
  14.3 2.8 %collective-permute-start.4 = (bf16[64,1536]{1,0:T(8,128)(2,1)S(1)}, bf16[64,1536]{1,0:T(8,128)(2,1)S(1)}, u32[]{:S(2)}, u32[]{:S(2)}) collective-permute-start(bf16[64,1536]{1,0:T(8,128)(2,1)S(1)} %get-tuple-element.51), channel_id=1, source_target_pairs={{0,1},{1,0},{2,3},{3,2},{4,5},{5,4},{6,7},{7,6},{8,9},{9,8},{10,11... | collective-permute-start | bytes 589832 | tf_op jit(solution)/shard_map/ppermute | solution.py:317
  14.4 7.4 %collective-permute-start.5 = (bf16[64,1024]{1,0:T(8,128)(2,1)S(1)}, bf16[64,1024]{1,0:T(8,128)(2,1)S(1)}, u32[]{:S(2)}, u32[]{:S(2)}) collective-permute-start(bf16[64,1024]{1,0:T(8,128)(2,1)S(1)} %get-tuple-element.50.refs_1_), channel_id=1, source_target_pairs={{0,15},{1,2},{2,1},{3,4},{4,3},{5,6},{6,5},{7,8},{8,7},{9,10},{10,... | collective-permute-start | bytes 393224 | tf_op jit(solution)/shard_map/ppermute | solution.py:316
  17.1 5.1 %collective-permute-start.6 = (bf16[64,128]{1,0:T(8,128)(2,1)S(1)}, bf16[64,128]{1,0:T(8,128)(2,1)S(1)}, u32[]{:S(2)}, u32[]{:S(2)}) collective-permute-start(bf16[64,128]{1,0:T(8,128)(2,1)S(1)} %get-tuple-element.53.refs_4_), channel_id=1, source_target_pairs={{0,9},{1,10},{2,8},{3,11},{4,12},{5,14},{6,13},{7,15},{8,0},{9,2},... | collective-permute-start | bytes 49160 | tf_op jit(solution)/shard_map/ppermute | solution.py:329
  17.6 5.6 %collective-permute-start.7 = (bf16[64,128]{1,0:T(8,128)(2,1)S(1)}, bf16[64,128]{1,0:T(8,128)(2,1)S(1)}, u32[]{:S(2)}, u32[]{:S(2)}) collective-permute-start(bf16[64,128]{1,0:T(8,128)(2,1)S(1)} %get-tuple-element.54.refs_5_), channel_id=1, source_target_pairs={{0,8},{1,11},{2,9},{3,10},{4,13},{5,15},{6,12},{7,14},{8,1},{9,3},... | collective-permute-start | bytes 49160 | tf_op jit(solution)/shard_map/ppermute | solution.py:329
  23.8 2.1 %collective-permute-start.8 = (bf16[64,1536]{1,0:T(8,128)(2,1)S(1)}, bf16[64,1536]{1,0:T(8,128)(2,1)S(1)}, u32[]{:S(2)}, u32[]{:S(2)}) collective-permute-start(bf16[64,1536]{1,0:T(8,128)(2,1)S(1)} %get-tuple-element.57), channel_id=1, source_target_pairs={{0,1},{1,0},{2,3},{3,2},{4,5},{5,4},{6,7},{7,6},{8,9},{9,8},{10,11... | collective-permute-start | bytes 589832 | tf_op jit(solution)/shard_map/ppermute | solution.py:317
  23.9 7.4 %collective-permute-start.9 = (bf16[64,1024]{1,0:T(8,128)(2,1)S(1)}, bf16[64,1024]{1,0:T(8,128)(2,1)S(1)}, u32[]{:S(2)}, u32[]{:S(2)}) collective-permute-start(bf16[64,1024]{1,0:T(8,128)(2,1)S(1)} %get-tuple-element.56.refs_1_), channel_id=1, source_target_pairs={{0,15},{1,2},{2,1},{3,4},{4,3},{5,6},{6,5},{7,8},{8,7},{9,10},{10,... | collective-permute-start | bytes 393224 | tf_op jit(solution)/shard_map/ppermute | solution.py:316
  25.9 5.9 %collective-permute-start.10 = (bf16[64,128]{1,0:T(8,128)(2,1)S(1)}, bf16[64,128]{1,0:T(8,128)(2,1)S(1)}, u32[]{:S(2)}, u32[]{:S(2)}) collective-permute-start(bf16[64,128]{1,0:T(8,128)(2,1)S(1)} %get-tuple-element.59.refs_4_), channel_id=1, source_target_pairs={{0,9},{1,10},{2,8},{3,11},{4,12},{5,14},{6,13},{7,15},{8,0},{9,2},... | collective-permute-start | bytes 49160 | tf_op jit(solution)/shard_map/ppermute | solution.py:329
  26.7 5.9 %collective-permute-start.11 = (bf16[64,128]{1,0:T(8,128)(2,1)S(1)}, bf16[64,128]{1,0:T(8,128)(2,1)S(1)}, u32[]{:S(2)}, u32[]{:S(2)}) collective-permute-start(bf16[64,128]{1,0:T(8,128)(2,1)S(1)} %get-tuple-element.60.refs_5_), channel_id=1, source_target_pairs={{0,8},{1,11},{2,9},{3,10},{4,13},{5,15},{6,12},{7,14},{8,1},{9,3},... | collective-permute-start | bytes 49160 | tf_op jit(solution)/shard_map/ppermute | solution.py:329
  33.1 2.0 %collective-permute-start.12 = (bf16[64,1536]{1,0:T(8,128)(2,1)S(1)}, bf16[64,1536]{1,0:T(8,128)(2,1)S(1)}, u32[]{:S(2)}, u32[]{:S(2)}) collective-permute-start(bf16[64,1536]{1,0:T(8,128)(2,1)S(1)} %get-tuple-element.64), channel_id=1, source_target_pairs={{0,1},{1,0},{2,3},{3,2},{4,5},{5,4},{6,7},{7,6},{8,9},{9,8},{10,11... | collective-permute-start | bytes 589832 | tf_op jit(solution)/shard_map/ppermute | solution.py:317
  33.2 7.4 %collective-permute-start.13 = (bf16[64,1024]{1,0:T(8,128)(2,1)S(1)}, bf16[64,1024]{1,0:T(8,128)(2,1)S(1)}, u32[]{:S(2)}, u32[]{:S(2)}) collective-permute-start(bf16[64,1024]{1,0:T(8,128)(2,1)S(1)} %get-tuple-element.63.refs_1_), channel_id=1, source_target_pairs={{0,15},{1,2},{2,1},{3,4},{4,3},{5,6},{6,5},{7,8},{8,7},{9,10},{10,... | collective-permute-start | bytes 393224 | tf_op jit(solution)/shard_map/ppermute | solution.py:316
  35.2 6.0 %collective-permute-start.14 = (bf16[64,128]{1,0:T(8,128)(2,1)S(1)}, bf16[64,128]{1,0:T(8,128)(2,1)S(1)}, u32[]{:S(2)}, u32[]{:S(2)}) collective-permute-start(bf16[64,128]{1,0:T(8,128)(2,1)S(1)} %get-tuple-element.66.refs_4_), channel_id=1, source_target_pairs={{0,9},{1,10},{2,8},{3,11},{4,12},{5,14},{6,13},{7,15},{8,0},{9,2},... | collective-permute-start | bytes 49160 | tf_op jit(solution)/shard_map/ppermute | solution.py:329
  35.5 5.8 %collective-permute-start.15 = (bf16[64,128]{1,0:T(8,128)(2,1)S(1)}, bf16[64,128]{1,0:T(8,128)(2,1)S(1)}, u32[]{:S(2)}, u32[]{:S(2)}) collective-permute-start(bf16[64,128]{1,0:T(8,128)(2,1)S(1)} %get-tuple-element.67.refs_5_), channel_id=1, source_target_pairs={{0,8},{1,11},{2,9},{3,10},{4,13},{5,15},{6,12},{7,14},{8,1},{9,3},... | collective-permute-start | bytes 49160 | tf_op jit(solution)/shard_map/ppermute | solution.py:329

commit v23 on v22

--- a/solution.py
+++ b/solution.py
@@ -11,7 +11,7 @@
 REACH = 4
 LEVELS = 3
 SPAN = 2 * REACH + 1
-TURNED = 0b00011000
+TURNED = 0b10000001
 
 F32 = jnp.float32
 BF16 = jnp.bfloat16

time: 42.3 us -> 43.3 us (1.024)
  waiting for transfers between devices: 4.62 us -> 10.9 us
  starting transfers between devices: 25 us -> 19.8 us
    ppermute x8, starting transfers between devices: 11.9 us -> 3.64 us  [on_device(): fars = [lax.ppermute(s, axes, route) for s, route in zip(sends, routes)]]
    ppermute x8, waiting for transfers between devices: 2.04 us -> 5.43 us  [on_device(): fars = [lax.ppermute(s, axes, route) for s, route in zip(sends, routes)]]
    ppermute x4, waiting for transfers between devices: 2.57 us -> 5.42 us  [on_device(): over = lax.ppermute(current, axes, plan.over)]
    ppermute x4, starting transfers between devices: 12.4 us -> 15.2 us  [on_device(): over = lax.ppermute(current, axes, plan.over)]
  transfers between devices with their start and end apart: 16 -> 16, of which waited for: 7 -> 8; matrix products, arithmetic and copies ran while one was open for 0% -> 0% of each run, Pallas kernels for 19% -> 18%
where the time goes in v23:
time: 43.3 us; the launch traced here: 43.2 us
  starting transfers between devices  19.8 us (46%)
  Pallas kernels  12.3 us (28%)
  waiting for transfers between devices  10.9 us (25%)
    ppermute x4, starting transfers between devices, on_device(): over = lax.ppermute(current, axes, plan.over)  15.2 us
    pallas_call x17, Pallas kernels, call(): pl.pallas_call(kernel, in_specs=list(specs), out_specs=out_specs or [IN_V...  12.3 us
    ppermute x8, waiting for transfers between devices, on_device(): fars = [lax.ppermute(s, axes, route) for s, route in zip(sends, routes)]  5.43 us
    ppermute x4, waiting for transfers between devices, on_device(): over = lax.ppermute(current, axes, plan.over)  5.42 us
    ppermute x8, starting transfers between devices, on_device(): fars = [lax.ppermute(s, axes, route) for s, route in zip(sends, routes)]  3.64 us
    ppermute x4, starting transfers between devices, on_device(): near = lax.ppermute(sends[0] if plan.paired else current, axes, plan.near)  1.06 us
  transfers between devices with their start and end apart: 16, of which 8 were waited for; matrix products, arithmetic and copies ran while one was open for 0% of the time, Pallas kernels for 18%

profile of v23, /device:TPU:0, one launch (start us, length us, event | category | flops | bytes accessed | tf_op | source)
XLA Modules:
  0.0 43.2 jit_solution(11950839515884227477)
XLA Ops:
  0.0 0.0 copy-start.1
  0.0 0.0 copy-start
  0.0 1.8 %prepare.1 = (bf16[64,1024]{1,0:T(8,128)(2,1)S(1)}, bf16[1,512,256]{2,1,0:T(8,128)(2,1)S(1)}, bf16[128,1024]{1,0:T(8,128)(2,1)S(1)}, s32[32]{0:T(128)S(4)}, s32[...) custom-call(s32[1]{0:T(128)} %bitcast.index_ref.refs_0_, s32[32]{0:T(128)} %refs_0_.1, s32[32]{0:T(128)} %refs_1_.1, ...), custom_call_target="tpu_custom_call" | custom-call | flops 1000000000 | bytes 4194304 | tf_op jit(solution)/shard_map/prepare/pallas_call | solution.py:255
  1.8 0.5 %collective-permute-start = (bf16[64,1536]{1,0:T(8,128)(2,1)S(1)}, bf16[64,1536]{1,0:T(8,128)(2,1)S(1)}, u32[]{:S(2)}, u32[]{:S(2)}) collective-permute-start(bf16[64,1536]{1,0:T(8,128)(2,1)S(1)} %get-tuple-element.41), channel_id=1, source_target_pairs={{0,1},{1,0},{2,3},{3,2},{4,5},{5,4},{6,7},{7,6},{8,9},{9,8},{10,11... | collective-permute-start | bytes 589832 | tf_op jit(solution)/shard_map/ppermute | solution.py:317
  2.4 5.6 %collective-permute-start.1 = (bf16[64,1024]{1,0:T(8,128)(2,1)S(1)}, bf16[64,1024]{1,0:T(8,128)(2,1)S(1)}, u32[]{:S(2)}, u32[]{:S(2)}) collective-permute-start(bf16[64,1024]{1,0:T(8,128)(2,1)S(1)} %get-tuple-element.40.refs_3_), channel_id=1, source_target_pairs={{0,15},{1,2},{2,1},{3,4},{4,3},{5,6},{6,5},{7,8},{8,7},{9,10},{10,... | collective-permute-start | bytes 393224 | tf_op jit(solution)/shard_map/ppermute | solution.py:316
  8.0 0.0 collective-permute-done.message_ref.refs_4_
  8.0 0.1 collective-permute-start.2
  8.1 0.4 collective-permute-start.3
  8.4 0.0 copy-done.1
  8.5 0.0 copy-done
  8.5 1.9 %first_own.1 = (f32[64,1024]{1,0:T(8,128)S(1)}, bf16[36,256,256]{2,1,0:T(8,128)(2,1)S(1)}, bf16[256,1024]{1,0:T(8,128)(2,1)S(1)}) custom-call(s32[1]{0:T(128)} %bitcast.index_ref.refs_0_, s32[32]{0:T(128)S(4)} %get-tuple-element.38.refs_1_, s32[32]{0:T(128)S(4)} %get-tuple-element.39.refs_2_, bf16[64,1024]{1,0:T(8,128)(2,1)S(1)} %get-tuple-element.40.refs_3_, ...), custom_call_target="tpu_custom_call" | custom-call | flops 1000000000 | bytes 4194304 | tf_op jit(solution)/shard_map/first_own/pallas_call | solution.py:255
  10.3 0.4 collective-permute-done.1.over_ref
  10.8 0.5 %halo.4.refs_1_ = f32[64,1024]{1,0:T(8,128)S(1)} custom-call(s32[1]{0:T(128)} %bitcast.index_ref.refs_0_, f32[64,1024]{1,0:T(8,128)S(1)} %get-tuple-element.45.acc_ref, bf16[64,1024]{1,0:T(8,128)(2,1)S(1)} %collective-permute-done.1.over_ref, bf16[36,256,256]{2,1,0:T(8,128)(2,1)S(1)} %get-tuple-element.46.d_ref.refs_3_), custom_call_target="tpu_custom_call" | custom-call | flops 1000000000 | bytes 4194304 | tf_op jit(solution)/shard_map/halo/pallas_call | solution.py:255
  11.3 2.3 %collective-permute-done.2.refs_5_ = bf16[64,128]{1,0:T(8,128)(2,1)S(1)} collective-permute-done((bf16[64,128]{1,0:T(8,128)(2,1)S(1)}, bf16[64,128]{1,0:T(8,128)(2,1)S(1)}, u32[]{:S(2)}, u32[]{:S(2)}) %collective-permute-start.2) | collective-permute-done | bytes 16416 | tf_op jit(solution)/shard_map/ppermute | solution.py:329
  13.6 0.0 collective-permute-done.3.refs_6_
  13.6 0.6 %finish.3 = (bf16[64,1024]{1,0:T(8,128)(2,1)S(1)}, bf16[64,1536]{1,0:T(8,128)(2,1)S(1)}, f32[64,256]{1,0:T(8,128)S(1)}) custom-call(s32[1]{0:T(128)} %bitcast.index_ref.refs_0_, f32[64,1024]{1,0:T(8,128)S(1)} %halo.4.refs_1_, bf16[256,1024]{1,0:T(8,128)(2,1)S(1)} %get-tuple-element.47.refs_2_.refs_1_, bf16[128,1024]{1,0:T(8,128)(2,1)S(1)} %get-tuple-element.48.refs_3_, ...), custom_call_target="tpu_custom_call" | custom-call | flops 1000000000 | bytes 4194304 | tf_op jit(solution)/shard_map/finish/pallas_call | solution.py:255
  14.2 0.2 collective-permute-start.4
  14.4 3.1 %collective-permute-start.5 = (bf16[64,1024]{1,0:T(8,128)(2,1)S(1)}, bf16[64,1024]{1,0:T(8,128)(2,1)S(1)}, u32[]{:S(2)}, u32[]{:S(2)}) collective-permute-start(bf16[64,1024]{1,0:T(8,128)(2,1)S(1)} %get-tuple-element.50.refs_1_), channel_id=1, source_target_pairs={{0,15},{1,2},{2,1},{3,4},{4,3},{5,6},{6,5},{7,8},{8,7},{9,10},{10,... | collective-permute-start | bytes 393224 | tf_op jit(solution)/shard_map/ppermute | solution.py:316
  17.5 0.0 collective-permute-done.4.message_ref.refs_2_
  17.5 0.1 collective-permute-start.6
  17.6 1.3 %collective-permute-start.7 = (bf16[64,128]{1,0:T(8,128)(2,1)S(1)}, bf16[64,128]{1,0:T(8,128)(2,1)S(1)}, u32[]{:S(2)}, u32[]{:S(2)}) collective-permute-start(bf16[64,128]{1,0:T(8,128)(2,1)S(1)} %get-tuple-element.54.refs_5_), channel_id=1, source_target_pairs={{0,9},{1,11},{2,8},{3,10},{4,13},{5,14},{6,12},{7,15},{8,0},{9,3},... | collective-permute-start | bytes 49160 | tf_op jit(solution)/shard_map/ppermute | solution.py:329
  18.9 1.3 %own.3 = (f32[64,1024]{1,0:T(8,128)S(1)}, bf16[4,64,1024]{2,1,0:T(8,128)(2,1)}) custom-call(s32[1]{0:T(128)} %bitcast.index_ref.refs_0_, bf16[64,1024]{1,0:T(8,128)(2,1)S(1)} %get-tuple-element.50.refs_1_, bf16[64,1536]{1,0:T(8,128)(2,1)S(1)} %collective-permute-done.4.message_ref.refs_2_, bf16[36,256,256]{2,1,0:T(8,128)(2,1)S(1)} %get-tuple-element.46.d_ref.refs_3_, ...), custom_call_target="tpu_custom_call" | custom-call | flops 1000000000 | bytes 4194304 | tf_op jit(solution)/shard_map/own/pallas_call | solution.py:255
  20.2 1.5 %collective-permute-done.5.over_ref = bf16[64,1024]{1,0:T(8,128)(2,1)S(1)} collective-permute-done((bf16[64,1024]{1,0:T(8,128)(2,1)S(1)}, bf16[64,1024]{1,0:T(8,128)(2,1)S(1)}, u32[]{:S(2)}, u32[]{:S(2)}) %collective-permute-start.5) | collective-permute-done | bytes 131104 | tf_op jit(solution)/shard_map/ppermute | solution.py:316
  21.7 0.5 %halo.5.refs_1_ = f32[64,1024]{1,0:T(8,128)S(1)} custom-call(s32[1]{0:T(128)} %bitcast.index_ref.refs_0_, f32[64,1024]{1,0:T(8,128)S(1)} %get-tuple-element.55.acc_ref, bf16[64,1024]{1,0:T(8,128)(2,1)S(1)} %collective-permute-done.5.over_ref, bf16[36,256,256]{2,1,0:T(8,128)(2,1)S(1)} %get-tuple-element.46.d_ref.refs_3_), custom_call_target="tpu_custom_call" | custom-call | flops 1000000000 | bytes 4194304 | tf_op jit(solution)/shard_map/halo/pallas_call | solution.py:255
  22.2 0.9 %collective-permute-done.6.refs_5_ = bf16[64,128]{1,0:T(8,128)(2,1)S(1)} collective-permute-done((bf16[64,128]{1,0:T(8,128)(2,1)S(1)}, bf16[64,128]{1,0:T(8,128)(2,1)S(1)}, u32[]{:S(2)}, u32[]{:S(2)}) %collective-permute-start.6) | collective-permute-done | bytes 16416 | tf_op jit(solution)/shard_map/ppermute | solution.py:329
  23.1 0.0 collective-permute-done.7.refs_6_
  23.1 0.6 %finish.4 = (bf16[64,1024]{1,0:T(8,128)(2,1)S(1)}, bf16[64,1536]{1,0:T(8,128)(2,1)S(1)}, f32[64,256]{1,0:T(8,128)S(1)}) custom-call(s32[1]{0:T(128)} %bitcast.index_ref.refs_0_, f32[64,1024]{1,0:T(8,128)S(1)} %halo.5.refs_1_, bf16[256,1024]{1,0:T(8,128)(2,1)S(1)} %get-tuple-element.47.refs_2_.refs_1_, bf16[128,1024]{1,0:T(8,128)(2,1)S(1)} %get-tuple-element.48.refs_3_, ...), custom_call_target="tpu_custom_call" | custom-call | flops 1000000000 | bytes 4194304 | tf_op jit(solution)/shard_map/finish/pallas_call | solution.py:255
  23.7 0.2 collective-permute-start.8
  23.9 3.3 %collective-permute-start.9 = (bf16[64,1024]{1,0:T(8,128)(2,1)S(1)}, bf16[64,1024]{1,0:T(8,128)(2,1)S(1)}, u32[]{:S(2)}, u32[]{:S(2)}) collective-permute-start(bf16[64,1024]{1,0:T(8,128)(2,1)S(1)} %get-tuple-element.56.refs_1_), channel_id=1, source_target_pairs={{0,15},{1,2},{2,1},{3,4},{4,3},{5,6},{6,5},{7,8},{8,7},{9,10},{10,... | collective-permute-start | bytes 393224 | tf_op jit(solution)/shard_map/ppermute | solution.py:316
  27.2 0.0 collective-permute-done.8.message_ref.refs_2_
  27.2 0.1 collective-permute-start.10
  27.3 0.7 %collective-permute-start.11 = (bf16[64,128]{1,0:T(8,128)(2,1)S(1)}, bf16[64,128]{1,0:T(8,128)(2,1)S(1)}, u32[]{:S(2)}, u32[]{:S(2)}) collective-permute-start(bf16[64,128]{1,0:T(8,128)(2,1)S(1)} %get-tuple-element.60.refs_5_), channel_id=1, source_target_pairs={{0,9},{1,11},{2,8},{3,10},{4,13},{5,14},{6,12},{7,15},{8,0},{9,3},... | collective-permute-start | bytes 49160 | tf_op jit(solution)/shard_map/ppermute | solution.py:329
  28.0 1.3 %own.4 = (f32[64,1024]{1,0:T(8,128)S(1)}, bf16[4,64,1024]{2,1,0:T(8,128)(2,1)}) custom-call(s32[1]{0:T(128)} %bitcast.index_ref.refs_0_, bf16[64,1024]{1,0:T(8,128)(2,1)S(1)} %get-tuple-element.56.refs_1_, bf16[64,1536]{1,0:T(8,128)(2,1)S(1)} %collective-permute-done.8.message_ref.refs_2_, ...), custom_call_target="tpu_custom_call", output_to_operand_aliasing={{1}: (6, {})} | custom-call | flops 1000000000 | bytes 4194304 | tf_op jit(solution)/shard_map/own/pallas_call | solution.py:255
  29.3 1.7 %collective-permute-done.9.over_ref = bf16[64,1024]{1,0:T(8,128)(2,1)S(1)} collective-permute-done((bf16[64,1024]{1,0:T(8,128)(2,1)S(1)}, bf16[64,1024]{1,0:T(8,128)(2,1)S(1)}, u32[]{:S(2)}, u32[]{:S(2)}) %collective-permute-start.9) | collective-permute-done | bytes 131104 | tf_op jit(solution)/shard_map/ppermute | solution.py:316
  31.1 0.5 %halo.6.refs_1_ = f32[64,1024]{1,0:T(8,128)S(1)} custom-call(s32[1]{0:T(128)} %bitcast.index_ref.refs_0_, f32[64,1024]{1,0:T(8,128)S(1)} %get-tuple-element.62.acc_ref, bf16[64,1024]{1,0:T(8,128)(2,1)S(1)} %collective-permute-done.9.over_ref, bf16[36,256,256]{2,1,0:T(8,128)(2,1)S(1)} %get-tuple-element.46.d_ref.refs_3_), custom_call_target="tpu_custom_call" | custom-call | flops 1000000000 | bytes 4194304 | tf_op jit(solution)/shard_map/halo/pallas_call | solution.py:255
  31.6 1.3 %collective-permute-done.10.refs_5_ = bf16[64,128]{1,0:T(8,128)(2,1)S(1)} collective-permute-done((bf16[64,128]{1,0:T(8,128)(2,1)S(1)}, bf16[64,128]{1,0:T(8,128)(2,1)S(1)}, u32[]{:S(2)}, u32[]{:S(2)}) %collective-permute-start.10) | collective-permute-done | bytes 16416 | tf_op jit(solution)/shard_map/ppermute | solution.py:329
  32.8 0.0 collective-permute-done.11.refs_6_
  32.8 0.6 %finish.5 = (bf16[64,1024]{1,0:T(8,128)(2,1)S(1)}, bf16[64,1536]{1,0:T(8,128)(2,1)S(1)}, f32[64,256]{1,0:T(8,128)S(1)}) custom-call(s32[1]{0:T(128)} %bitcast.index_ref.refs_0_, f32[64,1024]{1,0:T(8,128)S(1)} %halo.6.refs_1_, bf16[256,1024]{1,0:T(8,128)(2,1)S(1)} %get-tuple-element.47.refs_2_.refs_1_, bf16[128,1024]{1,0:T(8,128)(2,1)S(1)} %get-tuple-element.48.refs_3_, ...), custom_call_target="tpu_custom_call" | custom-call | flops 1000000000 | bytes 4194304 | tf_op jit(solution)/shard_map/finish/pallas_call | solution.py:255
  33.4 0.2 collective-permute-start.12
  33.6 3.1 %collective-permute-start.13 = (bf16[64,1024]{1,0:T(8,128)(2,1)S(1)}, bf16[64,1024]{1,0:T(8,128)(2,1)S(1)}, u32[]{:S(2)}, u32[]{:S(2)}) collective-permute-start(bf16[64,1024]{1,0:T(8,128)(2,1)S(1)} %get-tuple-element.63.refs_1_), channel_id=1, source_target_pairs={{0,15},{1,2},{2,1},{3,4},{4,3},{5,6},{6,5},{7,8},{8,7},{9,10},{10,... | collective-permute-start | bytes 393224 | tf_op jit(solution)/shard_map/ppermute | solution.py:316
  36.7 0.0 collective-permute-done.12.message_ref.refs_2_
  36.7 0.1 collective-permute-start.14
  36.8 1.0 %collective-permute-start.15 = (bf16[64,128]{1,0:T(8,128)(2,1)S(1)}, bf16[64,128]{1,0:T(8,128)(2,1)S(1)}, u32[]{:S(2)}, u32[]{:S(2)}) collective-permute-start(bf16[64,128]{1,0:T(8,128)(2,1)S(1)} %get-tuple-element.67.refs_5_), channel_id=1, source_target_pairs={{0,9},{1,11},{2,8},{3,10},{4,13},{5,14},{6,12},{7,15},{8,0},{9,3},... | collective-permute-start | bytes 49160 | tf_op jit(solution)/shard_map/ppermute | solution.py:329
  37.8 1.3 %own.5 = (f32[64,1024]{1,0:T(8,128)S(1)}, bf16[4,64,1024]{2,1,0:T(8,128)(2,1)}) custom-call(s32[1]{0:T(128)} %bitcast.index_ref.refs_0_, bf16[64,1024]{1,0:T(8,128)(2,1)S(1)} %get-tuple-element.63.refs_1_, bf16[64,1536]{1,0:T(8,128)(2,1)S(1)} %collective-permute-done.12.message_ref.refs_2_, ...), custom_call_target="tpu_custom_call", output_to_operand_aliasing={{1}: (6, {})} | custom-call | flops 1000000000 | bytes 4194304 | tf_op jit(solution)/shard_map/own/pallas_call | solution.py:255
  39.1 1.8 %collective-permute-done.13.over_ref = bf16[64,1024]{1,0:T(8,128)(2,1)S(1)} collective-permute-done((bf16[64,1024]{1,0:T(8,128)(2,1)S(1)}, bf16[64,1024]{1,0:T(8,128)(2,1)S(1)}, u32[]{:S(2)}, u32[]{:S(2)}) %collective-permute-start.13) | collective-permute-done | bytes 131104 | tf_op jit(solution)/shard_map/ppermute | solution.py:316
  40.8 0.5 %halo.7.refs_0_ = f32[64,1024]{1,0:T(8,128)S(1)} custom-call(s32[1]{0:T(128)} %bitcast.index_ref.refs_0_, f32[64,1024]{1,0:T(8,128)S(1)} %get-tuple-element.69.acc_ref, bf16[64,1024]{1,0:T(8,128)(2,1)S(1)} %collective-permute-done.13.over_ref, bf16[36,256,256]{2,1,0:T(8,128)(2,1)S(1)} %get-tuple-element.46.d_ref.refs_3_), custom_call_target="tpu_custom_call" | custom-call | flops 1000000000 | bytes 4194304 | tf_op jit(solution)/shard_map/halo/pallas_call | solution.py:255
  41.4 0.9 %collective-permute-done.14.refs_2_ = bf16[64,128]{1,0:T(8,128)(2,1)S(1)} collective-permute-done((bf16[64,128]{1,0:T(8,128)(2,1)S(1)}, bf16[64,128]{1,0:T(8,128)(2,1)S(1)}, u32[]{:S(2)}, u32[]{:S(2)}) %collective-permute-start.14) | collective-permute-done | bytes 16416 | tf_op jit(solution)/shard_map/ppermute | solution.py:329
  42.3 0.0 collective-permute-done.15.refs_3_
  42.3 0.9 %last.1 = bf16[4,64,1024]{2,1,0:T(8,128)(2,1)} custom-call(f32[64,1024]{1,0:T(8,128)S(1)} %halo.7.refs_0_, bf16[256,1024]{1,0:T(8,128)(2,1)S(1)} %get-tuple-element.47.refs_2_.refs_1_, bf16[64,128]{1,0:T(8,128)(2,1)S(1)} %collective-permute-done.14.refs_2_, bf16[64,128]{1,0:T(8,128)(2,1)S(1)} %collective-permute-done.15.refs_3_, ...), custom_call_target="tpu_custom_call", output_to_operand_aliasing={{}: (4, {})} | custom-call | flops 1000000000 | bytes 4194304 | tf_op jit(solution)/shard_map/last/pallas_call | solution.py:255
  (4 shorter events, 0.1 us)
Async XLA Ops:
  0.0 8.4 %copy-start.1 = (bf16[4,32,256]{2,1,0:T(8,128)(2,1)S(1)}, bf16[4,32,256]{2,1,0:T(8,128)(2,1)}, u32[]{:S(2)}) copy-start(bf16[4,32,256]{2,1,0:T(8,128)(2,1)} %refs_5_.3) | copy-start | bytes 196612
  0.0 8.5 %copy-start = (bf16[32,256,256]{2,1,0:T(8,128)(2,1)S(1)}, bf16[32,256,256]{2,1,0:T(8,128)(2,1)}, u32[]{:S(2)}) copy-start(bf16[32,256,256]{2,1,0:T(8,128)(2,1)} %refs_6_.3) | copy-start | bytes 12582916
  1.8 6.2 %collective-permute-start = (bf16[64,1536]{1,0:T(8,128)(2,1)S(1)}, bf16[64,1536]{1,0:T(8,128)(2,1)S(1)}, u32[]{:S(2)}, u32[]{:S(2)}) collective-permute-start(bf16[64,1536]{1,0:T(8,128)(2,1)S(1)} %get-tuple-element.41), channel_id=1, source_target_pairs={{0,1},{1,0},{2,3},{3,2},{4,5},{5,4},{6,7},{7,6},{8,9},{9,8},{10,11... | collective-permute-start | bytes 589832 | tf_op jit(solution)/shard_map/ppermute | solution.py:317
  2.4 8.4 %collective-permute-start.1 = (bf16[64,1024]{1,0:T(8,128)(2,1)S(1)}, bf16[64,1024]{1,0:T(8,128)(2,1)S(1)}, u32[]{:S(2)}, u32[]{:S(2)}) collective-permute-start(bf16[64,1024]{1,0:T(8,128)(2,1)S(1)} %get-tuple-element.40.refs_3_), channel_id=1, source_target_pairs={{0,15},{1,2},{2,1},{3,4},{4,3},{5,6},{6,5},{7,8},{8,7},{9,10},{10,... | collective-permute-start | bytes 393224 | tf_op jit(solution)/shard_map/ppermute | solution.py:316
  8.0 5.6 %collective-permute-start.2 = (bf16[64,128]{1,0:T(8,128)(2,1)S(1)}, bf16[64,128]{1,0:T(8,128)(2,1)S(1)}, u32[]{:S(2)}, u32[]{:S(2)}) collective-permute-start(bf16[64,128]{1,0:T(8,128)(2,1)S(1)} %get-tuple-element.43.refs_7_), channel_id=1, source_target_pairs={{0,8},{1,10},{2,9},{3,11},{4,12},{5,15},{6,13},{7,14},{8,1},{9,2},... | collective-permute-start | bytes 49160 | tf_op jit(solution)/shard_map/ppermute | solution.py:329
  8.1 5.5 %collective-permute-start.3 = (bf16[64,128]{1,0:T(8,128)(2,1)S(1)}, bf16[64,128]{1,0:T(8,128)(2,1)S(1)}, u32[]{:S(2)}, u32[]{:S(2)}) collective-permute-start(bf16[64,128]{1,0:T(8,128)(2,1)S(1)} %get-tuple-element.44.refs_8_), channel_id=1, source_target_pairs={{0,9},{1,11},{2,8},{3,10},{4,13},{5,14},{6,12},{7,15},{8,0},{9,3},... | collective-permute-start | bytes 49160 | tf_op jit(solution)/shard_map/ppermute | solution.py:329
  14.2 3.3 %collective-permute-start.4 = (bf16[64,1536]{1,0:T(8,128)(2,1)S(1)}, bf16[64,1536]{1,0:T(8,128)(2,1)S(1)}, u32[]{:S(2)}, u32[]{:S(2)}) collective-permute-start(bf16[64,1536]{1,0:T(8,128)(2,1)S(1)} %get-tuple-element.51), channel_id=1, source_target_pairs={{0,1},{1,0},{2,3},{3,2},{4,5},{5,4},{6,7},{7,6},{8,9},{9,8},{10,11... | collective-permute-start | bytes 589832 | tf_op jit(solution)/shard_map/ppermute | solution.py:317
  14.4 7.3 %collective-permute-start.5 = (bf16[64,1024]{1,0:T(8,128)(2,1)S(1)}, bf16[64,1024]{1,0:T(8,128)(2,1)S(1)}, u32[]{:S(2)}, u32[]{:S(2)}) collective-permute-start(bf16[64,1024]{1,0:T(8,128)(2,1)S(1)} %get-tuple-element.50.refs_1_), channel_id=1, source_target_pairs={{0,15},{1,2},{2,1},{3,4},{4,3},{5,6},{6,5},{7,8},{8,7},{9,10},{10,... | collective-permute-start | bytes 393224 | tf_op jit(solution)/shard_map/ppermute | solution.py:316
  17.5 5.6 %collective-permute-start.6 = (bf16[64,128]{1,0:T(8,128)(2,1)S(1)}, bf16[64,128]{1,0:T(8,128)(2,1)S(1)}, u32[]{:S(2)}, u32[]{:S(2)}) collective-permute-start(bf16[64,128]{1,0:T(8,128)(2,1)S(1)} %get-tuple-element.53.refs_4_), channel_id=1, source_target_pairs={{0,8},{1,10},{2,9},{3,11},{4,12},{5,15},{6,13},{7,14},{8,1},{9,2},... | collective-permute-start | bytes 49160 | tf_op jit(solution)/shard_map/ppermute | solution.py:329
  17.6 5.5 %collective-permute-start.7 = (bf16[64,128]{1,0:T(8,128)(2,1)S(1)}, bf16[64,128]{1,0:T(8,128)(2,1)S(1)}, u32[]{:S(2)}, u32[]{:S(2)}) collective-permute-start(bf16[64,128]{1,0:T(8,128)(2,1)S(1)} %get-tuple-element.54.refs_5_), channel_id=1, source_target_pairs={{0,9},{1,11},{2,8},{3,10},{4,13},{5,14},{6,12},{7,15},{8,0},{9,3},... | collective-permute-start | bytes 49160 | tf_op jit(solution)/shard_map/ppermute | solution.py:329
  23.7 3.5 %collective-permute-start.8 = (bf16[64,1536]{1,0:T(8,128)(2,1)S(1)}, bf16[64,1536]{1,0:T(8,128)(2,1)S(1)}, u32[]{:S(2)}, u32[]{:S(2)}) collective-permute-start(bf16[64,1536]{1,0:T(8,128)(2,1)S(1)} %get-tuple-element.57), channel_id=1, source_target_pairs={{0,1},{1,0},{2,3},{3,2},{4,5},{5,4},{6,7},{7,6},{8,9},{9,8},{10,11... | collective-permute-start | bytes 589832 | tf_op jit(solution)/shard_map/ppermute | solution.py:317
  23.9 7.2 %collective-permute-start.9 = (bf16[64,1024]{1,0:T(8,128)(2,1)S(1)}, bf16[64,1024]{1,0:T(8,128)(2,1)S(1)}, u32[]{:S(2)}, u32[]{:S(2)}) collective-permute-start(bf16[64,1024]{1,0:T(8,128)(2,1)S(1)} %get-tuple-element.56.refs_1_), channel_id=1, source_target_pairs={{0,15},{1,2},{2,1},{3,4},{4,3},{5,6},{6,5},{7,8},{8,7},{9,10},{10,... | collective-permute-start | bytes 393224 | tf_op jit(solution)/shard_map/ppermute | solution.py:316
  27.2 5.6 %collective-permute-start.10 = (bf16[64,128]{1,0:T(8,128)(2,1)S(1)}, bf16[64,128]{1,0:T(8,128)(2,1)S(1)}, u32[]{:S(2)}, u32[]{:S(2)}) collective-permute-start(bf16[64,128]{1,0:T(8,128)(2,1)S(1)} %get-tuple-element.59.refs_4_), channel_id=1, source_target_pairs={{0,8},{1,10},{2,9},{3,11},{4,12},{5,15},{6,13},{7,14},{8,1},{9,2},... | collective-permute-start | bytes 49160 | tf_op jit(solution)/shard_map/ppermute | solution.py:329
  27.3 5.5 %collective-permute-start.11 = (bf16[64,128]{1,0:T(8,128)(2,1)S(1)}, bf16[64,128]{1,0:T(8,128)(2,1)S(1)}, u32[]{:S(2)}, u32[]{:S(2)}) collective-permute-start(bf16[64,128]{1,0:T(8,128)(2,1)S(1)} %get-tuple-element.60.refs_5_), channel_id=1, source_target_pairs={{0,9},{1,11},{2,8},{3,10},{4,13},{5,14},{6,12},{7,15},{8,0},{9,3},... | collective-permute-start | bytes 49160 | tf_op jit(solution)/shard_map/ppermute | solution.py:329
  33.4 3.3 %collective-permute-start.12 = (bf16[64,1536]{1,0:T(8,128)(2,1)S(1)}, bf16[64,1536]{1,0:T(8,128)(2,1)S(1)}, u32[]{:S(2)}, u32[]{:S(2)}) collective-permute-start(bf16[64,1536]{1,0:T(8,128)(2,1)S(1)} %get-tuple-element.64), channel_id=1, source_target_pairs={{0,1},{1,0},{2,3},{3,2},{4,5},{5,4},{6,7},{7,6},{8,9},{9,8},{10,11... | collective-permute-start | bytes 589832 | tf_op jit(solution)/shard_map/ppermute | solution.py:317
  33.6 7.2 %collective-permute-start.13 = (bf16[64,1024]{1,0:T(8,128)(2,1)S(1)}, bf16[64,1024]{1,0:T(8,128)(2,1)S(1)}, u32[]{:S(2)}, u32[]{:S(2)}) collective-permute-start(bf16[64,1024]{1,0:T(8,128)(2,1)S(1)} %get-tuple-element.63.refs_1_), channel_id=1, source_target_pairs={{0,15},{1,2},{2,1},{3,4},{4,3},{5,6},{6,5},{7,8},{8,7},{9,10},{10,... | collective-permute-start | bytes 393224 | tf_op jit(solution)/shard_map/ppermute | solution.py:316
  36.7 5.6 %collective-permute-start.14 = (bf16[64,128]{1,0:T(8,128)(2,1)S(1)}, bf16[64,128]{1,0:T(8,128)(2,1)S(1)}, u32[]{:S(2)}, u32[]{:S(2)}) collective-permute-start(bf16[64,128]{1,0:T(8,128)(2,1)S(1)} %get-tuple-element.66.refs_4_), channel_id=1, source_target_pairs={{0,8},{1,10},{2,9},{3,11},{4,12},{5,15},{6,13},{7,14},{8,1},{9,2},... | collective-permute-start | bytes 49160 | tf_op jit(solution)/shard_map/ppermute | solution.py:329
  36.8 5.5 %collective-permute-start.15 = (bf16[64,128]{1,0:T(8,128)(2,1)S(1)}, bf16[64,128]{1,0:T(8,128)(2,1)S(1)}, u32[]{:S(2)}, u32[]{:S(2)}) collective-permute-start(bf16[64,128]{1,0:T(8,128)(2,1)S(1)} %get-tuple-element.67.refs_5_), channel_id=1, source_target_pairs={{0,9},{1,11},{2,8},{3,10},{4,13},{5,14},{6,12},{7,15},{8,0},{9,3},... | collective-permute-start | bytes 49160 | tf_op jit(solution)/shard_map/ppermute | solution.py:329

commit v24 on v23

--- a/solution.py
+++ b/solution.py
@@ -11,7 +11,7 @@
 REACH = 4
 LEVELS = 3
 SPAN = 2 * REACH + 1
-TURNED = 0b10000001
+TURNED = 0
 
 F32 = jnp.float32
 BF16 = jnp.bfloat16

time: 43.3 us -> 43.8 us (1.012)
    ppermute x8, starting transfers between devices: 3.64 us -> 7.67 us  [on_device(): fars = [lax.ppermute(s, axes, route) for s, route in zip(sends, routes)]]
    ppermute x4, starting transfers between devices: 15.2 us -> 11.7 us  [on_device(): over = lax.ppermute(current, axes, plan.over)]
    ppermute x8, waiting for transfers between devices: 5.43 us -> 5.96 us  [on_device(): fars = [lax.ppermute(s, axes, route) for s, route in zip(sends, routes)]]
  transfers between devices with their start and end apart: 16 -> 16, of which waited for: 8 -> 9; matrix products, arithmetic and copies ran while one was open for 0% -> 0% of each run, Pallas kernels for 18% -> 18%
where the time goes in v24:
time: 43.8 us; the launch traced here: 43.7 us
  starting transfers between devices  20.1 us (46%)
  Pallas kernels  12.3 us (28%)
  waiting for transfers between devices  11.1 us (25%)
    pallas_call x17, Pallas kernels, call(): pl.pallas_call(kernel, in_specs=list(specs), out_specs=out_specs or [IN_V...  12.3 us
    ppermute x4, starting transfers between devices, on_device(): over = lax.ppermute(current, axes, plan.over)  11.7 us
    ppermute x8, starting transfers between devices, on_device(): fars = [lax.ppermute(s, axes, route) for s, route in zip(sends, routes)]  7.67 us
    ppermute x8, waiting for transfers between devices, on_device(): fars = [lax.ppermute(s, axes, route) for s, route in zip(sends, routes)]  5.96 us
    ppermute x4, waiting for transfers between devices, on_device(): over = lax.ppermute(current, axes, plan.over)  5.13 us
  transfers between devices with their start and end apart: 16, of which 9 were waited for; matrix products, arithmetic and copies ran while one was open for 0% of the time, Pallas kernels for 18%

profile of v24, /device:TPU:0, one launch (start us, length us, event | category | flops | bytes accessed | tf_op | source)
XLA Modules:
  0.0 43.7 jit_solution(6783697652182879057)
XLA Ops:
  0.0 0.0 copy-start.1
  0.0 0.0 copy-start
  0.0 1.8 %prepare.1 = (bf16[64,1024]{1,0:T(8,128)(2,1)S(1)}, bf16[1,512,256]{2,1,0:T(8,128)(2,1)S(1)}, bf16[128,1024]{1,0:T(8,128)(2,1)S(1)}, s32[32]{0:T(128)S(4)}, s32[...) custom-call(s32[1]{0:T(128)} %bitcast.index_ref.refs_0_, s32[32]{0:T(128)} %refs_0_.1, s32[32]{0:T(128)} %refs_1_.1, ...), custom_call_target="tpu_custom_call" | custom-call | flops 1000000000 | bytes 4194304 | tf_op jit(solution)/shard_map/prepare/pallas_call | solution.py:255
  1.8 0.5 %collective-permute-start = (bf16[64,1536]{1,0:T(8,128)(2,1)S(1)}, bf16[64,1536]{1,0:T(8,128)(2,1)S(1)}, u32[]{:S(2)}, u32[]{:S(2)}) collective-permute-start(bf16[64,1536]{1,0:T(8,128)(2,1)S(1)} %get-tuple-element.41), channel_id=1, source_target_pairs={{0,1},{1,0},{2,3},{3,2},{4,5},{5,4},{6,7},{7,6},{8,9},{9,8},{10,11... | collective-permute-start | bytes 589832 | tf_op jit(solution)/shard_map/ppermute | solution.py:317
  2.4 5.6 %collective-permute-start.1 = (bf16[64,1024]{1,0:T(8,128)(2,1)S(1)}, bf16[64,1024]{1,0:T(8,128)(2,1)S(1)}, u32[]{:S(2)}, u32[]{:S(2)}) collective-permute-start(bf16[64,1024]{1,0:T(8,128)(2,1)S(1)} %get-tuple-element.40.refs_3_), channel_id=1, source_target_pairs={{0,15},{1,2},{2,1},{3,4},{4,3},{5,6},{6,5},{7,8},{8,7},{9,10},{10,... | collective-permute-start | bytes 393224 | tf_op jit(solution)/shard_map/ppermute | solution.py:316
  8.0 0.0 collective-permute-done.message_ref.refs_4_
  8.0 0.1 collective-permute-start.2
  8.1 0.4 collective-permute-start.3
  8.5 0.0 copy-done.1
  8.5 0.0 copy-done
  8.5 1.9 %first_own.1 = (f32[64,1024]{1,0:T(8,128)S(1)}, bf16[36,256,256]{2,1,0:T(8,128)(2,1)S(1)}, bf16[256,1024]{1,0:T(8,128)(2,1)S(1)}) custom-call(s32[1]{0:T(128)} %bitcast.index_ref.refs_0_, s32[32]{0:T(128)S(4)} %get-tuple-element.38.refs_1_, s32[32]{0:T(128)S(4)} %get-tuple-element.39.refs_2_, bf16[64,1024]{1,0:T(8,128)(2,1)S(1)} %get-tuple-element.40.refs_3_, ...), custom_call_target="tpu_custom_call" | custom-call | flops 1000000000 | bytes 4194304 | tf_op jit(solution)/shard_map/first_own/pallas_call | solution.py:255
  10.3 0.4 collective-permute-done.1.over_ref
  10.8 0.5 %halo.4.refs_1_ = f32[64,1024]{1,0:T(8,128)S(1)} custom-call(s32[1]{0:T(128)} %bitcast.index_ref.refs_0_, f32[64,1024]{1,0:T(8,128)S(1)} %get-tuple-element.45.acc_ref, bf16[64,1024]{1,0:T(8,128)(2,1)S(1)} %collective-permute-done.1.over_ref, bf16[36,256,256]{2,1,0:T(8,128)(2,1)S(1)} %get-tuple-element.46.d_ref.refs_3_), custom_call_target="tpu_custom_call" | custom-call | flops 1000000000 | bytes 4194304 | tf_op jit(solution)/shard_map/halo/pallas_call | solution.py:255
  11.3 1.5 %collective-permute-done.2.refs_5_ = bf16[64,128]{1,0:T(8,128)(2,1)S(1)} collective-permute-done((bf16[64,128]{1,0:T(8,128)(2,1)S(1)}, bf16[64,128]{1,0:T(8,128)(2,1)S(1)}, u32[]{:S(2)}, u32[]{:S(2)}) %collective-permute-start.2) | collective-permute-done | bytes 16416 | tf_op jit(solution)/shard_map/ppermute | solution.py:329
  12.7 1.0 %collective-permute-done.3.refs_6_ = bf16[64,128]{1,0:T(8,128)(2,1)S(1)} collective-permute-done((bf16[64,128]{1,0:T(8,128)(2,1)S(1)}, bf16[64,128]{1,0:T(8,128)(2,1)S(1)}, u32[]{:S(2)}, u32[]{:S(2)}) %collective-permute-start.3) | collective-permute-done | bytes 16416 | tf_op jit(solution)/shard_map/ppermute | solution.py:329
  13.7 0.6 %finish.3 = (bf16[64,1024]{1,0:T(8,128)(2,1)S(1)}, bf16[64,1536]{1,0:T(8,128)(2,1)S(1)}, f32[64,256]{1,0:T(8,128)S(1)}) custom-call(s32[1]{0:T(128)} %bitcast.index_ref.refs_0_, f32[64,1024]{1,0:T(8,128)S(1)} %halo.4.refs_1_, bf16[256,1024]{1,0:T(8,128)(2,1)S(1)} %get-tuple-element.47.refs_2_.refs_1_, bf16[128,1024]{1,0:T(8,128)(2,1)S(1)} %get-tuple-element.48.refs_3_, ...), custom_call_target="tpu_custom_call" | custom-call | flops 1000000000 | bytes 4194304 | tf_op jit(solution)/shard_map/finish/pallas_call | solution.py:255
  14.3 0.1 collective-permute-start.4
  14.4 2.9 %collective-permute-start.5 = (bf16[64,1024]{1,0:T(8,128)(2,1)S(1)}, bf16[64,1024]{1,0:T(8,128)(2,1)S(1)}, u32[]{:S(2)}, u32[]{:S(2)}) collective-permute-start(bf16[64,1024]{1,0:T(8,128)(2,1)S(1)} %get-tuple-element.50.refs_1_), channel_id=1, source_target_pairs={{0,15},{1,2},{2,1},{3,4},{4,3},{5,6},{6,5},{7,8},{8,7},{9,10},{10,... | collective-permute-start | bytes 393224 | tf_op jit(solution)/shard_map/ppermute | solution.py:316
  17.3 0.0 collective-permute-done.4.message_ref.refs_2_
  17.3 1.4 %collective-permute-start.6 = (bf16[64,128]{1,0:T(8,128)(2,1)S(1)}, bf16[64,128]{1,0:T(8,128)(2,1)S(1)}, u32[]{:S(2)}, u32[]{:S(2)}) collective-permute-start(bf16[64,128]{1,0:T(8,128)(2,1)S(1)} %get-tuple-element.53.refs_4_), channel_id=1, source_target_pairs={{0,8},{1,10},{2,9},{3,11},{4,12},{5,14},{6,13},{7,15},{8,0},{9,2},... | collective-permute-start | bytes 49160 | tf_op jit(solution)/shard_map/ppermute | solution.py:329
  18.7 0.4 %collective-permute-start.7 = (bf16[64,128]{1,0:T(8,128)(2,1)S(1)}, bf16[64,128]{1,0:T(8,128)(2,1)S(1)}, u32[]{:S(2)}, u32[]{:S(2)}) collective-permute-start(bf16[64,128]{1,0:T(8,128)(2,1)S(1)} %get-tuple-element.54.refs_5_), channel_id=1, source_target_pairs={{0,9},{1,11},{2,8},{3,10},{4,13},{5,15},{6,12},{7,14},{8,1},{9,3},... | collective-permute-start | bytes 49160 | tf_op jit(solution)/shard_map/ppermute | solution.py:329
  19.2 1.3 %own.3 = (f32[64,1024]{1,0:T(8,128)S(1)}, bf16[4,64,1024]{2,1,0:T(8,128)(2,1)}) custom-call(s32[1]{0:T(128)} %bitcast.index_ref.refs_0_, bf16[64,1024]{1,0:T(8,128)(2,1)S(1)} %get-tuple-element.50.refs_1_, bf16[64,1536]{1,0:T(8,128)(2,1)S(1)} %collective-permute-done.4.message_ref.refs_2_, bf16[36,256,256]{2,1,0:T(8,128)(2,1)S(1)} %get-tuple-element.46.d_ref.refs_3_, ...), custom_call_target="tpu_custom_call" | custom-call | flops 1000000000 | bytes 4194304 | tf_op jit(solution)/shard_map/own/pallas_call | solution.py:255
  20.5 1.3 %collective-permute-done.5.over_ref = bf16[64,1024]{1,0:T(8,128)(2,1)S(1)} collective-permute-done((bf16[64,1024]{1,0:T(8,128)(2,1)S(1)}, bf16[64,1024]{1,0:T(8,128)(2,1)S(1)}, u32[]{:S(2)}, u32[]{:S(2)}) %collective-permute-start.5) | collective-permute-done | bytes 131104 | tf_op jit(solution)/shard_map/ppermute | solution.py:316
  21.8 0.5 %halo.5.refs_1_ = f32[64,1024]{1,0:T(8,128)S(1)} custom-call(s32[1]{0:T(128)} %bitcast.index_ref.refs_0_, f32[64,1024]{1,0:T(8,128)S(1)} %get-tuple-element.55.acc_ref, bf16[64,1024]{1,0:T(8,128)(2,1)S(1)} %collective-permute-done.5.over_ref, bf16[36,256,256]{2,1,0:T(8,128)(2,1)S(1)} %get-tuple-element.46.d_ref.refs_3_), custom_call_target="tpu_custom_call" | custom-call | flops 1000000000 | bytes 4194304 | tf_op jit(solution)/shard_map/halo/pallas_call | solution.py:255
  22.3 0.0 collective-permute-done.6.refs_5_
  22.3 2.0 %collective-permute-done.7.refs_6_ = bf16[64,128]{1,0:T(8,128)(2,1)S(1)} collective-permute-done((bf16[64,128]{1,0:T(8,128)(2,1)S(1)}, bf16[64,128]{1,0:T(8,128)(2,1)S(1)}, u32[]{:S(2)}, u32[]{:S(2)}) %collective-permute-start.7) | collective-permute-done | bytes 16416 | tf_op jit(solution)/shard_map/ppermute | solution.py:329
  24.3 0.6 %finish.4 = (bf16[64,1024]{1,0:T(8,128)(2,1)S(1)}, bf16[64,1536]{1,0:T(8,128)(2,1)S(1)}, f32[64,256]{1,0:T(8,128)S(1)}) custom-call(s32[1]{0:T(128)} %bitcast.index_ref.refs_0_, f32[64,1024]{1,0:T(8,128)S(1)} %halo.5.refs_1_, bf16[256,1024]{1,0:T(8,128)(2,1)S(1)} %get-tuple-element.47.refs_2_.refs_1_, bf16[128,1024]{1,0:T(8,128)(2,1)S(1)} %get-tuple-element.48.refs_3_, ...), custom_call_target="tpu_custom_call" | custom-call | flops 1000000000 | bytes 4194304 | tf_op jit(solution)/shard_map/finish/pallas_call | solution.py:255
  24.9 0.1 collective-permute-start.8
  24.9 1.6 %collective-permute-start.9 = (bf16[64,1024]{1,0:T(8,128)(2,1)S(1)}, bf16[64,1024]{1,0:T(8,128)(2,1)S(1)}, u32[]{:S(2)}, u32[]{:S(2)}) collective-permute-start(bf16[64,1024]{1,0:T(8,128)(2,1)S(1)} %get-tuple-element.56.refs_1_), channel_id=1, source_target_pairs={{0,15},{1,2},{2,1},{3,4},{4,3},{5,6},{6,5},{7,8},{8,7},{9,10},{10,... | collective-permute-start | bytes 393224 | tf_op jit(solution)/shard_map/ppermute | solution.py:316
  26.5 0.0 collective-permute-done.8.message_ref.refs_2_
  26.6 1.4 %collective-permute-start.10 = (bf16[64,128]{1,0:T(8,128)(2,1)S(1)}, bf16[64,128]{1,0:T(8,128)(2,1)S(1)}, u32[]{:S(2)}, u32[]{:S(2)}) collective-permute-start(bf16[64,128]{1,0:T(8,128)(2,1)S(1)} %get-tuple-element.59.refs_4_), channel_id=1, source_target_pairs={{0,8},{1,10},{2,9},{3,11},{4,12},{5,14},{6,13},{7,15},{8,0},{9,2},... | collective-permute-start | bytes 49160 | tf_op jit(solution)/shard_map/ppermute | solution.py:329
  28.0 1.2 %collective-permute-start.11 = (bf16[64,128]{1,0:T(8,128)(2,1)S(1)}, bf16[64,128]{1,0:T(8,128)(2,1)S(1)}, u32[]{:S(2)}, u32[]{:S(2)}) collective-permute-start(bf16[64,128]{1,0:T(8,128)(2,1)S(1)} %get-tuple-element.60.refs_5_), channel_id=1, source_target_pairs={{0,9},{1,11},{2,8},{3,10},{4,13},{5,15},{6,12},{7,14},{8,1},{9,3},... | collective-permute-start | bytes 49160 | tf_op jit(solution)/shard_map/ppermute | solution.py:329
  29.2 1.3 %own.4 = (f32[64,1024]{1,0:T(8,128)S(1)}, bf16[4,64,1024]{2,1,0:T(8,128)(2,1)}) custom-call(s32[1]{0:T(128)} %bitcast.index_ref.refs_0_, bf16[64,1024]{1,0:T(8,128)(2,1)S(1)} %get-tuple-element.56.refs_1_, bf16[64,1536]{1,0:T(8,128)(2,1)S(1)} %collective-permute-done.8.message_ref.refs_2_, ...), custom_call_target="tpu_custom_call", output_to_operand_aliasing={{1}: (6, {})} | custom-call | flops 1000000000 | bytes 4194304 | tf_op jit(solution)/shard_map/own/pallas_call | solution.py:255
  30.5 1.6 %collective-permute-done.9.over_ref = bf16[64,1024]{1,0:T(8,128)(2,1)S(1)} collective-permute-done((bf16[64,1024]{1,0:T(8,128)(2,1)S(1)}, bf16[64,1024]{1,0:T(8,128)(2,1)S(1)}, u32[]{:S(2)}, u32[]{:S(2)}) %collective-permute-start.9) | collective-permute-done | bytes 131104 | tf_op jit(solution)/shard_map/ppermute | solution.py:316
  32.2 0.5 %halo.6.refs_1_ = f32[64,1024]{1,0:T(8,128)S(1)} custom-call(s32[1]{0:T(128)} %bitcast.index_ref.refs_0_, f32[64,1024]{1,0:T(8,128)S(1)} %get-tuple-element.62.acc_ref, bf16[64,1024]{1,0:T(8,128)(2,1)S(1)} %collective-permute-done.9.over_ref, bf16[36,256,256]{2,1,0:T(8,128)(2,1)S(1)} %get-tuple-element.46.d_ref.refs_3_), custom_call_target="tpu_custom_call" | custom-call | flops 1000000000 | bytes 4194304 | tf_op jit(solution)/shard_map/halo/pallas_call | solution.py:255
  32.7 0.0 collective-permute-done.10.refs_5_
  32.7 0.9 %collective-permute-done.11.refs_6_ = bf16[64,128]{1,0:T(8,128)(2,1)S(1)} collective-permute-done((bf16[64,128]{1,0:T(8,128)(2,1)S(1)}, bf16[64,128]{1,0:T(8,128)(2,1)S(1)}, u32[]{:S(2)}, u32[]{:S(2)}) %collective-permute-start.11) | collective-permute-done | bytes 16416 | tf_op jit(solution)/shard_map/ppermute | solution.py:329
  33.6 0.6 %finish.5 = (bf16[64,1024]{1,0:T(8,128)(2,1)S(1)}, bf16[64,1536]{1,0:T(8,128)(2,1)S(1)}, f32[64,256]{1,0:T(8,128)S(1)}) custom-call(s32[1]{0:T(128)} %bitcast.index_ref.refs_0_, f32[64,1024]{1,0:T(8,128)S(1)} %halo.6.refs_1_, bf16[256,1024]{1,0:T(8,128)(2,1)S(1)} %get-tuple-element.47.refs_2_.refs_1_, bf16[128,1024]{1,0:T(8,128)(2,1)S(1)} %get-tuple-element.48.refs_3_, ...), custom_call_target="tpu_custom_call" | custom-call | flops 1000000000 | bytes 4194304 | tf_op jit(solution)/shard_map/finish/pallas_call | solution.py:255
  34.1 0.1 collective-permute-start.12
  34.2 1.6 %collective-permute-start.13 = (bf16[64,1024]{1,0:T(8,128)(2,1)S(1)}, bf16[64,1024]{1,0:T(8,128)(2,1)S(1)}, u32[]{:S(2)}, u32[]{:S(2)}) collective-permute-start(bf16[64,1024]{1,0:T(8,128)(2,1)S(1)} %get-tuple-element.63.refs_1_), channel_id=1, source_target_pairs={{0,15},{1,2},{2,1},{3,4},{4,3},{5,6},{6,5},{7,8},{8,7},{9,10},{10,... | collective-permute-start | bytes 393224 | tf_op jit(solution)/shard_map/ppermute | solution.py:316
  35.8 0.0 collective-permute-done.12.message_ref.refs_2_
  35.8 1.5 %collective-permute-start.14 = (bf16[64,128]{1,0:T(8,128)(2,1)S(1)}, bf16[64,128]{1,0:T(8,128)(2,1)S(1)}, u32[]{:S(2)}, u32[]{:S(2)}) collective-permute-start(bf16[64,128]{1,0:T(8,128)(2,1)S(1)} %get-tuple-element.66.refs_4_), channel_id=1, source_target_pairs={{0,8},{1,10},{2,9},{3,11},{4,12},{5,14},{6,13},{7,15},{8,0},{9,2},... | collective-permute-start | bytes 49160 | tf_op jit(solution)/shard_map/ppermute | solution.py:329
  37.3 1.2 %collective-permute-start.15 = (bf16[64,128]{1,0:T(8,128)(2,1)S(1)}, bf16[64,128]{1,0:T(8,128)(2,1)S(1)}, u32[]{:S(2)}, u32[]{:S(2)}) collective-permute-start(bf16[64,128]{1,0:T(8,128)(2,1)S(1)} %get-tuple-element.67.refs_5_), channel_id=1, source_target_pairs={{0,9},{1,11},{2,8},{3,10},{4,13},{5,15},{6,12},{7,14},{8,1},{9,3},... | collective-permute-start | bytes 49160 | tf_op jit(solution)/shard_map/ppermute | solution.py:329
  38.5 1.3 %own.5 = (f32[64,1024]{1,0:T(8,128)S(1)}, bf16[4,64,1024]{2,1,0:T(8,128)(2,1)}) custom-call(s32[1]{0:T(128)} %bitcast.index_ref.refs_0_, bf16[64,1024]{1,0:T(8,128)(2,1)S(1)} %get-tuple-element.63.refs_1_, bf16[64,1536]{1,0:T(8,128)(2,1)S(1)} %collective-permute-done.12.message_ref.refs_2_, ...), custom_call_target="tpu_custom_call", output_to_operand_aliasing={{1}: (6, {})} | custom-call | flops 1000000000 | bytes 4194304 | tf_op jit(solution)/shard_map/own/pallas_call | solution.py:255
  39.8 1.8 %collective-permute-done.13.over_ref = bf16[64,1024]{1,0:T(8,128)(2,1)S(1)} collective-permute-done((bf16[64,1024]{1,0:T(8,128)(2,1)S(1)}, bf16[64,1024]{1,0:T(8,128)(2,1)S(1)}, u32[]{:S(2)}, u32[]{:S(2)}) %collective-permute-start.13) | collective-permute-done | bytes 131104 | tf_op jit(solution)/shard_map/ppermute | solution.py:316
  41.6 0.5 %halo.7.refs_0_ = f32[64,1024]{1,0:T(8,128)S(1)} custom-call(s32[1]{0:T(128)} %bitcast.index_ref.refs_0_, f32[64,1024]{1,0:T(8,128)S(1)} %get-tuple-element.69.acc_ref, bf16[64,1024]{1,0:T(8,128)(2,1)S(1)} %collective-permute-done.13.over_ref, bf16[36,256,256]{2,1,0:T(8,128)(2,1)S(1)} %get-tuple-element.46.d_ref.refs_3_), custom_call_target="tpu_custom_call" | custom-call | flops 1000000000 | bytes 4194304 | tf_op jit(solution)/shard_map/halo/pallas_call | solution.py:255
  42.2 0.0 collective-permute-done.14.refs_2_
  42.2 0.7 %collective-permute-done.15.refs_3_ = bf16[64,128]{1,0:T(8,128)(2,1)S(1)} collective-permute-done((bf16[64,128]{1,0:T(8,128)(2,1)S(1)}, bf16[64,128]{1,0:T(8,128)(2,1)S(1)}, u32[]{:S(2)}, u32[]{:S(2)}) %collective-permute-start.15) | collective-permute-done | bytes 16416 | tf_op jit(solution)/shard_map/ppermute | solution.py:329
  42.8 0.9 %last.1 = bf16[4,64,1024]{2,1,0:T(8,128)(2,1)} custom-call(f32[64,1024]{1,0:T(8,128)S(1)} %halo.7.refs_0_, bf16[256,1024]{1,0:T(8,128)(2,1)S(1)} %get-tuple-element.47.refs_2_.refs_1_, bf16[64,128]{1,0:T(8,128)(2,1)S(1)} %collective-permute-done.14.refs_2_, bf16[64,128]{1,0:T(8,128)(2,1)S(1)} %collective-permute-done.15.refs_3_, ...), custom_call_target="tpu_custom_call", output_to_operand_aliasing={{}: (4, {})} | custom-call | flops 1000000000 | bytes 4194304 | tf_op jit(solution)/shard_map/last/pallas_call | solution.py:255
  (4 shorter events, 0.1 us)
Async XLA Ops:
  0.0 8.5 %copy-start.1 = (bf16[4,32,256]{2,1,0:T(8,128)(2,1)S(1)}, bf16[4,32,256]{2,1,0:T(8,128)(2,1)}, u32[]{:S(2)}) copy-start(bf16[4,32,256]{2,1,0:T(8,128)(2,1)} %refs_5_.3) | copy-start | bytes 196612
  0.0 8.5 %copy-start = (bf16[32,256,256]{2,1,0:T(8,128)(2,1)S(1)}, bf16[32,256,256]{2,1,0:T(8,128)(2,1)}, u32[]{:S(2)}) copy-start(bf16[32,256,256]{2,1,0:T(8,128)(2,1)} %refs_6_.3) | copy-start | bytes 12582916
  1.8 6.2 %collective-permute-start = (bf16[64,1536]{1,0:T(8,128)(2,1)S(1)}, bf16[64,1536]{1,0:T(8,128)(2,1)S(1)}, u32[]{:S(2)}, u32[]{:S(2)}) collective-permute-start(bf16[64,1536]{1,0:T(8,128)(2,1)S(1)} %get-tuple-element.41), channel_id=1, source_target_pairs={{0,1},{1,0},{2,3},{3,2},{4,5},{5,4},{6,7},{7,6},{8,9},{9,8},{10,11... | collective-permute-start | bytes 589832 | tf_op jit(solution)/shard_map/ppermute | solution.py:317
  2.4 8.4 %collective-permute-start.1 = (bf16[64,1024]{1,0:T(8,128)(2,1)S(1)}, bf16[64,1024]{1,0:T(8,128)(2,1)S(1)}, u32[]{:S(2)}, u32[]{:S(2)}) collective-permute-start(bf16[64,1024]{1,0:T(8,128)(2,1)S(1)} %get-tuple-element.40.refs_3_), channel_id=1, source_target_pairs={{0,15},{1,2},{2,1},{3,4},{4,3},{5,6},{6,5},{7,8},{8,7},{9,10},{10,... | collective-permute-start | bytes 393224 | tf_op jit(solution)/shard_map/ppermute | solution.py:316
  8.0 4.7 %collective-permute-start.2 = (bf16[64,128]{1,0:T(8,128)(2,1)S(1)}, bf16[64,128]{1,0:T(8,128)(2,1)S(1)}, u32[]{:S(2)}, u32[]{:S(2)}) collective-permute-start(bf16[64,128]{1,0:T(8,128)(2,1)S(1)} %get-tuple-element.43.refs_7_), channel_id=1, source_target_pairs={{0,8},{1,10},{2,9},{3,11},{4,12},{5,14},{6,13},{7,15},{8,0},{9,2},... | collective-permute-start | bytes 49160 | tf_op jit(solution)/shard_map/ppermute | solution.py:329
  8.1 5.6 %collective-permute-start.3 = (bf16[64,128]{1,0:T(8,128)(2,1)S(1)}, bf16[64,128]{1,0:T(8,128)(2,1)S(1)}, u32[]{:S(2)}, u32[]{:S(2)}) collective-permute-start(bf16[64,128]{1,0:T(8,128)(2,1)S(1)} %get-tuple-element.44.refs_8_), channel_id=1, source_target_pairs={{0,9},{1,11},{2,8},{3,10},{4,13},{5,15},{6,12},{7,14},{8,1},{9,3},... | collective-permute-start | bytes 49160 | tf_op jit(solution)/shard_map/ppermute | solution.py:329
  14.3 3.0 %collective-permute-start.4 = (bf16[64,1536]{1,0:T(8,128)(2,1)S(1)}, bf16[64,1536]{1,0:T(8,128)(2,1)S(1)}, u32[]{:S(2)}, u32[]{:S(2)}) collective-permute-start(bf16[64,1536]{1,0:T(8,128)(2,1)S(1)} %get-tuple-element.51), channel_id=1, source_target_pairs={{0,1},{1,0},{2,3},{3,2},{4,5},{5,4},{6,7},{7,6},{8,9},{9,8},{10,11... | collective-permute-start | bytes 589832 | tf_op jit(solution)/shard_map/ppermute | solution.py:317
  14.4 7.4 %collective-permute-start.5 = (bf16[64,1024]{1,0:T(8,128)(2,1)S(1)}, bf16[64,1024]{1,0:T(8,128)(2,1)S(1)}, u32[]{:S(2)}, u32[]{:S(2)}) collective-permute-start(bf16[64,1024]{1,0:T(8,128)(2,1)S(1)} %get-tuple-element.50.refs_1_), channel_id=1, source_target_pairs={{0,15},{1,2},{2,1},{3,4},{4,3},{5,6},{6,5},{7,8},{8,7},{9,10},{10,... | collective-permute-start | bytes 393224 | tf_op jit(solution)/shard_map/ppermute | solution.py:316
  17.3 5.0 %collective-permute-start.6 = (bf16[64,128]{1,0:T(8,128)(2,1)S(1)}, bf16[64,128]{1,0:T(8,128)(2,1)S(1)}, u32[]{:S(2)}, u32[]{:S(2)}) collective-permute-start(bf16[64,128]{1,0:T(8,128)(2,1)S(1)} %get-tuple-element.53.refs_4_), channel_id=1, source_target_pairs={{0,8},{1,10},{2,9},{3,11},{4,12},{5,14},{6,13},{7,15},{8,0},{9,2},... | collective-permute-start | bytes 49160 | tf_op jit(solution)/shard_map/ppermute | solution.py:329
  18.7 5.5 %collective-permute-start.7 = (bf16[64,128]{1,0:T(8,128)(2,1)S(1)}, bf16[64,128]{1,0:T(8,128)(2,1)S(1)}, u32[]{:S(2)}, u32[]{:S(2)}) collective-permute-start(bf16[64,128]{1,0:T(8,128)(2,1)S(1)} %get-tuple-element.54.refs_5_), channel_id=1, source_target_pairs={{0,9},{1,11},{2,8},{3,10},{4,13},{5,15},{6,12},{7,14},{8,1},{9,3},... | collective-permute-start | bytes 49160 | tf_op jit(solution)/shard_map/ppermute | solution.py:329
  24.9 1.7 %collective-permute-start.8 = (bf16[64,1536]{1,0:T(8,128)(2,1)S(1)}, bf16[64,1536]{1,0:T(8,128)(2,1)S(1)}, u32[]{:S(2)}, u32[]{:S(2)}) collective-permute-start(bf16[64,1536]{1,0:T(8,128)(2,1)S(1)} %get-tuple-element.57), channel_id=1, source_target_pairs={{0,1},{1,0},{2,3},{3,2},{4,5},{5,4},{6,7},{7,6},{8,9},{9,8},{10,11... | collective-permute-start | bytes 589832 | tf_op jit(solution)/shard_map/ppermute | solution.py:317
  24.9 7.2 %collective-permute-start.9 = (bf16[64,1024]{1,0:T(8,128)(2,1)S(1)}, bf16[64,1024]{1,0:T(8,128)(2,1)S(1)}, u32[]{:S(2)}, u32[]{:S(2)}) collective-permute-start(bf16[64,1024]{1,0:T(8,128)(2,1)S(1)} %get-tuple-element.56.refs_1_), channel_id=1, source_target_pairs={{0,15},{1,2},{2,1},{3,4},{4,3},{5,6},{6,5},{7,8},{8,7},{9,10},{10,... | collective-permute-start | bytes 393224 | tf_op jit(solution)/shard_map/ppermute | solution.py:316
  26.6 6.1 %collective-permute-start.10 = (bf16[64,128]{1,0:T(8,128)(2,1)S(1)}, bf16[64,128]{1,0:T(8,128)(2,1)S(1)}, u32[]{:S(2)}, u32[]{:S(2)}) collective-permute-start(bf16[64,128]{1,0:T(8,128)(2,1)S(1)} %get-tuple-element.59.refs_4_), channel_id=1, source_target_pairs={{0,8},{1,10},{2,9},{3,11},{4,12},{5,14},{6,13},{7,15},{8,0},{9,2},... | collective-permute-start | bytes 49160 | tf_op jit(solution)/shard_map/ppermute | solution.py:329
  28.0 5.5 %collective-permute-start.11 = (bf16[64,128]{1,0:T(8,128)(2,1)S(1)}, bf16[64,128]{1,0:T(8,128)(2,1)S(1)}, u32[]{:S(2)}, u32[]{:S(2)}) collective-permute-start(bf16[64,128]{1,0:T(8,128)(2,1)S(1)} %get-tuple-element.60.refs_5_), channel_id=1, source_target_pairs={{0,9},{1,11},{2,8},{3,10},{4,13},{5,15},{6,12},{7,14},{8,1},{9,3},... | collective-permute-start | bytes 49160 | tf_op jit(solution)/shard_map/ppermute | solution.py:329
  34.1 1.7 %collective-permute-start.12 = (bf16[64,1536]{1,0:T(8,128)(2,1)S(1)}, bf16[64,1536]{1,0:T(8,128)(2,1)S(1)}, u32[]{:S(2)}, u32[]{:S(2)}) collective-permute-start(bf16[64,1536]{1,0:T(8,128)(2,1)S(1)} %get-tuple-element.64), channel_id=1, source_target_pairs={{0,1},{1,0},{2,3},{3,2},{4,5},{5,4},{6,7},{7,6},{8,9},{9,8},{10,11... | collective-permute-start | bytes 589832 | tf_op jit(solution)/shard_map/ppermute | solution.py:317
  34.2 7.4 %collective-permute-start.13 = (bf16[64,1024]{1,0:T(8,128)(2,1)S(1)}, bf16[64,1024]{1,0:T(8,128)(2,1)S(1)}, u32[]{:S(2)}, u32[]{:S(2)}) collective-permute-start(bf16[64,1024]{1,0:T(8,128)(2,1)S(1)} %get-tuple-element.63.refs_1_), channel_id=1, source_target_pairs={{0,15},{1,2},{2,1},{3,4},{4,3},{5,6},{6,5},{7,8},{8,7},{9,10},{10,... | collective-permute-start | bytes 393224 | tf_op jit(solution)/shard_map/ppermute | solution.py:316
  35.8 6.3 %collective-permute-start.14 = (bf16[64,128]{1,0:T(8,128)(2,1)S(1)}, bf16[64,128]{1,0:T(8,128)(2,1)S(1)}, u32[]{:S(2)}, u32[]{:S(2)}) collective-permute-start(bf16[64,128]{1,0:T(8,128)(2,1)S(1)} %get-tuple-element.66.refs_4_), channel_id=1, source_target_pairs={{0,8},{1,10},{2,9},{3,11},{4,12},{5,14},{6,13},{7,15},{8,0},{9,2},... | collective-permute-start | bytes 49160 | tf_op jit(solution)/shard_map/ppermute | solution.py:329
  37.3 5.5 %collective-permute-start.15 = (bf16[64,128]{1,0:T(8,128)(2,1)S(1)}, bf16[64,128]{1,0:T(8,128)(2,1)S(1)}, u32[]{:S(2)}, u32[]{:S(2)}) collective-permute-start(bf16[64,128]{1,0:T(8,128)(2,1)S(1)} %get-tuple-element.67.refs_5_), channel_id=1, source_target_pairs={{0,9},{1,11},{2,8},{3,10},{4,13},{5,15},{6,12},{7,14},{8,1},{9,3},... | collective-permute-start | bytes 49160 | tf_op jit(solution)/shard_map/ppermute | solution.py:329

commit v25 on v20

--- a/solution.py
+++ b/solution.py
@@ -11,7 +11,7 @@
 REACH = 4
 LEVELS = 3
 SPAN = 2 * REACH + 1
-OTHER_CORE_FIRST = 0b11011111
+OTHER_CORE_FIRST = 0b11011011
 
 F32 = jnp.float32
 BF16 = jnp.bfloat16
@@ -314,7 +314,7 @@
                 scratch=scratch_for(far_rows, far_cols, col_basis, couplings)
                 + [pltpu.VMEM(matrix[:2] + (width,), F32), pltpu.SemaphoreType.DMA((7,))],
             )
-        over = lax.ppermute(block if product == 0 else current, axes, plan.over)
+        over = lax.ppermute(current, axes, plan.over)
         near = lax.ppermute(sends[0] if plan.paired else current, axes, plan.near)
         if plan.paired:
             sends = call(

time: 41.9 us -> 41.8 us (level)
  no operation moved by 1% of the time
where the time goes in v25:
time: 41.8 us; the launch traced here: 41.6 us
  starting transfers between devices  19.4 us (46%)
  Pallas kernels  12.3 us (29%)
  waiting for transfers between devices  9.78 us (23%)
    ppermute x4, starting transfers between devices, on_device(): over = lax.ppermute(current, axes, plan.over)  15.2 us
    pallas_call x17, Pallas kernels, call(): pl.pallas_call(kernel, in_specs=list(specs), out_specs=out_specs or [IN_V...  12.3 us
    ppermute x4, waiting for transfers between devices, on_device(): over = lax.ppermute(current, axes, plan.over)  6.68 us
    ppermute x8, waiting for transfers between devices, on_device(): fars = [lax.ppermute(s, axes, route) for s, route in zip(sends, routes)]  3.08 us
    ppermute x8, starting transfers between devices, on_device(): fars = [lax.ppermute(s, axes, route) for s, route in zip(sends, routes)]  2.6 us
    ppermute x4, starting transfers between devices, on_device(): near = lax.ppermute(sends[0] if plan.paired else current, axes, plan.near)  1.55 us
  transfers between devices with their start and end apart: 16, of which 8 were waited for; matrix products, arithmetic and copies ran while one was open for 0% of the time, Pallas kernels for 19%

profile of v25, /device:TPU:0, one launch (start us, length us, event | category | flops | bytes accessed | tf_op | source)
XLA Modules:
  0.0 41.6 jit_solution(6546717685416154077)
XLA Ops:
  0.0 0.0 copy-start.1
  0.0 0.0 copy-start
  0.0 1.8 %prepare.1 = (bf16[64,1024]{1,0:T(8,128)(2,1)S(1)}, bf16[1,512,256]{2,1,0:T(8,128)(2,1)S(1)}, bf16[128,1024]{1,0:T(8,128)(2,1)S(1)}, s32[32]{0:T(128)S(4)}, s32[...) custom-call(s32[1]{0:T(128)} %bitcast.index_ref.refs_0_, s32[32]{0:T(128)} %refs_0_.1, s32[32]{0:T(128)} %refs_1_.1, ...), custom_call_target="tpu_custom_call" | custom-call | flops 1000000000 | bytes 4194304 | tf_op jit(solution)/shard_map/prepare/pallas_call | solution.py:256
  1.8 0.5 %collective-permute-start = (bf16[64,1536]{1,0:T(8,128)(2,1)S(1)}, bf16[64,1536]{1,0:T(8,128)(2,1)S(1)}, u32[]{:S(2)}, u32[]{:S(2)}) collective-permute-start(bf16[64,1536]{1,0:T(8,128)(2,1)S(1)} %get-tuple-element.41), channel_id=1, source_target_pairs={{0,1},{1,0},{2,3},{3,2},{4,5},{5,4},{6,7},{7,6},{8,9},{9,8},{10,11... | collective-permute-start | bytes 589832 | tf_op jit(solution)/shard_map/ppermute | solution.py:318
  2.4 5.6 %collective-permute-start.1 = (bf16[64,1024]{1,0:T(8,128)(2,1)S(1)}, bf16[64,1024]{1,0:T(8,128)(2,1)S(1)}, u32[]{:S(2)}, u32[]{:S(2)}) collective-permute-start(bf16[64,1024]{1,0:T(8,128)(2,1)S(1)} %get-tuple-element.40.refs_3_), channel_id=1, source_target_pairs={{0,15},{1,2},{2,1},{3,4},{4,3},{5,6},{6,5},{7,8},{8,7},{9,10},{10,... | collective-permute-start | bytes 393224 | tf_op jit(solution)/shard_map/ppermute | solution.py:317
  8.0 0.0 collective-permute-done.message_ref.refs_4_
  8.0 0.1 collective-permute-start.2
  8.1 0.1 collective-permute-start.3
  8.2 0.0 copy-done.1
  8.2 0.0 copy-done
  8.2 1.9 %first_own.1 = (f32[64,1024]{1,0:T(8,128)S(1)}, bf16[36,256,256]{2,1,0:T(8,128)(2,1)S(1)}, bf16[256,1024]{1,0:T(8,128)(2,1)S(1)}) custom-call(s32[1]{0:T(128)} %bitcast.index_ref.refs_0_, s32[32]{0:T(128)S(4)} %get-tuple-element.38.refs_1_, s32[32]{0:T(128)S(4)} %get-tuple-element.39.refs_2_, bf16[64,1024]{1,0:T(8,128)(2,1)S(1)} %get-tuple-element.40.refs_3_, ...), custom_call_target="tpu_custom_call" | custom-call | flops 1000000000 | bytes 4194304 | tf_op jit(solution)/shard_map/first_own/pallas_call | solution.py:256
  10.1 0.6 %collective-permute-done.1.over_ref = bf16[64,1024]{1,0:T(8,128)(2,1)S(1)} collective-permute-done((bf16[64,1024]{1,0:T(8,128)(2,1)S(1)}, bf16[64,1024]{1,0:T(8,128)(2,1)S(1)}, u32[]{:S(2)}, u32[]{:S(2)}) %collective-permute-start.1) | collective-permute-done | bytes 131104 | tf_op jit(solution)/shard_map/ppermute | solution.py:317
  10.7 0.5 %halo.4.refs_1_ = f32[64,1024]{1,0:T(8,128)S(1)} custom-call(s32[1]{0:T(128)} %bitcast.index_ref.refs_0_, f32[64,1024]{1,0:T(8,128)S(1)} %get-tuple-element.45.acc_ref, bf16[64,1024]{1,0:T(8,128)(2,1)S(1)} %collective-permute-done.1.over_ref, bf16[36,256,256]{2,1,0:T(8,128)(2,1)S(1)} %get-tuple-element.46.d_ref.refs_3_), custom_call_target="tpu_custom_call" | custom-call | flops 1000000000 | bytes 4194304 | tf_op jit(solution)/shard_map/halo/pallas_call | solution.py:256
  11.2 2.0 %collective-permute-done.2.refs_5_ = bf16[64,128]{1,0:T(8,128)(2,1)S(1)} collective-permute-done((bf16[64,128]{1,0:T(8,128)(2,1)S(1)}, bf16[64,128]{1,0:T(8,128)(2,1)S(1)}, u32[]{:S(2)}, u32[]{:S(2)}) %collective-permute-start.2) | collective-permute-done | bytes 16416 | tf_op jit(solution)/shard_map/ppermute | solution.py:330
  13.2 0.0 collective-permute-done.3.refs_6_
  13.2 0.6 %finish.3 = (bf16[64,1024]{1,0:T(8,128)(2,1)S(1)}, bf16[64,1536]{1,0:T(8,128)(2,1)S(1)}, f32[64,256]{1,0:T(8,128)S(1)}) custom-call(s32[1]{0:T(128)} %bitcast.index_ref.refs_0_, f32[64,1024]{1,0:T(8,128)S(1)} %halo.4.refs_1_, bf16[256,1024]{1,0:T(8,128)(2,1)S(1)} %get-tuple-element.47.refs_2_.refs_1_, bf16[128,1024]{1,0:T(8,128)(2,1)S(1)} %get-tuple-element.48.refs_3_, ...), custom_call_target="tpu_custom_call" | custom-call | flops 1000000000 | bytes 4194304 | tf_op jit(solution)/shard_map/finish/pallas_call | solution.py:256
  13.8 0.2 collective-permute-start.4
  14.0 3.2 %collective-permute-start.5 = (bf16[64,1024]{1,0:T(8,128)(2,1)S(1)}, bf16[64,1024]{1,0:T(8,128)(2,1)S(1)}, u32[]{:S(2)}, u32[]{:S(2)}) collective-permute-start(bf16[64,1024]{1,0:T(8,128)(2,1)S(1)} %get-tuple-element.50.refs_1_), channel_id=1, source_target_pairs={{0,15},{1,2},{2,1},{3,4},{4,3},{5,6},{6,5},{7,8},{8,7},{9,10},{10,... | collective-permute-start | bytes 393224 | tf_op jit(solution)/shard_map/ppermute | solution.py:317
  17.2 0.0 collective-permute-done.4.message_ref.refs_2_
  17.2 0.1 collective-permute-start.6
  17.3 0.8 %collective-permute-start.7 = (bf16[64,128]{1,0:T(8,128)(2,1)S(1)}, bf16[64,128]{1,0:T(8,128)(2,1)S(1)}, u32[]{:S(2)}, u32[]{:S(2)}) collective-permute-start(bf16[64,128]{1,0:T(8,128)(2,1)S(1)} %get-tuple-element.54.refs_5_), channel_id=1, source_target_pairs={{0,8},{1,10},{2,11},{3,9},{4,12},{5,15},{6,14},{7,13},{8,0},{9,3},... | collective-permute-start | bytes 49160 | tf_op jit(solution)/shard_map/ppermute | solution.py:330
  18.1 1.3 %own.3 = (f32[64,1024]{1,0:T(8,128)S(1)}, bf16[4,64,1024]{2,1,0:T(8,128)(2,1)}) custom-call(s32[1]{0:T(128)} %bitcast.index_ref.refs_0_, bf16[64,1024]{1,0:T(8,128)(2,1)S(1)} %get-tuple-element.50.refs_1_, bf16[64,1536]{1,0:T(8,128)(2,1)S(1)} %collective-permute-done.4.message_ref.refs_2_, bf16[36,256,256]{2,1,0:T(8,128)(2,1)S(1)} %get-tuple-element.46.d_ref.refs_3_, ...), custom_call_target="tpu_custom_call" | custom-call | flops 1000000000 | bytes 4194304 | tf_op jit(solution)/shard_map/own/pallas_call | solution.py:256
  19.4 2.0 %collective-permute-done.5.over_ref = bf16[64,1024]{1,0:T(8,128)(2,1)S(1)} collective-permute-done((bf16[64,1024]{1,0:T(8,128)(2,1)S(1)}, bf16[64,1024]{1,0:T(8,128)(2,1)S(1)}, u32[]{:S(2)}, u32[]{:S(2)}) %collective-permute-start.5) | collective-permute-done | bytes 131104 | tf_op jit(solution)/shard_map/ppermute | solution.py:317
  21.4 0.5 %halo.5.refs_1_ = f32[64,1024]{1,0:T(8,128)S(1)} custom-call(s32[1]{0:T(128)} %bitcast.index_ref.refs_0_, f32[64,1024]{1,0:T(8,128)S(1)} %get-tuple-element.55.acc_ref, bf16[64,1024]{1,0:T(8,128)(2,1)S(1)} %collective-permute-done.5.over_ref, bf16[36,256,256]{2,1,0:T(8,128)(2,1)S(1)} %get-tuple-element.46.d_ref.refs_3_), custom_call_target="tpu_custom_call" | custom-call | flops 1000000000 | bytes 4194304 | tf_op jit(solution)/shard_map/halo/pallas_call | solution.py:256
  21.9 0.3 collective-permute-done.6.refs_5_
  22.3 0.0 collective-permute-done.7.refs_6_
  22.3 0.6 %finish.4 = (bf16[64,1024]{1,0:T(8,128)(2,1)S(1)}, bf16[64,1536]{1,0:T(8,128)(2,1)S(1)}, f32[64,256]{1,0:T(8,128)S(1)}) custom-call(s32[1]{0:T(128)} %bitcast.index_ref.refs_0_, f32[64,1024]{1,0:T(8,128)S(1)} %halo.5.refs_1_, bf16[256,1024]{1,0:T(8,128)(2,1)S(1)} %get-tuple-element.47.refs_2_.refs_1_, bf16[128,1024]{1,0:T(8,128)(2,1)S(1)} %get-tuple-element.48.refs_3_, ...), custom_call_target="tpu_custom_call" | custom-call | flops 1000000000 | bytes 4194304 | tf_op jit(solution)/shard_map/finish/pallas_call | solution.py:256
  22.9 0.5 %collective-permute-start.8 = (bf16[64,1536]{1,0:T(8,128)(2,1)S(1)}, bf16[64,1536]{1,0:T(8,128)(2,1)S(1)}, u32[]{:S(2)}, u32[]{:S(2)}) collective-permute-start(bf16[64,1536]{1,0:T(8,128)(2,1)S(1)} %get-tuple-element.57), channel_id=1, source_target_pairs={{0,1},{1,0},{2,3},{3,2},{4,5},{5,4},{6,7},{7,6},{8,9},{9,8},{10,11... | collective-permute-start | bytes 589832 | tf_op jit(solution)/shard_map/ppermute | solution.py:318
  23.4 3.1 %collective-permute-start.9 = (bf16[64,1024]{1,0:T(8,128)(2,1)S(1)}, bf16[64,1024]{1,0:T(8,128)(2,1)S(1)}, u32[]{:S(2)}, u32[]{:S(2)}) collective-permute-start(bf16[64,1024]{1,0:T(8,128)(2,1)S(1)} %get-tuple-element.56.refs_1_), channel_id=1, source_target_pairs={{0,15},{1,2},{2,1},{3,4},{4,3},{5,6},{6,5},{7,8},{8,7},{9,10},{10,... | collective-permute-start | bytes 393224 | tf_op jit(solution)/shard_map/ppermute | solution.py:317
  26.5 0.0 collective-permute-done.8.message_ref.refs_2_
  26.5 0.1 collective-permute-start.10
  26.6 0.9 %collective-permute-start.11 = (bf16[64,128]{1,0:T(8,128)(2,1)S(1)}, bf16[64,128]{1,0:T(8,128)(2,1)S(1)}, u32[]{:S(2)}, u32[]{:S(2)}) collective-permute-start(bf16[64,128]{1,0:T(8,128)(2,1)S(1)} %get-tuple-element.60.refs_5_), channel_id=1, source_target_pairs={{0,8},{1,10},{2,11},{3,9},{4,12},{5,15},{6,14},{7,13},{8,0},{9,3},... | collective-permute-start | bytes 49160 | tf_op jit(solution)/shard_map/ppermute | solution.py:330
  27.4 1.3 %own.4 = (f32[64,1024]{1,0:T(8,128)S(1)}, bf16[4,64,1024]{2,1,0:T(8,128)(2,1)}) custom-call(s32[1]{0:T(128)} %bitcast.index_ref.refs_0_, bf16[64,1024]{1,0:T(8,128)(2,1)S(1)} %get-tuple-element.56.refs_1_, bf16[64,1536]{1,0:T(8,128)(2,1)S(1)} %collective-permute-done.8.message_ref.refs_2_, ...), custom_call_target="tpu_custom_call", output_to_operand_aliasing={{1}: (6, {})} | custom-call | flops 1000000000 | bytes 4194304 | tf_op jit(solution)/shard_map/own/pallas_call | solution.py:256
  28.7 2.0 %collective-permute-done.9.over_ref = bf16[64,1024]{1,0:T(8,128)(2,1)S(1)} collective-permute-done((bf16[64,1024]{1,0:T(8,128)(2,1)S(1)}, bf16[64,1024]{1,0:T(8,128)(2,1)S(1)}, u32[]{:S(2)}, u32[]{:S(2)}) %collective-permute-start.9) | collective-permute-done | bytes 131104 | tf_op jit(solution)/shard_map/ppermute | solution.py:317
  30.7 0.5 %halo.6.refs_1_ = f32[64,1024]{1,0:T(8,128)S(1)} custom-call(s32[1]{0:T(128)} %bitcast.index_ref.refs_0_, f32[64,1024]{1,0:T(8,128)S(1)} %get-tuple-element.62.acc_ref, bf16[64,1024]{1,0:T(8,128)(2,1)S(1)} %collective-permute-done.9.over_ref, bf16[36,256,256]{2,1,0:T(8,128)(2,1)S(1)} %get-tuple-element.46.d_ref.refs_3_), custom_call_target="tpu_custom_call" | custom-call | flops 1000000000 | bytes 4194304 | tf_op jit(solution)/shard_map/halo/pallas_call | solution.py:256
  31.2 0.3 collective-permute-done.10.refs_5_
  31.5 0.0 collective-permute-done.11.refs_6_
  31.5 0.6 %finish.5 = (bf16[64,1024]{1,0:T(8,128)(2,1)S(1)}, bf16[64,1536]{1,0:T(8,128)(2,1)S(1)}, f32[64,256]{1,0:T(8,128)S(1)}) custom-call(s32[1]{0:T(128)} %bitcast.index_ref.refs_0_, f32[64,1024]{1,0:T(8,128)S(1)} %halo.6.refs_1_, bf16[256,1024]{1,0:T(8,128)(2,1)S(1)} %get-tuple-element.47.refs_2_.refs_1_, bf16[128,1024]{1,0:T(8,128)(2,1)S(1)} %get-tuple-element.48.refs_3_, ...), custom_call_target="tpu_custom_call" | custom-call | flops 1000000000 | bytes 4194304 | tf_op jit(solution)/shard_map/finish/pallas_call | solution.py:256
  32.1 0.3 collective-permute-start.12
  32.4 3.3 %collective-permute-start.13 = (bf16[64,1024]{1,0:T(8,128)(2,1)S(1)}, bf16[64,1024]{1,0:T(8,128)(2,1)S(1)}, u32[]{:S(2)}, u32[]{:S(2)}) collective-permute-start(bf16[64,1024]{1,0:T(8,128)(2,1)S(1)} %get-tuple-element.63.refs_1_), channel_id=1, source_target_pairs={{0,15},{1,2},{2,1},{3,4},{4,3},{5,6},{6,5},{7,8},{8,7},{9,10},{10,... | collective-permute-start | bytes 393224 | tf_op jit(solution)/shard_map/ppermute | solution.py:317
  35.7 0.0 collective-permute-done.12.message_ref.refs_2_
  35.7 0.1 collective-permute-start.14
  35.8 0.6 %collective-permute-start.15 = (bf16[64,128]{1,0:T(8,128)(2,1)S(1)}, bf16[64,128]{1,0:T(8,128)(2,1)S(1)}, u32[]{:S(2)}, u32[]{:S(2)}) collective-permute-start(bf16[64,128]{1,0:T(8,128)(2,1)S(1)} %get-tuple-element.67.refs_5_), channel_id=1, source_target_pairs={{0,8},{1,10},{2,11},{3,9},{4,12},{5,15},{6,14},{7,13},{8,0},{9,3},... | collective-permute-start | bytes 49160 | tf_op jit(solution)/shard_map/ppermute | solution.py:330
  36.5 1.3 %own.5 = (f32[64,1024]{1,0:T(8,128)S(1)}, bf16[4,64,1024]{2,1,0:T(8,128)(2,1)}) custom-call(s32[1]{0:T(128)} %bitcast.index_ref.refs_0_, bf16[64,1024]{1,0:T(8,128)(2,1)S(1)} %get-tuple-element.63.refs_1_, bf16[64,1536]{1,0:T(8,128)(2,1)S(1)} %collective-permute-done.12.message_ref.refs_2_, ...), custom_call_target="tpu_custom_call", output_to_operand_aliasing={{1}: (6, {})} | custom-call | flops 1000000000 | bytes 4194304 | tf_op jit(solution)/shard_map/own/pallas_call | solution.py:256
  37.8 2.0 %collective-permute-done.13.over_ref = bf16[64,1024]{1,0:T(8,128)(2,1)S(1)} collective-permute-done((bf16[64,1024]{1,0:T(8,128)(2,1)S(1)}, bf16[64,1024]{1,0:T(8,128)(2,1)S(1)}, u32[]{:S(2)}, u32[]{:S(2)}) %collective-permute-start.13) | collective-permute-done | bytes 131104 | tf_op jit(solution)/shard_map/ppermute | solution.py:317
  39.8 0.5 %halo.7.refs_0_ = f32[64,1024]{1,0:T(8,128)S(1)} custom-call(s32[1]{0:T(128)} %bitcast.index_ref.refs_0_, f32[64,1024]{1,0:T(8,128)S(1)} %get-tuple-element.69.acc_ref, bf16[64,1024]{1,0:T(8,128)(2,1)S(1)} %collective-permute-done.13.over_ref, bf16[36,256,256]{2,1,0:T(8,128)(2,1)S(1)} %get-tuple-element.46.d_ref.refs_3_), custom_call_target="tpu_custom_call" | custom-call | flops 1000000000 | bytes 4194304 | tf_op jit(solution)/shard_map/halo/pallas_call | solution.py:256
  40.3 0.5 %collective-permute-done.14.refs_2_ = bf16[64,128]{1,0:T(8,128)(2,1)S(1)} collective-permute-done((bf16[64,128]{1,0:T(8,128)(2,1)S(1)}, bf16[64,128]{1,0:T(8,128)(2,1)S(1)}, u32[]{:S(2)}, u32[]{:S(2)}) %collective-permute-start.14) | collective-permute-done | bytes 16416 | tf_op jit(solution)/shard_map/ppermute | solution.py:330
  40.8 0.0 collective-permute-done.15.refs_3_
  40.8 0.9 %last.1 = bf16[4,64,1024]{2,1,0:T(8,128)(2,1)} custom-call(f32[64,1024]{1,0:T(8,128)S(1)} %halo.7.refs_0_, bf16[256,1024]{1,0:T(8,128)(2,1)S(1)} %get-tuple-element.47.refs_2_.refs_1_, bf16[64,128]{1,0:T(8,128)(2,1)S(1)} %collective-permute-done.14.refs_2_, bf16[64,128]{1,0:T(8,128)(2,1)S(1)} %collective-permute-done.15.refs_3_, ...), custom_call_target="tpu_custom_call", output_to_operand_aliasing={{}: (4, {})} | custom-call | flops 1000000000 | bytes 4194304 | tf_op jit(solution)/shard_map/last/pallas_call | solution.py:256
  (4 shorter events, 0.1 us)
Async XLA Ops:
  0.0 8.2 %copy-start.1 = (bf16[4,32,256]{2,1,0:T(8,128)(2,1)S(1)}, bf16[4,32,256]{2,1,0:T(8,128)(2,1)}, u32[]{:S(2)}) copy-start(bf16[4,32,256]{2,1,0:T(8,128)(2,1)} %refs_5_.3) | copy-start | bytes 196612
  0.0 8.2 %copy-start = (bf16[32,256,256]{2,1,0:T(8,128)(2,1)S(1)}, bf16[32,256,256]{2,1,0:T(8,128)(2,1)}, u32[]{:S(2)}) copy-start(bf16[32,256,256]{2,1,0:T(8,128)(2,1)} %refs_6_.3) | copy-start | bytes 12582916
  1.8 6.2 %collective-permute-start = (bf16[64,1536]{1,0:T(8,128)(2,1)S(1)}, bf16[64,1536]{1,0:T(8,128)(2,1)S(1)}, u32[]{:S(2)}, u32[]{:S(2)}) collective-permute-start(bf16[64,1536]{1,0:T(8,128)(2,1)S(1)} %get-tuple-element.41), channel_id=1, source_target_pairs={{0,1},{1,0},{2,3},{3,2},{4,5},{5,4},{6,7},{7,6},{8,9},{9,8},{10,11... | collective-permute-start | bytes 589832 | tf_op jit(solution)/shard_map/ppermute | solution.py:318
  2.4 8.3 %collective-permute-start.1 = (bf16[64,1024]{1,0:T(8,128)(2,1)S(1)}, bf16[64,1024]{1,0:T(8,128)(2,1)S(1)}, u32[]{:S(2)}, u32[]{:S(2)}) collective-permute-start(bf16[64,1024]{1,0:T(8,128)(2,1)S(1)} %get-tuple-element.40.refs_3_), channel_id=1, source_target_pairs={{0,15},{1,2},{2,1},{3,4},{4,3},{5,6},{6,5},{7,8},{8,7},{9,10},{10,... | collective-permute-start | bytes 393224 | tf_op jit(solution)/shard_map/ppermute | solution.py:317
  8.0 5.2 %collective-permute-start.2 = (bf16[64,128]{1,0:T(8,128)(2,1)S(1)}, bf16[64,128]{1,0:T(8,128)(2,1)S(1)}, u32[]{:S(2)}, u32[]{:S(2)}) collective-permute-start(bf16[64,128]{1,0:T(8,128)(2,1)S(1)} %get-tuple-element.43.refs_7_), channel_id=1, source_target_pairs={{0,9},{1,11},{2,10},{3,8},{4,13},{5,14},{6,15},{7,12},{8,1},{9,2},... | collective-permute-start | bytes 49160 | tf_op jit(solution)/shard_map/ppermute | solution.py:330
  8.1 5.1 %collective-permute-start.3 = (bf16[64,128]{1,0:T(8,128)(2,1)S(1)}, bf16[64,128]{1,0:T(8,128)(2,1)S(1)}, u32[]{:S(2)}, u32[]{:S(2)}) collective-permute-start(bf16[64,128]{1,0:T(8,128)(2,1)S(1)} %get-tuple-element.44.refs_8_), channel_id=1, source_target_pairs={{0,8},{1,10},{2,11},{3,9},{4,12},{5,15},{6,14},{7,13},{8,0},{9,3},... | collective-permute-start | bytes 49160 | tf_op jit(solution)/shard_map/ppermute | solution.py:330
  13.8 3.4 %collective-permute-start.4 = (bf16[64,1536]{1,0:T(8,128)(2,1)S(1)}, bf16[64,1536]{1,0:T(8,128)(2,1)S(1)}, u32[]{:S(2)}, u32[]{:S(2)}) collective-permute-start(bf16[64,1536]{1,0:T(8,128)(2,1)S(1)} %get-tuple-element.51), channel_id=1, source_target_pairs={{0,1},{1,0},{2,3},{3,2},{4,5},{5,4},{6,7},{7,6},{8,9},{9,8},{10,11... | collective-permute-start | bytes 589832 | tf_op jit(solution)/shard_map/ppermute | solution.py:318
  14.0 7.4 %collective-permute-start.5 = (bf16[64,1024]{1,0:T(8,128)(2,1)S(1)}, bf16[64,1024]{1,0:T(8,128)(2,1)S(1)}, u32[]{:S(2)}, u32[]{:S(2)}) collective-permute-start(bf16[64,1024]{1,0:T(8,128)(2,1)S(1)} %get-tuple-element.50.refs_1_), channel_id=1, source_target_pairs={{0,15},{1,2},{2,1},{3,4},{4,3},{5,6},{6,5},{7,8},{8,7},{9,10},{10,... | collective-permute-start | bytes 393224 | tf_op jit(solution)/shard_map/ppermute | solution.py:317
  17.2 5.0 %collective-permute-start.6 = (bf16[64,128]{1,0:T(8,128)(2,1)S(1)}, bf16[64,128]{1,0:T(8,128)(2,1)S(1)}, u32[]{:S(2)}, u32[]{:S(2)}) collective-permute-start(bf16[64,128]{1,0:T(8,128)(2,1)S(1)} %get-tuple-element.53.refs_4_), channel_id=1, source_target_pairs={{0,9},{1,11},{2,10},{3,8},{4,13},{5,14},{6,15},{7,12},{8,1},{9,2},... | collective-permute-start | bytes 49160 | tf_op jit(solution)/shard_map/ppermute | solution.py:330
  17.3 5.0 %collective-permute-start.7 = (bf16[64,128]{1,0:T(8,128)(2,1)S(1)}, bf16[64,128]{1,0:T(8,128)(2,1)S(1)}, u32[]{:S(2)}, u32[]{:S(2)}) collective-permute-start(bf16[64,128]{1,0:T(8,128)(2,1)S(1)} %get-tuple-element.54.refs_5_), channel_id=1, source_target_pairs={{0,8},{1,10},{2,11},{3,9},{4,12},{5,15},{6,14},{7,13},{8,0},{9,3},... | collective-permute-start | bytes 49160 | tf_op jit(solution)/shard_map/ppermute | solution.py:330
  22.9 3.6 %collective-permute-start.8 = (bf16[64,1536]{1,0:T(8,128)(2,1)S(1)}, bf16[64,1536]{1,0:T(8,128)(2,1)S(1)}, u32[]{:S(2)}, u32[]{:S(2)}) collective-permute-start(bf16[64,1536]{1,0:T(8,128)(2,1)S(1)} %get-tuple-element.57), channel_id=1, source_target_pairs={{0,1},{1,0},{2,3},{3,2},{4,5},{5,4},{6,7},{7,6},{8,9},{9,8},{10,11... | collective-permute-start | bytes 589832 | tf_op jit(solution)/shard_map/ppermute | solution.py:318
  23.4 7.4 %collective-permute-start.9 = (bf16[64,1024]{1,0:T(8,128)(2,1)S(1)}, bf16[64,1024]{1,0:T(8,128)(2,1)S(1)}, u32[]{:S(2)}, u32[]{:S(2)}) collective-permute-start(bf16[64,1024]{1,0:T(8,128)(2,1)S(1)} %get-tuple-element.56.refs_1_), channel_id=1, source_target_pairs={{0,15},{1,2},{2,1},{3,4},{4,3},{5,6},{6,5},{7,8},{8,7},{9,10},{10,... | collective-permute-start | bytes 393224 | tf_op jit(solution)/shard_map/ppermute | solution.py:317
  26.5 5.0 %collective-permute-start.10 = (bf16[64,128]{1,0:T(8,128)(2,1)S(1)}, bf16[64,128]{1,0:T(8,128)(2,1)S(1)}, u32[]{:S(2)}, u32[]{:S(2)}) collective-permute-start(bf16[64,128]{1,0:T(8,128)(2,1)S(1)} %get-tuple-element.59.refs_4_), channel_id=1, source_target_pairs={{0,9},{1,11},{2,10},{3,8},{4,13},{5,14},{6,15},{7,12},{8,1},{9,2},... | collective-permute-start | bytes 49160 | tf_op jit(solution)/shard_map/ppermute | solution.py:330
  26.6 5.0 %collective-permute-start.11 = (bf16[64,128]{1,0:T(8,128)(2,1)S(1)}, bf16[64,128]{1,0:T(8,128)(2,1)S(1)}, u32[]{:S(2)}, u32[]{:S(2)}) collective-permute-start(bf16[64,128]{1,0:T(8,128)(2,1)S(1)} %get-tuple-element.60.refs_5_), channel_id=1, source_target_pairs={{0,8},{1,10},{2,11},{3,9},{4,12},{5,15},{6,14},{7,13},{8,0},{9,3},... | collective-permute-start | bytes 49160 | tf_op jit(solution)/shard_map/ppermute | solution.py:330
  32.1 3.6 %collective-permute-start.12 = (bf16[64,1536]{1,0:T(8,128)(2,1)S(1)}, bf16[64,1536]{1,0:T(8,128)(2,1)S(1)}, u32[]{:S(2)}, u32[]{:S(2)}) collective-permute-start(bf16[64,1536]{1,0:T(8,128)(2,1)S(1)} %get-tuple-element.64), channel_id=1, source_target_pairs={{0,1},{1,0},{2,3},{3,2},{4,5},{5,4},{6,7},{7,6},{8,9},{9,8},{10,11... | collective-permute-start | bytes 589832 | tf_op jit(solution)/shard_map/ppermute | solution.py:318
  32.4 7.4 %collective-permute-start.13 = (bf16[64,1024]{1,0:T(8,128)(2,1)S(1)}, bf16[64,1024]{1,0:T(8,128)(2,1)S(1)}, u32[]{:S(2)}, u32[]{:S(2)}) collective-permute-start(bf16[64,1024]{1,0:T(8,128)(2,1)S(1)} %get-tuple-element.63.refs_1_), channel_id=1, source_target_pairs={{0,15},{1,2},{2,1},{3,4},{4,3},{5,6},{6,5},{7,8},{8,7},{9,10},{10,... | collective-permute-start | bytes 393224 | tf_op jit(solution)/shard_map/ppermute | solution.py:317
  35.7 5.0 %collective-permute-start.14 = (bf16[64,128]{1,0:T(8,128)(2,1)S(1)}, bf16[64,128]{1,0:T(8,128)(2,1)S(1)}, u32[]{:S(2)}, u32[]{:S(2)}) collective-permute-start(bf16[64,128]{1,0:T(8,128)(2,1)S(1)} %get-tuple-element.66.refs_4_), channel_id=1, source_target_pairs={{0,9},{1,11},{2,10},{3,8},{4,13},{5,14},{6,15},{7,12},{8,1},{9,2},... | collective-permute-start | bytes 49160 | tf_op jit(solution)/shard_map/ppermute | solution.py:330
  35.8 5.0 %collective-permute-start.15 = (bf16[64,128]{1,0:T(8,128)(2,1)S(1)}, bf16[64,128]{1,0:T(8,128)(2,1)S(1)}, u32[]{:S(2)}, u32[]{:S(2)}) collective-permute-start(bf16[64,128]{1,0:T(8,128)(2,1)S(1)} %get-tuple-element.67.refs_5_), channel_id=1, source_target_pairs={{0,8},{1,10},{2,11},{3,9},{4,12},{5,15},{6,14},{7,13},{8,0},{9,3},... | collective-permute-start | bytes 49160 | tf_op jit(solution)/shard_map/ppermute | solution.py:330

commit v26 on v14

--- a/solution.py
+++ b/solution.py
@@ -54,10 +54,10 @@
         places = [(l, m) for l in range(loop_size) for m in range(members)]
         self.across = [
             [
-                (l * members + m, (l + self.hops[0]) % loop_size * members + (m ^ (m % 2 * 2) ^ other))
+                (l * members + m, (l + self.hops[0]) % loop_size * members + (m ^ 2 ^ (m % 2 * 2) ^ other))
                 for l, m in places
             ]
-            for other in range(2)
+            for other in (0, 1)
         ]
         self.routes = [
             [(l * members + m, (l + hop) % loop_size * members + (m + step) % members) for l, m in places]
@@ -83,7 +83,7 @@
         message_ref, keep_ref = out_refs
         (total,) = totals
         member = self.member(index_ref)
-        second = lax.rem(member, 2) != lax.div(member, 2)
+        second = lax.rem(member, 2) == lax.div(member, 2)
         first, last = total[:, : 2 * self.width], total[:, 2 * self.width :]
         keep_ref[...] = jnp.where(second, last, first)
         upper, lower = halves(jnp.where(second, first, last))
@@ -298,7 +298,7 @@
                 scratch=scratch_for(far_rows, far_cols, col_basis, couplings)
                 + [pltpu.VMEM(matrix[:2] + (width,), F32), pltpu.SemaphoreType.DMA((7,))],
             )
-        over = lax.ppermute(block if product == 0 else current, axes, plan.over)
+        over = lax.ppermute(current, axes, plan.over)
         near = lax.ppermute(sends[0] if plan.paired else current, axes, plan.near)
         if plan.paired:
             sends = call(

time: 43.1 us -> 42.7 us (level)
  starting transfers between devices: 19.6 us -> 18.3 us
  waiting for transfers between devices: 10.9 us -> 11.9 us
    ppermute x4, starting transfers between devices: 14.7 us -> 13.4 us  [on_device(): over = lax.ppermute(current, axes, plan.over)]
    ppermute x4, waiting for transfers between devices: 5.92 us -> 6.93 us  [on_device(): over = lax.ppermute(current, axes, plan.over)]
  transfers between devices with their start and end apart: 16 -> 16, of which waited for: 10 -> 8; matrix products, arithmetic and copies ran while one was open for 0% -> 0% of each run, Pallas kernels for 18% -> 18%
where the time goes in v26:
time: 42.7 us; the launch traced here: 42.6 us
  starting transfers between devices  18.3 us (43%)
  Pallas kernels  12.3 us (29%)
  waiting for transfers between devices  11.9 us (28%)
    ppermute x4, starting transfers between devices, on_device(): over = lax.ppermute(current, axes, plan.over)  13.4 us
    pallas_call x17, Pallas kernels, call(): pl.pallas_call(kernel, in_specs=list(specs), out_specs=out_specs or [IN_V...  12.3 us
    ppermute x4, waiting for transfers between devices, on_device(): over = lax.ppermute(current, axes, plan.over)  6.93 us
    ppermute x8, waiting for transfers between devices, on_device(): fars = [lax.ppermute(s, axes, route) for s, route in zip(sends, routes)]  4.96 us
    ppermute x8, starting transfers between devices, on_device(): fars = [lax.ppermute(s, axes, route) for s, route in zip(sends, routes)]  3.79 us
    ppermute x4, starting transfers between devices, on_device(): near = lax.ppermute(sends[0] if plan.paired else current, axes, plan.near)  1.05 us
  transfers between devices with their start and end apart: 16, of which 8 were waited for; matrix products, arithmetic and copies ran while one was open for 0% of the time, Pallas kernels for 18%

profile of v26, /device:TPU:0, one launch (start us, length us, event | category | flops | bytes accessed | tf_op | source)
XLA Modules:
  0.0 42.6 jit_solution(12760492750901163128)
XLA Ops:
  0.0 0.0 copy-start.1
  0.0 0.0 copy-start
  0.0 1.8 %prepare.1 = (bf16[64,1024]{1,0:T(8,128)(2,1)S(1)}, bf16[1,512,256]{2,1,0:T(8,128)(2,1)S(1)}, bf16[128,1024]{1,0:T(8,128)(2,1)S(1)}, s32[32]{0:T(128)S(4)}, s32[...) custom-call(s32[1]{0:T(128)} %bitcast.index_ref.refs_0_, s32[32]{0:T(128)} %refs_0_.1, s32[32]{0:T(128)} %refs_1_.1, ...), custom_call_target="tpu_custom_call" | custom-call | flops 1000000000 | bytes 4194304 | tf_op jit(solution)/shard_map/prepare/pallas_call | solution.py:240
  1.8 0.5 %collective-permute-start = (bf16[64,1536]{1,0:T(8,128)(2,1)S(1)}, bf16[64,1536]{1,0:T(8,128)(2,1)S(1)}, u32[]{:S(2)}, u32[]{:S(2)}) collective-permute-start(bf16[64,1536]{1,0:T(8,128)(2,1)S(1)} %get-tuple-element.41), channel_id=1, source_target_pairs={{0,1},{1,0},{2,3},{3,2},{4,5},{5,4},{6,7},{7,6},{8,9},{9,8},{10,11... | collective-permute-start | bytes 589832 | tf_op jit(solution)/shard_map/ppermute | solution.py:302
  2.4 5.6 %collective-permute-start.1 = (bf16[64,1024]{1,0:T(8,128)(2,1)S(1)}, bf16[64,1024]{1,0:T(8,128)(2,1)S(1)}, u32[]{:S(2)}, u32[]{:S(2)}) collective-permute-start(bf16[64,1024]{1,0:T(8,128)(2,1)S(1)} %get-tuple-element.40.refs_3_), channel_id=1, source_target_pairs={{0,15},{1,2},{2,1},{3,4},{4,3},{5,6},{6,5},{7,8},{8,7},{9,10},{10,... | collective-permute-start | bytes 393224 | tf_op jit(solution)/shard_map/ppermute | solution.py:301
  8.0 0.0 collective-permute-done.message_ref.refs_4_
  8.0 0.4 collective-permute-start.2
  8.4 0.0 collective-permute-start.3
  8.4 0.0 copy-done.1
  8.4 0.0 copy-done
  8.4 1.9 %first_own.1 = (f32[64,1024]{1,0:T(8,128)S(1)}, bf16[36,256,256]{2,1,0:T(8,128)(2,1)S(1)}, bf16[256,1024]{1,0:T(8,128)(2,1)S(1)}) custom-call(s32[1]{0:T(128)} %bitcast.index_ref.refs_0_, s32[32]{0:T(128)S(4)} %get-tuple-element.38.refs_1_, s32[32]{0:T(128)S(4)} %get-tuple-element.39.refs_2_, bf16[64,1024]{1,0:T(8,128)(2,1)S(1)} %get-tuple-element.40.refs_3_, ...), custom_call_target="tpu_custom_call" | custom-call | flops 1000000000 | bytes 4194304 | tf_op jit(solution)/shard_map/first_own/pallas_call | solution.py:240
  10.3 0.4 %collective-permute-done.1.over_ref = bf16[64,1024]{1,0:T(8,128)(2,1)S(1)} collective-permute-done((bf16[64,1024]{1,0:T(8,128)(2,1)S(1)}, bf16[64,1024]{1,0:T(8,128)(2,1)S(1)}, u32[]{:S(2)}, u32[]{:S(2)}) %collective-permute-start.1) | collective-permute-done | bytes 131104 | tf_op jit(solution)/shard_map/ppermute | solution.py:301
  10.8 0.5 %halo.4.refs_1_ = f32[64,1024]{1,0:T(8,128)S(1)} custom-call(s32[1]{0:T(128)} %bitcast.index_ref.refs_0_, f32[64,1024]{1,0:T(8,128)S(1)} %get-tuple-element.45.acc_ref, bf16[64,1024]{1,0:T(8,128)(2,1)S(1)} %collective-permute-done.1.over_ref, bf16[36,256,256]{2,1,0:T(8,128)(2,1)S(1)} %get-tuple-element.46.d_ref.refs_3_), custom_call_target="tpu_custom_call" | custom-call | flops 1000000000 | bytes 4194304 | tf_op jit(solution)/shard_map/halo/pallas_call | solution.py:240
  11.3 2.6 %collective-permute-done.2.refs_5_ = bf16[64,128]{1,0:T(8,128)(2,1)S(1)} collective-permute-done((bf16[64,128]{1,0:T(8,128)(2,1)S(1)}, bf16[64,128]{1,0:T(8,128)(2,1)S(1)}, u32[]{:S(2)}, u32[]{:S(2)}) %collective-permute-start.2) | collective-permute-done | bytes 16416 | tf_op jit(solution)/shard_map/ppermute | solution.py:314
  13.9 0.0 collective-permute-done.3.refs_6_
  13.9 0.6 %finish.3 = (bf16[64,1024]{1,0:T(8,128)(2,1)S(1)}, bf16[64,1536]{1,0:T(8,128)(2,1)S(1)}, f32[64,256]{1,0:T(8,128)S(1)}) custom-call(s32[1]{0:T(128)} %bitcast.index_ref.refs_0_, f32[64,1024]{1,0:T(8,128)S(1)} %halo.4.refs_1_, bf16[256,1024]{1,0:T(8,128)(2,1)S(1)} %get-tuple-element.47.refs_2_.refs_1_, bf16[128,1024]{1,0:T(8,128)(2,1)S(1)} %get-tuple-element.48.refs_3_, ...), custom_call_target="tpu_custom_call" | custom-call | flops 1000000000 | bytes 4194304 | tf_op jit(solution)/shard_map/finish/pallas_call | solution.py:240
  14.4 0.2 collective-permute-start.4
  14.6 2.7 %collective-permute-start.5 = (bf16[64,1024]{1,0:T(8,128)(2,1)S(1)}, bf16[64,1024]{1,0:T(8,128)(2,1)S(1)}, u32[]{:S(2)}, u32[]{:S(2)}) collective-permute-start(bf16[64,1024]{1,0:T(8,128)(2,1)S(1)} %get-tuple-element.50.refs_1_), channel_id=1, source_target_pairs={{0,15},{1,2},{2,1},{3,4},{4,3},{5,6},{6,5},{7,8},{8,7},{9,10},{10,... | collective-permute-start | bytes 393224 | tf_op jit(solution)/shard_map/ppermute | solution.py:301
  17.3 0.0 collective-permute-done.4.message_ref.refs_2_
  17.3 0.8 %collective-permute-start.6 = (bf16[64,128]{1,0:T(8,128)(2,1)S(1)}, bf16[64,128]{1,0:T(8,128)(2,1)S(1)}, u32[]{:S(2)}, u32[]{:S(2)}) collective-permute-start(bf16[64,128]{1,0:T(8,128)(2,1)S(1)} %get-tuple-element.53.refs_4_), channel_id=1, source_target_pairs={{0,10},{1,9},{2,8},{3,11},{4,14},{5,13},{6,12},{7,15},{8,2},{9,1},... | collective-permute-start | bytes 49160 | tf_op jit(solution)/shard_map/ppermute | solution.py:314
  18.2 0.7 %collective-permute-start.7 = (bf16[64,128]{1,0:T(8,128)(2,1)S(1)}, bf16[64,128]{1,0:T(8,128)(2,1)S(1)}, u32[]{:S(2)}, u32[]{:S(2)}) collective-permute-start(bf16[64,128]{1,0:T(8,128)(2,1)S(1)} %get-tuple-element.54.refs_5_), channel_id=1, source_target_pairs={{0,11},{1,8},{2,9},{3,10},{4,15},{5,12},{6,13},{7,14},{8,3},{9,0},... | collective-permute-start | bytes 49160 | tf_op jit(solution)/shard_map/ppermute | solution.py:314
  18.9 1.3 %own.3 = (f32[64,1024]{1,0:T(8,128)S(1)}, bf16[4,64,1024]{2,1,0:T(8,128)(2,1)}) custom-call(s32[1]{0:T(128)} %bitcast.index_ref.refs_0_, bf16[64,1024]{1,0:T(8,128)(2,1)S(1)} %get-tuple-element.50.refs_1_, bf16[64,1536]{1,0:T(8,128)(2,1)S(1)} %collective-permute-done.4.message_ref.refs_2_, bf16[36,256,256]{2,1,0:T(8,128)(2,1)S(1)} %get-tuple-element.46.d_ref.refs_3_, ...), custom_call_target="tpu_custom_call" | custom-call | flops 1000000000 | bytes 4194304 | tf_op jit(solution)/shard_map/own/pallas_call | solution.py:240
  20.2 1.6 %collective-permute-done.5.over_ref = bf16[64,1024]{1,0:T(8,128)(2,1)S(1)} collective-permute-done((bf16[64,1024]{1,0:T(8,128)(2,1)S(1)}, bf16[64,1024]{1,0:T(8,128)(2,1)S(1)}, u32[]{:S(2)}, u32[]{:S(2)}) %collective-permute-start.5) | collective-permute-done | bytes 131104 | tf_op jit(solution)/shard_map/ppermute | solution.py:301
  21.7 0.5 %halo.5.refs_1_ = f32[64,1024]{1,0:T(8,128)S(1)} custom-call(s32[1]{0:T(128)} %bitcast.index_ref.refs_0_, f32[64,1024]{1,0:T(8,128)S(1)} %get-tuple-element.55.acc_ref, bf16[64,1024]{1,0:T(8,128)(2,1)S(1)} %collective-permute-done.5.over_ref, bf16[36,256,256]{2,1,0:T(8,128)(2,1)S(1)} %get-tuple-element.46.d_ref.refs_3_), custom_call_target="tpu_custom_call" | custom-call | flops 1000000000 | bytes 4194304 | tf_op jit(solution)/shard_map/halo/pallas_call | solution.py:240
  22.2 1.1 %collective-permute-done.6.refs_5_ = bf16[64,128]{1,0:T(8,128)(2,1)S(1)} collective-permute-done((bf16[64,128]{1,0:T(8,128)(2,1)S(1)}, bf16[64,128]{1,0:T(8,128)(2,1)S(1)}, u32[]{:S(2)}, u32[]{:S(2)}) %collective-permute-start.6) | collective-permute-done | bytes 16416 | tf_op jit(solution)/shard_map/ppermute | solution.py:314
  23.3 0.0 collective-permute-done.7.refs_6_
  23.3 0.6 %finish.4 = (bf16[64,1024]{1,0:T(8,128)(2,1)S(1)}, bf16[64,1536]{1,0:T(8,128)(2,1)S(1)}, f32[64,256]{1,0:T(8,128)S(1)}) custom-call(s32[1]{0:T(128)} %bitcast.index_ref.refs_0_, f32[64,1024]{1,0:T(8,128)S(1)} %halo.5.refs_1_, bf16[256,1024]{1,0:T(8,128)(2,1)S(1)} %get-tuple-element.47.refs_2_.refs_1_, bf16[128,1024]{1,0:T(8,128)(2,1)S(1)} %get-tuple-element.48.refs_3_, ...), custom_call_target="tpu_custom_call" | custom-call | flops 1000000000 | bytes 4194304 | tf_op jit(solution)/shard_map/finish/pallas_call | solution.py:240
  23.9 0.2 collective-permute-start.8
  24.1 2.6 %collective-permute-start.9 = (bf16[64,1024]{1,0:T(8,128)(2,1)S(1)}, bf16[64,1024]{1,0:T(8,128)(2,1)S(1)}, u32[]{:S(2)}, u32[]{:S(2)}) collective-permute-start(bf16[64,1024]{1,0:T(8,128)(2,1)S(1)} %get-tuple-element.56.refs_1_), channel_id=1, source_target_pairs={{0,15},{1,2},{2,1},{3,4},{4,3},{5,6},{6,5},{7,8},{8,7},{9,10},{10,... | collective-permute-start | bytes 393224 | tf_op jit(solution)/shard_map/ppermute | solution.py:301
  26.6 0.0 collective-permute-done.8.message_ref.refs_2_
  26.7 0.8 %collective-permute-start.10 = (bf16[64,128]{1,0:T(8,128)(2,1)S(1)}, bf16[64,128]{1,0:T(8,128)(2,1)S(1)}, u32[]{:S(2)}, u32[]{:S(2)}) collective-permute-start(bf16[64,128]{1,0:T(8,128)(2,1)S(1)} %get-tuple-element.59.refs_4_), channel_id=1, source_target_pairs={{0,10},{1,9},{2,8},{3,11},{4,14},{5,13},{6,12},{7,15},{8,2},{9,1},... | collective-permute-start | bytes 49160 | tf_op jit(solution)/shard_map/ppermute | solution.py:314
  27.5 0.1 collective-permute-start.11
  27.6 1.3 %own.4 = (f32[64,1024]{1,0:T(8,128)S(1)}, bf16[4,64,1024]{2,1,0:T(8,128)(2,1)}) custom-call(s32[1]{0:T(128)} %bitcast.index_ref.refs_0_, bf16[64,1024]{1,0:T(8,128)(2,1)S(1)} %get-tuple-element.56.refs_1_, bf16[64,1536]{1,0:T(8,128)(2,1)S(1)} %collective-permute-done.8.message_ref.refs_2_, ...), custom_call_target="tpu_custom_call", output_to_operand_aliasing={{1}: (6, {})} | custom-call | flops 1000000000 | bytes 4194304 | tf_op jit(solution)/shard_map/own/pallas_call | solution.py:240
  28.9 2.5 %collective-permute-done.9.over_ref = bf16[64,1024]{1,0:T(8,128)(2,1)S(1)} collective-permute-done((bf16[64,1024]{1,0:T(8,128)(2,1)S(1)}, bf16[64,1024]{1,0:T(8,128)(2,1)S(1)}, u32[]{:S(2)}, u32[]{:S(2)}) %collective-permute-start.9) | collective-permute-done | bytes 131104 | tf_op jit(solution)/shard_map/ppermute | solution.py:301
  31.3 0.5 %halo.6.refs_1_ = f32[64,1024]{1,0:T(8,128)S(1)} custom-call(s32[1]{0:T(128)} %bitcast.index_ref.refs_0_, f32[64,1024]{1,0:T(8,128)S(1)} %get-tuple-element.62.acc_ref, bf16[64,1024]{1,0:T(8,128)(2,1)S(1)} %collective-permute-done.9.over_ref, bf16[36,256,256]{2,1,0:T(8,128)(2,1)S(1)} %get-tuple-element.46.d_ref.refs_3_), custom_call_target="tpu_custom_call" | custom-call | flops 1000000000 | bytes 4194304 | tf_op jit(solution)/shard_map/halo/pallas_call | solution.py:240
  31.9 0.8 %collective-permute-done.10.refs_5_ = bf16[64,128]{1,0:T(8,128)(2,1)S(1)} collective-permute-done((bf16[64,128]{1,0:T(8,128)(2,1)S(1)}, bf16[64,128]{1,0:T(8,128)(2,1)S(1)}, u32[]{:S(2)}, u32[]{:S(2)}) %collective-permute-start.10) | collective-permute-done | bytes 16416 | tf_op jit(solution)/shard_map/ppermute | solution.py:314
  32.6 0.0 collective-permute-done.11.refs_6_
  32.6 0.6 %finish.5 = (bf16[64,1024]{1,0:T(8,128)(2,1)S(1)}, bf16[64,1536]{1,0:T(8,128)(2,1)S(1)}, f32[64,256]{1,0:T(8,128)S(1)}) custom-call(s32[1]{0:T(128)} %bitcast.index_ref.refs_0_, f32[64,1024]{1,0:T(8,128)S(1)} %halo.6.refs_1_, bf16[256,1024]{1,0:T(8,128)(2,1)S(1)} %get-tuple-element.47.refs_2_.refs_1_, bf16[128,1024]{1,0:T(8,128)(2,1)S(1)} %get-tuple-element.48.refs_3_, ...), custom_call_target="tpu_custom_call" | custom-call | flops 1000000000 | bytes 4194304 | tf_op jit(solution)/shard_map/finish/pallas_call | solution.py:240
  33.2 0.2 collective-permute-start.12
  33.4 2.5 %collective-permute-start.13 = (bf16[64,1024]{1,0:T(8,128)(2,1)S(1)}, bf16[64,1024]{1,0:T(8,128)(2,1)S(1)}, u32[]{:S(2)}, u32[]{:S(2)}) collective-permute-start(bf16[64,1024]{1,0:T(8,128)(2,1)S(1)} %get-tuple-element.63.refs_1_), channel_id=1, source_target_pairs={{0,15},{1,2},{2,1},{3,4},{4,3},{5,6},{6,5},{7,8},{8,7},{9,10},{10,... | collective-permute-start | bytes 393224 | tf_op jit(solution)/shard_map/ppermute | solution.py:301
  35.9 0.0 collective-permute-done.12.message_ref.refs_2_
  35.9 0.8 %collective-permute-start.14 = (bf16[64,128]{1,0:T(8,128)(2,1)S(1)}, bf16[64,128]{1,0:T(8,128)(2,1)S(1)}, u32[]{:S(2)}, u32[]{:S(2)}) collective-permute-start(bf16[64,128]{1,0:T(8,128)(2,1)S(1)} %get-tuple-element.66.refs_4_), channel_id=1, source_target_pairs={{0,10},{1,9},{2,8},{3,11},{4,14},{5,13},{6,12},{7,15},{8,2},{9,1},... | collective-permute-start | bytes 49160 | tf_op jit(solution)/shard_map/ppermute | solution.py:314
  36.8 0.1 collective-permute-start.15
  36.9 1.3 %own.5 = (f32[64,1024]{1,0:T(8,128)S(1)}, bf16[4,64,1024]{2,1,0:T(8,128)(2,1)}) custom-call(s32[1]{0:T(128)} %bitcast.index_ref.refs_0_, bf16[64,1024]{1,0:T(8,128)(2,1)S(1)} %get-tuple-element.63.refs_1_, bf16[64,1536]{1,0:T(8,128)(2,1)S(1)} %collective-permute-done.12.message_ref.refs_2_, ...), custom_call_target="tpu_custom_call", output_to_operand_aliasing={{1}: (6, {})} | custom-call | flops 1000000000 | bytes 4194304 | tf_op jit(solution)/shard_map/own/pallas_call | solution.py:240
  38.2 2.5 %collective-permute-done.13.over_ref = bf16[64,1024]{1,0:T(8,128)(2,1)S(1)} collective-permute-done((bf16[64,1024]{1,0:T(8,128)(2,1)S(1)}, bf16[64,1024]{1,0:T(8,128)(2,1)S(1)}, u32[]{:S(2)}, u32[]{:S(2)}) %collective-permute-start.13) | collective-permute-done | bytes 131104 | tf_op jit(solution)/shard_map/ppermute | solution.py:301
  40.7 0.5 %halo.7.refs_0_ = f32[64,1024]{1,0:T(8,128)S(1)} custom-call(s32[1]{0:T(128)} %bitcast.index_ref.refs_0_, f32[64,1024]{1,0:T(8,128)S(1)} %get-tuple-element.69.acc_ref, bf16[64,1024]{1,0:T(8,128)(2,1)S(1)} %collective-permute-done.13.over_ref, bf16[36,256,256]{2,1,0:T(8,128)(2,1)S(1)} %get-tuple-element.46.d_ref.refs_3_), custom_call_target="tpu_custom_call" | custom-call | flops 1000000000 | bytes 4194304 | tf_op jit(solution)/shard_map/halo/pallas_call | solution.py:240
  41.2 0.6 %collective-permute-done.14.refs_2_ = bf16[64,128]{1,0:T(8,128)(2,1)S(1)} collective-permute-done((bf16[64,128]{1,0:T(8,128)(2,1)S(1)}, bf16[64,128]{1,0:T(8,128)(2,1)S(1)}, u32[]{:S(2)}, u32[]{:S(2)}) %collective-permute-start.14) | collective-permute-done | bytes 16416 | tf_op jit(solution)/shard_map/ppermute | solution.py:314
  41.7 0.0 collective-permute-done.15.refs_3_
  41.7 0.9 %last.1 = bf16[4,64,1024]{2,1,0:T(8,128)(2,1)} custom-call(f32[64,1024]{1,0:T(8,128)S(1)} %halo.7.refs_0_, bf16[256,1024]{1,0:T(8,128)(2,1)S(1)} %get-tuple-element.47.refs_2_.refs_1_, bf16[64,128]{1,0:T(8,128)(2,1)S(1)} %collective-permute-done.14.refs_2_, bf16[64,128]{1,0:T(8,128)(2,1)S(1)} %collective-permute-done.15.refs_3_, ...), custom_call_target="tpu_custom_call", output_to_operand_aliasing={{}: (4, {})} | custom-call | flops 1000000000 | bytes 4194304 | tf_op jit(solution)/shard_map/last/pallas_call | solution.py:240
  (4 shorter events, 0.1 us)
Async XLA Ops:
  0.0 8.4 %copy-start.1 = (bf16[4,32,256]{2,1,0:T(8,128)(2,1)S(1)}, bf16[4,32,256]{2,1,0:T(8,128)(2,1)}, u32[]{:S(2)}) copy-start(bf16[4,32,256]{2,1,0:T(8,128)(2,1)} %refs_5_.3) | copy-start | bytes 196612
  0.0 8.4 %copy-start = (bf16[32,256,256]{2,1,0:T(8,128)(2,1)S(1)}, bf16[32,256,256]{2,1,0:T(8,128)(2,1)}, u32[]{:S(2)}) copy-start(bf16[32,256,256]{2,1,0:T(8,128)(2,1)} %refs_6_.3) | copy-start | bytes 12582916
  1.8 6.2 %collective-permute-start = (bf16[64,1536]{1,0:T(8,128)(2,1)S(1)}, bf16[64,1536]{1,0:T(8,128)(2,1)S(1)}, u32[]{:S(2)}, u32[]{:S(2)}) collective-permute-start(bf16[64,1536]{1,0:T(8,128)(2,1)S(1)} %get-tuple-element.41), channel_id=1, source_target_pairs={{0,1},{1,0},{2,3},{3,2},{4,5},{5,4},{6,7},{7,6},{8,9},{9,8},{10,11... | collective-permute-start | bytes 589832 | tf_op jit(solution)/shard_map/ppermute | solution.py:302
  2.4 8.4 %collective-permute-start.1 = (bf16[64,1024]{1,0:T(8,128)(2,1)S(1)}, bf16[64,1024]{1,0:T(8,128)(2,1)S(1)}, u32[]{:S(2)}, u32[]{:S(2)}) collective-permute-start(bf16[64,1024]{1,0:T(8,128)(2,1)S(1)} %get-tuple-element.40.refs_3_), channel_id=1, source_target_pairs={{0,15},{1,2},{2,1},{3,4},{4,3},{5,6},{6,5},{7,8},{8,7},{9,10},{10,... | collective-permute-start | bytes 393224 | tf_op jit(solution)/shard_map/ppermute | solution.py:301
  8.0 5.8 %collective-permute-start.2 = (bf16[64,128]{1,0:T(8,128)(2,1)S(1)}, bf16[64,128]{1,0:T(8,128)(2,1)S(1)}, u32[]{:S(2)}, u32[]{:S(2)}) collective-permute-start(bf16[64,128]{1,0:T(8,128)(2,1)S(1)} %get-tuple-element.43.refs_7_), channel_id=1, source_target_pairs={{0,10},{1,9},{2,8},{3,11},{4,14},{5,13},{6,12},{7,15},{8,2},{9,1},... | collective-permute-start | bytes 49160 | tf_op jit(solution)/shard_map/ppermute | solution.py:314
  8.4 5.4 %collective-permute-start.3 = (bf16[64,128]{1,0:T(8,128)(2,1)S(1)}, bf16[64,128]{1,0:T(8,128)(2,1)S(1)}, u32[]{:S(2)}, u32[]{:S(2)}) collective-permute-start(bf16[64,128]{1,0:T(8,128)(2,1)S(1)} %get-tuple-element.44.refs_8_), channel_id=1, source_target_pairs={{0,11},{1,8},{2,9},{3,10},{4,15},{5,12},{6,13},{7,14},{8,3},{9,0},... | collective-permute-start | bytes 49160 | tf_op jit(solution)/shard_map/ppermute | solution.py:314
  14.4 2.9 %collective-permute-start.4 = (bf16[64,1536]{1,0:T(8,128)(2,1)S(1)}, bf16[64,1536]{1,0:T(8,128)(2,1)S(1)}, u32[]{:S(2)}, u32[]{:S(2)}) collective-permute-start(bf16[64,1536]{1,0:T(8,128)(2,1)S(1)} %get-tuple-element.51), channel_id=1, source_target_pairs={{0,1},{1,0},{2,3},{3,2},{4,5},{5,4},{6,7},{7,6},{8,9},{9,8},{10,11... | collective-permute-start | bytes 589832 | tf_op jit(solution)/shard_map/ppermute | solution.py:302
  14.6 7.1 %collective-permute-start.5 = (bf16[64,1024]{1,0:T(8,128)(2,1)S(1)}, bf16[64,1024]{1,0:T(8,128)(2,1)S(1)}, u32[]{:S(2)}, u32[]{:S(2)}) collective-permute-start(bf16[64,1024]{1,0:T(8,128)(2,1)S(1)} %get-tuple-element.50.refs_1_), channel_id=1, source_target_pairs={{0,15},{1,2},{2,1},{3,4},{4,3},{5,6},{6,5},{7,8},{8,7},{9,10},{10,... | collective-permute-start | bytes 393224 | tf_op jit(solution)/shard_map/ppermute | solution.py:301
  17.3 6.0 %collective-permute-start.6 = (bf16[64,128]{1,0:T(8,128)(2,1)S(1)}, bf16[64,128]{1,0:T(8,128)(2,1)S(1)}, u32[]{:S(2)}, u32[]{:S(2)}) collective-permute-start(bf16[64,128]{1,0:T(8,128)(2,1)S(1)} %get-tuple-element.53.refs_4_), channel_id=1, source_target_pairs={{0,10},{1,9},{2,8},{3,11},{4,14},{5,13},{6,12},{7,15},{8,2},{9,1},... | collective-permute-start | bytes 49160 | tf_op jit(solution)/shard_map/ppermute | solution.py:314
  18.2 5.1 %collective-permute-start.7 = (bf16[64,128]{1,0:T(8,128)(2,1)S(1)}, bf16[64,128]{1,0:T(8,128)(2,1)S(1)}, u32[]{:S(2)}, u32[]{:S(2)}) collective-permute-start(bf16[64,128]{1,0:T(8,128)(2,1)S(1)} %get-tuple-element.54.refs_5_), channel_id=1, source_target_pairs={{0,11},{1,8},{2,9},{3,10},{4,15},{5,12},{6,13},{7,14},{8,3},{9,0},... | collective-permute-start | bytes 49160 | tf_op jit(solution)/shard_map/ppermute | solution.py:314
  23.9 2.7 %collective-permute-start.8 = (bf16[64,1536]{1,0:T(8,128)(2,1)S(1)}, bf16[64,1536]{1,0:T(8,128)(2,1)S(1)}, u32[]{:S(2)}, u32[]{:S(2)}) collective-permute-start(bf16[64,1536]{1,0:T(8,128)(2,1)S(1)} %get-tuple-element.57), channel_id=1, source_target_pairs={{0,1},{1,0},{2,3},{3,2},{4,5},{5,4},{6,7},{7,6},{8,9},{9,8},{10,11... | collective-permute-start | bytes 589832 | tf_op jit(solution)/shard_map/ppermute | solution.py:302
  24.1 7.3 %collective-permute-start.9 = (bf16[64,1024]{1,0:T(8,128)(2,1)S(1)}, bf16[64,1024]{1,0:T(8,128)(2,1)S(1)}, u32[]{:S(2)}, u32[]{:S(2)}) collective-permute-start(bf16[64,1024]{1,0:T(8,128)(2,1)S(1)} %get-tuple-element.56.refs_1_), channel_id=1, source_target_pairs={{0,15},{1,2},{2,1},{3,4},{4,3},{5,6},{6,5},{7,8},{8,7},{9,10},{10,... | collective-permute-start | bytes 393224 | tf_op jit(solution)/shard_map/ppermute | solution.py:301
  26.7 6.0 %collective-permute-start.10 = (bf16[64,128]{1,0:T(8,128)(2,1)S(1)}, bf16[64,128]{1,0:T(8,128)(2,1)S(1)}, u32[]{:S(2)}, u32[]{:S(2)}) collective-permute-start(bf16[64,128]{1,0:T(8,128)(2,1)S(1)} %get-tuple-element.59.refs_4_), channel_id=1, source_target_pairs={{0,10},{1,9},{2,8},{3,11},{4,14},{5,13},{6,12},{7,15},{8,2},{9,1},... | collective-permute-start | bytes 49160 | tf_op jit(solution)/shard_map/ppermute | solution.py:314
  27.5 5.1 %collective-permute-start.11 = (bf16[64,128]{1,0:T(8,128)(2,1)S(1)}, bf16[64,128]{1,0:T(8,128)(2,1)S(1)}, u32[]{:S(2)}, u32[]{:S(2)}) collective-permute-start(bf16[64,128]{1,0:T(8,128)(2,1)S(1)} %get-tuple-element.60.refs_5_), channel_id=1, source_target_pairs={{0,11},{1,8},{2,9},{3,10},{4,15},{5,12},{6,13},{7,14},{8,3},{9,0},... | collective-permute-start | bytes 49160 | tf_op jit(solution)/shard_map/ppermute | solution.py:314
  33.2 2.7 %collective-permute-start.12 = (bf16[64,1536]{1,0:T(8,128)(2,1)S(1)}, bf16[64,1536]{1,0:T(8,128)(2,1)S(1)}, u32[]{:S(2)}, u32[]{:S(2)}) collective-permute-start(bf16[64,1536]{1,0:T(8,128)(2,1)S(1)} %get-tuple-element.64), channel_id=1, source_target_pairs={{0,1},{1,0},{2,3},{3,2},{4,5},{5,4},{6,7},{7,6},{8,9},{9,8},{10,11... | collective-permute-start | bytes 589832 | tf_op jit(solution)/shard_map/ppermute | solution.py:302
  33.4 7.3 %collective-permute-start.13 = (bf16[64,1024]{1,0:T(8,128)(2,1)S(1)}, bf16[64,1024]{1,0:T(8,128)(2,1)S(1)}, u32[]{:S(2)}, u32[]{:S(2)}) collective-permute-start(bf16[64,1024]{1,0:T(8,128)(2,1)S(1)} %get-tuple-element.63.refs_1_), channel_id=1, source_target_pairs={{0,15},{1,2},{2,1},{3,4},{4,3},{5,6},{6,5},{7,8},{8,7},{9,10},{10,... | collective-permute-start | bytes 393224 | tf_op jit(solution)/shard_map/ppermute | solution.py:301
  35.9 5.8 %collective-permute-start.14 = (bf16[64,128]{1,0:T(8,128)(2,1)S(1)}, bf16[64,128]{1,0:T(8,128)(2,1)S(1)}, u32[]{:S(2)}, u32[]{:S(2)}) collective-permute-start(bf16[64,128]{1,0:T(8,128)(2,1)S(1)} %get-tuple-element.66.refs_4_), channel_id=1, source_target_pairs={{0,10},{1,9},{2,8},{3,11},{4,14},{5,13},{6,12},{7,15},{8,2},{9,1},... | collective-permute-start | bytes 49160 | tf_op jit(solution)/shard_map/ppermute | solution.py:314
  36.8 4.9 %collective-permute-start.15 = (bf16[64,128]{1,0:T(8,128)(2,1)S(1)}, bf16[64,128]{1,0:T(8,128)(2,1)S(1)}, u32[]{:S(2)}, u32[]{:S(2)}) collective-permute-start(bf16[64,128]{1,0:T(8,128)(2,1)S(1)} %get-tuple-element.67.refs_5_), channel_id=1, source_target_pairs={{0,11},{1,8},{2,9},{3,10},{4,15},{5,12},{6,13},{7,14},{8,3},{9,0},... | collective-permute-start | bytes 49160 | tf_op jit(solution)/shard_map/ppermute | solution.py:314

commit v27 on v15

--- a/solution.py
+++ b/solution.py
@@ -216,19 +216,37 @@
 
 
 def last_kernel(plan, fars, slot, *refs):
-    acc_ref, rb_ref = refs[:2]
-    far_refs, (_, krylov_ref, x_ref, sem) = refs[2 : 2 + fars], refs[2 + fars :]
+    index_ref, acc_ref, over_ref, d_ref, rb_ref = refs[:5]
+    far_refs, (_, krylov_ref, x_ref, sem) = refs[5 : 5 + fars], refs[5 + fars :]
     both = plan.far_halves(far_refs)
-    copies = []
-    for c in range(plan.per_device):
-        columns = pl.ds(c * plan.size, plan.size)
-        x_ref[:, columns] = plan.next_panel(acc_ref, rb_ref, both, c)
-        copies.append(
-            pltpu.make_async_copy(x_ref.at[:, columns], krylov_ref.at[slot, :, columns], sem.at[c])
-        )
-        copies[-1].start()
-    for copy in copies:
-        copy.wait()
+    over = [plan.panel(over_ref, c) for c in range(plan.per_device)]
+
+    def copy(r):
+        columns = pl.ds(r * plan.size, plan.size)
+        return pltpu.make_async_copy(x_ref.at[:, columns], krylov_ref.at[slot, :, columns], sem.at[r])
+
+    def sums(first):
+        for r in range(plan.per_device):
+            value = plan.panel(acc_ref, r) + dot_nn(both, plan.panel(rb_ref, r))
+            for c in range(plan.per_device):
+                offset = first + c - r
+                if -REACH <= offset <= REACH:
+                    value = value + dot_nt(over[c], d_ref[r * SPAN + offset + REACH])
+            x_ref[:, r * plan.size : (r + 1) * plan.size] = value.astype(BF16)
+            copy(r).start()
+
+    below = lax.rem(index_ref[0], 2) == 0
+
+    @pl.when(below)
+    def _():
+        sums(-plan.per_device)
+
+    @pl.when(jnp.logical_not(below))
+    def _():
+        sums(plan.per_device)
+
+    for r in range(plan.per_device):
+        copy(r).wait()
 
 
 def call(kernel, name, ins, specs, outs, out_specs=None, scratch=(), aliases=None):
@@ -338,14 +356,14 @@
                 [pltpu.SemaphoreType.DMA],
                 {len(ins) - 1: 1} if product > 1 else None,
             )
-        (acc,) = call(
-            functools.partial(halo_kernel, plan),
-            "halo",
-            [index, acc, over, dense],
-            [IN_SMEM] + [IN_VMEM] * 3,
-            [acc_out],
-        )
         if product < PRODUCTS - 1:
+            (acc,) = call(
+                functools.partial(halo_kernel, plan),
+                "halo",
+                [index, acc, over, dense],
+                [IN_SMEM] + [IN_VMEM] * 3,
+                [acc_out],
+            )
             ins = [index, acc, row_wide, col_wide, coupled, *fars]
             current, *sends = call(
                 functools.partial(finish_kernel, plan, len(fars)),
@@ -355,12 +373,12 @@
                 [block_out, *sends_out],
             )
         else:
-            ins = [acc, row_wide, *fars, krylov]
+            ins = [index, acc, over, dense, row_wide, *fars, krylov]
             (krylov,) = call(
                 functools.partial(last_kernel, plan, len(fars), product),
                 "last",
                 ins,
-                [IN_VMEM] * (len(ins) - 1) + [ANYWHERE],
+                [IN_SMEM] + [IN_VMEM] * (len(ins) - 2) + [ANYWHERE],
                 [krylov_out],
                 [ANYWHERE],
                 [

time: 41.7 us -> 41.9 us (level)
  waiting for transfers between devices: 8.49 us -> 8.92 us
    ppermute x8, waiting for transfers between devices: 1.67 us -> 2.1 us  [on_device(): fars = [lax.ppermute(s, axes, route) for s, route in zip(sends, routes)]]
    pallas_call x17 -> x16, Pallas kernels: 12.3 us -> 12.2 us  [call(): pl.pallas_call(kernel, in_specs=list(specs), out_specs=out_specs or [IN_V...]
  transfers between devices with their start and end apart: 16 -> 16, of which waited for: 5 -> 6; matrix products, arithmetic and copies ran while one was open for 0% -> 0% of each run, Pallas kernels for 19% -> 18%
where the time goes in v27:
time: 41.9 us; the launch traced here: 41.8 us
  starting transfers between devices  20.5 us (49%)
  Pallas kernels  12.2 us (29%)
  waiting for transfers between devices  8.92 us (21%)
    ppermute x4, starting transfers between devices, on_device(): over = lax.ppermute(block if product == 0 else current, axes, plan.over)  12.8 us
    pallas_call x16, Pallas kernels, call(): pl.pallas_call(kernel, in_specs=list(specs), out_specs=out_specs or [IN_V...  12.2 us
    ppermute x4, waiting for transfers between devices, on_device(): over = lax.ppermute(block if product == 0 else current, axes, plan.over)  6.81 us
    ppermute x8, starting transfers between devices, on_device(): fars = [lax.ppermute(s, axes, route) for s, route in zip(sends, routes)]  5.02 us
    ppermute x4, starting transfers between devices, on_device(): near = lax.ppermute(sends[0] if plan.paired else current, axes, plan.near)  2.68 us
    ppermute x8, waiting for transfers between devices, on_device(): fars = [lax.ppermute(s, axes, route) for s, route in zip(sends, routes)]  2.1 us
  transfers between devices with their start and end apart: 16, of which 6 were waited for; matrix products, arithmetic and copies ran while one was open for 0% of the time, Pallas kernels for 18%

profile of v27, /device:TPU:0, one launch (start us, length us, event | category | flops | bytes accessed | tf_op | source)
XLA Modules:
  0.0 41.8 jit_solution(716157233365351894)
XLA Ops:
  0.0 0.0 copy-start.1
  0.0 0.0 copy-start
  0.0 1.8 %prepare.1 = (bf16[64,1024]{1,0:T(8,128)(2,1)S(1)}, bf16[1,512,256]{2,1,0:T(8,128)(2,1)S(1)}, bf16[128,1024]{1,0:T(8,128)(2,1)S(1)}, s32[32]{0:T(128)S(4)}, s32[...) custom-call(s32[1]{0:T(128)} %bitcast.index_ref.refs_0_, s32[32]{0:T(128)} %refs_0_.1, s32[32]{0:T(128)} %refs_1_.1, ...), custom_call_target="tpu_custom_call" | custom-call | flops 1000000000 | bytes 4194304 | tf_op jit(solution)/shard_map/prepare/pallas_call | solution.py:258
  1.9 0.5 %collective-permute-start = (bf16[64,1536]{1,0:T(8,128)(2,1)S(1)}, bf16[64,1536]{1,0:T(8,128)(2,1)S(1)}, u32[]{:S(2)}, u32[]{:S(2)}) collective-permute-start(bf16[64,1536]{1,0:T(8,128)(2,1)S(1)} %get-tuple-element.41), channel_id=1, source_target_pairs={{0,1},{1,0},{2,3},{3,2},{4,5},{5,4},{6,7},{7,6},{8,9},{9,8},{10,11... | collective-permute-start | bytes 589832 | tf_op jit(solution)/shard_map/ppermute | solution.py:320
  2.4 5.6 %collective-permute-start.1 = (bf16[64,1024]{1,0:T(8,128)(2,1)}, bf16[64,1024]{1,0:T(8,128)(2,1)S(1)}, u32[]{:S(2)}, u32[]{:S(2)}) collective-permute-start(bf16[64,1024]{1,0:T(8,128)(2,1)} %refs_4_.1), channel_id=1, source_target_pairs={{0,15},{1,2},{2,1},{3,4},{4,3},{5,6},{6,5},{7,8},{8,7},{9,10},{10,... | collective-permute-start | bytes 393224 | tf_op jit(solution)/shard_map/ppermute | solution.py:319
  8.0 0.0 collective-permute-done.message_ref.refs_4_
  8.0 0.1 collective-permute-start.2
  8.1 0.1 collective-permute-start.3
  8.2 0.0 copy-done.1
  8.2 0.0 copy-done
  8.2 1.9 %first_own.1 = (f32[64,1024]{1,0:T(8,128)S(1)}, bf16[36,256,256]{2,1,0:T(8,128)(2,1)S(1)}, bf16[256,1024]{1,0:T(8,128)(2,1)S(1)}) custom-call(s32[1]{0:T(128)} %bitcast.index_ref.refs_0_, s32[32]{0:T(128)S(4)} %get-tuple-element.38.refs_1_, s32[32]{0:T(128)S(4)} %get-tuple-element.39.refs_2_, bf16[64,1024]{1,0:T(8,128)(2,1)S(1)} %get-tuple-element.40.refs_3_, ...), custom_call_target="tpu_custom_call" | custom-call | flops 1000000000 | bytes 4194304 | tf_op jit(solution)/shard_map/first_own/pallas_call | solution.py:258
  10.1 0.9 %collective-permute-done.1.over_ref = bf16[64,1024]{1,0:T(8,128)(2,1)S(1)} collective-permute-done((bf16[64,1024]{1,0:T(8,128)(2,1)}, bf16[64,1024]{1,0:T(8,128)(2,1)S(1)}, u32[]{:S(2)}, u32[]{:S(2)}) %collective-permute-start.1) | collective-permute-done | bytes 131104 | tf_op jit(solution)/shard_map/ppermute | solution.py:319
  10.9 0.5 %halo.3.refs_1_ = f32[64,1024]{1,0:T(8,128)S(1)} custom-call(s32[1]{0:T(128)} %bitcast.index_ref.refs_0_, f32[64,1024]{1,0:T(8,128)S(1)} %get-tuple-element.45.acc_ref, bf16[64,1024]{1,0:T(8,128)(2,1)S(1)} %collective-permute-done.1.over_ref, bf16[36,256,256]{2,1,0:T(8,128)(2,1)S(1)} %get-tuple-element.46.d_ref.refs_3_), custom_call_target="tpu_custom_call" | custom-call | flops 1000000000 | bytes 4194304 | tf_op jit(solution)/shard_map/halo/pallas_call | solution.py:258
  11.5 1.7 %collective-permute-done.2.refs_5_ = bf16[64,128]{1,0:T(8,128)(2,1)S(1)} collective-permute-done((bf16[64,128]{1,0:T(8,128)(2,1)S(1)}, bf16[64,128]{1,0:T(8,128)(2,1)S(1)}, u32[]{:S(2)}, u32[]{:S(2)}) %collective-permute-start.2) | collective-permute-done | bytes 16416 | tf_op jit(solution)/shard_map/ppermute | solution.py:332
  13.1 0.0 collective-permute-done.3.refs_6_
  13.1 0.6 %finish.3 = (bf16[64,1024]{1,0:T(8,128)(2,1)S(1)}, bf16[64,1536]{1,0:T(8,128)(2,1)S(1)}, f32[64,256]{1,0:T(8,128)S(1)}) custom-call(s32[1]{0:T(128)} %bitcast.index_ref.refs_0_, f32[64,1024]{1,0:T(8,128)S(1)} %halo.3.refs_1_, bf16[256,1024]{1,0:T(8,128)(2,1)S(1)} %get-tuple-element.47.refs_2_.refs_4_, bf16[128,1024]{1,0:T(8,128)(2,1)S(1)} %get-tuple-element.48.refs_3_, ...), custom_call_target="tpu_custom_call" | custom-call | flops 1000000000 | bytes 4194304 | tf_op jit(solution)/shard_map/finish/pallas_call | solution.py:258
  13.7 1.1 %collective-permute-start.4 = (bf16[64,1536]{1,0:T(8,128)(2,1)S(1)}, bf16[64,1536]{1,0:T(8,128)(2,1)S(1)}, u32[]{:S(2)}, u32[]{:S(2)}) collective-permute-start(bf16[64,1536]{1,0:T(8,128)(2,1)S(1)} %get-tuple-element.51), channel_id=1, source_target_pairs={{0,1},{1,0},{2,3},{3,2},{4,5},{5,4},{6,7},{7,6},{8,9},{9,8},{10,11... | collective-permute-start | bytes 589832 | tf_op jit(solution)/shard_map/ppermute | solution.py:320
  14.8 2.3 %collective-permute-start.5 = (bf16[64,1024]{1,0:T(8,128)(2,1)S(1)}, bf16[64,1024]{1,0:T(8,128)(2,1)S(1)}, u32[]{:S(2)}, u32[]{:S(2)}) collective-permute-start(bf16[64,1024]{1,0:T(8,128)(2,1)S(1)} %get-tuple-element.50.refs_1_), channel_id=1, source_target_pairs={{0,15},{1,2},{2,1},{3,4},{4,3},{5,6},{6,5},{7,8},{8,7},{9,10},{10,... | collective-permute-start | bytes 393224 | tf_op jit(solution)/shard_map/ppermute | solution.py:319
  17.1 0.0 collective-permute-done.4.message_ref.refs_2_
  17.1 0.3 collective-permute-start.6
  17.4 1.4 %collective-permute-start.7 = (bf16[64,128]{1,0:T(8,128)(2,1)S(1)}, bf16[64,128]{1,0:T(8,128)(2,1)S(1)}, u32[]{:S(2)}, u32[]{:S(2)}) collective-permute-start(bf16[64,128]{1,0:T(8,128)(2,1)S(1)} %get-tuple-element.54.refs_5_), channel_id=1, source_target_pairs={{0,8},{1,11},{2,10},{3,9},{4,12},{5,15},{6,14},{7,13},{8,0},{9,3},... | collective-permute-start | bytes 49160 | tf_op jit(solution)/shard_map/ppermute | solution.py:332
  18.8 1.3 %own.3 = (f32[64,1024]{1,0:T(8,128)S(1)}, bf16[4,64,1024]{2,1,0:T(8,128)(2,1)}) custom-call(s32[1]{0:T(128)} %bitcast.index_ref.refs_0_, bf16[64,1024]{1,0:T(8,128)(2,1)S(1)} %get-tuple-element.50.refs_1_, bf16[64,1536]{1,0:T(8,128)(2,1)S(1)} %collective-permute-done.4.message_ref.refs_2_, bf16[36,256,256]{2,1,0:T(8,128)(2,1)S(1)} %get-tuple-element.46.d_ref.refs_3_, ...), custom_call_target="tpu_custom_call" | custom-call | flops 1000000000 | bytes 4194304 | tf_op jit(solution)/shard_map/own/pallas_call | solution.py:258
  20.1 1.9 %collective-permute-done.5.over_ref = bf16[64,1024]{1,0:T(8,128)(2,1)S(1)} collective-permute-done((bf16[64,1024]{1,0:T(8,128)(2,1)S(1)}, bf16[64,1024]{1,0:T(8,128)(2,1)S(1)}, u32[]{:S(2)}, u32[]{:S(2)}) %collective-permute-start.5) | collective-permute-done | bytes 131104 | tf_op jit(solution)/shard_map/ppermute | solution.py:319
  22.0 0.5 %halo.4.refs_1_ = f32[64,1024]{1,0:T(8,128)S(1)} custom-call(s32[1]{0:T(128)} %bitcast.index_ref.refs_0_, f32[64,1024]{1,0:T(8,128)S(1)} %get-tuple-element.55.acc_ref, bf16[64,1024]{1,0:T(8,128)(2,1)S(1)} %collective-permute-done.5.over_ref, bf16[36,256,256]{2,1,0:T(8,128)(2,1)S(1)} %get-tuple-element.46.d_ref.refs_3_), custom_call_target="tpu_custom_call" | custom-call | flops 1000000000 | bytes 4194304 | tf_op jit(solution)/shard_map/halo/pallas_call | solution.py:258
  22.5 0.0 collective-permute-done.6.refs_5_
  22.5 0.0 collective-permute-done.7.refs_6_
  22.6 0.6 %finish.4 = (bf16[64,1024]{1,0:T(8,128)(2,1)S(1)}, bf16[64,1536]{1,0:T(8,128)(2,1)S(1)}, f32[64,256]{1,0:T(8,128)S(1)}) custom-call(s32[1]{0:T(128)} %bitcast.index_ref.refs_0_, f32[64,1024]{1,0:T(8,128)S(1)} %halo.4.refs_1_, bf16[256,1024]{1,0:T(8,128)(2,1)S(1)} %get-tuple-element.47.refs_2_.refs_4_, bf16[128,1024]{1,0:T(8,128)(2,1)S(1)} %get-tuple-element.48.refs_3_, ...), custom_call_target="tpu_custom_call" | custom-call | flops 1000000000 | bytes 4194304 | tf_op jit(solution)/shard_map/finish/pallas_call | solution.py:258
  23.1 0.3 collective-permute-start.8
  23.5 2.4 %collective-permute-start.9 = (bf16[64,1024]{1,0:T(8,128)(2,1)S(1)}, bf16[64,1024]{1,0:T(8,128)(2,1)S(1)}, u32[]{:S(2)}, u32[]{:S(2)}) collective-permute-start(bf16[64,1024]{1,0:T(8,128)(2,1)S(1)} %get-tuple-element.56.refs_1_), channel_id=1, source_target_pairs={{0,15},{1,2},{2,1},{3,4},{4,3},{5,6},{6,5},{7,8},{8,7},{9,10},{10,... | collective-permute-start | bytes 393224 | tf_op jit(solution)/shard_map/ppermute | solution.py:319
  25.9 0.0 collective-permute-done.8.message_ref.refs_2_
  25.9 0.6 %collective-permute-start.10 = (bf16[64,128]{1,0:T(8,128)(2,1)S(1)}, bf16[64,128]{1,0:T(8,128)(2,1)S(1)}, u32[]{:S(2)}, u32[]{:S(2)}) collective-permute-start(bf16[64,128]{1,0:T(8,128)(2,1)S(1)} %get-tuple-element.59.refs_4_), channel_id=1, source_target_pairs={{0,9},{1,10},{2,11},{3,8},{4,13},{5,14},{6,15},{7,12},{8,1},{9,2},... | collective-permute-start | bytes 49160 | tf_op jit(solution)/shard_map/ppermute | solution.py:332
  26.5 1.0 %collective-permute-start.11 = (bf16[64,128]{1,0:T(8,128)(2,1)S(1)}, bf16[64,128]{1,0:T(8,128)(2,1)S(1)}, u32[]{:S(2)}, u32[]{:S(2)}) collective-permute-start(bf16[64,128]{1,0:T(8,128)(2,1)S(1)} %get-tuple-element.60.refs_5_), channel_id=1, source_target_pairs={{0,8},{1,11},{2,10},{3,9},{4,12},{5,15},{6,14},{7,13},{8,0},{9,3},... | collective-permute-start | bytes 49160 | tf_op jit(solution)/shard_map/ppermute | solution.py:332
  27.5 1.3 %own.4 = (f32[64,1024]{1,0:T(8,128)S(1)}, bf16[4,64,1024]{2,1,0:T(8,128)(2,1)}) custom-call(s32[1]{0:T(128)} %bitcast.index_ref.refs_0_, bf16[64,1024]{1,0:T(8,128)(2,1)S(1)} %get-tuple-element.56.refs_1_, bf16[64,1536]{1,0:T(8,128)(2,1)S(1)} %collective-permute-done.8.message_ref.refs_2_, ...), custom_call_target="tpu_custom_call", output_to_operand_aliasing={{1}: (6, {})} | custom-call | flops 1000000000 | bytes 4194304 | tf_op jit(solution)/shard_map/own/pallas_call | solution.py:258
  28.8 2.0 %collective-permute-done.9.over_ref = bf16[64,1024]{1,0:T(8,128)(2,1)S(1)} collective-permute-done((bf16[64,1024]{1,0:T(8,128)(2,1)S(1)}, bf16[64,1024]{1,0:T(8,128)(2,1)S(1)}, u32[]{:S(2)}, u32[]{:S(2)}) %collective-permute-start.9) | collective-permute-done | bytes 131104 | tf_op jit(solution)/shard_map/ppermute | solution.py:319
  30.8 0.5 %halo.5.refs_1_ = f32[64,1024]{1,0:T(8,128)S(1)} custom-call(s32[1]{0:T(128)} %bitcast.index_ref.refs_0_, f32[64,1024]{1,0:T(8,128)S(1)} %get-tuple-element.62.acc_ref, bf16[64,1024]{1,0:T(8,128)(2,1)S(1)} %collective-permute-done.9.over_ref, bf16[36,256,256]{2,1,0:T(8,128)(2,1)S(1)} %get-tuple-element.46.d_ref.refs_3_), custom_call_target="tpu_custom_call" | custom-call | flops 1000000000 | bytes 4194304 | tf_op jit(solution)/shard_map/halo/pallas_call | solution.py:258
  31.4 0.0 collective-permute-done.10.refs_5_
  31.4 0.0 collective-permute-done.11.refs_6_
  31.4 0.6 %finish.5 = (bf16[64,1024]{1,0:T(8,128)(2,1)S(1)}, bf16[64,1536]{1,0:T(8,128)(2,1)S(1)}, f32[64,256]{1,0:T(8,128)S(1)}) custom-call(s32[1]{0:T(128)} %bitcast.index_ref.refs_0_, f32[64,1024]{1,0:T(8,128)S(1)} %halo.5.refs_1_, bf16[256,1024]{1,0:T(8,128)(2,1)S(1)} %get-tuple-element.47.refs_2_.refs_4_, bf16[128,1024]{1,0:T(8,128)(2,1)S(1)} %get-tuple-element.48.refs_3_, ...), custom_call_target="tpu_custom_call" | custom-call | flops 1000000000 | bytes 4194304 | tf_op jit(solution)/shard_map/finish/pallas_call | solution.py:258
  32.0 0.8 %collective-permute-start.12 = (bf16[64,1536]{1,0:T(8,128)(2,1)S(1)}, bf16[64,1536]{1,0:T(8,128)(2,1)S(1)}, u32[]{:S(2)}, u32[]{:S(2)}) collective-permute-start(bf16[64,1536]{1,0:T(8,128)(2,1)S(1)} %get-tuple-element.64), channel_id=1, source_target_pairs={{0,1},{1,0},{2,3},{3,2},{4,5},{5,4},{6,7},{7,6},{8,9},{9,8},{10,11... | collective-permute-start | bytes 589832 | tf_op jit(solution)/shard_map/ppermute | solution.py:320
  32.7 2.5 %collective-permute-start.13 = (bf16[64,1024]{1,0:T(8,128)(2,1)S(1)}, bf16[64,1024]{1,0:T(8,128)(2,1)S(1)}, u32[]{:S(2)}, u32[]{:S(2)}) collective-permute-start(bf16[64,1024]{1,0:T(8,128)(2,1)S(1)} %get-tuple-element.63.refs_1_), channel_id=1, source_target_pairs={{0,15},{1,2},{2,1},{3,4},{4,3},{5,6},{6,5},{7,8},{8,7},{9,10},{10,... | collective-permute-start | bytes 393224 | tf_op jit(solution)/shard_map/ppermute | solution.py:319
  35.2 0.0 collective-permute-done.12.message_ref.refs_2_
  35.2 0.1 collective-permute-start.14
  35.3 1.5 %collective-permute-start.15 = (bf16[64,128]{1,0:T(8,128)(2,1)S(1)}, bf16[64,128]{1,0:T(8,128)(2,1)S(1)}, u32[]{:S(2)}, u32[]{:S(2)}) collective-permute-start(bf16[64,128]{1,0:T(8,128)(2,1)S(1)} %get-tuple-element.67.refs_5_), channel_id=1, source_target_pairs={{0,8},{1,11},{2,10},{3,9},{4,12},{5,15},{6,14},{7,13},{8,0},{9,3},... | collective-permute-start | bytes 49160 | tf_op jit(solution)/shard_map/ppermute | solution.py:332
  36.8 1.3 %own.5 = (f32[64,1024]{1,0:T(8,128)S(1)}, bf16[4,64,1024]{2,1,0:T(8,128)(2,1)}) custom-call(s32[1]{0:T(128)} %bitcast.index_ref.refs_0_, bf16[64,1024]{1,0:T(8,128)(2,1)S(1)} %get-tuple-element.63.refs_1_, bf16[64,1536]{1,0:T(8,128)(2,1)S(1)} %collective-permute-done.12.message_ref.refs_2_, ...), custom_call_target="tpu_custom_call", output_to_operand_aliasing={{1}: (6, {})} | custom-call | flops 1000000000 | bytes 4194304 | tf_op jit(solution)/shard_map/own/pallas_call | solution.py:258
  38.1 2.0 %collective-permute-done.13.refs_2_ = bf16[64,1024]{1,0:T(8,128)(2,1)S(1)} collective-permute-done((bf16[64,1024]{1,0:T(8,128)(2,1)S(1)}, bf16[64,1024]{1,0:T(8,128)(2,1)S(1)}, u32[]{:S(2)}, u32[]{:S(2)}) %collective-permute-start.13) | collective-permute-done | bytes 131104 | tf_op jit(solution)/shard_map/ppermute | solution.py:319
  40.1 0.4 %collective-permute-done.14.refs_5_ = bf16[64,128]{1,0:T(8,128)(2,1)S(1)} collective-permute-done((bf16[64,128]{1,0:T(8,128)(2,1)S(1)}, bf16[64,128]{1,0:T(8,128)(2,1)S(1)}, u32[]{:S(2)}, u32[]{:S(2)}) %collective-permute-start.14) | collective-permute-done | bytes 16416 | tf_op jit(solution)/shard_map/ppermute | solution.py:332
  40.5 0.0 collective-permute-done.15.refs_6_
  40.5 1.3 %last.1 = bf16[4,64,1024]{2,1,0:T(8,128)(2,1)} custom-call(s32[1]{0:T(128)} %bitcast.index_ref.refs_0_, f32[64,1024]{1,0:T(8,128)S(1)} %get-tuple-element.69.refs_1_, bf16[64,1024]{1,0:T(8,128)(2,1)S(1)} %collective-permute-done.13.refs_2_, bf16[36,256,256]{2,1,0:T(8,128)(2,1)S(1)} %get-tuple-element.46.d_ref.refs_3_, ...), custom_call_target="tpu_custom_call", output_to_operand_aliasing={{}: (7, {})} | custom-call | flops 1000000000 | bytes 4194304 | tf_op jit(solution)/shard_map/last/pallas_call | solution.py:258
  (4 shorter events, 0.1 us)
Async XLA Ops:
  0.0 8.2 %copy-start.1 = (bf16[4,32,256]{2,1,0:T(8,128)(2,1)S(1)}, bf16[4,32,256]{2,1,0:T(8,128)(2,1)}, u32[]{:S(2)}) copy-start(bf16[4,32,256]{2,1,0:T(8,128)(2,1)} %refs_5_.3) | copy-start | bytes 196612
  0.0 8.2 %copy-start = (bf16[32,256,256]{2,1,0:T(8,128)(2,1)S(1)}, bf16[32,256,256]{2,1,0:T(8,128)(2,1)}, u32[]{:S(2)}) copy-start(bf16[32,256,256]{2,1,0:T(8,128)(2,1)} %refs_6_.3) | copy-start | bytes 12582916
  1.9 6.2 %collective-permute-start = (bf16[64,1536]{1,0:T(8,128)(2,1)S(1)}, bf16[64,1536]{1,0:T(8,128)(2,1)S(1)}, u32[]{:S(2)}, u32[]{:S(2)}) collective-permute-start(bf16[64,1536]{1,0:T(8,128)(2,1)S(1)} %get-tuple-element.41), channel_id=1, source_target_pairs={{0,1},{1,0},{2,3},{3,2},{4,5},{5,4},{6,7},{7,6},{8,9},{9,8},{10,11... | collective-permute-start | bytes 589832 | tf_op jit(solution)/shard_map/ppermute | solution.py:320
  2.4 8.6 %collective-permute-start.1 = (bf16[64,1024]{1,0:T(8,128)(2,1)}, bf16[64,1024]{1,0:T(8,128)(2,1)S(1)}, u32[]{:S(2)}, u32[]{:S(2)}) collective-permute-start(bf16[64,1024]{1,0:T(8,128)(2,1)} %refs_4_.1), channel_id=1, source_target_pairs={{0,15},{1,2},{2,1},{3,4},{4,3},{5,6},{6,5},{7,8},{8,7},{9,10},{10,... | collective-permute-start | bytes 393224 | tf_op jit(solution)/shard_map/ppermute | solution.py:319
  8.0 5.1 %collective-permute-start.2 = (bf16[64,128]{1,0:T(8,128)(2,1)S(1)}, bf16[64,128]{1,0:T(8,128)(2,1)S(1)}, u32[]{:S(2)}, u32[]{:S(2)}) collective-permute-start(bf16[64,128]{1,0:T(8,128)(2,1)S(1)} %get-tuple-element.43.refs_7_), channel_id=1, source_target_pairs={{0,9},{1,10},{2,11},{3,8},{4,13},{5,14},{6,15},{7,12},{8,1},{9,2},... | collective-permute-start | bytes 49160 | tf_op jit(solution)/shard_map/ppermute | solution.py:332
  8.1 5.0 %collective-permute-start.3 = (bf16[64,128]{1,0:T(8,128)(2,1)S(1)}, bf16[64,128]{1,0:T(8,128)(2,1)S(1)}, u32[]{:S(2)}, u32[]{:S(2)}) collective-permute-start(bf16[64,128]{1,0:T(8,128)(2,1)S(1)} %get-tuple-element.44.refs_8_), channel_id=1, source_target_pairs={{0,8},{1,11},{2,10},{3,9},{4,12},{5,15},{6,14},{7,13},{8,0},{9,3},... | collective-permute-start | bytes 49160 | tf_op jit(solution)/shard_map/ppermute | solution.py:332
  13.7 3.4 %collective-permute-start.4 = (bf16[64,1536]{1,0:T(8,128)(2,1)S(1)}, bf16[64,1536]{1,0:T(8,128)(2,1)S(1)}, u32[]{:S(2)}, u32[]{:S(2)}) collective-permute-start(bf16[64,1536]{1,0:T(8,128)(2,1)S(1)} %get-tuple-element.51), channel_id=1, source_target_pairs={{0,1},{1,0},{2,3},{3,2},{4,5},{5,4},{6,7},{7,6},{8,9},{9,8},{10,11... | collective-permute-start | bytes 589832 | tf_op jit(solution)/shard_map/ppermute | solution.py:320
  14.8 7.2 %collective-permute-start.5 = (bf16[64,1024]{1,0:T(8,128)(2,1)S(1)}, bf16[64,1024]{1,0:T(8,128)(2,1)S(1)}, u32[]{:S(2)}, u32[]{:S(2)}) collective-permute-start(bf16[64,1024]{1,0:T(8,128)(2,1)S(1)} %get-tuple-element.50.refs_1_), channel_id=1, source_target_pairs={{0,15},{1,2},{2,1},{3,4},{4,3},{5,6},{6,5},{7,8},{8,7},{9,10},{10,... | collective-permute-start | bytes 393224 | tf_op jit(solution)/shard_map/ppermute | solution.py:319
  17.1 5.4 %collective-permute-start.6 = (bf16[64,128]{1,0:T(8,128)(2,1)S(1)}, bf16[64,128]{1,0:T(8,128)(2,1)S(1)}, u32[]{:S(2)}, u32[]{:S(2)}) collective-permute-start(bf16[64,128]{1,0:T(8,128)(2,1)S(1)} %get-tuple-element.53.refs_4_), channel_id=1, source_target_pairs={{0,9},{1,10},{2,11},{3,8},{4,13},{5,14},{6,15},{7,12},{8,1},{9,2},... | collective-permute-start | bytes 49160 | tf_op jit(solution)/shard_map/ppermute | solution.py:332
  17.4 5.1 %collective-permute-start.7 = (bf16[64,128]{1,0:T(8,128)(2,1)S(1)}, bf16[64,128]{1,0:T(8,128)(2,1)S(1)}, u32[]{:S(2)}, u32[]{:S(2)}) collective-permute-start(bf16[64,128]{1,0:T(8,128)(2,1)S(1)} %get-tuple-element.54.refs_5_), channel_id=1, source_target_pairs={{0,8},{1,11},{2,10},{3,9},{4,12},{5,15},{6,14},{7,13},{8,0},{9,3},... | collective-permute-start | bytes 49160 | tf_op jit(solution)/shard_map/ppermute | solution.py:332
  23.1 2.7 %collective-permute-start.8 = (bf16[64,1536]{1,0:T(8,128)(2,1)S(1)}, bf16[64,1536]{1,0:T(8,128)(2,1)S(1)}, u32[]{:S(2)}, u32[]{:S(2)}) collective-permute-start(bf16[64,1536]{1,0:T(8,128)(2,1)S(1)} %get-tuple-element.57), channel_id=1, source_target_pairs={{0,1},{1,0},{2,3},{3,2},{4,5},{5,4},{6,7},{7,6},{8,9},{9,8},{10,11... | collective-permute-start | bytes 589832 | tf_op jit(solution)/shard_map/ppermute | solution.py:320
  23.5 7.4 %collective-permute-start.9 = (bf16[64,1024]{1,0:T(8,128)(2,1)S(1)}, bf16[64,1024]{1,0:T(8,128)(2,1)S(1)}, u32[]{:S(2)}, u32[]{:S(2)}) collective-permute-start(bf16[64,1024]{1,0:T(8,128)(2,1)S(1)} %get-tuple-element.56.refs_1_), channel_id=1, source_target_pairs={{0,15},{1,2},{2,1},{3,4},{4,3},{5,6},{6,5},{7,8},{8,7},{9,10},{10,... | collective-permute-start | bytes 393224 | tf_op jit(solution)/shard_map/ppermute | solution.py:319
  25.9 5.4 %collective-permute-start.10 = (bf16[64,128]{1,0:T(8,128)(2,1)S(1)}, bf16[64,128]{1,0:T(8,128)(2,1)S(1)}, u32[]{:S(2)}, u32[]{:S(2)}) collective-permute-start(bf16[64,128]{1,0:T(8,128)(2,1)S(1)} %get-tuple-element.59.refs_4_), channel_id=1, source_target_pairs={{0,9},{1,10},{2,11},{3,8},{4,13},{5,14},{6,15},{7,12},{8,1},{9,2},... | collective-permute-start | bytes 49160 | tf_op jit(solution)/shard_map/ppermute | solution.py:332
  26.5 4.9 %collective-permute-start.11 = (bf16[64,128]{1,0:T(8,128)(2,1)S(1)}, bf16[64,128]{1,0:T(8,128)(2,1)S(1)}, u32[]{:S(2)}, u32[]{:S(2)}) collective-permute-start(bf16[64,128]{1,0:T(8,128)(2,1)S(1)} %get-tuple-element.60.refs_5_), channel_id=1, source_target_pairs={{0,8},{1,11},{2,10},{3,9},{4,12},{5,15},{6,14},{7,13},{8,0},{9,3},... | collective-permute-start | bytes 49160 | tf_op jit(solution)/shard_map/ppermute | solution.py:332
  32.0 3.2 %collective-permute-start.12 = (bf16[64,1536]{1,0:T(8,128)(2,1)S(1)}, bf16[64,1536]{1,0:T(8,128)(2,1)S(1)}, u32[]{:S(2)}, u32[]{:S(2)}) collective-permute-start(bf16[64,1536]{1,0:T(8,128)(2,1)S(1)} %get-tuple-element.64), channel_id=1, source_target_pairs={{0,1},{1,0},{2,3},{3,2},{4,5},{5,4},{6,7},{7,6},{8,9},{9,8},{10,11... | collective-permute-start | bytes 589832 | tf_op jit(solution)/shard_map/ppermute | solution.py:320
  32.7 7.4 %collective-permute-start.13 = (bf16[64,1024]{1,0:T(8,128)(2,1)S(1)}, bf16[64,1024]{1,0:T(8,128)(2,1)S(1)}, u32[]{:S(2)}, u32[]{:S(2)}) collective-permute-start(bf16[64,1024]{1,0:T(8,128)(2,1)S(1)} %get-tuple-element.63.refs_1_), channel_id=1, source_target_pairs={{0,15},{1,2},{2,1},{3,4},{4,3},{5,6},{6,5},{7,8},{8,7},{9,10},{10,... | collective-permute-start | bytes 393224 | tf_op jit(solution)/shard_map/ppermute | solution.py:319
  35.2 5.3 %collective-permute-start.14 = (bf16[64,128]{1,0:T(8,128)(2,1)S(1)}, bf16[64,128]{1,0:T(8,128)(2,1)S(1)}, u32[]{:S(2)}, u32[]{:S(2)}) collective-permute-start(bf16[64,128]{1,0:T(8,128)(2,1)S(1)} %get-tuple-element.66.refs_4_), channel_id=1, source_target_pairs={{0,9},{1,10},{2,11},{3,8},{4,13},{5,14},{6,15},{7,12},{8,1},{9,2},... | collective-permute-start | bytes 49160 | tf_op jit(solution)/shard_map/ppermute | solution.py:332
  35.3 5.2 %collective-permute-start.15 = (bf16[64,128]{1,0:T(8,128)(2,1)S(1)}, bf16[64,128]{1,0:T(8,128)(2,1)S(1)}, u32[]{:S(2)}, u32[]{:S(2)}) collective-permute-start(bf16[64,128]{1,0:T(8,128)(2,1)S(1)} %get-tuple-element.67.refs_5_), channel_id=1, source_target_pairs={{0,8},{1,11},{2,10},{3,9},{4,12},{5,15},{6,14},{7,13},{8,0},{9,3},... | collective-permute-start | bytes 49160 | tf_op jit(solution)/shard_map/ppermute | solution.py:332

commit v28 on v20

--- a/solution.py
+++ b/solution.py
@@ -11,7 +11,7 @@
 REACH = 4
 LEVELS = 3
 SPAN = 2 * REACH + 1
-OTHER_CORE_FIRST = 0b11011111
+OTHER_CORE_FIRST = 0b11101111
 
 F32 = jnp.float32
 BF16 = jnp.bfloat16

time: 41.9 us -> 41.7 us (level)
  waiting for transfers between devices: 9.83 us -> 7.99 us
  starting transfers between devices: 19.5 us -> 21.1 us
    ppermute x8, starting transfers between devices: 2.71 us -> 5.61 us  [on_device(): fars = [lax.ppermute(s, axes, route) for s, route in zip(sends, routes)]]
    ppermute x4, starting transfers between devices: 15.2 us -> 12.8 us  [on_device(): over = lax.ppermute(block if product == 0 else current, axes, plan.over)]
    ppermute x8, waiting for transfers between devices: 2.98 us -> 1.84 us  [on_device(): fars = [lax.ppermute(s, axes, route) for s, route in zip(sends, routes)]]
    ppermute x4, starting transfers between devices: 1.57 us -> 2.66 us  [on_device(): near = lax.ppermute(sends[0] if plan.paired else current, axes, plan.near)]
    ppermute x4, waiting for transfers between devices: 6.84 us -> 6.13 us  [on_device(): over = lax.ppermute(block if product == 0 else current, axes, plan.over)]
  transfers between devices with their start and end apart: 16 -> 16, of which waited for: 8 -> 6; matrix products, arithmetic and copies ran while one was open for 0% -> 0% of each run, Pallas kernels for 19% -> 19%
where the time goes in v28:
time: 41.7 us; the launch traced here: 41.5 us
  starting transfers between devices  21.1 us (51%)
  Pallas kernels  12.3 us (29%)
  waiting for transfers between devices  7.99 us (19%)
    ppermute x4, starting transfers between devices, on_device(): over = lax.ppermute(block if product == 0 else current, axes, plan.over)  12.8 us
    pallas_call x17, Pallas kernels, call(): pl.pallas_call(kernel, in_specs=list(specs), out_specs=out_specs or [IN_V...  12.3 us
    ppermute x4, waiting for transfers between devices, on_device(): over = lax.ppermute(block if product == 0 else current, axes, plan.over)  6.13 us
    ppermute x8, starting transfers between devices, on_device(): fars = [lax.ppermute(s, axes, route) for s, route in zip(sends, routes)]  5.61 us
    ppermute x4, starting transfers between devices, on_device(): near = lax.ppermute(sends[0] if plan.paired else current, axes, plan.near)  2.66 us
    ppermute x8, waiting for transfers between devices, on_device(): fars = [lax.ppermute(s, axes, route) for s, route in zip(sends, routes)]  1.84 us
  transfers between devices with their start and end apart: 16, of which 6 were waited for; matrix products, arithmetic and copies ran while one was open for 0% of the time, Pallas kernels for 19%

profile of v28, /device:TPU:0, one launch (start us, length us, event | category | flops | bytes accessed | tf_op | source)
XLA Modules:
  0.0 41.5 jit_solution(14148228426251508836)
XLA Ops:
  0.0 0.0 copy-start.1
  0.0 0.0 copy-start
  0.0 1.8 %prepare.1 = (bf16[64,1024]{1,0:T(8,128)(2,1)S(1)}, bf16[1,512,256]{2,1,0:T(8,128)(2,1)S(1)}, bf16[128,1024]{1,0:T(8,128)(2,1)S(1)}, s32[32]{0:T(128)S(4)}, s32[...) custom-call(s32[1]{0:T(128)} %bitcast.index_ref.refs_0_, s32[32]{0:T(128)} %refs_0_.1, s32[32]{0:T(128)} %refs_1_.1, ...), custom_call_target="tpu_custom_call" | custom-call | flops 1000000000 | bytes 4194304 | tf_op jit(solution)/shard_map/prepare/pallas_call | solution.py:256
  1.8 0.5 %collective-permute-start = (bf16[64,1536]{1,0:T(8,128)(2,1)S(1)}, bf16[64,1536]{1,0:T(8,128)(2,1)S(1)}, u32[]{:S(2)}, u32[]{:S(2)}) collective-permute-start(bf16[64,1536]{1,0:T(8,128)(2,1)S(1)} %get-tuple-element.41), channel_id=1, source_target_pairs={{0,1},{1,0},{2,3},{3,2},{4,5},{5,4},{6,7},{7,6},{8,9},{9,8},{10,11... | collective-permute-start | bytes 589832 | tf_op jit(solution)/shard_map/ppermute | solution.py:318
  2.4 5.6 %collective-permute-start.1 = (bf16[64,1024]{1,0:T(8,128)(2,1)}, bf16[64,1024]{1,0:T(8,128)(2,1)S(1)}, u32[]{:S(2)}, u32[]{:S(2)}) collective-permute-start(bf16[64,1024]{1,0:T(8,128)(2,1)} %refs_4_.1), channel_id=1, source_target_pairs={{0,15},{1,2},{2,1},{3,4},{4,3},{5,6},{6,5},{7,8},{8,7},{9,10},{10,... | collective-permute-start | bytes 393224 | tf_op jit(solution)/shard_map/ppermute | solution.py:317
  8.0 0.0 collective-permute-done.message_ref.refs_4_
  8.0 0.1 collective-permute-start.2
  8.1 0.4 collective-permute-start.3
  8.5 0.0 copy-done.1
  8.5 0.0 copy-done
  8.5 1.9 %first_own.1 = (f32[64,1024]{1,0:T(8,128)S(1)}, bf16[36,256,256]{2,1,0:T(8,128)(2,1)S(1)}, bf16[256,1024]{1,0:T(8,128)(2,1)S(1)}) custom-call(s32[1]{0:T(128)} %bitcast.index_ref.refs_0_, s32[32]{0:T(128)S(4)} %get-tuple-element.38.refs_1_, s32[32]{0:T(128)S(4)} %get-tuple-element.39.refs_2_, bf16[64,1024]{1,0:T(8,128)(2,1)S(1)} %get-tuple-element.40.refs_3_, ...), custom_call_target="tpu_custom_call" | custom-call | flops 1000000000 | bytes 4194304 | tf_op jit(solution)/shard_map/first_own/pallas_call | solution.py:256
  10.3 0.6 %collective-permute-done.1.over_ref = bf16[64,1024]{1,0:T(8,128)(2,1)S(1)} collective-permute-done((bf16[64,1024]{1,0:T(8,128)(2,1)}, bf16[64,1024]{1,0:T(8,128)(2,1)S(1)}, u32[]{:S(2)}, u32[]{:S(2)}) %collective-permute-start.1) | collective-permute-done | bytes 131104 | tf_op jit(solution)/shard_map/ppermute | solution.py:317
  10.9 0.5 %halo.4.refs_1_ = f32[64,1024]{1,0:T(8,128)S(1)} custom-call(s32[1]{0:T(128)} %bitcast.index_ref.refs_0_, f32[64,1024]{1,0:T(8,128)S(1)} %get-tuple-element.45.acc_ref, bf16[64,1024]{1,0:T(8,128)(2,1)S(1)} %collective-permute-done.1.over_ref, bf16[36,256,256]{2,1,0:T(8,128)(2,1)S(1)} %get-tuple-element.46.d_ref.refs_3_), custom_call_target="tpu_custom_call" | custom-call | flops 1000000000 | bytes 4194304 | tf_op jit(solution)/shard_map/halo/pallas_call | solution.py:256
  11.5 1.7 %collective-permute-done.2.refs_5_ = bf16[64,128]{1,0:T(8,128)(2,1)S(1)} collective-permute-done((bf16[64,128]{1,0:T(8,128)(2,1)S(1)}, bf16[64,128]{1,0:T(8,128)(2,1)S(1)}, u32[]{:S(2)}, u32[]{:S(2)}) %collective-permute-start.2) | collective-permute-done | bytes 16416 | tf_op jit(solution)/shard_map/ppermute | solution.py:330
  13.1 0.0 collective-permute-done.3.refs_6_
  13.1 0.6 %finish.3 = (bf16[64,1024]{1,0:T(8,128)(2,1)S(1)}, bf16[64,1536]{1,0:T(8,128)(2,1)S(1)}, f32[64,256]{1,0:T(8,128)S(1)}) custom-call(s32[1]{0:T(128)} %bitcast.index_ref.refs_0_, f32[64,1024]{1,0:T(8,128)S(1)} %halo.4.refs_1_, bf16[256,1024]{1,0:T(8,128)(2,1)S(1)} %get-tuple-element.47.refs_2_.refs_1_, bf16[128,1024]{1,0:T(8,128)(2,1)S(1)} %get-tuple-element.48.refs_3_, ...), custom_call_target="tpu_custom_call" | custom-call | flops 1000000000 | bytes 4194304 | tf_op jit(solution)/shard_map/finish/pallas_call | solution.py:256
  13.7 1.1 %collective-permute-start.4 = (bf16[64,1536]{1,0:T(8,128)(2,1)S(1)}, bf16[64,1536]{1,0:T(8,128)(2,1)S(1)}, u32[]{:S(2)}, u32[]{:S(2)}) collective-permute-start(bf16[64,1536]{1,0:T(8,128)(2,1)S(1)} %get-tuple-element.51), channel_id=1, source_target_pairs={{0,1},{1,0},{2,3},{3,2},{4,5},{5,4},{6,7},{7,6},{8,9},{9,8},{10,11... | collective-permute-start | bytes 589832 | tf_op jit(solution)/shard_map/ppermute | solution.py:318
  14.8 2.3 %collective-permute-start.5 = (bf16[64,1024]{1,0:T(8,128)(2,1)S(1)}, bf16[64,1024]{1,0:T(8,128)(2,1)S(1)}, u32[]{:S(2)}, u32[]{:S(2)}) collective-permute-start(bf16[64,1024]{1,0:T(8,128)(2,1)S(1)} %get-tuple-element.50.refs_1_), channel_id=1, source_target_pairs={{0,15},{1,2},{2,1},{3,4},{4,3},{5,6},{6,5},{7,8},{8,7},{9,10},{10,... | collective-permute-start | bytes 393224 | tf_op jit(solution)/shard_map/ppermute | solution.py:317
  17.1 0.0 collective-permute-done.4.message_ref.refs_2_
  17.1 0.1 collective-permute-start.6
  17.2 1.5 %collective-permute-start.7 = (bf16[64,128]{1,0:T(8,128)(2,1)S(1)}, bf16[64,128]{1,0:T(8,128)(2,1)S(1)}, u32[]{:S(2)}, u32[]{:S(2)}) collective-permute-start(bf16[64,128]{1,0:T(8,128)(2,1)S(1)} %get-tuple-element.54.refs_5_), channel_id=1, source_target_pairs={{0,9},{1,11},{2,10},{3,8},{4,12},{5,15},{6,14},{7,13},{8,0},{9,3},... | collective-permute-start | bytes 49160 | tf_op jit(solution)/shard_map/ppermute | solution.py:330
  18.7 1.3 %own.3 = (f32[64,1024]{1,0:T(8,128)S(1)}, bf16[4,64,1024]{2,1,0:T(8,128)(2,1)}) custom-call(s32[1]{0:T(128)} %bitcast.index_ref.refs_0_, bf16[64,1024]{1,0:T(8,128)(2,1)S(1)} %get-tuple-element.50.refs_1_, bf16[64,1536]{1,0:T(8,128)(2,1)S(1)} %collective-permute-done.4.message_ref.refs_2_, bf16[36,256,256]{2,1,0:T(8,128)(2,1)S(1)} %get-tuple-element.46.d_ref.refs_3_, ...), custom_call_target="tpu_custom_call" | custom-call | flops 1000000000 | bytes 4194304 | tf_op jit(solution)/shard_map/own/pallas_call | solution.py:256
  20.0 1.9 %collective-permute-done.5.over_ref = bf16[64,1024]{1,0:T(8,128)(2,1)S(1)} collective-permute-done((bf16[64,1024]{1,0:T(8,128)(2,1)S(1)}, bf16[64,1024]{1,0:T(8,128)(2,1)S(1)}, u32[]{:S(2)}, u32[]{:S(2)}) %collective-permute-start.5) | collective-permute-done | bytes 131104 | tf_op jit(solution)/shard_map/ppermute | solution.py:317
  21.9 0.5 %halo.5.refs_1_ = f32[64,1024]{1,0:T(8,128)S(1)} custom-call(s32[1]{0:T(128)} %bitcast.index_ref.refs_0_, f32[64,1024]{1,0:T(8,128)S(1)} %get-tuple-element.55.acc_ref, bf16[64,1024]{1,0:T(8,128)(2,1)S(1)} %collective-permute-done.5.over_ref, bf16[36,256,256]{2,1,0:T(8,128)(2,1)S(1)} %get-tuple-element.46.d_ref.refs_3_), custom_call_target="tpu_custom_call" | custom-call | flops 1000000000 | bytes 4194304 | tf_op jit(solution)/shard_map/halo/pallas_call | solution.py:256
  22.4 0.0 collective-permute-done.6.refs_5_
  22.4 0.0 collective-permute-done.7.refs_6_
  22.4 0.6 %finish.4 = (bf16[64,1024]{1,0:T(8,128)(2,1)S(1)}, bf16[64,1536]{1,0:T(8,128)(2,1)S(1)}, f32[64,256]{1,0:T(8,128)S(1)}) custom-call(s32[1]{0:T(128)} %bitcast.index_ref.refs_0_, f32[64,1024]{1,0:T(8,128)S(1)} %halo.5.refs_1_, bf16[256,1024]{1,0:T(8,128)(2,1)S(1)} %get-tuple-element.47.refs_2_.refs_1_, bf16[128,1024]{1,0:T(8,128)(2,1)S(1)} %get-tuple-element.48.refs_3_, ...), custom_call_target="tpu_custom_call" | custom-call | flops 1000000000 | bytes 4194304 | tf_op jit(solution)/shard_map/finish/pallas_call | solution.py:256
  23.0 0.5 %collective-permute-start.8 = (bf16[64,1536]{1,0:T(8,128)(2,1)S(1)}, bf16[64,1536]{1,0:T(8,128)(2,1)S(1)}, u32[]{:S(2)}, u32[]{:S(2)}) collective-permute-start(bf16[64,1536]{1,0:T(8,128)(2,1)S(1)} %get-tuple-element.57), channel_id=1, source_target_pairs={{0,1},{1,0},{2,3},{3,2},{4,5},{5,4},{6,7},{7,6},{8,9},{9,8},{10,11... | collective-permute-start | bytes 589832 | tf_op jit(solution)/shard_map/ppermute | solution.py:318
  23.5 2.4 %collective-permute-start.9 = (bf16[64,1024]{1,0:T(8,128)(2,1)S(1)}, bf16[64,1024]{1,0:T(8,128)(2,1)S(1)}, u32[]{:S(2)}, u32[]{:S(2)}) collective-permute-start(bf16[64,1024]{1,0:T(8,128)(2,1)S(1)} %get-tuple-element.56.refs_1_), channel_id=1, source_target_pairs={{0,15},{1,2},{2,1},{3,4},{4,3},{5,6},{6,5},{7,8},{8,7},{9,10},{10,... | collective-permute-start | bytes 393224 | tf_op jit(solution)/shard_map/ppermute | solution.py:317
  25.9 0.0 collective-permute-done.8.message_ref.refs_2_
  25.9 0.9 %collective-permute-start.10 = (bf16[64,128]{1,0:T(8,128)(2,1)S(1)}, bf16[64,128]{1,0:T(8,128)(2,1)S(1)}, u32[]{:S(2)}, u32[]{:S(2)}) collective-permute-start(bf16[64,128]{1,0:T(8,128)(2,1)S(1)} %get-tuple-element.59.refs_4_), channel_id=1, source_target_pairs={{0,8},{1,10},{2,11},{3,9},{4,13},{5,14},{6,15},{7,12},{8,1},{9,2},... | collective-permute-start | bytes 49160 | tf_op jit(solution)/shard_map/ppermute | solution.py:330
  26.8 0.9 %collective-permute-start.11 = (bf16[64,128]{1,0:T(8,128)(2,1)S(1)}, bf16[64,128]{1,0:T(8,128)(2,1)S(1)}, u32[]{:S(2)}, u32[]{:S(2)}) collective-permute-start(bf16[64,128]{1,0:T(8,128)(2,1)S(1)} %get-tuple-element.60.refs_5_), channel_id=1, source_target_pairs={{0,9},{1,11},{2,10},{3,8},{4,12},{5,15},{6,14},{7,13},{8,0},{9,3},... | collective-permute-start | bytes 49160 | tf_op jit(solution)/shard_map/ppermute | solution.py:330
  27.8 1.3 %own.4 = (f32[64,1024]{1,0:T(8,128)S(1)}, bf16[4,64,1024]{2,1,0:T(8,128)(2,1)}) custom-call(s32[1]{0:T(128)} %bitcast.index_ref.refs_0_, bf16[64,1024]{1,0:T(8,128)(2,1)S(1)} %get-tuple-element.56.refs_1_, bf16[64,1536]{1,0:T(8,128)(2,1)S(1)} %collective-permute-done.8.message_ref.refs_2_, ...), custom_call_target="tpu_custom_call", output_to_operand_aliasing={{1}: (6, {})} | custom-call | flops 1000000000 | bytes 4194304 | tf_op jit(solution)/shard_map/own/pallas_call | solution.py:256
  29.1 1.8 %collective-permute-done.9.over_ref = bf16[64,1024]{1,0:T(8,128)(2,1)S(1)} collective-permute-done((bf16[64,1024]{1,0:T(8,128)(2,1)S(1)}, bf16[64,1024]{1,0:T(8,128)(2,1)S(1)}, u32[]{:S(2)}, u32[]{:S(2)}) %collective-permute-start.9) | collective-permute-done | bytes 131104 | tf_op jit(solution)/shard_map/ppermute | solution.py:317
  30.9 0.5 %halo.6.refs_1_ = f32[64,1024]{1,0:T(8,128)S(1)} custom-call(s32[1]{0:T(128)} %bitcast.index_ref.refs_0_, f32[64,1024]{1,0:T(8,128)S(1)} %get-tuple-element.62.acc_ref, bf16[64,1024]{1,0:T(8,128)(2,1)S(1)} %collective-permute-done.9.over_ref, bf16[36,256,256]{2,1,0:T(8,128)(2,1)S(1)} %get-tuple-element.46.d_ref.refs_3_), custom_call_target="tpu_custom_call" | custom-call | flops 1000000000 | bytes 4194304 | tf_op jit(solution)/shard_map/halo/pallas_call | solution.py:256
  31.4 0.0 collective-permute-done.10.refs_5_
  31.4 0.2 collective-permute-done.11.refs_6_
  31.6 0.6 %finish.5 = (bf16[64,1024]{1,0:T(8,128)(2,1)S(1)}, bf16[64,1536]{1,0:T(8,128)(2,1)S(1)}, f32[64,256]{1,0:T(8,128)S(1)}) custom-call(s32[1]{0:T(128)} %bitcast.index_ref.refs_0_, f32[64,1024]{1,0:T(8,128)S(1)} %halo.6.refs_1_, bf16[256,1024]{1,0:T(8,128)(2,1)S(1)} %get-tuple-element.47.refs_2_.refs_1_, bf16[128,1024]{1,0:T(8,128)(2,1)S(1)} %get-tuple-element.48.refs_3_, ...), custom_call_target="tpu_custom_call" | custom-call | flops 1000000000 | bytes 4194304 | tf_op jit(solution)/shard_map/finish/pallas_call | solution.py:256
  32.2 0.6 %collective-permute-start.12 = (bf16[64,1536]{1,0:T(8,128)(2,1)S(1)}, bf16[64,1536]{1,0:T(8,128)(2,1)S(1)}, u32[]{:S(2)}, u32[]{:S(2)}) collective-permute-start(bf16[64,1536]{1,0:T(8,128)(2,1)S(1)} %get-tuple-element.64), channel_id=1, source_target_pairs={{0,1},{1,0},{2,3},{3,2},{4,5},{5,4},{6,7},{7,6},{8,9},{9,8},{10,11... | collective-permute-start | bytes 589832 | tf_op jit(solution)/shard_map/ppermute | solution.py:318
  32.7 2.5 %collective-permute-start.13 = (bf16[64,1024]{1,0:T(8,128)(2,1)S(1)}, bf16[64,1024]{1,0:T(8,128)(2,1)S(1)}, u32[]{:S(2)}, u32[]{:S(2)}) collective-permute-start(bf16[64,1024]{1,0:T(8,128)(2,1)S(1)} %get-tuple-element.63.refs_1_), channel_id=1, source_target_pairs={{0,15},{1,2},{2,1},{3,4},{4,3},{5,6},{6,5},{7,8},{8,7},{9,10},{10,... | collective-permute-start | bytes 393224 | tf_op jit(solution)/shard_map/ppermute | solution.py:317
  35.2 0.0 collective-permute-done.12.message_ref.refs_2_
  35.2 0.3 collective-permute-start.14
  35.5 1.5 %collective-permute-start.15 = (bf16[64,128]{1,0:T(8,128)(2,1)S(1)}, bf16[64,128]{1,0:T(8,128)(2,1)S(1)}, u32[]{:S(2)}, u32[]{:S(2)}) collective-permute-start(bf16[64,128]{1,0:T(8,128)(2,1)S(1)} %get-tuple-element.67.refs_5_), channel_id=1, source_target_pairs={{0,9},{1,11},{2,10},{3,8},{4,12},{5,15},{6,14},{7,13},{8,0},{9,3},... | collective-permute-start | bytes 49160 | tf_op jit(solution)/shard_map/ppermute | solution.py:330
  37.0 1.3 %own.5 = (f32[64,1024]{1,0:T(8,128)S(1)}, bf16[4,64,1024]{2,1,0:T(8,128)(2,1)}) custom-call(s32[1]{0:T(128)} %bitcast.index_ref.refs_0_, bf16[64,1024]{1,0:T(8,128)(2,1)S(1)} %get-tuple-element.63.refs_1_, bf16[64,1536]{1,0:T(8,128)(2,1)S(1)} %collective-permute-done.12.message_ref.refs_2_, ...), custom_call_target="tpu_custom_call", output_to_operand_aliasing={{1}: (6, {})} | custom-call | flops 1000000000 | bytes 4194304 | tf_op jit(solution)/shard_map/own/pallas_call | solution.py:256
  38.3 1.8 %collective-permute-done.13.over_ref = bf16[64,1024]{1,0:T(8,128)(2,1)S(1)} collective-permute-done((bf16[64,1024]{1,0:T(8,128)(2,1)S(1)}, bf16[64,1024]{1,0:T(8,128)(2,1)S(1)}, u32[]{:S(2)}, u32[]{:S(2)}) %collective-permute-start.13) | collective-permute-done | bytes 131104 | tf_op jit(solution)/shard_map/ppermute | solution.py:317
  40.1 0.5 %halo.7.refs_0_ = f32[64,1024]{1,0:T(8,128)S(1)} custom-call(s32[1]{0:T(128)} %bitcast.index_ref.refs_0_, f32[64,1024]{1,0:T(8,128)S(1)} %get-tuple-element.69.acc_ref, bf16[64,1024]{1,0:T(8,128)(2,1)S(1)} %collective-permute-done.13.over_ref, bf16[36,256,256]{2,1,0:T(8,128)(2,1)S(1)} %get-tuple-element.46.d_ref.refs_3_), custom_call_target="tpu_custom_call" | custom-call | flops 1000000000 | bytes 4194304 | tf_op jit(solution)/shard_map/halo/pallas_call | solution.py:256
  40.6 0.0 collective-permute-done.14.refs_2_
  40.6 0.0 collective-permute-done.15.refs_3_
  40.7 0.9 %last.1 = bf16[4,64,1024]{2,1,0:T(8,128)(2,1)} custom-call(f32[64,1024]{1,0:T(8,128)S(1)} %halo.7.refs_0_, bf16[256,1024]{1,0:T(8,128)(2,1)S(1)} %get-tuple-element.47.refs_2_.refs_1_, bf16[64,128]{1,0:T(8,128)(2,1)S(1)} %collective-permute-done.14.refs_2_, bf16[64,128]{1,0:T(8,128)(2,1)S(1)} %collective-permute-done.15.refs_3_, ...), custom_call_target="tpu_custom_call", output_to_operand_aliasing={{}: (4, {})} | custom-call | flops 1000000000 | bytes 4194304 | tf_op jit(solution)/shard_map/last/pallas_call | solution.py:256
  (4 shorter events, 0.1 us)
Async XLA Ops:
  0.0 8.5 %copy-start.1 = (bf16[4,32,256]{2,1,0:T(8,128)(2,1)S(1)}, bf16[4,32,256]{2,1,0:T(8,128)(2,1)}, u32[]{:S(2)}) copy-start(bf16[4,32,256]{2,1,0:T(8,128)(2,1)} %refs_5_.3) | copy-start | bytes 196612
  0.0 8.5 %copy-start = (bf16[32,256,256]{2,1,0:T(8,128)(2,1)S(1)}, bf16[32,256,256]{2,1,0:T(8,128)(2,1)}, u32[]{:S(2)}) copy-start(bf16[32,256,256]{2,1,0:T(8,128)(2,1)} %refs_6_.3) | copy-start | bytes 12582916
  1.8 6.2 %collective-permute-start = (bf16[64,1536]{1,0:T(8,128)(2,1)S(1)}, bf16[64,1536]{1,0:T(8,128)(2,1)S(1)}, u32[]{:S(2)}, u32[]{:S(2)}) collective-permute-start(bf16[64,1536]{1,0:T(8,128)(2,1)S(1)} %get-tuple-element.41), channel_id=1, source_target_pairs={{0,1},{1,0},{2,3},{3,2},{4,5},{5,4},{6,7},{7,6},{8,9},{9,8},{10,11... | collective-permute-start | bytes 589832 | tf_op jit(solution)/shard_map/ppermute | solution.py:318
  2.4 8.6 %collective-permute-start.1 = (bf16[64,1024]{1,0:T(8,128)(2,1)}, bf16[64,1024]{1,0:T(8,128)(2,1)S(1)}, u32[]{:S(2)}, u32[]{:S(2)}) collective-permute-start(bf16[64,1024]{1,0:T(8,128)(2,1)} %refs_4_.1), channel_id=1, source_target_pairs={{0,15},{1,2},{2,1},{3,4},{4,3},{5,6},{6,5},{7,8},{8,7},{9,10},{10,... | collective-permute-start | bytes 393224 | tf_op jit(solution)/shard_map/ppermute | solution.py:317
  8.0 5.1 %collective-permute-start.2 = (bf16[64,128]{1,0:T(8,128)(2,1)S(1)}, bf16[64,128]{1,0:T(8,128)(2,1)S(1)}, u32[]{:S(2)}, u32[]{:S(2)}) collective-permute-start(bf16[64,128]{1,0:T(8,128)(2,1)S(1)} %get-tuple-element.43.refs_7_), channel_id=1, source_target_pairs={{0,8},{1,10},{2,11},{3,9},{4,13},{5,14},{6,15},{7,12},{8,1},{9,2},... | collective-permute-start | bytes 49160 | tf_op jit(solution)/shard_map/ppermute | solution.py:330
  8.1 5.0 %collective-permute-start.3 = (bf16[64,128]{1,0:T(8,128)(2,1)S(1)}, bf16[64,128]{1,0:T(8,128)(2,1)S(1)}, u32[]{:S(2)}, u32[]{:S(2)}) collective-permute-start(bf16[64,128]{1,0:T(8,128)(2,1)S(1)} %get-tuple-element.44.refs_8_), channel_id=1, source_target_pairs={{0,9},{1,11},{2,10},{3,8},{4,12},{5,15},{6,14},{7,13},{8,0},{9,3},... | collective-permute-start | bytes 49160 | tf_op jit(solution)/shard_map/ppermute | solution.py:330
  13.7 3.4 %collective-permute-start.4 = (bf16[64,1536]{1,0:T(8,128)(2,1)S(1)}, bf16[64,1536]{1,0:T(8,128)(2,1)S(1)}, u32[]{:S(2)}, u32[]{:S(2)}) collective-permute-start(bf16[64,1536]{1,0:T(8,128)(2,1)S(1)} %get-tuple-element.51), channel_id=1, source_target_pairs={{0,1},{1,0},{2,3},{3,2},{4,5},{5,4},{6,7},{7,6},{8,9},{9,8},{10,11... | collective-permute-start | bytes 589832 | tf_op jit(solution)/shard_map/ppermute | solution.py:318
  14.8 7.1 %collective-permute-start.5 = (bf16[64,1024]{1,0:T(8,128)(2,1)S(1)}, bf16[64,1024]{1,0:T(8,128)(2,1)S(1)}, u32[]{:S(2)}, u32[]{:S(2)}) collective-permute-start(bf16[64,1024]{1,0:T(8,128)(2,1)S(1)} %get-tuple-element.50.refs_1_), channel_id=1, source_target_pairs={{0,15},{1,2},{2,1},{3,4},{4,3},{5,6},{6,5},{7,8},{8,7},{9,10},{10,... | collective-permute-start | bytes 393224 | tf_op jit(solution)/shard_map/ppermute | solution.py:317
  17.1 5.3 %collective-permute-start.6 = (bf16[64,128]{1,0:T(8,128)(2,1)S(1)}, bf16[64,128]{1,0:T(8,128)(2,1)S(1)}, u32[]{:S(2)}, u32[]{:S(2)}) collective-permute-start(bf16[64,128]{1,0:T(8,128)(2,1)S(1)} %get-tuple-element.53.refs_4_), channel_id=1, source_target_pairs={{0,8},{1,10},{2,11},{3,9},{4,13},{5,14},{6,15},{7,12},{8,1},{9,2},... | collective-permute-start | bytes 49160 | tf_op jit(solution)/shard_map/ppermute | solution.py:330
  17.2 5.2 %collective-permute-start.7 = (bf16[64,128]{1,0:T(8,128)(2,1)S(1)}, bf16[64,128]{1,0:T(8,128)(2,1)S(1)}, u32[]{:S(2)}, u32[]{:S(2)}) collective-permute-start(bf16[64,128]{1,0:T(8,128)(2,1)S(1)} %get-tuple-element.54.refs_5_), channel_id=1, source_target_pairs={{0,9},{1,11},{2,10},{3,8},{4,12},{5,15},{6,14},{7,13},{8,0},{9,3},... | collective-permute-start | bytes 49160 | tf_op jit(solution)/shard_map/ppermute | solution.py:330
  23.0 2.9 %collective-permute-start.8 = (bf16[64,1536]{1,0:T(8,128)(2,1)S(1)}, bf16[64,1536]{1,0:T(8,128)(2,1)S(1)}, u32[]{:S(2)}, u32[]{:S(2)}) collective-permute-start(bf16[64,1536]{1,0:T(8,128)(2,1)S(1)} %get-tuple-element.57), channel_id=1, source_target_pairs={{0,1},{1,0},{2,3},{3,2},{4,5},{5,4},{6,7},{7,6},{8,9},{9,8},{10,11... | collective-permute-start | bytes 589832 | tf_op jit(solution)/shard_map/ppermute | solution.py:318
  23.5 7.4 %collective-permute-start.9 = (bf16[64,1024]{1,0:T(8,128)(2,1)S(1)}, bf16[64,1024]{1,0:T(8,128)(2,1)S(1)}, u32[]{:S(2)}, u32[]{:S(2)}) collective-permute-start(bf16[64,1024]{1,0:T(8,128)(2,1)S(1)} %get-tuple-element.56.refs_1_), channel_id=1, source_target_pairs={{0,15},{1,2},{2,1},{3,4},{4,3},{5,6},{6,5},{7,8},{8,7},{9,10},{10,... | collective-permute-start | bytes 393224 | tf_op jit(solution)/shard_map/ppermute | solution.py:317
  25.9 5.5 %collective-permute-start.10 = (bf16[64,128]{1,0:T(8,128)(2,1)S(1)}, bf16[64,128]{1,0:T(8,128)(2,1)S(1)}, u32[]{:S(2)}, u32[]{:S(2)}) collective-permute-start(bf16[64,128]{1,0:T(8,128)(2,1)S(1)} %get-tuple-element.59.refs_4_), channel_id=1, source_target_pairs={{0,8},{1,10},{2,11},{3,9},{4,13},{5,14},{6,15},{7,12},{8,1},{9,2},... | collective-permute-start | bytes 49160 | tf_op jit(solution)/shard_map/ppermute | solution.py:330
  26.8 4.7 %collective-permute-start.11 = (bf16[64,128]{1,0:T(8,128)(2,1)S(1)}, bf16[64,128]{1,0:T(8,128)(2,1)S(1)}, u32[]{:S(2)}, u32[]{:S(2)}) collective-permute-start(bf16[64,128]{1,0:T(8,128)(2,1)S(1)} %get-tuple-element.60.refs_5_), channel_id=1, source_target_pairs={{0,9},{1,11},{2,10},{3,8},{4,12},{5,15},{6,14},{7,13},{8,0},{9,3},... | collective-permute-start | bytes 49160 | tf_op jit(solution)/shard_map/ppermute | solution.py:330
  32.2 3.0 %collective-permute-start.12 = (bf16[64,1536]{1,0:T(8,128)(2,1)S(1)}, bf16[64,1536]{1,0:T(8,128)(2,1)S(1)}, u32[]{:S(2)}, u32[]{:S(2)}) collective-permute-start(bf16[64,1536]{1,0:T(8,128)(2,1)S(1)} %get-tuple-element.64), channel_id=1, source_target_pairs={{0,1},{1,0},{2,3},{3,2},{4,5},{5,4},{6,7},{7,6},{8,9},{9,8},{10,11... | collective-permute-start | bytes 589832 | tf_op jit(solution)/shard_map/ppermute | solution.py:318
  32.7 7.4 %collective-permute-start.13 = (bf16[64,1024]{1,0:T(8,128)(2,1)S(1)}, bf16[64,1024]{1,0:T(8,128)(2,1)S(1)}, u32[]{:S(2)}, u32[]{:S(2)}) collective-permute-start(bf16[64,1024]{1,0:T(8,128)(2,1)S(1)} %get-tuple-element.63.refs_1_), channel_id=1, source_target_pairs={{0,15},{1,2},{2,1},{3,4},{4,3},{5,6},{6,5},{7,8},{8,7},{9,10},{10,... | collective-permute-start | bytes 393224 | tf_op jit(solution)/shard_map/ppermute | solution.py:317
  35.2 5.4 %collective-permute-start.14 = (bf16[64,128]{1,0:T(8,128)(2,1)S(1)}, bf16[64,128]{1,0:T(8,128)(2,1)S(1)}, u32[]{:S(2)}, u32[]{:S(2)}) collective-permute-start(bf16[64,128]{1,0:T(8,128)(2,1)S(1)} %get-tuple-element.66.refs_4_), channel_id=1, source_target_pairs={{0,8},{1,10},{2,11},{3,9},{4,13},{5,14},{6,15},{7,12},{8,1},{9,2},... | collective-permute-start | bytes 49160 | tf_op jit(solution)/shard_map/ppermute | solution.py:330
  35.5 5.1 %collective-permute-start.15 = (bf16[64,128]{1,0:T(8,128)(2,1)S(1)}, bf16[64,128]{1,0:T(8,128)(2,1)S(1)}, u32[]{:S(2)}, u32[]{:S(2)}) collective-permute-start(bf16[64,128]{1,0:T(8,128)(2,1)S(1)} %get-tuple-element.67.refs_5_), channel_id=1, source_target_pairs={{0,9},{1,11},{2,10},{3,8},{4,12},{5,15},{6,14},{7,13},{8,0},{9,3},... | collective-permute-start | bytes 49160 | tf_op jit(solution)/shard_map/ppermute | solution.py:330

commit v29 on v28

--- a/solution.py
+++ b/solution.py
@@ -11,7 +11,7 @@
 REACH = 4
 LEVELS = 3
 SPAN = 2 * REACH + 1
-OTHER_CORE_FIRST = 0b11101111
+OTHER_CORE_FIRST = 0b11001111
 
 F32 = jnp.float32
 BF16 = jnp.bfloat16

time: 41.7 us -> 41.9 us (level)
    ppermute x4, starting transfers between devices: 12.8 us -> 15.2 us  [on_device(): over = lax.ppermute(block if product == 0 else current, axes, plan.over)]
    ppermute x8, starting transfers between devices: 5.61 us -> 4.32 us  [on_device(): fars = [lax.ppermute(s, axes, route) for s, route in zip(sends, routes)]]
    ppermute x8, waiting for transfers between devices: 1.84 us -> 2.98 us  [on_device(): fars = [lax.ppermute(s, axes, route) for s, route in zip(sends, routes)]]
    ppermute x4, starting transfers between devices: 2.66 us -> 1.57 us  [on_device(): near = lax.ppermute(sends[0] if plan.paired else current, axes, plan.near)]
    ppermute x4, waiting for transfers between devices: 6.13 us -> 5.26 us  [on_device(): over = lax.ppermute(block if product == 0 else current, axes, plan.over)]
  transfers between devices with their start and end apart: 16 -> 16, of which waited for: 6 -> 8; matrix products, arithmetic and copies ran while one was open for 0% -> 0% of each run, Pallas kernels for 19% -> 19%
where the time goes in v29:
time: 41.9 us; the launch traced here: 41.8 us
  starting transfers between devices  21.1 us (50%)
  Pallas kernels  12.3 us (29%)
  waiting for transfers between devices  8.25 us (20%)
    ppermute x4, starting transfers between devices, on_device(): over = lax.ppermute(block if product == 0 else current, axes, plan.over)  15.2 us
    pallas_call x17, Pallas kernels, call(): pl.pallas_call(kernel, in_specs=list(specs), out_specs=out_specs or [IN_V...  12.3 us
    ppermute x4, waiting for transfers between devices, on_device(): over = lax.ppermute(block if product == 0 else current, axes, plan.over)  5.26 us
    ppermute x8, starting transfers between devices, on_device(): fars = [lax.ppermute(s, axes, route) for s, route in zip(sends, routes)]  4.32 us
    ppermute x8, waiting for transfers between devices, on_device(): fars = [lax.ppermute(s, axes, route) for s, route in zip(sends, routes)]  2.98 us
    ppermute x4, starting transfers between devices, on_device(): near = lax.ppermute(sends[0] if plan.paired else current, axes, plan.near)  1.57 us
  transfers between devices with their start and end apart: 16, of which 8 were waited for; matrix products, arithmetic and copies ran while one was open for 0% of the time, Pallas kernels for 19%

profile of v29, /device:TPU:0, one launch (start us, length us, event | category | flops | bytes accessed | tf_op | source)
XLA Modules:
  0.0 41.8 jit_solution(872069406826881815)
XLA Ops:
  0.0 0.0 copy-start.1
  0.0 0.0 copy-start
  0.0 1.8 %prepare.1 = (bf16[64,1024]{1,0:T(8,128)(2,1)S(1)}, bf16[1,512,256]{2,1,0:T(8,128)(2,1)S(1)}, bf16[128,1024]{1,0:T(8,128)(2,1)S(1)}, s32[32]{0:T(128)S(4)}, s32[...) custom-call(s32[1]{0:T(128)} %bitcast.index_ref.refs_0_, s32[32]{0:T(128)} %refs_0_.1, s32[32]{0:T(128)} %refs_1_.1, ...), custom_call_target="tpu_custom_call" | custom-call | flops 1000000000 | bytes 4194304 | tf_op jit(solution)/shard_map/prepare/pallas_call | solution.py:256
  1.9 0.5 %collective-permute-start = (bf16[64,1536]{1,0:T(8,128)(2,1)S(1)}, bf16[64,1536]{1,0:T(8,128)(2,1)S(1)}, u32[]{:S(2)}, u32[]{:S(2)}) collective-permute-start(bf16[64,1536]{1,0:T(8,128)(2,1)S(1)} %get-tuple-element.41), channel_id=1, source_target_pairs={{0,1},{1,0},{2,3},{3,2},{4,5},{5,4},{6,7},{7,6},{8,9},{9,8},{10,11... | collective-permute-start | bytes 589832 | tf_op jit(solution)/shard_map/ppermute | solution.py:318
  2.4 5.6 %collective-permute-start.1 = (bf16[64,1024]{1,0:T(8,128)(2,1)}, bf16[64,1024]{1,0:T(8,128)(2,1)S(1)}, u32[]{:S(2)}, u32[]{:S(2)}) collective-permute-start(bf16[64,1024]{1,0:T(8,128)(2,1)} %refs_4_.1), channel_id=1, source_target_pairs={{0,15},{1,2},{2,1},{3,4},{4,3},{5,6},{6,5},{7,8},{8,7},{9,10},{10,... | collective-permute-start | bytes 393224 | tf_op jit(solution)/shard_map/ppermute | solution.py:317
  8.0 0.0 collective-permute-done.message_ref.refs_4_
  8.0 0.1 collective-permute-start.2
  8.1 0.3 collective-permute-start.3
  8.5 0.0 copy-done.1
  8.5 0.0 copy-done
  8.5 1.9 %first_own.1 = (f32[64,1024]{1,0:T(8,128)S(1)}, bf16[36,256,256]{2,1,0:T(8,128)(2,1)S(1)}, bf16[256,1024]{1,0:T(8,128)(2,1)S(1)}) custom-call(s32[1]{0:T(128)} %bitcast.index_ref.refs_0_, s32[32]{0:T(128)S(4)} %get-tuple-element.38.refs_1_, s32[32]{0:T(128)S(4)} %get-tuple-element.39.refs_2_, bf16[64,1024]{1,0:T(8,128)(2,1)S(1)} %get-tuple-element.40.refs_3_, ...), custom_call_target="tpu_custom_call" | custom-call | flops 1000000000 | bytes 4194304 | tf_op jit(solution)/shard_map/first_own/pallas_call | solution.py:256
  10.3 0.6 %collective-permute-done.1.over_ref = bf16[64,1024]{1,0:T(8,128)(2,1)S(1)} collective-permute-done((bf16[64,1024]{1,0:T(8,128)(2,1)}, bf16[64,1024]{1,0:T(8,128)(2,1)S(1)}, u32[]{:S(2)}, u32[]{:S(2)}) %collective-permute-start.1) | collective-permute-done | bytes 131104 | tf_op jit(solution)/shard_map/ppermute | solution.py:317
  10.9 0.5 %halo.4.refs_1_ = f32[64,1024]{1,0:T(8,128)S(1)} custom-call(s32[1]{0:T(128)} %bitcast.index_ref.refs_0_, f32[64,1024]{1,0:T(8,128)S(1)} %get-tuple-element.45.acc_ref, bf16[64,1024]{1,0:T(8,128)(2,1)S(1)} %collective-permute-done.1.over_ref, bf16[36,256,256]{2,1,0:T(8,128)(2,1)S(1)} %get-tuple-element.46.d_ref.refs_3_), custom_call_target="tpu_custom_call" | custom-call | flops 1000000000 | bytes 4194304 | tf_op jit(solution)/shard_map/halo/pallas_call | solution.py:256
  11.5 1.8 %collective-permute-done.2.refs_5_ = bf16[64,128]{1,0:T(8,128)(2,1)S(1)} collective-permute-done((bf16[64,128]{1,0:T(8,128)(2,1)S(1)}, bf16[64,128]{1,0:T(8,128)(2,1)S(1)}, u32[]{:S(2)}, u32[]{:S(2)}) %collective-permute-start.2) | collective-permute-done | bytes 16416 | tf_op jit(solution)/shard_map/ppermute | solution.py:330
  13.2 0.0 collective-permute-done.3.refs_6_
  13.2 0.6 %finish.3 = (bf16[64,1024]{1,0:T(8,128)(2,1)S(1)}, bf16[64,1536]{1,0:T(8,128)(2,1)S(1)}, f32[64,256]{1,0:T(8,128)S(1)}) custom-call(s32[1]{0:T(128)} %bitcast.index_ref.refs_0_, f32[64,1024]{1,0:T(8,128)S(1)} %halo.4.refs_1_, bf16[256,1024]{1,0:T(8,128)(2,1)S(1)} %get-tuple-element.47.refs_2_.refs_1_, bf16[128,1024]{1,0:T(8,128)(2,1)S(1)} %get-tuple-element.48.refs_3_, ...), custom_call_target="tpu_custom_call" | custom-call | flops 1000000000 | bytes 4194304 | tf_op jit(solution)/shard_map/finish/pallas_call | solution.py:256
  13.8 0.2 collective-permute-start.4
  14.0 3.2 %collective-permute-start.5 = (bf16[64,1024]{1,0:T(8,128)(2,1)S(1)}, bf16[64,1024]{1,0:T(8,128)(2,1)S(1)}, u32[]{:S(2)}, u32[]{:S(2)}) collective-permute-start(bf16[64,1024]{1,0:T(8,128)(2,1)S(1)} %get-tuple-element.50.refs_1_), channel_id=1, source_target_pairs={{0,15},{1,2},{2,1},{3,4},{4,3},{5,6},{6,5},{7,8},{8,7},{9,10},{10,... | collective-permute-start | bytes 393224 | tf_op jit(solution)/shard_map/ppermute | solution.py:317
  17.2 0.0 collective-permute-done.4.message_ref.refs_2_
  17.2 0.1 collective-permute-start.6
  17.3 1.6 %collective-permute-start.7 = (bf16[64,128]{1,0:T(8,128)(2,1)S(1)}, bf16[64,128]{1,0:T(8,128)(2,1)S(1)}, u32[]{:S(2)}, u32[]{:S(2)}) collective-permute-start(bf16[64,128]{1,0:T(8,128)(2,1)S(1)} %get-tuple-element.54.refs_5_), channel_id=1, source_target_pairs={{0,9},{1,10},{2,11},{3,8},{4,12},{5,15},{6,14},{7,13},{8,0},{9,3},... | collective-permute-start | bytes 49160 | tf_op jit(solution)/shard_map/ppermute | solution.py:330
  18.9 1.3 %own.3 = (f32[64,1024]{1,0:T(8,128)S(1)}, bf16[4,64,1024]{2,1,0:T(8,128)(2,1)}) custom-call(s32[1]{0:T(128)} %bitcast.index_ref.refs_0_, bf16[64,1024]{1,0:T(8,128)(2,1)S(1)} %get-tuple-element.50.refs_1_, bf16[64,1536]{1,0:T(8,128)(2,1)S(1)} %collective-permute-done.4.message_ref.refs_2_, bf16[36,256,256]{2,1,0:T(8,128)(2,1)S(1)} %get-tuple-element.46.d_ref.refs_3_, ...), custom_call_target="tpu_custom_call" | custom-call | flops 1000000000 | bytes 4194304 | tf_op jit(solution)/shard_map/own/pallas_call | solution.py:256
  20.2 1.1 %collective-permute-done.5.over_ref = bf16[64,1024]{1,0:T(8,128)(2,1)S(1)} collective-permute-done((bf16[64,1024]{1,0:T(8,128)(2,1)S(1)}, bf16[64,1024]{1,0:T(8,128)(2,1)S(1)}, u32[]{:S(2)}, u32[]{:S(2)}) %collective-permute-start.5) | collective-permute-done | bytes 131104 | tf_op jit(solution)/shard_map/ppermute | solution.py:317
  21.3 0.5 %halo.5.refs_1_ = f32[64,1024]{1,0:T(8,128)S(1)} custom-call(s32[1]{0:T(128)} %bitcast.index_ref.refs_0_, f32[64,1024]{1,0:T(8,128)S(1)} %get-tuple-element.55.acc_ref, bf16[64,1024]{1,0:T(8,128)(2,1)S(1)} %collective-permute-done.5.over_ref, bf16[36,256,256]{2,1,0:T(8,128)(2,1)S(1)} %get-tuple-element.46.d_ref.refs_3_), custom_call_target="tpu_custom_call" | custom-call | flops 1000000000 | bytes 4194304 | tf_op jit(solution)/shard_map/halo/pallas_call | solution.py:256
  21.8 0.4 %collective-permute-done.6.refs_5_ = bf16[64,128]{1,0:T(8,128)(2,1)S(1)} collective-permute-done((bf16[64,128]{1,0:T(8,128)(2,1)S(1)}, bf16[64,128]{1,0:T(8,128)(2,1)S(1)}, u32[]{:S(2)}, u32[]{:S(2)}) %collective-permute-start.6) | collective-permute-done | bytes 16416 | tf_op jit(solution)/shard_map/ppermute | solution.py:330
  22.3 0.0 collective-permute-done.7.refs_6_
  22.3 0.6 %finish.4 = (bf16[64,1024]{1,0:T(8,128)(2,1)S(1)}, bf16[64,1536]{1,0:T(8,128)(2,1)S(1)}, f32[64,256]{1,0:T(8,128)S(1)}) custom-call(s32[1]{0:T(128)} %bitcast.index_ref.refs_0_, f32[64,1024]{1,0:T(8,128)S(1)} %halo.5.refs_1_, bf16[256,1024]{1,0:T(8,128)(2,1)S(1)} %get-tuple-element.47.refs_2_.refs_1_, bf16[128,1024]{1,0:T(8,128)(2,1)S(1)} %get-tuple-element.48.refs_3_, ...), custom_call_target="tpu_custom_call" | custom-call | flops 1000000000 | bytes 4194304 | tf_op jit(solution)/shard_map/finish/pallas_call | solution.py:256
  22.9 0.3 collective-permute-start.8
  23.2 3.0 %collective-permute-start.9 = (bf16[64,1024]{1,0:T(8,128)(2,1)S(1)}, bf16[64,1024]{1,0:T(8,128)(2,1)S(1)}, u32[]{:S(2)}, u32[]{:S(2)}) collective-permute-start(bf16[64,1024]{1,0:T(8,128)(2,1)S(1)} %get-tuple-element.56.refs_1_), channel_id=1, source_target_pairs={{0,15},{1,2},{2,1},{3,4},{4,3},{5,6},{6,5},{7,8},{8,7},{9,10},{10,... | collective-permute-start | bytes 393224 | tf_op jit(solution)/shard_map/ppermute | solution.py:317
  26.2 0.0 collective-permute-done.8.message_ref.refs_2_
  26.2 0.1 collective-permute-start.10
  26.3 1.2 %collective-permute-start.11 = (bf16[64,128]{1,0:T(8,128)(2,1)S(1)}, bf16[64,128]{1,0:T(8,128)(2,1)S(1)}, u32[]{:S(2)}, u32[]{:S(2)}) collective-permute-start(bf16[64,128]{1,0:T(8,128)(2,1)S(1)} %get-tuple-element.60.refs_5_), channel_id=1, source_target_pairs={{0,9},{1,10},{2,11},{3,8},{4,12},{5,15},{6,14},{7,13},{8,0},{9,3},... | collective-permute-start | bytes 49160 | tf_op jit(solution)/shard_map/ppermute | solution.py:330
  27.5 1.3 %own.4 = (f32[64,1024]{1,0:T(8,128)S(1)}, bf16[4,64,1024]{2,1,0:T(8,128)(2,1)}) custom-call(s32[1]{0:T(128)} %bitcast.index_ref.refs_0_, bf16[64,1024]{1,0:T(8,128)(2,1)S(1)} %get-tuple-element.56.refs_1_, bf16[64,1536]{1,0:T(8,128)(2,1)S(1)} %collective-permute-done.8.message_ref.refs_2_, ...), custom_call_target="tpu_custom_call", output_to_operand_aliasing={{1}: (6, {})} | custom-call | flops 1000000000 | bytes 4194304 | tf_op jit(solution)/shard_map/own/pallas_call | solution.py:256
  28.8 1.7 %collective-permute-done.9.over_ref = bf16[64,1024]{1,0:T(8,128)(2,1)S(1)} collective-permute-done((bf16[64,1024]{1,0:T(8,128)(2,1)S(1)}, bf16[64,1024]{1,0:T(8,128)(2,1)S(1)}, u32[]{:S(2)}, u32[]{:S(2)}) %collective-permute-start.9) | collective-permute-done | bytes 131104 | tf_op jit(solution)/shard_map/ppermute | solution.py:317
  30.5 0.5 %halo.6.refs_1_ = f32[64,1024]{1,0:T(8,128)S(1)} custom-call(s32[1]{0:T(128)} %bitcast.index_ref.refs_0_, f32[64,1024]{1,0:T(8,128)S(1)} %get-tuple-element.62.acc_ref, bf16[64,1024]{1,0:T(8,128)(2,1)S(1)} %collective-permute-done.9.over_ref, bf16[36,256,256]{2,1,0:T(8,128)(2,1)S(1)} %get-tuple-element.46.d_ref.refs_3_), custom_call_target="tpu_custom_call" | custom-call | flops 1000000000 | bytes 4194304 | tf_op jit(solution)/shard_map/halo/pallas_call | solution.py:256
  31.1 0.2 collective-permute-done.10.refs_5_
  31.2 0.0 collective-permute-done.11.refs_6_
  31.3 0.6 %finish.5 = (bf16[64,1024]{1,0:T(8,128)(2,1)S(1)}, bf16[64,1536]{1,0:T(8,128)(2,1)S(1)}, f32[64,256]{1,0:T(8,128)S(1)}) custom-call(s32[1]{0:T(128)} %bitcast.index_ref.refs_0_, f32[64,1024]{1,0:T(8,128)S(1)} %halo.6.refs_1_, bf16[256,1024]{1,0:T(8,128)(2,1)S(1)} %get-tuple-element.47.refs_2_.refs_1_, bf16[128,1024]{1,0:T(8,128)(2,1)S(1)} %get-tuple-element.48.refs_3_, ...), custom_call_target="tpu_custom_call" | custom-call | flops 1000000000 | bytes 4194304 | tf_op jit(solution)/shard_map/finish/pallas_call | solution.py:256
  31.8 0.6 %collective-permute-start.12 = (bf16[64,1536]{1,0:T(8,128)(2,1)S(1)}, bf16[64,1536]{1,0:T(8,128)(2,1)S(1)}, u32[]{:S(2)}, u32[]{:S(2)}) collective-permute-start(bf16[64,1536]{1,0:T(8,128)(2,1)S(1)} %get-tuple-element.64), channel_id=1, source_target_pairs={{0,1},{1,0},{2,3},{3,2},{4,5},{5,4},{6,7},{7,6},{8,9},{9,8},{10,11... | collective-permute-start | bytes 589832 | tf_op jit(solution)/shard_map/ppermute | solution.py:318
  32.4 3.3 %collective-permute-start.13 = (bf16[64,1024]{1,0:T(8,128)(2,1)S(1)}, bf16[64,1024]{1,0:T(8,128)(2,1)S(1)}, u32[]{:S(2)}, u32[]{:S(2)}) collective-permute-start(bf16[64,1024]{1,0:T(8,128)(2,1)S(1)} %get-tuple-element.63.refs_1_), channel_id=1, source_target_pairs={{0,15},{1,2},{2,1},{3,4},{4,3},{5,6},{6,5},{7,8},{8,7},{9,10},{10,... | collective-permute-start | bytes 393224 | tf_op jit(solution)/shard_map/ppermute | solution.py:317
  35.7 0.0 collective-permute-done.12.message_ref.refs_2_
  35.7 0.1 collective-permute-start.14
  35.8 0.9 %collective-permute-start.15 = (bf16[64,128]{1,0:T(8,128)(2,1)S(1)}, bf16[64,128]{1,0:T(8,128)(2,1)S(1)}, u32[]{:S(2)}, u32[]{:S(2)}) collective-permute-start(bf16[64,128]{1,0:T(8,128)(2,1)S(1)} %get-tuple-element.67.refs_5_), channel_id=1, source_target_pairs={{0,9},{1,10},{2,11},{3,8},{4,12},{5,15},{6,14},{7,13},{8,0},{9,3},... | collective-permute-start | bytes 49160 | tf_op jit(solution)/shard_map/ppermute | solution.py:330
  36.7 1.3 %own.5 = (f32[64,1024]{1,0:T(8,128)S(1)}, bf16[4,64,1024]{2,1,0:T(8,128)(2,1)}) custom-call(s32[1]{0:T(128)} %bitcast.index_ref.refs_0_, bf16[64,1024]{1,0:T(8,128)(2,1)S(1)} %get-tuple-element.63.refs_1_, bf16[64,1536]{1,0:T(8,128)(2,1)S(1)} %collective-permute-done.12.message_ref.refs_2_, ...), custom_call_target="tpu_custom_call", output_to_operand_aliasing={{1}: (6, {})} | custom-call | flops 1000000000 | bytes 4194304 | tf_op jit(solution)/shard_map/own/pallas_call | solution.py:256
  38.0 1.8 %collective-permute-done.13.over_ref = bf16[64,1024]{1,0:T(8,128)(2,1)S(1)} collective-permute-done((bf16[64,1024]{1,0:T(8,128)(2,1)S(1)}, bf16[64,1024]{1,0:T(8,128)(2,1)S(1)}, u32[]{:S(2)}, u32[]{:S(2)}) %collective-permute-start.13) | collective-permute-done | bytes 131104 | tf_op jit(solution)/shard_map/ppermute | solution.py:317
  39.8 0.5 %halo.7.refs_0_ = f32[64,1024]{1,0:T(8,128)S(1)} custom-call(s32[1]{0:T(128)} %bitcast.index_ref.refs_0_, f32[64,1024]{1,0:T(8,128)S(1)} %get-tuple-element.69.acc_ref, bf16[64,1024]{1,0:T(8,128)(2,1)S(1)} %collective-permute-done.13.over_ref, bf16[36,256,256]{2,1,0:T(8,128)(2,1)S(1)} %get-tuple-element.46.d_ref.refs_3_), custom_call_target="tpu_custom_call" | custom-call | flops 1000000000 | bytes 4194304 | tf_op jit(solution)/shard_map/halo/pallas_call | solution.py:256
  40.3 0.6 %collective-permute-done.14.refs_2_ = bf16[64,128]{1,0:T(8,128)(2,1)S(1)} collective-permute-done((bf16[64,128]{1,0:T(8,128)(2,1)S(1)}, bf16[64,128]{1,0:T(8,128)(2,1)S(1)}, u32[]{:S(2)}, u32[]{:S(2)}) %collective-permute-start.14) | collective-permute-done | bytes 16416 | tf_op jit(solution)/shard_map/ppermute | solution.py:330
  40.9 0.0 collective-permute-done.15.refs_3_
  40.9 0.9 %last.1 = bf16[4,64,1024]{2,1,0:T(8,128)(2,1)} custom-call(f32[64,1024]{1,0:T(8,128)S(1)} %halo.7.refs_0_, bf16[256,1024]{1,0:T(8,128)(2,1)S(1)} %get-tuple-element.47.refs_2_.refs_1_, bf16[64,128]{1,0:T(8,128)(2,1)S(1)} %collective-permute-done.14.refs_2_, bf16[64,128]{1,0:T(8,128)(2,1)S(1)} %collective-permute-done.15.refs_3_, ...), custom_call_target="tpu_custom_call", output_to_operand_aliasing={{}: (4, {})} | custom-call | flops 1000000000 | bytes 4194304 | tf_op jit(solution)/shard_map/last/pallas_call | solution.py:256
  (4 shorter events, 0.1 us)
Async XLA Ops:
  0.0 8.5 %copy-start.1 = (bf16[4,32,256]{2,1,0:T(8,128)(2,1)S(1)}, bf16[4,32,256]{2,1,0:T(8,128)(2,1)}, u32[]{:S(2)}) copy-start(bf16[4,32,256]{2,1,0:T(8,128)(2,1)} %refs_5_.3) | copy-start | bytes 196612
  0.0 8.5 %copy-start = (bf16[32,256,256]{2,1,0:T(8,128)(2,1)S(1)}, bf16[32,256,256]{2,1,0:T(8,128)(2,1)}, u32[]{:S(2)}) copy-start(bf16[32,256,256]{2,1,0:T(8,128)(2,1)} %refs_6_.3) | copy-start | bytes 12582916
  1.9 6.2 %collective-permute-start = (bf16[64,1536]{1,0:T(8,128)(2,1)S(1)}, bf16[64,1536]{1,0:T(8,128)(2,1)S(1)}, u32[]{:S(2)}, u32[]{:S(2)}) collective-permute-start(bf16[64,1536]{1,0:T(8,128)(2,1)S(1)} %get-tuple-element.41), channel_id=1, source_target_pairs={{0,1},{1,0},{2,3},{3,2},{4,5},{5,4},{6,7},{7,6},{8,9},{9,8},{10,11... | collective-permute-start | bytes 589832 | tf_op jit(solution)/shard_map/ppermute | solution.py:318
  2.4 8.6 %collective-permute-start.1 = (bf16[64,1024]{1,0:T(8,128)(2,1)}, bf16[64,1024]{1,0:T(8,128)(2,1)S(1)}, u32[]{:S(2)}, u32[]{:S(2)}) collective-permute-start(bf16[64,1024]{1,0:T(8,128)(2,1)} %refs_4_.1), channel_id=1, source_target_pairs={{0,15},{1,2},{2,1},{3,4},{4,3},{5,6},{6,5},{7,8},{8,7},{9,10},{10,... | collective-permute-start | bytes 393224 | tf_op jit(solution)/shard_map/ppermute | solution.py:317
  8.0 5.2 %collective-permute-start.2 = (bf16[64,128]{1,0:T(8,128)(2,1)S(1)}, bf16[64,128]{1,0:T(8,128)(2,1)S(1)}, u32[]{:S(2)}, u32[]{:S(2)}) collective-permute-start(bf16[64,128]{1,0:T(8,128)(2,1)S(1)} %get-tuple-element.43.refs_7_), channel_id=1, source_target_pairs={{0,8},{1,11},{2,10},{3,9},{4,13},{5,14},{6,15},{7,12},{8,1},{9,2},... | collective-permute-start | bytes 49160 | tf_op jit(solution)/shard_map/ppermute | solution.py:330
  8.1 5.1 %collective-permute-start.3 = (bf16[64,128]{1,0:T(8,128)(2,1)S(1)}, bf16[64,128]{1,0:T(8,128)(2,1)S(1)}, u32[]{:S(2)}, u32[]{:S(2)}) collective-permute-start(bf16[64,128]{1,0:T(8,128)(2,1)S(1)} %get-tuple-element.44.refs_8_), channel_id=1, source_target_pairs={{0,9},{1,10},{2,11},{3,8},{4,12},{5,15},{6,14},{7,13},{8,0},{9,3},... | collective-permute-start | bytes 49160 | tf_op jit(solution)/shard_map/ppermute | solution.py:330
  13.8 3.4 %collective-permute-start.4 = (bf16[64,1536]{1,0:T(8,128)(2,1)S(1)}, bf16[64,1536]{1,0:T(8,128)(2,1)S(1)}, u32[]{:S(2)}, u32[]{:S(2)}) collective-permute-start(bf16[64,1536]{1,0:T(8,128)(2,1)S(1)} %get-tuple-element.51), channel_id=1, source_target_pairs={{0,1},{1,0},{2,3},{3,2},{4,5},{5,4},{6,7},{7,6},{8,9},{9,8},{10,11... | collective-permute-start | bytes 589832 | tf_op jit(solution)/shard_map/ppermute | solution.py:318
  14.0 7.3 %collective-permute-start.5 = (bf16[64,1024]{1,0:T(8,128)(2,1)S(1)}, bf16[64,1024]{1,0:T(8,128)(2,1)S(1)}, u32[]{:S(2)}, u32[]{:S(2)}) collective-permute-start(bf16[64,1024]{1,0:T(8,128)(2,1)S(1)} %get-tuple-element.50.refs_1_), channel_id=1, source_target_pairs={{0,15},{1,2},{2,1},{3,4},{4,3},{5,6},{6,5},{7,8},{8,7},{9,10},{10,... | collective-permute-start | bytes 393224 | tf_op jit(solution)/shard_map/ppermute | solution.py:317
  17.2 5.0 %collective-permute-start.6 = (bf16[64,128]{1,0:T(8,128)(2,1)S(1)}, bf16[64,128]{1,0:T(8,128)(2,1)S(1)}, u32[]{:S(2)}, u32[]{:S(2)}) collective-permute-start(bf16[64,128]{1,0:T(8,128)(2,1)S(1)} %get-tuple-element.53.refs_4_), channel_id=1, source_target_pairs={{0,8},{1,11},{2,10},{3,9},{4,13},{5,14},{6,15},{7,12},{8,1},{9,2},... | collective-permute-start | bytes 49160 | tf_op jit(solution)/shard_map/ppermute | solution.py:330
  17.3 5.0 %collective-permute-start.7 = (bf16[64,128]{1,0:T(8,128)(2,1)S(1)}, bf16[64,128]{1,0:T(8,128)(2,1)S(1)}, u32[]{:S(2)}, u32[]{:S(2)}) collective-permute-start(bf16[64,128]{1,0:T(8,128)(2,1)S(1)} %get-tuple-element.54.refs_5_), channel_id=1, source_target_pairs={{0,9},{1,10},{2,11},{3,8},{4,12},{5,15},{6,14},{7,13},{8,0},{9,3},... | collective-permute-start | bytes 49160 | tf_op jit(solution)/shard_map/ppermute | solution.py:330
  22.9 3.3 %collective-permute-start.8 = (bf16[64,1536]{1,0:T(8,128)(2,1)S(1)}, bf16[64,1536]{1,0:T(8,128)(2,1)S(1)}, u32[]{:S(2)}, u32[]{:S(2)}) collective-permute-start(bf16[64,1536]{1,0:T(8,128)(2,1)S(1)} %get-tuple-element.57), channel_id=1, source_target_pairs={{0,1},{1,0},{2,3},{3,2},{4,5},{5,4},{6,7},{7,6},{8,9},{9,8},{10,11... | collective-permute-start | bytes 589832 | tf_op jit(solution)/shard_map/ppermute | solution.py:318
  23.2 7.4 %collective-permute-start.9 = (bf16[64,1024]{1,0:T(8,128)(2,1)S(1)}, bf16[64,1024]{1,0:T(8,128)(2,1)S(1)}, u32[]{:S(2)}, u32[]{:S(2)}) collective-permute-start(bf16[64,1024]{1,0:T(8,128)(2,1)S(1)} %get-tuple-element.56.refs_1_), channel_id=1, source_target_pairs={{0,15},{1,2},{2,1},{3,4},{4,3},{5,6},{6,5},{7,8},{8,7},{9,10},{10,... | collective-permute-start | bytes 393224 | tf_op jit(solution)/shard_map/ppermute | solution.py:317
  26.2 5.0 %collective-permute-start.10 = (bf16[64,128]{1,0:T(8,128)(2,1)S(1)}, bf16[64,128]{1,0:T(8,128)(2,1)S(1)}, u32[]{:S(2)}, u32[]{:S(2)}) collective-permute-start(bf16[64,128]{1,0:T(8,128)(2,1)S(1)} %get-tuple-element.59.refs_4_), channel_id=1, source_target_pairs={{0,8},{1,11},{2,10},{3,9},{4,13},{5,14},{6,15},{7,12},{8,1},{9,2},... | collective-permute-start | bytes 49160 | tf_op jit(solution)/shard_map/ppermute | solution.py:330
  26.3 5.0 %collective-permute-start.11 = (bf16[64,128]{1,0:T(8,128)(2,1)S(1)}, bf16[64,128]{1,0:T(8,128)(2,1)S(1)}, u32[]{:S(2)}, u32[]{:S(2)}) collective-permute-start(bf16[64,128]{1,0:T(8,128)(2,1)S(1)} %get-tuple-element.60.refs_5_), channel_id=1, source_target_pairs={{0,9},{1,10},{2,11},{3,8},{4,12},{5,15},{6,14},{7,13},{8,0},{9,3},... | collective-permute-start | bytes 49160 | tf_op jit(solution)/shard_map/ppermute | solution.py:330
  31.8 3.8 %collective-permute-start.12 = (bf16[64,1536]{1,0:T(8,128)(2,1)S(1)}, bf16[64,1536]{1,0:T(8,128)(2,1)S(1)}, u32[]{:S(2)}, u32[]{:S(2)}) collective-permute-start(bf16[64,1536]{1,0:T(8,128)(2,1)S(1)} %get-tuple-element.64), channel_id=1, source_target_pairs={{0,1},{1,0},{2,3},{3,2},{4,5},{5,4},{6,7},{7,6},{8,9},{9,8},{10,11... | collective-permute-start | bytes 589832 | tf_op jit(solution)/shard_map/ppermute | solution.py:318
  32.4 7.4 %collective-permute-start.13 = (bf16[64,1024]{1,0:T(8,128)(2,1)S(1)}, bf16[64,1024]{1,0:T(8,128)(2,1)S(1)}, u32[]{:S(2)}, u32[]{:S(2)}) collective-permute-start(bf16[64,1024]{1,0:T(8,128)(2,1)S(1)} %get-tuple-element.63.refs_1_), channel_id=1, source_target_pairs={{0,15},{1,2},{2,1},{3,4},{4,3},{5,6},{6,5},{7,8},{8,7},{9,10},{10,... | collective-permute-start | bytes 393224 | tf_op jit(solution)/shard_map/ppermute | solution.py:317
  35.7 5.2 %collective-permute-start.14 = (bf16[64,128]{1,0:T(8,128)(2,1)S(1)}, bf16[64,128]{1,0:T(8,128)(2,1)S(1)}, u32[]{:S(2)}, u32[]{:S(2)}) collective-permute-start(bf16[64,128]{1,0:T(8,128)(2,1)S(1)} %get-tuple-element.66.refs_4_), channel_id=1, source_target_pairs={{0,8},{1,11},{2,10},{3,9},{4,13},{5,14},{6,15},{7,12},{8,1},{9,2},... | collective-permute-start | bytes 49160 | tf_op jit(solution)/shard_map/ppermute | solution.py:330
  35.8 5.1 %collective-permute-start.15 = (bf16[64,128]{1,0:T(8,128)(2,1)S(1)}, bf16[64,128]{1,0:T(8,128)(2,1)S(1)}, u32[]{:S(2)}, u32[]{:S(2)}) collective-permute-start(bf16[64,128]{1,0:T(8,128)(2,1)S(1)} %get-tuple-element.67.refs_5_), channel_id=1, source_target_pairs={{0,9},{1,10},{2,11},{3,8},{4,12},{5,15},{6,14},{7,13},{8,0},{9,3},... | collective-permute-start | bytes 49160 | tf_op jit(solution)/shard_map/ppermute | solution.py:330

commit v30 on v29

--- a/solution.py
+++ b/solution.py
@@ -11,7 +11,7 @@
 REACH = 4
 LEVELS = 3
 SPAN = 2 * REACH + 1
-OTHER_CORE_FIRST = 0b11001111
+OTHER_CORE_FIRST = 0b11110111
 
 F32 = jnp.float32
 BF16 = jnp.bfloat16

time: 41.9 us -> 41.6 us (level)
  starting transfers between devices: 21.1 us -> 20.4 us
    ppermute x4, starting transfers between devices: 15.2 us -> 13.3 us  [on_device(): over = lax.ppermute(block if product == 0 else current, axes, plan.over)]
    ppermute x4, waiting for transfers between devices: 5.26 us -> 6.51 us  [on_device(): over = lax.ppermute(block if product == 0 else current, axes, plan.over)]
    ppermute x8, waiting for transfers between devices: 2.98 us -> 1.83 us  [on_device(): fars = [lax.ppermute(s, axes, route) for s, route in zip(sends, routes)]]
    ppermute x4, starting transfers between devices: 1.57 us -> 2.59 us  [on_device(): near = lax.ppermute(sends[0] if plan.paired else current, axes, plan.near)]
  transfers between devices with their start and end apart: 16 -> 16, of which waited for: 8 -> 7; matrix products, arithmetic and copies ran while one was open for 0% -> 0% of each run, Pallas kernels for 19% -> 19%
where the time goes in v30:
time: 41.6 us; the launch traced here: 41.2 us
  starting transfers between devices  20.4 us (49%)
  Pallas kernels  12.3 us (30%)
  waiting for transfers between devices  8.35 us (20%)
    ppermute x4, starting transfers between devices, on_device(): over = lax.ppermute(block if product == 0 else current, axes, plan.over)  13.3 us
    pallas_call x17, Pallas kernels, call(): pl.pallas_call(kernel, in_specs=list(specs), out_specs=out_specs or [IN_V...  12.3 us
    ppermute x4, waiting for transfers between devices, on_device(): over = lax.ppermute(block if product == 0 else current, axes, plan.over)  6.51 us
    ppermute x8, starting transfers between devices, on_device(): fars = [lax.ppermute(s, axes, route) for s, route in zip(sends, routes)]  4.53 us
    ppermute x4, starting transfers between devices, on_device(): near = lax.ppermute(sends[0] if plan.paired else current, axes, plan.near)  2.59 us
    ppermute x8, waiting for transfers between devices, on_device(): fars = [lax.ppermute(s, axes, route) for s, route in zip(sends, routes)]  1.83 us
  transfers between devices with their start and end apart: 16, of which 7 were waited for; matrix products, arithmetic and copies ran while one was open for 0% of the time, Pallas kernels for 19%

profile of v30, /device:TPU:0, one launch (start us, length us, event | category | flops | bytes accessed | tf_op | source)
XLA Modules:
  0.0 41.2 jit_solution(16209838241513240520)
XLA Ops:
  0.0 0.0 copy-start.1
  0.0 0.0 copy-start
  0.0 1.8 %prepare.1 = (bf16[64,1024]{1,0:T(8,128)(2,1)S(1)}, bf16[1,512,256]{2,1,0:T(8,128)(2,1)S(1)}, bf16[128,1024]{1,0:T(8,128)(2,1)S(1)}, s32[32]{0:T(128)S(4)}, s32[...) custom-call(s32[1]{0:T(128)} %bitcast.index_ref.refs_0_, s32[32]{0:T(128)} %refs_0_.1, s32[32]{0:T(128)} %refs_1_.1, ...), custom_call_target="tpu_custom_call" | custom-call | flops 1000000000 | bytes 4194304 | tf_op jit(solution)/shard_map/prepare/pallas_call | solution.py:256
  1.8 0.5 %collective-permute-start = (bf16[64,1536]{1,0:T(8,128)(2,1)S(1)}, bf16[64,1536]{1,0:T(8,128)(2,1)S(1)}, u32[]{:S(2)}, u32[]{:S(2)}) collective-permute-start(bf16[64,1536]{1,0:T(8,128)(2,1)S(1)} %get-tuple-element.41), channel_id=1, source_target_pairs={{0,1},{1,0},{2,3},{3,2},{4,5},{5,4},{6,7},{7,6},{8,9},{9,8},{10,11... | collective-permute-start | bytes 589832 | tf_op jit(solution)/shard_map/ppermute | solution.py:318
  2.4 5.6 %collective-permute-start.1 = (bf16[64,1024]{1,0:T(8,128)(2,1)}, bf16[64,1024]{1,0:T(8,128)(2,1)S(1)}, u32[]{:S(2)}, u32[]{:S(2)}) collective-permute-start(bf16[64,1024]{1,0:T(8,128)(2,1)} %refs_4_.1), channel_id=1, source_target_pairs={{0,15},{1,2},{2,1},{3,4},{4,3},{5,6},{6,5},{7,8},{8,7},{9,10},{10,... | collective-permute-start | bytes 393224 | tf_op jit(solution)/shard_map/ppermute | solution.py:317
  8.0 0.0 collective-permute-done.message_ref.refs_4_
  8.0 0.1 collective-permute-start.2
  8.1 0.1 collective-permute-start.3
  8.2 0.0 copy-done.1
  8.2 0.0 copy-done
  8.2 1.9 %first_own.1 = (f32[64,1024]{1,0:T(8,128)S(1)}, bf16[36,256,256]{2,1,0:T(8,128)(2,1)S(1)}, bf16[256,1024]{1,0:T(8,128)(2,1)S(1)}) custom-call(s32[1]{0:T(128)} %bitcast.index_ref.refs_0_, s32[32]{0:T(128)S(4)} %get-tuple-element.38.refs_1_, s32[32]{0:T(128)S(4)} %get-tuple-element.39.refs_2_, bf16[64,1024]{1,0:T(8,128)(2,1)S(1)} %get-tuple-element.40.refs_3_, ...), custom_call_target="tpu_custom_call" | custom-call | flops 1000000000 | bytes 4194304 | tf_op jit(solution)/shard_map/first_own/pallas_call | solution.py:256
  10.1 0.9 %collective-permute-done.1.over_ref = bf16[64,1024]{1,0:T(8,128)(2,1)S(1)} collective-permute-done((bf16[64,1024]{1,0:T(8,128)(2,1)}, bf16[64,1024]{1,0:T(8,128)(2,1)S(1)}, u32[]{:S(2)}, u32[]{:S(2)}) %collective-permute-start.1) | collective-permute-done | bytes 131104 | tf_op jit(solution)/shard_map/ppermute | solution.py:317
  10.9 0.5 %halo.4.refs_1_ = f32[64,1024]{1,0:T(8,128)S(1)} custom-call(s32[1]{0:T(128)} %bitcast.index_ref.refs_0_, f32[64,1024]{1,0:T(8,128)S(1)} %get-tuple-element.45.acc_ref, bf16[64,1024]{1,0:T(8,128)(2,1)S(1)} %collective-permute-done.1.over_ref, bf16[36,256,256]{2,1,0:T(8,128)(2,1)S(1)} %get-tuple-element.46.d_ref.refs_3_), custom_call_target="tpu_custom_call" | custom-call | flops 1000000000 | bytes 4194304 | tf_op jit(solution)/shard_map/halo/pallas_call | solution.py:256
  11.5 1.7 %collective-permute-done.2.refs_5_ = bf16[64,128]{1,0:T(8,128)(2,1)S(1)} collective-permute-done((bf16[64,128]{1,0:T(8,128)(2,1)S(1)}, bf16[64,128]{1,0:T(8,128)(2,1)S(1)}, u32[]{:S(2)}, u32[]{:S(2)}) %collective-permute-start.2) | collective-permute-done | bytes 16416 | tf_op jit(solution)/shard_map/ppermute | solution.py:330
  13.1 0.0 collective-permute-done.3.refs_6_
  13.1 0.6 %finish.3 = (bf16[64,1024]{1,0:T(8,128)(2,1)S(1)}, bf16[64,1536]{1,0:T(8,128)(2,1)S(1)}, f32[64,256]{1,0:T(8,128)S(1)}) custom-call(s32[1]{0:T(128)} %bitcast.index_ref.refs_0_, f32[64,1024]{1,0:T(8,128)S(1)} %halo.4.refs_1_, bf16[256,1024]{1,0:T(8,128)(2,1)S(1)} %get-tuple-element.47.refs_2_.refs_1_, bf16[128,1024]{1,0:T(8,128)(2,1)S(1)} %get-tuple-element.48.refs_3_, ...), custom_call_target="tpu_custom_call" | custom-call | flops 1000000000 | bytes 4194304 | tf_op jit(solution)/shard_map/finish/pallas_call | solution.py:256
  13.7 1.1 %collective-permute-start.4 = (bf16[64,1536]{1,0:T(8,128)(2,1)S(1)}, bf16[64,1536]{1,0:T(8,128)(2,1)S(1)}, u32[]{:S(2)}, u32[]{:S(2)}) collective-permute-start(bf16[64,1536]{1,0:T(8,128)(2,1)S(1)} %get-tuple-element.51), channel_id=1, source_target_pairs={{0,1},{1,0},{2,3},{3,2},{4,5},{5,4},{6,7},{7,6},{8,9},{9,8},{10,11... | collective-permute-start | bytes 589832 | tf_op jit(solution)/shard_map/ppermute | solution.py:318
  14.8 2.3 %collective-permute-start.5 = (bf16[64,1024]{1,0:T(8,128)(2,1)S(1)}, bf16[64,1024]{1,0:T(8,128)(2,1)S(1)}, u32[]{:S(2)}, u32[]{:S(2)}) collective-permute-start(bf16[64,1024]{1,0:T(8,128)(2,1)S(1)} %get-tuple-element.50.refs_1_), channel_id=1, source_target_pairs={{0,15},{1,2},{2,1},{3,4},{4,3},{5,6},{6,5},{7,8},{8,7},{9,10},{10,... | collective-permute-start | bytes 393224 | tf_op jit(solution)/shard_map/ppermute | solution.py:317
  17.1 0.0 collective-permute-done.4.message_ref.refs_2_
  17.1 0.3 collective-permute-start.6
  17.4 1.4 %collective-permute-start.7 = (bf16[64,128]{1,0:T(8,128)(2,1)S(1)}, bf16[64,128]{1,0:T(8,128)(2,1)S(1)}, u32[]{:S(2)}, u32[]{:S(2)}) collective-permute-start(bf16[64,128]{1,0:T(8,128)(2,1)S(1)} %get-tuple-element.54.refs_5_), channel_id=1, source_target_pairs={{0,8},{1,11},{2,10},{3,9},{4,12},{5,15},{6,14},{7,13},{8,0},{9,3},... | collective-permute-start | bytes 49160 | tf_op jit(solution)/shard_map/ppermute | solution.py:330
  18.8 1.3 %own.3 = (f32[64,1024]{1,0:T(8,128)S(1)}, bf16[4,64,1024]{2,1,0:T(8,128)(2,1)}) custom-call(s32[1]{0:T(128)} %bitcast.index_ref.refs_0_, bf16[64,1024]{1,0:T(8,128)(2,1)S(1)} %get-tuple-element.50.refs_1_, bf16[64,1536]{1,0:T(8,128)(2,1)S(1)} %collective-permute-done.4.message_ref.refs_2_, bf16[36,256,256]{2,1,0:T(8,128)(2,1)S(1)} %get-tuple-element.46.d_ref.refs_3_, ...), custom_call_target="tpu_custom_call" | custom-call | flops 1000000000 | bytes 4194304 | tf_op jit(solution)/shard_map/own/pallas_call | solution.py:256
  20.1 1.9 %collective-permute-done.5.over_ref = bf16[64,1024]{1,0:T(8,128)(2,1)S(1)} collective-permute-done((bf16[64,1024]{1,0:T(8,128)(2,1)S(1)}, bf16[64,1024]{1,0:T(8,128)(2,1)S(1)}, u32[]{:S(2)}, u32[]{:S(2)}) %collective-permute-start.5) | collective-permute-done | bytes 131104 | tf_op jit(solution)/shard_map/ppermute | solution.py:317
  22.1 0.5 %halo.5.refs_1_ = f32[64,1024]{1,0:T(8,128)S(1)} custom-call(s32[1]{0:T(128)} %bitcast.index_ref.refs_0_, f32[64,1024]{1,0:T(8,128)S(1)} %get-tuple-element.55.acc_ref, bf16[64,1024]{1,0:T(8,128)(2,1)S(1)} %collective-permute-done.5.over_ref, bf16[36,256,256]{2,1,0:T(8,128)(2,1)S(1)} %get-tuple-element.46.d_ref.refs_3_), custom_call_target="tpu_custom_call" | custom-call | flops 1000000000 | bytes 4194304 | tf_op jit(solution)/shard_map/halo/pallas_call | solution.py:256
  22.6 0.0 collective-permute-done.6.refs_5_
  22.6 0.0 collective-permute-done.7.refs_6_
  22.6 0.6 %finish.4 = (bf16[64,1024]{1,0:T(8,128)(2,1)S(1)}, bf16[64,1536]{1,0:T(8,128)(2,1)S(1)}, f32[64,256]{1,0:T(8,128)S(1)}) custom-call(s32[1]{0:T(128)} %bitcast.index_ref.refs_0_, f32[64,1024]{1,0:T(8,128)S(1)} %halo.5.refs_1_, bf16[256,1024]{1,0:T(8,128)(2,1)S(1)} %get-tuple-element.47.refs_2_.refs_1_, bf16[128,1024]{1,0:T(8,128)(2,1)S(1)} %get-tuple-element.48.refs_3_, ...), custom_call_target="tpu_custom_call" | custom-call | flops 1000000000 | bytes 4194304 | tf_op jit(solution)/shard_map/finish/pallas_call | solution.py:256
  23.2 0.3 collective-permute-start.8
  23.5 2.7 %collective-permute-start.9 = (bf16[64,1024]{1,0:T(8,128)(2,1)S(1)}, bf16[64,1024]{1,0:T(8,128)(2,1)S(1)}, u32[]{:S(2)}, u32[]{:S(2)}) collective-permute-start(bf16[64,1024]{1,0:T(8,128)(2,1)S(1)} %get-tuple-element.56.refs_1_), channel_id=1, source_target_pairs={{0,15},{1,2},{2,1},{3,4},{4,3},{5,6},{6,5},{7,8},{8,7},{9,10},{10,... | collective-permute-start | bytes 393224 | tf_op jit(solution)/shard_map/ppermute | solution.py:317
  26.2 0.0 collective-permute-done.8.message_ref.refs_2_
  26.2 0.3 collective-permute-start.10
  26.5 1.0 %collective-permute-start.11 = (bf16[64,128]{1,0:T(8,128)(2,1)S(1)}, bf16[64,128]{1,0:T(8,128)(2,1)S(1)}, u32[]{:S(2)}, u32[]{:S(2)}) collective-permute-start(bf16[64,128]{1,0:T(8,128)(2,1)S(1)} %get-tuple-element.60.refs_5_), channel_id=1, source_target_pairs={{0,8},{1,11},{2,10},{3,9},{4,12},{5,15},{6,14},{7,13},{8,0},{9,3},... | collective-permute-start | bytes 49160 | tf_op jit(solution)/shard_map/ppermute | solution.py:330
  27.5 1.3 %own.4 = (f32[64,1024]{1,0:T(8,128)S(1)}, bf16[4,64,1024]{2,1,0:T(8,128)(2,1)}) custom-call(s32[1]{0:T(128)} %bitcast.index_ref.refs_0_, bf16[64,1024]{1,0:T(8,128)(2,1)S(1)} %get-tuple-element.56.refs_1_, bf16[64,1536]{1,0:T(8,128)(2,1)S(1)} %collective-permute-done.8.message_ref.refs_2_, ...), custom_call_target="tpu_custom_call", output_to_operand_aliasing={{1}: (6, {})} | custom-call | flops 1000000000 | bytes 4194304 | tf_op jit(solution)/shard_map/own/pallas_call | solution.py:256
  28.8 1.8 %collective-permute-done.9.over_ref = bf16[64,1024]{1,0:T(8,128)(2,1)S(1)} collective-permute-done((bf16[64,1024]{1,0:T(8,128)(2,1)S(1)}, bf16[64,1024]{1,0:T(8,128)(2,1)S(1)}, u32[]{:S(2)}, u32[]{:S(2)}) %collective-permute-start.9) | collective-permute-done | bytes 131104 | tf_op jit(solution)/shard_map/ppermute | solution.py:317
  30.7 0.5 %halo.6.refs_1_ = f32[64,1024]{1,0:T(8,128)S(1)} custom-call(s32[1]{0:T(128)} %bitcast.index_ref.refs_0_, f32[64,1024]{1,0:T(8,128)S(1)} %get-tuple-element.62.acc_ref, bf16[64,1024]{1,0:T(8,128)(2,1)S(1)} %collective-permute-done.9.over_ref, bf16[36,256,256]{2,1,0:T(8,128)(2,1)S(1)} %get-tuple-element.46.d_ref.refs_3_), custom_call_target="tpu_custom_call" | custom-call | flops 1000000000 | bytes 4194304 | tf_op jit(solution)/shard_map/halo/pallas_call | solution.py:256
  31.2 0.1 collective-permute-done.10.refs_5_
  31.3 0.0 collective-permute-done.11.refs_6_
  31.3 0.6 %finish.5 = (bf16[64,1024]{1,0:T(8,128)(2,1)S(1)}, bf16[64,1536]{1,0:T(8,128)(2,1)S(1)}, f32[64,256]{1,0:T(8,128)S(1)}) custom-call(s32[1]{0:T(128)} %bitcast.index_ref.refs_0_, f32[64,1024]{1,0:T(8,128)S(1)} %halo.6.refs_1_, bf16[256,1024]{1,0:T(8,128)(2,1)S(1)} %get-tuple-element.47.refs_2_.refs_1_, bf16[128,1024]{1,0:T(8,128)(2,1)S(1)} %get-tuple-element.48.refs_3_, ...), custom_call_target="tpu_custom_call" | custom-call | flops 1000000000 | bytes 4194304 | tf_op jit(solution)/shard_map/finish/pallas_call | solution.py:256
  31.9 0.7 %collective-permute-start.12 = (bf16[64,1536]{1,0:T(8,128)(2,1)S(1)}, bf16[64,1536]{1,0:T(8,128)(2,1)S(1)}, u32[]{:S(2)}, u32[]{:S(2)}) collective-permute-start(bf16[64,1536]{1,0:T(8,128)(2,1)S(1)} %get-tuple-element.64), channel_id=1, source_target_pairs={{0,1},{1,0},{2,3},{3,2},{4,5},{5,4},{6,7},{7,6},{8,9},{9,8},{10,11... | collective-permute-start | bytes 589832 | tf_op jit(solution)/shard_map/ppermute | solution.py:318
  32.6 2.7 %collective-permute-start.13 = (bf16[64,1024]{1,0:T(8,128)(2,1)S(1)}, bf16[64,1024]{1,0:T(8,128)(2,1)S(1)}, u32[]{:S(2)}, u32[]{:S(2)}) collective-permute-start(bf16[64,1024]{1,0:T(8,128)(2,1)S(1)} %get-tuple-element.63.refs_1_), channel_id=1, source_target_pairs={{0,15},{1,2},{2,1},{3,4},{4,3},{5,6},{6,5},{7,8},{8,7},{9,10},{10,... | collective-permute-start | bytes 393224 | tf_op jit(solution)/shard_map/ppermute | solution.py:317
  35.3 0.0 collective-permute-done.12.message_ref.refs_2_
  35.3 0.3 collective-permute-start.14
  35.6 1.0 %collective-permute-start.15 = (bf16[64,128]{1,0:T(8,128)(2,1)S(1)}, bf16[64,128]{1,0:T(8,128)(2,1)S(1)}, u32[]{:S(2)}, u32[]{:S(2)}) collective-permute-start(bf16[64,128]{1,0:T(8,128)(2,1)S(1)} %get-tuple-element.67.refs_5_), channel_id=1, source_target_pairs={{0,8},{1,11},{2,10},{3,9},{4,12},{5,15},{6,14},{7,13},{8,0},{9,3},... | collective-permute-start | bytes 49160 | tf_op jit(solution)/shard_map/ppermute | solution.py:330
  36.6 1.3 %own.5 = (f32[64,1024]{1,0:T(8,128)S(1)}, bf16[4,64,1024]{2,1,0:T(8,128)(2,1)}) custom-call(s32[1]{0:T(128)} %bitcast.index_ref.refs_0_, bf16[64,1024]{1,0:T(8,128)(2,1)S(1)} %get-tuple-element.63.refs_1_, bf16[64,1536]{1,0:T(8,128)(2,1)S(1)} %collective-permute-done.12.message_ref.refs_2_, ...), custom_call_target="tpu_custom_call", output_to_operand_aliasing={{1}: (6, {})} | custom-call | flops 1000000000 | bytes 4194304 | tf_op jit(solution)/shard_map/own/pallas_call | solution.py:256
  37.9 1.9 %collective-permute-done.13.over_ref = bf16[64,1024]{1,0:T(8,128)(2,1)S(1)} collective-permute-done((bf16[64,1024]{1,0:T(8,128)(2,1)S(1)}, bf16[64,1024]{1,0:T(8,128)(2,1)S(1)}, u32[]{:S(2)}, u32[]{:S(2)}) %collective-permute-start.13) | collective-permute-done | bytes 131104 | tf_op jit(solution)/shard_map/ppermute | solution.py:317
  39.8 0.5 %halo.7.refs_0_ = f32[64,1024]{1,0:T(8,128)S(1)} custom-call(s32[1]{0:T(128)} %bitcast.index_ref.refs_0_, f32[64,1024]{1,0:T(8,128)S(1)} %get-tuple-element.69.acc_ref, bf16[64,1024]{1,0:T(8,128)(2,1)S(1)} %collective-permute-done.13.over_ref, bf16[36,256,256]{2,1,0:T(8,128)(2,1)S(1)} %get-tuple-element.46.d_ref.refs_3_), custom_call_target="tpu_custom_call" | custom-call | flops 1000000000 | bytes 4194304 | tf_op jit(solution)/shard_map/halo/pallas_call | solution.py:256
  40.3 0.1 collective-permute-done.14.refs_2_
  40.4 0.0 collective-permute-done.15.refs_3_
  40.4 0.9 %last.1 = bf16[4,64,1024]{2,1,0:T(8,128)(2,1)} custom-call(f32[64,1024]{1,0:T(8,128)S(1)} %halo.7.refs_0_, bf16[256,1024]{1,0:T(8,128)(2,1)S(1)} %get-tuple-element.47.refs_2_.refs_1_, bf16[64,128]{1,0:T(8,128)(2,1)S(1)} %collective-permute-done.14.refs_2_, bf16[64,128]{1,0:T(8,128)(2,1)S(1)} %collective-permute-done.15.refs_3_, ...), custom_call_target="tpu_custom_call", output_to_operand_aliasing={{}: (4, {})} | custom-call | flops 1000000000 | bytes 4194304 | tf_op jit(solution)/shard_map/last/pallas_call | solution.py:256
  (4 shorter events, 0.1 us)
Async XLA Ops:
  0.0 8.2 %copy-start.1 = (bf16[4,32,256]{2,1,0:T(8,128)(2,1)S(1)}, bf16[4,32,256]{2,1,0:T(8,128)(2,1)}, u32[]{:S(2)}) copy-start(bf16[4,32,256]{2,1,0:T(8,128)(2,1)} %refs_5_.3) | copy-start | bytes 196612
  0.0 8.2 %copy-start = (bf16[32,256,256]{2,1,0:T(8,128)(2,1)S(1)}, bf16[32,256,256]{2,1,0:T(8,128)(2,1)}, u32[]{:S(2)}) copy-start(bf16[32,256,256]{2,1,0:T(8,128)(2,1)} %refs_6_.3) | copy-start | bytes 12582916
  1.8 6.2 %collective-permute-start = (bf16[64,1536]{1,0:T(8,128)(2,1)S(1)}, bf16[64,1536]{1,0:T(8,128)(2,1)S(1)}, u32[]{:S(2)}, u32[]{:S(2)}) collective-permute-start(bf16[64,1536]{1,0:T(8,128)(2,1)S(1)} %get-tuple-element.41), channel_id=1, source_target_pairs={{0,1},{1,0},{2,3},{3,2},{4,5},{5,4},{6,7},{7,6},{8,9},{9,8},{10,11... | collective-permute-start | bytes 589832 | tf_op jit(solution)/shard_map/ppermute | solution.py:318
  2.4 8.6 %collective-permute-start.1 = (bf16[64,1024]{1,0:T(8,128)(2,1)}, bf16[64,1024]{1,0:T(8,128)(2,1)S(1)}, u32[]{:S(2)}, u32[]{:S(2)}) collective-permute-start(bf16[64,1024]{1,0:T(8,128)(2,1)} %refs_4_.1), channel_id=1, source_target_pairs={{0,15},{1,2},{2,1},{3,4},{4,3},{5,6},{6,5},{7,8},{8,7},{9,10},{10,... | collective-permute-start | bytes 393224 | tf_op jit(solution)/shard_map/ppermute | solution.py:317
  8.0 5.1 %collective-permute-start.2 = (bf16[64,128]{1,0:T(8,128)(2,1)S(1)}, bf16[64,128]{1,0:T(8,128)(2,1)S(1)}, u32[]{:S(2)}, u32[]{:S(2)}) collective-permute-start(bf16[64,128]{1,0:T(8,128)(2,1)S(1)} %get-tuple-element.43.refs_7_), channel_id=1, source_target_pairs={{0,9},{1,10},{2,11},{3,8},{4,13},{5,14},{6,15},{7,12},{8,1},{9,2},... | collective-permute-start | bytes 49160 | tf_op jit(solution)/shard_map/ppermute | solution.py:330
  8.1 5.0 %collective-permute-start.3 = (bf16[64,128]{1,0:T(8,128)(2,1)S(1)}, bf16[64,128]{1,0:T(8,128)(2,1)S(1)}, u32[]{:S(2)}, u32[]{:S(2)}) collective-permute-start(bf16[64,128]{1,0:T(8,128)(2,1)S(1)} %get-tuple-element.44.refs_8_), channel_id=1, source_target_pairs={{0,8},{1,11},{2,10},{3,9},{4,12},{5,15},{6,14},{7,13},{8,0},{9,3},... | collective-permute-start | bytes 49160 | tf_op jit(solution)/shard_map/ppermute | solution.py:330
  13.7 3.4 %collective-permute-start.4 = (bf16[64,1536]{1,0:T(8,128)(2,1)S(1)}, bf16[64,1536]{1,0:T(8,128)(2,1)S(1)}, u32[]{:S(2)}, u32[]{:S(2)}) collective-permute-start(bf16[64,1536]{1,0:T(8,128)(2,1)S(1)} %get-tuple-element.51), channel_id=1, source_target_pairs={{0,1},{1,0},{2,3},{3,2},{4,5},{5,4},{6,7},{7,6},{8,9},{9,8},{10,11... | collective-permute-start | bytes 589832 | tf_op jit(solution)/shard_map/ppermute | solution.py:318
  14.8 7.3 %collective-permute-start.5 = (bf16[64,1024]{1,0:T(8,128)(2,1)S(1)}, bf16[64,1024]{1,0:T(8,128)(2,1)S(1)}, u32[]{:S(2)}, u32[]{:S(2)}) collective-permute-start(bf16[64,1024]{1,0:T(8,128)(2,1)S(1)} %get-tuple-element.50.refs_1_), channel_id=1, source_target_pairs={{0,15},{1,2},{2,1},{3,4},{4,3},{5,6},{6,5},{7,8},{8,7},{9,10},{10,... | collective-permute-start | bytes 393224 | tf_op jit(solution)/shard_map/ppermute | solution.py:317
  17.1 5.5 %collective-permute-start.6 = (bf16[64,128]{1,0:T(8,128)(2,1)S(1)}, bf16[64,128]{1,0:T(8,128)(2,1)S(1)}, u32[]{:S(2)}, u32[]{:S(2)}) collective-permute-start(bf16[64,128]{1,0:T(8,128)(2,1)S(1)} %get-tuple-element.53.refs_4_), channel_id=1, source_target_pairs={{0,9},{1,10},{2,11},{3,8},{4,13},{5,14},{6,15},{7,12},{8,1},{9,2},... | collective-permute-start | bytes 49160 | tf_op jit(solution)/shard_map/ppermute | solution.py:330
  17.4 5.2 %collective-permute-start.7 = (bf16[64,128]{1,0:T(8,128)(2,1)S(1)}, bf16[64,128]{1,0:T(8,128)(2,1)S(1)}, u32[]{:S(2)}, u32[]{:S(2)}) collective-permute-start(bf16[64,128]{1,0:T(8,128)(2,1)S(1)} %get-tuple-element.54.refs_5_), channel_id=1, source_target_pairs={{0,8},{1,11},{2,10},{3,9},{4,12},{5,15},{6,14},{7,13},{8,0},{9,3},... | collective-permute-start | bytes 49160 | tf_op jit(solution)/shard_map/ppermute | solution.py:330
  23.2 3.0 %collective-permute-start.8 = (bf16[64,1536]{1,0:T(8,128)(2,1)S(1)}, bf16[64,1536]{1,0:T(8,128)(2,1)S(1)}, u32[]{:S(2)}, u32[]{:S(2)}) collective-permute-start(bf16[64,1536]{1,0:T(8,128)(2,1)S(1)} %get-tuple-element.57), channel_id=1, source_target_pairs={{0,1},{1,0},{2,3},{3,2},{4,5},{5,4},{6,7},{7,6},{8,9},{9,8},{10,11... | collective-permute-start | bytes 589832 | tf_op jit(solution)/shard_map/ppermute | solution.py:318
  23.5 7.2 %collective-permute-start.9 = (bf16[64,1024]{1,0:T(8,128)(2,1)S(1)}, bf16[64,1024]{1,0:T(8,128)(2,1)S(1)}, u32[]{:S(2)}, u32[]{:S(2)}) collective-permute-start(bf16[64,1024]{1,0:T(8,128)(2,1)S(1)} %get-tuple-element.56.refs_1_), channel_id=1, source_target_pairs={{0,15},{1,2},{2,1},{3,4},{4,3},{5,6},{6,5},{7,8},{8,7},{9,10},{10,... | collective-permute-start | bytes 393224 | tf_op jit(solution)/shard_map/ppermute | solution.py:317
  26.2 5.1 %collective-permute-start.10 = (bf16[64,128]{1,0:T(8,128)(2,1)S(1)}, bf16[64,128]{1,0:T(8,128)(2,1)S(1)}, u32[]{:S(2)}, u32[]{:S(2)}) collective-permute-start(bf16[64,128]{1,0:T(8,128)(2,1)S(1)} %get-tuple-element.59.refs_4_), channel_id=1, source_target_pairs={{0,9},{1,10},{2,11},{3,8},{4,13},{5,14},{6,15},{7,12},{8,1},{9,2},... | collective-permute-start | bytes 49160 | tf_op jit(solution)/shard_map/ppermute | solution.py:330
  26.5 4.8 %collective-permute-start.11 = (bf16[64,128]{1,0:T(8,128)(2,1)S(1)}, bf16[64,128]{1,0:T(8,128)(2,1)S(1)}, u32[]{:S(2)}, u32[]{:S(2)}) collective-permute-start(bf16[64,128]{1,0:T(8,128)(2,1)S(1)} %get-tuple-element.60.refs_5_), channel_id=1, source_target_pairs={{0,8},{1,11},{2,10},{3,9},{4,12},{5,15},{6,14},{7,13},{8,0},{9,3},... | collective-permute-start | bytes 49160 | tf_op jit(solution)/shard_map/ppermute | solution.py:330
  31.9 3.4 %collective-permute-start.12 = (bf16[64,1536]{1,0:T(8,128)(2,1)S(1)}, bf16[64,1536]{1,0:T(8,128)(2,1)S(1)}, u32[]{:S(2)}, u32[]{:S(2)}) collective-permute-start(bf16[64,1536]{1,0:T(8,128)(2,1)S(1)} %get-tuple-element.64), channel_id=1, source_target_pairs={{0,1},{1,0},{2,3},{3,2},{4,5},{5,4},{6,7},{7,6},{8,9},{9,8},{10,11... | collective-permute-start | bytes 589832 | tf_op jit(solution)/shard_map/ppermute | solution.py:318
  32.6 7.2 %collective-permute-start.13 = (bf16[64,1024]{1,0:T(8,128)(2,1)S(1)}, bf16[64,1024]{1,0:T(8,128)(2,1)S(1)}, u32[]{:S(2)}, u32[]{:S(2)}) collective-permute-start(bf16[64,1024]{1,0:T(8,128)(2,1)S(1)} %get-tuple-element.63.refs_1_), channel_id=1, source_target_pairs={{0,15},{1,2},{2,1},{3,4},{4,3},{5,6},{6,5},{7,8},{8,7},{9,10},{10,... | collective-permute-start | bytes 393224 | tf_op jit(solution)/shard_map/ppermute | solution.py:317
  35.3 5.1 %collective-permute-start.14 = (bf16[64,128]{1,0:T(8,128)(2,1)S(1)}, bf16[64,128]{1,0:T(8,128)(2,1)S(1)}, u32[]{:S(2)}, u32[]{:S(2)}) collective-permute-start(bf16[64,128]{1,0:T(8,128)(2,1)S(1)} %get-tuple-element.66.refs_4_), channel_id=1, source_target_pairs={{0,9},{1,10},{2,11},{3,8},{4,13},{5,14},{6,15},{7,12},{8,1},{9,2},... | collective-permute-start | bytes 49160 | tf_op jit(solution)/shard_map/ppermute | solution.py:330
  35.6 4.8 %collective-permute-start.15 = (bf16[64,128]{1,0:T(8,128)(2,1)S(1)}, bf16[64,128]{1,0:T(8,128)(2,1)S(1)}, u32[]{:S(2)}, u32[]{:S(2)}) collective-permute-start(bf16[64,128]{1,0:T(8,128)(2,1)S(1)} %get-tuple-element.67.refs_5_), channel_id=1, source_target_pairs={{0,8},{1,11},{2,10},{3,9},{4,12},{5,15},{6,14},{7,13},{8,0},{9,3},... | collective-permute-start | bytes 49160 | tf_op jit(solution)/shard_map/ppermute | solution.py:330

commit v31 on v30

--- a/solution.py
+++ b/solution.py
@@ -11,7 +11,7 @@
 REACH = 4
 LEVELS = 3
 SPAN = 2 * REACH + 1
-OTHER_CORE_FIRST = 0b11110111
+OTHER_CORE_FIRST = 0b11100111
 
 F32 = jnp.float32
 BF16 = jnp.bfloat16

time: 41.6 us -> 41.7 us (level)
    ppermute x8, waiting for transfers between devices: 1.83 us -> 2.61 us  [on_device(): fars = [lax.ppermute(s, axes, route) for s, route in zip(sends, routes)]]
    ppermute x8, starting transfers between devices: 4.53 us -> 5.1 us  [on_device(): fars = [lax.ppermute(s, axes, route) for s, route in zip(sends, routes)]]
    ppermute x4, waiting for transfers between devices: 6.51 us -> 5.97 us  [on_device(): over = lax.ppermute(block if product == 0 else current, axes, plan.over)]
    ppermute x4, starting transfers between devices: 2.59 us -> 2.08 us  [on_device(): near = lax.ppermute(sends[0] if plan.paired else current, axes, plan.near)]
  transfers between devices with their start and end apart: 16 -> 16, of which waited for: 7 -> 9; matrix products, arithmetic and copies ran while one was open for 0% -> 0% of each run, Pallas kernels for 19% -> 19%
where the time goes in v31:
time: 41.7 us; the launch traced here: 41.5 us
  starting transfers between devices  20.5 us (49%)
  Pallas kernels  12.3 us (29%)
  waiting for transfers between devices  8.6 us (21%)
    ppermute x4, starting transfers between devices, on_device(): over = lax.ppermute(block if product == 0 else current, axes, plan.over)  13.3 us
    pallas_call x17, Pallas kernels, call(): pl.pallas_call(kernel, in_specs=list(specs), out_specs=out_specs or [IN_V...  12.3 us
    ppermute x4, waiting for transfers between devices, on_device(): over = lax.ppermute(block if product == 0 else current, axes, plan.over)  5.97 us
    ppermute x8, starting transfers between devices, on_device(): fars = [lax.ppermute(s, axes, route) for s, route in zip(sends, routes)]  5.1 us
    ppermute x8, waiting for transfers between devices, on_device(): fars = [lax.ppermute(s, axes, route) for s, route in zip(sends, routes)]  2.61 us
    ppermute x4, starting transfers between devices, on_device(): near = lax.ppermute(sends[0] if plan.paired else current, axes, plan.near)  2.08 us
  transfers between devices with their start and end apart: 16, of which 9 were waited for; matrix products, arithmetic and copies ran while one was open for 0% of the time, Pallas kernels for 19%

profile of v31, /device:TPU:0, one launch (start us, length us, event | category | flops | bytes accessed | tf_op | source)
XLA Modules:
  0.0 41.5 jit_solution(14966100480980037003)
XLA Ops:
  0.0 0.0 copy-start.1
  0.0 0.0 copy-start
  0.0 1.8 %prepare.1 = (bf16[64,1024]{1,0:T(8,128)(2,1)S(1)}, bf16[1,512,256]{2,1,0:T(8,128)(2,1)S(1)}, bf16[128,1024]{1,0:T(8,128)(2,1)S(1)}, s32[32]{0:T(128)S(4)}, s32[...) custom-call(s32[1]{0:T(128)} %bitcast.index_ref.refs_0_, s32[32]{0:T(128)} %refs_0_.1, s32[32]{0:T(128)} %refs_1_.1, ...), custom_call_target="tpu_custom_call" | custom-call | flops 1000000000 | bytes 4194304 | tf_op jit(solution)/shard_map/prepare/pallas_call | solution.py:256
  1.8 0.5 %collective-permute-start = (bf16[64,1536]{1,0:T(8,128)(2,1)S(1)}, bf16[64,1536]{1,0:T(8,128)(2,1)S(1)}, u32[]{:S(2)}, u32[]{:S(2)}) collective-permute-start(bf16[64,1536]{1,0:T(8,128)(2,1)S(1)} %get-tuple-element.41), channel_id=1, source_target_pairs={{0,1},{1,0},{2,3},{3,2},{4,5},{5,4},{6,7},{7,6},{8,9},{9,8},{10,11... | collective-permute-start | bytes 589832 | tf_op jit(solution)/shard_map/ppermute | solution.py:318
  2.4 5.6 %collective-permute-start.1 = (bf16[64,1024]{1,0:T(8,128)(2,1)}, bf16[64,1024]{1,0:T(8,128)(2,1)S(1)}, u32[]{:S(2)}, u32[]{:S(2)}) collective-permute-start(bf16[64,1024]{1,0:T(8,128)(2,1)} %refs_4_.1), channel_id=1, source_target_pairs={{0,15},{1,2},{2,1},{3,4},{4,3},{5,6},{6,5},{7,8},{8,7},{9,10},{10,... | collective-permute-start | bytes 393224 | tf_op jit(solution)/shard_map/ppermute | solution.py:317
  8.0 0.0 collective-permute-done.message_ref.refs_4_
  8.0 0.1 collective-permute-start.2
  8.1 0.4 collective-permute-start.3
  8.5 0.0 copy-done.1
  8.5 0.0 copy-done
  8.5 1.9 %first_own.1 = (f32[64,1024]{1,0:T(8,128)S(1)}, bf16[36,256,256]{2,1,0:T(8,128)(2,1)S(1)}, bf16[256,1024]{1,0:T(8,128)(2,1)S(1)}) custom-call(s32[1]{0:T(128)} %bitcast.index_ref.refs_0_, s32[32]{0:T(128)S(4)} %get-tuple-element.38.refs_1_, s32[32]{0:T(128)S(4)} %get-tuple-element.39.refs_2_, bf16[64,1024]{1,0:T(8,128)(2,1)S(1)} %get-tuple-element.40.refs_3_, ...), custom_call_target="tpu_custom_call" | custom-call | flops 1000000000 | bytes 4194304 | tf_op jit(solution)/shard_map/first_own/pallas_call | solution.py:256
  10.3 0.6 %collective-permute-done.1.over_ref = bf16[64,1024]{1,0:T(8,128)(2,1)S(1)} collective-permute-done((bf16[64,1024]{1,0:T(8,128)(2,1)}, bf16[64,1024]{1,0:T(8,128)(2,1)S(1)}, u32[]{:S(2)}, u32[]{:S(2)}) %collective-permute-start.1) | collective-permute-done | bytes 131104 | tf_op jit(solution)/shard_map/ppermute | solution.py:317
  10.9 0.5 %halo.4.refs_1_ = f32[64,1024]{1,0:T(8,128)S(1)} custom-call(s32[1]{0:T(128)} %bitcast.index_ref.refs_0_, f32[64,1024]{1,0:T(8,128)S(1)} %get-tuple-element.45.acc_ref, bf16[64,1024]{1,0:T(8,128)(2,1)S(1)} %collective-permute-done.1.over_ref, bf16[36,256,256]{2,1,0:T(8,128)(2,1)S(1)} %get-tuple-element.46.d_ref.refs_3_), custom_call_target="tpu_custom_call" | custom-call | flops 1000000000 | bytes 4194304 | tf_op jit(solution)/shard_map/halo/pallas_call | solution.py:256
  11.5 1.7 %collective-permute-done.2.refs_5_ = bf16[64,128]{1,0:T(8,128)(2,1)S(1)} collective-permute-done((bf16[64,128]{1,0:T(8,128)(2,1)S(1)}, bf16[64,128]{1,0:T(8,128)(2,1)S(1)}, u32[]{:S(2)}, u32[]{:S(2)}) %collective-permute-start.2) | collective-permute-done | bytes 16416 | tf_op jit(solution)/shard_map/ppermute | solution.py:330
  13.1 0.0 collective-permute-done.3.refs_6_
  13.1 0.6 %finish.3 = (bf16[64,1024]{1,0:T(8,128)(2,1)S(1)}, bf16[64,1536]{1,0:T(8,128)(2,1)S(1)}, f32[64,256]{1,0:T(8,128)S(1)}) custom-call(s32[1]{0:T(128)} %bitcast.index_ref.refs_0_, f32[64,1024]{1,0:T(8,128)S(1)} %halo.4.refs_1_, bf16[256,1024]{1,0:T(8,128)(2,1)S(1)} %get-tuple-element.47.refs_2_.refs_1_, bf16[128,1024]{1,0:T(8,128)(2,1)S(1)} %get-tuple-element.48.refs_3_, ...), custom_call_target="tpu_custom_call" | custom-call | flops 1000000000 | bytes 4194304 | tf_op jit(solution)/shard_map/finish/pallas_call | solution.py:256
  13.7 1.1 %collective-permute-start.4 = (bf16[64,1536]{1,0:T(8,128)(2,1)S(1)}, bf16[64,1536]{1,0:T(8,128)(2,1)S(1)}, u32[]{:S(2)}, u32[]{:S(2)}) collective-permute-start(bf16[64,1536]{1,0:T(8,128)(2,1)S(1)} %get-tuple-element.51), channel_id=1, source_target_pairs={{0,1},{1,0},{2,3},{3,2},{4,5},{5,4},{6,7},{7,6},{8,9},{9,8},{10,11... | collective-permute-start | bytes 589832 | tf_op jit(solution)/shard_map/ppermute | solution.py:318
  14.8 2.3 %collective-permute-start.5 = (bf16[64,1024]{1,0:T(8,128)(2,1)S(1)}, bf16[64,1024]{1,0:T(8,128)(2,1)S(1)}, u32[]{:S(2)}, u32[]{:S(2)}) collective-permute-start(bf16[64,1024]{1,0:T(8,128)(2,1)S(1)} %get-tuple-element.50.refs_1_), channel_id=1, source_target_pairs={{0,15},{1,2},{2,1},{3,4},{4,3},{5,6},{6,5},{7,8},{8,7},{9,10},{10,... | collective-permute-start | bytes 393224 | tf_op jit(solution)/shard_map/ppermute | solution.py:317
  17.1 0.0 collective-permute-done.4.message_ref.refs_2_
  17.1 0.1 collective-permute-start.6
  17.2 1.5 %collective-permute-start.7 = (bf16[64,128]{1,0:T(8,128)(2,1)S(1)}, bf16[64,128]{1,0:T(8,128)(2,1)S(1)}, u32[]{:S(2)}, u32[]{:S(2)}) collective-permute-start(bf16[64,128]{1,0:T(8,128)(2,1)S(1)} %get-tuple-element.54.refs_5_), channel_id=1, source_target_pairs={{0,9},{1,11},{2,10},{3,8},{4,12},{5,15},{6,14},{7,13},{8,0},{9,3},... | collective-permute-start | bytes 49160 | tf_op jit(solution)/shard_map/ppermute | solution.py:330
  18.7 1.3 %own.3 = (f32[64,1024]{1,0:T(8,128)S(1)}, bf16[4,64,1024]{2,1,0:T(8,128)(2,1)}) custom-call(s32[1]{0:T(128)} %bitcast.index_ref.refs_0_, bf16[64,1024]{1,0:T(8,128)(2,1)S(1)} %get-tuple-element.50.refs_1_, bf16[64,1536]{1,0:T(8,128)(2,1)S(1)} %collective-permute-done.4.message_ref.refs_2_, bf16[36,256,256]{2,1,0:T(8,128)(2,1)S(1)} %get-tuple-element.46.d_ref.refs_3_, ...), custom_call_target="tpu_custom_call" | custom-call | flops 1000000000 | bytes 4194304 | tf_op jit(solution)/shard_map/own/pallas_call | solution.py:256
  20.0 2.1 %collective-permute-done.5.over_ref = bf16[64,1024]{1,0:T(8,128)(2,1)S(1)} collective-permute-done((bf16[64,1024]{1,0:T(8,128)(2,1)S(1)}, bf16[64,1024]{1,0:T(8,128)(2,1)S(1)}, u32[]{:S(2)}, u32[]{:S(2)}) %collective-permute-start.5) | collective-permute-done | bytes 131104 | tf_op jit(solution)/shard_map/ppermute | solution.py:317
  22.1 0.5 %halo.5.refs_1_ = f32[64,1024]{1,0:T(8,128)S(1)} custom-call(s32[1]{0:T(128)} %bitcast.index_ref.refs_0_, f32[64,1024]{1,0:T(8,128)S(1)} %get-tuple-element.55.acc_ref, bf16[64,1024]{1,0:T(8,128)(2,1)S(1)} %collective-permute-done.5.over_ref, bf16[36,256,256]{2,1,0:T(8,128)(2,1)S(1)} %get-tuple-element.46.d_ref.refs_3_), custom_call_target="tpu_custom_call" | custom-call | flops 1000000000 | bytes 4194304 | tf_op jit(solution)/shard_map/halo/pallas_call | solution.py:256
  22.6 0.0 collective-permute-done.6.refs_5_
  22.6 0.0 collective-permute-done.7.refs_6_
  22.6 0.6 %finish.4 = (bf16[64,1024]{1,0:T(8,128)(2,1)S(1)}, bf16[64,1536]{1,0:T(8,128)(2,1)S(1)}, f32[64,256]{1,0:T(8,128)S(1)}) custom-call(s32[1]{0:T(128)} %bitcast.index_ref.refs_0_, f32[64,1024]{1,0:T(8,128)S(1)} %halo.5.refs_1_, bf16[256,1024]{1,0:T(8,128)(2,1)S(1)} %get-tuple-element.47.refs_2_.refs_1_, bf16[128,1024]{1,0:T(8,128)(2,1)S(1)} %get-tuple-element.48.refs_3_, ...), custom_call_target="tpu_custom_call" | custom-call | flops 1000000000 | bytes 4194304 | tf_op jit(solution)/shard_map/finish/pallas_call | solution.py:256
  23.2 0.3 collective-permute-start.8
  23.5 2.7 %collective-permute-start.9 = (bf16[64,1024]{1,0:T(8,128)(2,1)S(1)}, bf16[64,1024]{1,0:T(8,128)(2,1)S(1)}, u32[]{:S(2)}, u32[]{:S(2)}) collective-permute-start(bf16[64,1024]{1,0:T(8,128)(2,1)S(1)} %get-tuple-element.56.refs_1_), channel_id=1, source_target_pairs={{0,15},{1,2},{2,1},{3,4},{4,3},{5,6},{6,5},{7,8},{8,7},{9,10},{10,... | collective-permute-start | bytes 393224 | tf_op jit(solution)/shard_map/ppermute | solution.py:317
  26.2 0.0 collective-permute-done.8.message_ref.refs_2_
  26.2 1.0 %collective-permute-start.10 = (bf16[64,128]{1,0:T(8,128)(2,1)S(1)}, bf16[64,128]{1,0:T(8,128)(2,1)S(1)}, u32[]{:S(2)}, u32[]{:S(2)}) collective-permute-start(bf16[64,128]{1,0:T(8,128)(2,1)S(1)} %get-tuple-element.59.refs_4_), channel_id=1, source_target_pairs={{0,8},{1,10},{2,11},{3,9},{4,13},{5,14},{6,15},{7,12},{8,1},{9,2},... | collective-permute-start | bytes 49160 | tf_op jit(solution)/shard_map/ppermute | solution.py:330
  27.2 0.6 %collective-permute-start.11 = (bf16[64,128]{1,0:T(8,128)(2,1)S(1)}, bf16[64,128]{1,0:T(8,128)(2,1)S(1)}, u32[]{:S(2)}, u32[]{:S(2)}) collective-permute-start(bf16[64,128]{1,0:T(8,128)(2,1)S(1)} %get-tuple-element.60.refs_5_), channel_id=1, source_target_pairs={{0,9},{1,11},{2,10},{3,8},{4,12},{5,15},{6,14},{7,13},{8,0},{9,3},... | collective-permute-start | bytes 49160 | tf_op jit(solution)/shard_map/ppermute | solution.py:330
  27.8 1.3 %own.4 = (f32[64,1024]{1,0:T(8,128)S(1)}, bf16[4,64,1024]{2,1,0:T(8,128)(2,1)}) custom-call(s32[1]{0:T(128)} %bitcast.index_ref.refs_0_, bf16[64,1024]{1,0:T(8,128)(2,1)S(1)} %get-tuple-element.56.refs_1_, bf16[64,1536]{1,0:T(8,128)(2,1)S(1)} %collective-permute-done.8.message_ref.refs_2_, ...), custom_call_target="tpu_custom_call", output_to_operand_aliasing={{1}: (6, {})} | custom-call | flops 1000000000 | bytes 4194304 | tf_op jit(solution)/shard_map/own/pallas_call | solution.py:256
  29.1 1.6 %collective-permute-done.9.over_ref = bf16[64,1024]{1,0:T(8,128)(2,1)S(1)} collective-permute-done((bf16[64,1024]{1,0:T(8,128)(2,1)S(1)}, bf16[64,1024]{1,0:T(8,128)(2,1)S(1)}, u32[]{:S(2)}, u32[]{:S(2)}) %collective-permute-start.9) | collective-permute-done | bytes 131104 | tf_op jit(solution)/shard_map/ppermute | solution.py:317
  30.7 0.5 %halo.6.refs_1_ = f32[64,1024]{1,0:T(8,128)S(1)} custom-call(s32[1]{0:T(128)} %bitcast.index_ref.refs_0_, f32[64,1024]{1,0:T(8,128)S(1)} %get-tuple-element.62.acc_ref, bf16[64,1024]{1,0:T(8,128)(2,1)S(1)} %collective-permute-done.9.over_ref, bf16[36,256,256]{2,1,0:T(8,128)(2,1)S(1)} %get-tuple-element.46.d_ref.refs_3_), custom_call_target="tpu_custom_call" | custom-call | flops 1000000000 | bytes 4194304 | tf_op jit(solution)/shard_map/halo/pallas_call | solution.py:256
  31.2 0.1 collective-permute-done.10.refs_5_
  31.3 0.5 %collective-permute-done.11.refs_6_ = bf16[64,128]{1,0:T(8,128)(2,1)S(1)} collective-permute-done((bf16[64,128]{1,0:T(8,128)(2,1)S(1)}, bf16[64,128]{1,0:T(8,128)(2,1)S(1)}, u32[]{:S(2)}, u32[]{:S(2)}) %collective-permute-start.11) | collective-permute-done | bytes 16416 | tf_op jit(solution)/shard_map/ppermute | solution.py:330
  31.8 0.6 %finish.5 = (bf16[64,1024]{1,0:T(8,128)(2,1)S(1)}, bf16[64,1536]{1,0:T(8,128)(2,1)S(1)}, f32[64,256]{1,0:T(8,128)S(1)}) custom-call(s32[1]{0:T(128)} %bitcast.index_ref.refs_0_, f32[64,1024]{1,0:T(8,128)S(1)} %halo.6.refs_1_, bf16[256,1024]{1,0:T(8,128)(2,1)S(1)} %get-tuple-element.47.refs_2_.refs_1_, bf16[128,1024]{1,0:T(8,128)(2,1)S(1)} %get-tuple-element.48.refs_3_, ...), custom_call_target="tpu_custom_call" | custom-call | flops 1000000000 | bytes 4194304 | tf_op jit(solution)/shard_map/finish/pallas_call | solution.py:256
  32.4 0.2 collective-permute-start.12
  32.6 2.7 %collective-permute-start.13 = (bf16[64,1024]{1,0:T(8,128)(2,1)S(1)}, bf16[64,1024]{1,0:T(8,128)(2,1)S(1)}, u32[]{:S(2)}, u32[]{:S(2)}) collective-permute-start(bf16[64,1024]{1,0:T(8,128)(2,1)S(1)} %get-tuple-element.63.refs_1_), channel_id=1, source_target_pairs={{0,15},{1,2},{2,1},{3,4},{4,3},{5,6},{6,5},{7,8},{8,7},{9,10},{10,... | collective-permute-start | bytes 393224 | tf_op jit(solution)/shard_map/ppermute | solution.py:317
  35.3 0.0 collective-permute-done.12.message_ref.refs_2_
  35.3 0.6 %collective-permute-start.14 = (bf16[64,128]{1,0:T(8,128)(2,1)S(1)}, bf16[64,128]{1,0:T(8,128)(2,1)S(1)}, u32[]{:S(2)}, u32[]{:S(2)}) collective-permute-start(bf16[64,128]{1,0:T(8,128)(2,1)S(1)} %get-tuple-element.66.refs_4_), channel_id=1, source_target_pairs={{0,8},{1,10},{2,11},{3,9},{4,13},{5,14},{6,15},{7,12},{8,1},{9,2},... | collective-permute-start | bytes 49160 | tf_op jit(solution)/shard_map/ppermute | solution.py:330
  35.9 1.0 %collective-permute-start.15 = (bf16[64,128]{1,0:T(8,128)(2,1)S(1)}, bf16[64,128]{1,0:T(8,128)(2,1)S(1)}, u32[]{:S(2)}, u32[]{:S(2)}) collective-permute-start(bf16[64,128]{1,0:T(8,128)(2,1)S(1)} %get-tuple-element.67.refs_5_), channel_id=1, source_target_pairs={{0,9},{1,11},{2,10},{3,8},{4,12},{5,15},{6,14},{7,13},{8,0},{9,3},... | collective-permute-start | bytes 49160 | tf_op jit(solution)/shard_map/ppermute | solution.py:330
  36.9 1.3 %own.5 = (f32[64,1024]{1,0:T(8,128)S(1)}, bf16[4,64,1024]{2,1,0:T(8,128)(2,1)}) custom-call(s32[1]{0:T(128)} %bitcast.index_ref.refs_0_, bf16[64,1024]{1,0:T(8,128)(2,1)S(1)} %get-tuple-element.63.refs_1_, bf16[64,1536]{1,0:T(8,128)(2,1)S(1)} %collective-permute-done.12.message_ref.refs_2_, ...), custom_call_target="tpu_custom_call", output_to_operand_aliasing={{1}: (6, {})} | custom-call | flops 1000000000 | bytes 4194304 | tf_op jit(solution)/shard_map/own/pallas_call | solution.py:256
  38.1 1.6 %collective-permute-done.13.over_ref = bf16[64,1024]{1,0:T(8,128)(2,1)S(1)} collective-permute-done((bf16[64,1024]{1,0:T(8,128)(2,1)S(1)}, bf16[64,1024]{1,0:T(8,128)(2,1)S(1)}, u32[]{:S(2)}, u32[]{:S(2)}) %collective-permute-start.13) | collective-permute-done | bytes 131104 | tf_op jit(solution)/shard_map/ppermute | solution.py:317
  39.8 0.5 %halo.7.refs_0_ = f32[64,1024]{1,0:T(8,128)S(1)} custom-call(s32[1]{0:T(128)} %bitcast.index_ref.refs_0_, f32[64,1024]{1,0:T(8,128)S(1)} %get-tuple-element.69.acc_ref, bf16[64,1024]{1,0:T(8,128)(2,1)S(1)} %collective-permute-done.13.over_ref, bf16[36,256,256]{2,1,0:T(8,128)(2,1)S(1)} %get-tuple-element.46.d_ref.refs_3_), custom_call_target="tpu_custom_call" | custom-call | flops 1000000000 | bytes 4194304 | tf_op jit(solution)/shard_map/halo/pallas_call | solution.py:256
  40.3 0.1 collective-permute-done.14.refs_2_
  40.4 0.3 collective-permute-done.15.refs_3_
  40.7 0.9 %last.1 = bf16[4,64,1024]{2,1,0:T(8,128)(2,1)} custom-call(f32[64,1024]{1,0:T(8,128)S(1)} %halo.7.refs_0_, bf16[256,1024]{1,0:T(8,128)(2,1)S(1)} %get-tuple-element.47.refs_2_.refs_1_, bf16[64,128]{1,0:T(8,128)(2,1)S(1)} %collective-permute-done.14.refs_2_, bf16[64,128]{1,0:T(8,128)(2,1)S(1)} %collective-permute-done.15.refs_3_, ...), custom_call_target="tpu_custom_call", output_to_operand_aliasing={{}: (4, {})} | custom-call | flops 1000000000 | bytes 4194304 | tf_op jit(solution)/shard_map/last/pallas_call | solution.py:256
  (4 shorter events, 0.1 us)
Async XLA Ops:
  0.0 8.5 %copy-start.1 = (bf16[4,32,256]{2,1,0:T(8,128)(2,1)S(1)}, bf16[4,32,256]{2,1,0:T(8,128)(2,1)}, u32[]{:S(2)}) copy-start(bf16[4,32,256]{2,1,0:T(8,128)(2,1)} %refs_5_.3) | copy-start | bytes 196612
  0.0 8.5 %copy-start = (bf16[32,256,256]{2,1,0:T(8,128)(2,1)S(1)}, bf16[32,256,256]{2,1,0:T(8,128)(2,1)}, u32[]{:S(2)}) copy-start(bf16[32,256,256]{2,1,0:T(8,128)(2,1)} %refs_6_.3) | copy-start | bytes 12582916
  1.8 6.2 %collective-permute-start = (bf16[64,1536]{1,0:T(8,128)(2,1)S(1)}, bf16[64,1536]{1,0:T(8,128)(2,1)S(1)}, u32[]{:S(2)}, u32[]{:S(2)}) collective-permute-start(bf16[64,1536]{1,0:T(8,128)(2,1)S(1)} %get-tuple-element.41), channel_id=1, source_target_pairs={{0,1},{1,0},{2,3},{3,2},{4,5},{5,4},{6,7},{7,6},{8,9},{9,8},{10,11... | collective-permute-start | bytes 589832 | tf_op jit(solution)/shard_map/ppermute | solution.py:318
  2.4 8.6 %collective-permute-start.1 = (bf16[64,1024]{1,0:T(8,128)(2,1)}, bf16[64,1024]{1,0:T(8,128)(2,1)S(1)}, u32[]{:S(2)}, u32[]{:S(2)}) collective-permute-start(bf16[64,1024]{1,0:T(8,128)(2,1)} %refs_4_.1), channel_id=1, source_target_pairs={{0,15},{1,2},{2,1},{3,4},{4,3},{5,6},{6,5},{7,8},{8,7},{9,10},{10,... | collective-permute-start | bytes 393224 | tf_op jit(solution)/shard_map/ppermute | solution.py:317
  8.0 5.1 %collective-permute-start.2 = (bf16[64,128]{1,0:T(8,128)(2,1)S(1)}, bf16[64,128]{1,0:T(8,128)(2,1)S(1)}, u32[]{:S(2)}, u32[]{:S(2)}) collective-permute-start(bf16[64,128]{1,0:T(8,128)(2,1)S(1)} %get-tuple-element.43.refs_7_), channel_id=1, source_target_pairs={{0,8},{1,10},{2,11},{3,9},{4,13},{5,14},{6,15},{7,12},{8,1},{9,2},... | collective-permute-start | bytes 49160 | tf_op jit(solution)/shard_map/ppermute | solution.py:330
  8.1 5.0 %collective-permute-start.3 = (bf16[64,128]{1,0:T(8,128)(2,1)S(1)}, bf16[64,128]{1,0:T(8,128)(2,1)S(1)}, u32[]{:S(2)}, u32[]{:S(2)}) collective-permute-start(bf16[64,128]{1,0:T(8,128)(2,1)S(1)} %get-tuple-element.44.refs_8_), channel_id=1, source_target_pairs={{0,9},{1,11},{2,10},{3,8},{4,12},{5,15},{6,14},{7,13},{8,0},{9,3},... | collective-permute-start | bytes 49160 | tf_op jit(solution)/shard_map/ppermute | solution.py:330
  13.7 3.4 %collective-permute-start.4 = (bf16[64,1536]{1,0:T(8,128)(2,1)S(1)}, bf16[64,1536]{1,0:T(8,128)(2,1)S(1)}, u32[]{:S(2)}, u32[]{:S(2)}) collective-permute-start(bf16[64,1536]{1,0:T(8,128)(2,1)S(1)} %get-tuple-element.51), channel_id=1, source_target_pairs={{0,1},{1,0},{2,3},{3,2},{4,5},{5,4},{6,7},{7,6},{8,9},{9,8},{10,11... | collective-permute-start | bytes 589832 | tf_op jit(solution)/shard_map/ppermute | solution.py:318
  14.8 7.3 %collective-permute-start.5 = (bf16[64,1024]{1,0:T(8,128)(2,1)S(1)}, bf16[64,1024]{1,0:T(8,128)(2,1)S(1)}, u32[]{:S(2)}, u32[]{:S(2)}) collective-permute-start(bf16[64,1024]{1,0:T(8,128)(2,1)S(1)} %get-tuple-element.50.refs_1_), channel_id=1, source_target_pairs={{0,15},{1,2},{2,1},{3,4},{4,3},{5,6},{6,5},{7,8},{8,7},{9,10},{10,... | collective-permute-start | bytes 393224 | tf_op jit(solution)/shard_map/ppermute | solution.py:317
  17.1 5.5 %collective-permute-start.6 = (bf16[64,128]{1,0:T(8,128)(2,1)S(1)}, bf16[64,128]{1,0:T(8,128)(2,1)S(1)}, u32[]{:S(2)}, u32[]{:S(2)}) collective-permute-start(bf16[64,128]{1,0:T(8,128)(2,1)S(1)} %get-tuple-element.53.refs_4_), channel_id=1, source_target_pairs={{0,8},{1,10},{2,11},{3,9},{4,13},{5,14},{6,15},{7,12},{8,1},{9,2},... | collective-permute-start | bytes 49160 | tf_op jit(solution)/shard_map/ppermute | solution.py:330
  17.2 5.4 %collective-permute-start.7 = (bf16[64,128]{1,0:T(8,128)(2,1)S(1)}, bf16[64,128]{1,0:T(8,128)(2,1)S(1)}, u32[]{:S(2)}, u32[]{:S(2)}) collective-permute-start(bf16[64,128]{1,0:T(8,128)(2,1)S(1)} %get-tuple-element.54.refs_5_), channel_id=1, source_target_pairs={{0,9},{1,11},{2,10},{3,8},{4,12},{5,15},{6,14},{7,13},{8,0},{9,3},... | collective-permute-start | bytes 49160 | tf_op jit(solution)/shard_map/ppermute | solution.py:330
  23.2 3.0 %collective-permute-start.8 = (bf16[64,1536]{1,0:T(8,128)(2,1)S(1)}, bf16[64,1536]{1,0:T(8,128)(2,1)S(1)}, u32[]{:S(2)}, u32[]{:S(2)}) collective-permute-start(bf16[64,1536]{1,0:T(8,128)(2,1)S(1)} %get-tuple-element.57), channel_id=1, source_target_pairs={{0,1},{1,0},{2,3},{3,2},{4,5},{5,4},{6,7},{7,6},{8,9},{9,8},{10,11... | collective-permute-start | bytes 589832 | tf_op jit(solution)/shard_map/ppermute | solution.py:318
  23.5 7.2 %collective-permute-start.9 = (bf16[64,1024]{1,0:T(8,128)(2,1)S(1)}, bf16[64,1024]{1,0:T(8,128)(2,1)S(1)}, u32[]{:S(2)}, u32[]{:S(2)}) collective-permute-start(bf16[64,1024]{1,0:T(8,128)(2,1)S(1)} %get-tuple-element.56.refs_1_), channel_id=1, source_target_pairs={{0,15},{1,2},{2,1},{3,4},{4,3},{5,6},{6,5},{7,8},{8,7},{9,10},{10,... | collective-permute-start | bytes 393224 | tf_op jit(solution)/shard_map/ppermute | solution.py:317
  26.2 5.1 %collective-permute-start.10 = (bf16[64,128]{1,0:T(8,128)(2,1)S(1)}, bf16[64,128]{1,0:T(8,128)(2,1)S(1)}, u32[]{:S(2)}, u32[]{:S(2)}) collective-permute-start(bf16[64,128]{1,0:T(8,128)(2,1)S(1)} %get-tuple-element.59.refs_4_), channel_id=1, source_target_pairs={{0,8},{1,10},{2,11},{3,9},{4,13},{5,14},{6,15},{7,12},{8,1},{9,2},... | collective-permute-start | bytes 49160 | tf_op jit(solution)/shard_map/ppermute | solution.py:330
  27.2 4.6 %collective-permute-start.11 = (bf16[64,128]{1,0:T(8,128)(2,1)S(1)}, bf16[64,128]{1,0:T(8,128)(2,1)S(1)}, u32[]{:S(2)}, u32[]{:S(2)}) collective-permute-start(bf16[64,128]{1,0:T(8,128)(2,1)S(1)} %get-tuple-element.60.refs_5_), channel_id=1, source_target_pairs={{0,9},{1,11},{2,10},{3,8},{4,12},{5,15},{6,14},{7,13},{8,0},{9,3},... | collective-permute-start | bytes 49160 | tf_op jit(solution)/shard_map/ppermute | solution.py:330
  32.4 2.9 %collective-permute-start.12 = (bf16[64,1536]{1,0:T(8,128)(2,1)S(1)}, bf16[64,1536]{1,0:T(8,128)(2,1)S(1)}, u32[]{:S(2)}, u32[]{:S(2)}) collective-permute-start(bf16[64,1536]{1,0:T(8,128)(2,1)S(1)} %get-tuple-element.64), channel_id=1, source_target_pairs={{0,1},{1,0},{2,3},{3,2},{4,5},{5,4},{6,7},{7,6},{8,9},{9,8},{10,11... | collective-permute-start | bytes 589832 | tf_op jit(solution)/shard_map/ppermute | solution.py:318
  32.6 7.2 %collective-permute-start.13 = (bf16[64,1024]{1,0:T(8,128)(2,1)S(1)}, bf16[64,1024]{1,0:T(8,128)(2,1)S(1)}, u32[]{:S(2)}, u32[]{:S(2)}) collective-permute-start(bf16[64,1024]{1,0:T(8,128)(2,1)S(1)} %get-tuple-element.63.refs_1_), channel_id=1, source_target_pairs={{0,15},{1,2},{2,1},{3,4},{4,3},{5,6},{6,5},{7,8},{8,7},{9,10},{10,... | collective-permute-start | bytes 393224 | tf_op jit(solution)/shard_map/ppermute | solution.py:317
  35.3 5.1 %collective-permute-start.14 = (bf16[64,128]{1,0:T(8,128)(2,1)S(1)}, bf16[64,128]{1,0:T(8,128)(2,1)S(1)}, u32[]{:S(2)}, u32[]{:S(2)}) collective-permute-start(bf16[64,128]{1,0:T(8,128)(2,1)S(1)} %get-tuple-element.66.refs_4_), channel_id=1, source_target_pairs={{0,8},{1,10},{2,11},{3,9},{4,13},{5,14},{6,15},{7,12},{8,1},{9,2},... | collective-permute-start | bytes 49160 | tf_op jit(solution)/shard_map/ppermute | solution.py:330
  35.9 4.8 %collective-permute-start.15 = (bf16[64,128]{1,0:T(8,128)(2,1)S(1)}, bf16[64,128]{1,0:T(8,128)(2,1)S(1)}, u32[]{:S(2)}, u32[]{:S(2)}) collective-permute-start(bf16[64,128]{1,0:T(8,128)(2,1)S(1)} %get-tuple-element.67.refs_5_), channel_id=1, source_target_pairs={{0,9},{1,11},{2,10},{3,8},{4,12},{5,15},{6,14},{7,13},{8,0},{9,3},... | collective-permute-start | bytes 49160 | tf_op jit(solution)/shard_map/ppermute | solution.py:330
